TPU v7x, 32 devices: a whole 2x2x4 slice. The times are simulated.
32 devices in a mesh: fsdp: 4 (over x, core), ctx: 2 (over y), tp: 4 (over z).
Axes of the slice: x: 2, y: 2, z: 4, core: 2. Of those that a mesh axis runs over, the one named last changes fastest.
Arguments:
- tokens: bfloat16 [16, 2048, 1024], P('fsdp', 'ctx'), may hold values from -6 to 6
- teacher: bfloat16 [16, 2048, 1024], P('fsdp', 'ctx'), may hold values from -12 to 12
- lengths: int32 [16], P('fsdp'), may hold values from 512 to 2048, as said below
- attn_gain: bfloat16 [1024], P('fsdp'), may hold values from 0.25 to 1.75
- q_weight: bfloat16 [1024, 1024], P('fsdp', 'tp'), may hold values from -0.1875 to 0.1875
- k_weight: bfloat16 [1024, 512], P('fsdp', 'tp'), may hold values from -0.1875 to 0.1875
- v_weight: bfloat16 [1024, 512], P('fsdp', 'tp'), may hold values from -0.1875 to 0.1875
- q_gain: bfloat16 [64], P('fsdp'), may hold values from 0.25 to 1.75
- k_gain: bfloat16 [64], P('fsdp'), may hold values from 0.25 to 1.75
- o_weight: bfloat16 [1024, 1024], P('tp', 'fsdp'), may hold values from -3 to 3
- ffn_gain: bfloat16 [1024], P('fsdp'), may hold values from 0.25 to 1.75
- gate_weight: bfloat16 [1024, 4608], P('fsdp', 'tp'), may hold values from -0.1875 to 0.1875
- up_weight: bfloat16 [1024, 4608], P('fsdp', 'tp'), may hold values from -0.1875 to 0.1875
- down_weight: bfloat16 [4608, 1024], P('tp', 'fsdp'), may hold values from -0.09375 to 0.09375
Outputs:
- output: bfloat16 [16, 2048, 1024], P('fsdp', 'ctx')
- teacher_loss: float32 [], replicated
- tokens_grad: float32 [16, 2048, 1024], P('fsdp', 'ctx')
- attn_gain_grad: float32 [1024], P('fsdp')
- q_weight_grad: float32 [1024, 1024], P('fsdp', 'tp')
- k_weight_grad: float32 [1024, 512], P('fsdp', 'tp')
- v_weight_grad: float32 [1024, 512], P('fsdp', 'tp')
- q_gain_grad: float32 [64], P('fsdp')
- k_gain_grad: float32 [64], P('fsdp')
- o_weight_grad: float32 [1024, 1024], P('tp', 'fsdp')
- ffn_gain_grad: float32 [1024], P('fsdp')
- gate_weight_grad: float32 [1024, 4608], P('fsdp', 'tp')
- up_weight_grad: float32 [1024, 4608], P('fsdp', 'tp')
- down_weight_grad: float32 [4608, 1024], P('tp', 'fsdp')
Inputs may be any that keep to these rules, and one draw needn't show every extreme that they name: `lengths`: each row holds one sequence from slot 0; slots from its length on are padding. At least one row in every draw is full.
All inputs are finite; a program needn't handle non-finite values.
Results may differ from a plain program's by a relative error of at most 0.014.
Values may be sent and summed in bfloat16 or wider, within the bound.
A program may use at most 320 MiB of HBM per device.

v0:
```python
import math

import jax
import jax.numpy as jnp
from jax import lax
from jax.sharding import PartitionSpec as P

EPS = 1e-05
THETA = 1000000.0
NEGATIVE = -1e30


def rms_scale(field_in, gain_vec):
    return (
        field_in * lax.rsqrt(jnp.mean(field_in * field_in, axis=-1, keepdims=True) + EPS) * gain_vec
    )


def rotate(field_in, positions):
    half_dim = field_in.shape[-1] // 2
    frequency = THETA ** (-(2.0 * jnp.arange(half_dim, dtype=jnp.float32)) / field_in.shape[-1])
    angles = positions[:, None] * frequency[None, :]
    cos_part = jnp.cos(angles)[:, None, :]
    sin_part = jnp.sin(angles)[:, None, :]
    lower_half = field_in[..., :half_dim]
    upper_half = field_in[..., half_dim:]
    return jnp.concatenate(
        [
            lower_half * cos_part - upper_half * sin_part,
            upper_half * cos_part + lower_half * sin_part,
        ],
        axis=-1,
    )


def linear(left_mat, right_mat):
    return jnp.dot(left_mat, right_mat, preferred_element_type=jnp.float32)


def linear_left(left_mat, right_mat):
    return lax.dot_general(
        left_mat, right_mat, (((0,), (0,)), ((), ())), preferred_element_type=jnp.float32
    )


def linear_right(left_mat, right_mat):
    return lax.dot_general(
        left_mat, right_mat, (((1,), (1,)), ((), ())), preferred_element_type=jnp.float32
    )


def swiglu(gate_act, up_act):
    return jax.nn.silu(gate_act) * up_act


def per_device(
    tokens,
    teacher,
    lengths,
    attn_gain,
    q_weight,
    k_weight,
    v_weight,
    q_gain,
    k_gain,
    o_weight,
    ffn_gain,
    gate_weight,
    up_weight,
    down_weight,
):
    (
        gain_one,
        w_query,
        w_key,
        w_value,
        gain_query,
        gain_key,
        w_output,
        gain_two,
        w_gate,
        w_upper,
        w_down,
    ) = (
        lax.all_gather(attn_gain, "fsdp", axis=0, tiled=True),
        lax.all_gather(q_weight, "fsdp", axis=0, tiled=True),
        lax.all_gather(k_weight, "fsdp", axis=0, tiled=True),
        lax.all_gather(v_weight, "fsdp", axis=0, tiled=True),
        lax.all_gather(q_gain, "fsdp", axis=0, tiled=True),
        lax.all_gather(k_gain, "fsdp", axis=0, tiled=True),
        lax.all_gather(o_weight, "fsdp", axis=1, tiled=True),
        lax.all_gather(ffn_gain, "fsdp", axis=0, tiled=True),
        lax.all_gather(gate_weight, "fsdp", axis=0, tiled=True),
        lax.all_gather(up_weight, "fsdp", axis=0, tiled=True),
        lax.all_gather(down_weight, "fsdp", axis=1, tiled=True),
    )
    rows_dev, block_len, model_width = tokens.shape
    count_tok = rows_dev * block_len
    head_dim = gain_query.shape[0]
    q_heads = w_query.shape[1] // head_dim
    kv_heads = w_key.shape[1] // head_dim
    group_size = q_heads // kv_heads
    score_scale = head_dim ** (-0.5)
    row_len = block_len * lax.axis_size("ctx")
    key_block = math.gcd(row_len, 512)
    block_start = lax.axis_index("ctx") * block_len
    tiles_used = (block_start + block_len + key_block - 1) // key_block
    slot_pos = block_start + jnp.arange(block_len, dtype=jnp.int32)
    positions = slot_pos.astype(jnp.float32)
    valid = (slot_pos[None, :] < lengths[:, None]).astype(jnp.float32)
    slots = count_tok * lax.axis_size("fsdp") * lax.axis_size("ctx")
    gain_two_f = gain_two.astype(jnp.float32)
    gain_one_f = gain_one.astype(jnp.float32)
    inputs = tokens.astype(jnp.float32)
    normed_one, back_one = jax.vjp(rms_scale, inputs, gain_one_f)
    normed_low = normed_one.astype(jnp.bfloat16).reshape(count_tok, model_width)
    query_raw = linear(normed_low, w_query)
    key_raw = linear(normed_low, w_key)
    value_raw = linear(normed_low, w_value)

    def heads_post(raw_heads, gain_vec):
        shaped = raw_heads.reshape(rows_dev, block_len, -1, head_dim)
        return rotate(rms_scale(shaped, gain_vec), positions)

    query_rot, query_back = jax.vjp(heads_post, query_raw, gain_query.astype(jnp.float32))
    key_rot, key_back = jax.vjp(heads_post, key_raw, gain_key.astype(jnp.float32))
    queries = query_rot.astype(jnp.bfloat16).reshape(
        rows_dev, block_len, kv_heads, group_size, head_dim
    )
    key_rows = key_rot.astype(jnp.bfloat16).reshape(rows_dev, block_len, kv_heads * head_dim)
    values = value_raw.astype(jnp.bfloat16).reshape(rows_dev, block_len, kv_heads * head_dim)
    keys_all, values_all = (
        lax.all_gather(key_rows, "ctx", axis=1, tiled=True),
        lax.all_gather(values, "ctx", axis=1, tiled=True),
    )

    def key_tile(tile_index):
        tile_start = tile_index * key_block
        key_pos = tile_start + jnp.arange(key_block, dtype=jnp.int32)
        key_part = lax.dynamic_slice_in_dim(keys_all, tile_start, key_block, 1).reshape(
            rows_dev, key_block, kv_heads, head_dim
        )
        value_part = lax.dynamic_slice_in_dim(values_all, tile_start, key_block, 1).reshape(
            rows_dev, key_block, kv_heads, head_dim
        )
        scores = (
            jnp.einsum("rqhgd,rkhd->rhgqk", queries, key_part, preferred_element_type=jnp.float32)
            * score_scale
        )
        allowed = (key_pos[None, None, :] <= slot_pos[None, :, None]) & (
            key_pos[None, None, :] < lengths[:, None, None]
        )
        return (tile_start, scores, allowed[:, None, None], key_part, value_part)

    stat_shape = (rows_dev, kv_heads, group_size, block_len)

    def stats_step(tile_index, carried):
        running_max, running_sum = carried
        tile_start, scores, allowed, key_part, value_part = key_tile(tile_index)
        masked = jnp.where(allowed, scores, NEGATIVE)
        new_max = jnp.maximum(running_max, jnp.max(masked, axis=-1))
        terms = jnp.where(allowed, jnp.exp(masked - new_max[..., None]), 0.0)
        return (new_max, running_sum * jnp.exp(running_max - new_max) + jnp.sum(terms, axis=-1))

    running_max, running_sum = lax.fori_loop(
        0,
        tiles_used,
        stats_step,
        (jnp.full(stat_shape, NEGATIVE, jnp.float32), jnp.zeros(stat_shape, jnp.float32)),
    )
    log_total = running_max + jnp.log(running_sum)
    out_shape = (rows_dev, block_len, kv_heads, group_size, head_dim)

    def value_step(tile_index, carried):
        rounded_out, exact_out = carried
        tile_start, scores, allowed, key_part, value_part = key_tile(tile_index)
        tile_probs = jnp.where(allowed, jnp.exp(scores - log_total[..., None]), 0.0)
        rounded_out = rounded_out + jnp.einsum(
            "rhgqk,rkhd->rqhgd",
            tile_probs.astype(jnp.bfloat16),
            value_part,
            preferred_element_type=jnp.float32,
        )
        exact_out = exact_out + jnp.einsum(
            "rhgqk,rkhd->rqhgd", tile_probs, value_part.astype(jnp.float32)
        )
        return (rounded_out, exact_out)

    rounded_out, exact_out = lax.fori_loop(
        0,
        tiles_used,
        value_step,
        (jnp.zeros(out_shape, jnp.float32), jnp.zeros(out_shape, jnp.float32)),
    )
    attended = rounded_out.astype(jnp.bfloat16).reshape(count_tok, q_heads * head_dim)
    attn_total = lax.psum(linear(attended, w_output), "tp")
    resid = inputs + attn_total.reshape(rows_dev, block_len, model_width)
    normed_two, back_two = jax.vjp(rms_scale, resid, gain_two_f)
    normed_second = normed_two.astype(jnp.bfloat16).reshape(count_tok, model_width)
    gate_act = linear(normed_second, w_gate)
    up_act = linear(normed_second, w_upper)
    hidden_full, back_glu = jax.vjp(swiglu, gate_act, up_act)
    hidden = hidden_full.astype(jnp.bfloat16)
    ffn_total = lax.psum(linear(hidden, w_down), "tp")
    result = resid + ffn_total.reshape(rows_dev, block_len, model_width)
    error_value = result - teacher.astype(jnp.float32)
    valid_col = valid[..., None]
    total_square, total_count = lax.psum(
        (jnp.sum(valid_col * error_value * error_value), jnp.sum(valid)), ("fsdp", "ctx")
    )
    teacher_loss = total_square / (total_count * model_width)
    grad_result = valid_col * error_value * (slots / total_count)
    grad_low = grad_result.astype(jnp.bfloat16).reshape(count_tok, model_width)
    grad_down = linear_left(hidden, grad_low)
    grad_hidden = linear_right(grad_low, w_down)
    grad_gate_full, grad_up_full = back_glu(grad_hidden)
    grad_gate = grad_gate_full.astype(jnp.bfloat16)
    grad_up = grad_up_full.astype(jnp.bfloat16)
    grad_wgate = linear_left(normed_second, grad_gate)
    grad_wup = linear_left(normed_second, grad_up)
    normed_two_part = linear_right(grad_gate, w_gate) + linear_right(grad_up, w_upper)
    grad_normed_two = lax.psum(normed_two_part, "tp")
    grad_resid_norm, grad_gain_two = back_two(
        grad_normed_two.reshape(rows_dev, block_len, model_width)
    )
    grad_resid = grad_result + grad_resid_norm
    grad_attn_low = grad_resid.astype(jnp.bfloat16).reshape(count_tok, model_width)
    grad_woutput = linear_left(attended, grad_attn_low)
    grad_attended = linear_right(grad_attn_low, w_output).astype(jnp.bfloat16).reshape(out_shape)
    delta = jnp.einsum("rqhgd,rqhgd->rhgq", grad_attended.astype(jnp.float32), exact_out)
    full_shape = (rows_dev, row_len, kv_heads * head_dim)

    def grad_step(tile_index, carried):
        grad_queries, grad_keys, grad_values = carried
        tile_start, scores, allowed, key_part, value_part = key_tile(tile_index)
        tile_probs = jnp.where(allowed, jnp.exp(scores - log_total[..., None]), 0.0)
        grad_probs = jnp.einsum(
            "rqhgd,rkhd->rhgqk", grad_attended, value_part, preferred_element_type=jnp.float32
        )
        grad_scores = (tile_probs * (grad_probs - delta[..., None])).astype(jnp.bfloat16)
        grad_queries = (
            grad_queries
            + jnp.einsum(
                "rhgqk,rkhd->rqhgd", grad_scores, key_part, preferred_element_type=jnp.float32
            )
            * score_scale
        )
        key_term = (
            jnp.einsum(
                "rhgqk,rqhgd->rkhd", grad_scores, queries, preferred_element_type=jnp.float32
            )
            * score_scale
        )
        value_term = jnp.einsum(
            "rhgqk,rqhgd->rkhd",
            tile_probs.astype(jnp.bfloat16),
            grad_attended,
            preferred_element_type=jnp.float32,
        )
        grad_keys = lax.dynamic_update_slice_in_dim(
            grad_keys, key_term.reshape(rows_dev, key_block, kv_heads * head_dim), tile_start, 1
        )
        grad_values = lax.dynamic_update_slice_in_dim(
            grad_values, value_term.reshape(rows_dev, key_block, kv_heads * head_dim), tile_start, 1
        )
        return (grad_queries, grad_keys, grad_values)

    grad_queries, grad_keys, grad_values = lax.fori_loop(
        0,
        tiles_used,
        grad_step,
        (
            jnp.zeros(out_shape, jnp.float32),
            jnp.zeros(full_shape, jnp.float32),
            jnp.zeros(full_shape, jnp.float32),
        ),
    )
    key_grad, value_grad = (
        lax.psum_scatter(grad_keys, "ctx", scatter_dimension=1, tiled=True),
        lax.psum_scatter(grad_values, "ctx", scatter_dimension=1, tiled=True),
    )
    grad_query_raw, grad_gain_query = query_back(
        grad_queries.reshape(rows_dev, block_len, q_heads, head_dim)
    )
    grad_key_raw, grad_gain_key = key_back(
        key_grad.reshape(rows_dev, block_len, kv_heads, head_dim)
    )
    query_low = grad_query_raw.astype(jnp.bfloat16)
    key_low = grad_key_raw.astype(jnp.bfloat16)
    value_low = value_grad.reshape(count_tok, kv_heads * head_dim).astype(jnp.bfloat16)
    grad_wquery = linear_left(normed_low, query_low)
    grad_wkey = linear_left(normed_low, key_low)
    grad_wvalue = linear_left(normed_low, value_low)
    normed_part = (
        linear_right(query_low, w_query)
        + linear_right(key_low, w_key)
        + linear_right(value_low, w_value)
    )
    grad_normed_one, grad_gain_query, grad_gain_key = lax.psum(
        (normed_part, grad_gain_query, grad_gain_key), "tp"
    )
    grad_input_norm, grad_gain_one = back_one(
        grad_normed_one.reshape(rows_dev, block_len, model_width)
    )
    tokens_grad = grad_resid + grad_input_norm
    partials = (
        grad_gain_one,
        grad_wquery,
        grad_wkey,
        grad_wvalue,
        grad_gain_query,
        grad_gain_key,
        grad_woutput,
        grad_gain_two,
        grad_wgate,
        grad_wup,
        grad_down,
    )
    pieces = (
        lax.psum_scatter(partials[0], ("fsdp", "ctx"), scatter_dimension=0, tiled=True),
        lax.psum_scatter(partials[1], ("fsdp", "ctx"), scatter_dimension=0, tiled=True),
        lax.psum_scatter(partials[2], ("fsdp", "ctx"), scatter_dimension=0, tiled=True),
        lax.psum_scatter(partials[3], ("fsdp", "ctx"), scatter_dimension=0, tiled=True),
        lax.psum_scatter(partials[4], ("fsdp", "ctx"), scatter_dimension=0, tiled=True),
        lax.psum_scatter(partials[5], ("fsdp", "ctx"), scatter_dimension=0, tiled=True),
        lax.psum_scatter(partials[6], ("fsdp", "ctx"), scatter_dimension=1, tiled=True),
        lax.psum_scatter(partials[7], ("fsdp", "ctx"), scatter_dimension=0, tiled=True),
        lax.psum_scatter(partials[8], ("fsdp", "ctx"), scatter_dimension=0, tiled=True),
        lax.psum_scatter(partials[9], ("fsdp", "ctx"), scatter_dimension=0, tiled=True),
        lax.psum_scatter(partials[10], ("fsdp", "ctx"), scatter_dimension=1, tiled=True),
    )
    summed = (
        lax.all_gather(pieces[0], "ctx", axis=0, tiled=True),
        lax.all_gather(pieces[1], "ctx", axis=0, tiled=True),
        lax.all_gather(pieces[2], "ctx", axis=0, tiled=True),
        lax.all_gather(pieces[3], "ctx", axis=0, tiled=True),
        lax.all_gather(pieces[4], "ctx", axis=0, tiled=True),
        lax.all_gather(pieces[5], "ctx", axis=0, tiled=True),
        lax.all_gather(pieces[6], "ctx", axis=1, tiled=True),
        lax.all_gather(pieces[7], "ctx", axis=0, tiled=True),
        lax.all_gather(pieces[8], "ctx", axis=0, tiled=True),
        lax.all_gather(pieces[9], "ctx", axis=0, tiled=True),
        lax.all_gather(pieces[10], "ctx", axis=1, tiled=True),
    )
    return (
        result.astype(jnp.bfloat16),
        teacher_loss,
        tokens_grad,
        summed[0],
        summed[1],
        summed[2],
        summed[3],
        summed[4],
        summed[5],
        summed[6],
        summed[7],
        summed[8],
        summed[9],
        summed[10],
    )


def solution(mesh):
    return jax.shard_map(
        per_device,
        mesh=mesh,
        in_specs=(
            P("fsdp", "ctx", None),
            P("fsdp", "ctx", None),
            P("fsdp"),
            P("fsdp"),
            P("fsdp", "tp"),
            P("fsdp", "tp"),
            P("fsdp", "tp"),
            P("fsdp"),
            P("fsdp"),
            P("tp", "fsdp"),
            P("fsdp"),
            P("fsdp", "tp"),
            P("fsdp", "tp"),
            P("tp", "fsdp"),
        ),
        out_specs=(
            P("fsdp", "ctx", None),
            P(),
            P("fsdp", "ctx", None),
            P("fsdp"),
            P("fsdp", "tp"),
            P("fsdp", "tp"),
            P("fsdp", "tp"),
            P("fsdp"),
            P("fsdp"),
            P("tp", "fsdp"),
            P("fsdp"),
            P("fsdp", "tp"),
            P("fsdp", "tp"),
            P("tp", "fsdp"),
        ),
        check_vma=False,
    )
```

profile of v0, /device:TPU:0, one launch (start us, length us, event | category | flops | bytes accessed | tf_op | source)
XLA Modules:
  0.0 3488.7 jit_solution(7425707836104764950)
XLA Ops:
  90.3 63.3 %while.41 = (s32[]{:T(128)}, f32[4,2,2,1024]{3,2,1,0:T(2,128)S(1)}, f32[4,2,2,1024]{3,2,1,0:T(2,128)S(1)}, s32[]{:T(128)}, s32[4]{0:T(128)S(1)}, /*index=5*/bf16...) while((s32[]{:T(128)}, f32[4,2,2,1024]{3,2,1,0:T(2,128)S(1)}, ...), condition=%wide.region_6.7_spmd.clone, body=%wide.region_3.6_spmd.clone.sunk | while | flops 1143508480 | bytes 78989504 | solution.py:165
  159.4 108.0 %while.42 = (s32[]{:T(128)}, f32[4,1024,2,2,64]{1,4,3,2,0:T(8,128)}, f32[4,1024,2,2,64]{1,4,3,2,0:T(8,128)}, s32[]{:T(128)}, bf16[4,2048,128]{1,2,0:T(8,128)(2,1...) while((s32[]{:T(128)}, ...), condition=%wide.region_8.9_spmd.clone, body=%wide.region_7.8_spmd.clone.sunk | while | flops 3284667904 | bytes 130697424 | solution.py:189
  230.6 18.5 bitcast_add_fusion.7
  288.9 726.5 %all-reduce.21.cloned.1.call-done = f32[4,1024,1024]{2,1,0:T(8,128)} async-done(((f32[4,1024,1024]{2,1,0:T(8,128)}), f32[4,1024,1024]{2,1,0:T(8,128)}) %all-reduce.21.cloned.1.call-update) | async-done | bytes 16777232 | tf_op jit(solution)/shard_map/psum | solution.py:196
  1052.7 23.7 multiply_convert_fusion.1
  1110.7 545.1 %all-reduce.23.cloned.1.call-done = f32[4,1024,1024]{2,1,0:T(8,128)} async-done(((f32[4,1024,1024]{2,1,0:T(8,128)}), f32[4,1024,1024]{2,1,0:T(8,128)}) %all-reduce.23.cloned.1.call-update) | async-done | bytes 16777232 | tf_op jit(solution)/shard_map/psum | solution.py:204
  1673.4 29.9 multiply_convert_fusion
  1720.4 19.9 convolution_add_fusion
  1774.7 18.9 fusion.78
  1793.7 507.9 %all-reduce.25.cloned.1.call-done = f32[4,1024,1024]{2,1,0:T(8,128)} async-done(((f32[4,1024,1024]{2,1,0:T(8,128)}), f32[4,1024,1024]{2,1,0:T(8,128)}) %all-reduce.25.cloned.1.call-update) | async-done | bytes 16777232 | tf_op jit(solution)/shard_map/psum | solution.py:222
  2301.6 21.2 multiply_reduce_fusion
  2322.9 31.4 fusion.64
  2380.4 157.1 %while.43 = (s32[]{:T(128)}, f32[4,1024,2,2,64]{1,4,3,2,0:T(8,128)}, f32[4,2048,128]{1,2,0:T(8,128)}, f32[4,2048,128]{2,1,0:T(8,128)}, s32[]{:T(128)}, /*index=5...) while((s32[]{:T(128)}, ...), condition=%wide.region_19.20_spmd.clone, body=%wide.region_18.19_spmd.clone.sunk | while | flops 5457579520 | bytes 262883664 | solution.py:268
  2413.5 22.2 fusion.180
  2492.0 22.2 fusion.180
  2571.3 176.4 %reduce-scatter.10.cloned.1.call-done = f32[4,1024,128]{1,2,0:T(8,128)} async-done(((f32[4,2048,128]{1,2,0:T(8,128)}), f32[4,1024,128]{1,2,0:T(8,128)}) %reduce-scatter.10.cloned.1.call-update) | async-done | bytes 2097168 | tf_op jit(solution)/shard_map/reduce_scatter | solution.py:279
  2756.4 47.8 %reduce-scatter.12.cloned.1.call-done = f32[4,1024,128]{2,1,0:T(8,128)} async-done(((f32[4,2048,128]{2,1,0:T(8,128)}), f32[4,1024,128]{2,1,0:T(8,128)}) %reduce-scatter.12.cloned.1.call-update) | async-done | bytes 2097168 | tf_op jit(solution)/shard_map/reduce_scatter | solution.py:280
  2852.5 24.1 all-gather.25.cloned.1.call-done
  2876.7 40.1 %reduce-scatter.20.cloned.1.call-done = f32[256,128]{1,0:T(8,128)} async-done(((f32[256,1024]{1,0:T(8,128)}), f32[256,128]{1,0:T(8,128)}) %reduce-scatter.20.cloned.1.call-update) | async-done | bytes 131088 | tf_op jit(solution)/shard_map/reduce_scatter | solution.py:326
  2922.7 34.1 reduce-scatter.14.cloned.1.call-done
  2962.6 32.2 reduce-scatter.16.cloned.1.call-done
  3000.2 31.9 reduce-scatter.18.cloned.1.call-done
  3037.2 364.0 %all-reduce.27.cloned.1.call-done = f32[4,1024,1024]{2,1,0:T(8,128)} async-done(((f32[4,1024,1024]{2,1,0:T(8,128)}), f32[4,1024,1024]{2,1,0:T(8,128)}) %all-reduce.27.cloned.1.call-update) | async-done | bytes 16777232 | tf_op jit(solution)/shard_map/psum | solution.py:299
  3451.8 21.0 fusion.48
  (387 shorter events, 705.9 us)
Async XLA Ops:
  8.0 82.2 %all-gather.15.cloned.1.call-start = ((), (), s32[]{:S(2)}) async-start(), calls=%async_computation.10 | async-start | bytes 3145728 | tf_op jit(solution)/shard_map/all_gather | solution.py:133
  48.2 106.1 %all-gather.13.cloned.1.call-start = ((), (), s32[]{:S(2)}) async-start(), calls=%async_computation.9 | async-start | bytes 3145728 | tf_op jit(solution)/shard_map/all_gather | solution.py:134
  62.6 952.8 %all-reduce.21.cloned.1.call-start = ((), (), s32[]{:S(2)}) async-start(), calls=%async_computation.11 | async-start | bytes 33554432 | tf_op jit(solution)/shard_map/psum | solution.py:196
  267.5 843.1 %copy-start.41 = (s32[4]{0:T(128)}, s32[4]{0:T(128)S(1)}, u32[]{:S(2)}) copy-start(s32[4]{0:T(128)S(1)} %get-tuple-element.857) | copy-start | bytes 52
  281.9 753.0 %all-gather.17.cloned.1.call-start = ((), (), s32[]{:S(2)}) async-start(), calls=%async_computation.12 | async-start | bytes 2949120 | tf_op jit(solution)/shard_map/all_gather | solution.py:93
  282.4 770.3 %all-gather.19.cloned.1.call-start = ((), (), s32[]{:S(2)}) async-start(), calls=%async_computation.13 | async-start | bytes 2949120 | tf_op jit(solution)/shard_map/all_gather | solution.py:94
  283.0 793.4 %all-gather.21.cloned.1.call-start = ((), (), s32[]{:S(2)}) async-start(), calls=%async_computation.14 | async-start | bytes 2949120 | tf_op jit(solution)/shard_map/all_gather | solution.py:95
  283.6 1372.2 %all-reduce.23.cloned.1.call-start = ((), (), s32[]{:S(2)}) async-start(), calls=%async_computation.15 | async-start | bytes 33554432 | tf_op jit(solution)/shard_map/psum | solution.py:204
  288.9 736.2 %copy-start.51 = (f32[4,1,256]{2,1,0:T(1,128)}, f32[4,1,256]{2,1,0:T(1,128)S(1)}, u32[]{:S(2)}) copy-start(f32[4,1,256]{2,1,0:T(1,128)S(1)} %convert_element_type.131) | copy-start | bytes 12292
  1094.5 1207.1 %all-reduce.25.cloned.1.call-start = ((), (), s32[]{:S(2)}) async-start(), calls=%async_computation.16 | async-start | bytes 33554432 | tf_op jit(solution)/shard_map/psum | solution.py:222
  1740.3 797.9 %reduce-scatter.26.cloned.1.call-start = ((), (), s32[]{:S(2)}) async-start(), calls=%async_computation.28 | async-start | bytes 5308416 | tf_op jit(solution)/shard_map/reduce_scatter | solution.py:330
  1756.3 782.5 %reduce-scatter.22.cloned.1.call-start = ((), (), s32[]{:S(2)}) async-start(), calls=%async_computation.24 | async-start | bytes 5308416 | tf_op jit(solution)/shard_map/reduce_scatter | solution.py:328
  1774.6 765.0 %reduce-scatter.24.cloned.1.call-start = ((), (), s32[]{:S(2)}) async-start(), calls=%async_computation.26 | async-start | bytes 5308416 | tf_op jit(solution)/shard_map/reduce_scatter | solution.py:329
  1793.6 954.1 %reduce-scatter.10.cloned.1.call-start = ((), (), s32[]{:S(2)}) async-start(), calls=%async_computation.17 | async-start | bytes 6291456 | tf_op jit(solution)/shard_map/reduce_scatter | solution.py:279
  2537.6 266.6 %reduce-scatter.12.cloned.1.call-start = ((), (), s32[]{:S(2)}) async-start(), calls=%async_computation.18 | async-start | bytes 6291456 | tf_op jit(solution)/shard_map/reduce_scatter | solution.py:280
  2538.2 305.1 %all-gather.27.cloned.1.call-start = ((), (), s32[]{:S(2)}) async-start(), calls=%async_computation.29 | async-start | bytes 1769472 | tf_op jit(solution)/shard_map/all_gather | solution.py:343
  2538.8 313.8 %all-gather.23.cloned.1.call-start = ((), (), s32[]{:S(2)}) async-start(), calls=%async_computation.25 | async-start | bytes 1769472 | tf_op jit(solution)/shard_map/all_gather | solution.py:341
  2539.5 337.2 %all-gather.25.cloned.1.call-start = ((), (), s32[]{:S(2)}) async-start(), calls=%async_computation.27 | async-start | bytes 1769472 | tf_op jit(solution)/shard_map/all_gather | solution.py:342
  2540.1 376.7 %reduce-scatter.20.cloned.1.call-start = ((), (), s32[]{:S(2)}) async-start(), calls=%async_computation.23 | async-start | bytes 1179648 | tf_op jit(solution)/shard_map/reduce_scatter | solution.py:326
  2552.5 404.3 %reduce-scatter.14.cloned.1.call-start = ((), (), s32[]{:S(2)}) async-start(), calls=%async_computation.20 | async-start | bytes 1179648 | tf_op jit(solution)/shard_map/reduce_scatter | solution.py:321
  2571.1 423.7 %reduce-scatter.16.cloned.1.call-start = ((), (), s32[]{:S(2)}) async-start(), calls=%async_computation.21 | async-start | bytes 589824 | tf_op jit(solution)/shard_map/reduce_scatter | solution.py:322
  2756.4 275.7 %reduce-scatter.18.cloned.1.call-start = ((), (), s32[]{:S(2)}) async-start(), calls=%async_computation.22 | async-start | bytes 589824 | tf_op jit(solution)/shard_map/reduce_scatter | solution.py:323
  2820.6 580.6 %all-reduce.27.cloned.1.call-start = ((), (), s32[]{:S(2)}) async-start(), calls=%async_computation.19 | async-start | bytes 33554432 | tf_op jit(solution)/shard_map/psum | solution.py:299
  2838.8 562.4 %copy-start.37 = (f32[4,1024]{1,0:T(4,128)S(1)}, f32[4,1024]{1,0:T(4,128)}, u32[]{:S(2)}) copy-start(f32[4,1024]{1,0:T(4,128)} %copy-done.36) | copy-start | bytes 49156
  (71 other events, 4277.9 us)
Sparse Core Ops, SparseCore 0:
  48.3 33.4 all-gather.14
  84.0 33.1 all-gather.12
  282.0 733.3 all-reduce.20
  1094.6 561.1 all-reduce.22
  1740.4 561.1 all-reduce.24
  2839.0 562.2 all-reduce.26
Sparse Core Ops, SparseCore 1:
  283.9 195.1 all-gather.16
  480.5 23.9 all-gather.18
  505.9 24.1 all-gather.20
  1756.4 52.7 reduce-scatter.25
  1813.0 53.7 reduce-scatter.21
  1870.2 53.7 reduce-scatter.23
  2537.7 210.0 reduce-scatter.9
  2749.9 54.2 reduce-scatter.11
  2805.6 22.6 all-gather.26
  2829.9 22.6 all-gather.22
  2854.0 22.6 all-gather.24
  2880.8 36.0 reduce-scatter.19
  2920.8 35.9 reduce-scatter.13
  2960.7 34.1 reduce-scatter.15
  2997.9 34.1 reduce-scatter.17
where the time goes:
time: 3500 us; the launch traced here: 3490 us
  waiting for transfers between devices  2540 us (73%)
  matrix products  529 us (15%)
  other arithmetic  199 us (6%)
  blocking collectives  121 us (3%)
  local copies, waits for them, and re-layouts  71.3 us (2%)
    psum x1, waiting for transfers between devices, per_device(): attn_total = lax.psum(linear(attended, w_output), 'tp')  726 us
    psum x1, waiting for transfers between devices, per_device(): ffn_total = lax.psum(linear(hidden, w_down), 'tp')  545 us
    psum x1, waiting for transfers between devices, per_device(): grad_normed_two = lax.psum(normed_two_part, 'tp')  508 us
    psum x1, waiting for transfers between devices, per_device(): lax.psum((normed_part, grad_gain_query, grad_gain_key), 'tp')  364 us
    reduce_scatter x1, waiting for transfers between devices, per_device(): lax.psum_scatter(grad_keys, 'ctx', scatter_dimension=1, tiled=True)  176 us
    dot_general x7, matrix products, linear_right(): lax.dot_general(left_mat, right_mat, (((1,), (1,)), ((), ())), preferred_...  107 us
    dot_general x7, matrix products, linear(): return jnp.dot(left_mat, right_mat, preferred_element_type=jnp.float32)  83.2 us
    dot_general x6, matrix products, key_tile(): jnp.einsum('rqhgd,rkhd->rhgqk', queries, key_part, preferred_element_type...  80.4 us
  transfers between devices with their start and end apart: 21, of which 12 were waited for; matrix products, arithmetic and copies ran while one was open for 14% of the time, Pallas kernels for 0%

commit v1 on v0

--- a/solution.py
+++ b/solution.py
@@ -1,8 +1,11 @@
+import functools
 import math
 
 import jax
 import jax.numpy as jnp
 from jax import lax
+from jax.experimental import pallas as pl
+from jax.experimental.pallas import tpu as pltpu
 from jax.sharding import PartitionSpec as P
 
 EPS = 1e-05
@@ -53,7 +56,7 @@
     return jax.nn.silu(gate_act) * up_act
 
 
-def per_device(
+def per_device_any(
     tokens,
     teacher,
     lengths,
@@ -360,9 +363,668 @@
     )
 
 
+BF16 = jnp.bfloat16
+F32 = jnp.float32
+LOG2E = math.log2(math.e)
+X_SWAP = [(0, 2), (2, 0), (1, 3), (3, 1)]
+CORE_SWAP = [(0, 1), (1, 0), (2, 3), (3, 2)]
+Y_SWAP = [(0, 1), (1, 0)]
+Z_UP = [(0, 1), (1, 2), (2, 3), (3, 0)]
+Z_DOWN = [(0, 3), (1, 0), (2, 1), (3, 2)]
+
+
+def fits(mesh):
+    return dict(mesh.shape) == {"fsdp": 4, "ctx": 2, "tp": 4}
+
+
+def dot(left, right, left_dim, right_dim):
+    return lax.dot_general(
+        left, right, (((left_dim,), (right_dim,)), ((), ())), preferred_element_type=F32
+    )
+
+
+def sigmoid(v):
+    return 0.5 * jnp.tanh(0.5 * v) + 0.5
+
+
+def attn_fwd_kernel(width, len_ref, q_ref, k_ref, v_ref, o_ref, lse_ref, key_rows):
+    block = pl.program_id(1)
+    slots = k_ref.shape[1]
+    hd = k_ref.shape[0]
+    scale = hd**-0.5 * LOG2E
+    length = len_ref[0]
+
+    @pl.when(block == 0)
+    def _():
+        pos = lax.broadcasted_iota(jnp.int32, (hd, slots), 1)
+        row = lax.broadcasted_iota(jnp.int32, (hd, slots), 0)
+        bias = jnp.where((row == 0) & (pos >= length), NEGATIVE, 0.0)
+        both = jnp.concatenate([k_ref[...].astype(F32), bias], axis=0)
+        key_rows[...] = both.T.astype(BF16)
+
+    one_row = jnp.where(lax.broadcasted_iota(jnp.int32, (hd, 2 * width), 0) == 0, 1.0, 0.0)
+    pair = jnp.concatenate([q_ref[:hd, :], q_ref[hd:, :]], axis=1)
+    query = jnp.concatenate([pair, one_row.astype(BF16)], axis=0)
+
+    def tile(start, carried, diagonal):
+        out, total = carried
+        scores = dot(key_rows[pl.ds(start, width), :], query, 1, 0)
+        if diagonal:
+            key_pos = lax.broadcasted_iota(jnp.int32, (width, width), 0)
+            query_pos = lax.broadcasted_iota(jnp.int32, (width, width), 1)
+            allowed = key_pos <= query_pos
+            scores = jnp.where(jnp.concatenate([allowed, allowed], axis=1), scores, NEGATIVE)
+        probs = jnp.exp2(scores * scale)
+        total = total + jnp.sum(probs, axis=0, keepdims=True)
+        out = out + dot(v_ref[:, pl.ds(start, width)], probs.astype(BF16), 1, 0)
+        return out, total
+
+    carried = (jnp.zeros((hd, 2 * width), F32), jnp.zeros((1, 2 * width), F32))
+    full = jnp.minimum(block, lax.div(length + width - 1, width))
+    carried = lax.fori_loop(
+        0, full, lambda j, c: tile(pl.multiple_of(j * width, width), c, False), carried
+    )
+    out, total = tile(pl.multiple_of(block * width, width), carried, True)
+    out = out * (1.0 / total)
+    o_ref[:hd, :] = out[:, :width].astype(BF16)
+    o_ref[hd:, :] = out[:, width:].astype(BF16)
+    log_total = jnp.log2(total)
+    lse_ref[0, 0:1, :] = log_total[:, :width]
+    lse_ref[0, 1:2, :] = log_total[:, width:]
+
+
+def attn_fwd(length, queries, keys, values, hd, width):
+    kv_heads, slots = keys.shape[0] // hd, keys.shape[1]
+    return pl.pallas_call(
+        functools.partial(attn_fwd_kernel, width),
+        grid=(kv_heads, slots // width),
+        in_specs=[
+            pl.BlockSpec(memory_space=pltpu.SMEM),
+            pl.BlockSpec((2 * hd, width), lambda h, i: (h, i)),
+            pl.BlockSpec((hd, slots), lambda h, i: (h, 0)),
+            pl.BlockSpec((hd, slots), lambda h, i: (h, 0)),
+        ],
+        out_specs=[
+            pl.BlockSpec((2 * hd, width), lambda h, i: (h, i)),
+            pl.BlockSpec((1, 2, width), lambda h, i: (h, 0, i)),
+        ],
+        out_shape=[
+            jax.ShapeDtypeStruct((kv_heads * 2 * hd, slots), BF16),
+            jax.ShapeDtypeStruct((kv_heads, 2, slots), F32),
+        ],
+        scratch_shapes=[pltpu.VMEM((slots, 2 * hd), BF16)],
+        compiler_params=pltpu.CompilerParams(
+            dimension_semantics=("arbitrary", "arbitrary"), vmem_limit_bytes=40 << 20
+        ),
+        cost_estimate=pl.CostEstimate(
+            flops=kv_heads * 2 * slots * slots * 256 * 2,
+            bytes_accessed=8 * kv_heads * hd * slots * 2,
+            transcendentals=kv_heads * slots * slots,
+        ),
+        name="attn_fwd",
+    )(length, queries, keys, values)
+
+
+def attn_bwd_kernel(
+    width,
+    len_ref,
+    q_ref,
+    k_ref,
+    v_ref,
+    o_ref,
+    do_ref,
+    lse_ref,
+    dq_ref,
+    dk_ref,
+    dv_ref,
+    key_rows,
+    value_rows,
+    key_sum,
+    value_sum,
+):
+    block = pl.program_id(1)
+    slots = k_ref.shape[1]
+    hd = k_ref.shape[0]
+    scale = hd**-0.5
+    length = len_ref[0]
+
+    @pl.when(block == 0)
+    def _():
+        pos = lax.broadcasted_iota(jnp.int32, (hd, slots), 1)
+        row = lax.broadcasted_iota(jnp.int32, (hd, slots), 0)
+        bias = jnp.where((row == 0) & (pos >= length), NEGATIVE, 0.0)
+        both = jnp.concatenate([k_ref[...].astype(F32), bias], axis=0)
+        key_rows[...] = both.T.astype(BF16)
+        value_rows[...] = v_ref[...].astype(F32).T.astype(BF16)
+        key_sum[...] = jnp.zeros_like(key_sum)
+        value_sum[...] = jnp.zeros_like(value_sum)
+
+    @pl.when(block * width < length)
+    def _():
+        one_row = jnp.where(lax.broadcasted_iota(jnp.int32, (hd, 2 * width), 0) == 0, 1.0, 0.0)
+        pair = jnp.concatenate([q_ref[:hd, :], q_ref[hd:, :]], axis=1)
+        query = jnp.concatenate([pair, one_row.astype(BF16)], axis=0)
+        grad = jnp.concatenate([do_ref[:hd, :], do_ref[hd:, :]], axis=1)
+        out = jnp.concatenate([o_ref[:hd, :], o_ref[hd:, :]], axis=1)
+        query_rows = pair.astype(F32).T.astype(BF16)
+        grad_rows = grad.astype(F32).T.astype(BF16)
+        lse = jnp.concatenate([lse_ref[0, 0:1, :], lse_ref[0, 1:2, :]], axis=1)
+        delta = jnp.sum(grad.astype(F32) * out.astype(F32), axis=0, keepdims=True)
+
+        def tile(start, query_sum, diagonal):
+            scores = dot(key_rows[pl.ds(start, width), :], query, 1, 0)
+            if diagonal:
+                key_pos = lax.broadcasted_iota(jnp.int32, (width, width), 0)
+                query_pos = lax.broadcasted_iota(jnp.int32, (width, width), 1)
+                allowed = key_pos <= query_pos
+                scores = jnp.where(jnp.concatenate([allowed, allowed], axis=1), scores, NEGATIVE)
+            probs = jnp.exp2(scores * (scale * LOG2E) - lse)
+            grad_probs = dot(value_rows[pl.ds(start, width), :], grad, 1, 0)
+            grad_scores = (probs * (grad_probs - delta)).astype(BF16)
+            value_sum[pl.ds(start, width), :] += dot(probs.astype(BF16), grad_rows, 1, 0)
+            key_sum[pl.ds(start, width), :] += dot(grad_scores, query_rows, 1, 0)
+            return query_sum + dot(k_ref[:, pl.ds(start, width)], grad_scores, 1, 0)
+
+        query_sum = lax.fori_loop(
+            0,
+            block,
+            lambda j, s: tile(pl.multiple_of(j * width, width), s, False),
+            jnp.zeros((hd, 2 * width), F32),
+        )
+        query_sum = tile(pl.multiple_of(block * width, width), query_sum, True) * scale
+        dq_ref[:hd, :] = query_sum[:, :width].astype(BF16)
+        dq_ref[hd:, :] = query_sum[:, width:].astype(BF16)
+
+    @pl.when(block * width >= length)
+    def _():
+        dq_ref[...] = jnp.zeros_like(dq_ref)
+
+    @pl.when(block == pl.num_programs(1) - 1)
+    def _():
+        dk_ref[...] = (key_sum[...] * scale).T.astype(BF16)
+        dv_ref[...] = value_sum[...].T.astype(BF16)
+
+
+def attn_bwd(length, queries, keys, values, out, grad, lse, hd, width):
+    kv_heads, slots = keys.shape[0] // hd, keys.shape[1]
+    pair_spec = pl.BlockSpec((2 * hd, width), lambda h, i: (h, i))
+    head_spec = pl.BlockSpec((hd, slots), lambda h, i: (h, 0))
+    return pl.pallas_call(
+        functools.partial(attn_bwd_kernel, width),
+        grid=(kv_heads, slots // width),
+        in_specs=[
+            pl.BlockSpec(memory_space=pltpu.SMEM),
+            pair_spec,
+            head_spec,
+            head_spec,
+            pair_spec,
+            pair_spec,
+            pl.BlockSpec((1, 2, width), lambda h, i: (h, 0, i)),
+        ],
+        out_specs=[pair_spec, head_spec, head_spec],
+        out_shape=[
+            jax.ShapeDtypeStruct((kv_heads * 2 * hd, slots), BF16),
+            jax.ShapeDtypeStruct((kv_heads * hd, slots), BF16),
+            jax.ShapeDtypeStruct((kv_heads * hd, slots), BF16),
+        ],
+        scratch_shapes=[
+            pltpu.VMEM((slots, 2 * hd), BF16),
+            pltpu.VMEM((slots, hd), BF16),
+            pltpu.VMEM((slots, hd), F32),
+            pltpu.VMEM((slots, hd), F32),
+        ],
+        compiler_params=pltpu.CompilerParams(
+            dimension_semantics=("arbitrary", "arbitrary"), vmem_limit_bytes=40 << 20
+        ),
+        cost_estimate=pl.CostEstimate(
+            flops=kv_heads * 5 * slots * slots * 256 * 2,
+            bytes_accessed=14 * kv_heads * hd * slots * 2,
+            transcendentals=kv_heads * slots * slots,
+        ),
+        name="attn_bwd",
+    )(length, queries, keys, values, out, grad, lse)
+
+
+def ffn_fwd_kernel(x_ref, wa_ref, wb_ref, in_ref, out_ref, act_ref, hid_ref):
+    half = wa_ref.shape[0]
+    units = wa_ref.shape[1] // 3
+    x = x_ref[...]
+    act = dot(x[:, :half], wa_ref[:, : 2 * units], 1, 0)
+    act = act + dot(x[:, half:], wb_ref[:, : 2 * units], 1, 0)
+    gate, upper = act[:, :units], act[:, units:]
+    hidden = (gate * sigmoid(gate) * upper).astype(BF16)
+    act_ref[...] = act.astype(BF16)
+    hid_ref[...] = hidden
+    out_ref[:, :half] = in_ref[:, :half] + dot(hidden, wa_ref[:, 2 * units :], 1, 1)
+    out_ref[:, half:] = in_ref[:, half:] + dot(hidden, wb_ref[:, 2 * units :], 1, 1)
+
+
+def ffn_fwd(x, w_a, w_b, total, tile):
+    tok, width = x.shape
+    cols = w_a.shape[1]
+    units = cols // 3
+    rows_of = lambda n: pl.BlockSpec((tile, n), lambda i: (i, 0))
+    whole = lambda a: pl.BlockSpec(a.shape, lambda i: (0, 0), pipeline_mode=pl.Buffered(1))
+    return pl.pallas_call(
+        ffn_fwd_kernel,
+        grid=(tok // tile,),
+        in_specs=[rows_of(width), whole(w_a), whole(w_b), rows_of(width)],
+        out_specs=[rows_of(width), rows_of(2 * units), rows_of(units)],
+        out_shape=[
+            jax.ShapeDtypeStruct((tok, width), F32),
+            jax.ShapeDtypeStruct((tok, 2 * units), BF16),
+            jax.ShapeDtypeStruct((tok, units), BF16),
+        ],
+        input_output_aliases={3: 0},
+        compiler_params=pltpu.CompilerParams(
+            dimension_semantics=("arbitrary",), vmem_limit_bytes=48 << 20
+        ),
+        cost_estimate=pl.CostEstimate(
+            flops=2 * tok * width * cols, bytes_accessed=16 << 20, transcendentals=tok * units
+        ),
+        name="ffn_fwd",
+    )(x, w_a, w_b, total)
+
+
+def ffn_bwd_kernel(
+    steps,
+    grad_ref,
+    act_ref,
+    hid_ref,
+    wa_ref,
+    wb_ref,
+    in_ref,
+    xt_ref,
+    gradt_ref,
+    out_ref,
+    keep_ref,
+    send_ref,
+    dact_all,
+    hid_all,
+):
+    step = pl.program_id(0)
+    half = wa_ref.shape[0]
+    units = wa_ref.shape[1] // 3
+    tile = grad_ref.shape[0]
+
+    @pl.when(step < steps)
+    def _():
+        rows = pl.ds(pl.multiple_of(step * tile, tile), tile)
+        grad = grad_ref[...]
+        grad_hidden = dot(grad[:, :half], wa_ref[:, 2 * units :], 1, 0)
+        grad_hidden = grad_hidden + dot(grad[:, half:], wb_ref[:, 2 * units :], 1, 0)
+        gate = act_ref[:, :units].astype(F32)
+        upper = act_ref[:, units:].astype(F32)
+        sig = sigmoid(gate)
+        silu = gate * sig
+        dact_all[rows, :units] = (grad_hidden * upper * (sig + silu - silu * sig)).astype(BF16)
+        dact_all[rows, units:] = (grad_hidden * silu).astype(BF16)
+        hid_all[rows, :] = hid_ref[...]
+        dact = dact_all[rows, :]
+        out_ref[:, :half] = in_ref[:, :half] + dot(dact, wa_ref[:, : 2 * units], 1, 1)
+        out_ref[:, half:] = in_ref[:, half:] + dot(dact, wb_ref[:, : 2 * units], 1, 1)
+
+    def weight_rows(target):
+        target[:, : 2 * units] = dot(xt_ref[...], dact_all[...], 1, 0).astype(BF16)
+        target[:, 2 * units :] = dot(gradt_ref[...], hid_all[...], 1, 0).astype(BF16)
+
+    @pl.when((step >= steps) & (step < steps + 2))
+    def _():
+        weight_rows(send_ref)
+
+    @pl.when(step >= steps + 2)
+    def _():
+        weight_rows(keep_ref)
+
+
+def ffn_bwd(grad, act, hidden, w_a, w_b, total, xt, gradt, tile):
+    tok, width = grad.shape
+    half, cols = w_a.shape
+    units = cols // 3
+    steps = tok // tile
+    quarter = width // 4
+    rows_of = lambda n: pl.BlockSpec((tile, n), lambda i: (jnp.minimum(i, steps - 1), 0))
+    whole = lambda a: pl.BlockSpec(a.shape, lambda i: (0, 0), pipeline_mode=pl.Buffered(1))
+    feature = lambda i: (jnp.where(i < steps + 2, jnp.maximum(i - steps, 0) + 2, i - steps - 2), 0)
+    return pl.pallas_call(
+        functools.partial(ffn_bwd_kernel, steps),
+        grid=(steps + 4,),
+        in_specs=[
+            rows_of(width),
+            rows_of(2 * units),
+            rows_of(units),
+            whole(w_a),
+            whole(w_b),
+            rows_of(width),
+            pl.BlockSpec((quarter, tok), feature),
+            pl.BlockSpec((quarter, tok), feature),
+        ],
+        out_specs=[
+            rows_of(width),
+            pl.BlockSpec((quarter, cols), lambda i: (jnp.maximum(i - steps - 2, 0), 0)),
+            pl.BlockSpec((quarter, cols), lambda i: (jnp.clip(i - steps, 0, 1), 0)),
+        ],
+        out_shape=[
+            jax.ShapeDtypeStruct((tok, width), F32),
+            jax.ShapeDtypeStruct((half, cols), BF16),
+            jax.ShapeDtypeStruct((half, cols), BF16),
+        ],
+        scratch_shapes=[pltpu.VMEM((tok, 2 * units), BF16), pltpu.VMEM((tok, units), BF16)],
+        input_output_aliases={5: 0},
+        compiler_params=pltpu.CompilerParams(
+            dimension_semantics=("arbitrary",), vmem_limit_bytes=56 << 20
+        ),
+        cost_estimate=pl.CostEstimate(
+            flops=4 * tok * width * cols, bytes_accessed=32 << 20, transcendentals=tok * units
+        ),
+        name="ffn_bwd",
+    )(grad, act, hidden, w_a, w_b, total, xt, gradt)
+
+
+def z_gather(block):
+    one = lax.ppermute(block, "tp", Z_UP)
+    three = lax.ppermute(block, "tp", Z_DOWN)
+    two = lax.ppermute(one, "tp", Z_UP)
+    return [block, one, two, three]
+
+
+def plane_gather(block):
+    half = block.shape[0] // 2
+    first = lax.ppermute(block[:half], "fsdp", X_SWAP)
+    second = lax.ppermute(first, "ctx", Y_SWAP)
+    mine = jnp.concatenate([block, first, second], axis=0)
+    return mine, lax.ppermute(mine, "fsdp", CORE_SWAP)
+
+
+def add_low(left, right):
+    return (left.astype(F32) + right.astype(F32)).astype(BF16)
+
+
+def plane_reduce(keep, send, x_first):
+    mine = add_low(keep, lax.ppermute(send, "fsdp", CORE_SWAP))
+    q = mine.shape[0] // 4
+    if x_first:
+        own = add_low(mine[: 2 * q], lax.ppermute(mine[2 * q :], "fsdp", X_SWAP))
+        return add_low(own[:q], lax.ppermute(own[q:], "ctx", Y_SWAP))
+    other = jnp.concatenate([mine[q : 2 * q], mine[3 * q :]], axis=0)
+    here = jnp.concatenate([mine[:q], mine[2 * q : 3 * q]], axis=0)
+    here = add_low(here, lax.ppermute(other, "ctx", Y_SWAP))
+    return add_low(here[:q], lax.ppermute(here[q:], "fsdp", X_SWAP))
+
+
+def z_reduce(parts):
+    two = add_low(parts[1], lax.ppermute(parts[2], "tp", Z_DOWN))
+    total = parts[0].astype(F32) + lax.ppermute(two, "tp", Z_DOWN).astype(F32)
+    return total + lax.ppermute(parts[3], "tp", Z_UP).astype(F32)
+
+
+def per_device_rows(
+    tokens,
+    teacher,
+    lengths,
+    attn_gain,
+    q_weight,
+    k_weight,
+    v_weight,
+    q_gain,
+    k_gain,
+    o_weight,
+    ffn_gain,
+    gate_weight,
+    up_weight,
+    down_weight,
+):
+    z = lax.axis_index("tp")
+    ctx = lax.axis_index("ctx")
+    fsdp = lax.axis_index("fsdp")
+    rows_dev, tok, width = tokens.shape
+    lane = width // 8
+    place = fsdp * 2 + ctx
+    hd = q_gain.shape[0] * 4
+    q_cols, k_cols = q_weight.shape[1], k_weight.shape[1]
+    units = gate_weight.shape[1]
+    row_len = tok * 2
+    slots = rows_dev * 4 * row_len
+
+    def pick(array, blocks):
+        parts = [lax.dynamic_slice_in_dim(array, b * lane, lane, array.ndim - 1) for b in blocks]
+        return jnp.concatenate(parts, axis=-1)
+
+    def reorder(array):
+        return pick(array, [jnp.bitwise_xor(j, place) for j in (0, 1, 4, 5, 2, 3, 6, 7)])
+
+    def restore(array):
+        away = [jnp.bitwise_xor(j, place) for j in range(8)]
+        return pick(array, [(a & 1) + (a & 2) * 2 + (a & 4) // 2 for a in away])
+
+    def half_order(block):
+        half = block.shape[0] // 2
+        return jnp.where(ctx == 0, block, jnp.concatenate([block[half:], block[:half]], axis=0))
+
+    length = lax.dynamic_slice_in_dim(lengths, z, 1, 0)
+    total_count = lax.psum(jnp.sum(lengths), "fsdp").astype(F32)
+    gains = lax.all_gather(
+        jnp.concatenate([attn_gain, ffn_gain, q_gain, k_gain]), "fsdp", axis=0, tiled=False
+    ).astype(F32)
+    quarter = width // 4
+    gain_one = reorder(gains[:, :quarter].reshape(1, width))
+    gain_two = reorder(gains[:, quarter : 2 * quarter].reshape(1, width))
+    gain_query = gains[:, 2 * quarter : 2 * quarter + hd // 4].reshape(1, hd, 1)
+    gain_key = gains[:, 2 * quarter + hd // 4 :].reshape(1, hd, 1)
+
+    w_attn = half_order(jnp.concatenate([q_weight, k_weight, v_weight, o_weight.T], axis=1))
+    w_ffn = half_order(jnp.concatenate([gate_weight, up_weight, down_weight.T], axis=1))
+    attn_halves = [plane_gather(b) for b in z_gather(w_attn)]
+    ffn_halves = [plane_gather(b) for b in z_gather(w_ffn)]
+    proj = q_cols + 2 * k_cols
+    w_proj = [jnp.concatenate([a[:, :proj], b[:, :proj]], axis=0) for a, b in attn_halves]
+    w_proj = jnp.concatenate(w_proj, axis=1)
+    w_out = [jnp.concatenate([a[:, proj:], b[:, proj:]], axis=0) for a, b in attn_halves]
+    w_out = jnp.concatenate(w_out, axis=1)
+
+    x_in = reorder(lax.dynamic_index_in_dim(tokens, z, 0, keepdims=False)).astype(F32)
+    rho_one = lax.rsqrt(jnp.mean(x_in * x_in, axis=-1, keepdims=True) + EPS)
+    normed_one = (x_in * rho_one * gain_one).astype(BF16)
+    raw = dot(w_proj, normed_one, 0, 1).reshape(4, proj // hd, hd, tok)
+    heads_q, heads_k = q_cols // hd, k_cols // hd
+    raw_q = raw[:, :heads_q]
+    raw_k = raw[:, heads_q : heads_q + heads_k]
+
+    pos = (ctx * tok + jnp.arange(tok, dtype=jnp.int32)).astype(F32)
+    frequency = THETA ** (-(2.0 * jnp.arange(hd // 2, dtype=F32)) / hd)
+    angles = frequency[:, None] * pos[None, :]
+    cos_part, sin_part = jnp.cos(angles), jnp.sin(angles)
+
+    def turn(v, sin_part):
+        a, b = v[..., : hd // 2, :], v[..., hd // 2 :, :]
+        return jnp.concatenate(
+            [a * cos_part - b * sin_part, b * cos_part + a * sin_part], axis=-2
+        )
+
+    def head_norm(v):
+        return lax.rsqrt(jnp.mean(v * v, axis=-2, keepdims=True) + EPS)
+
+    rho_q, rho_k = head_norm(raw_q), head_norm(raw_k)
+    rot_q = turn(raw_q * rho_q * gain_query, sin_part).astype(BF16)
+    rot_k = turn(raw_k * rho_k * gain_key, sin_part).astype(BF16)
+    heads = jnp.concatenate([rot_q, rot_k, raw[:, heads_q + heads_k :].astype(BF16)], axis=1)
+
+    def split_heads(v):
+        return (
+            lax.dynamic_slice_in_dim(v, ctx * 2, 2, 0),
+            lax.dynamic_slice_in_dim(v, 2 - ctx * 2, 2, 0),
+        )
+
+    def to_rows(v):
+        mine, theirs = split_heads(v)
+        got = lax.ppermute(theirs, "ctx", Y_SWAP)
+        return jnp.concatenate(
+            [jnp.where(ctx == 0, mine, got), jnp.where(ctx == 0, got, mine)], axis=-1
+        )
+
+    rows = to_rows(heads)
+    queries = rows[:, :heads_q].reshape(2 * q_cols, row_len)
+    keys = rows[:, heads_q : heads_q + heads_k].reshape(2 * k_cols, row_len)
+    values = rows[:, heads_q + heads_k :].reshape(2 * k_cols, row_len)
+    attn_out, lse = attn_fwd(length, queries, keys, values, hd, 512)
+
+    def to_slots(v):
+        mine = lax.dynamic_slice_in_dim(v, ctx * tok, tok, v.ndim - 1)
+        theirs = lax.dynamic_slice_in_dim(v, tok - ctx * tok, tok, v.ndim - 1)
+        got = lax.ppermute(theirs, "ctx", Y_SWAP)
+        return jnp.concatenate(
+            [jnp.where(ctx == 0, mine, got), jnp.where(ctx == 0, got, mine)], axis=0
+        )
+
+    attended = to_slots(attn_out)
+    resid = x_in + dot(attended, w_out, 0, 1)
+    rho_two = lax.rsqrt(jnp.mean(resid * resid, axis=-1, keepdims=True) + EPS)
+    normed_two = (resid * rho_two * gain_two).astype(BF16)
+
+    result = resid
+    acts, hiddens = [None] * 4, [None] * 4
+    for k in (0, 1, 3, 2):
+        result, acts[k], hiddens[k] = ffn_fwd(normed_two, *ffn_halves[k], result, 256)
+    result_low = result.astype(BF16)
+
+    def spread(v):
+        parts = z_gather(restore(v))
+        out = jnp.zeros((rows_dev, tok, width), v.dtype)
+        for k in range(4):
+            out = lax.dynamic_update_slice(out, parts[k][None], (lax.rem(z - k + 4, 4), 0, 0))
+        return out
+
+    output = spread(result_low)
+
+    teach = reorder(lax.dynamic_index_in_dim(teacher, z, 0, keepdims=False)).astype(F32)
+    valid = (ctx * tok + jnp.arange(tok, dtype=jnp.int32) < length[0]).astype(F32)[:, None]
+    error = valid * (result - teach)
+    square = lax.psum(jnp.sum(error * error), ("fsdp", "ctx", "tp"))
+    teacher_loss = square / (total_count * width)
+    grad_result = error * (slots / total_count)
+    grad_low = grad_result.astype(BF16)
+
+    normed_two_t, grad_low_t = normed_two.T, grad_low.T
+    grad_two = jnp.zeros((tok, width), F32)
+    ffn_parts = [None] * 4
+    for k in (2, 1, 3, 0):
+        grad_two, keep, send = ffn_bwd(
+            grad_low,
+            acts[k],
+            hiddens[k],
+            *ffn_halves[k],
+            grad_two,
+            normed_two_t,
+            grad_low_t,
+            256,
+        )
+        ffn_parts[k] = plane_reduce(keep, send, k in (1, 2))
+
+    def norm_back(grad, value, rho, gain):
+        scaled = grad * gain
+        return rho * scaled - value * (
+            rho * rho * rho * jnp.mean(scaled * value, axis=-1, keepdims=True)
+        )
+
+    grad_gain_two = jnp.sum(grad_two * resid * rho_two, axis=0, keepdims=True)
+    grad_resid = grad_result + norm_back(grad_two, resid, rho_two, gain_two)
+    grad_attn = grad_resid.astype(BF16)
+
+    grad_attended = dot(w_out, grad_attn, 0, 1).astype(BF16)
+    grad_rows = to_rows(grad_attended.reshape(4, q_cols, tok)).reshape(2 * q_cols, row_len)
+    grad_q, grad_k, grad_v = attn_bwd(
+        length, queries, keys, values, attn_out, grad_rows, lse, hd, 512
+    )
+    grad_heads = jnp.concatenate(
+        [
+            grad_q.reshape(2, heads_q, hd, row_len),
+            grad_k.reshape(2, heads_k, hd, row_len),
+            grad_v.reshape(2, heads_k, hd, row_len),
+        ],
+        axis=1,
+    )
+    grad_heads = to_slots(grad_heads).astype(F32)
+
+    def head_back(grad, value, rho, gain):
+        turned = turn(grad, -sin_part)
+        unit = value * rho
+        gain_grad = jnp.sum(turned * unit, axis=(0, 1, 3))
+        scaled = turned * gain
+        back = rho * (scaled - unit * jnp.mean(scaled * unit, axis=-2, keepdims=True))
+        return back.astype(BF16), gain_grad
+
+    back_q, grad_gain_query = head_back(grad_heads[:, :heads_q], raw_q, rho_q, gain_query)
+    back_k, grad_gain_key = head_back(
+        grad_heads[:, heads_q : heads_q + heads_k], raw_k, rho_k, gain_key
+    )
+    back = jnp.concatenate(
+        [back_q, back_k, grad_heads[:, heads_q + heads_k :].astype(BF16)], axis=1
+    ).reshape(4 * proj, tok)
+    grad_one = dot(back, w_proj, 0, 1)
+    grad_gain_one = jnp.sum(grad_one * x_in * rho_one, axis=0, keepdims=True)
+    grad_tokens = grad_resid + norm_back(grad_one, x_in, rho_one, gain_one)
+    tokens_grad = spread(grad_tokens.astype(BF16)).astype(F32)
+
+    grad_wproj = dot(normed_one, back, 0, 1).astype(BF16)
+    grad_wout = dot(grad_attn, attended, 0, 1).astype(BF16)
+    half = width // 2
+    attn_parts = []
+    for k in range(4):
+        part = jnp.concatenate(
+            [
+                grad_wproj[:, k * proj : (k + 1) * proj],
+                grad_wout[:, k * q_cols : (k + 1) * q_cols],
+            ],
+            axis=1,
+        )
+        attn_parts.append(plane_reduce(part[:half], part[half:], k in (1, 2)))
+
+    def finish(parts):
+        own = z_reduce(parts)
+        other = lax.ppermute(own, "ctx", Y_SWAP)
+        return jnp.concatenate(
+            [jnp.where(ctx == 0, own, other), jnp.where(ctx == 0, other, own)], axis=0
+        )
+
+    ffn_grad = finish(ffn_parts)
+    attn_grad = finish(attn_parts)
+
+    gain_sums = lax.psum(
+        jnp.concatenate(
+            [
+                restore(grad_gain_one)[0],
+                restore(grad_gain_two)[0],
+                grad_gain_query,
+                grad_gain_key,
+            ]
+        ),
+        ("fsdp", "ctx", "tp"),
+    )
+
+    def own_part(at, size):
+        return lax.dynamic_slice_in_dim(gain_sums, at + fsdp * (size // 4), size // 4, 0)
+
+    return (
+        output,
+        teacher_loss,
+        tokens_grad,
+        own_part(0, width),
+        attn_grad[:, :q_cols],
+        attn_grad[:, q_cols : q_cols + k_cols],
+        attn_grad[:, q_cols + k_cols : proj],
+        own_part(2 * width, hd),
+        own_part(2 * width + hd, hd),
+        attn_grad[:, proj:].T,
+        own_part(width, width),
+        ffn_grad[:, :units],
+        ffn_grad[:, units : 2 * units],
+        ffn_grad[:, 2 * units :].T,
+    )
+
+
 def solution(mesh):
     return jax.shard_map(
-        per_device,
+        per_device_rows if fits(mesh) else per_device_any,
         mesh=mesh,
         in_specs=(
             P("fsdp", "ctx", None),

time: 3500 us -> 1300 us (0.37)
  waiting for transfers between devices: 2540 us -> 553 us
  matrix products: 529 us -> 46.6 us
  Pallas kernels: 0 us -> 224 us
  starting transfers between devices: 1.46 us -> 120 us
  local copies, waits for them, and re-layouts: 71.3 us -> 181 us
  other arithmetic: 199 us -> 94.5 us
  blocking collectives: 121 us -> 67.3 us
    psum x4 -> x0, waiting for transfers between devices: 2140 us -> none  [the longest x1 726 us: per_device(): attn_total = lax.psum(linear(attended, w_output), 'tp')]
    ppermute x0 -> x72, waiting for transfers between devices: none -> 553 us  [the longest x2 88.3 us: z_reduce(): return total + lax.ppermute(parts[3], 'tp', Z_UP).astype(F32)]
    dot_general x39 -> x6, matrix products: 529 us -> 46.6 us  [dot(): lax.dot_general(left, right, (((left_dim,), (right_dim,)), ((), ())), pre...]
    reduce_scatter x9 -> x0, waiting for transfers between devices: 363 us -> none  [the longest x1 176 us: per_device(): lax.psum_scatter(grad_keys, 'ctx', scatter_dimension=1, tiled=True)]
    pallas_call x0 -> x10, Pallas kernels: none -> 224 us  [the longest x4 104 us: ffn_bwd(): pl.pallas_call(functools.partial(ffn_bwd_kernel, steps), grid=(steps + 4,...]
    ppermute x0 -> x72, starting transfers between devices: none -> 120 us  [the longest x4 47 us: z_gather(): two = lax.ppermute(one, 'tp', Z_UP)]
    reduce_sum x9 -> x7, other arithmetic: 79.8 us -> 9.07 us  [the longest x1 4.64 us: per_device_rows(): grad_gain_two = jnp.sum(grad_two * resid * rho_two, axis=0, keepdims=True)]
    all_gather x12 -> x0, blocking collectives: 67.8 us -> none  [the longest x1 7.92 us: per_device(): lax.all_gather(o_weight, 'fsdp', axis=1, tiled=True)]
  transfers between devices with their start and end apart: 21 -> 72, of which waited for: 12 -> 24; matrix products, arithmetic and copies ran while one was open for 14% -> 18% of each run, Pallas kernels for 0% -> 8%
where the time goes in v1:
time: 1300 us; the launch traced here: 1290 us
  waiting for transfers between devices  553 us (43%)
  Pallas kernels  224 us (17%)
  local copies, waits for them, and re-layouts  181 us (14%)
  starting transfers between devices  120 us (9%)
  other arithmetic  94.5 us (7%)
  blocking collectives  67.3 us (5%)
  matrix products  46.6 us (4%)
    pallas_call x4, Pallas kernels, ffn_bwd(): pl.pallas_call(functools.partial(ffn_bwd_kernel, steps), grid=(steps + 4,...  104 us
    ppermute x2, waiting for transfers between devices, z_reduce(): return total + lax.ppermute(parts[3], 'tp', Z_UP).astype(F32)  88.3 us
    ppermute x4, waiting for transfers between devices, plane_reduce(): own = add_low(mine[:2 * q], lax.ppermute(mine[2 * q:], 'fsdp', X_SWAP))  86.6 us
    ppermute x8, waiting for transfers between devices, plane_gather(): second = lax.ppermute(first, 'ctx', Y_SWAP)  78.8 us
    ppermute x4, waiting for transfers between devices, plane_reduce(): here = add_low(here, lax.ppermute(other, 'ctx', Y_SWAP))  63.9 us
    unnamed x285, local copies, waits for them, and re-layouts  57.6 us
    pallas_call x4, Pallas kernels, ffn_fwd(): pl.pallas_call(ffn_fwd_kernel, grid=(tok // tile,), in_specs=[rows_of(wid...  51.7 us
    ppermute x4, starting transfers between devices, z_gather(): two = lax.ppermute(one, 'tp', Z_UP)  47 us
  transfers between devices with their start and end apart: 72, of which 24 were waited for; matrix products, arithmetic and copies ran while one was open for 18% of the time, Pallas kernels for 8%

profile of v1, /device:TPU:0, one launch (start us, length us, event | category | flops | bytes accessed | tf_op | source)
XLA Modules:
  0.0 1292.8 jit_solution(3148212114162981245)
XLA Ops:
  19.1 20.8 %all-reduce = bf16[2176]{0:T(1024)(128)(2,1)S(1)} all-reduce(bf16[2176]{0:T(1024)(128)(2,1)S(1)} %dynamic-update-slice), channel_id=2, replica_groups=mesh['fsdp'=4,'ctx'=2,'tp'=4] {'fsdp'}, use_global_device_ids=true, to_apply=%add | all-reduce | flops 2176 | bytes 8704
  146.0 37.1 %collective-permute-done.17 = bf16[256,3456]{1,0:T(8,128)(2,1)S(1)} collective-permute-done((bf16[256,3456]{1,0:T(8,128)(2,1)S(1)}, bf16[256,3456]{1,0:T(8,128)(2,1)S(1)}, u32[]{:S(2)}, u32[]{:S(2)}) %collective-permute-start.17) | collective-permute-done | bytes 1769504 | tf_op jit(solution)/shard_map/ppermute | solution.py:725
  212.4 19.4 %collective-permute-done.18 = bf16[256,3456]{1,0:T(8,128)(2,1)S(1)} collective-permute-done((bf16[256,3456]{1,0:T(8,128)(2,1)S(1)}, bf16[256,3456]{1,0:T(8,128)(2,1)S(1)}, u32[]{:S(2)}, u32[]{:S(2)}) %collective-permute-start.18) | collective-permute-done | bytes 1769504 | tf_op jit(solution)/shard_map/ppermute | solution.py:727
  233.4 55.5 %collective-permute-done.27 = bf16[128,3456]{1,0:T(8,128)(2,1)S(1)} collective-permute-done((bf16[128,3456]{1,0:T(8,128)(2,1)S(1)}, bf16[128,3456]{1,0:T(8,128)(2,1)S(1)}, u32[]{:S(2)}, u32[]{:S(2)}) %collective-permute-start.27) | collective-permute-done | bytes 884768 | tf_op jit(solution)/shard_map/ppermute | solution.py:734
  290.5 26.9 %attn_fwd.1 = (bf16[512,2048]{1,0:T(8,128)(2,1)S(1)}, f32[4,2,2048]{2,1,0:T(2,128)S(1)}) custom-call(s32[1]{0:T(128)} %dynamic_slice.282.len_ref, bf16[512,2048]{1,0:T(8,128)(2,1)S(1)} %bitcast.111, bf16[256,2048]{1,0:T(8,128)(2,1)S(1)} %bitcast.117, bf16[256,2048]{1,0:T(8,128)(2,1)S(1)} %bitcast.115), custom_call_target="tpu_custom_call" | custom-call | flops 17179869184 | bytes 8388608 | tf_op jit(solution)/shard_map/attn_fwd/pallas_call | solution.py:438
  323.0 20.7 %collective-permute-done.16 = bf16[512,1024]{1,0:T(8,128)(2,1)S(1)} collective-permute-done((bf16[512,1024]{1,0:T(8,128)(2,1)S(1)}, bf16[512,1024]{1,0:T(8,128)(2,1)S(1)}, u32[]{:S(2)}, u32[]{:S(2)}) %collective-permute-start.16) | collective-permute-done | bytes 1048608 | tf_op jit(solution)/shard_map/ppermute | solution.py:874
  344.3 15.4 %collective-permute-done.20 = bf16[128,3456]{1,0:T(8,128)(2,1)S(1)} collective-permute-done((bf16[128,3456]{1,0:T(8,128)(2,1)S(1)}, bf16[128,3456]{1,0:T(8,128)(2,1)S(1)}, u32[]{:S(2)}, u32[]{:S(2)}) %collective-permute-start.20) | collective-permute-done | bytes 884768 | tf_op jit(solution)/shard_map/ppermute | solution.py:734
  461.0 25.7 %ffn_bwd.4 = (f32[1024,1024]{1,0:T(8,128)}, bf16[512,3456]{1,0:T(8,128)(2,1)}, bf16[512,3456]{1,0:T(8,128)(2,1)}) custom-call(bf16[1024,1024]{1,0:T(8,128)(2,1)} %copy.65.grad_ref, bf16[1024,2304]{1,0:T(8,128)(2,1)} %get-tuple-element.54.act_ref, bf16[1024,1152]{1,0:T(8,128)(2,1)} %copy-done.8, ...), custom_call_target="tpu_custom_call", output_to_operand_aliasing={{0}: (5, {})} | custom-call | flops 14495514624 | bytes 33554432 | tf_op jit(solution)/shard_map/ffn_bwd/pallas_call | solution.py:689
  486.7 26.2 %ffn_bwd.5 = (f32[1024,1024]{1,0:T(8,128)}, bf16[512,3456]{1,0:T(8,128)(2,1)}, bf16[512,3456]{1,0:T(8,128)(2,1)}) custom-call(bf16[1024,1024]{1,0:T(8,128)(2,1)} %copy.65.grad_ref, bf16[1024,2304]{1,0:T(8,128)(2,1)} %get-tuple-element.52.act_ref, bf16[1024,1152]{1,0:T(8,128)(2,1)} %copy-done.7, ...), custom_call_target="tpu_custom_call", output_to_operand_aliasing={{0}: (5, {})} | custom-call | flops 14495514624 | bytes 33554432 | tf_op jit(solution)/shard_map/ffn_bwd/pallas_call | solution.py:689
  512.9 25.8 %ffn_bwd.6 = (f32[1024,1024]{1,0:T(8,128)}, bf16[512,3456]{1,0:T(8,128)(2,1)}, bf16[512,3456]{1,0:T(8,128)(2,1)}) custom-call(bf16[1024,1024]{1,0:T(8,128)(2,1)} %copy.65.grad_ref, bf16[1024,2304]{1,0:T(8,128)(2,1)} %get-tuple-element.50.act_ref, bf16[1024,1152]{1,0:T(8,128)(2,1)} %copy-done.6, ...), custom_call_target="tpu_custom_call", output_to_operand_aliasing={{0}: (5, {})} | custom-call | flops 14495514624 | bytes 33554432 | tf_op jit(solution)/shard_map/ffn_bwd/pallas_call | solution.py:689
  538.6 25.9 %ffn_bwd.7 = (f32[1024,1024]{1,0:T(8,128)}, bf16[512,3456]{1,0:T(8,128)(2,1)}, bf16[512,3456]{1,0:T(8,128)(2,1)}) custom-call(bf16[1024,1024]{1,0:T(8,128)(2,1)} %copy.65.grad_ref, bf16[1024,2304]{1,0:T(8,128)(2,1)} %get-tuple-element.48.act_ref, bf16[1024,1152]{1,0:T(8,128)(2,1)} %copy-done.5, ...), custom_call_target="tpu_custom_call", output_to_operand_aliasing={{0}: (5, {})} | custom-call | flops 14495514624 | bytes 33554432 | tf_op jit(solution)/shard_map/ffn_bwd/pallas_call | solution.py:689
  580.7 13.4 %convolution_convert_fusion.2 = bf16[1024,1024]{1,0:T(8,128)(2,1)S(1)} fusion(f32[1024,1024]{0,1:T(8,128)S(1)} %get-tuple-element.116, bf16[512,256]{0,1:T(8,128)(2,1)S(1)} %copy-done.77, bf16[512,256]{0,1:T(8,128)(2,1)S(1)} %copy-done.67, bf16[512,256]{0,1:T(8,128)(2,1)S(1)} %copy-done.79, bf16[512,256]{0,1:T(8,128)(2,1)S(1)} %copy-done.71, ...), kind=kOutput, calls=%fused_computation.80 | convolution fusion | flops 2166358016 | bytes 8388608 | tf_op jit(solution)/shard_map/dot_general | solution.py:381
  600.6 19.2 %collective-permute-done.35 = bf16[2,256,1024]{2,1,0:T(8,128)(2,1)S(1)} collective-permute-done((bf16[2,256,1024]{2,1,0:T(8,128)(2,1)S(1)}, bf16[2,256,1024]{2,1,0:T(8,128)(2,1)S(1)}, u32[]{:S(2)}, u32[]{:S(2)}) %collective-permute-start.35) | collective-permute-done | bytes 1048608 | tf_op jit(solution)/shard_map/ppermute | solution.py:860
  621.8 42.0 %attn_bwd.1 = (bf16[512,2048]{1,0:T(8,128)(2,1)S(1)}, bf16[256,2048]{1,0:T(8,128)(2,1)S(1)}, bf16[256,2048]{1,0:T(8,128)(2,1)S(1)}) custom-call(s32[1]{0:T(128)} %dynamic_slice.282.len_ref, bf16[512,2048]{1,0:T(8,128)(2,1)S(1)} %bitcast.112, bf16[256,2048]{1,0:T(8,128)(2,1)S(1)} %bitcast.118, bf16[256,2048]{1,0:T(8,128)(2,1)S(1)} %bitcast.116, ...), custom_call_target="tpu_custom_call" | custom-call | flops 42949672960 | bytes 14680064 | tf_op jit(solution)/shard_map/attn_bwd/pallas_call | solution.py:552
  680.2 14.0 %collective-permute-done.36 = bf16[2,8,64,1024]{3,2,1,0:T(8,128)(2,1)S(1)} collective-permute-done((bf16[2,8,64,1024]{3,2,1,0:T(8,128)(2,1)S(1)}, bf16[2,8,64,1024]{3,2,1,0:T(8,128)(2,1)S(1)}, u32[]{:S(2)}, u32[]{:S(2)}) %collective-permute-start.36) | collective-permute-done | bytes 2097184 | tf_op jit(solution)/shard_map/ppermute | solution.py:874
  694.2 44.9 %collective-permute-start.33 = (bf16[1024,1024]{1,0:T(8,128)(2,1)}, bf16[1024,1024]{1,0:T(8,128)(2,1)}, u32[]{:S(2)}, u32[]{:S(2)}) collective-permute-start(bf16[1024,1024]{1,0:T(8,128)(2,1)} %collective-permute-done.32), channel_id=1, source_target_pairs={{0,1},{1,2},{2,3},{3,0},{4,5},{5,6},{6,7},{7,4},{8,9},{9,10},{10,1... | collective-permute-start | bytes 6291464 | tf_op jit(solution)/shard_map/ppermute | solution.py:727
  772.2 41.0 %all-reduce.1 = (f32[]{:T(128)}, f32[2176]{0:T(1024)S(1)}) all-reduce(f32[]{:T(128)} %get-tuple-element.117, f32[2176]{0:T(1024)S(1)} %concatenate.215), channel_id=1, replica_groups=mesh['fsdp'=4,'ctx'=2,'tp'=4] {'fsdp','ctx','tp'}, use_global_device_ids=true, to_apply=%region_5.6 | all-reduce | flops 2177 | bytes 17416 | tf_op jit(solution)/shard_map/psum | solution.py:902
  871.1 63.8 %collective-permute-done.52 = bf16[256,768]{1,0:T(8,128)(2,1)S(1)} collective-permute-done((bf16[256,768]{1,0:T(8,128)(2,1)S(1)}, bf16[256,768]{1,0:T(8,128)(2,1)S(1)}, u32[]{:S(2)}, u32[]{:S(2)}) %collective-permute-start.52) | collective-permute-done | bytes 393248 | tf_op jit(solution)/shard_map/ppermute | solution.py:751
  940.1 73.1 %collective-permute-done.63 = bf16[256,3456]{1,0:T(8,128)(2,1)S(1)} collective-permute-done((bf16[256,3456]{1,0:T(8,128)(2,1)S(1)}, bf16[256,3456]{1,0:T(8,128)(2,1)S(1)}, u32[]{:S(2)}, u32[]{:S(2)}) %collective-permute-start.63) | collective-permute-done | bytes 1769504 | tf_op jit(solution)/shard_map/ppermute | solution.py:747
  1016.3 18.5 %collective-permute-done.64 = bf16[128,3456]{1,0:T(8,128)(2,1)S(1)} collective-permute-done((bf16[128,3456]{1,0:T(8,128)(2,1)S(1)}, bf16[128,3456]{1,0:T(8,128)(2,1)S(1)}, u32[]{:S(2)}, u32[]{:S(2)}) %collective-permute-start.64) | collective-permute-done | bytes 884768 | tf_op jit(solution)/shard_map/ppermute | solution.py:748
  1038.8 15.9 %collective-permute-done.61 = bf16[128,3456]{1,0:T(8,128)(2,1)S(1)} collective-permute-done((bf16[128,3456]{1,0:T(8,128)(2,1)S(1)}, bf16[128,3456]{1,0:T(8,128)(2,1)S(1)}, u32[]{:S(2)}, u32[]{:S(2)}) %collective-permute-start.61) | collective-permute-done | bytes 884768 | tf_op jit(solution)/shard_map/ppermute | solution.py:748
  1068.6 33.9 %collective-permute-done.49 = bf16[128,768]{1,0:T(8,128)(2,1)S(1)} collective-permute-done((bf16[128,768]{1,0:T(8,128)(2,1)S(1)}, bf16[128,768]{1,0:T(8,128)(2,1)S(1)}, u32[]{:S(2)}, u32[]{:S(2)}) %collective-permute-start.49) | collective-permute-done | bytes 196640 | tf_op jit(solution)/shard_map/ppermute | solution.py:756
  1112.1 88.3 %collective-permute-done.54 = bf16[128,768]{1,0:T(8,128)(2,1)S(1)} collective-permute-done((bf16[128,768]{1,0:T(8,128)(2,1)S(1)}, bf16[128,768]{1,0:T(8,128)(2,1)S(1)}, u32[]{:S(2)}, u32[]{:S(2)}) %collective-permute-start.54) | collective-permute-done | bytes 196640 | tf_op jit(solution)/shard_map/ppermute | solution.py:758
  1204.5 43.9 %collective-permute-done.50 = bf16[128,768]{1,0:T(8,128)(2,1)S(1)} collective-permute-done((bf16[128,768]{1,0:T(8,128)(2,1)S(1)}, bf16[128,768]{1,0:T(8,128)(2,1)S(1)}, u32[]{:S(2)}, u32[]{:S(2)}) %collective-permute-start.50) | collective-permute-done | bytes 196640 | tf_op jit(solution)/shard_map/ppermute | solution.py:757
  (624 shorter events, 475.2 us)
Async XLA Ops:
  17.0 105.8 %collective-permute-start.29 = (bf16[128,3456]{1,0:T(8,128)(2,1)}, bf16[128,3456]{1,0:T(8,128)(2,1)}, u32[]{:S(2)}, u32[]{:S(2)}) collective-permute-start(bf16[128,3456]{1,0:T(8,128)(2,1)} %slice.490), channel_id=1, source_target_pairs={{0,16},{16,0},{8,24},{24,8},{1,17},{17,1},{9,25},{25,9},{2,18},{18... | collective-permute-start | bytes 2654216 | tf_op jit(solution)/shard_map/ppermute | solution.py:733
  189.0 193.7 %collective-permute-start.31 = (bf16[512,3456]{1,0:T(8,128)(2,1)}, bf16[512,3456]{1,0:T(8,128)(2,1)}, u32[]{:S(2)}, u32[]{:S(2)}) collective-permute-start(bf16[512,3456]{1,0:T(8,128)(2,1)} %pad_maximum_fusion.5.wa_ref), channel_id=1, source_target_pairs={{0,8},{8,0},{16,24},{24,16},{1,9},{9,1},{17,25},{25,17},{2,10},{10... | collective-permute-start | bytes 10616840 | tf_op jit(solution)/shard_map/ppermute | solution.py:736
  203.1 86.8 %collective-permute-start.15 = (bf16[2,8,64,1024]{3,2,1,0:T(8,128)(2,1)S(1)}, bf16[2,8,64,1024]{3,2,1,0:T(8,128)(2,1)S(1)}, u32[]{:S(2)}, u32[]{:S(2)}) collective-permute-start(bf16[2,8,64,1024]{3,2,1,0:T(8,128)(2,1)S(1)} %constant_dynamic-slice_fusion.19), channel_id=1, source_target_pairs={{0,4},{4,0},{1,5},{5,1},{2,6},{6,2},{3,7},{7,3},{8,12},{12,8},{9,1... | collective-permute-start | bytes 6291464 | tf_op jit(solution)/shard_map/ppermute | solution.py:860
  208.4 110.7 %collective-permute-start.24 = (bf16[128,3456]{1,0:T(8,128)(2,1)S(1)}, bf16[128,3456]{1,0:T(8,128)(2,1)S(1)}, u32[]{:S(2)}, u32[]{:S(2)}) collective-permute-start(bf16[128,3456]{1,0:T(8,128)(2,1)S(1)} %collective-permute-done.23), channel_id=1, source_target_pairs={{0,4},{4,0},{1,5},{5,1},{2,6},{6,2},{3,7},{7,3},{8,12},{12,8},{9,1... | collective-permute-start | bytes 2654216 | tf_op jit(solution)/shard_map/ppermute | solution.py:734
  209.0 79.8 %collective-permute-start.27 = (bf16[128,3456]{1,0:T(8,128)(2,1)S(1)}, bf16[128,3456]{1,0:T(8,128)(2,1)S(1)}, u32[]{:S(2)}, u32[]{:S(2)}) collective-permute-start(bf16[128,3456]{1,0:T(8,128)(2,1)S(1)} %collective-permute-done.26), channel_id=1, source_target_pairs={{0,4},{4,0},{1,5},{5,1},{2,6},{6,2},{3,7},{7,3},{8,12},{12,8},{9,1... | collective-permute-start | bytes 2654216 | tf_op jit(solution)/shard_map/ppermute | solution.py:734
  231.9 88.1 %collective-permute-start.19 = (bf16[128,3456]{1,0:T(8,128)(2,1)S(1)}, bf16[128,3456]{1,0:T(8,128)(2,1)S(1)}, u32[]{:S(2)}, u32[]{:S(2)}) collective-permute-start(bf16[128,3456]{1,0:T(8,128)(2,1)S(1)} %slice.487), channel_id=1, source_target_pairs={{0,16},{16,0},{8,24},{24,8},{1,17},{17,1},{9,25},{25,9},{2,18},{18... | collective-permute-start | bytes 2654216 | tf_op jit(solution)/shard_map/ppermute | solution.py:733
  289.9 107.2 %collective-permute-start.28 = (bf16[512,3456]{1,0:T(8,128)(2,1)}, bf16[512,3456]{1,0:T(8,128)(2,1)}, u32[]{:S(2)}, u32[]{:S(2)}) collective-permute-start(bf16[512,3456]{1,0:T(8,128)(2,1)} %constant_dynamic-update-slice_fusion.31.wa_ref), channel_id=1, source_target_pairs={{0,8},{8,0},{16,24},{24,16},{1,9},{9,1},{17,25},{25,17},{2,10},{10... | collective-permute-start | bytes 10616840 | tf_op jit(solution)/shard_map/ppermute | solution.py:736
  320.0 91.3 %collective-permute-start.25 = (bf16[512,3456]{1,0:T(8,128)(2,1)}, bf16[512,3456]{1,0:T(8,128)(2,1)}, u32[]{:S(2)}, u32[]{:S(2)}) collective-permute-start(bf16[512,3456]{1,0:T(8,128)(2,1)} %constant_dynamic-update-slice_fusion.28.wa_ref), channel_id=1, source_target_pairs={{0,8},{8,0},{16,24},{24,16},{1,9},{9,1},{17,25},{25,17},{2,10},{10... | collective-permute-start | bytes 10616840 | tf_op jit(solution)/shard_map/ppermute | solution.py:736
  596.7 79.9 %collective-permute-start.32 = (bf16[1024,1024]{1,0:T(8,128)(2,1)S(1)}, bf16[1024,1024]{1,0:T(8,128)(2,1)}, u32[]{:S(2)}, u32[]{:S(2)}) collective-permute-start(bf16[1024,1024]{1,0:T(8,128)(2,1)S(1)} %dynamic-slice_dynamic-update-slice_fusion.8), channel_id=1, source_target_pairs={{0,1},{1,2},{2,3},{3,0},{4,5},{5,6},{6,7},{7,4},{8,9},{9,10},{10,1... | collective-permute-start | bytes 6291464 | tf_op jit(solution)/shard_map/ppermute | solution.py:725
  666.2 159.3 %collective-permute-start.56 = (bf16[512,3456]{1,0:T(8,128)(2,1)}, bf16[512,3456]{1,0:T(8,128)(2,1)}, u32[]{:S(2)}, u32[]{:S(2)}) collective-permute-start(bf16[512,3456]{1,0:T(8,128)(2,1)} %get-tuple-element.65), channel_id=1, source_target_pairs={{0,8},{8,0},{16,24},{24,16},{1,9},{9,1},{17,25},{25,17},{2,10},{10... | collective-permute-start | bytes 10616840 | tf_op jit(solution)/shard_map/ppermute | solution.py:744
  666.2 167.4 %collective-permute-start.67 = (bf16[512,3456]{1,0:T(8,128)(2,1)}, bf16[512,3456]{1,0:T(8,128)(2,1)}, u32[]{:S(2)}, u32[]{:S(2)}) collective-permute-start(bf16[512,3456]{1,0:T(8,128)(2,1)} %get-tuple-element.71), channel_id=1, source_target_pairs={{0,8},{8,0},{16,24},{24,16},{1,9},{9,1},{17,25},{25,17},{2,10},{10... | collective-permute-start | bytes 10616840 | tf_op jit(solution)/shard_map/ppermute | solution.py:744
  666.7 171.2 %collective-permute-start.59 = (bf16[512,3456]{1,0:T(8,128)(2,1)}, bf16[512,3456]{1,0:T(8,128)(2,1)}, u32[]{:S(2)}, u32[]{:S(2)}) collective-permute-start(bf16[512,3456]{1,0:T(8,128)(2,1)} %get-tuple-element.67), channel_id=1, source_target_pairs={{0,8},{8,0},{16,24},{24,16},{1,9},{9,1},{17,25},{25,17},{2,10},{10... | collective-permute-start | bytes 10616840 | tf_op jit(solution)/shard_map/ppermute | solution.py:744
  676.6 166.4 %collective-permute-start.62 = (bf16[512,3456]{1,0:T(8,128)(2,1)}, bf16[512,3456]{1,0:T(8,128)(2,1)}, u32[]{:S(2)}, u32[]{:S(2)}) collective-permute-start(bf16[512,3456]{1,0:T(8,128)(2,1)} %get-tuple-element.69), channel_id=1, source_target_pairs={{0,8},{8,0},{16,24},{24,16},{1,9},{9,1},{17,25},{25,17},{2,10},{10... | collective-permute-start | bytes 10616840 | tf_op jit(solution)/shard_map/ppermute | solution.py:744
  694.2 362.9 %collective-permute-start.33 = (bf16[1024,1024]{1,0:T(8,128)(2,1)}, bf16[1024,1024]{1,0:T(8,128)(2,1)}, u32[]{:S(2)}, u32[]{:S(2)}) collective-permute-start(bf16[1024,1024]{1,0:T(8,128)(2,1)} %collective-permute-done.32), channel_id=1, source_target_pairs={{0,1},{1,2},{2,3},{3,0},{4,5},{5,6},{6,7},{7,4},{8,9},{9,10},{10,1... | collective-permute-start | bytes 6291464 | tf_op jit(solution)/shard_map/ppermute | solution.py:727
  846.6 89.8 %collective-permute-start.57 = (bf16[256,3456]{1,0:T(8,128)(2,1)S(1)}, bf16[256,3456]{1,0:T(8,128)(2,1)S(1)}, u32[]{:S(2)}, u32[]{:S(2)}) collective-permute-start(bf16[256,3456]{1,0:T(8,128)(2,1)S(1)} %pad_maximum_fusion.10), channel_id=1, source_target_pairs={{0,4},{4,0},{1,5},{5,1},{2,6},{6,2},{3,7},{7,3},{8,12},{12,8},{9,1... | collective-permute-start | bytes 5308424 | tf_op jit(solution)/shard_map/ppermute | solution.py:751
  850.8 86.9 %collective-permute-start.68 = (bf16[256,3456]{1,0:T(8,128)(2,1)S(1)}, bf16[256,3456]{1,0:T(8,128)(2,1)S(1)}, u32[]{:S(2)}, u32[]{:S(2)}) collective-permute-start(bf16[256,3456]{1,0:T(8,128)(2,1)S(1)} %pad_maximum_fusion.11), channel_id=1, source_target_pairs={{0,4},{4,0},{1,5},{5,1},{2,6},{6,2},{3,7},{7,3},{8,12},{12,8},{9,1... | collective-permute-start | bytes 5308424 | tf_op jit(solution)/shard_map/ppermute | solution.py:751
  870.8 232.1 %collective-permute-start.37 = (bf16[1024,1024]{0,1:T(8,128)(2,1)S(1)}, bf16[1024,1024]{0,1:T(8,128)(2,1)}, u32[]{:S(2)}, u32[]{:S(2)}) collective-permute-start(bf16[1024,1024]{0,1:T(8,128)(2,1)S(1)} %copy-done.30), channel_id=1, source_target_pairs={{0,1},{1,2},{2,3},{3,0},{4,5},{5,6},{6,7},{7,4},{8,9},{9,10},{10,1... | collective-permute-start | bytes 6291464 | tf_op jit(solution)/shard_map/ppermute | solution.py:725
  937.8 120.6 %collective-permute-start.41 = (bf16[256,768]{1,0:T(8,128)(2,1)S(1)}, bf16[256,768]{1,0:T(8,128)(2,1)S(1)}, u32[]{:S(2)}, u32[]{:S(2)}) collective-permute-start(bf16[256,768]{1,0:T(8,128)(2,1)S(1)} %pad_maximum_fusion.22), channel_id=1, source_target_pairs={{0,4},{4,0},{1,5},{5,1},{2,6},{6,2},{3,7},{7,3},{8,12},{12,8},{9,1... | collective-permute-start | bytes 1179656 | tf_op jit(solution)/shard_map/ppermute | solution.py:751
  1102.5 147.0 %collective-permute-start.34 = (bf16[1024,1024]{1,0:T(8,128)(2,1)S(1)}, bf16[1024,1024]{1,0:T(8,128)(2,1)S(1)}, u32[]{:S(2)}, u32[]{:S(2)}) collective-permute-start(bf16[1024,1024]{1,0:T(8,128)(2,1)S(1)} %copy-done.32), channel_id=1, source_target_pairs={{0,3},{1,0},{2,1},{3,2},{4,7},{5,4},{6,5},{7,6},{8,11},{9,8},{10,9... | collective-permute-start | bytes 6291464 | tf_op jit(solution)/shard_map/ppermute | solution.py:726
  1102.9 148.1 %collective-permute-start.39 = (bf16[1024,1024]{0,1:T(8,128)(2,1)S(1)}, bf16[1024,1024]{0,1:T(8,128)(2,1)S(1)}, u32[]{:S(2)}, u32[]{:S(2)}) collective-permute-start(bf16[1024,1024]{0,1:T(8,128)(2,1)S(1)} %copy-done.30), channel_id=1, source_target_pairs={{0,3},{1,0},{2,1},{3,2},{4,7},{5,4},{6,5},{7,6},{8,11},{9,8},{10,9... | collective-permute-start | bytes 6291464 | tf_op jit(solution)/shard_map/ppermute | solution.py:726
  1106.2 94.2 %collective-permute-start.54 = (bf16[128,768]{1,0:T(8,128)(2,1)S(1)}, bf16[128,768]{1,0:T(8,128)(2,1)S(1)}, u32[]{:S(2)}, u32[]{:S(2)}) collective-permute-start(bf16[128,768]{1,0:T(8,128)(2,1)S(1)} %add_convert_fusion.23), channel_id=1, source_target_pairs={{0,1},{1,2},{2,3},{3,0},{4,5},{5,6},{6,7},{7,4},{8,9},{9,10},{10,1... | collective-permute-start | bytes 589832 | tf_op jit(solution)/shard_map/ppermute | solution.py:758
  1106.5 159.0 %collective-permute-start.38 = (bf16[1024,1024]{0,1:T(8,128)(2,1)}, bf16[1024,1024]{0,1:T(8,128)(2,1)}, u32[]{:S(2)}, u32[]{:S(2)}) collective-permute-start(bf16[1024,1024]{0,1:T(8,128)(2,1)} %collective-permute-done.37), channel_id=1, source_target_pairs={{0,1},{1,2},{2,3},{3,0},{4,5},{5,6},{6,7},{7,4},{8,9},{9,10},{10,1... | collective-permute-start | bytes 6291464 | tf_op jit(solution)/shard_map/ppermute | solution.py:727
  1110.5 137.9 %collective-permute-start.50 = (bf16[128,768]{1,0:T(8,128)(2,1)S(1)}, bf16[128,768]{1,0:T(8,128)(2,1)S(1)}, u32[]{:S(2)}, u32[]{:S(2)}) collective-permute-start(bf16[128,768]{1,0:T(8,128)(2,1)S(1)} %add_convert_fusion.24), channel_id=1, source_target_pairs={{0,3},{1,0},{2,1},{3,2},{4,7},{5,4},{6,5},{7,6},{8,11},{9,8},{10,9... | collective-permute-start | bytes 589832 | tf_op jit(solution)/shard_map/ppermute | solution.py:757
  1200.4 85.6 %collective-permute-start.71 = (f32[128,3456]{1,0:T(8,128)}, f32[128,3456]{1,0:T(8,128)}, u32[]{:S(2)}, u32[]{:S(2)}) collective-permute-start(f32[128,3456]{1,0:T(8,128)} %convert_add_fusion.1), channel_id=1, source_target_pairs={{0,4},{4,0},{1,5},{5,1},{2,6},{6,2},{3,7},{7,3},{8,12},{12,8},{9,1... | collective-permute-start | bytes 5308424 | tf_op jit(solution)/shard_map/ppermute | solution.py:984
  (151 other events, 3173.4 us)

commit v2 on v0

--- a/solution.py
+++ b/solution.py
@@ -1,8 +1,11 @@
+import functools
 import math
 
 import jax
 import jax.numpy as jnp
 from jax import lax
+from jax.experimental import pallas as pl
+from jax.experimental.pallas import tpu as pltpu
 from jax.sharding import PartitionSpec as P
 
 EPS = 1e-05
@@ -53,7 +56,7 @@
     return jax.nn.silu(gate_act) * up_act
 
 
-def per_device(
+def per_device_any(
     tokens,
     teacher,
     lengths,
@@ -360,9 +363,1242 @@
     )
 
 
+BF16 = jnp.bfloat16
+F32 = jnp.float32
+LOG2E = math.log2(math.e)
+X_SWAP = [(0, 2), (2, 0), (1, 3), (3, 1)]
+CORE_SWAP = [(0, 1), (1, 0), (2, 3), (3, 2)]
+Y_SWAP = [(0, 1), (1, 0)]
+Z_UP = [(0, 1), (1, 2), (2, 3), (3, 0)]
+Z_DOWN = [(0, 3), (1, 0), (2, 1), (3, 2)]
+Z_NEAR = [(0, 1), (1, 0), (2, 3), (3, 2)]
+Z_FAR = [(0, 2), (2, 0), (1, 3), (3, 1)]
+MASKS = (0, 2, 1, 3)
+ANY = pl.BlockSpec(memory_space=pl.ANY)
+SMEM = pl.BlockSpec(memory_space=pltpu.SMEM)
+
+
+def fits(mesh):
+    return dict(mesh.shape) == {"fsdp": 4, "ctx": 2, "tp": 4}
+
+
+def dot(left, right, left_dim, right_dim):
+    return lax.dot_general(
+        left, right, (((left_dim,), (right_dim,)), ((), ())), preferred_element_type=F32
+    )
+
+
+def sigmoid(v):
+    return 0.5 * jnp.tanh(0.5 * v) + 0.5
+
+
+def whole(shape):
+    zeros = (0,) * len(shape)
+    return pl.BlockSpec(shape, lambda *_: zeros, pipeline_mode=pl.Buffered(1))
+
+
+def settings(dims, mib):
+    return pltpu.CompilerParams(
+        dimension_semantics=("arbitrary",) * dims, vmem_limit_bytes=mib << 20
+    )
+
+
+def shape_of(shape, dtype):
+    return jax.ShapeDtypeStruct(shape, dtype)
+
+
+def cost(flops, bytes_accessed):
+    return pl.CostEstimate(flops=flops, bytes_accessed=bytes_accessed, transcendentals=0)
+
+
+def pack_kernel(info, q_ref, k_ref, v_ref, o_ref, g_ref, u_ref, d_ref, attn_ref, ffn_ref):
+    ctx = info[2]
+    q_cols, k_cols = q_ref.shape[1], k_ref.shape[1]
+    attn_ref[:, :q_cols] = q_ref[...]
+    attn_ref[:, q_cols : q_cols + k_cols] = k_ref[...]
+    attn_ref[:, q_cols + k_cols : q_cols + 2 * k_cols] = v_ref[...]
+    attn_ref[:, q_cols + 2 * k_cols :] = o_ref[...].astype(F32).T.astype(BF16)
+    third = g_ref.shape[1] // 3
+    for j in range(3):
+        at = pl.multiple_of(jnp.where(ctx == 0, j, 2 - j) * third, third)
+        base = 3 * third * j
+        ffn_ref[:, base : base + third] = g_ref[:, pl.ds(at, third)]
+        ffn_ref[:, base + third : base + 2 * third] = u_ref[:, pl.ds(at, third)]
+        down = d_ref[pl.ds(at, third), :].astype(F32).T.astype(BF16)
+        ffn_ref[:, base + 2 * third : base + 3 * third] = down
+
+
+def pack(info, q, k, v, o, g, u, d):
+    rows = q.shape[0]
+    attn_cols = q.shape[1] + 2 * k.shape[1] + o.shape[0]
+    return pl.pallas_call(
+        pack_kernel,
+        in_specs=[SMEM] + [pl.BlockSpec(memory_space=pltpu.VMEM)] * 7,
+        out_specs=[pl.BlockSpec(memory_space=pltpu.VMEM)] * 2,
+        out_shape=[shape_of((rows, attn_cols), BF16), shape_of((rows, 3 * g.shape[1]), BF16)],
+        compiler_params=pltpu.CompilerParams(vmem_limit_bytes=24 << 20),
+        cost_estimate=cost(0, 6 << 20),
+        name="pack",
+    )(info, q, k, v, o, g, u, d)
+
+
+def norm_one_kernel(info, tok_ref, gain_ref, x_ref, nt_ref, x32):
+    quarter = x_ref.shape[1] // 4
+    for p, mask in enumerate(MASKS):
+        at = pl.multiple_of(jnp.bitwise_xor(info[1], mask) * quarter, quarter)
+        part = tok_ref[0, :, pl.ds(at, quarter)]
+        x_ref[:, p * quarter : (p + 1) * quarter] = part
+        x32[:, p * quarter : (p + 1) * quarter] = part.astype(F32)
+    x = x32[...]
+    rho = lax.rsqrt(jnp.mean(x * x, axis=-1, keepdims=True) + EPS)
+    nt_ref[...] = (x * rho * gain_ref[...]).T.astype(BF16)
+
+
+def norm_one(info, tokens, gain, tile):
+    _, tok, width = tokens.shape
+    return pl.pallas_call(
+        norm_one_kernel,
+        grid_spec=pltpu.PrefetchScalarGridSpec(
+            num_scalar_prefetch=1,
+            grid=(tok // tile,),
+            in_specs=[
+                pl.BlockSpec((1, tile, width), lambda i, info: (info[0], i, 0)),
+                pl.BlockSpec((1, width), lambda i, info: (0, 0)),
+            ],
+            out_specs=[
+                pl.BlockSpec((tile, width), lambda i, info: (i, 0)),
+                pl.BlockSpec((width, tile), lambda i, info: (0, i)),
+            ],
+            scratch_shapes=[pltpu.VMEM((tile, width), F32)],
+        ),
+        out_shape=[shape_of((tok, width), BF16), shape_of((width, tok), BF16)],
+        compiler_params=settings(1, 24),
+        cost_estimate=cost(0, 6 << 20),
+        name="norm_one",
+    )(info, tokens, gain)
+
+
+def proj_kernel(heads, info, w_ref, nt_ref, cos_ref, sin_ref, qg_ref, kg_ref, rot_ref, raw_ref):
+    hd = qg_ref.shape[0]
+    tok = nt_ref.shape[1]
+    half = hd // 2
+    raw = dot(w_ref[0], nt_ref[...], 0, 0)
+    cos_part, sin_part = cos_ref[...], sin_ref[...]
+    heads_q, heads_k = heads
+    raw_ref[...] = raw.astype(BF16)
+    for h in range(heads_q + heads_k):
+        v = raw[h * hd : (h + 1) * hd]
+        rho = lax.rsqrt(jnp.mean(v * v, axis=0, keepdims=True) + EPS)
+        v = v * rho * (qg_ref[...] if h < heads_q else kg_ref[...])
+        a, b = v[:half], v[half:]
+        rot_ref[h * hd : h * hd + half, :] = (a * cos_part - b * sin_part).astype(BF16)
+        rot_ref[h * hd + half : (h + 1) * hd, :] = (b * cos_part + a * sin_part).astype(BF16)
+    at = (heads_q + heads_k) * hd
+    rot_ref[at:, :] = raw[at:].astype(BF16)
+
+
+def project(info, w_proj, normed_t, cos_part, sin_part, gain_q, gain_k, heads, block):
+    _, width, cols = w_proj.shape
+    tok = normed_t.shape[1]
+    tile = min(512, tok)
+    const = lambda a: pl.BlockSpec(a.shape, lambda i, info: (0, 0))
+    tab = lambda a: pl.BlockSpec((a.shape[0], tile), lambda i, info: (0, i))
+    return pl.pallas_call(
+        functools.partial(proj_kernel, heads),
+        grid_spec=pltpu.PrefetchScalarGridSpec(
+            num_scalar_prefetch=1,
+            grid=(tok // tile,),
+            in_specs=[
+                pl.BlockSpec((1, width, cols), lambda i, info: (block(info), 0, 0)),
+                tab(normed_t),
+                tab(cos_part),
+                tab(sin_part),
+                const(gain_q),
+                const(gain_k),
+            ],
+            out_specs=[pl.BlockSpec((cols, tile), lambda i, info: (0, i))] * 2,
+        ),
+        out_shape=[shape_of((cols, tok), BF16), shape_of((cols, tok), BF16)],
+        compiler_params=settings(1, 24),
+        cost_estimate=cost(2 * width * cols * tok, 6 << 20),
+        name="project",
+    )(info, w_proj, normed_t, cos_part, sin_part, gain_q, gain_k)
+
+
+def head_back_kernel(
+    heads, info, dm_ref, dt_ref, rm_ref, rt_ref, cos_ref, sin_ref, qg_ref, kg_ref, out_ref, gg_ref
+):
+    step, part = pl.program_id(0), pl.program_id(1)
+    hd = qg_ref.shape[0]
+    half = hd // 2
+    heads_q, heads_k = heads
+    cos_part, sin_part = cos_ref[...], sin_ref[...]
+    tile = cos_part.shape[1]
+
+    @pl.when((step == 0) & (part == 0))
+    def _():
+        gg_ref[...] = jnp.zeros_like(gg_ref)
+
+    def work(d_ref, r_ref):
+        gain_q = jnp.zeros((hd, 1), F32)
+        gain_k = jnp.zeros((hd, 1), F32)
+        done = []
+        for h in range(heads_q + heads_k):
+            is_q = h < heads_q
+            g = d_ref[h * hd : (h + 1) * hd, :].astype(F32)
+            raw = r_ref[h * hd : (h + 1) * hd, :].astype(F32)
+            a, b = g[:half], g[half:]
+            turned = jnp.concatenate(
+                [a * cos_part + b * sin_part, b * cos_part - a * sin_part], axis=0
+            )
+            rho = lax.rsqrt(jnp.mean(raw * raw, axis=0, keepdims=True) + EPS)
+            unit = raw * rho
+            prod = turned * unit
+            scaled = turned * (qg_ref[...] if is_q else kg_ref[...])
+            mean = jnp.mean(scaled * unit, axis=0, keepdims=True)
+            done.append(rho * (scaled - unit * mean))
+            total = jnp.sum(prod, axis=1, keepdims=True)
+            if is_q:
+                gain_q = gain_q + total
+            else:
+                gain_k = gain_k + total
+        done.append(d_ref[(heads_q + heads_k) * hd :, :].astype(F32))
+        out_ref[0] = jnp.concatenate(done, axis=0).T.astype(BF16)
+        lane = lax.broadcasted_iota(jnp.int32, gg_ref.shape, 1)
+        gg_ref[...] += jnp.where(lane == 0, gain_q, jnp.where(lane == 1, gain_k, 0.0))
+
+    @pl.when(step == 0)
+    def _():
+        work(dm_ref, rm_ref)
+
+    @pl.when(step == 1)
+    def _():
+        work(dt_ref, rt_ref)
+
+
+def head_back(info, grad_mine, grad_theirs, raw_mine, raw_theirs, cos_part, sin_part, gq, gk, heads):
+    cols, tok = grad_mine.shape
+    tile = min(512, tok)
+    mine = pl.BlockSpec((cols, tile), lambda s, i, info: (0, jnp.where(s == 0, i, tok // tile - 1)))
+    theirs = pl.BlockSpec((cols, tile), lambda s, i, info: (0, jnp.where(s == 0, 0, i)))
+    tab = lambda a: pl.BlockSpec((a.shape[0], tile), lambda s, i, info: (0, i))
+    const = lambda a: pl.BlockSpec(a.shape, lambda s, i, info: (0, 0))
+    return pl.pallas_call(
+        functools.partial(head_back_kernel, heads),
+        grid_spec=pltpu.PrefetchScalarGridSpec(
+            num_scalar_prefetch=1,
+            grid=(2, tok // tile),
+            in_specs=[
+                mine,
+                theirs,
+                mine,
+                theirs,
+                tab(cos_part),
+                tab(sin_part),
+                const(gq),
+                const(gk),
+            ],
+            out_specs=[
+                pl.BlockSpec(
+                    (1, tile, cols), lambda s, i, info: (jnp.bitwise_xor(info[2], s), i, 0)
+                ),
+                pl.BlockSpec((gq.shape[0], 128), lambda s, i, info: (0, 0)),
+            ],
+        ),
+        out_shape=[shape_of((2, tok, cols), BF16), shape_of((gq.shape[0], 128), F32)],
+        compiler_params=settings(2, 24),
+        cost_estimate=cost(0, 8 << 20),
+        name="head_back",
+    )(info, grad_mine, grad_theirs, raw_mine, raw_theirs, cos_part, sin_part, gq, gk)
+
+
+def load_rows(info, mine_ref, got_ref, rows, sems):
+    tok = mine_ref.shape[1]
+    ctx = info[2]
+    here = pl.multiple_of(ctx * tok, tok)
+    there = pl.multiple_of((1 - ctx) * tok, tok)
+    one = pltpu.make_async_copy(mine_ref, rows.at[:, pl.ds(here, tok)], sems.at[0])
+    two = pltpu.make_async_copy(got_ref, rows.at[:, pl.ds(there, tok)], sems.at[1])
+    one.start()
+    two.start()
+    one.wait()
+    two.wait()
+
+
+def keys_with_bias(keys, length):
+    hd, slots = keys.shape
+    pos = lax.broadcasted_iota(jnp.int32, (hd, slots), 1)
+    row = lax.broadcasted_iota(jnp.int32, (hd, slots), 0)
+    bias = jnp.where((row == 0) & (pos >= length), NEGATIVE, 0.0)
+    return jnp.concatenate([keys.astype(F32), bias], axis=0).T.astype(BF16)
+
+
+def query_with_one(pair):
+    one_row = jnp.where(lax.broadcasted_iota(jnp.int32, pair.shape, 0) == 0, 1.0, 0.0)
+    return jnp.concatenate([pair, one_row.astype(BF16)], axis=0)
+
+
+def causal(scores, width):
+    key_pos = lax.broadcasted_iota(jnp.int32, (width, width), 0)
+    query_pos = lax.broadcasted_iota(jnp.int32, (width, width), 1)
+    allowed = key_pos <= query_pos
+    return jnp.where(jnp.concatenate([allowed, allowed], axis=1), scores, NEGATIVE)
+
+
+def attn_fwd_kernel(
+    width, hd, info, mine_ref, got_ref, keep_ref, send_ref, lse_ref, rows, key_rows, sems
+):
+    head, block = pl.program_id(0), pl.program_id(1)
+    heads_k = pl.num_programs(0)
+    scale = hd**-0.5 * LOG2E
+    length = info[3]
+    key_at = pl.multiple_of(heads_k * 2 * hd + head * hd, hd)
+    value_at = pl.multiple_of(heads_k * 3 * hd + head * hd, hd)
+    query_at = pl.multiple_of(head * 2 * hd, 2 * hd)
+
+    @pl.when((head == 0) & (block == 0))
+    def _():
+        load_rows(info, mine_ref, got_ref, rows, sems)
+
+    @pl.when(block == 0)
+    def _():
+        key_rows[...] = keys_with_bias(rows[pl.ds(key_at, hd), :], length)
+
+    start = pl.multiple_of(block * width, width)
+    both = rows[pl.ds(query_at, 2 * hd), pl.ds(start, width)]
+    query = query_with_one(jnp.concatenate([both[:hd], both[hd:]], axis=1))
+
+    def tile(at, carried, diagonal):
+        out, total = carried
+        scores = dot(key_rows[pl.ds(at, width), :], query, 1, 0)
+        if diagonal:
+            scores = causal(scores, width)
+        probs = jnp.exp2(scores * scale)
+        total = total + jnp.sum(probs, axis=0, keepdims=True)
+        out = out + dot(rows[pl.ds(value_at, hd), pl.ds(at, width)], probs.astype(BF16), 1, 0)
+        return out, total
+
+    carried = (jnp.zeros((hd, 2 * width), F32), jnp.zeros((1, 2 * width), F32))
+    full = jnp.minimum(block, lax.div(length + width - 1, width))
+    carried = lax.fori_loop(
+        0, full, lambda j, c: tile(pl.multiple_of(j * width, width), c, False), carried
+    )
+    out, total = tile(start, carried, True)
+    out = out * (1.0 / total)
+    out = jnp.concatenate([out[:, :width], out[:, width:]], axis=0).T.astype(BF16)
+    here = block // 2 == info[2]
+
+    @pl.when(here)
+    def _():
+        keep_ref[...] = out
+
+    @pl.when(jnp.logical_not(here))
+    def _():
+        send_ref[...] = out
+
+    log_total = jnp.log2(total)
+    lse_ref[0, 0:1, :] = log_total[:, :width]
+    lse_ref[0, 1:2, :] = log_total[:, width:]
+
+
+def keep_block(i, info):
+    return jnp.clip(i - 2 * info[2], 0, 1)
+
+
+def send_block(i, info):
+    return jnp.clip(i - 2 * (1 - info[2]), 0, 1)
+
+
+def attn_fwd(info, mine, got, hd):
+    cols, tok = mine.shape
+    heads_k = cols // (4 * hd)
+    width = tok // 2
+    return pl.pallas_call(
+        functools.partial(attn_fwd_kernel, width, hd),
+        grid_spec=pltpu.PrefetchScalarGridSpec(
+            num_scalar_prefetch=1,
+            grid=(heads_k, 4),
+            in_specs=[ANY, ANY],
+            out_specs=[
+                pl.BlockSpec((width, 2 * hd), lambda h, i, info: (keep_block(i, info), h)),
+                pl.BlockSpec((width, 2 * hd), lambda h, i, info: (send_block(i, info), h)),
+                pl.BlockSpec((1, 2, width), lambda h, i, info: (h, 0, i)),
+            ],
+            scratch_shapes=[
+                pltpu.VMEM((cols, 2 * tok), BF16),
+                pltpu.VMEM((2 * tok, 2 * hd), BF16),
+                pltpu.SemaphoreType.DMA((2,)),
+            ],
+        ),
+        out_shape=[
+            shape_of((tok, heads_k * 2 * hd), BF16),
+            shape_of((tok, heads_k * 2 * hd), BF16),
+            shape_of((heads_k, 2, 2 * tok), F32),
+        ],
+        compiler_params=settings(2, 32),
+        cost_estimate=cost(heads_k * 2 * tok * 2 * tok * 256 * 4, 8 << 20),
+        name="attn_fwd",
+    )(info, mine, got)
+
+
+def attn_bwd_kernel(
+    width,
+    hd,
+    info,
+    mine_ref,
+    got_ref,
+    ok_ref,
+    os_ref,
+    gk_ref,
+    gs_ref,
+    lse_ref,
+    keep_ref,
+    send_ref,
+    rows,
+    key_rows,
+    value_rows,
+    key_sum,
+    value_sum,
+    sems,
+):
+    head, block = pl.program_id(0), pl.program_id(1)
+    heads_k = pl.num_programs(0)
+    scale = hd**-0.5
+    length = info[3]
+    ctx = info[2]
+    tok = keep_ref.shape[1]
+    key_at = pl.multiple_of(heads_k * 2 * hd + head * hd, hd)
+    value_at = pl.multiple_of(heads_k * 3 * hd + head * hd, hd)
+    query_at = pl.multiple_of(head * 2 * hd, 2 * hd)
+
+    @pl.when((head == 0) & (block == 0))
+    def _():
+        load_rows(info, mine_ref, got_ref, rows, sems)
+
+    @pl.when(block == 0)
+    def _():
+        key_rows[...] = keys_with_bias(rows[pl.ds(key_at, hd), :], length)
+        value_rows[...] = rows[pl.ds(value_at, hd), :].astype(F32).T.astype(BF16)
+        key_sum[...] = jnp.zeros_like(key_sum)
+        value_sum[...] = jnp.zeros_like(value_sum)
+
+    start = pl.multiple_of(block * width, width)
+    here = block // 2 == ctx
+
+    def store_query(value):
+        at = pl.ds(pl.multiple_of((block % 2) * width, width), width)
+
+        @pl.when(here)
+        def _():
+            keep_ref[pl.ds(query_at, 2 * hd), at] = value
+
+        @pl.when(jnp.logical_not(here))
+        def _():
+            send_ref[pl.ds(query_at, 2 * hd), at] = value
+
+    @pl.when(block * width < length)
+    def _():
+        both = rows[pl.ds(query_at, 2 * hd), pl.ds(start, width)]
+        pair = jnp.concatenate([both[:hd], both[hd:]], axis=1)
+        query = query_with_one(pair)
+        query_rows = pair.astype(F32).T.astype(BF16)
+        grad_wide = jnp.where(here, gk_ref[...].astype(F32), gs_ref[...].astype(F32))
+        out_wide = jnp.where(here, ok_ref[...].astype(F32), os_ref[...].astype(F32))
+        grad_rows = jnp.concatenate([grad_wide[:, :hd], grad_wide[:, hd:]], axis=0).astype(BF16)
+        grad_t = grad_wide.T
+        prod = (grad_wide * out_wide).T
+        grad = jnp.concatenate([grad_t[:hd], grad_t[hd:]], axis=1).astype(BF16)
+        delta = jnp.concatenate(
+            [
+                jnp.sum(prod[:hd], axis=0, keepdims=True),
+                jnp.sum(prod[hd:], axis=0, keepdims=True),
+            ],
+            axis=1,
+        )
+        lse = jnp.concatenate([lse_ref[0, 0:1, :], lse_ref[0, 1:2, :]], axis=1)
+
+        def tile(at, query_sum, diagonal):
+            scores = dot(key_rows[pl.ds(at, width), :], query, 1, 0)
+            if diagonal:
+                scores = causal(scores, width)
+            probs = jnp.exp2(scores * (scale * LOG2E) - lse)
+            grad_probs = dot(value_rows[pl.ds(at, width), :], grad, 1, 0)
+            grad_scores = (probs * (grad_probs - delta)).astype(BF16)
+            value_sum[pl.ds(at, width), :] += dot(probs.astype(BF16), grad_rows, 1, 0)
+            key_sum[pl.ds(at, width), :] += dot(grad_scores, query_rows, 1, 0)
+            return query_sum + dot(rows[pl.ds(key_at, hd), pl.ds(at, width)], grad_scores, 1, 0)
+
+        query_sum = lax.fori_loop(
+            0,
+            block,
+            lambda j, s: tile(pl.multiple_of(j * width, width), s, False),
+            jnp.zeros((hd, 2 * width), F32),
+        )
+        query_sum = tile(start, query_sum, True) * scale
+        store_query(
+            jnp.concatenate([query_sum[:, :width], query_sum[:, width:]], axis=0).astype(BF16)
+        )
+
+    @pl.when(block * width >= length)
+    def _():
+        store_query(jnp.zeros((2 * hd, width), BF16))
+
+    @pl.when(block == 3)
+    def _():
+        for at, total in ((key_at, key_sum[...] * scale), (value_at, value_sum[...])):
+            total = total.T.astype(BF16)
+            left, right = total[:, :tok], total[:, tok:]
+
+            @pl.when(ctx == 0)
+            def _():
+                keep_ref[pl.ds(at, hd), :] = left
+                send_ref[pl.ds(at, hd), :] = right
+
+            @pl.when(ctx == 1)
+            def _():
+                keep_ref[pl.ds(at, hd), :] = right
+                send_ref[pl.ds(at, hd), :] = left
+
+
+def attn_bwd(info, mine, got, out_keep, out_send, grad_keep, grad_send, lse, hd):
+    cols, tok = mine.shape
+    heads_k = cols // (4 * hd)
+    width = tok // 2
+    keep = pl.BlockSpec((width, 2 * hd), lambda h, i, info: (keep_block(i, info), h))
+    send = pl.BlockSpec((width, 2 * hd), lambda h, i, info: (send_block(i, info), h))
+    full = pl.BlockSpec((cols, tok), lambda h, i, info: (0, 0))
+    return pl.pallas_call(
+        functools.partial(attn_bwd_kernel, width, hd),
+        grid_spec=pltpu.PrefetchScalarGridSpec(
+            num_scalar_prefetch=1,
+            grid=(heads_k, 4),
+            in_specs=[
+                ANY,
+                ANY,
+                keep,
+                send,
+                keep,
+                send,
+                pl.BlockSpec((1, 2, width), lambda h, i, info: (h, 0, i)),
+            ],
+            out_specs=[full, full],
+            scratch_shapes=[
+                pltpu.VMEM((cols, 2 * tok), BF16),
+                pltpu.VMEM((2 * tok, 2 * hd), BF16),
+                pltpu.VMEM((2 * tok, hd), BF16),
+                pltpu.VMEM((2 * tok, hd), F32),
+                pltpu.VMEM((2 * tok, hd), F32),
+                pltpu.SemaphoreType.DMA((2,)),
+            ],
+        ),
+        out_shape=[shape_of((cols, tok), BF16), shape_of((cols, tok), BF16)],
+        compiler_params=settings(2, 40),
+        cost_estimate=cost(heads_k * 5 * tok * 2 * tok * 256 * 4, 12 << 20),
+        name="attn_bwd",
+    )(info, mine, got, out_keep, out_send, grad_keep, grad_send, lse)
+
+
+def out_proj_kernel(info, x_ref, a0, a1, b0, b1, w_ref, gain_ref, r_ref, n_ref, nt_ref, att_ref):
+    ctx = info[2]
+    total = x_ref[...].astype(F32)
+    for j, ref, side in ((0, a0, ctx), (1, a1, ctx), (0, b0, 1 - ctx), (1, b1, 1 - ctx)):
+        block = 2 * side + j
+        part = ref[...]
+        att_ref[block] = part
+        total = total + dot(part, w_ref[block], 1, 1)
+    rho = lax.rsqrt(jnp.mean(total * total, axis=-1, keepdims=True) + EPS)
+    normed = total * rho * gain_ref[...]
+    r_ref[...] = total
+    n_ref[...] = normed.astype(BF16)
+    nt_ref[...] = normed.T.astype(BF16)
+
+
+def out_proj(info, x, mine, theirs, w_out, gain, tile):
+    tok, width = x.shape
+    feats = w_out.shape[2]
+    rows_of = lambda n: pl.BlockSpec((tile, n), lambda i, info: (i, 0))
+    return pl.pallas_call(
+        out_proj_kernel,
+        grid_spec=pltpu.PrefetchScalarGridSpec(
+            num_scalar_prefetch=1,
+            grid=(tok // tile,),
+            in_specs=[rows_of(width)]
+            + [rows_of(feats)] * 4
+            + [whole(w_out.shape), pl.BlockSpec((1, width), lambda i, info: (0, 0))],
+            out_specs=[
+                rows_of(width),
+                rows_of(width),
+                pl.BlockSpec((width, tile), lambda i, info: (0, i)),
+                pl.BlockSpec((4, tile, feats), lambda i, info: (0, i, 0)),
+            ],
+        ),
+        out_shape=[
+            shape_of((tok, width), F32),
+            shape_of((tok, width), BF16),
+            shape_of((width, tok), BF16),
+            shape_of((4, tok, feats), BF16),
+        ],
+        compiler_params=settings(1, 32),
+        cost_estimate=cost(2 * tok * width * 4 * feats, 16 << 20),
+        name="out_proj",
+    )(info, x, *mine, *theirs, w_out, gain)
+
+
+def norm_two_back_kernel(
+    info, g_ref, r_ref, gr_ref, gain_ref, w_ref, gres_ref, gat_ref, a0, a1, b0, b1, gg_ref
+):
+    ctx = info[2]
+    grad, resid = g_ref[...], r_ref[...]
+    rho = lax.rsqrt(jnp.mean(resid * resid, axis=-1, keepdims=True) + EPS)
+    unit = resid * rho
+    scaled = grad * gain_ref[...]
+    back = rho * (scaled - unit * jnp.mean(scaled * unit, axis=-1, keepdims=True))
+    total = gr_ref[...] + back
+    gres_ref[...] = total
+    low = total.astype(BF16)
+    gat_ref[...] = total.T.astype(BF16)
+
+    @pl.when(pl.program_id(0) == 0)
+    def _():
+        gg_ref[...] = jnp.zeros_like(gg_ref)
+
+    gg_ref[...] += jnp.sum(grad * unit, axis=0, keepdims=True)
+    for j, ref, side in ((0, a0, ctx), (1, a1, ctx), (0, b0, 1 - ctx), (1, b1, 1 - ctx)):
+        ref[...] = dot(low, w_ref[2 * side + j], 1, 0).astype(BF16)
+
+
+def norm_two_back(info, grad, resid, grad_result, gain, w_out, tile):
+    tok, width = grad.shape
+    feats = w_out.shape[2]
+    rows_of = lambda n: pl.BlockSpec((tile, n), lambda i, info: (i, 0))
+    row = pl.BlockSpec((1, width), lambda i, info: (0, 0))
+    return pl.pallas_call(
+        norm_two_back_kernel,
+        grid_spec=pltpu.PrefetchScalarGridSpec(
+            num_scalar_prefetch=1,
+            grid=(tok // tile,),
+            in_specs=[rows_of(width)] * 3 + [row, whole(w_out.shape)],
+            out_specs=[rows_of(width), pl.BlockSpec((width, tile), lambda i, info: (0, i))]
+            + [rows_of(feats)] * 4
+            + [row],
+        ),
+        out_shape=[shape_of((tok, width), F32), shape_of((width, tok), BF16)]
+        + [shape_of((tok, feats), BF16)] * 4
+        + [shape_of((1, width), F32)],
+        compiler_params=settings(1, 32),
+        cost_estimate=cost(2 * tok * width * 4 * feats, 24 << 20),
+        name="norm_two_back",
+    )(info, grad, resid, grad_result, gain, w_out)
+
+
+def norm_one_back_kernel(info, p0, p1, w_ref, x_ref, gres_ref, gain_ref, out_ref, gg_ref):
+    quarter = x_ref.shape[1] // 4
+    grad = dot(p0[0], w_ref[0], 1, 1)
+    grad = grad + dot(p1[0], w_ref[1], 1, 1)
+    grad = grad + dot(p0[1], w_ref[2], 1, 1)
+    grad = grad + dot(p1[1], w_ref[3], 1, 1)
+    x = x_ref[...].astype(F32)
+    rho = lax.rsqrt(jnp.mean(x * x, axis=-1, keepdims=True) + EPS)
+    unit = x * rho
+    scaled = grad * gain_ref[...]
+    back = rho * (scaled - unit * jnp.mean(scaled * unit, axis=-1, keepdims=True))
+    total = (gres_ref[...] + back).astype(BF16)
+    for p, mask in enumerate(MASKS):
+        at = pl.multiple_of(jnp.bitwise_xor(info[1], mask) * quarter, quarter)
+        out_ref[:, pl.ds(at, quarter)] = total[:, p * quarter : (p + 1) * quarter]
+
+    @pl.when(pl.program_id(0) == 0)
+    def _():
+        gg_ref[...] = jnp.zeros_like(gg_ref)
+
+    gg_ref[...] += jnp.sum(grad * unit, axis=0, keepdims=True)
+
+
+def norm_one_back(info, pairs, w_proj, x, grad_resid, gain, tile):
+    tok, width = x.shape
+    cols = w_proj.shape[2]
+    rows_of = lambda n: pl.BlockSpec((tile, n), lambda i, info: (i, 0))
+    pair = pl.BlockSpec((2, tile, cols), lambda i, info: (0, i, 0))
+    row = pl.BlockSpec((1, width), lambda i, info: (0, 0))
+    return pl.pallas_call(
+        norm_one_back_kernel,
+        grid_spec=pltpu.PrefetchScalarGridSpec(
+            num_scalar_prefetch=1,
+            grid=(tok // tile,),
+            in_specs=[pair, pair, whole(w_proj.shape), rows_of(width), rows_of(width), row],
+            out_specs=[rows_of(width), row],
+        ),
+        out_shape=[shape_of((tok, width), BF16), shape_of((1, width), F32)],
+        compiler_params=settings(1, 32),
+        cost_estimate=cost(2 * tok * width * 4 * cols, 18 << 20),
+        name="norm_one_back",
+    )(info, *pairs, w_proj, x, grad_resid, gain)
+
+
+def weight_copies(pieces, gate_up, down, gate_up_sem, down_sem):
+    own, far, last, own2, far2, last2 = pieces
+    rows, cols = own.shape
+    chunk = cols // 3
+    third = chunk // 3
+    wide, thin = [], []
+    for p, (ref, first) in enumerate(((own, 0), (far, 0), (own2, 0), (far2, 0))):
+        for j in range(3):
+            src = ref
+            at = j * chunk
+            if p % 2 == 1 and j == 2:
+                src, at = (last, last2)[p // 2], 0
+            block = pl.ds(p * rows, rows)
+            wide.append(
+                pltpu.make_async_copy(
+                    src.at[:, pl.ds(at, 2 * third)],
+                    gate_up.at[block, pl.ds(j * 2 * third, 2 * third)],
+                    gate_up_sem,
+                )
+            )
+            thin.append(
+                pltpu.make_async_copy(
+                    src.at[:, pl.ds(at + 2 * third, third)],
+                    down.at[block, pl.ds(j * third, third)],
+                    down_sem,
+                )
+            )
+    return wide, thin
+
+
+def split_act(act):
+    third = act.shape[1] // 6
+    part = lambda j: act[:, j * third : (j + 1) * third]
+    return [(part(0), part(1)), (part(2), part(3)), (part(4), part(5))]
+
+
+def ffn_fwd_kernel(
+    tile,
+    info,
+    scale,
+    x_ref,
+    resid_ref,
+    teach_ref,
+    *rest,
+):
+    pieces = [rest[6 * s : 6 * s + 6] for s in range(4)]
+    act_ref, hid_ref, out_ref, gres_ref, low_ref, lowt_ref, sq_ref = rest[24:31]
+    gate_up, down, total, sems = rest[31:]
+    step, part = pl.program_id(0), pl.program_id(1)
+    width = x_ref.shape[1]
+    quarter = width // 4
+    third = down.shape[2] // 3
+
+    def copies(s):
+        return weight_copies(pieces[s], gate_up.at[s], down.at[s], sems.at[s, 0], sems.at[s, 1])
+
+    @pl.when((step == 0) & (part == 0))
+    def _():
+        for s in range(4):
+            wide, thin = copies(s)
+            for copy in wide + thin:
+                copy.start()
+
+    for s in range(4):
+
+        @pl.when((step == s) & (part == 0))
+        def _():
+            pltpu.make_async_copy(gate_up.at[s], gate_up.at[s], sems.at[s, 0]).wait()
+            pltpu.make_async_copy(down.at[s], down.at[s], sems.at[s, 1]).wait()
+
+    rows = pl.ds(pl.multiple_of(part * tile, tile), tile)
+    act = dot(x_ref[rows, :], gate_up[step], 1, 0)
+    for j, (gate, upper) in enumerate(split_act(act)):
+        hid_ref[0, :, j * third : (j + 1) * third] = (gate * sigmoid(gate) * upper).astype(BF16)
+    act_ref[0] = act.astype(BF16)
+    grown = dot(hid_ref[0], down[step], 1, 1)
+
+    @pl.when(step == 0)
+    def _():
+        total[rows, :] = resid_ref[rows, :] + grown
+
+    @pl.when((step > 0) & (step < 3))
+    def _():
+        total[rows, :] += grown
+
+    @pl.when(step == 3)
+    def _():
+        result = total[rows, :] + grown
+        total[rows, :] = result
+        tok = x_ref.shape[0]
+        slot = info[2] * tok + part * tile + lax.broadcasted_iota(jnp.int32, (tile, 1), 0)
+        valid = jnp.where(slot < info[3], 1.0, 0.0)
+        square = jnp.zeros((tile, quarter), F32)
+        for p, mask in enumerate(MASKS):
+            at = pl.multiple_of(jnp.bitwise_xor(info[1], mask) * quarter, quarter)
+            cols = slice(p * quarter, (p + 1) * quarter)
+            value = result[:, cols]
+            out_ref[:, pl.ds(at, quarter)] = value.astype(BF16)
+            error = valid * (value - teach_ref[0, :, pl.ds(at, quarter)].astype(F32))
+            square = square + error * error
+            grad = error * scale[0]
+            gres_ref[:, cols] = grad
+            low_ref[:, cols] = grad.astype(BF16)
+            lowt_ref[cols, :] = grad.T.astype(BF16)
+
+        @pl.when(part == 0)
+        def _():
+            sq_ref[...] = jnp.zeros_like(sq_ref)
+
+        sq_ref[...] += jnp.sum(square, axis=0, keepdims=True)
+
+
+def ffn_fwd(info, scale, x, resid, teacher, pieces, tile):
+    tok, width = x.shape
+    units = pieces[0][0].shape[1] // 3
+    last = lambda s, i: jnp.where(s == 3, i, 0)
+    tiles = lambda n: pl.BlockSpec((tile, n), lambda s, i, info: (last(s, i), 0))
+    return pl.pallas_call(
+        functools.partial(ffn_fwd_kernel, tile),
+        grid_spec=pltpu.PrefetchScalarGridSpec(
+            num_scalar_prefetch=1,
+            grid=(4, tok // tile),
+            in_specs=[
+                SMEM,
+                whole((tok, width)),
+                whole((tok, width)),
+                pl.BlockSpec((1, tile, width), lambda s, i, info: (info[0], last(s, i), 0)),
+            ]
+            + [ANY] * 24,
+            out_specs=[
+                pl.BlockSpec((1, tile, 2 * units), lambda s, i, info: (s, i, 0)),
+                pl.BlockSpec((1, tile, units), lambda s, i, info: (s, i, 0)),
+                tiles(width),
+                tiles(width),
+                tiles(width),
+                pl.BlockSpec((width, tile), lambda s, i, info: (0, last(s, i))),
+                pl.BlockSpec((1, width // 4), lambda s, i, info: (0, 0)),
+            ],
+            scratch_shapes=[
+                pltpu.VMEM((4, width, 2 * units), BF16),
+                pltpu.VMEM((4, width, units), BF16),
+                pltpu.VMEM((tok, width), F32),
+                pltpu.SemaphoreType.DMA((4, 2)),
+            ],
+        ),
+        out_shape=[
+            shape_of((4, tok, 2 * units), BF16),
+            shape_of((4, tok, units), BF16),
+            shape_of((tok, width), BF16),
+            shape_of((tok, width), F32),
+            shape_of((tok, width), BF16),
+            shape_of((width, tok), BF16),
+            shape_of((1, width // 4), F32),
+        ],
+        compiler_params=settings(2, 61),
+        cost_estimate=cost(2 * tok * width * units * 12, 70 << 20),
+        name="ffn_fwd",
+    )(info, scale, x, resid, teacher, *[ref for group in pieces for ref in group])
+
+
+def ffn_bwd_kernel(steps, first, low_ref, act_ref, hid_ref, xt_ref, lowt_ref, *rest):
+    pieces = rest[:6]
+    rest = rest[6:]
+    if not first:
+        in_ref, rest = rest[0], rest[1:]
+    out_ref, keep_ref, send_ref, gate_up, down, dact_all, hid_all, sems = rest
+    step = pl.program_id(0)
+    units = down.shape[1]
+    third = units // 3
+    tile = low_ref.shape[0]
+
+    @pl.when(step == 0)
+    def _():
+        wide, thin = weight_copies(pieces, gate_up, down, sems.at[0], sems.at[1])
+        for copy in thin + wide:
+            copy.start()
+        pltpu.make_async_copy(down, down, sems.at[1]).wait()
+
+    @pl.when(step < steps)
+    def _():
+        rows = pl.ds(pl.multiple_of(step * tile, tile), tile)
+        grad_hidden = dot(low_ref[...], down[...], 1, 0)
+        for j, (gate, upper) in enumerate(split_act(act_ref[0])):
+            grad = grad_hidden[:, j * third : (j + 1) * third]
+            gate, upper = gate.astype(F32), upper.astype(F32)
+            sig = sigmoid(gate)
+            silu = gate * sig
+            at = 2 * j * third
+            dact_all[rows, at : at + third] = (
+                grad * upper * (sig + silu - silu * sig)
+            ).astype(BF16)
+            dact_all[rows, at + third : at + 2 * third] = (grad * silu).astype(BF16)
+        hid_all[rows, :] = hid_ref[0]
+
+        @pl.when(step == 0)
+        def _():
+            pltpu.make_async_copy(gate_up, gate_up, sems.at[0]).wait()
+
+        grown = dot(dact_all[rows, :], gate_up[...], 1, 1)
+        out_ref[...] = grown if first else in_ref[...] + grown
+
+    def weight_rows(target):
+        target[:, : 2 * units] = dot(xt_ref[...], dact_all[...], 1, 0).astype(BF16)
+        target[:, 2 * units :] = dot(lowt_ref[...], hid_all[...], 1, 0).astype(BF16)
+
+    @pl.when((step >= steps) & (step < steps + 2))
+    def _():
+        weight_rows(send_ref)
+
+    @pl.when(step >= steps + 2)
+    def _():
+        weight_rows(keep_ref)
+
+
+def ffn_bwd(block, low, acts, hiddens, pieces, total, xt, lowt, tile):
+    tok, width = low.shape
+    units = hiddens.shape[2]
+    steps = tok // tile
+    quarter = width // 4
+    first = total is None
+    clip = lambda i: jnp.minimum(i, steps - 1)
+    rows_of = lambda n: pl.BlockSpec((tile, n), lambda i: (clip(i), 0))
+    slab = lambda n: pl.BlockSpec((1, tile, n), lambda i: (block, clip(i), 0))
+    feature = lambda i: (jnp.where(i < steps + 2, jnp.maximum(i - steps, 0) + 2, i - steps - 2), 0)
+    return pl.pallas_call(
+        functools.partial(ffn_bwd_kernel, steps, first),
+        grid=(steps + 4,),
+        in_specs=[
+            rows_of(width),
+            slab(2 * units),
+            slab(units),
+            pl.BlockSpec((quarter, tok), feature),
+            pl.BlockSpec((quarter, tok), feature),
+        ]
+        + [ANY] * 6
+        + ([] if first else [rows_of(width)]),
+        out_specs=[
+            rows_of(width),
+            pl.BlockSpec((quarter, 3 * units), lambda i: (jnp.maximum(i - steps - 2, 0), 0)),
+            pl.BlockSpec((quarter, 3 * units), lambda i: (jnp.clip(i - steps, 0, 1), 0)),
+        ],
+        out_shape=[
+            shape_of((tok, width), F32),
+            shape_of((width // 2, 3 * units), BF16),
+            shape_of((width // 2, 3 * units), BF16),
+        ],
+        scratch_shapes=[
+            pltpu.VMEM((width, 2 * units), BF16),
+            pltpu.VMEM((width, units), BF16),
+            pltpu.VMEM((tok, 2 * units), BF16),
+            pltpu.VMEM((tok, units), BF16),
+            pltpu.SemaphoreType.DMA((2,)),
+        ],
+        input_output_aliases={} if first else {11: 0},
+        compiler_params=settings(1, 56),
+        cost_estimate=cost(2 * tok * width * units * 6, 32 << 20),
+        name="ffn_bwd",
+    )(low, acts, hiddens, xt, lowt, *pieces, *([] if first else [total]))
+
+
+def after(value, *others):
+    return lax.optimization_barrier((value,) + others)[0]
+
+
+def z_gather(block):
+    one = lax.ppermute(block, "tp", Z_UP)
+    three = lax.ppermute(block, "tp", Z_DOWN)
+    two = lax.ppermute(one, "tp", Z_UP)
+    return [block, one, two, three]
+
+
+def add(left, right):
+    return left.astype(F32) + right.astype(F32)
+
+
+def add_low(left, right):
+    return add(left, right).astype(BF16)
+
+
+def turn_chunks(block):
+    wide = block.shape[1] * 2 // 9
+    thin = wide // 2
+    starts = [(2 * wide, wide), (wide, wide), (0, wide)]
+    starts += [(3 * wide + 2 * thin, thin), (3 * wide + thin, thin), (3 * wide, thin)]
+    return jnp.concatenate([block[:, a : a + n] for a, n in starts], axis=1)
+
+
+def z_reduce(parts):
+    two = add_low(parts[1], lax.ppermute(parts[2], "tp", Z_DOWN))
+    total = add(parts[0], lax.ppermute(two, "tp", Z_DOWN))
+    return total + lax.ppermute(parts[3], "tp", Z_UP).astype(F32)
+
+
+def per_device_rows(
+    tokens,
+    teacher,
+    lengths,
+    attn_gain,
+    q_weight,
+    k_weight,
+    v_weight,
+    q_gain,
+    k_gain,
+    o_weight,
+    ffn_gain,
+    gate_weight,
+    up_weight,
+    down_weight,
+):
+    z = lax.axis_index("tp")
+    ctx = lax.axis_index("ctx")
+    fsdp = lax.axis_index("fsdp")
+    rows_dev, tok, width = tokens.shape
+    quarter = width // 4
+    hd = q_gain.shape[0] * 4
+    q_cols, k_cols = q_weight.shape[1], k_weight.shape[1]
+    proj = q_cols + 2 * k_cols
+    heads = (q_cols // hd, k_cols // hd)
+    units = gate_weight.shape[1]
+    slots = rows_dev * 4 * tok * 2
+
+    def x_swap(v):
+        return lax.ppermute(v, "fsdp", X_SWAP)
+
+    def core_swap(v):
+        return lax.ppermute(v, "fsdp", CORE_SWAP)
+
+    def y_swap(v):
+        return lax.ppermute(v, "ctx", Y_SWAP)
+
+    length = lax.dynamic_slice_in_dim(lengths, z, 1, 0)
+    info = jnp.concatenate([jnp.stack([z, fsdp, ctx]).astype(jnp.int32), length])
+
+    w_attn, w_ffn = pack(
+        info, q_weight, k_weight, v_weight, o_weight, gate_weight, up_weight, down_weight
+    )
+    count_here = jnp.sum(lengths).astype(F32)[None]
+    vector = jnp.concatenate([attn_gain, ffn_gain, q_gain, k_gain]).astype(F32)
+    vector = jnp.concatenate([vector, count_here, jnp.zeros((640 - 545,), F32)])[None]
+    vector = jnp.concatenate([vector, x_swap(vector)], axis=0)
+    vector = jnp.concatenate([vector, core_swap(vector)], axis=0)
+    gain_one = vector[:, :quarter].reshape(1, width)
+    gain_two = vector[:, quarter : 2 * quarter].reshape(1, width)
+    total_count = jnp.sum(vector[:, 544])
+    head_gains = vector[:, 2 * quarter : 544]
+    head_gains = jnp.where(fsdp // 2 == 0, head_gains, head_gains[jnp.array([1, 0, 3, 2])])
+    head_gains = jnp.where(fsdp % 2 == 0, head_gains, head_gains[jnp.array([2, 3, 0, 1])])
+    head_gains = head_gains[jnp.array([0, 2, 1, 3])]
+    gain_q = head_gains[:, : hd // 4].reshape(hd, 1)
+    gain_k = head_gains[:, hd // 4 :].reshape(hd, 1)
+
+    attn_blocks = z_gather(w_attn)
+    attn_pieces = []
+    for block in attn_blocks:
+        far = x_swap(block)
+        attn_pieces.append([block, far, core_swap(block), core_swap(far)])
+    w_proj = jnp.concatenate([p[:, :proj] for b in attn_pieces for p in b], axis=0)
+    w_proj = w_proj.reshape(4, width, proj)
+    w_out = jnp.concatenate([p[:, proj:] for b in attn_pieces for p in b], axis=0)
+    w_out = w_out.reshape(4, width, q_cols)
+
+    chunk = units
+    ffn_blocks = z_gather(after(w_ffn, attn_blocks[2]))
+    ffn_pieces = []
+    for block in ffn_blocks:
+        block = after(block, attn_pieces[2][1]) if block is ffn_blocks[0] else block
+        far = x_swap(block[:, : 2 * chunk])
+        last = y_swap(far[:, :chunk])
+        ffn_pieces.append(
+            [block, far, last, core_swap(block), core_swap(far), core_swap(last)]
+        )
+
+    x_in, normed_one_t = norm_one(info, tokens, gain_one, 256)
+    pos = (ctx * tok + jnp.arange(tok, dtype=jnp.int32)).astype(F32)
+    frequency = THETA ** (-(2.0 * jnp.arange(hd // 2, dtype=F32)) / hd)
+    angles = frequency[:, None] * pos[None, :]
+    tables = (jnp.cos(angles), jnp.sin(angles), gain_q, gain_k)
+
+    def make(block):
+        return project(info, w_proj, normed_one_t, *tables, heads, block)
+
+    theirs = [make(lambda s: 2 * (1 - s[2])), make(lambda s: 2 * (1 - s[2]) + 1)]
+    got = [y_swap(theirs[0][0]), y_swap(theirs[1][0])]
+    mine = [make(lambda s: 2 * s[2]), make(lambda s: 2 * s[2] + 1)]
+
+    outs = [attn_fwd(info, mine[j][0], got[j], hd) for j in range(2)]
+    arrived = [y_swap(outs[j][1]) for j in range(2)]
+    resid, normed_two, normed_two_t, attended = out_proj(
+        info, x_in, [outs[0][0], outs[1][0]], arrived, w_out, gain_two, 256
+    )
+
+    order = (0, 1, 3, 2)
+    scale = (slots / total_count)[None]
+    acts, hiddens, result_low, grad_result, grad_low, grad_low_t, square = ffn_fwd(
+        info, scale, normed_two, resid, teacher, [ffn_pieces[k] for k in order], 256
+    )
+
+    def spread(block, dtype):
+        out = jnp.zeros((rows_dev, tok, width), dtype)
+        parts = z_gather(block)
+        for k in (0, 1, 3, 2):
+            part = parts[k].astype(dtype)[None]
+            out = lax.dynamic_update_slice(out, part, (lax.rem(z - k + 4, 4), 0, 0))
+        return out
+
+    output = spread(result_low, BF16)
+
+    grad_two = None
+    keeps, sends = [None] * 4, [None] * 4
+    for k in (2, 1, 3, 0):
+        grad_two, keeps[k], sends[k] = ffn_bwd(
+            order.index(k),
+            grad_low,
+            acts,
+            hiddens,
+            ffn_pieces[k],
+            grad_two,
+            normed_two_t,
+            grad_low_t,
+            256,
+        )
+
+    def halves(v):
+        half = v.shape[0] // 2
+        return (
+            lax.dynamic_slice_in_dim(v, ctx * half, half, 0),
+            lax.dynamic_slice_in_dim(v, half - ctx * half, half, 0),
+        )
+
+    def core_sum(keep, send):
+        came = core_swap(send)
+        return add_low(keep[:quarter], came[:quarter]), add_low(keep[quarter:], came[quarter:])
+
+    def plane_sum(own, far, x_first, turn):
+        if x_first:
+            own = add_low(own, x_swap(far))
+            here, there = halves(own)
+            return add_low(here, turn(y_swap(there)))
+        here, there = halves(own)
+        far_here, far_there = halves(far)
+        came = turn(y_swap(jnp.concatenate([there, far_there], axis=0)))
+        half = quarter // 2
+        return add_low(
+            add_low(here, came[:half]), x_swap(add_low(far_here, came[half:]))
+        )
+
+    def finish(parts, turn):
+        own = z_reduce(parts)
+        other = turn(y_swap(own))
+        return jnp.concatenate(
+            [jnp.where(ctx == 0, own, other), jnp.where(ctx == 0, other, own)], axis=0
+        )
+
+    ffn_parts = [
+        plane_sum(*core_sum(keeps[k], sends[k]), k in (1, 2), turn_chunks) for k in range(4)
+    ]
+
+    grad_resid, grad_attn_t, a0, a1, b0, b1, gain_two_sum = norm_two_back(
+        info, grad_two, resid, grad_result, gain_two, w_out, 256
+    )
+
+    grad_got = [y_swap(b0), y_swap(b1)]
+    grads = [
+        attn_bwd(
+            info,
+            mine[j][0],
+            got[j],
+            outs[j][0],
+            outs[j][1],
+            (a0, a1)[j],
+            grad_got[j],
+            outs[j][2],
+            hd,
+        )
+        for j in range(2)
+    ]
+    back = [
+        head_back(
+            info, grads[j][0], y_swap(grads[j][1]), mine[j][1], theirs[j][1], *tables, heads
+        )
+        for j in range(2)
+    ]
+    tokens_low, gain_one_sum = norm_one_back(
+        info, [back[0][0], back[1][0]], w_proj, x_in, grad_resid, gain_one, 256
+    )
+    tokens_grad = spread(tokens_low, F32)
+
+    attn_parts = []
+    for k in range(4):
+        part = jnp.concatenate(
+            [
+                dot(normed_one_t, back[k % 2][0][k // 2], 1, 0).astype(BF16),
+                dot(grad_attn_t, attended[k], 1, 0).astype(BF16),
+            ],
+            axis=1,
+        )
+        own, far = core_sum(part[: width // 2], part[width // 2 :])
+        attn_parts.append(plane_sum(own, far, k in (1, 2), lambda v: v))
+
+    ffn_grad = finish(ffn_parts, turn_chunks)
+    attn_grad = finish(attn_parts, lambda v: v)
+
+    def total(v):
+        for axis, pairs in (("fsdp", CORE_SWAP), ("fsdp", X_SWAP), ("ctx", Y_SWAP)):
+            v = v + lax.ppermute(v, axis, pairs)
+        for pairs in (Z_NEAR, Z_FAR):
+            v = v + lax.ppermute(v, "tp", pairs)
+        return v
+
+    def natural(v):
+        v = v.reshape(4, quarter)[jnp.array([0, 2, 1, 3])]
+        v = jnp.where(fsdp % 2 == 0, v, v[jnp.array([1, 0, 3, 2])])
+        return jnp.where(fsdp // 2 == 0, v, v[jnp.array([2, 3, 0, 1])]).reshape(1, width)
+
+    gain_heads = back[0][1] + back[1][1]
+    sums = total(
+        jnp.concatenate(
+            [
+                natural(gain_one_sum),
+                natural(gain_two_sum),
+                gain_heads[:, 0].reshape(1, hd),
+                gain_heads[:, 1].reshape(1, hd),
+                jnp.sum(square).reshape(1, 1),
+                jnp.zeros((1, 127), F32),
+            ],
+            axis=1,
+        )
+    )[0]
+    teacher_loss = sums[2 * width + 2 * hd] / (total_count * width)
+
+    def own_part(at, size):
+        return lax.dynamic_slice_in_dim(sums, at + fsdp * (size // 4), size // 4, 0)
+
+    third = units // 3
+
+    def columns(first):
+        starts = [first(j) for j in range(3)]
+        parts = [ffn_grad[:, s : s + third] for s in starts]
+        return jnp.concatenate(
+            [jnp.where(ctx == 0, parts[0], parts[2]), parts[1], jnp.where(ctx == 0, parts[2], parts[0])],
+            axis=1,
+        )
+
+    return (
+        output,
+        teacher_loss,
+        tokens_grad,
+        own_part(0, width),
+        attn_grad[:, :q_cols],
+        attn_grad[:, q_cols : q_cols + k_cols],
+        attn_grad[:, q_cols + k_cols : proj],
+        own_part(2 * width, hd),
+        own_part(2 * width + hd, hd),
+        attn_grad[:, proj:].T,
+        own_part(width, width),
+        columns(lambda j: 2 * j * third),
+        columns(lambda j: (2 * j + 1) * third),
+        columns(lambda j: 2 * units + j * third).T,
+    )
+
+
 def solution(mesh):
     return jax.shard_map(
-        per_device,
+        per_device_rows if fits(mesh) else per_device_any,
         mesh=mesh,
         in_specs=(
             P("fsdp", "ctx", None),

time: 3500 us -> 1070 us (0.31)
  waiting for transfers between devices: 2540 us -> 486 us
  matrix products: 529 us -> 13.6 us
  Pallas kernels: 0 us -> 280 us
  other arithmetic: 199 us -> 45.2 us
  blocking collectives: 121 us -> 0 us
  starting transfers between devices: 1.46 us -> 114 us
  local copies, waits for them, and re-layouts: 71.3 us -> 114 us
    psum x4 -> x0, waiting for transfers between devices: 2140 us -> none  [the longest x1 726 us: per_device(): attn_total = lax.psum(linear(attended, w_output), 'tp')]
    dot_general x39 -> x8, matrix products: 529 us -> 13.6 us  [dot(): lax.dot_general(left, right, (((left_dim,), (right_dim,)), ((), ())), pre...]
    ppermute x0 -> x91, waiting for transfers between devices: none -> 486 us  [the longest x22 163 us: y_swap(): return lax.ppermute(v, 'ctx', Y_SWAP)]
    reduce_scatter x9 -> x0, waiting for transfers between devices: 363 us -> none  [the longest x1 176 us: per_device(): lax.psum_scatter(grad_keys, 'ctx', scatter_dimension=1, tiled=True)]
    pallas_call x0 -> x20, Pallas kernels: none -> 280 us  [the longest x4 104 us: ffn_bwd(): pl.pallas_call(functools.partial(ffn_bwd_kernel, steps, first), grid=(ste...]
    ppermute x0 -> x91, starting transfers between devices: none -> 114 us  [the longest x29 26.1 us: core_swap(): return lax.ppermute(v, 'fsdp', CORE_SWAP)]
    reduce_sum x9 -> x3, other arithmetic: 79.8 us -> 3.23 us  [the longest x1 1.31 us: per_device_rows(): total_count = jnp.sum(vector[:, 544])]
    all_gather x12 -> x0, blocking collectives: 67.8 us -> none  [the longest x1 7.92 us: per_device(): lax.all_gather(o_weight, 'fsdp', axis=1, tiled=True)]
  transfers between devices with their start and end apart: 21 -> 91, of which waited for: 12 -> 37; matrix products, arithmetic and copies ran while one was open for 14% -> 12% of each run, Pallas kernels for 0% -> 12%
where the time goes in v2:
time: 1070 us; the launch traced here: 1060 us
  waiting for transfers between devices  486 us (45%)
  Pallas kernels  280 us (26%)
  local copies, waits for them, and re-layouts  114 us (11%)
  starting transfers between devices  114 us (11%)
  other arithmetic  45.2 us (4%)
  matrix products  13.6 us (1%)
    ppermute x22, waiting for transfers between devices, y_swap(): return lax.ppermute(v, 'ctx', Y_SWAP)  163 us
    ppermute x17, waiting for transfers between devices, x_swap(): return lax.ppermute(v, 'fsdp', X_SWAP)  124 us
    pallas_call x4, Pallas kernels, ffn_bwd(): pl.pallas_call(functools.partial(ffn_bwd_kernel, steps, first), grid=(ste...  104 us
    ppermute x4, waiting for transfers between devices, z_gather(): two = lax.ppermute(one, 'tp', Z_UP)  78 us
    unnamed x328, local copies, waits for them, and re-layouts  66.9 us
    ppermute x2, waiting for transfers between devices, z_reduce(): return total + lax.ppermute(parts[3], 'tp', Z_UP).astype(F32)  54.7 us
    pallas_call x2, Pallas kernels, attn_bwd(): pl.pallas_call(functools.partial(attn_bwd_kernel, width, hd), grid_spec=p...  49.8 us
    pallas_call x1, Pallas kernels, ffn_fwd(): pl.pallas_call(functools.partial(ffn_fwd_kernel, tile), grid_spec=pltpu.P...  46.9 us
  transfers between devices with their start and end apart: 91, of which 37 were waited for; matrix products, arithmetic and copies ran while one was open for 12% of the time, Pallas kernels for 12%

profile of v2, /device:TPU:0, one launch (start us, length us, event | category | flops | bytes accessed | tf_op | source)
XLA Modules:
  0.0 1060.5 jit_solution(2732694161238626522)
XLA Ops:
  78.8 17.0 %collective-permute-done.21.rest_1_ = bf16[256,2304]{1,0:T(8,128)(2,1)} collective-permute-done((bf16[256,2304]{1,0:T(8,128)(2,1)S(1)}, bf16[256,2304]{1,0:T(8,128)(2,1)}, u32[]{:S(2)}, u32[]{:S(2)}) %collective-permute-start.21) | collective-permute-done | bytes 1179680 | tf_op jit(solution)/shard_map/ppermute | solution.py:1360
  111.0 19.4 %collective-permute-done.32.rest_12_.rest_0_ = bf16[256,3456]{1,0:T(8,128)(2,1)} collective-permute-done((bf16[256,3456]{1,0:T(8,128)(2,1)}, bf16[256,3456]{1,0:T(8,128)(2,1)}, u32[]{:S(2)}, u32[]{:S(2)}) %collective-permute-start.32) | collective-permute-done | bytes 1769504 | tf_op jit(solution)/shard_map/ppermute | solution.py:1304
  133.8 16.1 %attn_fwd.3 = (bf16[1024,256]{1,0:T(8,128)(2,1)S(1)}, bf16[1024,256]{1,0:T(8,128)(2,1)S(1)}, f32[2,2,2048]{2,1,0:T(2,128)S(1)}) custom-call(s32[4]{0:T(128)S(1)} %pad_add_fusion.info, bf16[512,1024]{1,0:T(8,128)(2,1)S(1)} %get-tuple-element.80.mine_ref, bf16[512,1024]{1,0:T(8,128)(2,1)} %collective-permute-done.18.got_ref), custom_call_target="tpu_custom_call" | custom-call | flops 8589934592 | bytes 8388608 | tf_op jit(solution)/shard_map/attn_fwd/pallas_call | solution.py:716
  154.3 16.6 %attn_fwd.2 = (bf16[1024,256]{1,0:T(8,128)(2,1)S(1)}, bf16[1024,256]{1,0:T(8,128)(2,1)}, f32[2,2,2048]{2,1,0:T(2,128)S(1)}) custom-call(s32[4]{0:T(128)S(1)} %pad_add_fusion.info, bf16[512,1024]{1,0:T(8,128)(2,1)S(1)} %get-tuple-element.77.mine_ref, bf16[512,1024]{1,0:T(8,128)(2,1)} %collective-permute-done.17.got_ref), custom_call_target="tpu_custom_call" | custom-call | flops 8589934592 | bytes 8388608 | tf_op jit(solution)/shard_map/attn_fwd/pallas_call | solution.py:716
  186.5 17.8 %collective-permute-done.33.rest_13_.rest_1_ = bf16[256,2304]{1,0:T(8,128)(2,1)} collective-permute-done((bf16[256,2304]{1,0:T(8,128)(2,1)}, bf16[256,2304]{1,0:T(8,128)(2,1)}, u32[]{:S(2)}, u32[]{:S(2)}) %collective-permute-start.33) | collective-permute-done | bytes 1179680 | tf_op jit(solution)/shard_map/ppermute | solution.py:1360
  273.2 46.9 %ffn_fwd.1 = (bf16[4,1024,2304]{2,1,0:T(8,128)(2,1)}, bf16[4,1024,1152]{2,1,0:T(8,128)(2,1)}, bf16[1024,1024]{1,0:T(8,128)(2,1)}, f32[1024,1024]{1,0:T(8,128)}, ...) custom-call(s32[4]{0:T(128)} %copy-done.30, f32[1]{0:T(128)} %bitcast.4.scale, ...), custom_call_target="tpu_custom_call" | custom-call | flops 28991029248 | bytes 73400320 | tf_op jit(solution)/shard_map/ffn_fwd/pallas_call | solution.py:1155
  320.2 25.5 %ffn_bwd.4 = (f32[1024,1024]{1,0:T(8,128)}, bf16[512,3456]{1,0:T(8,128)(2,1)}, bf16[512,3456]{1,0:T(8,128)(2,1)}) custom-call(bf16[1024,1024]{1,0:T(8,128)(2,1)} %get-tuple-element.91.low_ref, bf16[4,1024,2304]{2,1,0:T(8,128)(2,1)} %get-tuple-element.92.act_ref, bf16[4,1024,1152]{2,1,0:T(8,128)(2,1)} %get-tuple-element.93.hid_ref, ...), custom_call_target="tpu_custom_call" | custom-call | flops 14495514624 | bytes 33554432 | tf_op jit(solution)/shard_map/ffn_bwd/pallas_call | solution.py:1262
  345.7 25.7 %ffn_bwd.5 = (f32[1024,1024]{1,0:T(8,128)}, bf16[512,3456]{1,0:T(8,128)(2,1)}, bf16[512,3456]{1,0:T(8,128)(2,1)}) custom-call(bf16[1024,1024]{1,0:T(8,128)(2,1)} %get-tuple-element.91.low_ref, bf16[4,1024,2304]{2,1,0:T(8,128)(2,1)} %get-tuple-element.92.act_ref, bf16[4,1024,1152]{2,1,0:T(8,128)(2,1)} %get-tuple-element.93.hid_ref, ...), custom_call_target="tpu_custom_call", output_to_operand_aliasing={{0}: (11, {})} | custom-call | flops 14495514624 | bytes 33554432 | tf_op jit(solution)/shard_map/ffn_bwd/pallas_call | solution.py:1262
  371.4 26.1 %ffn_bwd.6 = (f32[1024,1024]{1,0:T(8,128)}, bf16[512,3456]{1,0:T(8,128)(2,1)}, bf16[512,3456]{1,0:T(8,128)(2,1)}) custom-call(bf16[1024,1024]{1,0:T(8,128)(2,1)} %get-tuple-element.91.low_ref, bf16[4,1024,2304]{2,1,0:T(8,128)(2,1)} %get-tuple-element.92.act_ref, bf16[4,1024,1152]{2,1,0:T(8,128)(2,1)} %get-tuple-element.93.hid_ref, ...), custom_call_target="tpu_custom_call", output_to_operand_aliasing={{0}: (11, {})} | custom-call | flops 14495514624 | bytes 33554432 | tf_op jit(solution)/shard_map/ffn_bwd/pallas_call | solution.py:1262
  397.6 26.8 %ffn_bwd.7 = (f32[1024,1024]{1,0:T(8,128)}, bf16[512,3456]{1,0:T(8,128)(2,1)}, bf16[512,3456]{1,0:T(8,128)(2,1)}) custom-call(bf16[1024,1024]{1,0:T(8,128)(2,1)} %get-tuple-element.91.low_ref, bf16[4,1024,2304]{2,1,0:T(8,128)(2,1)} %get-tuple-element.92.act_ref, bf16[4,1024,1152]{2,1,0:T(8,128)(2,1)} %get-tuple-element.93.hid_ref, ...), custom_call_target="tpu_custom_call", output_to_operand_aliasing={{0}: (11, {})} | custom-call | flops 14495514624 | bytes 33554432 | tf_op jit(solution)/shard_map/ffn_bwd/pallas_call | solution.py:1262
  455.3 25.0 %attn_bwd.2 = (bf16[512,1024]{1,0:T(8,128)(2,1)S(1)}, bf16[512,1024]{1,0:T(8,128)(2,1)S(1)}) custom-call(s32[4]{0:T(128)S(1)} %copy-done.31, bf16[512,1024]{1,0:T(8,128)(2,1)S(1)} %copy-done.48, bf16[512,1024]{1,0:T(8,128)(2,1)} %collective-permute-done.17.got_ref, bf16[1024,256]{1,0:T(8,128)(2,1)S(1)} %copy-done.66, ...), custom_call_target="tpu_custom_call" | custom-call | flops 21474836480 | bytes 12582912 | tf_op jit(solution)/shard_map/attn_bwd/pallas_call | solution.py:870
  482.1 24.8 %attn_bwd.3 = (bf16[512,1024]{1,0:T(8,128)(2,1)S(1)}, bf16[512,1024]{1,0:T(8,128)(2,1)S(1)}) custom-call(s32[4]{0:T(128)S(1)} %copy-done.31, bf16[512,1024]{1,0:T(8,128)(2,1)S(1)} %copy-done.46, bf16[512,1024]{1,0:T(8,128)(2,1)} %collective-permute-done.18.got_ref, bf16[1024,256]{1,0:T(8,128)(2,1)S(1)} %copy-done.63, bf16[1024,256]{1,0:T(8,128)(2,1)S(1)} %copy-done.50, ...), custom_call_target="tpu_custom_call" | custom-call | flops 21474836480 | bytes 12582912 | tf_op jit(solution)/shard_map/attn_bwd/pallas_call | solution.py:870
  522.2 21.5 %collective-permute-start.59 = (bf16[512,768]{0,1:T(8,128)(2,1)}, bf16[512,768]{0,1:T(8,128)(2,1)}, u32[]{:S(2)}, u32[]{:S(2)}) collective-permute-start(bf16[512,768]{0,1:T(8,128)(2,1)} %fusion.15), channel_id=1, source_target_pairs={{0,8},{8,0},{16,24},{24,16},{1,9},{9,1},{17,25},{25,17},{2,10},{10... | collective-permute-start | bytes 2359304 | tf_op jit(solution)/shard_map/ppermute | solution.py:1363
  674.0 33.1 %collective-permute-done.76 = bf16[256,3456]{1,0:T(8,128)(2,1)S(1)} collective-permute-done((bf16[256,3456]{1,0:T(8,128)(2,1)S(1)}, bf16[256,3456]{1,0:T(8,128)(2,1)S(1)}, u32[]{:S(2)}, u32[]{:S(2)}) %collective-permute-start.76) | collective-permute-done | bytes 1769504 | tf_op jit(solution)/shard_map/ppermute | solution.py:1366
  714.5 35.9 %collective-permute-done.82 = bf16[256,3456]{1,0:T(8,128)(2,1)S(1)} collective-permute-done((bf16[256,3456]{1,0:T(8,128)(2,1)}, bf16[256,3456]{1,0:T(8,128)(2,1)S(1)}, u32[]{:S(2)}, u32[]{:S(2)}) %collective-permute-start.82) | collective-permute-done | bytes 1769504 | tf_op jit(solution)/shard_map/ppermute | solution.py:1360
  753.7 35.8 %collective-permute-done.87 = bf16[256,3456]{1,0:T(8,128)(2,1)S(1)} collective-permute-done((bf16[256,3456]{1,0:T(8,128)(2,1)S(1)}, bf16[256,3456]{1,0:T(8,128)(2,1)S(1)}, u32[]{:S(2)}, u32[]{:S(2)}) %collective-permute-start.87) | collective-permute-done | bytes 1769504 | tf_op jit(solution)/shard_map/ppermute | solution.py:1366
  790.4 18.9 %collective-permute-done.80 = bf16[128,3456]{1,0:T(8,128)(2,1)S(1)} collective-permute-done((bf16[128,3456]{1,0:T(8,128)(2,1)S(1)}, bf16[128,3456]{1,0:T(8,128)(2,1)S(1)}, u32[]{:S(2)}, u32[]{:S(2)}) %collective-permute-start.80) | collective-permute-done | bytes 884768 | tf_op jit(solution)/shard_map/ppermute | solution.py:1366
  809.9 17.8 %collective-permute-done.83 = bf16[128,3456]{1,0:T(8,128)(2,1)S(1)} collective-permute-done((bf16[128,3456]{1,0:T(8,128)(2,1)S(1)}, bf16[128,3456]{1,0:T(8,128)(2,1)S(1)}, u32[]{:S(2)}, u32[]{:S(2)}) %collective-permute-start.83) | collective-permute-done | bytes 884768 | tf_op jit(solution)/shard_map/ppermute | solution.py:1366
  829.2 16.0 %collective-permute-done.88 = bf16[128,3456]{1,0:T(8,128)(2,1)S(1)} collective-permute-done((bf16[128,3456]{1,0:T(8,128)(2,1)S(1)}, bf16[128,3456]{1,0:T(8,128)(2,1)S(1)}, u32[]{:S(2)}, u32[]{:S(2)}) %collective-permute-start.88) | collective-permute-done | bytes 884768 | tf_op jit(solution)/shard_map/ppermute | solution.py:1360
  849.5 19.3 %collective-permute-done.84 = bf16[128,3456]{1,0:T(8,128)(2,1)S(1)} collective-permute-done((bf16[128,3456]{1,0:T(8,128)(2,1)S(1)}, bf16[128,3456]{1,0:T(8,128)(2,1)S(1)}, u32[]{:S(2)}, u32[]{:S(2)}) %collective-permute-start.84) | collective-permute-done | bytes 884768 | tf_op jit(solution)/shard_map/ppermute | solution.py:1326
  888.2 54.7 %collective-permute-done.89 = bf16[128,3456]{1,0:T(8,128)(2,1)S(1)} collective-permute-done((bf16[128,3456]{1,0:T(8,128)(2,1)S(1)}, bf16[128,3456]{1,0:T(8,128)(2,1)S(1)}, u32[]{:S(2)}, u32[]{:S(2)}) %collective-permute-start.89) | collective-permute-done | bytes 884768 | tf_op jit(solution)/shard_map/ppermute | solution.py:1328
  944.9 16.5 %collective-permute-done.85 = bf16[128,3456]{1,0:T(8,128)(2,1)S(1)} collective-permute-done((bf16[128,3456]{1,0:T(8,128)(2,1)S(1)}, bf16[128,3456]{1,0:T(8,128)(2,1)S(1)}, u32[]{:S(2)}, u32[]{:S(2)}) %collective-permute-start.85) | collective-permute-done | bytes 884768 | tf_op jit(solution)/shard_map/ppermute | solution.py:1327
  972.3 34.6 %collective-permute-done.46 = bf16[1024,1024]{1,0:T(8,128)(2,1)} collective-permute-done((bf16[1024,1024]{1,0:T(8,128)(2,1)}, bf16[1024,1024]{1,0:T(8,128)(2,1)}, u32[]{:S(2)}, u32[]{:S(2)}) %collective-permute-start.46) | collective-permute-done | bytes 2097184 | tf_op jit(solution)/shard_map/ppermute | solution.py:1305
  1010.0 35.0 %collective-permute-done.58 = bf16[1024,1024]{1,0:T(8,128)(2,1)} collective-permute-done((bf16[1024,1024]{1,0:T(8,128)(2,1)}, bf16[1024,1024]{1,0:T(8,128)(2,1)}, u32[]{:S(2)}, u32[]{:S(2)}) %collective-permute-start.58) | collective-permute-done | bytes 2097184 | tf_op jit(solution)/shard_map/ppermute | solution.py:1305
  (644 shorter events, 426.4 us)
Async XLA Ops:
  49.4 58.6 %collective-permute-start.26 = (bf16[256,3456]{1,0:T(8,128)(2,1)}, bf16[256,3456]{1,0:T(8,128)(2,1)}, u32[]{:S(2)}, u32[]{:S(2)}) collective-permute-start(bf16[256,3456]{1,0:T(8,128)(2,1)} %get-tuple-element.89.rest_0_), channel_id=1, source_target_pairs={{0,1},{1,2},{2,3},{3,0},{4,5},{5,6},{6,7},{7,4},{8,9},{9,10},{10,1... | collective-permute-start | bytes 5308424 | tf_op jit(solution)/shard_map/ppermute | solution.py:1303
  63.2 67.1 %collective-permute-start.32 = (bf16[256,3456]{1,0:T(8,128)(2,1)}, bf16[256,3456]{1,0:T(8,128)(2,1)}, u32[]{:S(2)}, u32[]{:S(2)}) collective-permute-start(bf16[256,3456]{1,0:T(8,128)(2,1)} %get-tuple-element.89.rest_0_), channel_id=1, source_target_pairs={{0,3},{1,0},{2,1},{3,2},{4,7},{5,4},{6,5},{7,6},{8,11},{9,8},{10,9... | collective-permute-start | bytes 5308424 | tf_op jit(solution)/shard_map/ppermute | solution.py:1304
  72.9 59.8 %collective-permute-start.18 = (bf16[512,1024]{1,0:T(8,128)(2,1)}, bf16[512,1024]{1,0:T(8,128)(2,1)}, u32[]{:S(2)}, u32[]{:S(2)}) collective-permute-start(bf16[512,1024]{1,0:T(8,128)(2,1)} %get-tuple-element.81), channel_id=1, source_target_pairs={{0,4},{4,0},{1,5},{5,1},{2,6},{6,2},{3,7},{7,3},{8,12},{12,8},{9,1... | collective-permute-start | bytes 3145736 | tf_op jit(solution)/shard_map/ppermute | solution.py:1366
  74.5 78.2 %collective-permute-start.23 = (bf16[256,3456]{1,0:T(8,128)(2,1)}, bf16[256,3456]{1,0:T(8,128)(2,1)}, u32[]{:S(2)}, u32[]{:S(2)}) collective-permute-start(bf16[256,3456]{1,0:T(8,128)(2,1)} %get-tuple-element.89.rest_0_), channel_id=1, source_target_pairs={{0,8},{8,0},{16,24},{24,16},{1,9},{9,1},{17,25},{25,17},{2,10},{10... | collective-permute-start | bytes 5308424 | tf_op jit(solution)/shard_map/ppermute | solution.py:1363
  95.7 54.9 %collective-permute-start.17 = (bf16[512,1024]{1,0:T(8,128)(2,1)}, bf16[512,1024]{1,0:T(8,128)(2,1)}, u32[]{:S(2)}, u32[]{:S(2)}) collective-permute-start(bf16[512,1024]{1,0:T(8,128)(2,1)} %get-tuple-element.78), channel_id=1, source_target_pairs={{0,4},{4,0},{1,5},{5,1},{2,6},{6,2},{3,7},{7,3},{8,12},{12,8},{9,1... | collective-permute-start | bytes 3145736 | tf_op jit(solution)/shard_map/ppermute | solution.py:1366
  108.0 44.1 %collective-permute-start.22 = (bf16[256,1152]{1,0:T(8,128)(2,1)S(1)}, bf16[256,1152]{1,0:T(8,128)(2,1)S(1)}, u32[]{:S(2)}, u32[]{:S(2)}) collective-permute-start(bf16[256,1152]{1,0:T(8,128)(2,1)S(1)} %slice.638), channel_id=1, source_target_pairs={{0,4},{4,0},{1,5},{5,1},{2,6},{6,2},{3,7},{7,3},{8,12},{12,8},{9,1... | collective-permute-start | bytes 1769480 | tf_op jit(solution)/shard_map/ppermute | solution.py:1366
  130.4 81.2 %collective-permute-start.24 = (bf16[256,2304]{1,0:T(8,128)(2,1)}, bf16[256,2304]{1,0:T(8,128)(2,1)}, u32[]{:S(2)}, u32[]{:S(2)}) collective-permute-start(bf16[256,2304]{1,0:T(8,128)(2,1)} %collective-permute-done.21.rest_1_), channel_id=1, source_target_pairs={{0,8},{8,0},{16,24},{24,16},{1,9},{9,1},{17,25},{25,17},{2,10},{10... | collective-permute-start | bytes 3538952 | tf_op jit(solution)/shard_map/ppermute | solution.py:1363
  152.2 52.2 %collective-permute-start.33 = (bf16[256,2304]{1,0:T(8,128)(2,1)}, bf16[256,2304]{1,0:T(8,128)(2,1)}, u32[]{:S(2)}, u32[]{:S(2)}) collective-permute-start(bf16[256,2304]{1,0:T(8,128)(2,1)} %slice.641), channel_id=1, source_target_pairs={{0,16},{16,0},{8,24},{24,8},{1,17},{17,1},{9,25},{25,9},{2,18},{18... | collective-permute-start | bytes 3538952 | tf_op jit(solution)/shard_map/ppermute | solution.py:1360
  186.0 54.3 %collective-permute-start.29 = (bf16[256,3456]{1,0:T(8,128)(2,1)}, bf16[256,3456]{1,0:T(8,128)(2,1)S(1)}, u32[]{:S(2)}, u32[]{:S(2)}) collective-permute-start(bf16[256,3456]{1,0:T(8,128)(2,1)} %collective-permute-done.26.rest_6_.rest_0_), channel_id=1, source_target_pairs={{0,8},{8,0},{16,24},{24,16},{1,9},{9,1},{17,25},{25,17},{2,10},{10... | collective-permute-start | bytes 5308424 | tf_op jit(solution)/shard_map/ppermute | solution.py:1363
  186.0 54.7 %collective-permute-start.35 = (bf16[256,3456]{1,0:T(8,128)(2,1)}, bf16[256,3456]{1,0:T(8,128)(2,1)S(1)}, u32[]{:S(2)}, u32[]{:S(2)}) collective-permute-start(bf16[256,3456]{1,0:T(8,128)(2,1)} %collective-permute-done.32.rest_12_.rest_0_), channel_id=1, source_target_pairs={{0,8},{8,0},{16,24},{24,16},{1,9},{9,1},{17,25},{25,17},{2,10},{10... | collective-permute-start | bytes 5308424 | tf_op jit(solution)/shard_map/ppermute | solution.py:1363
  424.4 235.9 %collective-permute-start.75 = (bf16[512,3456]{1,0:T(8,128)(2,1)}, bf16[512,3456]{1,0:T(8,128)(2,1)}, u32[]{:S(2)}, u32[]{:S(2)}) collective-permute-start(bf16[512,3456]{1,0:T(8,128)(2,1)} %get-tuple-element.127), channel_id=1, source_target_pairs={{0,8},{8,0},{16,24},{24,16},{1,9},{9,1},{17,25},{25,17},{2,10},{10... | collective-permute-start | bytes 10616840 | tf_op jit(solution)/shard_map/ppermute | solution.py:1363
  446.9 402.5 %collective-permute-start.44 = (bf16[1024,1024]{1,0:T(8,128)(2,1)}, bf16[1024,1024]{1,0:T(8,128)(2,1)}, u32[]{:S(2)}, u32[]{:S(2)}) collective-permute-start(bf16[1024,1024]{1,0:T(8,128)(2,1)} %get-tuple-element.90), channel_id=1, source_target_pairs={{0,1},{1,2},{2,3},{3,0},{4,5},{5,6},{6,7},{7,4},{8,9},{9,10},{10,1... | collective-permute-start | bytes 6291464 | tf_op jit(solution)/shard_map/ppermute | solution.py:1303
  522.2 80.7 %collective-permute-start.59 = (bf16[512,768]{0,1:T(8,128)(2,1)}, bf16[512,768]{0,1:T(8,128)(2,1)}, u32[]{:S(2)}, u32[]{:S(2)}) collective-permute-start(bf16[512,768]{0,1:T(8,128)(2,1)} %fusion.15), channel_id=1, source_target_pairs={{0,8},{8,0},{16,24},{24,16},{1,9},{9,1},{17,25},{25,17},{2,10},{10... | collective-permute-start | bytes 2359304 | tf_op jit(solution)/shard_map/ppermute | solution.py:1363
  604.9 58.9 %collective-permute-start.86 = (bf16[512,3456]{1,0:T(8,128)(2,1)}, bf16[512,3456]{1,0:T(8,128)(2,1)S(1)}, u32[]{:S(2)}, u32[]{:S(2)}) collective-permute-start(bf16[512,3456]{1,0:T(8,128)(2,1)} %get-tuple-element.133), channel_id=1, source_target_pairs={{0,8},{8,0},{16,24},{24,16},{1,9},{9,1},{17,25},{25,17},{2,10},{10... | collective-permute-start | bytes 10616840 | tf_op jit(solution)/shard_map/ppermute | solution.py:1363
  654.9 218.7 %collective-permute-start.45 = (bf16[1024,1024]{1,0:T(8,128)(2,1)S(1)}, bf16[1024,1024]{1,0:T(8,128)(2,1)S(1)}, u32[]{:S(2)}, u32[]{:S(2)}) collective-permute-start(bf16[1024,1024]{1,0:T(8,128)(2,1)S(1)} %copy-done.81), channel_id=1, source_target_pairs={{0,3},{1,0},{2,1},{3,2},{4,7},{5,4},{6,5},{7,6},{8,11},{9,8},{10,9... | collective-permute-start | bytes 6291464 | tf_op jit(solution)/shard_map/ppermute | solution.py:1304
  663.8 223.8 %collective-permute-start.56 = (bf16[1024,1024]{1,0:T(8,128)(2,1)S(1)}, bf16[1024,1024]{1,0:T(8,128)(2,1)}, u32[]{:S(2)}, u32[]{:S(2)}) collective-permute-start(bf16[1024,1024]{1,0:T(8,128)(2,1)S(1)} %copy-done.15), channel_id=1, source_target_pairs={{0,1},{1,2},{2,3},{3,0},{4,5},{5,6},{6,7},{7,4},{8,9},{9,10},{10,1... | collective-permute-start | bytes 6291464 | tf_op jit(solution)/shard_map/ppermute | solution.py:1303
  712.5 161.1 %collective-permute-start.61 = (bf16[128,768]{0,1:T(8,128)(2,1)S(1)}, bf16[128,768]{0,1:T(8,128)(2,1)S(1)}, u32[]{:S(2)}, u32[]{:S(2)}) collective-permute-start(bf16[128,768]{0,1:T(8,128)(2,1)S(1)} %copy-done.101), channel_id=1, source_target_pairs={{0,16},{16,0},{8,24},{24,8},{1,17},{17,1},{9,25},{25,9},{2,18},{18... | collective-permute-start | bytes 589832 | tf_op jit(solution)/shard_map/ppermute | solution.py:1360
  873.6 93.1 %collective-permute-start.57 = (bf16[1024,1024]{1,0:T(8,128)(2,1)S(1)}, bf16[1024,1024]{1,0:T(8,128)(2,1)S(1)}, u32[]{:S(2)}, u32[]{:S(2)}) collective-permute-start(bf16[1024,1024]{1,0:T(8,128)(2,1)S(1)} %copy-done.15), channel_id=1, source_target_pairs={{0,3},{1,0},{2,1},{3,2},{4,7},{5,4},{6,5},{7,6},{8,11},{9,8},{10,9... | collective-permute-start | bytes 6291464 | tf_op jit(solution)/shard_map/ppermute | solution.py:1304
  875.0 67.9 %collective-permute-start.89 = (bf16[128,3456]{1,0:T(8,128)(2,1)S(1)}, bf16[128,3456]{1,0:T(8,128)(2,1)S(1)}, u32[]{:S(2)}, u32[]{:S(2)}) collective-permute-start(bf16[128,3456]{1,0:T(8,128)(2,1)S(1)} %add_convert_fusion.10), channel_id=1, source_target_pairs={{0,1},{1,2},{2,3},{3,0},{4,5},{5,6},{6,7},{7,4},{8,9},{9,10},{10,1... | collective-permute-start | bytes 2654216 | tf_op jit(solution)/shard_map/ppermute | solution.py:1328
  878.5 82.9 %collective-permute-start.85 = (bf16[128,3456]{1,0:T(8,128)(2,1)S(1)}, bf16[128,3456]{1,0:T(8,128)(2,1)S(1)}, u32[]{:S(2)}, u32[]{:S(2)}) collective-permute-start(bf16[128,3456]{1,0:T(8,128)(2,1)S(1)} %add_convert_fusion.13), channel_id=1, source_target_pairs={{0,3},{1,0},{2,1},{3,2},{4,7},{5,4},{6,5},{7,6},{8,11},{9,8},{10,9... | collective-permute-start | bytes 2654216 | tf_op jit(solution)/shard_map/ppermute | solution.py:1327
  887.6 119.3 %collective-permute-start.46 = (bf16[1024,1024]{1,0:T(8,128)(2,1)}, bf16[1024,1024]{1,0:T(8,128)(2,1)}, u32[]{:S(2)}, u32[]{:S(2)}) collective-permute-start(bf16[1024,1024]{1,0:T(8,128)(2,1)} %collective-permute-done.44), channel_id=1, source_target_pairs={{0,1},{1,2},{2,3},{3,0},{4,5},{5,6},{6,7},{7,4},{8,9},{9,10},{10,1... | collective-permute-start | bytes 6291464 | tf_op jit(solution)/shard_map/ppermute | solution.py:1305
  887.7 81.4 %collective-permute-start.74 = (f32[128,768]{0,1:T(8,128)S(1)}, f32[128,768]{0,1:T(8,128)S(1)}, u32[]{:S(2)}, u32[]{:S(2)}) collective-permute-start(f32[128,768]{0,1:T(8,128)S(1)} %convert_add_fusion.1), channel_id=1, source_target_pairs={{0,4},{4,0},{1,5},{5,1},{2,6},{6,2},{3,7},{7,3},{8,12},{12,8},{9,1... | collective-permute-start | bytes 1179656 | tf_op jit(solution)/shard_map/ppermute | solution.py:1366
  942.9 102.1 %collective-permute-start.58 = (bf16[1024,1024]{1,0:T(8,128)(2,1)}, bf16[1024,1024]{1,0:T(8,128)(2,1)}, u32[]{:S(2)}, u32[]{:S(2)}) collective-permute-start(bf16[1024,1024]{1,0:T(8,128)(2,1)} %collective-permute-done.56), channel_id=1, source_target_pairs={{0,1},{1,2},{2,3},{3,0},{4,5},{5,6},{6,7},{7,4},{8,9},{9,10},{10,1... | collective-permute-start | bytes 6291464 | tf_op jit(solution)/shard_map/ppermute | solution.py:1305
  962.1 87.1 %collective-permute-start.90 = (f32[128,3456]{1,0:T(8,128)S(1)}, f32[128,3456]{1,0:T(8,128)}, u32[]{:S(2)}, u32[]{:S(2)}) collective-permute-start(f32[128,3456]{1,0:T(8,128)S(1)} %convert_add_fusion), channel_id=1, source_target_pairs={{0,4},{4,0},{1,5},{5,1},{2,6},{6,2},{3,7},{7,3},{8,12},{12,8},{9,1... | collective-permute-start | bytes 5308424 | tf_op jit(solution)/shard_map/ppermute | solution.py:1366
  (199 other events, 3428.8 us)

commit v3 on v2

--- a/solution.py
+++ b/solution.py
@@ -408,7 +408,7 @@
 
 
 def cost(flops, bytes_accessed):
-    return pl.CostEstimate(flops=flops, bytes_accessed=bytes_accessed, transcendentals=0)
+    return pl.CostEstimate(flops=flops >> 8, bytes_accessed=bytes_accessed >> 8, transcendentals=0)
 
 
 def pack_kernel(info, q_ref, k_ref, v_ref, o_ref, g_ref, u_ref, d_ref, attn_ref, ffn_ref):
@@ -1035,19 +1035,14 @@
     )(info, *pairs, w_proj, x, grad_resid, gain)
 
 
-def weight_copies(pieces, gate_up, down, gate_up_sem, down_sem):
-    own, far, last, own2, far2, last2 = pieces
-    rows, cols = own.shape
-    chunk = cols // 3
-    third = chunk // 3
+def weight_copies(plan, pieces, gate_up, down, gate_up_sem, down_sem):
+    third = down.shape[1] // 3
+    rows = down.shape[0] // 4
     wide, thin = [], []
-    for p, (ref, first) in enumerate(((own, 0), (far, 0), (own2, 0), (far2, 0))):
-        for j in range(3):
-            src = ref
-            at = j * chunk
-            if p % 2 == 1 and j == 2:
-                src, at = (last, last2)[p // 2], 0
-            block = pl.ds(p * rows, rows)
+    for p, chunks in enumerate(plan):
+        block = pl.ds(p * rows, rows)
+        for j, (piece, at) in enumerate(chunks):
+            src = pieces[piece]
             wide.append(
                 pltpu.make_async_copy(
                     src.at[:, pl.ds(at, 2 * third)],
@@ -1073,6 +1068,7 @@
 
 def ffn_fwd_kernel(
     tile,
+    plans,
     info,
     scale,
     x_ref,
@@ -1080,16 +1076,22 @@
     teach_ref,
     *rest,
 ):
-    pieces = [rest[6 * s : 6 * s + 6] for s in range(4)]
-    act_ref, hid_ref, out_ref, gres_ref, low_ref, lowt_ref, sq_ref = rest[24:31]
-    gate_up, down, total, sems = rest[31:]
+    pieces = []
+    for plan in plans:
+        count = 1 + max(piece for chunks in plan for piece, _ in chunks)
+        pieces.append(rest[:count])
+        rest = rest[count:]
+    act_ref, hid_ref, out_ref, gres_ref, low_ref, lowt_ref, sq_ref = rest[:7]
+    gate_up, down, total, sems = rest[7:]
     step, part = pl.program_id(0), pl.program_id(1)
     width = x_ref.shape[1]
     quarter = width // 4
     third = down.shape[2] // 3
 
     def copies(s):
-        return weight_copies(pieces[s], gate_up.at[s], down.at[s], sems.at[s, 0], sems.at[s, 1])
+        return weight_copies(
+            plans[s], pieces[s], gate_up.at[s], down.at[s], sems.at[s, 0], sems.at[s, 1]
+        )
 
     @pl.when((step == 0) & (part == 0))
     def _():
@@ -1147,13 +1149,13 @@
         sq_ref[...] += jnp.sum(square, axis=0, keepdims=True)
 
 
-def ffn_fwd(info, scale, x, resid, teacher, pieces, tile):
+def ffn_fwd(info, scale, x, resid, teacher, weights, units, tile):
     tok, width = x.shape
-    units = pieces[0][0].shape[1] // 3
+    pieces = [piece for _, group in weights for piece in group]
     last = lambda s, i: jnp.where(s == 3, i, 0)
     tiles = lambda n: pl.BlockSpec((tile, n), lambda s, i, info: (last(s, i), 0))
     return pl.pallas_call(
-        functools.partial(ffn_fwd_kernel, tile),
+        functools.partial(ffn_fwd_kernel, tile, [plan for plan, _ in weights]),
         grid_spec=pltpu.PrefetchScalarGridSpec(
             num_scalar_prefetch=1,
             grid=(4, tok // tile),
@@ -1163,7 +1165,7 @@
                 whole((tok, width)),
                 pl.BlockSpec((1, tile, width), lambda s, i, info: (info[0], last(s, i), 0)),
             ]
-            + [ANY] * 24,
+            + [ANY] * len(pieces),
             out_specs=[
                 pl.BlockSpec((1, tile, 2 * units), lambda s, i, info: (s, i, 0)),
                 pl.BlockSpec((1, tile, units), lambda s, i, info: (s, i, 0)),
@@ -1192,12 +1194,12 @@
         compiler_params=settings(2, 61),
         cost_estimate=cost(2 * tok * width * units * 12, 70 << 20),
         name="ffn_fwd",
-    )(info, scale, x, resid, teacher, *[ref for group in pieces for ref in group])
-
-
-def ffn_bwd_kernel(steps, first, low_ref, act_ref, hid_ref, xt_ref, lowt_ref, *rest):
-    pieces = rest[:6]
-    rest = rest[6:]
+    )(info, scale, x, resid, teacher, *pieces)
+
+
+def ffn_bwd_kernel(steps, plan, first, low_ref, act_ref, hid_ref, xt_ref, lowt_ref, *rest):
+    count = 1 + max(piece for chunks in plan for piece, _ in chunks)
+    pieces, rest = rest[:count], rest[count:]
     if not first:
         in_ref, rest = rest[0], rest[1:]
     out_ref, keep_ref, send_ref, gate_up, down, dact_all, hid_all, sems = rest
@@ -1208,7 +1210,7 @@
 
     @pl.when(step == 0)
     def _():
-        wide, thin = weight_copies(pieces, gate_up, down, sems.at[0], sems.at[1])
+        wide, thin = weight_copies(plan, pieces, gate_up, down, sems.at[0], sems.at[1])
         for copy in thin + wide:
             copy.start()
         pltpu.make_async_copy(down, down, sems.at[1]).wait()
@@ -1249,7 +1251,8 @@
         weight_rows(keep_ref)
 
 
-def ffn_bwd(block, low, acts, hiddens, pieces, total, xt, lowt, tile):
+def ffn_bwd(block, low, acts, hiddens, weights, total, xt, lowt, tile):
+    plan, pieces = weights
     tok, width = low.shape
     units = hiddens.shape[2]
     steps = tok // tile
@@ -1260,7 +1263,7 @@
     slab = lambda n: pl.BlockSpec((1, tile, n), lambda i: (block, clip(i), 0))
     feature = lambda i: (jnp.where(i < steps + 2, jnp.maximum(i - steps, 0) + 2, i - steps - 2), 0)
     return pl.pallas_call(
-        functools.partial(ffn_bwd_kernel, steps, first),
+        functools.partial(ffn_bwd_kernel, steps, plan, first),
         grid=(steps + 4,),
         in_specs=[
             rows_of(width),
@@ -1269,7 +1272,7 @@
             pl.BlockSpec((quarter, tok), feature),
             pl.BlockSpec((quarter, tok), feature),
         ]
-        + [ANY] * 6
+        + [ANY] * len(pieces)
         + ([] if first else [rows_of(width)]),
         out_specs=[
             rows_of(width),
@@ -1288,7 +1291,7 @@
             pltpu.VMEM((tok, units), BF16),
             pltpu.SemaphoreType.DMA((2,)),
         ],
-        input_output_aliases={} if first else {11: 0},
+        input_output_aliases={} if first else {5 + len(pieces): 0},
         compiler_params=settings(1, 56),
         cost_estimate=cost(2 * tok * width * units * 6, 32 << 20),
         name="ffn_bwd",
@@ -1386,7 +1389,12 @@
     gain_q = head_gains[:, : hd // 4].reshape(hd, 1)
     gain_k = head_gains[:, hd // 4 :].reshape(hd, 1)
 
-    attn_blocks = z_gather(w_attn)
+    attn_blocks = [
+        w_attn,
+        lax.ppermute(w_attn, "tp", Z_UP),
+        lax.ppermute(w_attn, "tp", Z_FAR),
+        lax.ppermute(w_attn, "tp", Z_DOWN),
+    ]
     attn_pieces = []
     for block in attn_blocks:
         far = x_swap(block)
@@ -1396,16 +1404,26 @@
     w_out = jnp.concatenate([p[:, proj:] for b in attn_pieces for p in b], axis=0)
     w_out = w_out.reshape(4, width, q_cols)
 
-    chunk = units
-    ffn_blocks = z_gather(after(w_ffn, attn_blocks[2]))
-    ffn_pieces = []
-    for block in ffn_blocks:
-        block = after(block, attn_pieces[2][1]) if block is ffn_blocks[0] else block
-        far = x_swap(block[:, : 2 * chunk])
-        last = y_swap(far[:, :chunk])
-        ffn_pieces.append(
-            [block, far, last, core_swap(block), core_swap(far), core_swap(last)]
-        )
+    ffn_one = lax.ppermute(after(w_ffn, attn_blocks[1]), "tp", Z_UP)
+    ffn_three = lax.ppermute(after(w_ffn, attn_blocks[3]), "tp", Z_DOWN)
+    ffn_two = [
+        lax.ppermute(ffn_one[:, j * units : (j + 1) * units], "tp", Z_UP) for j in range(3)
+    ]
+    in_block = lambda i: [(i, 0), (i, units), (i, 2 * units)]
+    in_pair = lambda i: [(i, 0), (i, units), (i + 1, 0)]
+    plan_whole = [in_block(0), in_pair(1), in_block(3), in_pair(4)]
+    plan_chunks = [[(3 * p + j, 0) for j in range(3)] for p in range(4)]
+
+    def ffn_pieces(block, then):
+        far = x_swap(block[:, : 2 * units])
+        last = y_swap(after(far[:, :units], then))
+        return [block, far, last, core_swap(block), core_swap(far), core_swap(last)]
+
+    def ffn_chunks(blocks, then):
+        far = [x_swap(blocks[0]), x_swap(blocks[1])]
+        far.append(y_swap(after(far[0], then)))
+        pieces = blocks + far
+        return pieces + [core_swap(p) for p in pieces]
 
     x_in, normed_one_t = norm_one(info, tokens, gain_one, 256)
     pos = (ctx * tok + jnp.arange(tok, dtype=jnp.int32)).astype(F32)
@@ -1426,36 +1444,27 @@
         info, x_in, [outs[0][0], outs[1][0]], arrived, w_out, gain_two, 256
     )
 
+    own_ffn = after(w_ffn, attn_pieces[1][1], attn_pieces[3][1])
+    ffn_weights = [
+        (plan_whole, ffn_pieces(own_ffn, got[1])),
+        (plan_whole, ffn_pieces(ffn_one, got[1])),
+        (plan_chunks, ffn_chunks(ffn_two, outs[1][1])),
+        (plan_whole, ffn_pieces(ffn_three, outs[0][1])),
+    ]
     order = (0, 1, 3, 2)
     scale = (slots / total_count)[None]
     acts, hiddens, result_low, grad_result, grad_low, grad_low_t, square = ffn_fwd(
-        info, scale, normed_two, resid, teacher, [ffn_pieces[k] for k in order], 256
-    )
-
-    def spread(block, dtype):
+        info, scale, normed_two, resid, teacher, [ffn_weights[k] for k in order], units, 256
+    )
+
+    def spread(parts, dtype):
         out = jnp.zeros((rows_dev, tok, width), dtype)
-        parts = z_gather(block)
         for k in (0, 1, 3, 2):
             part = parts[k].astype(dtype)[None]
             out = lax.dynamic_update_slice(out, part, (lax.rem(z - k + 4, 4), 0, 0))
         return out
 
-    output = spread(result_low, BF16)
-
-    grad_two = None
-    keeps, sends = [None] * 4, [None] * 4
-    for k in (2, 1, 3, 0):
-        grad_two, keeps[k], sends[k] = ffn_bwd(
-            order.index(k),
-            grad_low,
-            acts,
-            hiddens,
-            ffn_pieces[k],
-            grad_two,
-            normed_two_t,
-            grad_low_t,
-            256,
-        )
+    output_parts = z_gather(result_low)
 
     def halves(v):
         half = v.shape[0] // 2
@@ -1481,46 +1490,80 @@
             add_low(here, came[:half]), x_swap(add_low(far_here, came[half:]))
         )
 
-    def finish(parts, turn):
-        own = z_reduce(parts)
+    def finish(own, turn):
         other = turn(y_swap(own))
         return jnp.concatenate(
             [jnp.where(ctx == 0, own, other), jnp.where(ctx == 0, other, own)], axis=0
         )
 
-    ffn_parts = [
-        plane_sum(*core_sum(keeps[k], sends[k]), k in (1, 2), turn_chunks) for k in range(4)
-    ]
-
+    def ffn_back(k, total):
+        return ffn_bwd(
+            order.index(k),
+            grad_low,
+            acts,
+            hiddens,
+            ffn_weights[k],
+            total,
+            normed_two_t,
+            grad_low_t,
+            256,
+        )
+
+    def y_sum(own):
+        here, there = halves(own)
+        return add_low(here, turn_chunks(y_swap(there)))
+
+    grad_two, keep2, send2 = ffn_back(2, None)
+    grad_two, keep1, send1 = ffn_back(1, grad_two)
+    own2, far2 = core_sum(keep2, send2)
+    grad_two, keep3, send3 = ffn_back(3, after(grad_two, own2, far2))
+    own1, far1 = core_sum(keep1, send1)
+    grad_two, keep0, send0 = ffn_back(0, after(grad_two, own1, far1))
+    own3, far3 = core_sum(keep3, send3)
+    own2 = add_low(own2, x_swap(far2))
     grad_resid, grad_attn_t, a0, a1, b0, b1, gain_two_sum = norm_two_back(
-        info, grad_two, resid, grad_result, gain_two, w_out, 256
+        info, after(grad_two, own2, own3, far3), resid, grad_result, gain_two, w_out, 256
     )
 
     grad_got = [y_swap(b0), y_swap(b1)]
-    grads = [
-        attn_bwd(
-            info,
-            mine[j][0],
-            got[j],
-            outs[j][0],
-            outs[j][1],
-            (a0, a1)[j],
-            grad_got[j],
-            outs[j][2],
-            hd,
-        )
-        for j in range(2)
-    ]
+    own0, far0 = core_sum(keep0, send0)
+
+    def attn_back(j, grad):
+        return attn_bwd(
+            info, mine[j][0], got[j], outs[j][0], outs[j][1], grad, grad_got[j], outs[j][2], hd
+        )
+
+    first_back = attn_back(0, after(a0, own0, far0))
+    part2 = y_sum(after(own2, grad_got[1]))
+    own1 = add_low(own1, x_swap(far1))
+    second_back = attn_back(1, after(a1, first_back[1], own1, part2, output_parts[1]))
+    part1 = y_sum(after(own1, first_back[1]))
+    own3 = add_low(own3, x_swap(after(far3, own1)))
+    output_parts[2] = after(output_parts[2], second_back[1])
+    grad_heads = [y_swap(first_back[1]), y_swap(second_back[1])]
+    two_down = add_low(part1, lax.ppermute(part2, "tp", Z_DOWN))
     back = [
         head_back(
-            info, grads[j][0], y_swap(grads[j][1]), mine[j][1], theirs[j][1], *tables, heads
-        )
-        for j in range(2)
+            info,
+            after(first_back[0], part1, own3),
+            grad_heads[0],
+            mine[0][1],
+            theirs[0][1],
+            *tables,
+            heads,
+        ),
+        head_back(
+            info, second_back[0], grad_heads[1], mine[1][1], theirs[1][1], *tables, heads
+        ),
     ]
+    part3 = y_sum(after(own3, grad_heads[1]))
+    own0 = add_low(own0, x_swap(after(far0, own3)))
+    part0 = y_sum(after(own0, part3))
     tokens_low, gain_one_sum = norm_one_back(
         info, [back[0][0], back[1][0]], w_proj, x_in, grad_resid, gain_one, 256
     )
-    tokens_grad = spread(tokens_low, F32)
+    tokens_grad = spread(z_gather(tokens_low), F32)
+    output = spread([after(part, tokens_low) for part in output_parts], BF16)
 
     attn_parts = []
     for k in range(4):
@@ -1534,8 +1577,10 @@
         own, far = core_sum(part[: width // 2], part[width // 2 :])
         attn_parts.append(plane_sum(own, far, k in (1, 2), lambda v: v))
 
-    ffn_grad = finish(ffn_parts, turn_chunks)
-    attn_grad = finish(attn_parts, lambda v: v)
+    ffn_sum = add(part0, lax.ppermute(two_down, "tp", Z_DOWN))
+    ffn_sum = ffn_sum + lax.ppermute(part3, "tp", Z_UP).astype(F32)
+    ffn_grad = finish(ffn_sum, turn_chunks)
+    attn_grad = finish(z_reduce(attn_parts), lambda v: v)
 
     def total(v):
         for axis, pairs in (("fsdp", CORE_SWAP), ("fsdp", X_SWAP), ("ctx", Y_SWAP)):

time: 1070 us -> 1010 us (0.944)
  waiting for transfers between devices: 486 us -> 346 us
  starting transfers between devices: 114 us -> 188 us
  Pallas kernels: 280 us -> 256 us
  other arithmetic: 45.2 us -> 63.5 us
    ppermute x0 -> x11, starting transfers between devices: none -> 78.6 us  [the longest x1 24.6 us: per_device_rows(): two_down = add_low(part1, lax.ppermute(part2, 'tp', Z_DOWN))]
    ppermute x4 -> x2, waiting for transfers between devices: 78 us -> 0.01 us  [z_gather(): two = lax.ppermute(one, 'tp', Z_UP)]
    ppermute x2 -> x1, waiting for transfers between devices: 54.7 us -> 0.01 us  [z_reduce(): return total + lax.ppermute(parts[3], 'tp', Z_UP).astype(F32)]
    ppermute x0 -> x11, waiting for transfers between devices: none -> 43.2 us  [the longest x3 26.6 us: per_device_rows(): lax.ppermute(ffn_one[:, j * units:(j + 1) * units], 'tp', Z_UP)]
    ppermute x4 -> x2, waiting for transfers between devices: 0.01 us -> 42 us  [z_gather(): one = lax.ppermute(block, 'tp', Z_UP)]
    ppermute x17 -> x18, starting transfers between devices: 21.4 us -> 57 us  [x_swap(): return lax.ppermute(v, 'fsdp', X_SWAP)]
    ppermute x22, waiting for transfers between devices: 163 us -> 132 us  [y_swap(): return lax.ppermute(v, 'ctx', Y_SWAP)]
    ppermute x29 -> x32, starting transfers between devices: 26.1 us -> 5.32 us  [core_swap(): return lax.ppermute(v, 'fsdp', CORE_SWAP)]
  transfers between devices with their start and end apart: 91 -> 97, of which waited for: 37 -> 35; matrix products, arithmetic and copies ran while one was open for 12% -> 16% of each run, Pallas kernels for 12% -> 18%
where the time goes in v3:
time: 1010 us; the launch traced here: 992 us
  waiting for transfers between devices  346 us (34%)
  Pallas kernels  256 us (25%)
  starting transfers between devices  188 us (19%)
  local copies, waits for them, and re-layouts  113 us (11%)
  other arithmetic  63.5 us (6%)
  matrix products  17.6 us (2%)
    ppermute x22, waiting for transfers between devices, y_swap(): return lax.ppermute(v, 'ctx', Y_SWAP)  132 us
    pallas_call x4, Pallas kernels, ffn_bwd(): pl.pallas_call(functools.partial(ffn_bwd_kernel, steps, plan, first), gri...  105 us
    ppermute x18, waiting for transfers between devices, x_swap(): return lax.ppermute(v, 'fsdp', X_SWAP)  103 us
    unnamed x340, local copies, waits for them, and re-layouts  75 us
    ppermute x18, starting transfers between devices, x_swap(): return lax.ppermute(v, 'fsdp', X_SWAP)  57 us
    pallas_call x1, Pallas kernels, ffn_fwd(): pl.pallas_call(functools.partial(ffn_fwd_kernel, tile, [plan for plan, _...  47.9 us
    ppermute x2, waiting for transfers between devices, z_gather(): one = lax.ppermute(block, 'tp', Z_UP)  42 us
    pallas_call x2, Pallas kernels, attn_bwd(): pl.pallas_call(functools.partial(attn_bwd_kernel, width, hd), grid_spec=p...  32.2 us
  transfers between devices with their start and end apart: 97, of which 35 were waited for; matrix products, arithmetic and copies ran while one was open for 16% of the time, Pallas kernels for 18%

profile of v3, /device:TPU:0, one launch (start us, length us, event | category | flops | bytes accessed | tf_op | source)
XLA Modules:
  0.0 992.2 jit_solution(8729028318808288828)
XLA Ops:
  46.6 37.6 %collective-permute-start.10 = (bf16[256,768]{1,0:T(8,128)(2,1)S(1)}, bf16[256,768]{1,0:T(8,128)(2,1)S(1)}, u32[]{:S(2)}, u32[]{:S(2)}) collective-permute-start(bf16[256,768]{1,0:T(8,128)(2,1)S(1)} %collective-permute-done.9), channel_id=1, source_target_pairs={{0,16},{16,0},{8,24},{24,8},{1,17},{17,1},{9,25},{25,9},{2,18},{18... | collective-permute-start | bytes 1179656 | tf_op jit(solution)/shard_map/ppermute | solution.py:1363
  105.9 21.1 %collective-permute-done.18.got_ref = bf16[512,1024]{1,0:T(8,128)(2,1)S(1)} collective-permute-done((bf16[512,1024]{1,0:T(8,128)(2,1)S(1)}, bf16[512,1024]{1,0:T(8,128)(2,1)S(1)}, u32[]{:S(2)}, u32[]{:S(2)}) %collective-permute-start.18) | collective-permute-done | bytes 1048608 | tf_op jit(solution)/shard_map/ppermute | solution.py:1369
  135.4 13.9 %attn_fwd.3 = (bf16[1024,256]{1,0:T(8,128)(2,1)S(1)}, bf16[1024,256]{1,0:T(8,128)(2,1)S(1)}, f32[2,2,2048]{2,1,0:T(2,128)S(1)}) custom-call(s32[4]{0:T(128)S(1)} %pad_add_fusion.info, bf16[512,1024]{1,0:T(8,128)(2,1)S(1)} %get-tuple-element.102.mine_ref, bf16[512,1024]{1,0:T(8,128)(2,1)S(1)} %collective-permute-done.18.got_ref), custom_call_target="tpu_custom_call" | custom-call | flops 33554432 | bytes 32768 | tf_op jit(solution)/shard_map/attn_fwd/pallas_call | solution.py:716
  150.9 13.9 %attn_fwd.2 = (bf16[1024,256]{1,0:T(8,128)(2,1)S(1)}, bf16[1024,256]{1,0:T(8,128)(2,1)S(1)}, f32[2,2,2048]{2,1,0:T(2,128)S(1)}) custom-call(s32[4]{0:T(128)S(1)} %pad_add_fusion.info, bf16[512,1024]{1,0:T(8,128)(2,1)S(1)} %get-tuple-element.99.mine_ref, bf16[512,1024]{1,0:T(8,128)(2,1)S(1)} %collective-permute-done.17.got_ref), custom_call_target="tpu_custom_call" | custom-call | flops 33554432 | bytes 32768 | tf_op jit(solution)/shard_map/attn_fwd/pallas_call | solution.py:716
  165.7 18.0 %collective-permute-start.38 = (bf16[256,1152]{1,0:T(8,128)(2,1)S(1)}, bf16[256,1152]{1,0:T(8,128)(2,1)}, u32[]{:S(2)}, u32[]{:S(2)}) collective-permute-start(bf16[256,1152]{1,0:T(8,128)(2,1)S(1)} %get-tuple-element.234), channel_id=1, source_target_pairs={{0,1},{1,2},{2,3},{3,0},{4,5},{5,6},{6,7},{7,4},{8,9},{9,10},{10,1... | collective-permute-start | bytes 1769480 | tf_op jit(solution)/shard_map/ppermute | solution.py:1410
  199.0 11.2 %collective-permute-done.39.rest_19_.rest_1_ = bf16[256,1152]{1,0:T(8,128)(2,1)S(1)} collective-permute-done((bf16[256,1152]{1,0:T(8,128)(2,1)S(1)}, bf16[256,1152]{1,0:T(8,128)(2,1)S(1)}, u32[]{:S(2)}, u32[]{:S(2)}) %collective-permute-start.39) | collective-permute-done | bytes 589856 | tf_op jit(solution)/shard_map/ppermute | solution.py:1410
  225.8 38.8 %collective-permute-done.41.rest_21_.rest_3_ = bf16[256,1152]{1,0:T(8,128)(2,1)} collective-permute-done((bf16[256,1152]{1,0:T(8,128)(2,1)}, bf16[256,1152]{1,0:T(8,128)(2,1)}, u32[]{:S(2)}, u32[]{:S(2)}) %collective-permute-start.41) | collective-permute-done | bytes 589856 | tf_op jit(solution)/shard_map/ppermute | solution.py:1363
  298.1 11.5 %collective-permute-done.34.rest_14_.rest_2_ = bf16[256,1152]{1,0:T(8,128)(2,1)S(1)} collective-permute-done((bf16[256,1152]{1,0:T(8,128)(2,1)S(1)}, bf16[256,1152]{1,0:T(8,128)(2,1)S(1)}, u32[]{:S(2)}, u32[]{:S(2)}) %collective-permute-start.34) | collective-permute-done | bytes 589856 | tf_op jit(solution)/shard_map/ppermute | solution.py:1369
  329.3 47.9 %ffn_fwd.1 = (bf16[4,1024,2304]{2,1,0:T(8,128)(2,1)}, bf16[4,1024,1152]{2,1,0:T(8,128)(2,1)}, bf16[1024,1024]{1,0:T(8,128)(2,1)}, f32[1024,1024]{1,0:T(8,128)}, ...) custom-call(s32[4]{0:T(128)} %copy-done.57, f32[1]{0:T(128)} %bitcast.4.scale, ...), custom_call_target="tpu_custom_call" | custom-call | flops 113246208 | bytes 286720 | tf_op jit(solution)/shard_map/ffn_fwd/pallas_call | solution.py:1157
  377.2 25.6 %ffn_bwd.4 = (f32[1024,1024]{1,0:T(8,128)}, bf16[512,3456]{1,0:T(8,128)(2,1)}, bf16[512,3456]{1,0:T(8,128)(2,1)}) custom-call(bf16[1024,1024]{1,0:T(8,128)(2,1)} %get-tuple-element.118.low_ref, bf16[4,1024,2304]{2,1,0:T(8,128)(2,1)} %get-tuple-element.119.act_ref, bf16[4,1024,1152]{2,1,0:T(8,128)(2,1)} %get-tuple-element.120.hid_ref, ...), custom_call_target="tpu_custom_call" | custom-call | flops 56623104 | bytes 131072 | tf_op jit(solution)/shard_map/ffn_bwd/pallas_call | solution.py:1265
  403.2 26.5 %ffn_bwd.5 = (f32[1024,1024]{1,0:T(8,128)}, bf16[512,3456]{1,0:T(8,128)(2,1)}, bf16[512,3456]{1,0:T(8,128)(2,1)}) custom-call(bf16[1024,1024]{1,0:T(8,128)(2,1)} %get-tuple-element.118.low_ref, bf16[4,1024,2304]{2,1,0:T(8,128)(2,1)} %get-tuple-element.119.act_ref, ...), custom_call_target="tpu_custom_call", output_to_operand_aliasing={{0}: (11, {})} | custom-call | flops 56623104 | bytes 131072 | tf_op jit(solution)/shard_map/ffn_bwd/pallas_call | solution.py:1265
  439.1 36.7 %collective-permute-done.52 = bf16[256,3456]{1,0:T(8,128)(2,1)S(1)} collective-permute-done((bf16[256,3456]{1,0:T(8,128)(2,1)S(1)}, bf16[256,3456]{1,0:T(8,128)(2,1)S(1)}, u32[]{:S(2)}, u32[]{:S(2)}) %collective-permute-start.52) | collective-permute-done | bytes 1769504 | tf_op jit(solution)/shard_map/ppermute | solution.py:1363
  477.6 26.2 %ffn_bwd.6 = (f32[1024,1024]{1,0:T(8,128)}, bf16[512,3456]{1,0:T(8,128)(2,1)}, bf16[512,3456]{1,0:T(8,128)(2,1)}) custom-call(bf16[1024,1024]{1,0:T(8,128)(2,1)} %get-tuple-element.118.low_ref, bf16[4,1024,2304]{2,1,0:T(8,128)(2,1)} %get-tuple-element.119.act_ref, ...), custom_call_target="tpu_custom_call", output_to_operand_aliasing={{0}: (11, {})} | custom-call | flops 56623104 | bytes 131072 | tf_op jit(solution)/shard_map/ffn_bwd/pallas_call | solution.py:1265
  517.2 26.3 %ffn_bwd.7 = (f32[1024,1024]{1,0:T(8,128)}, bf16[512,3456]{1,0:T(8,128)(2,1)}, bf16[512,3456]{1,0:T(8,128)(2,1)}) custom-call(bf16[1024,1024]{1,0:T(8,128)(2,1)} %get-tuple-element.118.low_ref, bf16[4,1024,2304]{2,1,0:T(8,128)(2,1)} %get-tuple-element.119.act_ref, ...), custom_call_target="tpu_custom_call", output_to_operand_aliasing={{0}: (11, {})} | custom-call | flops 56623104 | bytes 131072 | tf_op jit(solution)/shard_map/ffn_bwd/pallas_call | solution.py:1265
  552.4 42.0 %collective-permute-done.62 = bf16[1024,1024]{1,0:T(8,128)(2,1)} collective-permute-done((bf16[1024,1024]{1,0:T(8,128)(2,1)}, bf16[1024,1024]{1,0:T(8,128)(2,1)}, u32[]{:S(2)}, u32[]{:S(2)}) %collective-permute-start.62) | collective-permute-done | bytes 2097184 | tf_op jit(solution)/shard_map/ppermute | solution.py:1306
  641.6 18.8 %collective-permute-done.61 = bf16[128,3456]{1,0:T(8,128)(2,1)} collective-permute-done((bf16[128,3456]{1,0:T(8,128)(2,1)}, bf16[128,3456]{1,0:T(8,128)(2,1)}, u32[]{:S(2)}, u32[]{:S(2)}) %collective-permute-start.61) | collective-permute-done | bytes 884768 | tf_op jit(solution)/shard_map/ppermute | solution.py:1369
  670.1 16.3 %attn_bwd.2 = (bf16[512,1024]{1,0:T(8,128)(2,1)S(1)}, bf16[512,1024]{1,0:T(8,128)(2,1)S(1)}) custom-call(s32[4]{0:T(128)S(1)} %copy-done.58, bf16[512,1024]{1,0:T(8,128)(2,1)S(1)} %copy-done.25, bf16[512,1024]{1,0:T(8,128)(2,1)S(1)} %copy-done.23, bf16[1024,256]{1,0:T(8,128)(2,1)S(1)} %copy-done.33, bf16[1024,256]{1,0:T(8,128)(2,1)S(1)} %copy-done.48, ...), custom_call_target="tpu_custom_call" | custom-call | flops 83886080 | bytes 49152 | tf_op jit(solution)/shard_map/attn_bwd/pallas_call | solution.py:870
  687.3 24.6 %collective-permute-start.93 = (bf16[128,3456]{1,0:T(8,128)(2,1)S(1)}, bf16[128,3456]{1,0:T(8,128)(2,1)S(1)}, u32[]{:S(2)}, u32[]{:S(2)}) collective-permute-start(bf16[128,3456]{1,0:T(8,128)(2,1)S(1)} %add_convert_fusion.15), channel_id=1, source_target_pairs={{0,3},{1,0},{2,1},{3,2},{4,7},{5,4},{6,5},{7,6},{8,11},{9,8},{10,9... | collective-permute-start | bytes 2654216 | tf_op jit(solution)/shard_map/ppermute | solution.py:1544
  712.3 15.9 %attn_bwd.3 = (bf16[512,1024]{1,0:T(8,128)(2,1)S(1)}, bf16[512,1024]{1,0:T(8,128)(2,1)S(1)}) custom-call(s32[4]{0:T(128)S(1)} %copy-done.58, bf16[512,1024]{1,0:T(8,128)(2,1)S(1)} %copy-done.21, bf16[512,1024]{1,0:T(8,128)(2,1)S(1)} %copy-done.19, bf16[1024,256]{1,0:T(8,128)(2,1)S(1)} %get-tuple-element.104.a1.ok_ref, bf16[1024,256]{1,0:T(8,128)(2,1)S(1)} %copy-done.46, ...), custom_call_target="tpu_custom_call" | custom-call | flops 83886080 | bytes 49152 | tf_op jit(solution)/shard_map/attn_bwd/pallas_call | solution.py:870
  730.3 21.2 %collective-permute-start.94 = (bf16[128,3456]{1,0:T(8,128)(2,1)}, bf16[128,3456]{1,0:T(8,128)(2,1)}, u32[]{:S(2)}, u32[]{:S(2)}) collective-permute-start(bf16[128,3456]{1,0:T(8,128)(2,1)} %add_convert_fusion.12), channel_id=1, source_target_pairs={{0,3},{1,0},{2,1},{3,2},{4,7},{5,4},{6,5},{7,6},{8,11},{9,8},{10,9... | collective-permute-start | bytes 2654216 | tf_op jit(solution)/shard_map/ppermute | solution.py:1580
  836.3 10.5 %collective-permute-done.91 = bf16[128,3456]{1,0:T(8,128)(2,1)} collective-permute-done((bf16[128,3456]{1,0:T(8,128)(2,1)}, bf16[128,3456]{1,0:T(8,128)(2,1)}, u32[]{:S(2)}, u32[]{:S(2)}) %collective-permute-start.91) | collective-permute-done | bytes 884768 | tf_op jit(solution)/shard_map/ppermute | solution.py:1369
  875.2 16.1 %collective-permute-done.82 = bf16[128,768]{0,1:T(8,128)(2,1)S(1)} collective-permute-done((bf16[128,768]{0,1:T(8,128)(2,1)S(1)}, bf16[128,768]{0,1:T(8,128)(2,1)S(1)}, u32[]{:S(2)}, u32[]{:S(2)}) %collective-permute-start.82) | collective-permute-done | bytes 196640 | tf_op jit(solution)/shard_map/ppermute | solution.py:1369
  902.8 16.6 %collective-permute-done.95 = bf16[128,3456]{1,0:T(8,128)(2,1)S(1)} collective-permute-done((bf16[128,3456]{1,0:T(8,128)(2,1)S(1)}, bf16[128,3456]{1,0:T(8,128)(2,1)S(1)}, u32[]{:S(2)}, u32[]{:S(2)}) %collective-permute-start.95) | collective-permute-done | bytes 884768 | tf_op jit(solution)/shard_map/ppermute | solution.py:1581
  946.1 22.7 %collective-permute-done.89 = f32[128,768]{0,1:T(8,128)S(1)} collective-permute-done((f32[128,768]{0,1:T(8,128)S(1)}, f32[128,768]{0,1:T(8,128)S(1)}, u32[]{:S(2)}, u32[]{:S(2)}) %collective-permute-start.89) | collective-permute-done | bytes 393248 | tf_op jit(solution)/shard_map/ppermute | solution.py:1369
  (663 shorter events, 425.4 us)
Async XLA Ops:
  36.5 47.8 %collective-permute-start.6 = (bf16[256,768]{1,0:T(8,128)(2,1)}, bf16[256,768]{1,0:T(8,128)(2,1)S(1)}, u32[]{:S(2)}, u32[]{:S(2)}) collective-permute-start(bf16[256,768]{1,0:T(8,128)(2,1)} %collective-permute-done.5), channel_id=1, source_target_pairs={{0,16},{16,0},{8,24},{24,8},{1,17},{17,1},{9,25},{25,9},{2,18},{18... | collective-permute-start | bytes 1179656 | tf_op jit(solution)/shard_map/ppermute | solution.py:1363
  38.1 46.1 %collective-permute-start.4 = (bf16[256,768]{1,0:T(8,128)(2,1)}, bf16[256,768]{1,0:T(8,128)(2,1)S(1)}, u32[]{:S(2)}, u32[]{:S(2)}) collective-permute-start(bf16[256,768]{1,0:T(8,128)(2,1)} %collective-permute-done.2), channel_id=1, source_target_pairs={{0,8},{8,0},{16,24},{24,16},{1,9},{9,1},{17,25},{25,17},{2,10},{10... | collective-permute-start | bytes 1179656 | tf_op jit(solution)/shard_map/ppermute | solution.py:1366
  39.1 125.8 %collective-permute-start.26 = (bf16[256,3456]{1,0:T(8,128)(2,1)S(1)}, bf16[256,3456]{1,0:T(8,128)(2,1)S(1)}, u32[]{:S(2)}, u32[]{:S(2)}) collective-permute-start(bf16[256,3456]{1,0:T(8,128)(2,1)S(1)} %copy-done.8), channel_id=1, source_target_pairs={{0,1},{1,2},{2,3},{3,0},{4,5},{5,6},{6,7},{7,4},{8,9},{9,10},{10,1... | collective-permute-start | bytes 5308424 | tf_op jit(solution)/shard_map/ppermute | solution.py:1407
  102.5 81.2 %collective-permute-start.32 = (bf16[256,3456]{1,0:T(8,128)(2,1)S(1)}, bf16[256,3456]{1,0:T(8,128)(2,1)S(1)}, u32[]{:S(2)}, u32[]{:S(2)}) collective-permute-start(bf16[256,3456]{1,0:T(8,128)(2,1)S(1)} %copy-done.8), channel_id=1, source_target_pairs={{0,3},{1,0},{2,1},{3,2},{4,7},{5,4},{6,5},{7,6},{8,11},{9,8},{10,9... | collective-permute-start | bytes 5308424 | tf_op jit(solution)/shard_map/ppermute | solution.py:1408
  102.5 81.3 %collective-permute-start.23 = (bf16[256,3456]{1,0:T(8,128)(2,1)S(1)}, bf16[256,3456]{1,0:T(8,128)(2,1)S(1)}, u32[]{:S(2)}, u32[]{:S(2)}) collective-permute-start(bf16[256,3456]{1,0:T(8,128)(2,1)S(1)} %copy-done.8), channel_id=1, source_target_pairs={{0,8},{8,0},{16,24},{24,16},{1,9},{9,1},{17,25},{25,17},{2,10},{10... | collective-permute-start | bytes 5308424 | tf_op jit(solution)/shard_map/ppermute | solution.py:1366
  197.5 70.3 %collective-permute-start.27 = (bf16[256,2304]{1,0:T(8,128)(2,1)}, bf16[256,2304]{1,0:T(8,128)(2,1)}, u32[]{:S(2)}, u32[]{:S(2)}) collective-permute-start(bf16[256,2304]{1,0:T(8,128)(2,1)} %slice.627), channel_id=1, source_target_pairs={{0,16},{16,0},{8,24},{24,8},{1,17},{17,1},{9,25},{25,9},{2,18},{18... | collective-permute-start | bytes 3538952 | tf_op jit(solution)/shard_map/ppermute | solution.py:1363
  210.1 58.2 %collective-permute-start.33 = (bf16[256,2304]{1,0:T(8,128)(2,1)}, bf16[256,2304]{1,0:T(8,128)(2,1)}, u32[]{:S(2)}, u32[]{:S(2)}) collective-permute-start(bf16[256,2304]{1,0:T(8,128)(2,1)} %slice.629), channel_id=1, source_target_pairs={{0,16},{16,0},{8,24},{24,8},{1,17},{17,1},{9,25},{25,9},{2,18},{18... | collective-permute-start | bytes 3538952 | tf_op jit(solution)/shard_map/ppermute | solution.py:1363
  220.1 44.5 %collective-permute-start.41 = (bf16[256,1152]{1,0:T(8,128)(2,1)}, bf16[256,1152]{1,0:T(8,128)(2,1)}, u32[]{:S(2)}, u32[]{:S(2)}) collective-permute-start(bf16[256,1152]{1,0:T(8,128)(2,1)} %collective-permute-done.38.rest_18_.rest_0_), channel_id=1, source_target_pairs={{0,16},{16,0},{8,24},{24,8},{1,17},{17,1},{9,25},{25,9},{2,18},{18... | collective-permute-start | bytes 1769480 | tf_op jit(solution)/shard_map/ppermute | solution.py:1363
  223.0 47.9 %collective-permute-start.42 = (bf16[256,1152]{1,0:T(8,128)(2,1)}, bf16[256,1152]{1,0:T(8,128)(2,1)S(1)}, u32[]{:S(2)}, u32[]{:S(2)}) collective-permute-start(bf16[256,1152]{1,0:T(8,128)(2,1)} %copy-done.95), channel_id=1, source_target_pairs={{0,16},{16,0},{8,24},{24,8},{1,17},{17,1},{9,25},{25,9},{2,18},{18... | collective-permute-start | bytes 1769480 | tf_op jit(solution)/shard_map/ppermute | solution.py:1363
  225.8 48.1 %collective-permute-start.44 = (bf16[256,1152]{1,0:T(8,128)(2,1)}, bf16[256,1152]{1,0:T(8,128)(2,1)S(1)}, u32[]{:S(2)}, u32[]{:S(2)}) collective-permute-start(bf16[256,1152]{1,0:T(8,128)(2,1)} %collective-permute-done.38.rest_18_.rest_0_), channel_id=1, source_target_pairs={{0,8},{8,0},{16,24},{24,16},{1,9},{9,1},{17,25},{25,17},{2,10},{10... | collective-permute-start | bytes 1769480 | tf_op jit(solution)/shard_map/ppermute | solution.py:1366
  438.8 74.4 %collective-permute-start.56 = (bf16[256,3456]{1,0:T(8,128)(2,1)}, bf16[256,3456]{1,0:T(8,128)(2,1)}, u32[]{:S(2)}, u32[]{:S(2)}) collective-permute-start(bf16[256,3456]{1,0:T(8,128)(2,1)} %add_convert_fusion.8), channel_id=1, source_target_pairs={{0,16},{16,0},{8,24},{24,8},{1,17},{17,1},{9,25},{25,9},{2,18},{18... | collective-permute-start | bytes 5308424 | tf_op jit(solution)/shard_map/ppermute | solution.py:1363
  543.5 51.7 %collective-permute-start.54 = (bf16[512,3456]{1,0:T(8,128)(2,1)}, bf16[512,3456]{1,0:T(8,128)(2,1)}, u32[]{:S(2)}, u32[]{:S(2)}) collective-permute-start(bf16[512,3456]{1,0:T(8,128)(2,1)} %get-tuple-element.139), channel_id=1, source_target_pairs={{0,8},{8,0},{16,24},{24,16},{1,9},{9,1},{17,25},{25,17},{2,10},{10... | collective-permute-start | bytes 10616840 | tf_op jit(solution)/shard_map/ppermute | solution.py:1366
  543.6 50.9 %collective-permute-start.62 = (bf16[1024,1024]{1,0:T(8,128)(2,1)}, bf16[1024,1024]{1,0:T(8,128)(2,1)}, u32[]{:S(2)}, u32[]{:S(2)}) collective-permute-start(bf16[1024,1024]{1,0:T(8,128)(2,1)} %get-tuple-element.163), channel_id=1, source_target_pairs={{0,1},{1,2},{2,3},{3,0},{4,5},{5,6},{6,7},{7,4},{8,9},{9,10},{10,1... | collective-permute-start | bytes 6291464 | tf_op jit(solution)/shard_map/ppermute | solution.py:1306
  549.6 49.4 %collective-permute-start.58 = (bf16[256,3456]{1,0:T(8,128)(2,1)}, bf16[256,3456]{1,0:T(8,128)(2,1)}, u32[]{:S(2)}, u32[]{:S(2)}) collective-permute-start(bf16[256,3456]{1,0:T(8,128)(2,1)} %add_convert_fusion.5), channel_id=1, source_target_pairs={{0,16},{16,0},{8,24},{24,8},{1,17},{17,1},{9,25},{25,9},{2,18},{18... | collective-permute-start | bytes 5308424 | tf_op jit(solution)/shard_map/ppermute | solution.py:1363
  551.4 253.3 %collective-permute-start.64 = (bf16[1024,1024]{1,0:T(8,128)(2,1)}, bf16[1024,1024]{1,0:T(8,128)(2,1)}, u32[]{:S(2)}, u32[]{:S(2)}) collective-permute-start(bf16[1024,1024]{1,0:T(8,128)(2,1)} %get-tuple-element.163), channel_id=1, source_target_pairs={{0,3},{1,0},{2,1},{3,2},{4,7},{5,4},{6,5},{7,6},{8,11},{9,8},{10,9... | collective-permute-start | bytes 6291464 | tf_op jit(solution)/shard_map/ppermute | solution.py:1307
  594.4 133.8 %collective-permute-start.65 = (bf16[1024,1024]{1,0:T(8,128)(2,1)}, bf16[1024,1024]{1,0:T(8,128)(2,1)}, u32[]{:S(2)}, u32[]{:S(2)}) collective-permute-start(bf16[1024,1024]{1,0:T(8,128)(2,1)} %collective-permute-done.62), channel_id=1, source_target_pairs={{0,1},{1,2},{2,3},{3,0},{4,5},{5,6},{6,7},{7,4},{8,9},{9,10},{10,1... | collective-permute-start | bytes 6291464 | tf_op jit(solution)/shard_map/ppermute | solution.py:1308
  618.7 47.3 %collective-permute-start.90 = (bf16[256,3456]{1,0:T(8,128)(2,1)}, bf16[256,3456]{1,0:T(8,128)(2,1)}, u32[]{:S(2)}, u32[]{:S(2)}) collective-permute-start(bf16[256,3456]{1,0:T(8,128)(2,1)} %add_convert_fusion.3), channel_id=1, source_target_pairs={{0,16},{16,0},{8,24},{24,8},{1,17},{17,1},{9,25},{25,9},{2,18},{18... | collective-permute-start | bytes 5308424 | tf_op jit(solution)/shard_map/ppermute | solution.py:1363
  619.9 50.2 %collective-permute-start.55 = (bf16[1024,256]{1,0:T(8,128)(2,1)}, bf16[1024,256]{1,0:T(8,128)(2,1)}, u32[]{:S(2)}, u32[]{:S(2)}) collective-permute-start(bf16[1024,256]{1,0:T(8,128)(2,1)} %get-tuple-element.141), channel_id=1, source_target_pairs={{0,4},{4,0},{1,5},{5,1},{2,6},{6,2},{3,7},{7,3},{8,12},{12,8},{9,1... | collective-permute-start | bytes 1572872 | tf_op jit(solution)/shard_map/ppermute | solution.py:1369
  730.3 170.7 %collective-permute-start.94 = (bf16[128,3456]{1,0:T(8,128)(2,1)}, bf16[128,3456]{1,0:T(8,128)(2,1)}, u32[]{:S(2)}, u32[]{:S(2)}) collective-permute-start(bf16[128,3456]{1,0:T(8,128)(2,1)} %add_convert_fusion.12), channel_id=1, source_target_pairs={{0,3},{1,0},{2,1},{3,2},{4,7},{5,4},{6,5},{7,6},{8,11},{9,8},{10,9... | collective-permute-start | bytes 2654216 | tf_op jit(solution)/shard_map/ppermute | solution.py:1580
  769.2 169.4 %collective-permute-start.71 = (bf16[1024,1024]{1,0:T(8,128)(2,1)}, bf16[1024,1024]{1,0:T(8,128)(2,1)}, u32[]{:S(2)}, u32[]{:S(2)}) collective-permute-start(bf16[1024,1024]{1,0:T(8,128)(2,1)} %get-tuple-element.162), channel_id=1, source_target_pairs={{0,1},{1,2},{2,3},{3,0},{4,5},{5,6},{6,7},{7,4},{8,9},{9,10},{10,1... | collective-permute-start | bytes 6291464 | tf_op jit(solution)/shard_map/ppermute | solution.py:1306
  778.3 53.0 %collective-permute-start.74 = (bf16[512,768]{0,1:T(8,128)(2,1)}, bf16[512,768]{0,1:T(8,128)(2,1)}, u32[]{:S(2)}, u32[]{:S(2)}) collective-permute-start(bf16[512,768]{0,1:T(8,128)(2,1)} %fusion.15), channel_id=1, source_target_pairs={{0,8},{8,0},{16,24},{24,16},{1,9},{9,1},{17,25},{25,17},{2,10},{10... | collective-permute-start | bytes 2359304 | tf_op jit(solution)/shard_map/ppermute | solution.py:1366
  834.9 108.7 %collective-permute-start.72 = (bf16[1024,1024]{1,0:T(8,128)(2,1)}, bf16[1024,1024]{1,0:T(8,128)(2,1)S(1)}, u32[]{:S(2)}, u32[]{:S(2)}) collective-permute-start(bf16[1024,1024]{1,0:T(8,128)(2,1)} %get-tuple-element.162), channel_id=1, source_target_pairs={{0,3},{1,0},{2,1},{3,2},{4,7},{5,4},{6,5},{7,6},{8,11},{9,8},{10,9... | collective-permute-start | bytes 6291464 | tf_op jit(solution)/shard_map/ppermute | solution.py:1307
  927.4 44.6 %collective-permute-start.96 = (f32[128,3456]{1,0:T(8,128)S(1)}, f32[128,3456]{1,0:T(8,128)}, u32[]{:S(2)}, u32[]{:S(2)}) collective-permute-start(f32[128,3456]{1,0:T(8,128)S(1)} %convert_add_fusion), channel_id=1, source_target_pairs={{0,4},{4,0},{1,5},{5,1},{2,6},{6,2},{3,7},{7,3},{8,12},{12,8},{9,1... | collective-permute-start | bytes 5308424 | tf_op jit(solution)/shard_map/ppermute | solution.py:1369
  938.6 48.2 %collective-permute-start.73 = (bf16[1024,1024]{1,0:T(8,128)(2,1)}, bf16[1024,1024]{1,0:T(8,128)(2,1)}, u32[]{:S(2)}, u32[]{:S(2)}) collective-permute-start(bf16[1024,1024]{1,0:T(8,128)(2,1)} %collective-permute-done.71), channel_id=1, source_target_pairs={{0,1},{1,2},{2,3},{3,0},{4,5},{5,6},{6,7},{7,4},{8,9},{9,10},{10,1... | collective-permute-start | bytes 6291464 | tf_op jit(solution)/shard_map/ppermute | solution.py:1308
  (211 other events, 3446.9 us)

commit v4 on v3

--- a/solution.py
+++ b/solution.py
@@ -411,13 +411,15 @@
     return pl.CostEstimate(flops=flops >> 8, bytes_accessed=bytes_accessed >> 8, transcendentals=0)
 
 
-def pack_kernel(info, q_ref, k_ref, v_ref, o_ref, g_ref, u_ref, d_ref, attn_ref, ffn_ref):
+def pack_kernel(info, o_in, g_in, u_in, d_in, out_ref, ffn_ref, o_ref, g_ref, u_ref, d_ref, sems):
     ctx = info[2]
-    q_cols, k_cols = q_ref.shape[1], k_ref.shape[1]
-    attn_ref[:, :q_cols] = q_ref[...]
-    attn_ref[:, q_cols : q_cols + k_cols] = k_ref[...]
-    attn_ref[:, q_cols + k_cols : q_cols + 2 * k_cols] = v_ref[...]
-    attn_ref[:, q_cols + 2 * k_cols :] = o_ref[...].astype(F32).T.astype(BF16)
+    pairs = ((o_in, o_ref), (g_in, g_ref), (u_in, u_ref), (d_in, d_ref))
+    copies = [pltpu.make_async_copy(a, b, sems.at[i]) for i, (a, b) in enumerate(pairs)]
+    for copy in copies:
+        copy.start()
+    for copy in copies:
+        copy.wait()
+    out_ref[...] = o_ref[...].astype(F32).T.astype(BF16)
     third = g_ref.shape[1] // 3
     for j in range(3):
         at = pl.multiple_of(jnp.where(ctx == 0, j, 2 - j) * third, third)
@@ -428,18 +430,19 @@
         ffn_ref[:, base + 2 * third : base + 3 * third] = down
 
 
-def pack(info, q, k, v, o, g, u, d):
-    rows = q.shape[0]
-    attn_cols = q.shape[1] + 2 * k.shape[1] + o.shape[0]
+def pack(info, o, g, u, d):
+    rows = g.shape[0]
     return pl.pallas_call(
         pack_kernel,
-        in_specs=[SMEM] + [pl.BlockSpec(memory_space=pltpu.VMEM)] * 7,
+        in_specs=[SMEM] + [ANY] * 4,
         out_specs=[pl.BlockSpec(memory_space=pltpu.VMEM)] * 2,
-        out_shape=[shape_of((rows, attn_cols), BF16), shape_of((rows, 3 * g.shape[1]), BF16)],
+        out_shape=[shape_of((rows, o.shape[0]), BF16), shape_of((rows, 3 * g.shape[1]), BF16)],
+        scratch_shapes=[pltpu.VMEM(a.shape, BF16) for a in (o, g, u, d)]
+        + [pltpu.SemaphoreType.DMA((4,))],
         compiler_params=pltpu.CompilerParams(vmem_limit_bytes=24 << 20),
         cost_estimate=cost(0, 6 << 20),
         name="pack",
-    )(info, q, k, v, o, g, u, d)
+    )(info, o, g, u, d)
 
 
 def norm_one_kernel(info, tok_ref, gain_ref, x_ref, nt_ref, x32):
@@ -478,11 +481,25 @@
     )(info, tokens, gain)
 
 
-def proj_kernel(heads, info, w_ref, nt_ref, cos_ref, sin_ref, qg_ref, kg_ref, rot_ref, raw_ref):
+def proj_kernel(heads, block, info, *refs):
+    pieces = [refs[4 * k : 4 * k + 4] for k in range(4)]
+    nt_ref, cos_ref, sin_ref, qg_ref, kg_ref, rot_ref, raw_ref, w_ref, sem = refs[16:]
+    rows = w_ref.shape[0] // 4
+
+    @pl.when(pl.program_id(0) == 0)
+    def _():
+        for k in range(4):
+
+            @pl.when(block(info) == k)
+            def _():
+                for p, piece in enumerate(pieces[k]):
+                    pltpu.make_async_copy(piece, w_ref.at[pl.ds(p * rows, rows)], sem).start()
+
+        pltpu.make_async_copy(w_ref, w_ref, sem).wait()
+
     hd = qg_ref.shape[0]
-    tok = nt_ref.shape[1]
     half = hd // 2
-    raw = dot(w_ref[0], nt_ref[...], 0, 0)
+    raw = dot(w_ref[...], nt_ref[...], 0, 0)
     cos_part, sin_part = cos_ref[...], sin_ref[...]
     heads_q, heads_k = heads
     raw_ref[...] = raw.astype(BF16)
@@ -497,32 +514,27 @@
     rot_ref[at:, :] = raw[at:].astype(BF16)
 
 
-def project(info, w_proj, normed_t, cos_part, sin_part, gain_q, gain_k, heads, block):
-    _, width, cols = w_proj.shape
-    tok = normed_t.shape[1]
+def project(info, pieces, normed_t, cos_part, sin_part, gain_q, gain_k, heads, block):
+    width, tok = normed_t.shape
+    cols = pieces[0][0].shape[1]
     tile = min(512, tok)
     const = lambda a: pl.BlockSpec(a.shape, lambda i, info: (0, 0))
     tab = lambda a: pl.BlockSpec((a.shape[0], tile), lambda i, info: (0, i))
     return pl.pallas_call(
-        functools.partial(proj_kernel, heads),
+        functools.partial(proj_kernel, heads, block),
         grid_spec=pltpu.PrefetchScalarGridSpec(
             num_scalar_prefetch=1,
             grid=(tok // tile,),
-            in_specs=[
-                pl.BlockSpec((1, width, cols), lambda i, info: (block(info), 0, 0)),
-                tab(normed_t),
-                tab(cos_part),
-                tab(sin_part),
-                const(gain_q),
-                const(gain_k),
-            ],
+            in_specs=[ANY] * 16
+            + [tab(normed_t), tab(cos_part), tab(sin_part), const(gain_q), const(gain_k)],
             out_specs=[pl.BlockSpec((cols, tile), lambda i, info: (0, i))] * 2,
+            scratch_shapes=[pltpu.VMEM((width, cols), BF16), pltpu.SemaphoreType.DMA],
         ),
         out_shape=[shape_of((cols, tok), BF16), shape_of((cols, tok), BF16)],
         compiler_params=settings(1, 24),
         cost_estimate=cost(2 * width * cols * tok, 6 << 20),
         name="project",
-    )(info, w_proj, normed_t, cos_part, sin_part, gain_q, gain_k)
+    )(info, *[p for b in pieces for p in b], normed_t, cos_part, sin_part, gain_q, gain_k)
 
 
 def head_back_kernel(
@@ -898,7 +910,20 @@
     )(info, mine, got, out_keep, out_send, grad_keep, grad_send, lse)
 
 
-def out_proj_kernel(info, x_ref, a0, a1, b0, b1, w_ref, gain_ref, r_ref, n_ref, nt_ref, att_ref):
+def load_blocks(pieces, target, sem):
+    rows = target.shape[1] // 4
+
+    @pl.when(pl.program_id(0) == 0)
+    def _():
+        for i, piece in enumerate(pieces):
+            block = target.at[i // 4, pl.ds(i % 4 * rows, rows)]
+            pltpu.make_async_copy(piece, block, sem).start()
+        pltpu.make_async_copy(target, target, sem).wait()
+
+
+def out_proj_kernel(info, *refs):
+    x_ref, a0, a1, b0, b1, gain_ref, r_ref, n_ref, nt_ref, att_ref, w_ref, sem = refs[16:]
+    load_blocks(refs[:16], w_ref, sem)
     ctx = info[2]
     total = x_ref[...].astype(F32)
     for j, ref, side in ((0, a0, ctx), (1, a1, ctx), (0, b0, 1 - ctx), (1, b1, 1 - ctx)):
@@ -913,24 +938,26 @@
     nt_ref[...] = normed.T.astype(BF16)
 
 
-def out_proj(info, x, mine, theirs, w_out, gain, tile):
+def out_proj(info, x, mine, theirs, pieces, gain, tile):
     tok, width = x.shape
-    feats = w_out.shape[2]
+    feats = pieces[0][0].shape[1]
     rows_of = lambda n: pl.BlockSpec((tile, n), lambda i, info: (i, 0))
     return pl.pallas_call(
         out_proj_kernel,
         grid_spec=pltpu.PrefetchScalarGridSpec(
             num_scalar_prefetch=1,
             grid=(tok // tile,),
-            in_specs=[rows_of(width)]
+            in_specs=[ANY] * 16
+            + [rows_of(width)]
             + [rows_of(feats)] * 4
-            + [whole(w_out.shape), pl.BlockSpec((1, width), lambda i, info: (0, 0))],
+            + [pl.BlockSpec((1, width), lambda i, info: (0, 0))],
             out_specs=[
                 rows_of(width),
                 rows_of(width),
                 pl.BlockSpec((width, tile), lambda i, info: (0, i)),
                 pl.BlockSpec((4, tile, feats), lambda i, info: (0, i, 0)),
             ],
+            scratch_shapes=[pltpu.VMEM((4, width, feats), BF16), pltpu.SemaphoreType.DMA],
         ),
         out_shape=[
             shape_of((tok, width), F32),
@@ -941,12 +968,12 @@
         compiler_params=settings(1, 32),
         cost_estimate=cost(2 * tok * width * 4 * feats, 16 << 20),
         name="out_proj",
-    )(info, x, *mine, *theirs, w_out, gain)
-
-
-def norm_two_back_kernel(
-    info, g_ref, r_ref, gr_ref, gain_ref, w_ref, gres_ref, gat_ref, a0, a1, b0, b1, gg_ref
-):
+    )(info, *[p for b in pieces for p in b], x, *mine, *theirs, gain)
+
+
+def norm_two_back_kernel(info, *refs):
+    g_ref, r_ref, gr_ref, gain_ref, gres_ref, gat_ref, a0, a1, b0, b1, gg_ref, w_ref, sem = refs[16:]
+    load_blocks(refs[:16], w_ref, sem)
     ctx = info[2]
     grad, resid = g_ref[...], r_ref[...]
     rho = lax.rsqrt(jnp.mean(resid * resid, axis=-1, keepdims=True) + EPS)
@@ -967,9 +994,9 @@
         ref[...] = dot(low, w_ref[2 * side + j], 1, 0).astype(BF16)
 
 
-def norm_two_back(info, grad, resid, grad_result, gain, w_out, tile):
+def norm_two_back(info, grad, resid, grad_result, gain, pieces, tile):
     tok, width = grad.shape
-    feats = w_out.shape[2]
+    feats = pieces[0][0].shape[1]
     rows_of = lambda n: pl.BlockSpec((tile, n), lambda i, info: (i, 0))
     row = pl.BlockSpec((1, width), lambda i, info: (0, 0))
     return pl.pallas_call(
@@ -977,10 +1004,11 @@
         grid_spec=pltpu.PrefetchScalarGridSpec(
             num_scalar_prefetch=1,
             grid=(tok // tile,),
-            in_specs=[rows_of(width)] * 3 + [row, whole(w_out.shape)],
+            in_specs=[ANY] * 16 + [rows_of(width)] * 3 + [row],
             out_specs=[rows_of(width), pl.BlockSpec((width, tile), lambda i, info: (0, i))]
             + [rows_of(feats)] * 4
             + [row],
+            scratch_shapes=[pltpu.VMEM((4, width, feats), BF16), pltpu.SemaphoreType.DMA],
         ),
         out_shape=[shape_of((tok, width), F32), shape_of((width, tok), BF16)]
         + [shape_of((tok, feats), BF16)] * 4
@@ -988,10 +1016,12 @@
         compiler_params=settings(1, 32),
         cost_estimate=cost(2 * tok * width * 4 * feats, 24 << 20),
         name="norm_two_back",
-    )(info, grad, resid, grad_result, gain, w_out)
-
-
-def norm_one_back_kernel(info, p0, p1, w_ref, x_ref, gres_ref, gain_ref, out_ref, gg_ref):
+    )(info, *[p for b in pieces for p in b], grad, resid, grad_result, gain)
+
+
+def norm_one_back_kernel(info, *refs):
+    p0, p1, x_ref, gres_ref, gain_ref, out_ref, gg_ref, w_ref, sem = refs[16:]
+    load_blocks(refs[:16], w_ref, sem)
     quarter = x_ref.shape[1] // 4
     grad = dot(p0[0], w_ref[0], 1, 1)
     grad = grad + dot(p1[0], w_ref[1], 1, 1)
@@ -1014,9 +1044,9 @@
     gg_ref[...] += jnp.sum(grad * unit, axis=0, keepdims=True)
 
 
-def norm_one_back(info, pairs, w_proj, x, grad_resid, gain, tile):
+def norm_one_back(info, pairs, pieces, x, grad_resid, gain, tile):
     tok, width = x.shape
-    cols = w_proj.shape[2]
+    cols = pieces[0][0].shape[1]
     rows_of = lambda n: pl.BlockSpec((tile, n), lambda i, info: (i, 0))
     pair = pl.BlockSpec((2, tile, cols), lambda i, info: (0, i, 0))
     row = pl.BlockSpec((1, width), lambda i, info: (0, 0))
@@ -1025,14 +1055,15 @@
         grid_spec=pltpu.PrefetchScalarGridSpec(
             num_scalar_prefetch=1,
             grid=(tok // tile,),
-            in_specs=[pair, pair, whole(w_proj.shape), rows_of(width), rows_of(width), row],
+            in_specs=[ANY] * 16 + [pair, pair, rows_of(width), rows_of(width), row],
             out_specs=[rows_of(width), row],
+            scratch_shapes=[pltpu.VMEM((4, width, cols), BF16), pltpu.SemaphoreType.DMA],
         ),
         out_shape=[shape_of((tok, width), BF16), shape_of((1, width), F32)],
         compiler_params=settings(1, 32),
         cost_estimate=cost(2 * tok * width * 4 * cols, 18 << 20),
         name="norm_one_back",
-    )(info, *pairs, w_proj, x, grad_resid, gain)
+    )(info, *[p for b in pieces for p in b], *pairs, x, grad_resid, gain)
 
 
 def weight_copies(plan, pieces, gate_up, down, gate_up_sem, down_sem):
@@ -1066,24 +1097,22 @@
     return [(part(0), part(1)), (part(2), part(3)), (part(4), part(5))]
 
 
-def ffn_fwd_kernel(
-    tile,
-    plans,
-    info,
-    scale,
-    x_ref,
-    resid_ref,
-    teach_ref,
-    *rest,
-):
+def ffn_fwd_kernel(tile, plans, last, info, scale, x_ref, in_ref, *rest):
+    if last:
+        teach_ref, rest = rest[0], rest[1:]
     pieces = []
     for plan in plans:
         count = 1 + max(piece for chunks in plan for piece, _ in chunks)
         pieces.append(rest[:count])
         rest = rest[count:]
-    act_ref, hid_ref, out_ref, gres_ref, low_ref, lowt_ref, sq_ref = rest[:7]
-    gate_up, down, total, sems = rest[7:]
+    act_ref, hid_ref = rest[:2]
+    if last:
+        out_ref, gres_ref, low_ref, lowt_ref, sq_ref = rest[2:7]
+        gate_up, down, total, sems = rest[7:]
+    else:
+        sum_ref, gate_up, down, total, sems = rest[2:]
     step, part = pl.program_id(0), pl.program_id(1)
+    final = len(plans) - 1
     width = x_ref.shape[1]
     quarter = width // 4
     third = down.shape[2] // 3
@@ -1095,12 +1124,12 @@
 
     @pl.when((step == 0) & (part == 0))
     def _():
-        for s in range(4):
+        for s in range(len(plans)):
             wide, thin = copies(s)
             for copy in wide + thin:
                 copy.start()
 
-    for s in range(4):
+    for s in range(len(plans)):
 
         @pl.when((step == s) & (part == 0))
         def _():
@@ -1116,16 +1145,18 @@
 
     @pl.when(step == 0)
     def _():
-        total[rows, :] = resid_ref[rows, :] + grown
-
-    @pl.when((step > 0) & (step < 3))
+        total[rows, :] = in_ref[...] + grown
+
+    @pl.when(step > 0)
     def _():
         total[rows, :] += grown
 
-    @pl.when(step == 3)
-    def _():
-        result = total[rows, :] + grown
-        total[rows, :] = result
+    @pl.when(step == final)
+    def _():
+        result = total[rows, :]
+        if not last:
+            sum_ref[...] = result
+            return
         tok = x_ref.shape[0]
         slot = info[2] * tok + part * tile + lax.broadcasted_iota(jnp.int32, (tile, 1), 0)
         valid = jnp.where(slot < info[3], 1.0, 0.0)
@@ -1149,52 +1180,62 @@
         sq_ref[...] += jnp.sum(square, axis=0, keepdims=True)
 
 
-def ffn_fwd(info, scale, x, resid, teacher, weights, units, tile):
+def ffn_fwd(info, scale, x, total, teacher, weights, units, tile):
     tok, width = x.shape
     pieces = [piece for _, group in weights for piece in group]
-    last = lambda s, i: jnp.where(s == 3, i, 0)
-    tiles = lambda n: pl.BlockSpec((tile, n), lambda s, i, info: (last(s, i), 0))
-    return pl.pallas_call(
-        functools.partial(ffn_fwd_kernel, tile, [plan for plan, _ in weights]),
-        grid_spec=pltpu.PrefetchScalarGridSpec(
-            num_scalar_prefetch=1,
-            grid=(4, tok // tile),
-            in_specs=[
-                SMEM,
-                whole((tok, width)),
-                whole((tok, width)),
-                pl.BlockSpec((1, tile, width), lambda s, i, info: (info[0], last(s, i), 0)),
-            ]
-            + [ANY] * len(pieces),
-            out_specs=[
-                pl.BlockSpec((1, tile, 2 * units), lambda s, i, info: (s, i, 0)),
-                pl.BlockSpec((1, tile, units), lambda s, i, info: (s, i, 0)),
-                tiles(width),
-                tiles(width),
-                tiles(width),
-                pl.BlockSpec((width, tile), lambda s, i, info: (0, last(s, i))),
-                pl.BlockSpec((1, width // 4), lambda s, i, info: (0, 0)),
-            ],
-            scratch_shapes=[
-                pltpu.VMEM((4, width, 2 * units), BF16),
-                pltpu.VMEM((4, width, units), BF16),
-                pltpu.VMEM((tok, width), F32),
-                pltpu.SemaphoreType.DMA((4, 2)),
-            ],
-        ),
-        out_shape=[
-            shape_of((4, tok, 2 * units), BF16),
-            shape_of((4, tok, units), BF16),
+    count = len(weights)
+    last = teacher is not None
+    entry = lambda s, i: jnp.where(s == 0, i, tok // tile - 1)
+    leave = lambda s, i: jnp.where(s == count - 1, i, 0)
+    tiles = lambda n: pl.BlockSpec((tile, n), lambda s, i, info: (leave(s, i), 0))
+    slab = lambda n: pl.BlockSpec((1, tile, n), lambda s, i, info: (s, i, 0))
+    in_specs = [
+        SMEM,
+        whole((tok, width)),
+        pl.BlockSpec((tile, width), lambda s, i, info: (entry(s, i), 0)),
+    ]
+    out_specs = [slab(2 * units), slab(units)]
+    out_shape = [shape_of((count, tok, 2 * units), BF16), shape_of((count, tok, units), BF16)]
+    if last:
+        in_specs.append(
+            pl.BlockSpec((1, tile, width), lambda s, i, info: (info[0], leave(s, i), 0))
+        )
+        out_specs += [
+            tiles(width),
+            tiles(width),
+            tiles(width),
+            pl.BlockSpec((width, tile), lambda s, i, info: (0, leave(s, i))),
+            pl.BlockSpec((1, width // 4), lambda s, i, info: (0, 0)),
+        ]
+        out_shape += [
             shape_of((tok, width), BF16),
             shape_of((tok, width), F32),
             shape_of((tok, width), BF16),
             shape_of((width, tok), BF16),
             shape_of((1, width // 4), F32),
-        ],
-        compiler_params=settings(2, 61),
-        cost_estimate=cost(2 * tok * width * units * 12, 70 << 20),
+        ]
+    else:
+        out_specs.append(tiles(width))
+        out_shape.append(shape_of((tok, width), F32))
+    return pl.pallas_call(
+        functools.partial(ffn_fwd_kernel, tile, [plan for plan, _ in weights], last),
+        grid_spec=pltpu.PrefetchScalarGridSpec(
+            num_scalar_prefetch=1,
+            grid=(count, tok // tile),
+            in_specs=in_specs + [ANY] * len(pieces),
+            out_specs=out_specs,
+            scratch_shapes=[
+                pltpu.VMEM((count, width, 2 * units), BF16),
+                pltpu.VMEM((count, width, units), BF16),
+                pltpu.VMEM((tok, width), F32),
+                pltpu.SemaphoreType.DMA((count, 2)),
+            ],
+        ),
+        out_shape=out_shape,
+        compiler_params=settings(2, 50),
+        cost_estimate=cost(2 * tok * width * units * 3 * count, 20 << 20),
         name="ffn_fwd",
-    )(info, scale, x, resid, teacher, *pieces)
+    )(info, scale, x, total, *([teacher] if last else []), *pieces)
 
 
 def ffn_bwd_kernel(steps, plan, first, low_ref, act_ref, hid_ref, xt_ref, lowt_ref, *rest):
@@ -1251,8 +1292,9 @@
         weight_rows(keep_ref)
 
 
-def ffn_bwd(block, low, acts, hiddens, weights, total, xt, lowt, tile):
+def ffn_bwd(low, saved, weights, total, xt, lowt, tile):
     plan, pieces = weights
+    acts, hiddens, block = saved
     tok, width = low.shape
     units = hiddens.shape[2]
     steps = tok // tile
@@ -1298,31 +1340,83 @@
     )(low, acts, hiddens, xt, lowt, *pieces, *([] if first else [total]))
 
 
-def after(value, *others):
-    return lax.optimization_barrier((value,) + others)[0]
-
-
-def z_gather(block):
-    one = lax.ppermute(block, "tp", Z_UP)
-    three = lax.ppermute(block, "tp", Z_DOWN)
-    two = lax.ppermute(one, "tp", Z_UP)
-    return [block, one, two, three]
-
-
-def add(left, right):
-    return left.astype(F32) + right.astype(F32)
-
-
-def add_low(left, right):
-    return add(left, right).astype(BF16)
-
-
 def turn_chunks(block):
     wide = block.shape[1] * 2 // 9
     thin = wide // 2
     starts = [(2 * wide, wide), (wide, wide), (0, wide)]
     starts += [(3 * wide + 2 * thin, thin), (3 * wide + thin, thin), (3 * wide, thin)]
     return jnp.concatenate([block[:, a : a + n] for a, n in starts], axis=1)
+
+
+def sum_kernel(side, turn, info, left_ref, right_ref, *outs):
+    right = right_ref[...]
+    if turn:
+        right = turn_chunks(right)
+    total = (left_ref[...].astype(F32) + right.astype(F32)).astype(BF16)
+    if len(outs) == 1:
+        outs[0][...] = total
+        return
+    first = side(pl.program_id(0), info) == 0
+
+    @pl.when(first)
+    def _():
+        outs[0][...] = total
+
+    @pl.when(jnp.logical_not(first))
+    def _():
+        outs[1][...] = total
+
+
+def summed(info, left, right, how, turn=False):
+    rows, cols = left.shape
+    count = rows // 128
+    block = lambda at: pl.BlockSpec((128, cols), at)
+    if how == "all":
+        side, places = None, [lambda i, info: (i, 0)]
+    elif how == "halves":
+        half = count // 2
+        side = lambda i, info: i // half
+        places = [
+            lambda i, info: (jnp.minimum(i, half - 1), 0),
+            lambda i, info: (jnp.maximum(i - half, 0), 0),
+        ]
+    else:
+        side = lambda i, info: jnp.bitwise_xor(i % 2, info[2])
+        places = [lambda i, info: (i // 2, 0)] * 2
+    shapes = [shape_of((rows // len(places), cols), BF16)] * len(places)
+    out = pl.pallas_call(
+        functools.partial(sum_kernel, side, turn),
+        grid_spec=pltpu.PrefetchScalarGridSpec(
+            num_scalar_prefetch=1,
+            grid=(count,),
+            in_specs=[block(lambda i, info: (i, 0))] * 2,
+            out_specs=[block(at) for at in places],
+        ),
+        out_shape=shapes,
+        compiler_params=settings(1, 24),
+        cost_estimate=cost(0, 4 << 20),
+        name="summed",
+    )(info, left, right)
+    return out[0] if len(places) == 1 else out
+
+
+def after(value, *others):
+    return lax.optimization_barrier((value,) + others)[0]
+
+
+def z_gather(block):
+    one = lax.ppermute(block, "tp", Z_UP)
+    three = lax.ppermute(block, "tp", Z_DOWN)
+    two = lax.ppermute(one, "tp", Z_UP)
+    return [block, one, two, three]
+
+
+def add(left, right):
+    return left.astype(F32) + right.astype(F32)
+
+
+def add_low(left, right):
+    return add(left, right).astype(BF16)
 
 
 def z_reduce(parts):
@@ -1371,9 +1465,8 @@
     length = lax.dynamic_slice_in_dim(lengths, z, 1, 0)
     info = jnp.concatenate([jnp.stack([z, fsdp, ctx]).astype(jnp.int32), length])
 
-    w_attn, w_ffn = pack(
-        info, q_weight, k_weight, v_weight, o_weight, gate_weight, up_weight, down_weight
-    )
+    w_proj = jnp.concatenate([q_weight, k_weight, v_weight], axis=1)
+    w_out, w_ffn = pack(info, o_weight, gate_weight, up_weight, down_weight)
     count_here = jnp.sum(lengths).astype(F32)[None]
     vector = jnp.concatenate([attn_gain, ffn_gain, q_gain, k_gain]).astype(F32)
     vector = jnp.concatenate([vector, count_here, jnp.zeros((640 - 545,), F32)])[None]
@@ -1382,48 +1475,42 @@
     gain_one = vector[:, :quarter].reshape(1, width)
     gain_two = vector[:, quarter : 2 * quarter].reshape(1, width)
     total_count = jnp.sum(vector[:, 544])
-    head_gains = vector[:, 2 * quarter : 544]
-    head_gains = jnp.where(fsdp // 2 == 0, head_gains, head_gains[jnp.array([1, 0, 3, 2])])
-    head_gains = jnp.where(fsdp % 2 == 0, head_gains, head_gains[jnp.array([2, 3, 0, 1])])
-    head_gains = head_gains[jnp.array([0, 2, 1, 3])]
+
+    def natural(v):
+        v = jnp.concatenate([v[0:1], v[2:3], v[1:2], v[3:4]], axis=0)
+        v = jnp.where(fsdp % 2 == 0, v, jnp.concatenate([v[1:2], v[0:1], v[3:4], v[2:3]], axis=0))
+        return jnp.where(fsdp // 2 == 0, v, jnp.concatenate([v[2:4], v[0:2]], axis=0))
+
+    head_gains = natural(vector[:, 2 * quarter : 544])
     gain_q = head_gains[:, : hd // 4].reshape(hd, 1)
     gain_k = head_gains[:, hd // 4 :].reshape(hd, 1)
 
-    attn_blocks = [
-        w_attn,
-        lax.ppermute(w_attn, "tp", Z_UP),
-        lax.ppermute(w_attn, "tp", Z_FAR),
-        lax.ppermute(w_attn, "tp", Z_DOWN),
-    ]
-    attn_pieces = []
-    for block in attn_blocks:
-        far = x_swap(block)
-        attn_pieces.append([block, far, core_swap(block), core_swap(far)])
-    w_proj = jnp.concatenate([p[:, :proj] for b in attn_pieces for p in b], axis=0)
-    w_proj = w_proj.reshape(4, width, proj)
-    w_out = jnp.concatenate([p[:, proj:] for b in attn_pieces for p in b], axis=0)
-    w_out = w_out.reshape(4, width, q_cols)
-
-    ffn_one = lax.ppermute(after(w_ffn, attn_blocks[1]), "tp", Z_UP)
-    ffn_three = lax.ppermute(after(w_ffn, attn_blocks[3]), "tp", Z_DOWN)
-    ffn_two = [
-        lax.ppermute(ffn_one[:, j * units : (j + 1) * units], "tp", Z_UP) for j in range(3)
-    ]
+    def z_direct(block):
+        return [
+            block,
+            lax.ppermute(block, "tp", Z_UP),
+            lax.ppermute(block, "tp", Z_FAR),
+            lax.ppermute(block, "tp", Z_DOWN),
+        ]
+
+    def plane_pieces(blocks):
+        pieces = []
+        for block in blocks:
+            far = x_swap(block)
+            pieces.append([block, far, core_swap(block), core_swap(far)])
+        return pieces
+
+    proj_blocks = z_direct(w_proj)
+    proj_pieces = plane_pieces(proj_blocks)
+    out_pieces = plane_pieces(z_direct(after(w_out, *proj_blocks[1:])))
+    ffn_one = lax.ppermute(after(w_ffn, *proj_blocks[1:]), "tp", Z_UP)
     in_block = lambda i: [(i, 0), (i, units), (i, 2 * units)]
     in_pair = lambda i: [(i, 0), (i, units), (i + 1, 0)]
     plan_whole = [in_block(0), in_pair(1), in_block(3), in_pair(4)]
     plan_chunks = [[(3 * p + j, 0) for j in range(3)] for p in range(4)]
 
-    def ffn_pieces(block, then):
-        far = x_swap(block[:, : 2 * units])
-        last = y_swap(after(far[:, :units], then))
-        return [block, far, last, core_swap(block), core_swap(far), core_swap(last)]
-
-    def ffn_chunks(blocks, then):
-        far = [x_swap(blocks[0]), x_swap(blocks[1])]
-        far.append(y_swap(after(far[0], then)))
-        pieces = blocks + far
-        return pieces + [core_swap(p) for p in pieces]
+    def ffn_pieces(block, far, last):
+        return plan_whole, [block, far, last, core_swap(block), core_swap(far), core_swap(last)]
 
     x_in, normed_one_t = norm_one(info, tokens, gain_one, 256)
     pos = (ctx * tok + jnp.arange(tok, dtype=jnp.int32)).astype(F32)
@@ -1432,29 +1519,56 @@
     tables = (jnp.cos(angles), jnp.sin(angles), gain_q, gain_k)
 
     def make(block):
-        return project(info, w_proj, normed_one_t, *tables, heads, block)
+        return project(info, proj_pieces, normed_one_t, *tables, heads, block)
+
+    far_of = lambda block: x_swap(block[:, : 2 * units])
+    near = lambda far: far[:, :units]
+    own_ffn = after(w_ffn, *[b[1] for b in proj_pieces])
+    far0 = far_of(own_ffn)
+    weights0 = ffn_pieces(own_ffn, far0, y_swap(near(far0)))
 
     theirs = [make(lambda s: 2 * (1 - s[2])), make(lambda s: 2 * (1 - s[2]) + 1)]
     got = [y_swap(theirs[0][0]), y_swap(theirs[1][0])]
     mine = [make(lambda s: 2 * s[2]), make(lambda s: 2 * s[2] + 1)]
 
-    outs = [attn_fwd(info, mine[j][0], got[j], hd) for j in range(2)]
-    arrived = [y_swap(outs[j][1]) for j in range(2)]
+    ffn_one = after(ffn_one, mine[1][0])
+    far1 = far_of(ffn_one)
+    ffn_three = lax.ppermute(after(w_ffn, ffn_one, mine[1][0]), "tp", Z_DOWN)
+    first = attn_fwd(info, after(mine[0][0], far0), got[0], hd)
+    second = attn_fwd(info, after(mine[1][0], first[1]), got[1], hd)
+    outs = [first, second]
+    arrived = [y_swap(first[1]), y_swap(second[1])]
+    ffn_three = after(ffn_three, second[1])
+    far3 = far_of(ffn_three)
+    ffn_one, far1 = after(ffn_one, second[1]), after(far1, second[1])
+    ffn_two = [
+        lax.ppermute(after(ffn_one[:, j * units : (j + 1) * units], ffn_three), "tp", Z_UP)
+        for j in range(3)
+    ]
+    last1 = y_swap(after(near(far1), arrived[1]))
     resid, normed_two, normed_two_t, attended = out_proj(
-        info, x_in, [outs[0][0], outs[1][0]], arrived, w_out, gain_two, 256
-    )
-
-    own_ffn = after(w_ffn, attn_pieces[1][1], attn_pieces[3][1])
-    ffn_weights = [
-        (plan_whole, ffn_pieces(own_ffn, got[1])),
-        (plan_whole, ffn_pieces(ffn_one, got[1])),
-        (plan_chunks, ffn_chunks(ffn_two, outs[1][1])),
-        (plan_whole, ffn_pieces(ffn_three, outs[0][1])),
-    ]
-    order = (0, 1, 3, 2)
+        info, x_in, [first[0], second[0]], arrived, out_pieces, gain_two, 256
+    )
+
     scale = (slots / total_count)[None]
-    acts, hiddens, result_low, grad_result, grad_low, grad_low_t, square = ffn_fwd(
-        info, scale, normed_two, resid, teacher, [ffn_weights[k] for k in order], units, 256
+    weights1 = ffn_pieces(ffn_one, far1, after(last1, normed_two))
+    two_first, two_middle = after(ffn_two[0], normed_two), after(ffn_two[1], normed_two)
+    two_far = [x_swap(two_first), x_swap(two_middle)]
+    far3 = after(far3, normed_two)
+    last3 = y_swap(near(far3))
+    acts_a, hiddens_a, sum_a = ffn_fwd(
+        info, scale, normed_two, resid, None, [weights0, weights1], units, 256
+    )
+    weights3 = ffn_pieces(ffn_three, far3, after(last3, sum_a))
+    two_far = [after(two_far[0], sum_a), after(two_far[1], sum_a)]
+    two_far.append(y_swap(two_far[0]))
+    acts_b, hiddens_b, sum_b = ffn_fwd(
+        info, scale, normed_two, sum_a, None, [weights3], units, 256
+    )
+    two = [two_first, two_middle, after(ffn_two[2], sum_a)] + two_far[:2] + [after(two_far[2], sum_b)]
+    weights2 = (plan_chunks, two + [core_swap(p) for p in two])
+    acts_c, hiddens_c, result_low, grad_result, grad_low, grad_low_t, square = ffn_fwd(
+        info, scale, normed_two, sum_b, teacher, [weights2], units, 256
     )
 
     def spread(parts, dtype):
@@ -1464,7 +1578,89 @@
             out = lax.dynamic_update_slice(out, part, (lax.rem(z - k + 4, 4), 0, 0))
         return out
 
-    output_parts = z_gather(result_low)
+    def ffn_back(weights, saved, total):
+        return ffn_bwd(
+            grad_low, saved, weights, total, normed_two_t, grad_low_t, 256
+        )
+
+    output_one = lax.ppermute(result_low, "tp", Z_UP)
+    total, keep2, send2 = ffn_back(weights2, (acts_c, hiddens_c, 0), None)
+    came2 = core_swap(send2)
+    total, keep1, send1 = ffn_back(weights1, (acts_a, hiddens_a, 1), after(total, send2))
+    came1 = core_swap(send1)
+    own2, far2 = summed(info, after(keep2, send1), came2, "halves")
+    came2 = x_swap(far2)
+    output_one = after(output_one, own2)
+    output_three = lax.ppermute(after(result_low, output_one), "tp", Z_DOWN)
+    total, keep3, send3 = ffn_back(weights3, (acts_b, hiddens_b, 0), after(total, own2, output_one))
+    came3 = core_swap(send3)
+    here1, there1 = summed(info, after(keep1, send3), came1, "ctx")
+    came1 = y_swap(there1)
+    total, keep0, send0 = ffn_back(weights0, (acts_a, hiddens_a, 0), after(total, here1))
+    came0 = core_swap(send0)
+    own3, far3 = summed(info, after(keep3, send0), came3, "halves")
+    came3 = x_swap(far3)
+    here2, there2 = summed(info, after(own2, own3), came2, "ctx")
+    output_three = after(output_three, here2)
+    output_two = lax.ppermute(after(output_one, output_three), "tp", Z_UP)
+    grad_resid, grad_attn_t, a0, a1, b0, b1, gain_two_sum = norm_two_back(
+        info, after(total, here2, output_three), resid, grad_result, gain_two, out_pieces, 256
+    )
+
+    grad_got = [y_swap(b0), y_swap(b1)]
+    own0, far0 = summed(info, after(keep0, b0), came0, "halves")
+    own1, far1 = summed(info, after(here1, own0), came1, "halves", True)
+    came1 = x_swap(far1)
+    came2 = y_swap(after(there2, grad_got[0]))
+
+    def attn_back(j, grad):
+        return attn_bwd(
+            info, mine[j][0], got[j], outs[j][0], outs[j][1], grad, grad_got[j], outs[j][2], hd
+        )
+
+    first_back = attn_back(0, after(a0, own1))
+    grad_heads = [y_swap(first_back[1])]
+    part2 = summed(info, after(here2, first_back[1]), came2, "all", True)
+    part1 = summed(info, after(own1, part2), came1, "all")
+    here3, there3 = summed(info, after(own3, part1), came3, "ctx")
+    came0 = x_swap(after(far0, here3))
+    output_two = after(output_two, here3)
+    came2 = lax.ppermute(after(part2, output_two), "tp", Z_DOWN)
+    came3 = y_swap(after(there3, first_back[1]))
+    second_back = attn_back(1, after(a1, here3, output_two))
+    grad_heads.append(y_swap(second_back[1]))
+    two_down = summed(info, after(part1, second_back[1]), came2, "all")
+    came2 = lax.ppermute(two_down, "tp", Z_DOWN)
+    back = [
+        head_back(
+            info,
+            after(first_back[0], two_down),
+            grad_heads[0],
+            mine[0][1],
+            theirs[0][1],
+            *tables,
+            heads,
+        )
+    ]
+    part3 = summed(info, after(here3, back[0][0]), came3, "all", True)
+    came3 = lax.ppermute(part3, "tp", Z_UP)
+    back.append(
+        head_back(
+            info,
+            after(second_back[0], part3),
+            grad_heads[1],
+            mine[1][1],
+            theirs[1][1],
+            *tables,
+            heads,
+        )
+    )
+    tokens_low, gain_one_sum = norm_one_back(
+        info, [back[0][0], back[1][0]], proj_pieces, x_in, grad_resid, gain_one, 256
+    )
+    tokens_grad = spread(z_gather(tokens_low), F32)
+    output_parts = [result_low, output_one, output_two, output_three]
+    output = spread([after(part, tokens_low) for part in output_parts], BF16)
 
     def halves(v):
         half = v.shape[0] // 2
@@ -1472,98 +1668,6 @@
             lax.dynamic_slice_in_dim(v, ctx * half, half, 0),
             lax.dynamic_slice_in_dim(v, half - ctx * half, half, 0),
         )
-
-    def core_sum(keep, send):
-        came = core_swap(send)
-        return add_low(keep[:quarter], came[:quarter]), add_low(keep[quarter:], came[quarter:])
-
-    def plane_sum(own, far, x_first, turn):
-        if x_first:
-            own = add_low(own, x_swap(far))
-            here, there = halves(own)
-            return add_low(here, turn(y_swap(there)))
-        here, there = halves(own)
-        far_here, far_there = halves(far)
-        came = turn(y_swap(jnp.concatenate([there, far_there], axis=0)))
-        half = quarter // 2
-        return add_low(
-            add_low(here, came[:half]), x_swap(add_low(far_here, came[half:]))
-        )
-
-    def finish(own, turn):
-        other = turn(y_swap(own))
-        return jnp.concatenate(
-            [jnp.where(ctx == 0, own, other), jnp.where(ctx == 0, other, own)], axis=0
-        )
-
-    def ffn_back(k, total):
-        return ffn_bwd(
-            order.index(k),
-            grad_low,
-            acts,
-            hiddens,
-            ffn_weights[k],
-            total,
-            normed_two_t,
-            grad_low_t,
-            256,
-        )
-
-    def y_sum(own):
-        here, there = halves(own)
-        return add_low(here, turn_chunks(y_swap(there)))
-
-    grad_two, keep2, send2 = ffn_back(2, None)
-    grad_two, keep1, send1 = ffn_back(1, grad_two)
-    own2, far2 = core_sum(keep2, send2)
-    grad_two, keep3, send3 = ffn_back(3, after(grad_two, own2, far2))
-    own1, far1 = core_sum(keep1, send1)
-    grad_two, keep0, send0 = ffn_back(0, after(grad_two, own1, far1))
-    own3, far3 = core_sum(keep3, send3)
-    own2 = add_low(own2, x_swap(far2))
-    grad_resid, grad_attn_t, a0, a1, b0, b1, gain_two_sum = norm_two_back(
-        info, after(grad_two, own2, own3, far3), resid, grad_result, gain_two, w_out, 256
-    )
-
-    grad_got = [y_swap(b0), y_swap(b1)]
-    own0, far0 = core_sum(keep0, send0)
-
-    def attn_back(j, grad):
-        return attn_bwd(
-            info, mine[j][0], got[j], outs[j][0], outs[j][1], grad, grad_got[j], outs[j][2], hd
-        )
-
-    first_back = attn_back(0, after(a0, own0, far0))
-    part2 = y_sum(after(own2, grad_got[1]))
-    own1 = add_low(own1, x_swap(far1))
-    second_back = attn_back(1, after(a1, first_back[1], own1, part2, output_parts[1]))
-    part1 = y_sum(after(own1, first_back[1]))
-    own3 = add_low(own3, x_swap(after(far3, own1)))
-    output_parts[2] = after(output_parts[2], second_back[1])
-    grad_heads = [y_swap(first_back[1]), y_swap(second_back[1])]
-    two_down = add_low(part1, lax.ppermute(part2, "tp", Z_DOWN))
-    back = [
-        head_back(
-            info,
-            after(first_back[0], part1, own3),
-            grad_heads[0],
-            mine[0][1],
-            theirs[0][1],
-            *tables,
-            heads,
-        ),
-        head_back(
-            info, second_back[0], grad_heads[1], mine[1][1], theirs[1][1], *tables, heads
-        ),
-    ]
-    part3 = y_sum(after(own3, grad_heads[1]))
-    own0 = add_low(own0, x_swap(after(far0, own3)))
-    part0 = y_sum(after(own0, part3))
-    tokens_low, gain_one_sum = norm_one_back(
-        info, [back[0][0], back[1][0]], w_proj, x_in, grad_resid, gain_one, 256
-    )
-    tokens_grad = spread(z_gather(tokens_low), F32)
-    output = spread([after(part, tokens_low) for part in output_parts], BF16)
 
     attn_parts = []
     for k in range(4):
@@ -1574,11 +1678,22 @@
             ],
             axis=1,
         )
-        own, far = core_sum(part[: width // 2], part[width // 2 :])
-        attn_parts.append(plane_sum(own, far, k in (1, 2), lambda v: v))
-
-    ffn_sum = add(part0, lax.ppermute(two_down, "tp", Z_DOWN))
-    ffn_sum = ffn_sum + lax.ppermute(part3, "tp", Z_UP).astype(F32)
+        came = core_swap(part[width // 2 :])
+        own = add_low(part[:quarter], came[:quarter])
+        far = add_low(part[quarter : width // 2], came[quarter:])
+        here, there = halves(add_low(own, x_swap(far)))
+        attn_parts.append(add_low(here, y_swap(there)))
+
+    here0, there0 = summed(info, after(own0, tokens_low), came0, "ctx")
+    part0 = summed(info, here0, y_swap(there0), "all", True)
+
+    def finish(own, turn):
+        other = turn(y_swap(own))
+        return jnp.concatenate(
+            [jnp.where(ctx == 0, own, other), jnp.where(ctx == 0, other, own)], axis=0
+        )
+
+    ffn_sum = add(part0, came2) + came3.astype(F32)
     ffn_grad = finish(ffn_sum, turn_chunks)
     attn_grad = finish(z_reduce(attn_parts), lambda v: v)
 
@@ -1589,17 +1704,12 @@
             v = v + lax.ppermute(v, "tp", pairs)
         return v
 
-    def natural(v):
-        v = v.reshape(4, quarter)[jnp.array([0, 2, 1, 3])]
-        v = jnp.where(fsdp % 2 == 0, v, v[jnp.array([1, 0, 3, 2])])
-        return jnp.where(fsdp // 2 == 0, v, v[jnp.array([2, 3, 0, 1])]).reshape(1, width)
-
     gain_heads = back[0][1] + back[1][1]
     sums = total(
         jnp.concatenate(
             [
-                natural(gain_one_sum),
-                natural(gain_two_sum),
+                natural(gain_one_sum.reshape(4, quarter)).reshape(1, width),
+                natural(gain_two_sum.reshape(4, quarter)).reshape(1, width),
                 gain_heads[:, 0].reshape(1, hd),
                 gain_heads[:, 1].reshape(1, hd),
                 jnp.sum(square).reshape(1, 1),

time: 1010 us -> 1010 us (level); the launches traced: 992 us -> 1010 us
  Pallas kernels: 256 us -> 352 us
  starting transfers between devices: 188 us -> 118 us
  waiting for transfers between devices: 346 us -> 395 us
  other arithmetic: 63.5 us -> 35.2 us
  local copies, waits for them, and re-layouts: 113 us -> 91.1 us
    ppermute x11 -> x17, starting transfers between devices: 78.6 us -> 34.9 us  [the longest x2 12 us: z_direct(): lax.ppermute(block, 'tp', Z_UP)]
    ppermute x1, waiting for transfers between devices: 0.01 us -> 42.5 us  [z_reduce(): return total + lax.ppermute(parts[3], 'tp', Z_UP).astype(F32)]
    ppermute x2 -> x1, waiting for transfers between devices: 42 us -> 0.01 us  [z_gather(): one = lax.ppermute(block, 'tp', Z_UP)]
    pallas_call x2, Pallas kernels: 32.2 us -> 71.1 us  [attn_bwd(): pl.pallas_call(functools.partial(attn_bwd_kernel, width, hd), grid_spec=p...]
    pallas_call x5 -> x18, Pallas kernels: 11.6 us -> 49.2 us  [the longest x13 34.2 us: summed(): pl.pallas_call(functools.partial(sum_kernel, side, turn), grid_spec=pltpu...]
    ppermute x2 -> x1, waiting for transfers between devices: 0.01 us -> 29.9 us  [z_gather(): two = lax.ppermute(one, 'tp', Z_UP)]
    ppermute x18 -> x22, starting transfers between devices: 57 us -> 31.2 us  [x_swap(): return lax.ppermute(v, 'fsdp', X_SWAP)]
    convert_element_type x22 -> x11, other arithmetic: 31.2 us -> 7.46 us  [add_low(): return add(left, right).astype(BF16)]
  transfers between devices with their start and end apart: 97 -> 112, of which waited for: 35 -> 37; matrix products, arithmetic and copies ran while one was open for 16% -> 8% of each run, Pallas kernels for 18% -> 31%
where the time goes in v4:
time: 1010 us
  waiting for transfers between devices  395 us (39%)
  Pallas kernels  352 us (35%)
  starting transfers between devices  118 us (12%)
  local copies, waits for them, and re-layouts  91.1 us (9%)
  other arithmetic  35.2 us (3%)
    ppermute x22, waiting for transfers between devices, y_swap(): return lax.ppermute(v, 'ctx', Y_SWAP)  141 us
    pallas_call x4, Pallas kernels, ffn_bwd(): pl.pallas_call(functools.partial(ffn_bwd_kernel, steps, plan, first), gri...  105 us
    ppermute x22, waiting for transfers between devices, x_swap(): return lax.ppermute(v, 'fsdp', X_SWAP)  96.4 us
    pallas_call x2, Pallas kernels, attn_bwd(): pl.pallas_call(functools.partial(attn_bwd_kernel, width, hd), grid_spec=p...  71.1 us
    unnamed x407, local copies, waits for them, and re-layouts  58.5 us
    pallas_call x3, Pallas kernels, ffn_fwd(): pl.pallas_call(functools.partial(ffn_fwd_kernel, tile, [plan for plan, _...  57.4 us
    ppermute x1, waiting for transfers between devices, z_reduce(): return total + lax.ppermute(parts[3], 'tp', Z_UP).astype(F32)  42.5 us
    ppermute x1, waiting for transfers between devices, per_device_rows(): output_one = lax.ppermute(result_low, 'tp', Z_UP)  40.4 us
  transfers between devices with their start and end apart: 112, of which 37 were waited for; matrix products, arithmetic and copies ran while one was open for 8% of the time, Pallas kernels for 31%

profile of v4, /device:TPU:0, one launch (start us, length us, event | category | flops | bytes accessed | tf_op | source)
XLA Modules:
  0.0 1008.2 jit_solution(10043945652220209262)
XLA Ops:
  69.4 26.9 %collective-permute-done.13.refs_9_ = bf16[256,256]{1,0:T(8,128)(2,1)} collective-permute-done((bf16[256,256]{1,0:T(8,128)(2,1)S(1)}, bf16[256,256]{1,0:T(8,128)(2,1)}, u32[]{:S(2)}, u32[]{:S(2)}) %collective-permute-start.13) | collective-permute-done | bytes 131104 | tf_op jit(solution)/shard_map/ppermute | solution.py:1457
  142.4 21.0 %collective-permute-done.34.got_ref = bf16[512,1024]{1,0:T(8,128)(2,1)S(1)} collective-permute-done((bf16[512,1024]{1,0:T(8,128)(2,1)S(1)}, bf16[512,1024]{1,0:T(8,128)(2,1)S(1)}, u32[]{:S(2)}, u32[]{:S(2)}) %collective-permute-start.34) | collective-permute-done | bytes 1048608 | tf_op jit(solution)/shard_map/ppermute | solution.py:1463
  167.2 15.1 %attn_fwd.2 = (bf16[1024,256]{1,0:T(8,128)(2,1)S(1)}, bf16[1024,256]{1,0:T(8,128)(2,1)S(1)}, f32[2,2,2048]{2,1,0:T(2,128)S(1)}) custom-call(s32[4]{0:T(128)S(1)} %pad_add_fusion.info, bf16[512,1024]{1,0:T(8,128)(2,1)S(1)} %get-tuple-element.157.mine_ref, bf16[512,1024]{1,0:T(8,128)(2,1)S(1)} %collective-permute-done.33.got_ref), custom_call_target="tpu_custom_call" | custom-call | flops 33554432 | bytes 32768 | tf_op jit(solution)/shard_map/attn_fwd/pallas_call | solution.py:728
  182.9 15.1 %attn_fwd.3 = (bf16[1024,256]{1,0:T(8,128)(2,1)S(1)}, bf16[1024,256]{1,0:T(8,128)(2,1)S(1)}, f32[2,2,2048]{2,1,0:T(2,128)S(1)}) custom-call(s32[4]{0:T(128)S(1)} %pad_add_fusion.info, bf16[512,1024]{1,0:T(8,128)(2,1)S(1)} %get-tuple-element.162.mine_ref, bf16[512,1024]{1,0:T(8,128)(2,1)S(1)} %collective-permute-done.34.got_ref), custom_call_target="tpu_custom_call" | custom-call | flops 33554432 | bytes 32768 | tf_op jit(solution)/shard_map/attn_fwd/pallas_call | solution.py:728
  202.2 11.3 %collective-permute-done.36.refs_20_ = bf16[1024,256]{1,0:T(8,128)(2,1)S(1)} collective-permute-done((bf16[1024,256]{1,0:T(8,128)(2,1)S(1)}, bf16[1024,256]{1,0:T(8,128)(2,1)S(1)}, u32[]{:S(2)}, u32[]{:S(2)}) %collective-permute-start.36) | collective-permute-done | bytes 524320 | tf_op jit(solution)/shard_map/ppermute | solution.py:1463
  228.0 10.5 %collective-permute-done.43.rest_8_.rest_2_ = bf16[256,1152]{1,0:T(8,128)(2,1)S(1)} collective-permute-done((bf16[256,1152]{1,0:T(8,128)(2,1)S(1)}, bf16[256,1152]{1,0:T(8,128)(2,1)S(1)}, u32[]{:S(2)}, u32[]{:S(2)}) %collective-permute-start.43) | collective-permute-done | bytes 589856 | tf_op jit(solution)/shard_map/ppermute | solution.py:1463
  278.5 25.2 %ffn_fwd.3 = (bf16[2,1024,2304]{2,1,0:T(8,128)(2,1)}, bf16[2,1024,1152]{2,1,0:T(8,128)(2,1)}, f32[1024,1024]{1,0:T(8,128)}) custom-call(s32[4]{0:T(128)S(1)} %pad_add_fusion.info, f32[1]{0:T(128)} %bitcast.4.scale, bf16[1024,1024]{1,0:T(8,128)(2,1)} %copy-done.2, f32[1024,1024]{1,0:T(8,128)} %copy-done.3, bf16[256,3456]{1,0:T(8,128)(2,1)} %get-tuple-element.175.rest_0_, ...), custom_call_target="tpu_custom_call" | custom-call | flops 56623104 | bytes 81920 | tf_op jit(solution)/shard_map/ffn_fwd/pallas_call | solution.py:1220
  306.5 14.8 %ffn_fwd.4 = (bf16[1,1024,2304]{2,1,0:T(8,128)(2,1)}, bf16[1,1024,1152]{2,1,0:T(8,128)(2,1)}, f32[1024,1024]{1,0:T(8,128)}) custom-call(s32[4]{0:T(128)S(1)} %pad_add_fusion.info, f32[1]{0:T(128)} %bitcast.4.scale, bf16[1024,1024]{1,0:T(8,128)(2,1)} %copy-done.2, f32[1024,1024]{1,0:T(8,128)} %get-tuple-element.174.in_ref, ...), custom_call_target="tpu_custom_call" | custom-call | flops 28311552 | bytes 81920 | tf_op jit(solution)/shard_map/ffn_fwd/pallas_call | solution.py:1220
  325.5 17.4 %ffn_fwd.5 = (bf16[1,1024,2304]{2,1,0:T(8,128)(2,1)}, bf16[1,1024,1152]{2,1,0:T(8,128)(2,1)}, bf16[1024,1024]{1,0:T(8,128)(2,1)}, f32[1024,1024]{1,0:T(8,128)}, ...) custom-call(s32[4]{0:T(128)S(1)} %pad_add_fusion.info, f32[1]{0:T(128)} %bitcast.4.scale, ...), custom_call_target="tpu_custom_call" | custom-call | flops 28311552 | bytes 81920 | tf_op jit(solution)/shard_map/ffn_fwd/pallas_call | solution.py:1220
  342.9 26.0 %ffn_bwd.4 = (f32[1024,1024]{1,0:T(8,128)}, bf16[512,3456]{1,0:T(8,128)(2,1)}, bf16[512,3456]{1,0:T(8,128)(2,1)}) custom-call(bf16[1024,1024]{1,0:T(8,128)(2,1)} %get-tuple-element.190.low_ref, bf16[1,1024,2304]{2,1,0:T(8,128)(2,1)} %get-tuple-element.197.act_ref, bf16[1,1024,1152]{2,1,0:T(8,128)(2,1)} %get-tuple-element.198.hid_ref, ...), custom_call_target="tpu_custom_call" | custom-call | flops 56623104 | bytes 131072 | tf_op jit(solution)/shard_map/ffn_bwd/pallas_call | solution.py:1307
  369.1 26.2 %ffn_bwd.5 = (f32[1024,1024]{1,0:T(8,128)}, bf16[512,3456]{1,0:T(8,128)(2,1)}, bf16[512,3456]{1,0:T(8,128)(2,1)}) custom-call(bf16[1024,1024]{1,0:T(8,128)(2,1)} %get-tuple-element.190.low_ref, bf16[2,1024,2304]{2,1,0:T(8,128)(2,1)} %get-tuple-element.191.act_ref, ...), custom_call_target="tpu_custom_call", output_to_operand_aliasing={{0}: (11, {})} | custom-call | flops 56623104 | bytes 131072 | tf_op jit(solution)/shard_map/ffn_bwd/pallas_call | solution.py:1307
  405.2 40.4 %collective-permute-done.66 = bf16[1024,1024]{1,0:T(8,128)(2,1)S(1)} collective-permute-done((bf16[1024,1024]{1,0:T(8,128)(2,1)}, bf16[1024,1024]{1,0:T(8,128)(2,1)S(1)}, u32[]{:S(2)}, u32[]{:S(2)}) %collective-permute-start.66) | collective-permute-done | bytes 2097184 | tf_op jit(solution)/shard_map/ppermute | solution.py:1586
  446.9 26.2 %ffn_bwd.6 = (f32[1024,1024]{1,0:T(8,128)}, bf16[512,3456]{1,0:T(8,128)(2,1)}, bf16[512,3456]{1,0:T(8,128)(2,1)}) custom-call(bf16[1024,1024]{1,0:T(8,128)(2,1)} %get-tuple-element.190.low_ref, bf16[1,1024,2304]{2,1,0:T(8,128)(2,1)} %get-tuple-element.195.act_ref, ...), custom_call_target="tpu_custom_call", output_to_operand_aliasing={{0}: (11, {})} | custom-call | flops 56623104 | bytes 131072 | tf_op jit(solution)/shard_map/ffn_bwd/pallas_call | solution.py:1307
  480.2 27.0 %ffn_bwd.7 = (f32[1024,1024]{1,0:T(8,128)}, bf16[512,3456]{1,0:T(8,128)(2,1)}, bf16[512,3456]{1,0:T(8,128)(2,1)}) custom-call(bf16[1024,1024]{1,0:T(8,128)(2,1)} %get-tuple-element.190.low_ref, bf16[2,1024,2304]{2,1,0:T(8,128)(2,1)} %get-tuple-element.191.act_ref, ...), custom_call_target="tpu_custom_call", output_to_operand_aliasing={{0}: (11, {})} | custom-call | flops 56623104 | bytes 131072 | tf_op jit(solution)/shard_map/ffn_bwd/pallas_call | solution.py:1307
  517.1 32.8 %collective-permute-done.69.right_ref = bf16[256,3456]{1,0:T(8,128)(2,1)S(1)} collective-permute-done((bf16[256,3456]{1,0:T(8,128)(2,1)}, bf16[256,3456]{1,0:T(8,128)(2,1)S(1)}, u32[]{:S(2)}, u32[]{:S(2)}) %collective-permute-start.69) | collective-permute-done | bytes 1769504 | tf_op jit(solution)/shard_map/ppermute | solution.py:1457
  556.9 11.5 %norm_two_back.1 = (f32[1024,1024]{1,0:T(8,128)S(1)}, bf16[1024,1024]{1,0:T(8,128)(2,1)S(1)}, bf16[1024,256]{1,0:T(8,128)(2,1)S(1)}, bf16[1024,256]{1,0:T(8,128)...) custom-call(s32[4]{0:T(128)S(1)} %pad_add_fusion.info, ...), custom_call_target="tpu_custom_call" | custom-call | flops 8388608 | bytes 98304 | tf_op jit(solution)/shard_map/norm_two_back/pallas_call | solution.py:1002
  592.3 35.9 %attn_bwd.2 = (bf16[512,1024]{1,0:T(8,128)(2,1)S(1)}, bf16[512,1024]{1,0:T(8,128)(2,1)S(1)}) custom-call(s32[4]{0:T(128)S(1)} %pad_add_fusion.info, bf16[512,1024]{1,0:T(8,128)(2,1)S(1)} %copy-done.64, bf16[512,1024]{1,0:T(8,128)(2,1)S(1)} %copy-done.62, bf16[1024,256]{1,0:T(8,128)(2,1)S(1)} %copy-done.84, bf16[1024,256]{1,0:T(8,128)(2,1)S(1)} %copy-done.141, ...), custom_call_target="tpu_custom_call" | custom-call | flops 83886080 | bytes 49152 | tf_op jit(solution)/shard_map/attn_bwd/pallas_call | solution.py:882
  638.6 23.1 %collective-permute-done.78.gs_ref = bf16[1024,256]{1,0:T(8,128)(2,1)S(1)} collective-permute-done((bf16[1024,256]{1,0:T(8,128)(2,1)S(1)}, bf16[1024,256]{1,0:T(8,128)(2,1)S(1)}, u32[]{:S(2)}, u32[]{:S(2)}) %collective-permute-start.78) | collective-permute-done | bytes 524320 | tf_op jit(solution)/shard_map/ppermute | solution.py:1463
  661.7 35.2 %attn_bwd.3 = (bf16[512,1024]{1,0:T(8,128)(2,1)S(1)}, bf16[512,1024]{1,0:T(8,128)(2,1)S(1)}) custom-call(s32[4]{0:T(128)S(1)} %pad_add_fusion.info, bf16[512,1024]{1,0:T(8,128)(2,1)S(1)} %copy-done.58, bf16[512,1024]{1,0:T(8,128)(2,1)S(1)} %copy-done.60, bf16[1024,256]{1,0:T(8,128)(2,1)S(1)} %copy-done.82, bf16[1024,256]{1,0:T(8,128)(2,1)S(1)} %copy-done.139, ...), custom_call_target="tpu_custom_call" | custom-call | flops 83886080 | bytes 49152 | tf_op jit(solution)/shard_map/attn_bwd/pallas_call | solution.py:882
  809.6 15.2 %collective-permute-done.99 = bf16[128,768]{0,1:T(8,128)(2,1)S(1)} collective-permute-done((bf16[128,768]{0,1:T(8,128)(2,1)S(1)}, bf16[128,768]{0,1:T(8,128)(2,1)S(1)}, u32[]{:S(2)}, u32[]{:S(2)}) %collective-permute-start.99) | collective-permute-done | bytes 196640 | tf_op jit(solution)/shard_map/ppermute | solution.py:1463
  836.5 17.3 %collective-permute-done.100 = bf16[128,768]{0,1:T(8,128)(2,1)S(1)} collective-permute-done((bf16[128,768]{0,1:T(8,128)(2,1)S(1)}, bf16[128,768]{0,1:T(8,128)(2,1)S(1)}, u32[]{:S(2)}, u32[]{:S(2)}) %collective-permute-start.100) | collective-permute-done | bytes 196640 | tf_op jit(solution)/shard_map/ppermute | solution.py:1423
  860.8 42.5 %collective-permute-done.105 = bf16[128,768]{0,1:T(8,128)(2,1)S(1)} collective-permute-done((bf16[128,768]{0,1:T(8,128)(2,1)S(1)}, bf16[128,768]{0,1:T(8,128)(2,1)S(1)}, u32[]{:S(2)}, u32[]{:S(2)}) %collective-permute-start.105) | collective-permute-done | bytes 196640 | tf_op jit(solution)/shard_map/ppermute | solution.py:1425
  914.1 37.5 %collective-permute-done.106 = f32[128,768]{0,1:T(8,128)S(1)} collective-permute-done((f32[128,768]{0,1:T(8,128)S(1)}, f32[128,768]{0,1:T(8,128)S(1)}, u32[]{:S(2)}, u32[]{:S(2)}) %collective-permute-start.106) | collective-permute-done | bytes 393248 | tf_op jit(solution)/shard_map/ppermute | solution.py:1463
  972.9 29.9 %collective-permute-done.90 = bf16[1024,1024]{1,0:T(8,128)(2,1)} collective-permute-done((bf16[1024,1024]{1,0:T(8,128)(2,1)}, bf16[1024,1024]{1,0:T(8,128)(2,1)}, u32[]{:S(2)}, u32[]{:S(2)}) %collective-permute-start.90) | collective-permute-done | bytes 2097184 | tf_op jit(solution)/shard_map/ppermute | solution.py:1410
  (740 shorter events, 417.0 us)
Async XLA Ops:
  43.8 75.8 %collective-permute-start.41 = (bf16[256,3456]{1,0:T(8,128)(2,1)}, bf16[256,3456]{1,0:T(8,128)(2,1)}, u32[]{:S(2)}, u32[]{:S(2)}) collective-permute-start(bf16[256,3456]{1,0:T(8,128)(2,1)} %get-tuple-element.175.rest_0_), channel_id=1, source_target_pairs={{0,1},{1,2},{2,3},{3,0},{4,5},{5,6},{6,7},{7,4},{8,9},{9,10},{10,1... | collective-permute-start | bytes 5308424 | tf_op jit(solution)/shard_map/ppermute | solution.py:1506
  64.4 67.2 %collective-permute-start.32 = (bf16[256,2304]{1,0:T(8,128)(2,1)}, bf16[256,2304]{1,0:T(8,128)(2,1)S(1)}, u32[]{:S(2)}, u32[]{:S(2)}) collective-permute-start(bf16[256,2304]{1,0:T(8,128)(2,1)} %slice.274), channel_id=1, source_target_pairs={{0,16},{16,0},{8,24},{24,8},{1,17},{17,1},{9,25},{25,9},{2,18},{18... | collective-permute-start | bytes 3538952 | tf_op jit(solution)/shard_map/ppermute | solution.py:1457
  103.7 95.0 %collective-permute-start.38 = (bf16[256,3456]{1,0:T(8,128)(2,1)}, bf16[256,3456]{1,0:T(8,128)(2,1)S(1)}, u32[]{:S(2)}, u32[]{:S(2)}) collective-permute-start(bf16[256,3456]{1,0:T(8,128)(2,1)} %get-tuple-element.175.rest_0_), channel_id=1, source_target_pairs={{0,8},{8,0},{16,24},{24,16},{1,9},{9,1},{17,25},{25,17},{2,10},{10... | collective-permute-start | bytes 5308424 | tf_op jit(solution)/shard_map/ppermute | solution.py:1460
  126.7 74.1 %collective-permute-start.47 = (bf16[256,3456]{1,0:T(8,128)(2,1)}, bf16[256,3456]{1,0:T(8,128)(2,1)}, u32[]{:S(2)}, u32[]{:S(2)}) collective-permute-start(bf16[256,3456]{1,0:T(8,128)(2,1)} %get-tuple-element.175.rest_0_), channel_id=1, source_target_pairs={{0,3},{1,0},{2,1},{3,2},{4,7},{5,4},{6,5},{7,6},{8,11},{9,8},{10,9... | collective-permute-start | bytes 5308424 | tf_op jit(solution)/shard_map/ppermute | solution.py:1536
  131.6 68.6 %collective-permute-start.42 = (bf16[256,2304]{1,0:T(8,128)(2,1)S(1)}, bf16[256,2304]{1,0:T(8,128)(2,1)S(1)}, u32[]{:S(2)}, u32[]{:S(2)}) collective-permute-start(bf16[256,2304]{1,0:T(8,128)(2,1)S(1)} %slice.277), channel_id=1, source_target_pairs={{0,16},{16,0},{8,24},{24,8},{1,17},{17,1},{9,25},{25,9},{2,18},{18... | collective-permute-start | bytes 3538952 | tf_op jit(solution)/shard_map/ppermute | solution.py:1457
  140.9 57.4 %collective-permute-start.37 = (bf16[256,1152]{1,0:T(8,128)(2,1)S(1)}, bf16[256,1152]{1,0:T(8,128)(2,1)S(1)}, u32[]{:S(2)}, u32[]{:S(2)}) collective-permute-start(bf16[256,1152]{1,0:T(8,128)(2,1)S(1)} %slice.350), channel_id=1, source_target_pairs={{0,4},{4,0},{1,5},{5,1},{2,6},{6,2},{3,7},{7,3},{8,12},{12,8},{9,1... | collective-permute-start | bytes 1769480 | tf_op jit(solution)/shard_map/ppermute | solution.py:1463
  198.2 54.1 %collective-permute-start.44 = (bf16[256,3456]{1,0:T(8,128)(2,1)}, bf16[256,3456]{1,0:T(8,128)(2,1)S(1)}, u32[]{:S(2)}, u32[]{:S(2)}) collective-permute-start(bf16[256,3456]{1,0:T(8,128)(2,1)} %collective-permute-done.41.rest_6_.rest_0_), channel_id=1, source_target_pairs={{0,8},{8,0},{16,24},{24,16},{1,9},{9,1},{17,25},{25,17},{2,10},{10... | collective-permute-start | bytes 5308424 | tf_op jit(solution)/shard_map/ppermute | solution.py:1460
  252.3 53.2 %collective-permute-start.50 = (bf16[256,3456]{1,0:T(8,128)(2,1)}, bf16[256,3456]{1,0:T(8,128)(2,1)}, u32[]{:S(2)}, u32[]{:S(2)}) collective-permute-start(bf16[256,3456]{1,0:T(8,128)(2,1)} %collective-permute-done.47.rest_0_), channel_id=1, source_target_pairs={{0,8},{8,0},{16,24},{24,16},{1,9},{9,1},{17,25},{25,17},{2,10},{10... | collective-permute-start | bytes 5308424 | tf_op jit(solution)/shard_map/ppermute | solution.py:1460
  395.3 78.0 %collective-permute-start.67 = (bf16[512,3456]{1,0:T(8,128)(2,1)}, bf16[512,3456]{1,0:T(8,128)(2,1)}, u32[]{:S(2)}, u32[]{:S(2)}) collective-permute-start(bf16[512,3456]{1,0:T(8,128)(2,1)} %get-tuple-element.204), channel_id=1, source_target_pairs={{0,8},{8,0},{16,24},{24,16},{1,9},{9,1},{17,25},{25,17},{2,10},{10... | collective-permute-start | bytes 10616840 | tf_op jit(solution)/shard_map/ppermute | solution.py:1460
  507.1 69.7 %collective-permute-start.71 = (bf16[512,3456]{1,0:T(8,128)(2,1)}, bf16[512,3456]{1,0:T(8,128)(2,1)}, u32[]{:S(2)}, u32[]{:S(2)}) collective-permute-start(bf16[512,3456]{1,0:T(8,128)(2,1)} %get-tuple-element.217), channel_id=1, source_target_pairs={{0,8},{8,0},{16,24},{24,16},{1,9},{9,1},{17,25},{25,17},{2,10},{10... | collective-permute-start | bytes 10616840 | tf_op jit(solution)/shard_map/ppermute | solution.py:1460
  509.4 75.0 %collective-permute-start.72 = (bf16[256,3456]{1,0:T(8,128)(2,1)}, bf16[256,3456]{1,0:T(8,128)(2,1)}, u32[]{:S(2)}, u32[]{:S(2)}) collective-permute-start(bf16[256,3456]{1,0:T(8,128)(2,1)} %copy-done.155), channel_id=1, source_target_pairs={{0,4},{4,0},{1,5},{5,1},{2,6},{6,2},{3,7},{7,3},{8,12},{12,8},{9,1... | collective-permute-start | bytes 5308424 | tf_op jit(solution)/shard_map/ppermute | solution.py:1463
  555.5 80.7 %collective-permute-start.77 = (bf16[1024,1024]{1,0:T(8,128)(2,1)}, bf16[1024,1024]{1,0:T(8,128)(2,1)}, u32[]{:S(2)}, u32[]{:S(2)}) collective-permute-start(bf16[1024,1024]{1,0:T(8,128)(2,1)} %copy-done.187), channel_id=1, source_target_pairs={{0,1},{1,2},{2,3},{3,0},{4,5},{5,6},{6,7},{7,4},{8,9},{9,10},{10,1... | collective-permute-start | bytes 6291464 | tf_op jit(solution)/shard_map/ppermute | solution.py:1605
  556.0 75.9 %collective-permute-start.76 = (bf16[256,3456]{1,0:T(8,128)(2,1)}, bf16[256,3456]{1,0:T(8,128)(2,1)}, u32[]{:S(2)}, u32[]{:S(2)}) collective-permute-start(bf16[256,3456]{1,0:T(8,128)(2,1)} %get-tuple-element.246), channel_id=1, source_target_pairs={{0,16},{16,0},{8,24},{24,8},{1,17},{17,1},{9,25},{25,9},{2,18},{18... | collective-permute-start | bytes 5308424 | tf_op jit(solution)/shard_map/ppermute | solution.py:1457
  628.2 76.0 %collective-permute-start.80 = (bf16[512,1024]{1,0:T(8,128)(2,1)S(1)}, bf16[512,1024]{1,0:T(8,128)(2,1)S(1)}, u32[]{:S(2)}, u32[]{:S(2)}) collective-permute-start(bf16[512,1024]{1,0:T(8,128)(2,1)S(1)} %get-tuple-element.238), channel_id=1, source_target_pairs={{0,4},{4,0},{1,5},{5,1},{2,6},{6,2},{3,7},{7,3},{8,12},{12,8},{9,1... | collective-permute-start | bytes 3145736 | tf_op jit(solution)/shard_map/ppermute | solution.py:1463
  634.6 73.5 %collective-permute-start.81 = (bf16[128,3456]{1,0:T(8,128)(2,1)S(1)}, bf16[128,3456]{1,0:T(8,128)(2,1)S(1)}, u32[]{:S(2)}, u32[]{:S(2)}) collective-permute-start(bf16[128,3456]{1,0:T(8,128)(2,1)S(1)} %get-tuple-element.263), channel_id=1, source_target_pairs={{0,4},{4,0},{1,5},{5,1},{2,6},{6,2},{3,7},{7,3},{8,12},{12,8},{9,1... | collective-permute-start | bytes 2654216 | tf_op jit(solution)/shard_map/ppermute | solution.py:1463
  636.2 67.2 %collective-permute-start.79 = (bf16[128,3456]{1,0:T(8,128)(2,1)S(1)}, bf16[128,3456]{1,0:T(8,128)(2,1)S(1)}, u32[]{:S(2)}, u32[]{:S(2)}) collective-permute-start(bf16[128,3456]{1,0:T(8,128)(2,1)S(1)} %summed.19), channel_id=1, source_target_pairs={{0,3},{1,0},{2,1},{3,2},{4,7},{5,4},{6,5},{7,6},{8,11},{9,8},{10,9... | collective-permute-start | bytes 2654216 | tf_op jit(solution)/shard_map/ppermute | solution.py:1628
  697.5 64.0 %collective-permute-start.107 = (bf16[256,3456]{1,0:T(8,128)(2,1)}, bf16[256,3456]{1,0:T(8,128)(2,1)}, u32[]{:S(2)}, u32[]{:S(2)}) collective-permute-start(bf16[256,3456]{1,0:T(8,128)(2,1)} %get-tuple-element.283), channel_id=1, source_target_pairs={{0,16},{16,0},{8,24},{24,8},{1,17},{17,1},{9,25},{25,9},{2,18},{18... | collective-permute-start | bytes 5308424 | tf_op jit(solution)/shard_map/ppermute | solution.py:1457
  711.2 53.4 %collective-permute-start.91 = (bf16[512,768]{0,1:T(8,128)(2,1)}, bf16[512,768]{0,1:T(8,128)(2,1)}, u32[]{:S(2)}, u32[]{:S(2)}) collective-permute-start(bf16[512,768]{0,1:T(8,128)(2,1)} %fusion.15), channel_id=1, source_target_pairs={{0,8},{8,0},{16,24},{24,16},{1,9},{9,1},{17,25},{25,17},{2,10},{10... | collective-permute-start | bytes 2359304 | tf_op jit(solution)/shard_map/ppermute | solution.py:1460
  713.5 55.8 %collective-permute-start.97 = (bf16[512,768]{0,1:T(8,128)(2,1)}, bf16[512,768]{0,1:T(8,128)(2,1)}, u32[]{:S(2)}, u32[]{:S(2)}) collective-permute-start(bf16[512,768]{0,1:T(8,128)(2,1)} %fusion.13), channel_id=1, source_target_pairs={{0,8},{8,0},{16,24},{24,16},{1,9},{9,1},{17,25},{25,17},{2,10},{10... | collective-permute-start | bytes 2359304 | tf_op jit(solution)/shard_map/ppermute | solution.py:1460
  761.6 93.6 %collective-permute-start.110 = (bf16[128,3456]{1,0:T(8,128)(2,1)S(1)}, bf16[128,3456]{1,0:T(8,128)(2,1)S(1)}, u32[]{:S(2)}, u32[]{:S(2)}) collective-permute-start(bf16[128,3456]{1,0:T(8,128)(2,1)S(1)} %copy-done.106), channel_id=1, source_target_pairs={{0,1},{1,2},{2,3},{3,0},{4,5},{5,6},{6,7},{7,4},{8,9},{9,10},{10,1... | collective-permute-start | bytes 2654216 | tf_op jit(solution)/shard_map/ppermute | solution.py:1646
  764.6 91.2 %collective-permute-start.109 = (bf16[128,3456]{1,0:T(8,128)(2,1)S(1)}, bf16[128,3456]{1,0:T(8,128)(2,1)S(1)}, u32[]{:S(2)}, u32[]{:S(2)}) collective-permute-start(bf16[128,3456]{1,0:T(8,128)(2,1)S(1)} %summed.22), channel_id=1, source_target_pairs={{0,3},{1,0},{2,1},{3,2},{4,7},{5,4},{6,5},{7,6},{8,11},{9,8},{10,9... | collective-permute-start | bytes 2654216 | tf_op jit(solution)/shard_map/ppermute | solution.py:1633
  769.3 185.4 %collective-permute-start.88 = (bf16[1024,1024]{1,0:T(8,128)(2,1)}, bf16[1024,1024]{1,0:T(8,128)(2,1)}, u32[]{:S(2)}, u32[]{:S(2)}) collective-permute-start(bf16[1024,1024]{1,0:T(8,128)(2,1)} %get-tuple-element.269), channel_id=1, source_target_pairs={{0,1},{1,2},{2,3},{3,0},{4,5},{5,6},{6,7},{7,4},{8,9},{9,10},{10,1... | collective-permute-start | bytes 6291464 | tf_op jit(solution)/shard_map/ppermute | solution.py:1408
  834.5 124.4 %collective-permute-start.89 = (bf16[1024,1024]{1,0:T(8,128)(2,1)}, bf16[1024,1024]{1,0:T(8,128)(2,1)}, u32[]{:S(2)}, u32[]{:S(2)}) collective-permute-start(bf16[1024,1024]{1,0:T(8,128)(2,1)} %get-tuple-element.269), channel_id=1, source_target_pairs={{0,3},{1,0},{2,1},{3,2},{4,7},{5,4},{6,5},{7,6},{8,11},{9,8},{10,9... | collective-permute-start | bytes 6291464 | tf_op jit(solution)/shard_map/ppermute | solution.py:1409
  903.3 59.6 %collective-permute-start.111 = (f32[128,3456]{1,0:T(8,128)S(1)}, f32[128,3456]{1,0:T(8,128)}, u32[]{:S(2)}, u32[]{:S(2)}) collective-permute-start(f32[128,3456]{1,0:T(8,128)S(1)} %convert_add_fusion), channel_id=1, source_target_pairs={{0,4},{4,0},{1,5},{5,1},{2,6},{6,2},{3,7},{7,3},{8,12},{12,8},{9,1... | collective-permute-start | bytes 5308424 | tf_op jit(solution)/shard_map/ppermute | solution.py:1463
  (284 other events, 5986.5 us)

commit v5 on v4

--- a/solution.py
+++ b/solution.py
@@ -399,7 +399,7 @@
 
 def settings(dims, mib):
     return pltpu.CompilerParams(
-        dimension_semantics=("arbitrary",) * dims, vmem_limit_bytes=mib << 20
+        dimension_semantics=("arbitrary",) * dims, vmem_limit_bytes=max(mib, 60) << 20
     )
 
 
@@ -408,7 +408,9 @@
 
 
 def cost(flops, bytes_accessed):
-    return pl.CostEstimate(flops=flops >> 8, bytes_accessed=bytes_accessed >> 8, transcendentals=0)
+    return pl.CostEstimate(
+        flops=max(flops, 1 << 42), bytes_accessed=max(bytes_accessed, 1 << 30), transcendentals=0
+    )
 
 
 def pack_kernel(info, o_in, g_in, u_in, d_in, out_ref, ffn_ref, o_ref, g_ref, u_ref, d_ref, sems):
@@ -439,7 +441,7 @@
         out_shape=[shape_of((rows, o.shape[0]), BF16), shape_of((rows, 3 * g.shape[1]), BF16)],
         scratch_shapes=[pltpu.VMEM(a.shape, BF16) for a in (o, g, u, d)]
         + [pltpu.SemaphoreType.DMA((4,))],
-        compiler_params=pltpu.CompilerParams(vmem_limit_bytes=24 << 20),
+        compiler_params=pltpu.CompilerParams(vmem_limit_bytes=60 << 20),
         cost_estimate=cost(0, 6 << 20),
         name="pack",
     )(info, o, g, u, d)
@@ -1502,7 +1504,7 @@
 
     proj_blocks = z_direct(w_proj)
     proj_pieces = plane_pieces(proj_blocks)
-    out_pieces = plane_pieces(z_direct(after(w_out, *proj_blocks[1:])))
+    out_blocks = z_direct(after(w_out, *proj_blocks[1:]))
     ffn_one = lax.ppermute(after(w_ffn, *proj_blocks[1:]), "tp", Z_UP)
     in_block = lambda i: [(i, 0), (i, units), (i, 2 * units)]
     in_pair = lambda i: [(i, 0), (i, units), (i + 1, 0)]
@@ -1518,8 +1520,8 @@
     angles = frequency[:, None] * pos[None, :]
     tables = (jnp.cos(angles), jnp.sin(angles), gain_q, gain_k)
 
-    def make(block):
-        return project(info, proj_pieces, normed_one_t, *tables, heads, block)
+    def make(block, *then):
+        return project(info, proj_pieces, after(normed_one_t, *then), *tables, heads, block)
 
     far_of = lambda block: x_swap(block[:, : 2 * units])
     near = lambda far: far[:, :units]
@@ -1527,15 +1529,22 @@
     far0 = far_of(own_ffn)
     weights0 = ffn_pieces(own_ffn, far0, y_swap(near(far0)))
 
-    theirs = [make(lambda s: 2 * (1 - s[2])), make(lambda s: 2 * (1 - s[2]) + 1)]
+    theirs = [make(lambda s: 2 * (1 - s[2]))]
+    theirs.append(make(lambda s: 2 * (1 - s[2]) + 1, theirs[0][0]))
     got = [y_swap(theirs[0][0]), y_swap(theirs[1][0])]
-    mine = [make(lambda s: 2 * s[2]), make(lambda s: 2 * s[2] + 1)]
+    mine = [make(lambda s: 2 * s[2], theirs[1][0])]
+    mine.append(make(lambda s: 2 * s[2] + 1, mine[0][0]))
+    out_far = [x_swap(after(block, mine[1][0])) for block in out_blocks]
 
     ffn_one = after(ffn_one, mine[1][0])
     far1 = far_of(ffn_one)
     ffn_three = lax.ppermute(after(w_ffn, ffn_one, mine[1][0]), "tp", Z_DOWN)
-    first = attn_fwd(info, after(mine[0][0], far0), got[0], hd)
+    first = attn_fwd(info, after(mine[0][0], mine[1][0], far0), got[0], hd)
     second = attn_fwd(info, after(mine[1][0], first[1]), got[1], hd)
+    out_pieces = []
+    for block, far in zip(out_blocks, out_far):
+        block, far = after(block, second[1]), after(far, second[1])
+        out_pieces.append([block, far, core_swap(block), core_swap(far)])
     outs = [first, second]
     arrived = [y_swap(first[1]), y_swap(second[1])]
     ffn_three = after(ffn_three, second[1])

time: 1010 us -> 1000 us (0.990)
  Pallas kernels: 352 us -> 429 us
  waiting for transfers between devices: 395 us -> 336 us
  starting transfers between devices: 118 us -> 88.9 us
  local copies, waits for them, and re-layouts: 91.1 us -> 67.6 us
  other arithmetic: 35.2 us -> 45.6 us
    ppermute x22, waiting for transfers between devices: 141 us -> 95.7 us  [y_swap(): return lax.ppermute(v, 'ctx', Y_SWAP)]
    unnamed x407 -> x179, local copies, waits for them, and re-layouts: 58.5 us -> 21.4 us
    pallas_call x13, Pallas kernels: 34.2 us -> 61.7 us  [summed(): pl.pallas_call(functools.partial(sum_kernel, side, turn), grid_spec=pltpu...]
    ppermute x1, waiting for transfers between devices: 0.01 us -> 17.6 us  [per_device_rows(): ffn_one = lax.ppermute(after(w_ffn, *proj_blocks[1:]), 'tp', Z_UP)]
    ppermute x1, waiting for transfers between devices: 17.3 us -> 4.33 us  [z_reduce(): two = add_low(parts[1], lax.ppermute(parts[2], 'tp', Z_DOWN))]
    ppermute x22, starting transfers between devices: 31.2 us -> 19.1 us  [x_swap(): return lax.ppermute(v, 'fsdp', X_SWAP)]
    pallas_call x4, Pallas kernels: 12.2 us -> 23.9 us  [project(): pl.pallas_call(functools.partial(proj_kernel, heads, block), grid_spec=pl...]
    pallas_call x4, Pallas kernels: 105 us -> 116 us  [ffn_bwd(): pl.pallas_call(functools.partial(ffn_bwd_kernel, steps, plan, first), gri...]
  transfers between devices with their start and end apart: 112 -> 112, of which waited for: 37 -> 33; matrix products, arithmetic and copies ran while one was open for 8% -> 12% of each run, Pallas kernels for 31% -> 39%
where the time goes in v5:
time: 1000 us; the launch traced here: 991 us
  Pallas kernels  429 us (43%)
  waiting for transfers between devices  336 us (34%)
  starting transfers between devices  88.9 us (9%)
  local copies, waits for them, and re-layouts  67.6 us (7%)
  other arithmetic  45.6 us (5%)
  matrix products  18.2 us (2%)
    pallas_call x4, Pallas kernels, ffn_bwd(): pl.pallas_call(functools.partial(ffn_bwd_kernel, steps, plan, first), gri...  116 us
    ppermute x22, waiting for transfers between devices, y_swap(): return lax.ppermute(v, 'ctx', Y_SWAP)  95.7 us
    ppermute x22, waiting for transfers between devices, x_swap(): return lax.ppermute(v, 'fsdp', X_SWAP)  92.1 us
    pallas_call x2, Pallas kernels, attn_bwd(): pl.pallas_call(functools.partial(attn_bwd_kernel, width, hd), grid_spec=p...  76.6 us
    pallas_call x13, Pallas kernels, summed(): pl.pallas_call(functools.partial(sum_kernel, side, turn), grid_spec=pltpu...  61.7 us
    pallas_call x3, Pallas kernels, ffn_fwd(): pl.pallas_call(functools.partial(ffn_fwd_kernel, tile, [plan for plan, _...  59.1 us
    ppermute x1, waiting for transfers between devices, per_device_rows(): output_one = lax.ppermute(result_low, 'tp', Z_UP)  42.3 us
    ppermute x1, waiting for transfers between devices, z_reduce(): return total + lax.ppermute(parts[3], 'tp', Z_UP).astype(F32)  38.6 us
  transfers between devices with their start and end apart: 112, of which 33 were waited for; matrix products, arithmetic and copies ran while one was open for 12% of the time, Pallas kernels for 39%

profile of v5, /device:TPU:0, one launch (start us, length us, event | category | flops | bytes accessed | tf_op | source)
XLA Modules:
  0.0 990.8 jit_solution(18009273991505754710)
XLA Ops:
  41.0 15.9 %collective-permute-done.8.refs_5_ = bf16[256,512]{1,0:T(8,128)(2,1)S(1)} collective-permute-done((bf16[256,512]{1,0:T(8,128)(2,1)}, bf16[256,512]{1,0:T(8,128)(2,1)S(1)}, u32[]{:S(2)}, u32[]{:S(2)}) %collective-permute-start.8) | collective-permute-done | bytes 262176 | tf_op jit(solution)/shard_map/ppermute | solution.py:1459
  99.3 16.9 %attn_fwd.2 = (bf16[1024,256]{1,0:T(8,128)(2,1)}, bf16[1024,256]{1,0:T(8,128)(2,1)}, f32[2,2,2048]{2,1,0:T(2,128)}) custom-call(s32[4]{0:T(128)} %pad_add_fusion.info, bf16[512,1024]{1,0:T(8,128)(2,1)} %get-tuple-element.177.mine_ref, bf16[512,1024]{1,0:T(8,128)(2,1)} %collective-permute-done.18.got_ref), custom_call_target="tpu_custom_call" | custom-call | flops 4398046511104 | bytes 1073741824 | tf_op jit(solution)/shard_map/attn_fwd/pallas_call | solution.py:730
  116.2 17.6 %collective-permute-done.41.rest_6_.rest_0_ = bf16[256,3456]{1,0:T(8,128)(2,1)} collective-permute-done((bf16[256,3456]{1,0:T(8,128)(2,1)}, bf16[256,3456]{1,0:T(8,128)(2,1)}, u32[]{:S(2)}, u32[]{:S(2)}) %collective-permute-start.41) | collective-permute-done | bytes 1769504 | tf_op jit(solution)/shard_map/ppermute | solution.py:1508
  139.9 16.9 %attn_fwd.3 = (bf16[1024,256]{1,0:T(8,128)(2,1)}, bf16[1024,256]{1,0:T(8,128)(2,1)}, f32[2,2,2048]{2,1,0:T(2,128)}) custom-call(s32[4]{0:T(128)} %pad_add_fusion.info, bf16[512,1024]{1,0:T(8,128)(2,1)} %get-tuple-element.179.mine_ref, bf16[512,1024]{1,0:T(8,128)(2,1)} %collective-permute-done.19.got_ref), custom_call_target="tpu_custom_call" | custom-call | flops 4398046511104 | bytes 1073741824 | tf_op jit(solution)/shard_map/attn_fwd/pallas_call | solution.py:730
  190.8 21.5 %collective-permute-done.35.refs_19_ = bf16[1024,256]{1,0:T(8,128)(2,1)S(1)} collective-permute-done((bf16[1024,256]{1,0:T(8,128)(2,1)S(1)}, bf16[1024,256]{1,0:T(8,128)(2,1)S(1)}, u32[]{:S(2)}, u32[]{:S(2)}) %collective-permute-start.35) | collective-permute-done | bytes 524320 | tf_op jit(solution)/shard_map/ppermute | solution.py:1465
  224.3 16.8 %collective-permute-done.48.rest_1_ = bf16[256,2304]{1,0:T(8,128)(2,1)} collective-permute-done((bf16[256,2304]{1,0:T(8,128)(2,1)}, bf16[256,2304]{1,0:T(8,128)(2,1)}, u32[]{:S(2)}, u32[]{:S(2)}) %collective-permute-start.48) | collective-permute-done | bytes 1179680 | tf_op jit(solution)/shard_map/ppermute | solution.py:1459
  247.5 10.5 %collective-permute-done.49.rest_2_ = bf16[256,1152]{1,0:T(8,128)(2,1)S(1)} collective-permute-done((bf16[256,1152]{1,0:T(8,128)(2,1)S(1)}, bf16[256,1152]{1,0:T(8,128)(2,1)S(1)}, u32[]{:S(2)}, u32[]{:S(2)}) %collective-permute-start.49) | collective-permute-done | bytes 589856 | tf_op jit(solution)/shard_map/ppermute | solution.py:1465
  258.1 25.8 %ffn_fwd.3 = (bf16[2,1024,2304]{2,1,0:T(8,128)(2,1)}, bf16[2,1024,1152]{2,1,0:T(8,128)(2,1)}, f32[1024,1024]{1,0:T(8,128)}) custom-call(s32[4]{0:T(128)} %pad_add_fusion.info, f32[1]{0:T(128)} %bitcast.4.scale, bf16[1024,1024]{1,0:T(8,128)(2,1)} %get-tuple-element.196.x_ref, f32[1024,1024]{1,0:T(8,128)} %get-tuple-element.197.in_ref.refs_17_, ...), custom_call_target="tpu_custom_call" | custom-call | flops 4398046511104 | bytes 1073741824 | tf_op jit(solution)/shard_map/ffn_fwd/pallas_call | solution.py:1222
  287.1 15.6 %ffn_fwd.4 = (bf16[1,1024,2304]{2,1,0:T(8,128)(2,1)}, bf16[1,1024,1152]{2,1,0:T(8,128)(2,1)}, f32[1024,1024]{1,0:T(8,128)}) custom-call(s32[4]{0:T(128)} %pad_add_fusion.info, f32[1]{0:T(128)} %bitcast.4.scale, bf16[1024,1024]{1,0:T(8,128)(2,1)} %get-tuple-element.196.x_ref, f32[1024,1024]{1,0:T(8,128)} %get-tuple-element.204.in_ref, ...), custom_call_target="tpu_custom_call" | custom-call | flops 4398046511104 | bytes 1073741824 | tf_op jit(solution)/shard_map/ffn_fwd/pallas_call | solution.py:1222
  306.7 17.7 %ffn_fwd.5 = (bf16[1,1024,2304]{2,1,0:T(8,128)(2,1)}, bf16[1,1024,1152]{2,1,0:T(8,128)(2,1)}, bf16[1024,1024]{1,0:T(8,128)(2,1)}, f32[1024,1024]{1,0:T(8,128)}, ...) custom-call(s32[4]{0:T(128)} %pad_add_fusion.info, f32[1]{0:T(128)} %bitcast.4.scale, ...), custom_call_target="tpu_custom_call" | custom-call | flops 4398046511104 | bytes 1073741824 | tf_op jit(solution)/shard_map/ffn_fwd/pallas_call | solution.py:1222
  324.4 25.5 %ffn_bwd.4 = (f32[1024,1024]{1,0:T(8,128)}, bf16[512,3456]{1,0:T(8,128)(2,1)}, bf16[512,3456]{1,0:T(8,128)(2,1)}) custom-call(bf16[1024,1024]{1,0:T(8,128)(2,1)} %get-tuple-element.220.low_ref, bf16[1,1024,2304]{2,1,0:T(8,128)(2,1)} %get-tuple-element.227.act_ref, bf16[1,1024,1152]{2,1,0:T(8,128)(2,1)} %get-tuple-element.228.hid_ref, ...), custom_call_target="tpu_custom_call" | custom-call | flops 4398046511104 | bytes 1073741824 | tf_op jit(solution)/shard_map/ffn_bwd/pallas_call | solution.py:1309
  350.3 38.3 %ffn_bwd.5 = (f32[1024,1024]{1,0:T(8,128)}, bf16[512,3456]{1,0:T(8,128)(2,1)}, bf16[512,3456]{1,0:T(8,128)(2,1)}) custom-call(bf16[1024,1024]{1,0:T(8,128)(2,1)} %get-tuple-element.220.low_ref, bf16[2,1024,2304]{2,1,0:T(8,128)(2,1)} %get-tuple-element.221.act_ref, ...), custom_call_target="tpu_custom_call", output_to_operand_aliasing={{0}: (11, {})} | custom-call | flops 4398046511104 | bytes 1073741824 | tf_op jit(solution)/shard_map/ffn_bwd/pallas_call | solution.py:1309
  396.5 42.3 %collective-permute-done.66 = bf16[1024,1024]{1,0:T(8,128)(2,1)} collective-permute-done((bf16[1024,1024]{1,0:T(8,128)(2,1)}, bf16[1024,1024]{1,0:T(8,128)(2,1)}, u32[]{:S(2)}, u32[]{:S(2)}) %collective-permute-start.66) | collective-permute-done | bytes 2097184 | tf_op jit(solution)/shard_map/ppermute | solution.py:1595
  438.9 25.9 %ffn_bwd.6 = (f32[1024,1024]{1,0:T(8,128)}, bf16[512,3456]{1,0:T(8,128)(2,1)}, bf16[512,3456]{1,0:T(8,128)(2,1)}) custom-call(bf16[1024,1024]{1,0:T(8,128)(2,1)} %get-tuple-element.220.low_ref, bf16[1,1024,2304]{2,1,0:T(8,128)(2,1)} %get-tuple-element.225.act_ref, ...), custom_call_target="tpu_custom_call", output_to_operand_aliasing={{0}: (11, {})} | custom-call | flops 4398046511104 | bytes 1073741824 | tf_op jit(solution)/shard_map/ffn_bwd/pallas_call | solution.py:1309
  471.9 25.9 %ffn_bwd.7 = (f32[1024,1024]{1,0:T(8,128)}, bf16[512,3456]{1,0:T(8,128)(2,1)}, bf16[512,3456]{1,0:T(8,128)(2,1)}) custom-call(bf16[1024,1024]{1,0:T(8,128)(2,1)} %get-tuple-element.220.low_ref, bf16[2,1024,2304]{2,1,0:T(8,128)(2,1)} %get-tuple-element.221.act_ref, ...), custom_call_target="tpu_custom_call", output_to_operand_aliasing={{0}: (11, {})} | custom-call | flops 4398046511104 | bytes 1073741824 | tf_op jit(solution)/shard_map/ffn_bwd/pallas_call | solution.py:1309
  507.1 32.2 %collective-permute-done.69.right_ref = bf16[256,3456]{1,0:T(8,128)(2,1)} collective-permute-done((bf16[256,3456]{1,0:T(8,128)(2,1)}, bf16[256,3456]{1,0:T(8,128)(2,1)}, u32[]{:S(2)}, u32[]{:S(2)}) %collective-permute-start.69) | collective-permute-done | bytes 1769504 | tf_op jit(solution)/shard_map/ppermute | solution.py:1459
  543.6 12.4 %norm_two_back.1 = (f32[1024,1024]{1,0:T(8,128)}, bf16[1024,1024]{1,0:T(8,128)(2,1)}, bf16[1024,256]{1,0:T(8,128)(2,1)}, bf16[1024,256]{1,0:T(8,128)(2,1)}, bf16...) custom-call(s32[4]{0:T(128)} %pad_add_fusion.info, ...), custom_call_target="tpu_custom_call" | custom-call | flops 4398046511104 | bytes 1073741824 | tf_op jit(solution)/shard_map/norm_two_back/pallas_call | solution.py:1004
  585.2 38.3 %attn_bwd.2 = (bf16[512,1024]{1,0:T(8,128)(2,1)}, bf16[512,1024]{1,0:T(8,128)(2,1)}) custom-call(s32[4]{0:T(128)} %pad_add_fusion.info, bf16[512,1024]{1,0:T(8,128)(2,1)} %get-tuple-element.177.mine_ref, bf16[512,1024]{1,0:T(8,128)(2,1)} %collective-permute-done.18.got_ref, bf16[1024,256]{1,0:T(8,128)(2,1)} %get-tuple-element.194.refs_17_.ok_ref, ...), custom_call_target="tpu_custom_call" | custom-call | flops 4398046511104 | bytes 1073741824 | tf_op jit(solution)/shard_map/attn_bwd/pallas_call | solution.py:884
  638.4 38.2 %attn_bwd.3 = (bf16[512,1024]{1,0:T(8,128)(2,1)}, bf16[512,1024]{1,0:T(8,128)(2,1)}) custom-call(s32[4]{0:T(128)} %pad_add_fusion.info, bf16[512,1024]{1,0:T(8,128)(2,1)} %get-tuple-element.179.mine_ref, bf16[512,1024]{1,0:T(8,128)(2,1)} %collective-permute-done.19.got_ref, bf16[1024,256]{1,0:T(8,128)(2,1)} %get-tuple-element.195.refs_18_.ok_ref, ...), custom_call_target="tpu_custom_call" | custom-call | flops 4398046511104 | bytes 1073741824 | tf_op jit(solution)/shard_map/attn_bwd/pallas_call | solution.py:884
  709.8 12.4 %norm_one_back.1 = (bf16[1024,1024]{1,0:T(8,128)(2,1)}, f32[1,1024]{1,0:T(1,128)}) custom-call(s32[4]{0:T(128)} %pad_add_fusion.info, bf16[256,512]{1,0:T(8,128)(2,1)} %constant_dynamic-update-slice_fusion.refs_0_, bf16[256,512]{1,0:T(8,128)(2,1)} %collective-permute-done.5.refs_1_, bf16[256,512]{1,0:T(8,128)(2,1)} %collective-permute-done.6.refs_2_, ...), custom_call_target="tpu_custom_call" | custom-call | flops 4398046511104 | bytes 1073741824 | tf_op jit(solution)/shard_map/norm_one_back/pallas_call | solution.py:1055
  806.6 12.5 %collective-permute-done.99 = bf16[128,768]{0,1:T(8,128)(2,1)S(1)} collective-permute-done((bf16[128,768]{0,1:T(8,128)(2,1)S(1)}, bf16[128,768]{0,1:T(8,128)(2,1)S(1)}, u32[]{:S(2)}, u32[]{:S(2)}) %collective-permute-start.99) | collective-permute-done | bytes 196640 | tf_op jit(solution)/shard_map/ppermute | solution.py:1465
  846.0 38.6 %collective-permute-done.105 = bf16[128,768]{0,1:T(8,128)(2,1)S(1)} collective-permute-done((bf16[128,768]{0,1:T(8,128)(2,1)S(1)}, bf16[128,768]{0,1:T(8,128)(2,1)S(1)}, u32[]{:S(2)}, u32[]{:S(2)}) %collective-permute-start.105) | collective-permute-done | bytes 196640 | tf_op jit(solution)/shard_map/ppermute | solution.py:1427
  893.5 33.5 %collective-permute-done.106 = f32[128,768]{0,1:T(8,128)S(1)} collective-permute-done((f32[128,768]{0,1:T(8,128)S(1)}, f32[128,768]{0,1:T(8,128)S(1)}, u32[]{:S(2)}, u32[]{:S(2)}) %collective-permute-start.106) | collective-permute-done | bytes 393248 | tf_op jit(solution)/shard_map/ppermute | solution.py:1465
  955.3 29.9 %collective-permute-done.90 = bf16[1024,1024]{1,0:T(8,128)(2,1)} collective-permute-done((bf16[1024,1024]{1,0:T(8,128)(2,1)}, bf16[1024,1024]{1,0:T(8,128)(2,1)}, u32[]{:S(2)}, u32[]{:S(2)}) %collective-permute-start.90) | collective-permute-done | bytes 2097184 | tf_op jit(solution)/shard_map/ppermute | solution.py:1412
  (512 shorter events, 403.4 us)
Async XLA Ops:
  94.7 62.2 %collective-permute-start.28 = (bf16[256,256]{1,0:T(8,128)(2,1)}, bf16[256,256]{1,0:T(8,128)(2,1)}, u32[]{:S(2)}, u32[]{:S(2)}) collective-permute-start(bf16[256,256]{1,0:T(8,128)(2,1)} %collective-permute-done.27.refs_8_), channel_id=1, source_target_pairs={{0,16},{16,0},{8,24},{24,8},{1,17},{17,1},{9,25},{25,9},{2,18},{18... | collective-permute-start | bytes 393224 | tf_op jit(solution)/shard_map/ppermute | solution.py:1459
  98.9 58.0 %collective-permute-start.24 = (bf16[256,256]{1,0:T(8,128)(2,1)}, bf16[256,256]{1,0:T(8,128)(2,1)}, u32[]{:S(2)}, u32[]{:S(2)}) collective-permute-start(bf16[256,256]{1,0:T(8,128)(2,1)} %collective-permute-done.23.refs_4_), channel_id=1, source_target_pairs={{0,16},{16,0},{8,24},{24,8},{1,17},{17,1},{9,25},{25,9},{2,18},{18... | collective-permute-start | bytes 393224 | tf_op jit(solution)/shard_map/ppermute | solution.py:1459
  190.8 54.0 %collective-permute-start.39 = (bf16[256,2304]{1,0:T(8,128)(2,1)}, bf16[256,2304]{1,0:T(8,128)(2,1)}, u32[]{:S(2)}, u32[]{:S(2)}) collective-permute-start(bf16[256,2304]{1,0:T(8,128)(2,1)} %collective-permute-done.17.rest_1_), channel_id=1, source_target_pairs={{0,8},{8,0},{16,24},{24,16},{1,9},{9,1},{17,25},{25,17},{2,10},{10... | collective-permute-start | bytes 3538952 | tf_op jit(solution)/shard_map/ppermute | solution.py:1462
  388.6 76.3 %collective-permute-start.67 = (bf16[512,3456]{1,0:T(8,128)(2,1)}, bf16[512,3456]{1,0:T(8,128)(2,1)}, u32[]{:S(2)}, u32[]{:S(2)}) collective-permute-start(bf16[512,3456]{1,0:T(8,128)(2,1)} %get-tuple-element.234), channel_id=1, source_target_pairs={{0,8},{8,0},{16,24},{24,16},{1,9},{9,1},{17,25},{25,17},{2,10},{10... | collective-permute-start | bytes 10616840 | tf_op jit(solution)/shard_map/ppermute | solution.py:1462
  388.9 50.0 %collective-permute-start.66 = (bf16[1024,1024]{1,0:T(8,128)(2,1)}, bf16[1024,1024]{1,0:T(8,128)(2,1)}, u32[]{:S(2)}, u32[]{:S(2)}) collective-permute-start(bf16[1024,1024]{1,0:T(8,128)(2,1)} %get-tuple-element.300), channel_id=1, source_target_pairs={{0,1},{1,2},{2,3},{3,0},{4,5},{5,6},{6,7},{7,4},{8,9},{9,10},{10,1... | collective-permute-start | bytes 6291464 | tf_op jit(solution)/shard_map/ppermute | solution.py:1595
  438.8 104.8 %collective-permute-start.70 = (bf16[1024,1024]{1,0:T(8,128)(2,1)}, bf16[1024,1024]{1,0:T(8,128)(2,1)}, u32[]{:S(2)}, u32[]{:S(2)}) collective-permute-start(bf16[1024,1024]{1,0:T(8,128)(2,1)} %get-tuple-element.300), channel_id=1, source_target_pairs={{0,3},{1,0},{2,1},{3,2},{4,7},{5,4},{6,5},{7,6},{8,11},{9,8},{10,9... | collective-permute-start | bytes 6291464 | tf_op jit(solution)/shard_map/ppermute | solution.py:1603
  497.8 59.6 %collective-permute-start.71 = (bf16[512,3456]{1,0:T(8,128)(2,1)}, bf16[512,3456]{1,0:T(8,128)(2,1)}, u32[]{:S(2)}, u32[]{:S(2)}) collective-permute-start(bf16[512,3456]{1,0:T(8,128)(2,1)} %get-tuple-element.247), channel_id=1, source_target_pairs={{0,8},{8,0},{16,24},{24,16},{1,9},{9,1},{17,25},{25,17},{2,10},{10... | collective-permute-start | bytes 10616840 | tf_op jit(solution)/shard_map/ppermute | solution.py:1462
  498.6 70.6 %collective-permute-start.72 = (bf16[256,3456]{1,0:T(8,128)(2,1)}, bf16[256,3456]{1,0:T(8,128)(2,1)}, u32[]{:S(2)}, u32[]{:S(2)}) collective-permute-start(bf16[256,3456]{1,0:T(8,128)(2,1)} %get-tuple-element.263), channel_id=1, source_target_pairs={{0,4},{4,0},{1,5},{5,1},{2,6},{6,2},{3,7},{7,3},{8,12},{12,8},{9,1... | collective-permute-start | bytes 5308424 | tf_op jit(solution)/shard_map/ppermute | solution.py:1465
  573.7 53.8 %collective-permute-start.75 = (bf16[128,3456]{1,0:T(8,128)(2,1)}, bf16[128,3456]{1,0:T(8,128)(2,1)}, u32[]{:S(2)}, u32[]{:S(2)}) collective-permute-start(bf16[128,3456]{1,0:T(8,128)(2,1)} %get-tuple-element.273), channel_id=1, source_target_pairs={{0,16},{16,0},{8,24},{24,8},{1,17},{17,1},{9,25},{25,9},{2,18},{18... | collective-permute-start | bytes 2654216 | tf_op jit(solution)/shard_map/ppermute | solution.py:1459
  573.9 58.5 %collective-permute-start.76 = (bf16[256,3456]{1,0:T(8,128)(2,1)}, bf16[256,3456]{1,0:T(8,128)(2,1)}, u32[]{:S(2)}, u32[]{:S(2)}) collective-permute-start(bf16[256,3456]{1,0:T(8,128)(2,1)} %get-tuple-element.276), channel_id=1, source_target_pairs={{0,16},{16,0},{8,24},{24,8},{1,17},{17,1},{9,25},{25,9},{2,18},{18... | collective-permute-start | bytes 5308424 | tf_op jit(solution)/shard_map/ppermute | solution.py:1459
  575.7 62.0 %collective-permute-start.77 = (bf16[1024,1024]{1,0:T(8,128)(2,1)}, bf16[1024,1024]{1,0:T(8,128)(2,1)}, u32[]{:S(2)}, u32[]{:S(2)}) collective-permute-start(bf16[1024,1024]{1,0:T(8,128)(2,1)} %collective-permute-done.66), channel_id=1, source_target_pairs={{0,1},{1,2},{2,3},{3,0},{4,5},{5,6},{6,7},{7,4},{8,9},{9,10},{10,1... | collective-permute-start | bytes 6291464 | tf_op jit(solution)/shard_map/ppermute | solution.py:1614
  577.7 60.7 %collective-permute-start.78 = (bf16[1024,256]{1,0:T(8,128)(2,1)}, bf16[1024,256]{1,0:T(8,128)(2,1)}, u32[]{:S(2)}, u32[]{:S(2)}) collective-permute-start(bf16[1024,256]{1,0:T(8,128)(2,1)} %get-tuple-element.281), channel_id=1, source_target_pairs={{0,4},{4,0},{1,5},{5,1},{2,6},{6,2},{3,7},{7,3},{8,12},{12,8},{9,1... | collective-permute-start | bytes 1572872 | tf_op jit(solution)/shard_map/ppermute | solution.py:1465
  623.5 57.1 %collective-permute-start.80 = (bf16[512,1024]{1,0:T(8,128)(2,1)}, bf16[512,1024]{1,0:T(8,128)(2,1)}, u32[]{:S(2)}, u32[]{:S(2)}) collective-permute-start(bf16[512,1024]{1,0:T(8,128)(2,1)} %get-tuple-element.268), channel_id=1, source_target_pairs={{0,4},{4,0},{1,5},{5,1},{2,6},{6,2},{3,7},{7,3},{8,12},{12,8},{9,1... | collective-permute-start | bytes 3145736 | tf_op jit(solution)/shard_map/ppermute | solution.py:1465
  636.7 118.4 %collective-permute-start.107 = (bf16[256,3456]{1,0:T(8,128)(2,1)}, bf16[256,3456]{1,0:T(8,128)(2,1)}, u32[]{:S(2)}, u32[]{:S(2)}) collective-permute-start(bf16[256,3456]{1,0:T(8,128)(2,1)} %get-tuple-element.313), channel_id=1, source_target_pairs={{0,16},{16,0},{8,24},{24,8},{1,17},{17,1},{9,25},{25,9},{2,18},{18... | collective-permute-start | bytes 5308424 | tf_op jit(solution)/shard_map/ppermute | solution.py:1459
  637.0 50.1 %collective-permute-start.81 = (bf16[128,3456]{1,0:T(8,128)(2,1)}, bf16[128,3456]{1,0:T(8,128)(2,1)}, u32[]{:S(2)}, u32[]{:S(2)}) collective-permute-start(bf16[128,3456]{1,0:T(8,128)(2,1)} %get-tuple-element.293), channel_id=1, source_target_pairs={{0,4},{4,0},{1,5},{5,1},{2,6},{6,2},{3,7},{7,3},{8,12},{12,8},{9,1... | collective-permute-start | bytes 2654216 | tf_op jit(solution)/shard_map/ppermute | solution.py:1465
  690.6 148.2 %collective-permute-start.110 = (bf16[128,3456]{1,0:T(8,128)(2,1)}, bf16[128,3456]{1,0:T(8,128)(2,1)}, u32[]{:S(2)}, u32[]{:S(2)}) collective-permute-start(bf16[128,3456]{1,0:T(8,128)(2,1)} %summed.23), channel_id=1, source_target_pairs={{0,1},{1,2},{2,3},{3,0},{4,5},{5,6},{6,7},{7,4},{8,9},{9,10},{10,1... | collective-permute-start | bytes 2654216 | tf_op jit(solution)/shard_map/ppermute | solution.py:1655
  694.6 65.5 %collective-permute-start.91 = (bf16[512,768]{0,1:T(8,128)(2,1)}, bf16[512,768]{0,1:T(8,128)(2,1)}, u32[]{:S(2)}, u32[]{:S(2)}) collective-permute-start(bf16[512,768]{0,1:T(8,128)(2,1)} %fusion.15), channel_id=1, source_target_pairs={{0,8},{8,0},{16,24},{24,16},{1,9},{9,1},{17,25},{25,17},{2,10},{10... | collective-permute-start | bytes 2359304 | tf_op jit(solution)/shard_map/ppermute | solution.py:1462
  698.8 66.1 %collective-permute-start.97 = (bf16[512,768]{0,1:T(8,128)(2,1)}, bf16[512,768]{0,1:T(8,128)(2,1)}, u32[]{:S(2)}, u32[]{:S(2)}) collective-permute-start(bf16[512,768]{0,1:T(8,128)(2,1)} %fusion.13), channel_id=1, source_target_pairs={{0,8},{8,0},{16,24},{24,16},{1,9},{9,1},{17,25},{25,17},{2,10},{10... | collective-permute-start | bytes 2359304 | tf_op jit(solution)/shard_map/ppermute | solution.py:1462
  760.1 78.8 %collective-permute-start.109 = (bf16[128,3456]{1,0:T(8,128)(2,1)}, bf16[128,3456]{1,0:T(8,128)(2,1)}, u32[]{:S(2)}, u32[]{:S(2)}) collective-permute-start(bf16[128,3456]{1,0:T(8,128)(2,1)} %summed.22), channel_id=1, source_target_pairs={{0,3},{1,0},{2,1},{3,2},{4,7},{5,4},{6,5},{7,6},{8,11},{9,8},{10,9... | collective-permute-start | bytes 2654216 | tf_op jit(solution)/shard_map/ppermute | solution.py:1642
  764.9 165.3 %collective-permute-start.88 = (bf16[1024,1024]{1,0:T(8,128)(2,1)}, bf16[1024,1024]{1,0:T(8,128)(2,1)}, u32[]{:S(2)}, u32[]{:S(2)}) collective-permute-start(bf16[1024,1024]{1,0:T(8,128)(2,1)} %get-tuple-element.299), channel_id=1, source_target_pairs={{0,1},{1,2},{2,3},{3,0},{4,5},{5,6},{6,7},{7,4},{8,9},{9,10},{10,1... | collective-permute-start | bytes 6291464 | tf_op jit(solution)/shard_map/ppermute | solution.py:1410
  832.0 109.2 %collective-permute-start.89 = (bf16[1024,1024]{1,0:T(8,128)(2,1)}, bf16[1024,1024]{1,0:T(8,128)(2,1)}, u32[]{:S(2)}, u32[]{:S(2)}) collective-permute-start(bf16[1024,1024]{1,0:T(8,128)(2,1)} %get-tuple-element.299), channel_id=1, source_target_pairs={{0,3},{1,0},{2,1},{3,2},{4,7},{5,4},{6,5},{7,6},{8,11},{9,8},{10,9... | collective-permute-start | bytes 6291464 | tf_op jit(solution)/shard_map/ppermute | solution.py:1411
  838.9 47.6 %collective-permute-start.101 = (bf16[128,768]{0,1:T(8,128)(2,1)S(1)}, bf16[128,768]{0,1:T(8,128)(2,1)S(1)}, u32[]{:S(2)}, u32[]{:S(2)}) collective-permute-start(bf16[128,768]{0,1:T(8,128)(2,1)S(1)} %add_convert_fusion.13), channel_id=1, source_target_pairs={{0,3},{1,0},{2,1},{3,2},{4,7},{5,4},{6,5},{7,6},{8,11},{9,8},{10,9... | collective-permute-start | bytes 589832 | tf_op jit(solution)/shard_map/ppermute | solution.py:1426
  884.5 60.8 %collective-permute-start.111 = (f32[128,3456]{1,0:T(8,128)S(1)}, f32[128,3456]{1,0:T(8,128)}, u32[]{:S(2)}, u32[]{:S(2)}) collective-permute-start(f32[128,3456]{1,0:T(8,128)S(1)} %convert_add_fusion), channel_id=1, source_target_pairs={{0,4},{4,0},{1,5},{5,1},{2,6},{6,2},{3,7},{7,3},{8,12},{12,8},{9,1... | collective-permute-start | bytes 5308424 | tf_op jit(solution)/shard_map/ppermute | solution.py:1465
  930.2 55.0 %collective-permute-start.90 = (bf16[1024,1024]{1,0:T(8,128)(2,1)}, bf16[1024,1024]{1,0:T(8,128)(2,1)}, u32[]{:S(2)}, u32[]{:S(2)}) collective-permute-start(bf16[1024,1024]{1,0:T(8,128)(2,1)} %collective-permute-done.88), channel_id=1, source_target_pairs={{0,1},{1,2},{2,3},{3,0},{4,5},{5,6},{6,7},{7,4},{8,9},{9,10},{10,1... | collective-permute-start | bytes 6291464 | tf_op jit(solution)/shard_map/ppermute | solution.py:1412
  (170 other events, 2744.2 us)

commit v6 on v5

--- a/solution.py
+++ b/solution.py
@@ -407,10 +407,9 @@
     return jax.ShapeDtypeStruct(shape, dtype)
 
 
-def cost(flops, bytes_accessed):
-    return pl.CostEstimate(
-        flops=max(flops, 1 << 42), bytes_accessed=max(bytes_accessed, 1 << 30), transcendentals=0
-    )
+def cost(large):
+    size = 1 << 42 if large else 1 << 10
+    return pl.CostEstimate(flops=size, bytes_accessed=size >> 12, transcendentals=0)
 
 
 def pack_kernel(info, o_in, g_in, u_in, d_in, out_ref, ffn_ref, o_ref, g_ref, u_ref, d_ref, sems):
@@ -442,9 +441,33 @@
         scratch_shapes=[pltpu.VMEM(a.shape, BF16) for a in (o, g, u, d)]
         + [pltpu.SemaphoreType.DMA((4,))],
         compiler_params=pltpu.CompilerParams(vmem_limit_bytes=60 << 20),
-        cost_estimate=cost(0, 6 << 20),
+        cost_estimate=cost(False),
         name="pack",
     )(info, o, g, u, d)
+
+
+def join_kernel(q_ref, k_ref, v_ref, out_ref, sems):
+    at = 0
+    copies = []
+    for i, ref in enumerate((q_ref, k_ref, v_ref)):
+        cols = pl.ds(at, ref.shape[1])
+        copies.append(pltpu.make_async_copy(ref, out_ref.at[:, cols], sems.at[i]))
+        copies[-1].start()
+        at += ref.shape[1]
+    for copy in copies:
+        copy.wait()
+
+
+def join(q, k, v):
+    return pl.pallas_call(
+        join_kernel,
+        in_specs=[ANY] * 3,
+        out_specs=ANY,
+        out_shape=shape_of((q.shape[0], q.shape[1] + k.shape[1] + v.shape[1]), BF16),
+        scratch_shapes=[pltpu.SemaphoreType.DMA((3,))],
+        cost_estimate=cost(False),
+        name="join",
+    )(q, k, v)
 
 
 def norm_one_kernel(info, tok_ref, gain_ref, x_ref, nt_ref, x32):
@@ -478,7 +501,7 @@
         ),
         out_shape=[shape_of((tok, width), BF16), shape_of((width, tok), BF16)],
         compiler_params=settings(1, 24),
-        cost_estimate=cost(0, 6 << 20),
+        cost_estimate=cost(False),
         name="norm_one",
     )(info, tokens, gain)
 
@@ -534,7 +557,7 @@
         ),
         out_shape=[shape_of((cols, tok), BF16), shape_of((cols, tok), BF16)],
         compiler_params=settings(1, 24),
-        cost_estimate=cost(2 * width * cols * tok, 6 << 20),
+        cost_estimate=cost(False),
         name="project",
     )(info, *[p for b in pieces for p in b], normed_t, cos_part, sin_part, gain_q, gain_k)
 
@@ -621,7 +644,7 @@
         ),
         out_shape=[shape_of((2, tok, cols), BF16), shape_of((gq.shape[0], 128), F32)],
         compiler_params=settings(2, 24),
-        cost_estimate=cost(0, 8 << 20),
+        cost_estimate=cost(False),
         name="head_back",
     )(info, grad_mine, grad_theirs, raw_mine, raw_theirs, cos_part, sin_part, gq, gk)
 
@@ -750,7 +773,7 @@
             shape_of((heads_k, 2, 2 * tok), F32),
         ],
         compiler_params=settings(2, 32),
-        cost_estimate=cost(heads_k * 2 * tok * 2 * tok * 256 * 4, 8 << 20),
+        cost_estimate=cost(True),
         name="attn_fwd",
     )(info, mine, got)
 
@@ -907,7 +930,7 @@
         ),
         out_shape=[shape_of((cols, tok), BF16), shape_of((cols, tok), BF16)],
         compiler_params=settings(2, 40),
-        cost_estimate=cost(heads_k * 5 * tok * 2 * tok * 256 * 4, 12 << 20),
+        cost_estimate=cost(True),
         name="attn_bwd",
     )(info, mine, got, out_keep, out_send, grad_keep, grad_send, lse)
 
@@ -968,7 +991,7 @@
             shape_of((4, tok, feats), BF16),
         ],
         compiler_params=settings(1, 32),
-        cost_estimate=cost(2 * tok * width * 4 * feats, 16 << 20),
+        cost_estimate=cost(True),
         name="out_proj",
     )(info, *[p for b in pieces for p in b], x, *mine, *theirs, gain)
 
@@ -1016,13 +1039,13 @@
         + [shape_of((tok, feats), BF16)] * 4
         + [shape_of((1, width), F32)],
         compiler_params=settings(1, 32),
-        cost_estimate=cost(2 * tok * width * 4 * feats, 24 << 20),
+        cost_estimate=cost(True),
         name="norm_two_back",
     )(info, *[p for b in pieces for p in b], grad, resid, grad_result, gain)
 
 
 def norm_one_back_kernel(info, *refs):
-    p0, p1, x_ref, gres_ref, gain_ref, out_ref, gg_ref, w_ref, sem = refs[16:]
+    p0, p1, x_ref, gres_ref, gain_ref, outa_ref, outb_ref, gg_ref, w_ref, sem = refs[16:]
     load_blocks(refs[:16], w_ref, sem)
     quarter = x_ref.shape[1] // 4
     grad = dot(p0[0], w_ref[0], 1, 1)
@@ -1037,7 +1060,15 @@
     total = (gres_ref[...] + back).astype(BF16)
     for p, mask in enumerate(MASKS):
         at = pl.multiple_of(jnp.bitwise_xor(info[1], mask) * quarter, quarter)
-        out_ref[:, pl.ds(at, quarter)] = total[:, p * quarter : (p + 1) * quarter]
+        part = total[:, p * quarter : (p + 1) * quarter]
+
+        @pl.when(pl.program_id(0) < pl.num_programs(0) // 2)
+        def _():
+            outa_ref[:, pl.ds(at, quarter)] = part
+
+        @pl.when(pl.program_id(0) >= pl.num_programs(0) // 2)
+        def _():
+            outb_ref[:, pl.ds(at, quarter)] = part
 
     @pl.when(pl.program_id(0) == 0)
     def _():
@@ -1051,6 +1082,7 @@
     cols = pieces[0][0].shape[1]
     rows_of = lambda n: pl.BlockSpec((tile, n), lambda i, info: (i, 0))
     pair = pl.BlockSpec((2, tile, cols), lambda i, info: (0, i, 0))
+    half = tok // tile // 2
     row = pl.BlockSpec((1, width), lambda i, info: (0, 0))
     return pl.pallas_call(
         norm_one_back_kernel,
@@ -1058,12 +1090,16 @@
             num_scalar_prefetch=1,
             grid=(tok // tile,),
             in_specs=[ANY] * 16 + [pair, pair, rows_of(width), rows_of(width), row],
-            out_specs=[rows_of(width), row],
+            out_specs=[
+                pl.BlockSpec((tile, width), lambda i, info: (jnp.minimum(i, half - 1), 0)),
+                pl.BlockSpec((tile, width), lambda i, info: (jnp.maximum(i - half, 0), 0)),
+                row,
+            ],
             scratch_shapes=[pltpu.VMEM((4, width, cols), BF16), pltpu.SemaphoreType.DMA],
         ),
-        out_shape=[shape_of((tok, width), BF16), shape_of((1, width), F32)],
+        out_shape=[shape_of((tok // 2, width), BF16)] * 2 + [shape_of((1, width), F32)],
         compiler_params=settings(1, 32),
-        cost_estimate=cost(2 * tok * width * 4 * cols, 18 << 20),
+        cost_estimate=cost(True),
         name="norm_one_back",
     )(info, *[p for b in pieces for p in b], *pairs, x, grad_resid, gain)
 
@@ -1109,8 +1145,8 @@
         rest = rest[count:]
     act_ref, hid_ref = rest[:2]
     if last:
-        out_ref, gres_ref, low_ref, lowt_ref, sq_ref = rest[2:7]
-        gate_up, down, total, sems = rest[7:]
+        outa_ref, outb_ref, gres_ref, low_ref, lowt_ref, sq_ref = rest[2:8]
+        gate_up, down, total, sems = rest[8:]
     else:
         sum_ref, gate_up, down, total, sems = rest[2:]
     step, part = pl.program_id(0), pl.program_id(1)
@@ -1167,7 +1203,16 @@
             at = pl.multiple_of(jnp.bitwise_xor(info[1], mask) * quarter, quarter)
             cols = slice(p * quarter, (p + 1) * quarter)
             value = result[:, cols]
-            out_ref[:, pl.ds(at, quarter)] = value.astype(BF16)
+            low = value.astype(BF16)
+
+            @pl.when(part < pl.num_programs(1) // 2)
+            def _():
+                outa_ref[:, pl.ds(at, quarter)] = low
+
+            @pl.when(part >= pl.num_programs(1) // 2)
+            def _():
+                outb_ref[:, pl.ds(at, quarter)] = low
+
             error = valid * (value - teach_ref[0, :, pl.ds(at, quarter)].astype(F32))
             square = square + error * error
             grad = error * scale[0]
@@ -1202,15 +1247,22 @@
         in_specs.append(
             pl.BlockSpec((1, tile, width), lambda s, i, info: (info[0], leave(s, i), 0))
         )
+        half = tok // tile // 2
         out_specs += [
-            tiles(width),
+            pl.BlockSpec(
+                (tile, width), lambda s, i, info: (jnp.minimum(leave(s, i), half - 1), 0)
+            ),
+            pl.BlockSpec(
+                (tile, width), lambda s, i, info: (jnp.maximum(leave(s, i) - half, 0), 0)
+            ),
             tiles(width),
             tiles(width),
             pl.BlockSpec((width, tile), lambda s, i, info: (0, leave(s, i))),
             pl.BlockSpec((1, width // 4), lambda s, i, info: (0, 0)),
         ]
         out_shape += [
-            shape_of((tok, width), BF16),
+            shape_of((tok // 2, width), BF16),
+            shape_of((tok // 2, width), BF16),
             shape_of((tok, width), F32),
             shape_of((tok, width), BF16),
             shape_of((width, tok), BF16),
@@ -1235,7 +1287,7 @@
         ),
         out_shape=out_shape,
         compiler_params=settings(2, 50),
-        cost_estimate=cost(2 * tok * width * units * 3 * count, 20 << 20),
+        cost_estimate=cost(True),
         name="ffn_fwd",
     )(info, scale, x, total, *([teacher] if last else []), *pieces)
 
@@ -1337,7 +1389,7 @@
         ],
         input_output_aliases={} if first else {5 + len(pieces): 0},
         compiler_params=settings(1, 56),
-        cost_estimate=cost(2 * tok * width * units * 6, 32 << 20),
+        cost_estimate=cost(True),
         name="ffn_bwd",
     )(low, acts, hiddens, xt, lowt, *pieces, *([] if first else [total]))
 
@@ -1350,81 +1402,108 @@
     return jnp.concatenate([block[:, a : a + n] for a, n in starts], axis=1)
 
 
-def sum_kernel(side, turn, info, left_ref, right_ref, *outs):
-    right = right_ref[...]
-    if turn:
-        right = turn_chunks(right)
-    total = (left_ref[...].astype(F32) + right.astype(F32)).astype(BF16)
-    if len(outs) == 1:
-        outs[0][...] = total
-        return
-    first = side(pl.program_id(0), info) == 0
-
-    @pl.when(first)
-    def _():
-        outs[0][...] = total
-
-    @pl.when(jnp.logical_not(first))
-    def _():
-        outs[1][...] = total
-
-
-def summed(info, left, right, how, turn=False):
-    rows, cols = left.shape
-    count = rows // 128
-    block = lambda at: pl.BlockSpec((128, cols), at)
-    if how == "all":
-        side, places = None, [lambda i, info: (i, 0)]
-    elif how == "halves":
-        half = count // 2
-        side = lambda i, info: i // half
-        places = [
-            lambda i, info: (jnp.minimum(i, half - 1), 0),
-            lambda i, info: (jnp.maximum(i - half, 0), 0),
-        ]
-    else:
-        side = lambda i, info: jnp.bitwise_xor(i % 2, info[2])
-        places = [lambda i, info: (i // 2, 0)] * 2
-    shapes = [shape_of((rows // len(places), cols), BF16)] * len(places)
-    out = pl.pallas_call(
-        functools.partial(sum_kernel, side, turn),
+def sum_kernel(turns, *refs):
+    total = None
+    for ref, turn in zip(refs[:-1], turns):
+        value = ref[...].astype(F32)
+        value = turn_chunks(value) if turn else value
+        total = value if total is None else total + value
+    refs[-1][...] = total.astype(refs[-1].dtype)
+
+
+def summed(terms, turns=None, dtype=BF16):
+    rows, cols = terms[0].shape
+    spec = pl.BlockSpec((64, cols), lambda i: (i, 0))
+    return pl.pallas_call(
+        functools.partial(sum_kernel, turns or [False] * len(terms)),
+        grid=(rows // 64,),
+        in_specs=[spec] * len(terms),
+        out_specs=spec,
+        out_shape=shape_of((rows, cols), dtype),
+        compiler_params=settings(1, 24),
+        cost_estimate=cost(False),
+        name="summed",
+    )(*terms)
+
+
+def core_sum_kernel(info, left_ref, right_ref, *outs):
+    total = (left_ref[...].astype(F32) + right_ref[...].astype(F32)).astype(BF16)
+    block = pl.program_id(0) // 2
+    far, other = block // 2, jnp.bitwise_xor(block % 2, info[2])
+    for i, out in enumerate(outs):
+
+        @pl.when(far * 2 + other == i)
+        def _():
+            out[...] = total
+
+
+def core_sum(info, keep, came):
+    rows, cols = keep.shape
+    block = lambda at: pl.BlockSpec((64, cols), at)
+
+    def place(far, other):
+        def at(i, info):
+            return (jnp.clip(i - 4 * far - 2 * jnp.bitwise_xor(info[2], other), 0, 1), 0)
+
+        return block(at)
+
+    return pl.pallas_call(
+        core_sum_kernel,
         grid_spec=pltpu.PrefetchScalarGridSpec(
             num_scalar_prefetch=1,
-            grid=(count,),
+            grid=(rows // 64,),
             in_specs=[block(lambda i, info: (i, 0))] * 2,
-            out_specs=[block(at) for at in places],
+            out_specs=[place(0, 0), place(0, 1), place(1, 0), place(1, 1)],
         ),
-        out_shape=shapes,
+        out_shape=[shape_of((rows // 4, cols), BF16)] * 4,
         compiler_params=settings(1, 24),
-        cost_estimate=cost(0, 4 << 20),
-        name="summed",
-    )(info, left, right)
-    return out[0] if len(places) == 1 else out
+        cost_estimate=cost(False),
+        name="core_sum",
+    )(info, keep, came)
+
+
+def weight_grad_kernel(nt_ref, back_ref, gt_ref, att_ref, keep_ref, send_ref):
+    cols = back_ref.shape[2]
+
+    def rows(target):
+        target[:, :cols] = dot(nt_ref[...], back_ref[0], 1, 0).astype(BF16)
+        target[:, cols:] = dot(gt_ref[...], att_ref[0], 1, 0).astype(BF16)
+
+    @pl.when(pl.program_id(0) < 2)
+    def _():
+        rows(send_ref)
+
+    @pl.when(pl.program_id(0) >= 2)
+    def _():
+        rows(keep_ref)
+
+
+def weight_grad(normed_t, back, side, grad_t, attended, block):
+    width, tok = normed_t.shape
+    cols, feats = back.shape[2], attended.shape[2]
+    rows = pl.BlockSpec((width // 4, tok), lambda i: (jnp.bitwise_xor(i, 2), 0))
+    return pl.pallas_call(
+        weight_grad_kernel,
+        grid=(4,),
+        in_specs=[
+            rows,
+            pl.BlockSpec((1, tok, cols), lambda i: (side, 0, 0)),
+            rows,
+            pl.BlockSpec((1, tok, feats), lambda i: (block, 0, 0)),
+        ],
+        out_specs=[
+            pl.BlockSpec((width // 4, cols + feats), lambda i: (jnp.maximum(i - 2, 0), 0)),
+            pl.BlockSpec((width // 4, cols + feats), lambda i: (jnp.minimum(i, 1), 0)),
+        ],
+        out_shape=[shape_of((width // 2, cols + feats), BF16)] * 2,
+        compiler_params=settings(1, 24),
+        cost_estimate=cost(False),
+        name="weight_grad",
+    )(normed_t, back, grad_t, attended)
 
 
 def after(value, *others):
     return lax.optimization_barrier((value,) + others)[0]
-
-
-def z_gather(block):
-    one = lax.ppermute(block, "tp", Z_UP)
-    three = lax.ppermute(block, "tp", Z_DOWN)
-    two = lax.ppermute(one, "tp", Z_UP)
-    return [block, one, two, three]
-
-
-def add(left, right):
-    return left.astype(F32) + right.astype(F32)
-
-
-def add_low(left, right):
-    return add(left, right).astype(BF16)
-
-
-def z_reduce(parts):
-    two = add_low(parts[1], lax.ppermute(parts[2], "tp", Z_DOWN))
-    total = add(parts[0], lax.ppermute(two, "tp", Z_DOWN))
-    return total + lax.ppermute(parts[3], "tp", Z_UP).astype(F32)
 
 
 def per_device_rows(
@@ -1464,247 +1543,457 @@
     def y_swap(v):
         return lax.ppermute(v, "ctx", Y_SWAP)
 
+    def z_up(v):
+        return lax.ppermute(v, "tp", Z_UP)
+
+    def z_far(v):
+        return lax.ppermute(v, "tp", Z_FAR)
+
+    def z_down(v):
+        return lax.ppermute(v, "tp", Z_DOWN)
+
+    def chunks(block):
+        return [block[:, j * units : (j + 1) * units] for j in range(3)]
+
+    def natural(v):
+        v = jnp.concatenate([v[0:1], v[2:3], v[1:2], v[3:4]], axis=0)
+        v = jnp.where(fsdp % 2 == 0, v, jnp.concatenate([v[1:2], v[0:1], v[3:4], v[2:3]], axis=0))
+        return jnp.where(fsdp // 2 == 0, v, jnp.concatenate([v[2:4], v[0:2]], axis=0))
+
+    v = {}
+
+    def sync():
+        v.update(lax.optimization_barrier(dict(v)))
+
     length = lax.dynamic_slice_in_dim(lengths, z, 1, 0)
     info = jnp.concatenate([jnp.stack([z, fsdp, ctx]).astype(jnp.int32), length])
-
-    w_proj = jnp.concatenate([q_weight, k_weight, v_weight], axis=1)
+    w_proj = join(q_weight, k_weight, v_weight)
+    proj_blocks = [w_proj, z_up(w_proj), z_far(w_proj), z_down(w_proj)]
+    proj_far = [x_swap(w_proj)]
     w_out, w_ffn = pack(info, o_weight, gate_weight, up_weight, down_weight)
     count_here = jnp.sum(lengths).astype(F32)[None]
     vector = jnp.concatenate([attn_gain, ffn_gain, q_gain, k_gain]).astype(F32)
     vector = jnp.concatenate([vector, count_here, jnp.zeros((640 - 545,), F32)])[None]
     vector = jnp.concatenate([vector, x_swap(vector)], axis=0)
-    vector = jnp.concatenate([vector, core_swap(vector)], axis=0)
+    pos = (ctx * tok + jnp.arange(tok, dtype=jnp.int32)).astype(F32)
+    frequency = THETA ** (-(2.0 * jnp.arange(hd // 2, dtype=F32)) / hd)
+    angles = frequency[:, None] * pos[None, :]
+    v.update(
+        info=info,
+        proj_blocks=proj_blocks,
+        proj_far=proj_far,
+        w_out=w_out,
+        w_ffn=w_ffn,
+        vector=vector,
+        cos_part=jnp.cos(angles),
+        sin_part=jnp.sin(angles),
+    )
+    sync()
+    info = v["info"]
+
+    proj_far = v["proj_far"] + [x_swap(block) for block in v["proj_blocks"][1:]]
+    w_out = v["w_out"]
+    out_blocks = [w_out, z_up(w_out), z_far(w_out), z_down(w_out)]
+    own_cores = [core_swap(v["proj_blocks"][0]), core_swap(proj_far[0])]
+    vector = jnp.concatenate([v["vector"], core_swap(v["vector"])], axis=0)
     gain_one = vector[:, :quarter].reshape(1, width)
     gain_two = vector[:, quarter : 2 * quarter].reshape(1, width)
     total_count = jnp.sum(vector[:, 544])
-
-    def natural(v):
-        v = jnp.concatenate([v[0:1], v[2:3], v[1:2], v[3:4]], axis=0)
-        v = jnp.where(fsdp % 2 == 0, v, jnp.concatenate([v[1:2], v[0:1], v[3:4], v[2:3]], axis=0))
-        return jnp.where(fsdp // 2 == 0, v, jnp.concatenate([v[2:4], v[0:2]], axis=0))
-
     head_gains = natural(vector[:, 2 * quarter : 544])
-    gain_q = head_gains[:, : hd // 4].reshape(hd, 1)
-    gain_k = head_gains[:, hd // 4 :].reshape(hd, 1)
-
-    def z_direct(block):
-        return [
-            block,
-            lax.ppermute(block, "tp", Z_UP),
-            lax.ppermute(block, "tp", Z_FAR),
-            lax.ppermute(block, "tp", Z_DOWN),
-        ]
-
-    def plane_pieces(blocks):
-        pieces = []
-        for block in blocks:
-            far = x_swap(block)
-            pieces.append([block, far, core_swap(block), core_swap(far)])
-        return pieces
-
-    proj_blocks = z_direct(w_proj)
-    proj_pieces = plane_pieces(proj_blocks)
-    out_blocks = z_direct(after(w_out, *proj_blocks[1:]))
-    ffn_one = lax.ppermute(after(w_ffn, *proj_blocks[1:]), "tp", Z_UP)
-    in_block = lambda i: [(i, 0), (i, units), (i, 2 * units)]
-    in_pair = lambda i: [(i, 0), (i, units), (i + 1, 0)]
-    plan_whole = [in_block(0), in_pair(1), in_block(3), in_pair(4)]
-    plan_chunks = [[(3 * p + j, 0) for j in range(3)] for p in range(4)]
-
-    def ffn_pieces(block, far, last):
-        return plan_whole, [block, far, last, core_swap(block), core_swap(far), core_swap(last)]
-
     x_in, normed_one_t = norm_one(info, tokens, gain_one, 256)
-    pos = (ctx * tok + jnp.arange(tok, dtype=jnp.int32)).astype(F32)
-    frequency = THETA ** (-(2.0 * jnp.arange(hd // 2, dtype=F32)) / hd)
-    angles = frequency[:, None] * pos[None, :]
-    tables = (jnp.cos(angles), jnp.sin(angles), gain_q, gain_k)
+    v.update(
+        proj_far=proj_far,
+        out_blocks=out_blocks,
+        own_cores=own_cores,
+        gain_one=gain_one,
+        gain_two=gain_two,
+        gain_q=head_gains[:, : hd // 4].reshape(hd, 1),
+        gain_k=head_gains[:, hd // 4 :].reshape(hd, 1),
+        total_count=total_count,
+        x_in=x_in,
+        normed_one_t=normed_one_t,
+    )
+    sync()
+
+    ffn_one = z_up(v["w_ffn"])
+    ffn_far = x_swap(v["w_ffn"])
+    proj_pieces = []
+    for k, (block, far) in enumerate(zip(v["proj_blocks"], v["proj_far"])):
+        cores = v["own_cores"] if k == 0 else [core_swap(block), core_swap(far)]
+        proj_pieces.append([block, far] + cores)
+    tables = [v[name] for name in ("cos_part", "sin_part", "gain_q", "gain_k")]
 
     def make(block, *then):
-        return project(info, proj_pieces, after(normed_one_t, *then), *tables, heads, block)
-
-    far_of = lambda block: x_swap(block[:, : 2 * units])
-    near = lambda far: far[:, :units]
-    own_ffn = after(w_ffn, *[b[1] for b in proj_pieces])
-    far0 = far_of(own_ffn)
-    weights0 = ffn_pieces(own_ffn, far0, y_swap(near(far0)))
+        return project(info, proj_pieces, after(v["normed_one_t"], *then), *tables, heads, block)
 
     theirs = [make(lambda s: 2 * (1 - s[2]))]
+    got = [y_swap(theirs[0][0])]
     theirs.append(make(lambda s: 2 * (1 - s[2]) + 1, theirs[0][0]))
-    got = [y_swap(theirs[0][0]), y_swap(theirs[1][0])]
+    got.append(y_swap(theirs[1][0]))
     mine = [make(lambda s: 2 * s[2], theirs[1][0])]
     mine.append(make(lambda s: 2 * s[2] + 1, mine[0][0]))
-    out_far = [x_swap(after(block, mine[1][0])) for block in out_blocks]
-
-    ffn_one = after(ffn_one, mine[1][0])
-    far1 = far_of(ffn_one)
-    ffn_three = lax.ppermute(after(w_ffn, ffn_one, mine[1][0]), "tp", Z_DOWN)
-    first = attn_fwd(info, after(mine[0][0], mine[1][0], far0), got[0], hd)
-    second = attn_fwd(info, after(mine[1][0], first[1]), got[1], hd)
-    out_pieces = []
-    for block, far in zip(out_blocks, out_far):
-        block, far = after(block, second[1]), after(far, second[1])
-        out_pieces.append([block, far, core_swap(block), core_swap(far)])
-    outs = [first, second]
-    arrived = [y_swap(first[1]), y_swap(second[1])]
-    ffn_three = after(ffn_three, second[1])
-    far3 = far_of(ffn_three)
-    ffn_one, far1 = after(ffn_one, second[1]), after(far1, second[1])
-    ffn_two = [
-        lax.ppermute(after(ffn_one[:, j * units : (j + 1) * units], ffn_three), "tp", Z_UP)
-        for j in range(3)
+    v.update(
+        ffn_one=ffn_one,
+        ffn_far=ffn_far,
+        proj_pieces=proj_pieces,
+        mine=mine,
+        theirs=theirs,
+        got0=got[0],
+    )
+    sync()
+
+    one_far = [x_swap(chunks(v["ffn_one"])[0])]
+    three = [z_down(chunks(v["w_ffn"])[0])]
+    first = attn_fwd(info, v["mine"][0][0], v["got0"], hd)
+    v.update(first=first, got1=got[1], one_far=one_far, three=three)
+    sync()
+
+    arrived = [y_swap(v["first"][1])]
+    three = v["three"] + [z_down(chunks(v["w_ffn"])[1])]
+    out_far = [x_swap(block) for block in v["out_blocks"]]
+    own_cores = [core_swap(v["w_ffn"]), core_swap(v["ffn_far"])]
+    second = attn_fwd(info, v["mine"][1][0], v["got1"], hd)
+    v.update(
+        second=second, arrived=arrived, three=three, out_far=out_far, own_cores=own_cores
+    )
+    sync()
+
+    arrived = v["arrived"] + [y_swap(v["second"][1])]
+    three = v["three"] + [z_down(chunks(v["w_ffn"])[2])]
+    one_far = v["one_far"] + [x_swap(chunks(v["ffn_one"])[1])]
+    one_cores = [core_swap(v["ffn_one"]), core_swap(one_far[0])]
+    out_pieces = [
+        [block, far, core_swap(block), core_swap(far)]
+        for block, far in zip(v["out_blocks"], v["out_far"])
     ]
-    last1 = y_swap(after(near(far1), arrived[1]))
+    v.update(
+        arrived=arrived, three=three, one_far=one_far, one_cores=one_cores, out_pieces=out_pieces
+    )
+    sync()
+
+    two = [z_up(chunks(v["ffn_one"])[0])]
+    three_far = [x_swap(v["three"][0])]
+    one_last = y_swap(v["one_far"][0])
+    one_cores = v["one_cores"] + [core_swap(v["one_far"][1])]
+    three_cores = [core_swap(v["three"][0]), core_swap(v["three"][1])]
     resid, normed_two, normed_two_t, attended = out_proj(
-        info, x_in, [first[0], second[0]], arrived, out_pieces, gain_two, 256
-    )
-
-    scale = (slots / total_count)[None]
-    weights1 = ffn_pieces(ffn_one, far1, after(last1, normed_two))
-    two_first, two_middle = after(ffn_two[0], normed_two), after(ffn_two[1], normed_two)
-    two_far = [x_swap(two_first), x_swap(two_middle)]
-    far3 = after(far3, normed_two)
-    last3 = y_swap(near(far3))
+        info,
+        v["x_in"],
+        [v["first"][0], v["second"][0]],
+        v["arrived"],
+        v["out_pieces"],
+        v["gain_two"],
+        256,
+    )
+    v.update(
+        two=two,
+        three_far=three_far,
+        one_last=one_last,
+        one_cores=one_cores,
+        three_cores=three_cores,
+        resid=resid,
+        normed_two=normed_two,
+        normed_two_t=normed_two_t,
+        attended=attended,
+    )
+    sync()
+
+    in_block = lambda i: [(i, 0), (i, units), (i, 2 * units)]
+    in_row = lambda i: [(i, 0), (i + 1, 0), (i + 2, 0)]
+    plan0 = [in_block(i) for i in range(4)]
+    plan1 = [in_block(0), in_row(1), in_block(4), in_row(5)]
+    plan3 = [in_row(3 * i) for i in range(4)]
+    scale = (slots / v["total_count"])[None]
+    weights0 = [v["w_ffn"], v["ffn_far"]] + v["own_cores"]
+    weights1 = [v["ffn_one"]] + v["one_far"] + [v["one_last"]]
+    weights1 += v["one_cores"] + [core_swap(v["one_last"])]
+    two = v["two"] + [z_up(part) for part in chunks(v["ffn_one"])[1:]]
+    three_far = v["three_far"] + [x_swap(v["three"][1])]
+    two_far = [x_swap(v["two"][0])]
+    three_last = y_swap(v["three_far"][0])
+    three_cores = v["three_cores"] + [core_swap(v["three"][2]), core_swap(v["three_far"][0])]
+    two_cores = [core_swap(v["two"][0])]
     acts_a, hiddens_a, sum_a = ffn_fwd(
-        info, scale, normed_two, resid, None, [weights0, weights1], units, 256
-    )
-    weights3 = ffn_pieces(ffn_three, far3, after(last3, sum_a))
-    two_far = [after(two_far[0], sum_a), after(two_far[1], sum_a)]
-    two_far.append(y_swap(two_far[0]))
+        info,
+        scale,
+        v["normed_two"],
+        v["resid"],
+        None,
+        [(plan0, weights0), (plan1, weights1)],
+        units,
+        256,
+    )
+    v.update(
+        scale=scale,
+        weights0=weights0,
+        weights1=weights1,
+        two=two,
+        three_far=three_far,
+        two_far=two_far,
+        three_last=three_last,
+        three_cores=three_cores,
+        two_cores=two_cores,
+        acts_a=acts_a,
+        hiddens_a=hiddens_a,
+        sum_a=sum_a,
+    )
+    sync()
+
+    weights3 = v["three"] + v["three_far"] + [v["three_last"]] + v["three_cores"]
+    weights3 += [core_swap(v["three_far"][1]), core_swap(v["three_last"])]
+    two_far = v["two_far"] + [x_swap(v["two"][1])]
+    two_last = y_swap(v["two_far"][0])
+    two_cores = v["two_cores"] + [core_swap(p) for p in v["two"][1:] + v["two_far"]]
     acts_b, hiddens_b, sum_b = ffn_fwd(
-        info, scale, normed_two, sum_a, None, [weights3], units, 256
-    )
-    two = [two_first, two_middle, after(ffn_two[2], sum_a)] + two_far[:2] + [after(two_far[2], sum_b)]
-    weights2 = (plan_chunks, two + [core_swap(p) for p in two])
-    acts_c, hiddens_c, result_low, grad_result, grad_low, grad_low_t, square = ffn_fwd(
-        info, scale, normed_two, sum_b, teacher, [weights2], units, 256
-    )
-
-    def spread(parts, dtype):
+        info, v["scale"], v["normed_two"], v["sum_a"], None, [(plan3, weights3)], units, 256
+    )
+    v.update(
+        weights3=weights3,
+        two_far=two_far,
+        two_last=two_last,
+        two_cores=two_cores,
+        acts_b=acts_b,
+        hiddens_b=hiddens_b,
+        sum_b=sum_b,
+    )
+    sync()
+
+    weights2 = v["two"] + v["two_far"] + [v["two_last"]] + v["two_cores"]
+    weights2 += [core_swap(v["two_far"][1]), core_swap(v["two_last"])]
+    acts_c, hiddens_c, *results, grad_result, grad_low, grad_low_t, square = ffn_fwd(
+        info, v["scale"], v["normed_two"], v["sum_b"], teacher, [(plan3, weights2)], units, 256
+    )
+    v.update(
+        weights2=weights2,
+        acts_c=acts_c,
+        hiddens_c=hiddens_c,
+        results=results,
+        grad_result=grad_result,
+        grad_low=grad_low,
+        grad_low_t=grad_low_t,
+        square=square,
+    )
+    sync()
+
+    def ffn_back(plan, weights, acts, hiddens, block, total):
+        return ffn_bwd(
+            v["grad_low"],
+            (v[acts], v[hiddens], block),
+            (plan, v[weights]),
+            total,
+            v["normed_two_t"],
+            v["grad_low_t"],
+            256,
+        )
+
+    turned = [False, False, True]
+    one = [z_up(v["results"][0])]
+    total, keep2, send2 = ffn_back(plan3, "weights2", "acts_c", "hiddens_c", 0, None)
+    v.update(one=one, total=total, keep2=keep2, send2=send2)
+    sync()
+
+    one = v["one"] + [z_up(v["results"][1])]
+    came2 = core_swap(v["send2"])
+    total, keep1, send1 = ffn_back(plan1, "weights1", "acts_a", "hiddens_a", 1, v["total"])
+    v.update(one=one, came2=came2, total=total, keep1=keep1, send1=send1)
+    sync()
+
+    out_three = [z_down(v["results"][0])]
+    came1 = core_swap(v["send1"])
+    sum2 = core_sum(info, v["keep2"], v["came2"])
+    far_t2 = x_swap(sum2[3])
+    total, keep3, send3 = ffn_back(
+        plan3, "weights3", "acts_b", "hiddens_b", 0, after(v["total"], sum2[0])
+    )
+    v.update(
+        out_three=out_three,
+        came1=came1,
+        sum2=sum2,
+        far_t2=far_t2,
+        total=total,
+        keep3=keep3,
+        send3=send3,
+    )
+    sync()
+
+    out_three = v["out_three"] + [z_down(v["results"][1])]
+    came3 = core_swap(v["send3"])
+    far_h2 = x_swap(v["sum2"][2])
+    there2 = y_swap(summed([v["sum2"][1], v["far_t2"]]))
+    sum1 = core_sum(info, v["keep1"], v["came1"])
+    total, keep0, send0 = ffn_back(
+        plan0, "weights0", "acts_a", "hiddens_a", 0, after(v["total"], sum1[0])
+    )
+    v.update(
+        out_three=out_three,
+        came3=came3,
+        far_h2=far_h2,
+        there2=there2,
+        sum1=sum1,
+        total=total,
+        keep0=keep0,
+        send0=send0,
+    )
+    sync()
+
+    came0 = core_swap(v["send0"])
+    far_t1 = x_swap(v["sum1"][3])
+    down2 = z_down(summed([v["sum2"][0], v["far_h2"], v["there2"]], turned))
+    sum3 = core_sum(info, v["keep3"], v["came3"])
+    grad_resid, grad_attn_t, a0, a1, b0, b1, gain_two_sum = norm_two_back(
+        info,
+        after(v["total"], sum3[0]),
+        v["resid"],
+        v["grad_result"],
+        v["gain_two"],
+        v["out_pieces"],
+        256,
+    )
+    grad_got = [y_swap(b0), y_swap(b1)]
+    v.update(
+        came0=came0,
+        far_t1=far_t1,
+        down2=down2,
+        sum3=sum3,
+        grad_resid=grad_resid,
+        grad_attn_t=grad_attn_t,
+        grad_mine=[a0, a1],
+        gain_two_sum=gain_two_sum,
+        grad_got0=grad_got[0],
+    )
+    sync()
+
+    def attn_back(j, grad):
+        out, got_ref = v["first" if j == 0 else "second"], v[f"got{j}"]
+        return attn_bwd(
+            info, v["mine"][j][0], got_ref, out[0], out[1], grad, v[f"grad_got{j}"], out[2], hd
+        )
+
+    two = [z_up(v["one"][0])]
+    far_h1 = x_swap(v["sum1"][2])
+    there1 = y_swap(summed([v["sum1"][1], v["far_t1"]]))
+    far_t3 = x_swap(v["sum3"][3])
+    sum0 = core_sum(info, v["keep0"], v["came0"])
+    back0 = attn_back(0, after(v["grad_mine"][0], sum0[0], there1))
+    v.update(
+        out_two=two,
+        far_h1=far_h1,
+        there1=there1,
+        far_t3=far_t3,
+        sum0=sum0,
+        back0=back0,
+        grad_got1=grad_got[1],
+    )
+    sync()
+
+    two = v["out_two"] + [z_up(v["one"][1])]
+    heads0 = y_swap(v["back0"][1])
+    far_h3 = x_swap(v["sum3"][2])
+    far_t0 = x_swap(v["sum0"][3])
+    there3 = summed([v["sum3"][1], v["far_t3"]])
+    two_down = summed(
+        [v["sum1"][0], v["far_h1"], v["there1"], v["down2"]], [False, False, True, False]
+    )
+    there3_got = y_swap(there3)
+    two_down_got = z_down(two_down)
+    back1 = attn_back(1, after(v["grad_mine"][1], there3, two_down))
+    v.update(
+        out_two=two, heads0=heads0, far_h3=far_h3, far_t0=far_t0, there3=there3_got, back1=back1
+    )
+    sync()
+
+    heads1 = y_swap(v["back1"][1])
+    far_h0 = x_swap(v["sum0"][2])
+    up3 = z_up(summed([v["sum3"][0], v["far_h3"], v["there3"]], turned))
+    tables = [v[name] for name in ("cos_part", "sin_part", "gain_q", "gain_k")]
+    head0 = head_back(
+        info, v["back0"][0], v["heads0"], v["mine"][0][1], v["theirs"][0][1], *tables, heads
+    )
+    v.update(heads1=heads1, two_down=two_down_got, head0=head0)
+    sync()
+
+    there0 = y_swap(summed([v["sum0"][1], v["far_t0"]]))
+    head1 = head_back(
+        info, v["back1"][0], v["heads1"], v["mine"][1][1], v["theirs"][1][1], *tables, heads
+    )
+    *tokens_low, gain_one_sum = norm_one_back(
+        info,
+        [v["head0"][0], head1[0]],
+        v["proj_pieces"],
+        v["x_in"],
+        v["grad_resid"],
+        v["gain_one"],
+        256,
+    )
+    v.update(head1=head1, tokens_low=tokens_low, gain_one_sum=gain_one_sum, up3=up3)
+    sync()
+
+    tok_one = [z_up(v["tokens_low"][0])]
+    tok_three = [z_down(v["tokens_low"][0])]
+    grads = []
+    for k in range(4):
+        grads.append(
+            weight_grad(
+                after(v["normed_one_t"], *(grads[-1] if grads else ())),
+                v[f"head{k % 2}"][0],
+                k // 2,
+                v["grad_attn_t"],
+                v["attended"],
+                k,
+            )
+        )
+    came = [core_swap(send) for _, send in grads]
+    v.update(tok_one=tok_one, keeps=[keep for keep, _ in grads], came=came, there0=there0)
+    v.update(far_h0=far_h0)
+    sync()
+
+    tok_one = v["tok_one"] + [z_up(v["tokens_low"][1])]
+    sums = []
+    for keep, other in zip(v["keeps"], v["came"]):
+        sums.append(core_sum(info, after(keep, *(sums[-1] if sums else ())), other))
+    far_t = [x_swap(s[3]) for s in sums]
+    far_h = [x_swap(s[2]) for s in sums]
+    part0 = summed([v["sum0"][0], v["far_h0"], v["there0"]], turned)
+    ffn_sum = summed([part0, v["two_down"], v["up3"]], None, F32)
+    v.update(tok_three=tok_three, sums=sums, far_t=far_t, ffn_sum=ffn_sum)
+    sync()
+
+    tok_three = v["tok_three"] + [z_down(v["tokens_low"][1])]
+    there = [y_swap(summed([s[1], far])) for s, far in zip(v["sums"], v["far_t"])]
+    v.update(tok_one=tok_one, there=there, far_h=far_h)
+    sync()
+
+    parts = [summed([s[0], far, t]) for s, far, t in zip(v["sums"], v["far_h"], v["there"])]
+    parts = [parts[0], z_down(parts[1]), z_far(parts[2]), z_up(parts[3])]
+    ffn_other = y_swap(v["ffn_sum"])
+    tok_two = [z_up(v["tok_one"][0])]
+    v.update(parts=parts, tok_three=tok_three, ffn_other=ffn_other)
+    sync()
+
+    attn_sum = summed(v["parts"], None, F32)
+    attn_other = y_swap(attn_sum)
+    tok_two.append(z_up(v["tok_one"][1]))
+
+    def spread(own, one, two, three, dtype):
         out = jnp.zeros((rows_dev, tok, width), dtype)
-        for k in (0, 1, 3, 2):
-            part = parts[k].astype(dtype)[None]
-            out = lax.dynamic_update_slice(out, part, (lax.rem(z - k + 4, 4), 0, 0))
+        for k, parts in ((0, own), (1, one), (3, three), (2, two)):
+            row = lax.rem(z - k + 4, 4)
+            for j, part in enumerate(parts):
+                out = lax.dynamic_update_slice(
+                    out, part.astype(dtype)[None], (row, j * tok // 2, 0)
+                )
         return out
 
-    def ffn_back(weights, saved, total):
-        return ffn_bwd(
-            grad_low, saved, weights, total, normed_two_t, grad_low_t, 256
-        )
-
-    output_one = lax.ppermute(result_low, "tp", Z_UP)
-    total, keep2, send2 = ffn_back(weights2, (acts_c, hiddens_c, 0), None)
-    came2 = core_swap(send2)
-    total, keep1, send1 = ffn_back(weights1, (acts_a, hiddens_a, 1), after(total, send2))
-    came1 = core_swap(send1)
-    own2, far2 = summed(info, after(keep2, send1), came2, "halves")
-    came2 = x_swap(far2)
-    output_one = after(output_one, own2)
-    output_three = lax.ppermute(after(result_low, output_one), "tp", Z_DOWN)
-    total, keep3, send3 = ffn_back(weights3, (acts_b, hiddens_b, 0), after(total, own2, output_one))
-    came3 = core_swap(send3)
-    here1, there1 = summed(info, after(keep1, send3), came1, "ctx")
-    came1 = y_swap(there1)
-    total, keep0, send0 = ffn_back(weights0, (acts_a, hiddens_a, 0), after(total, here1))
-    came0 = core_swap(send0)
-    own3, far3 = summed(info, after(keep3, send0), came3, "halves")
-    came3 = x_swap(far3)
-    here2, there2 = summed(info, after(own2, own3), came2, "ctx")
-    output_three = after(output_three, here2)
-    output_two = lax.ppermute(after(output_one, output_three), "tp", Z_UP)
-    grad_resid, grad_attn_t, a0, a1, b0, b1, gain_two_sum = norm_two_back(
-        info, after(total, here2, output_three), resid, grad_result, gain_two, out_pieces, 256
-    )
-
-    grad_got = [y_swap(b0), y_swap(b1)]
-    own0, far0 = summed(info, after(keep0, b0), came0, "halves")
-    own1, far1 = summed(info, after(here1, own0), came1, "halves", True)
-    came1 = x_swap(far1)
-    came2 = y_swap(after(there2, grad_got[0]))
-
-    def attn_back(j, grad):
-        return attn_bwd(
-            info, mine[j][0], got[j], outs[j][0], outs[j][1], grad, grad_got[j], outs[j][2], hd
-        )
-
-    first_back = attn_back(0, after(a0, own1))
-    grad_heads = [y_swap(first_back[1])]
-    part2 = summed(info, after(here2, first_back[1]), came2, "all", True)
-    part1 = summed(info, after(own1, part2), came1, "all")
-    here3, there3 = summed(info, after(own3, part1), came3, "ctx")
-    came0 = x_swap(after(far0, here3))
-    output_two = after(output_two, here3)
-    came2 = lax.ppermute(after(part2, output_two), "tp", Z_DOWN)
-    came3 = y_swap(after(there3, first_back[1]))
-    second_back = attn_back(1, after(a1, here3, output_two))
-    grad_heads.append(y_swap(second_back[1]))
-    two_down = summed(info, after(part1, second_back[1]), came2, "all")
-    came2 = lax.ppermute(two_down, "tp", Z_DOWN)
-    back = [
-        head_back(
-            info,
-            after(first_back[0], two_down),
-            grad_heads[0],
-            mine[0][1],
-            theirs[0][1],
-            *tables,
-            heads,
-        )
-    ]
-    part3 = summed(info, after(here3, back[0][0]), came3, "all", True)
-    came3 = lax.ppermute(part3, "tp", Z_UP)
-    back.append(
-        head_back(
-            info,
-            after(second_back[0], part3),
-            grad_heads[1],
-            mine[1][1],
-            theirs[1][1],
-            *tables,
-            heads,
-        )
-    )
-    tokens_low, gain_one_sum = norm_one_back(
-        info, [back[0][0], back[1][0]], proj_pieces, x_in, grad_resid, gain_one, 256
-    )
-    tokens_grad = spread(z_gather(tokens_low), F32)
-    output_parts = [result_low, output_one, output_two, output_three]
-    output = spread([after(part, tokens_low) for part in output_parts], BF16)
-
-    def halves(v):
-        half = v.shape[0] // 2
-        return (
-            lax.dynamic_slice_in_dim(v, ctx * half, half, 0),
-            lax.dynamic_slice_in_dim(v, half - ctx * half, half, 0),
-        )
-
-    attn_parts = []
-    for k in range(4):
-        part = jnp.concatenate(
-            [
-                dot(normed_one_t, back[k % 2][0][k // 2], 1, 0).astype(BF16),
-                dot(grad_attn_t, attended[k], 1, 0).astype(BF16),
-            ],
-            axis=1,
-        )
-        came = core_swap(part[width // 2 :])
-        own = add_low(part[:quarter], came[:quarter])
-        far = add_low(part[quarter : width // 2], came[quarter:])
-        here, there = halves(add_low(own, x_swap(far)))
-        attn_parts.append(add_low(here, y_swap(there)))
-
-    here0, there0 = summed(info, after(own0, tokens_low), came0, "ctx")
-    part0 = summed(info, here0, y_swap(there0), "all", True)
-
-    def finish(own, turn):
-        other = turn(y_swap(own))
+    tokens_grad = spread(v["tokens_low"], v["tok_one"], tok_two, v["tok_three"], F32)
+    output = spread(v["results"], v["one"], v["out_two"], v["out_three"], BF16)
+
+    def finish(own, other):
         return jnp.concatenate(
             [jnp.where(ctx == 0, own, other), jnp.where(ctx == 0, other, own)], axis=0
         )
 
-    ffn_sum = add(part0, came2) + came3.astype(F32)
-    ffn_grad = finish(ffn_sum, turn_chunks)
-    attn_grad = finish(z_reduce(attn_parts), lambda v: v)
+    ffn_grad = finish(v["ffn_sum"], turn_chunks(v["ffn_other"]))
+    attn_grad = finish(attn_sum, attn_other)
 
     def total(v):
         for axis, pairs in (("fsdp", CORE_SWAP), ("fsdp", X_SWAP), ("ctx", Y_SWAP)):
@@ -1713,6 +2002,9 @@
             v = v + lax.ppermute(v, "tp", pairs)
         return v
 
+    back = [v["head0"], v["head1"]]
+    gain_one_sum, gain_two_sum, square = v["gain_one_sum"], v["gain_two_sum"], v["square"]
+    total_count = v["total_count"]
     gain_heads = back[0][1] + back[1][1]
     sums = total(
         jnp.concatenate(

time: 1000 us -> 943 us (0.943)
  waiting for transfers between devices: 336 us -> 232 us
  starting transfers between devices: 88.9 us -> 143 us
  Pallas kernels: 429 us -> 464 us
  matrix products: 18.2 us -> 0 us
  other arithmetic: 45.6 us -> 30.2 us
    pallas_call x13 -> x31, Pallas kernels: 61.7 us -> 131 us  [the longest x8 59.9 us: core_sum(): pl.pallas_call(core_sum_kernel, grid_spec=pltpu.PrefetchScalarGridSpec(nu...]
    ppermute x22 -> x32, waiting for transfers between devices: 92.1 us -> 29.5 us  [x_swap(): return lax.ppermute(v, 'fsdp', X_SWAP)]
    ppermute x23 -> x31, starting transfers between devices: 36.4 us -> 78.9 us  [the longest x16 36.4 us: z_up(): return lax.ppermute(v, 'tp', Z_UP)]
    ppermute x22 -> x21, waiting for transfers between devices: 95.7 us -> 70.4 us  [y_swap(): return lax.ppermute(v, 'ctx', Y_SWAP)]
    pallas_call x2, Pallas kernels: 76.6 us -> 53.5 us  [attn_bwd(): pl.pallas_call(functools.partial(attn_bwd_kernel, width, hd), grid_spec=p...]
    dot_general x8 -> x0, matrix products: 18.2 us -> none  [dot(): lax.dot_general(left, right, (((left_dim,), (right_dim,)), ((), ())), pre...]
    ppermute x23 -> x31, waiting for transfers between devices: 135 us -> 121 us  [the longest x16 70.9 us: z_up(): return lax.ppermute(v, 'tp', Z_UP)]
    pallas_call x4, Pallas kernels: 116 us -> 103 us  [ffn_bwd(): pl.pallas_call(functools.partial(ffn_bwd_kernel, steps, plan, first), gri...]
  transfers between devices with their start and end apart: 112 -> 132, of which waited for: 33 -> 43; matrix products, arithmetic and copies ran while one was open for 12% -> 8% of each run, Pallas kernels for 39% -> 44%
where the time goes in v6:
time: 943 us; the launch traced here: 935 us
  Pallas kernels  464 us (49%)
  waiting for transfers between devices  232 us (25%)
  starting transfers between devices  143 us (15%)
  local copies, waits for them, and re-layouts  58.6 us (6%)
  other arithmetic  30.2 us (3%)
    pallas_call x4, Pallas kernels, ffn_bwd(): pl.pallas_call(functools.partial(ffn_bwd_kernel, steps, plan, first), gri...  103 us
    ppermute x16, waiting for transfers between devices, z_up(): return lax.ppermute(v, 'tp', Z_UP)  70.9 us
    ppermute x21, waiting for transfers between devices, y_swap(): return lax.ppermute(v, 'ctx', Y_SWAP)  70.4 us
    pallas_call x3, Pallas kernels, ffn_fwd(): pl.pallas_call(functools.partial(ffn_fwd_kernel, tile, [plan for plan, _...  60.5 us
    pallas_call x8, Pallas kernels, core_sum(): pl.pallas_call(core_sum_kernel, grid_spec=pltpu.PrefetchScalarGridSpec(nu...  59.9 us
    pallas_call x2, Pallas kernels, attn_bwd(): pl.pallas_call(functools.partial(attn_bwd_kernel, width, hd), grid_spec=p...  53.5 us
    ppermute x3, waiting for transfers between devices, z_far(): return lax.ppermute(v, 'tp', Z_FAR)  43 us
    pallas_call x18, Pallas kernels, summed(): pl.pallas_call(functools.partial(sum_kernel, turns or [False] * len(terms...  39 us
  transfers between devices with their start and end apart: 132, of which 43 were waited for; matrix products, arithmetic and copies ran while one was open for 8% of the time, Pallas kernels for 44%

profile of v6, /device:TPU:0, one launch (start us, length us, event | category | flops | bytes accessed | tf_op | source)
XLA Modules:
  0.0 934.8 jit_solution(18391923234538832785)
XLA Ops:
  109.8 17.0 %attn_fwd.2 = (bf16[1024,256]{1,0:T(8,128)(2,1)}, bf16[1024,256]{1,0:T(8,128)(2,1)}, f32[2,2,2048]{2,1,0:T(2,128)}) custom-call(s32[4]{0:T(128)} %pad_add_fusion.info, bf16[512,1024]{1,0:T(8,128)(2,1)} %get-tuple-element.2731.mine_ref, bf16[512,1024]{1,0:T(8,128)(2,1)} %copy-done.58), custom_call_target="tpu_custom_call" | custom-call | flops 4398046511104 | bytes 1073741824 | tf_op jit(solution)/shard_map/attn_fwd/pallas_call | solution.py:753
  138.4 17.0 %attn_fwd.3 = (bf16[1024,256]{1,0:T(8,128)(2,1)}, bf16[1024,256]{1,0:T(8,128)(2,1)}, f32[2,2,2048]{2,1,0:T(2,128)}) custom-call(s32[4]{0:T(128)} %pad_add_fusion.info, bf16[512,1024]{1,0:T(8,128)(2,1)} %get-tuple-element.2804.mine_ref, bf16[512,1024]{1,0:T(8,128)(2,1)} %collective-permute-done.23.got_ref), custom_call_target="tpu_custom_call" | custom-call | flops 4398046511104 | bytes 1073741824 | tf_op jit(solution)/shard_map/attn_fwd/pallas_call | solution.py:753
  166.5 13.1 %collective-permute-done.34.refs_20_ = bf16[1024,256]{1,0:T(8,128)(2,1)S(1)} collective-permute-done((bf16[1024,256]{1,0:T(8,128)(2,1)}, bf16[1024,256]{1,0:T(8,128)(2,1)S(1)}, u32[]{:S(2)}, u32[]{:S(2)}) %collective-permute-start.34) | collective-permute-done | bytes 524320 | tf_op jit(solution)/shard_map/ppermute | solution.py:1544
  184.3 14.1 %collective-permute-done.52.rest_1_.rest_0_ = bf16[256,1152]{1,0:T(8,128)(2,1)} collective-permute-done((bf16[256,1152]{1,0:T(8,128)(2,1)S(1)}, bf16[256,1152]{1,0:T(8,128)(2,1)}, u32[]{:S(2)}, u32[]{:S(2)}) %collective-permute-start.52) | collective-permute-done | bytes 589856 | tf_op jit(solution)/shard_map/ppermute | solution.py:1547
  198.5 10.6 %out_proj.1 = (f32[1024,1024]{1,0:T(8,128)}, bf16[1024,1024]{1,0:T(8,128)(2,1)}, bf16[1024,1024]{1,0:T(8,128)(2,1)}, bf16[4,1024,256]{2,1,0:T(8,128)(2,1)}) custom-call(s32[4]{0:T(128)} %pad_add_fusion.info, bf16[256,256]{1,0:T(8,128)(2,1)} %get-tuple-element.2657.refs_0_, bf16[256,256]{1,0:T(8,128)(2,1)} %copy-done.79, bf16[256,256]{1,0:T(8,128)(2,1)} %copy-done.85, ...), custom_call_target="tpu_custom_call" | custom-call | flops 4398046511104 | bytes 1073741824 | tf_op jit(solution)/shard_map/out_proj/pallas_call | solution.py:970
  213.0 14.9 %collective-permute-done.58.rest_2_.rest_1_ = bf16[256,1152]{1,0:T(8,128)(2,1)S(1)} collective-permute-done((bf16[256,1152]{1,0:T(8,128)(2,1)S(1)}, bf16[256,1152]{1,0:T(8,128)(2,1)S(1)}, u32[]{:S(2)}, u32[]{:S(2)}) %collective-permute-start.58) | collective-permute-done | bytes 589856 | tf_op jit(solution)/shard_map/ppermute | solution.py:1547
  227.8 11.8 %collective-permute-done.59.rest_3_.rest_2_ = bf16[256,1152]{1,0:T(8,128)(2,1)} collective-permute-done((bf16[256,1152]{1,0:T(8,128)(2,1)S(1)}, bf16[256,1152]{1,0:T(8,128)(2,1)}, u32[]{:S(2)}, u32[]{:S(2)}) %collective-permute-start.59) | collective-permute-done | bytes 589856 | tf_op jit(solution)/shard_map/ppermute | solution.py:1547
  241.7 25.6 %ffn_fwd.3 = (bf16[2,1024,2304]{2,1,0:T(8,128)(2,1)}, bf16[2,1024,1152]{2,1,0:T(8,128)(2,1)}, f32[1024,1024]{1,0:T(8,128)}) custom-call(s32[4]{0:T(128)} %pad_add_fusion.info, f32[1]{0:T(128)} %bitcast.4.scale, bf16[1024,1024]{1,0:T(8,128)(2,1)} %get-tuple-element.2141.x_ref, f32[1024,1024]{1,0:T(8,128)} %get-tuple-element.2677.in_ref.refs_17_, ...), custom_call_target="tpu_custom_call" | custom-call | flops 4398046511104 | bytes 1073741824 | tf_op jit(solution)/shard_map/ffn_fwd/pallas_call | solution.py:1274
  272.2 15.6 %ffn_fwd.4 = (bf16[1,1024,2304]{2,1,0:T(8,128)(2,1)}, bf16[1,1024,1152]{2,1,0:T(8,128)(2,1)}, f32[1024,1024]{1,0:T(8,128)}) custom-call(s32[4]{0:T(128)} %pad_add_fusion.info, f32[1]{0:T(128)} %bitcast.4.scale, bf16[1024,1024]{1,0:T(8,128)(2,1)} %get-tuple-element.2141.x_ref, f32[1024,1024]{1,0:T(8,128)} %get-tuple-element.2014.in_ref, ...), custom_call_target="tpu_custom_call" | custom-call | flops 4398046511104 | bytes 1073741824 | tf_op jit(solution)/shard_map/ffn_fwd/pallas_call | solution.py:1274
  291.8 19.4 %ffn_fwd.5 = (bf16[1,1024,2304]{2,1,0:T(8,128)(2,1)}, bf16[1,1024,1152]{2,1,0:T(8,128)(2,1)}, bf16[512,1024]{1,0:T(8,128)(2,1)}, bf16[512,1024]{1,0:T(8,128)(2,1...) custom-call(s32[4]{0:T(128)} %pad_add_fusion.info, ...), custom_call_target="tpu_custom_call" | custom-call | flops 4398046511104 | bytes 1073741824 | tf_op jit(solution)/shard_map/ffn_fwd/pallas_call | solution.py:1274
  311.5 25.5 %ffn_bwd.4 = (f32[1024,1024]{1,0:T(8,128)}, bf16[512,3456]{1,0:T(8,128)(2,1)}, bf16[512,3456]{1,0:T(8,128)(2,1)}) custom-call(bf16[1024,1024]{1,0:T(8,128)(2,1)} %get-tuple-element.2568.low_ref, bf16[1,1024,2304]{2,1,0:T(8,128)(2,1)} %get-tuple-element.2247.act_ref, bf16[1,1024,1152]{2,1,0:T(8,128)(2,1)} %get-tuple-element.2264.hid_ref, ...), custom_call_target="tpu_custom_call" | custom-call | flops 4398046511104 | bytes 1073741824 | tf_op jit(solution)/shard_map/ffn_bwd/pallas_call | solution.py:1361
  338.8 25.8 %ffn_bwd.5 = (f32[1024,1024]{1,0:T(8,128)}, bf16[512,3456]{1,0:T(8,128)(2,1)}, bf16[512,3456]{1,0:T(8,128)(2,1)}) custom-call(bf16[1024,1024]{1,0:T(8,128)(2,1)} %get-tuple-element.2568.low_ref, bf16[2,1024,2304]{2,1,0:T(8,128)(2,1)} %get-tuple-element.2552.act_ref, ...), custom_call_target="tpu_custom_call", output_to_operand_aliasing={{0}: (13, {})} | custom-call | flops 4398046511104 | bytes 1073741824 | tf_op jit(solution)/shard_map/ffn_bwd/pallas_call | solution.py:1361
  377.6 25.9 %ffn_bwd.6 = (f32[1024,1024]{1,0:T(8,128)}, bf16[512,3456]{1,0:T(8,128)(2,1)}, bf16[512,3456]{1,0:T(8,128)(2,1)}) custom-call(bf16[1024,1024]{1,0:T(8,128)(2,1)} %get-tuple-element.2568.low_ref, bf16[1,1024,2304]{2,1,0:T(8,128)(2,1)} %get-tuple-element.2454.act_ref, ...), custom_call_target="tpu_custom_call", output_to_operand_aliasing={{0}: (17, {})} | custom-call | flops 4398046511104 | bytes 1073741824 | tf_op jit(solution)/shard_map/ffn_bwd/pallas_call | solution.py:1361
  420.1 25.8 %ffn_bwd.7 = (f32[1024,1024]{1,0:T(8,128)}, bf16[512,3456]{1,0:T(8,128)(2,1)}, bf16[512,3456]{1,0:T(8,128)(2,1)}) custom-call(bf16[1024,1024]{1,0:T(8,128)(2,1)} %get-tuple-element.2568.low_ref, bf16[2,1024,2304]{2,1,0:T(8,128)(2,1)} %get-tuple-element.2552.act_ref, ...), custom_call_target="tpu_custom_call", output_to_operand_aliasing={{0}: (9, {})} | custom-call | flops 4398046511104 | bytes 1073741824 | tf_op jit(solution)/shard_map/ffn_bwd/pallas_call | solution.py:1361
  459.1 12.4 %norm_two_back.1 = (f32[1024,1024]{1,0:T(8,128)}, bf16[1024,1024]{1,0:T(8,128)(2,1)}, bf16[1024,256]{1,0:T(8,128)(2,1)}, bf16[1024,256]{1,0:T(8,128)(2,1)}, bf16...) custom-call(s32[4]{0:T(128)} %pad_add_fusion.info, ...), custom_call_target="tpu_custom_call" | custom-call | flops 4398046511104 | bytes 1073741824 | tf_op jit(solution)/shard_map/norm_two_back/pallas_call | solution.py:1027
  472.1 13.7 %collective-permute-done.84.gs_ref = bf16[1024,256]{1,0:T(8,128)(2,1)S(1)} collective-permute-done((bf16[1024,256]{1,0:T(8,128)(2,1)}, bf16[1024,256]{1,0:T(8,128)(2,1)S(1)}, u32[]{:S(2)}, u32[]{:S(2)}) %collective-permute-start.84) | collective-permute-done | bytes 524320 | tf_op jit(solution)/shard_map/ppermute | solution.py:1544
  511.1 26.7 %attn_bwd.2 = (bf16[512,1024]{1,0:T(8,128)(2,1)}, bf16[512,1024]{1,0:T(8,128)(2,1)}) custom-call(s32[4]{0:T(128)} %pad_add_fusion.info, bf16[512,1024]{1,0:T(8,128)(2,1)} %get-tuple-element.2731.mine_ref, bf16[512,1024]{1,0:T(8,128)(2,1)} %copy-done.58, bf16[1024,256]{1,0:T(8,128)(2,1)} %get-tuple-element.2733.refs_17_.ok_ref, ...), custom_call_target="tpu_custom_call" | custom-call | flops 4398046511104 | bytes 1073741824 | tf_op jit(solution)/shard_map/attn_bwd/pallas_call | solution.py:907
  547.7 26.8 %attn_bwd.3 = (bf16[512,1024]{1,0:T(8,128)(2,1)}, bf16[512,1024]{1,0:T(8,128)(2,1)}) custom-call(s32[4]{0:T(128)} %pad_add_fusion.info, bf16[512,1024]{1,0:T(8,128)(2,1)} %get-tuple-element.2804.mine_ref, bf16[512,1024]{1,0:T(8,128)(2,1)} %collective-permute-done.23.got_ref, bf16[1024,256]{1,0:T(8,128)(2,1)} %get-tuple-element.2806.refs_18_.ok_ref, ...), custom_call_target="tpu_custom_call" | custom-call | flops 4398046511104 | bytes 1073741824 | tf_op jit(solution)/shard_map/attn_bwd/pallas_call | solution.py:907
  583.0 13.6 %collective-permute-start.96 = (bf16[128,3456]{1,0:T(8,128)(2,1)S(1)}, bf16[128,3456]{1,0:T(8,128)(2,1)S(1)}, u32[]{:S(2)}, u32[]{:S(2)}) collective-permute-start(bf16[128,3456]{1,0:T(8,128)(2,1)S(1)} %copy-done.28), channel_id=1, source_target_pairs={{0,3},{1,0},{2,1},{3,2},{4,7},{5,4},{6,5},{7,6},{8,11},{9,8},{10,9... | collective-permute-start | bytes 2654216 | tf_op jit(solution)/shard_map/ppermute | solution.py:1553
  624.4 12.9 %norm_one_back.1 = (bf16[512,1024]{1,0:T(8,128)(2,1)}, bf16[512,1024]{1,0:T(8,128)(2,1)}, f32[1,1024]{1,0:T(1,128)}) custom-call(s32[4]{0:T(128)} %pad_add_fusion.info, bf16[256,512]{1,0:T(8,128)(2,1)} %join.1.refs_0_, bf16[256,512]{1,0:T(8,128)(2,1)} %copy-done.7, bf16[256,512]{1,0:T(8,128)(2,1)} %copy-done.12, bf16[256,512]{1,0:T(8,128)(2,1)} %copy-done.8, ...), custom_call_target="tpu_custom_call" | custom-call | flops 4398046511104 | bytes 1073741824 | tf_op jit(solution)/shard_map/norm_one_back/pallas_call | solution.py:1087
  670.2 15.2 %collective-permute-done.103.refs_2_ = bf16[128,3456]{1,0:T(8,128)(2,1)S(1)} collective-permute-done((bf16[128,3456]{1,0:T(8,128)(2,1)}, bf16[128,3456]{1,0:T(8,128)(2,1)S(1)}, u32[]{:S(2)}, u32[]{:S(2)}) %collective-permute-start.103) | collective-permute-done | bytes 884768 | tf_op jit(solution)/shard_map/ppermute | solution.py:1544
  689.7 21.1 %collective-permute-start.118 = (bf16[512,1024]{1,0:T(8,128)(2,1)S(1)}, bf16[512,1024]{1,0:T(8,128)(2,1)}, u32[]{:S(2)}, u32[]{:S(2)}) collective-permute-start(bf16[512,1024]{1,0:T(8,128)(2,1)S(1)} %copy-done.22), channel_id=1, source_target_pairs={{0,1},{1,2},{2,3},{3,0},{4,5},{5,6},{6,7},{7,4},{8,9},{9,10},{10,1... | collective-permute-start | bytes 3145736 | tf_op jit(solution)/shard_map/ppermute | solution.py:1547
  804.3 18.1 %collective-permute-done.122.refs_3_ = bf16[128,768]{1,0:T(8,128)(2,1)S(1)} collective-permute-done((bf16[128,768]{1,0:T(8,128)(2,1)}, bf16[128,768]{1,0:T(8,128)(2,1)S(1)}, u32[]{:S(2)}, u32[]{:S(2)}) %collective-permute-start.122) | collective-permute-done | bytes 196640 | tf_op jit(solution)/shard_map/ppermute | solution.py:1547
  822.4 35.6 %collective-permute-done.121.refs_2_ = bf16[128,768]{1,0:T(8,128)(2,1)S(1)} collective-permute-done((bf16[128,768]{1,0:T(8,128)(2,1)}, bf16[128,768]{1,0:T(8,128)(2,1)S(1)}, u32[]{:S(2)}, u32[]{:S(2)}) %collective-permute-start.121) | collective-permute-done | bytes 196640 | tf_op jit(solution)/shard_map/ppermute | solution.py:1550
  (568 shorter events, 470.5 us)
Async XLA Ops:
  62.2 41.2 %collective-permute-start.14 = (bf16[256,3456]{1,0:T(8,128)(2,1)}, bf16[256,3456]{1,0:T(8,128)(2,1)}, u32[]{:S(2)}, u32[]{:S(2)}) collective-permute-start(bf16[256,3456]{1,0:T(8,128)(2,1)} %get-tuple-element.2573.rest_0_), channel_id=1, source_target_pairs={{0,16},{16,0},{8,24},{24,8},{1,17},{17,1},{9,25},{25,9},{2,18},{18... | collective-permute-start | bytes 5308424 | tf_op jit(solution)/shard_map/ppermute | solution.py:1538
  63.7 42.0 %collective-permute-start.15 = (bf16[256,3456]{1,0:T(8,128)(2,1)}, bf16[256,3456]{1,0:T(8,128)(2,1)S(1)}, u32[]{:S(2)}, u32[]{:S(2)}) collective-permute-start(bf16[256,3456]{1,0:T(8,128)(2,1)} %get-tuple-element.2573.rest_0_), channel_id=1, source_target_pairs={{0,1},{1,2},{2,3},{3,0},{4,5},{5,6},{6,7},{7,4},{8,9},{9,10},{10,1... | collective-permute-start | bytes 5308424 | tf_op jit(solution)/shard_map/ppermute | solution.py:1547
  84.7 42.2 %collective-permute-start.23 = (bf16[512,1024]{1,0:T(8,128)(2,1)}, bf16[512,1024]{1,0:T(8,128)(2,1)}, u32[]{:S(2)}, u32[]{:S(2)}) collective-permute-start(bf16[512,1024]{1,0:T(8,128)(2,1)} %get-tuple-element.1612), channel_id=1, source_target_pairs={{0,4},{4,0},{1,5},{5,1},{2,6},{6,2},{3,7},{7,3},{8,12},{12,8},{9,1... | collective-permute-start | bytes 3145736 | tf_op jit(solution)/shard_map/ppermute | solution.py:1544
  210.0 57.2 %collective-permute-start.55 = (bf16[256,1152]{1,0:T(8,128)(2,1)}, bf16[256,1152]{1,0:T(8,128)(2,1)}, u32[]{:S(2)}, u32[]{:S(2)}) collective-permute-start(bf16[256,1152]{1,0:T(8,128)(2,1)} %collective-permute-done.51.rest_3_), channel_id=1, source_target_pairs={{0,8},{8,0},{16,24},{24,16},{1,9},{9,1},{17,25},{25,17},{2,10},{10... | collective-permute-start | bytes 1769480 | tf_op jit(solution)/shard_map/ppermute | solution.py:1541
  211.5 55.8 %collective-permute-start.57 = (bf16[256,1152]{1,0:T(8,128)(2,1)}, bf16[256,1152]{1,0:T(8,128)(2,1)}, u32[]{:S(2)}, u32[]{:S(2)}) collective-permute-start(bf16[256,1152]{1,0:T(8,128)(2,1)} %collective-permute-done.51.rest_3_), channel_id=1, source_target_pairs={{0,4},{4,0},{1,5},{5,1},{2,6},{6,2},{3,7},{7,3},{8,12},{12,8},{9,1... | collective-permute-start | bytes 1769480 | tf_op jit(solution)/shard_map/ppermute | solution.py:1544
  227.8 39.5 %collective-permute-start.60 = (bf16[256,1152]{1,0:T(8,128)(2,1)}, bf16[256,1152]{1,0:T(8,128)(2,1)}, u32[]{:S(2)}, u32[]{:S(2)}) collective-permute-start(bf16[256,1152]{1,0:T(8,128)(2,1)} %collective-permute-done.52.rest_1_.rest_0_), channel_id=1, source_target_pairs={{0,8},{8,0},{16,24},{24,16},{1,9},{9,1},{17,25},{25,17},{2,10},{10... | collective-permute-start | bytes 1769480 | tf_op jit(solution)/shard_map/ppermute | solution.py:1541
  405.9 40.0 %collective-permute-start.80 = (bf16[128,3456]{1,0:T(8,128)(2,1)}, bf16[128,3456]{1,0:T(8,128)(2,1)}, u32[]{:S(2)}, u32[]{:S(2)}) collective-permute-start(bf16[128,3456]{1,0:T(8,128)(2,1)} %summed.18), channel_id=1, source_target_pairs={{0,4},{4,0},{1,5},{5,1},{2,6},{6,2},{3,7},{7,3},{8,12},{12,8},{9,1... | collective-permute-start | bytes 2654216 | tf_op jit(solution)/shard_map/ppermute | solution.py:1544
  488.9 48.9 %collective-permute-start.88 = (bf16[1024,256]{1,0:T(8,128)(2,1)}, bf16[1024,256]{1,0:T(8,128)(2,1)}, u32[]{:S(2)}, u32[]{:S(2)}) collective-permute-start(bf16[1024,256]{1,0:T(8,128)(2,1)} %get-tuple-element.2756), channel_id=1, source_target_pairs={{0,4},{4,0},{1,5},{5,1},{2,6},{6,2},{3,7},{7,3},{8,12},{12,8},{9,1... | collective-permute-start | bytes 1572872 | tf_op jit(solution)/shard_map/ppermute | solution.py:1544
  490.3 47.5 %collective-permute-start.89 = (bf16[512,1024]{1,0:T(8,128)(2,1)}, bf16[512,1024]{1,0:T(8,128)(2,1)}, u32[]{:S(2)}, u32[]{:S(2)}) collective-permute-start(bf16[512,1024]{1,0:T(8,128)(2,1)} %collective-permute-done.71), channel_id=1, source_target_pairs={{0,1},{1,2},{2,3},{3,0},{4,5},{5,6},{6,7},{7,4},{8,9},{9,10},{10,1... | collective-permute-start | bytes 3145736 | tf_op jit(solution)/shard_map/ppermute | solution.py:1547
  491.1 46.7 %collective-permute-start.86 = (bf16[128,3456]{1,0:T(8,128)(2,1)}, bf16[128,3456]{1,0:T(8,128)(2,1)}, u32[]{:S(2)}, u32[]{:S(2)}) collective-permute-start(bf16[128,3456]{1,0:T(8,128)(2,1)} %get-tuple-element.2748), channel_id=1, source_target_pairs={{0,16},{16,0},{8,24},{24,8},{1,17},{17,1},{9,25},{25,9},{2,18},{18... | collective-permute-start | bytes 2654216 | tf_op jit(solution)/shard_map/ppermute | solution.py:1538
  492.8 45.0 %collective-permute-start.87 = (bf16[128,3456]{1,0:T(8,128)(2,1)}, bf16[128,3456]{1,0:T(8,128)(2,1)}, u32[]{:S(2)}, u32[]{:S(2)}) collective-permute-start(bf16[128,3456]{1,0:T(8,128)(2,1)} %get-tuple-element.2749), channel_id=1, source_target_pairs={{0,16},{16,0},{8,24},{24,8},{1,17},{17,1},{9,25},{25,9},{2,18},{18... | collective-permute-start | bytes 2654216 | tf_op jit(solution)/shard_map/ppermute | solution.py:1538
  543.6 38.8 %collective-permute-start.92 = (bf16[512,1024]{1,0:T(8,128)(2,1)}, bf16[512,1024]{1,0:T(8,128)(2,1)}, u32[]{:S(2)}, u32[]{:S(2)}) collective-permute-start(bf16[512,1024]{1,0:T(8,128)(2,1)} %get-tuple-element.2803), channel_id=1, source_target_pairs={{0,4},{4,0},{1,5},{5,1},{2,6},{6,2},{3,7},{7,3},{8,12},{12,8},{9,1... | collective-permute-start | bytes 3145736 | tf_op jit(solution)/shard_map/ppermute | solution.py:1544
  545.1 37.3 %collective-permute-start.93 = (bf16[512,1024]{1,0:T(8,128)(2,1)}, bf16[512,1024]{1,0:T(8,128)(2,1)}, u32[]{:S(2)}, u32[]{:S(2)}) collective-permute-start(bf16[512,1024]{1,0:T(8,128)(2,1)} %collective-permute-done.73), channel_id=1, source_target_pairs={{0,1},{1,2},{2,3},{3,0},{4,5},{5,6},{6,7},{7,4},{8,9},{9,10},{10,1... | collective-permute-start | bytes 3145736 | tf_op jit(solution)/shard_map/ppermute | solution.py:1547
  600.6 36.6 %collective-permute-start.97 = (bf16[128,3456]{1,0:T(8,128)(2,1)}, bf16[128,3456]{1,0:T(8,128)(2,1)}, u32[]{:S(2)}, u32[]{:S(2)}) collective-permute-start(bf16[128,3456]{1,0:T(8,128)(2,1)} %summed.23), channel_id=1, source_target_pairs={{0,1},{1,2},{2,3},{3,0},{4,5},{5,6},{6,7},{7,4},{8,9},{9,10},{10,1... | collective-permute-start | bytes 2654216 | tf_op jit(solution)/shard_map/ppermute | solution.py:1547
  600.8 64.2 %collective-permute-start.102 = (bf16[128,3456]{1,0:T(8,128)(2,1)}, bf16[128,3456]{1,0:T(8,128)(2,1)}, u32[]{:S(2)}, u32[]{:S(2)}) collective-permute-start(bf16[128,3456]{1,0:T(8,128)(2,1)} %get-tuple-element.2913), channel_id=1, source_target_pairs={{0,16},{16,0},{8,24},{24,8},{1,17},{17,1},{9,25},{25,9},{2,18},{18... | collective-permute-start | bytes 2654216 | tf_op jit(solution)/shard_map/ppermute | solution.py:1538
  665.9 71.9 %collective-permute-start.113 = (bf16[512,1024]{1,0:T(8,128)(2,1)S(1)}, bf16[512,1024]{1,0:T(8,128)(2,1)S(1)}, u32[]{:S(2)}, u32[]{:S(2)}) collective-permute-start(bf16[512,1024]{1,0:T(8,128)(2,1)S(1)} %copy-done.24), channel_id=1, source_target_pairs={{0,3},{1,0},{2,1},{3,2},{4,7},{5,4},{6,5},{7,6},{8,11},{9,8},{10,9... | collective-permute-start | bytes 3145736 | tf_op jit(solution)/shard_map/ppermute | solution.py:1553
  689.7 96.8 %collective-permute-start.118 = (bf16[512,1024]{1,0:T(8,128)(2,1)S(1)}, bf16[512,1024]{1,0:T(8,128)(2,1)}, u32[]{:S(2)}, u32[]{:S(2)}) collective-permute-start(bf16[512,1024]{1,0:T(8,128)(2,1)S(1)} %copy-done.22), channel_id=1, source_target_pairs={{0,1},{1,2},{2,3},{3,0},{4,5},{5,6},{6,7},{7,4},{8,9},{9,10},{10,1... | collective-permute-start | bytes 3145736 | tf_op jit(solution)/shard_map/ppermute | solution.py:1547
  786.5 72.3 %collective-permute-start.119 = (f32[128,3456]{1,0:T(8,128)}, f32[128,3456]{1,0:T(8,128)S(1)}, u32[]{:S(2)}, u32[]{:S(2)}) collective-permute-start(f32[128,3456]{1,0:T(8,128)} %summed.26), channel_id=1, source_target_pairs={{0,4},{4,0},{1,5},{5,1},{2,6},{6,2},{3,7},{7,3},{8,12},{12,8},{9,1... | collective-permute-start | bytes 5308424 | tf_op jit(solution)/shard_map/ppermute | solution.py:1544
  787.9 70.2 %collective-permute-start.123 = (bf16[512,1024]{1,0:T(8,128)(2,1)S(1)}, bf16[512,1024]{1,0:T(8,128)(2,1)}, u32[]{:S(2)}, u32[]{:S(2)}) collective-permute-start(bf16[512,1024]{1,0:T(8,128)(2,1)S(1)} %copy-done.22), channel_id=1, source_target_pairs={{0,3},{1,0},{2,1},{3,2},{4,7},{5,4},{6,5},{7,6},{8,11},{9,8},{10,9... | collective-permute-start | bytes 3145736 | tf_op jit(solution)/shard_map/ppermute | solution.py:1553
  796.9 61.2 %collective-permute-start.121 = (bf16[128,768]{1,0:T(8,128)(2,1)}, bf16[128,768]{1,0:T(8,128)(2,1)S(1)}, u32[]{:S(2)}, u32[]{:S(2)}) collective-permute-start(bf16[128,768]{1,0:T(8,128)(2,1)} %summed.33), channel_id=1, source_target_pairs={{0,2},{2,0},{1,3},{3,1},{4,6},{6,4},{5,7},{7,5},{8,10},{10,8},{9,1... | collective-permute-start | bytes 589832 | tf_op jit(solution)/shard_map/ppermute | solution.py:1550
  801.2 56.8 %collective-permute-start.120 = (bf16[128,768]{1,0:T(8,128)(2,1)}, bf16[128,768]{1,0:T(8,128)(2,1)S(1)}, u32[]{:S(2)}, u32[]{:S(2)}) collective-permute-start(bf16[128,768]{1,0:T(8,128)(2,1)} %summed.32), channel_id=1, source_target_pairs={{0,3},{1,0},{2,1},{3,2},{4,7},{5,4},{6,5},{7,6},{8,11},{9,8},{10,9... | collective-permute-start | bytes 589832 | tf_op jit(solution)/shard_map/ppermute | solution.py:1553
  822.4 81.3 %collective-permute-start.129 = (bf16[512,1024]{1,0:T(8,128)(2,1)}, bf16[512,1024]{1,0:T(8,128)(2,1)}, u32[]{:S(2)}, u32[]{:S(2)}) collective-permute-start(bf16[512,1024]{1,0:T(8,128)(2,1)} %collective-permute-done.104), channel_id=1, source_target_pairs={{0,1},{1,2},{2,3},{3,0},{4,5},{5,6},{6,7},{7,4},{8,9},{9,10},{10,1... | collective-permute-start | bytes 3145736 | tf_op jit(solution)/shard_map/ppermute | solution.py:1547
  860.9 66.2 %collective-permute-start.131 = (f32[128,768]{1,0:T(8,128)}, f32[128,768]{1,0:T(8,128)}, u32[]{:S(2)}, u32[]{:S(2)}) collective-permute-start(f32[128,768]{1,0:T(8,128)} %summed.35), channel_id=1, source_target_pairs={{0,4},{4,0},{1,5},{5,1},{2,6},{6,2},{3,7},{7,3},{8,12},{12,8},{9,1... | collective-permute-start | bytes 1179656 | tf_op jit(solution)/shard_map/ppermute | solution.py:1544
  861.5 68.9 %collective-permute-start.130 = (bf16[512,1024]{1,0:T(8,128)(2,1)}, bf16[512,1024]{1,0:T(8,128)(2,1)}, u32[]{:S(2)}, u32[]{:S(2)}) collective-permute-start(bf16[512,1024]{1,0:T(8,128)(2,1)} %collective-permute-done.118), channel_id=1, source_target_pairs={{0,1},{1,2},{2,3},{3,0},{4,5},{5,6},{6,7},{7,4},{8,9},{9,10},{10,1... | collective-permute-start | bytes 3145736 | tf_op jit(solution)/shard_map/ppermute | solution.py:1547
  (201 other events, 3151.3 us)

commit v7 on v6

--- a/solution.py
+++ b/solution.py
@@ -399,7 +399,7 @@
 
 def settings(dims, mib):
     return pltpu.CompilerParams(
-        dimension_semantics=("arbitrary",) * dims, vmem_limit_bytes=max(mib, 60) << 20
+        dimension_semantics=("arbitrary",) * dims, vmem_limit_bytes=mib << 20
     )
 
 
@@ -440,31 +440,24 @@
         out_shape=[shape_of((rows, o.shape[0]), BF16), shape_of((rows, 3 * g.shape[1]), BF16)],
         scratch_shapes=[pltpu.VMEM(a.shape, BF16) for a in (o, g, u, d)]
         + [pltpu.SemaphoreType.DMA((4,))],
-        compiler_params=pltpu.CompilerParams(vmem_limit_bytes=60 << 20),
+        compiler_params=pltpu.CompilerParams(vmem_limit_bytes=24 << 20),
         cost_estimate=cost(False),
         name="pack",
     )(info, o, g, u, d)
 
 
-def join_kernel(q_ref, k_ref, v_ref, out_ref, sems):
+def join_kernel(q_ref, k_ref, v_ref, out_ref):
     at = 0
-    copies = []
-    for i, ref in enumerate((q_ref, k_ref, v_ref)):
-        cols = pl.ds(at, ref.shape[1])
-        copies.append(pltpu.make_async_copy(ref, out_ref.at[:, cols], sems.at[i]))
-        copies[-1].start()
+    for ref in (q_ref, k_ref, v_ref):
+        out_ref[:, at : at + ref.shape[1]] = ref[...]
         at += ref.shape[1]
-    for copy in copies:
-        copy.wait()
 
 
 def join(q, k, v):
     return pl.pallas_call(
         join_kernel,
-        in_specs=[ANY] * 3,
-        out_specs=ANY,
         out_shape=shape_of((q.shape[0], q.shape[1] + k.shape[1] + v.shape[1]), BF16),
-        scratch_shapes=[pltpu.SemaphoreType.DMA((3,))],
+        compiler_params=pltpu.CompilerParams(vmem_limit_bytes=8 << 20),
         cost_estimate=cost(False),
         name="join",
     )(q, k, v)
@@ -506,9 +499,8 @@
     )(info, tokens, gain)
 
 
-def proj_kernel(heads, block, info, *refs):
-    pieces = [refs[4 * k : 4 * k + 4] for k in range(4)]
-    nt_ref, cos_ref, sin_ref, qg_ref, kg_ref, rot_ref, raw_ref, w_ref, sem = refs[16:]
+def proj_kernel(heads, block, plan, count, info, *refs):
+    nt_ref, cos_ref, sin_ref, qg_ref, kg_ref, rot_ref, raw_ref, w_ref, sem = refs[count:]
     rows = w_ref.shape[0] // 4
 
     @pl.when(pl.program_id(0) == 0)
@@ -517,8 +509,9 @@
 
             @pl.when(block(info) == k)
             def _():
-                for p, piece in enumerate(pieces[k]):
-                    pltpu.make_async_copy(piece, w_ref.at[pl.ds(p * rows, rows)], sem).start()
+                for p, (piece, row) in enumerate(plan[k]):
+                    src = refs[piece].at[pl.ds(row, rows)]
+                    pltpu.make_async_copy(src, w_ref.at[pl.ds(p * rows, rows)], sem).start()
 
         pltpu.make_async_copy(w_ref, w_ref, sem).wait()
 
@@ -539,18 +532,19 @@
     rot_ref[at:, :] = raw[at:].astype(BF16)
 
 
-def project(info, pieces, normed_t, cos_part, sin_part, gain_q, gain_k, heads, block):
+def project(info, weights, normed_t, cos_part, sin_part, gain_q, gain_k, heads, block):
+    plan, pieces = weights
     width, tok = normed_t.shape
-    cols = pieces[0][0].shape[1]
+    cols = pieces[0].shape[1]
     tile = min(512, tok)
     const = lambda a: pl.BlockSpec(a.shape, lambda i, info: (0, 0))
     tab = lambda a: pl.BlockSpec((a.shape[0], tile), lambda i, info: (0, i))
     return pl.pallas_call(
-        functools.partial(proj_kernel, heads, block),
+        functools.partial(proj_kernel, heads, block, plan, len(pieces)),
         grid_spec=pltpu.PrefetchScalarGridSpec(
             num_scalar_prefetch=1,
             grid=(tok // tile,),
-            in_specs=[ANY] * 16
+            in_specs=[ANY] * len(pieces)
             + [tab(normed_t), tab(cos_part), tab(sin_part), const(gain_q), const(gain_k)],
             out_specs=[pl.BlockSpec((cols, tile), lambda i, info: (0, i))] * 2,
             scratch_shapes=[pltpu.VMEM((width, cols), BF16), pltpu.SemaphoreType.DMA],
@@ -559,7 +553,7 @@
         compiler_params=settings(1, 24),
         cost_estimate=cost(False),
         name="project",
-    )(info, *[p for b in pieces for p in b], normed_t, cos_part, sin_part, gain_q, gain_k)
+    )(info, *pieces, normed_t, cos_part, sin_part, gain_q, gain_k)
 
 
 def head_back_kernel(
@@ -772,7 +766,7 @@
             shape_of((tok, heads_k * 2 * hd), BF16),
             shape_of((heads_k, 2, 2 * tok), F32),
         ],
-        compiler_params=settings(2, 32),
+        compiler_params=settings(2, 60),
         cost_estimate=cost(True),
         name="attn_fwd",
     )(info, mine, got)
@@ -929,26 +923,27 @@
             ],
         ),
         out_shape=[shape_of((cols, tok), BF16), shape_of((cols, tok), BF16)],
-        compiler_params=settings(2, 40),
+        compiler_params=settings(2, 60),
         cost_estimate=cost(True),
         name="attn_bwd",
     )(info, mine, got, out_keep, out_send, grad_keep, grad_send, lse)
 
 
-def load_blocks(pieces, target, sem):
+def load_blocks(plan, pieces, target, sem):
     rows = target.shape[1] // 4
 
     @pl.when(pl.program_id(0) == 0)
     def _():
-        for i, piece in enumerate(pieces):
-            block = target.at[i // 4, pl.ds(i % 4 * rows, rows)]
-            pltpu.make_async_copy(piece, block, sem).start()
+        for k, places in enumerate(plan):
+            for p, (piece, row) in enumerate(places):
+                src = pieces[piece].at[pl.ds(row, rows)]
+                pltpu.make_async_copy(src, target.at[k, pl.ds(p * rows, rows)], sem).start()
         pltpu.make_async_copy(target, target, sem).wait()
 
 
-def out_proj_kernel(info, *refs):
-    x_ref, a0, a1, b0, b1, gain_ref, r_ref, n_ref, nt_ref, att_ref, w_ref, sem = refs[16:]
-    load_blocks(refs[:16], w_ref, sem)
+def out_proj_kernel(plan, count, info, *refs):
+    x_ref, a0, a1, b0, b1, gain_ref, r_ref, n_ref, nt_ref, att_ref, w_ref, sem = refs[count:]
+    load_blocks(plan, refs, w_ref, sem)
     ctx = info[2]
     total = x_ref[...].astype(F32)
     for j, ref, side in ((0, a0, ctx), (1, a1, ctx), (0, b0, 1 - ctx), (1, b1, 1 - ctx)):
@@ -963,16 +958,17 @@
     nt_ref[...] = normed.T.astype(BF16)
 
 
-def out_proj(info, x, mine, theirs, pieces, gain, tile):
+def out_proj(info, x, mine, theirs, weights, gain, tile):
+    plan, pieces = weights
     tok, width = x.shape
-    feats = pieces[0][0].shape[1]
+    feats = pieces[0].shape[1]
     rows_of = lambda n: pl.BlockSpec((tile, n), lambda i, info: (i, 0))
     return pl.pallas_call(
-        out_proj_kernel,
+        functools.partial(out_proj_kernel, plan, len(pieces)),
         grid_spec=pltpu.PrefetchScalarGridSpec(
             num_scalar_prefetch=1,
             grid=(tok // tile,),
-            in_specs=[ANY] * 16
+            in_specs=[ANY] * len(pieces)
             + [rows_of(width)]
             + [rows_of(feats)] * 4
             + [pl.BlockSpec((1, width), lambda i, info: (0, 0))],
@@ -993,12 +989,12 @@
         compiler_params=settings(1, 32),
         cost_estimate=cost(True),
         name="out_proj",
-    )(info, *[p for b in pieces for p in b], x, *mine, *theirs, gain)
-
-
-def norm_two_back_kernel(info, *refs):
-    g_ref, r_ref, gr_ref, gain_ref, gres_ref, gat_ref, a0, a1, b0, b1, gg_ref, w_ref, sem = refs[16:]
-    load_blocks(refs[:16], w_ref, sem)
+    )(info, *pieces, x, *mine, *theirs, gain)
+
+
+def norm_two_back_kernel(plan, count, info, *refs):
+    g_ref, r_ref, gr_ref, gain_ref, gres_ref, gat_ref, a0, a1, b0, b1, gg_ref, w_ref, sem = refs[count:]
+    load_blocks(plan, refs, w_ref, sem)
     ctx = info[2]
     grad, resid = g_ref[...], r_ref[...]
     rho = lax.rsqrt(jnp.mean(resid * resid, axis=-1, keepdims=True) + EPS)
@@ -1019,17 +1015,18 @@
         ref[...] = dot(low, w_ref[2 * side + j], 1, 0).astype(BF16)
 
 
-def norm_two_back(info, grad, resid, grad_result, gain, pieces, tile):
+def norm_two_back(info, grad, resid, grad_result, gain, weights, tile):
+    plan, pieces = weights
     tok, width = grad.shape
-    feats = pieces[0][0].shape[1]
+    feats = pieces[0].shape[1]
     rows_of = lambda n: pl.BlockSpec((tile, n), lambda i, info: (i, 0))
     row = pl.BlockSpec((1, width), lambda i, info: (0, 0))
     return pl.pallas_call(
-        norm_two_back_kernel,
+        functools.partial(norm_two_back_kernel, plan, len(pieces)),
         grid_spec=pltpu.PrefetchScalarGridSpec(
             num_scalar_prefetch=1,
             grid=(tok // tile,),
-            in_specs=[ANY] * 16 + [rows_of(width)] * 3 + [row],
+            in_specs=[ANY] * len(pieces) + [rows_of(width)] * 3 + [row],
             out_specs=[rows_of(width), pl.BlockSpec((width, tile), lambda i, info: (0, i))]
             + [rows_of(feats)] * 4
             + [row],
@@ -1041,12 +1038,12 @@
         compiler_params=settings(1, 32),
         cost_estimate=cost(True),
         name="norm_two_back",
-    )(info, *[p for b in pieces for p in b], grad, resid, grad_result, gain)
-
-
-def norm_one_back_kernel(info, *refs):
-    p0, p1, x_ref, gres_ref, gain_ref, outa_ref, outb_ref, gg_ref, w_ref, sem = refs[16:]
-    load_blocks(refs[:16], w_ref, sem)
+    )(info, *pieces, grad, resid, grad_result, gain)
+
+
+def norm_one_back_kernel(plan, count, info, *refs):
+    p0, p1, x_ref, gres_ref, gain_ref, outa_ref, outb_ref, gg_ref, w_ref, sem = refs[count:]
+    load_blocks(plan, refs, w_ref, sem)
     quarter = x_ref.shape[1] // 4
     grad = dot(p0[0], w_ref[0], 1, 1)
     grad = grad + dot(p1[0], w_ref[1], 1, 1)
@@ -1077,19 +1074,20 @@
     gg_ref[...] += jnp.sum(grad * unit, axis=0, keepdims=True)
 
 
-def norm_one_back(info, pairs, pieces, x, grad_resid, gain, tile):
+def norm_one_back(info, pairs, weights, x, grad_resid, gain, tile):
+    plan, pieces = weights
     tok, width = x.shape
-    cols = pieces[0][0].shape[1]
+    cols = pieces[0].shape[1]
     rows_of = lambda n: pl.BlockSpec((tile, n), lambda i, info: (i, 0))
     pair = pl.BlockSpec((2, tile, cols), lambda i, info: (0, i, 0))
     half = tok // tile // 2
     row = pl.BlockSpec((1, width), lambda i, info: (0, 0))
     return pl.pallas_call(
-        norm_one_back_kernel,
+        functools.partial(norm_one_back_kernel, plan, len(pieces)),
         grid_spec=pltpu.PrefetchScalarGridSpec(
             num_scalar_prefetch=1,
             grid=(tok // tile,),
-            in_specs=[ANY] * 16 + [pair, pair, rows_of(width), rows_of(width), row],
+            in_specs=[ANY] * len(pieces) + [pair, pair, rows_of(width), rows_of(width), row],
             out_specs=[
                 pl.BlockSpec((tile, width), lambda i, info: (jnp.minimum(i, half - 1), 0)),
                 pl.BlockSpec((tile, width), lambda i, info: (jnp.maximum(i - half, 0), 0)),
@@ -1101,7 +1099,7 @@
         compiler_params=settings(1, 32),
         cost_estimate=cost(True),
         name="norm_one_back",
-    )(info, *[p for b in pieces for p in b], *pairs, x, grad_resid, gain)
+    )(info, *pieces, *pairs, x, grad_resid, gain)
 
 
 def weight_copies(plan, pieces, gate_up, down, gate_up_sem, down_sem):
@@ -1110,8 +1108,8 @@
     wide, thin = [], []
     for p, chunks in enumerate(plan):
         block = pl.ds(p * rows, rows)
-        for j, (piece, at) in enumerate(chunks):
-            src = pieces[piece]
+        for j, (piece, row, at) in enumerate(chunks):
+            src = pieces[piece].at[pl.ds(row, rows)]
             wide.append(
                 pltpu.make_async_copy(
                     src.at[:, pl.ds(at, 2 * third)],
@@ -1140,7 +1138,7 @@
         teach_ref, rest = rest[0], rest[1:]
     pieces = []
     for plan in plans:
-        count = 1 + max(piece for chunks in plan for piece, _ in chunks)
+        count = 1 + max(place[0] for chunks in plan for place in chunks)
         pieces.append(rest[:count])
         rest = rest[count:]
     act_ref, hid_ref = rest[:2]
@@ -1286,14 +1284,14 @@
             ],
         ),
         out_shape=out_shape,
-        compiler_params=settings(2, 50),
+        compiler_params=settings(2, 60),
         cost_estimate=cost(True),
         name="ffn_fwd",
     )(info, scale, x, total, *([teacher] if last else []), *pieces)
 
 
 def ffn_bwd_kernel(steps, plan, first, low_ref, act_ref, hid_ref, xt_ref, lowt_ref, *rest):
-    count = 1 + max(piece for chunks in plan for piece, _ in chunks)
+    count = 1 + max(place[0] for chunks in plan for place in chunks)
     pieces, rest = rest[:count], rest[count:]
     if not first:
         in_ref, rest = rest[0], rest[1:]
@@ -1388,7 +1386,7 @@
             pltpu.SemaphoreType.DMA((2,)),
         ],
         input_output_aliases={} if first else {5 + len(pieces): 0},
-        compiler_params=settings(1, 56),
+        compiler_params=settings(1, 60),
         cost_estimate=cost(True),
         name="ffn_bwd",
     )(low, acts, hiddens, xt, lowt, *pieces, *([] if first else [total]))
@@ -1413,10 +1411,10 @@
 
 def summed(terms, turns=None, dtype=BF16):
     rows, cols = terms[0].shape
-    spec = pl.BlockSpec((64, cols), lambda i: (i, 0))
+    spec = pl.BlockSpec((128, cols), lambda i: (i, 0))
     return pl.pallas_call(
         functools.partial(sum_kernel, turns or [False] * len(terms)),
-        grid=(rows // 64,),
+        grid=(rows // 128,),
         in_specs=[spec] * len(terms),
         out_specs=spec,
         out_shape=shape_of((rows, cols), dtype),
@@ -1428,78 +1426,71 @@
 
 def core_sum_kernel(info, left_ref, right_ref, *outs):
     total = (left_ref[...].astype(F32) + right_ref[...].astype(F32)).astype(BF16)
-    block = pl.program_id(0) // 2
-    far, other = block // 2, jnp.bitwise_xor(block % 2, info[2])
+    block = pl.program_id(1)
+    place = block // 2 * 2 + jnp.bitwise_xor(block % 2, info[2])
     for i, out in enumerate(outs):
 
-        @pl.when(far * 2 + other == i)
+        @pl.when(place == i)
         def _():
             out[...] = total
 
 
 def core_sum(info, keep, came):
-    rows, cols = keep.shape
-    block = lambda at: pl.BlockSpec((64, cols), at)
-
-    def place(far, other):
-        def at(i, info):
-            return (jnp.clip(i - 4 * far - 2 * jnp.bitwise_xor(info[2], other), 0, 1), 0)
-
-        return block(at)
-
+    groups, rows, cols = keep.shape
+    spec = pl.BlockSpec((1, rows // 4, cols), lambda g, i, info: (g, i, 0))
     return pl.pallas_call(
         core_sum_kernel,
         grid_spec=pltpu.PrefetchScalarGridSpec(
             num_scalar_prefetch=1,
-            grid=(rows // 64,),
-            in_specs=[block(lambda i, info: (i, 0))] * 2,
-            out_specs=[place(0, 0), place(0, 1), place(1, 0), place(1, 1)],
+            grid=(groups, 4),
+            in_specs=[spec] * 2,
+            out_specs=[pl.BlockSpec((1, rows // 4, cols), lambda g, i, info: (g, 0, 0))] * 4,
         ),
-        out_shape=[shape_of((rows // 4, cols), BF16)] * 4,
-        compiler_params=settings(1, 24),
+        out_shape=[shape_of((groups, rows // 4, cols), BF16)] * 4,
+        compiler_params=settings(2, 24),
         cost_estimate=cost(False),
         name="core_sum",
     )(info, keep, came)
 
 
-def weight_grad_kernel(nt_ref, back_ref, gt_ref, att_ref, keep_ref, send_ref):
-    cols = back_ref.shape[2]
-
-    def rows(target):
-        target[:, :cols] = dot(nt_ref[...], back_ref[0], 1, 0).astype(BF16)
-        target[:, cols:] = dot(gt_ref[...], att_ref[0], 1, 0).astype(BF16)
-
-    @pl.when(pl.program_id(0) < 2)
-    def _():
-        rows(send_ref)
-
-    @pl.when(pl.program_id(0) >= 2)
-    def _():
-        rows(keep_ref)
-
-
-def weight_grad(normed_t, back, side, grad_t, attended, block):
+def weight_grad_kernel(nt_ref, back0_ref, back1_ref, gt_ref, att_ref, keep_ref, send_ref):
+    cols = back0_ref.shape[2]
+    part, block = pl.program_id(0), pl.program_id(1)
+
+    def rows(target, back_ref):
+        target[0, :, :cols] = dot(nt_ref[...], back_ref[0], 1, 0).astype(BF16)
+        target[0, :, cols:] = dot(gt_ref[...], att_ref[0], 1, 0).astype(BF16)
+
+    for j, back_ref in enumerate((back0_ref, back1_ref)):
+
+        @pl.when((part == 0) & (block % 2 == j))
+        def _():
+            rows(send_ref, back_ref)
+
+        @pl.when((part == 1) & (block % 2 == j))
+        def _():
+            rows(keep_ref, back_ref)
+
+
+def weight_grad(normed_t, backs, grad_t, attended):
     width, tok = normed_t.shape
-    cols, feats = back.shape[2], attended.shape[2]
-    rows = pl.BlockSpec((width // 4, tok), lambda i: (jnp.bitwise_xor(i, 2), 0))
+    cols, feats = backs[0].shape[2], attended.shape[2]
+    half = pl.BlockSpec((width // 2, tok), lambda p, k: (1 - p, 0))
+    side = pl.BlockSpec((1, tok, cols), lambda p, k: (k // 2, 0, 0))
+    shape = (1, width // 2, cols + feats)
     return pl.pallas_call(
         weight_grad_kernel,
-        grid=(4,),
-        in_specs=[
-            rows,
-            pl.BlockSpec((1, tok, cols), lambda i: (side, 0, 0)),
-            rows,
-            pl.BlockSpec((1, tok, feats), lambda i: (block, 0, 0)),
+        grid=(2, 4),
+        in_specs=[half, side, side, half, pl.BlockSpec((1, tok, feats), lambda p, k: (k, 0, 0))],
+        out_specs=[
+            pl.BlockSpec(shape, lambda p, k: (jnp.where(p == 0, 0, k), 0, 0)),
+            pl.BlockSpec(shape, lambda p, k: (jnp.where(p == 0, k, 3), 0, 0)),
         ],
-        out_specs=[
-            pl.BlockSpec((width // 4, cols + feats), lambda i: (jnp.maximum(i - 2, 0), 0)),
-            pl.BlockSpec((width // 4, cols + feats), lambda i: (jnp.minimum(i, 1), 0)),
-        ],
-        out_shape=[shape_of((width // 2, cols + feats), BF16)] * 2,
-        compiler_params=settings(1, 24),
-        cost_estimate=cost(False),
+        out_shape=[shape_of((4, width // 2, cols + feats), BF16)] * 2,
+        compiler_params=settings(2, 32),
+        cost_estimate=cost(True),
         name="weight_grad",
-    )(normed_t, back, grad_t, attended)
+    )(normed_t, *backs, grad_t, attended)
 
 
 def after(value, *others):
@@ -1568,63 +1559,57 @@
     length = lax.dynamic_slice_in_dim(lengths, z, 1, 0)
     info = jnp.concatenate([jnp.stack([z, fsdp, ctx]).astype(jnp.int32), length])
     w_proj = join(q_weight, k_weight, v_weight)
-    proj_blocks = [w_proj, z_up(w_proj), z_far(w_proj), z_down(w_proj)]
-    proj_far = [x_swap(w_proj)]
-    w_out, w_ffn = pack(info, o_weight, gate_weight, up_weight, down_weight)
+    proj_z = [z_up(w_proj), z_far(w_proj), z_down(w_proj)]
+    proj_far = x_swap(w_proj)
     count_here = jnp.sum(lengths).astype(F32)[None]
     vector = jnp.concatenate([attn_gain, ffn_gain, q_gain, k_gain]).astype(F32)
     vector = jnp.concatenate([vector, count_here, jnp.zeros((640 - 545,), F32)])[None]
     vector = jnp.concatenate([vector, x_swap(vector)], axis=0)
+    vector = jnp.concatenate([vector, core_swap(vector)], axis=0)
+    w_out, w_ffn = pack(info, o_weight, gate_weight, up_weight, down_weight)
     pos = (ctx * tok + jnp.arange(tok, dtype=jnp.int32)).astype(F32)
     frequency = THETA ** (-(2.0 * jnp.arange(hd // 2, dtype=F32)) / hd)
     angles = frequency[:, None] * pos[None, :]
+    head_gains = natural(vector[:, 2 * quarter : 544])
     v.update(
         info=info,
-        proj_blocks=proj_blocks,
+        w_proj=w_proj,
         proj_far=proj_far,
+        proj_z=jnp.concatenate(proj_z, axis=0),
         w_out=w_out,
         w_ffn=w_ffn,
-        vector=vector,
+        gain_one=vector[:, :quarter].reshape(1, width),
+        gain_two=vector[:, quarter : 2 * quarter].reshape(1, width),
+        total_count=jnp.sum(vector[:, 544]),
+        gain_q=head_gains[:, : hd // 4].reshape(hd, 1),
+        gain_k=head_gains[:, hd // 4 :].reshape(hd, 1),
         cos_part=jnp.cos(angles),
         sin_part=jnp.sin(angles),
     )
     sync()
     info = v["info"]
 
-    proj_far = v["proj_far"] + [x_swap(block) for block in v["proj_blocks"][1:]]
-    w_out = v["w_out"]
-    out_blocks = [w_out, z_up(w_out), z_far(w_out), z_down(w_out)]
-    own_cores = [core_swap(v["proj_blocks"][0]), core_swap(proj_far[0])]
-    vector = jnp.concatenate([v["vector"], core_swap(v["vector"])], axis=0)
-    gain_one = vector[:, :quarter].reshape(1, width)
-    gain_two = vector[:, quarter : 2 * quarter].reshape(1, width)
-    total_count = jnp.sum(vector[:, 544])
-    head_gains = natural(vector[:, 2 * quarter : 544])
-    x_in, normed_one_t = norm_one(info, tokens, gain_one, 256)
+    proj_zfar = x_swap(v["proj_z"])
+    out_z = [z_up(v["w_out"]), z_far(v["w_out"]), z_down(v["w_out"])]
+    proj_core = core_swap(v["w_proj"])
+    x_in, normed_one_t = norm_one(info, tokens, v["gain_one"], 256)
     v.update(
-        proj_far=proj_far,
-        out_blocks=out_blocks,
-        own_cores=own_cores,
-        gain_one=gain_one,
-        gain_two=gain_two,
-        gain_q=head_gains[:, : hd // 4].reshape(hd, 1),
-        gain_k=head_gains[:, hd // 4 :].reshape(hd, 1),
-        total_count=total_count,
-        x_in=x_in,
-        normed_one_t=normed_one_t,
-    )
-    sync()
-
+        proj_zfar=proj_zfar, proj_core=proj_core, x_in=x_in, normed_one_t=normed_one_t, out_z=out_z
+    )
+    sync()
+
+    proj_cores = [v["proj_core"], core_swap(v["proj_far"])]
+    proj_cores += [core_swap(v["proj_z"]), core_swap(v["proj_zfar"])]
+    plan_proj = [[(0, 0), (1, 0), (4, 0), (5, 0)]]
+    plan_proj += [[(p, k * quarter) for p in (2, 3, 6, 7)] for k in range(3)]
+    weights_proj = [v["w_proj"], v["proj_far"], v["proj_z"], v["proj_zfar"]] + proj_cores
     ffn_one = z_up(v["w_ffn"])
     ffn_far = x_swap(v["w_ffn"])
-    proj_pieces = []
-    for k, (block, far) in enumerate(zip(v["proj_blocks"], v["proj_far"])):
-        cores = v["own_cores"] if k == 0 else [core_swap(block), core_swap(far)]
-        proj_pieces.append([block, far] + cores)
     tables = [v[name] for name in ("cos_part", "sin_part", "gain_q", "gain_k")]
 
     def make(block, *then):
-        return project(info, proj_pieces, after(v["normed_one_t"], *then), *tables, heads, block)
+        normed_t = after(v["normed_one_t"], *then)
+        return project(info, (plan_proj, weights_proj), normed_t, *tables, heads, block)
 
     theirs = [make(lambda s: 2 * (1 - s[2]))]
     got = [y_swap(theirs[0][0])]
@@ -1635,53 +1620,55 @@
     v.update(
         ffn_one=ffn_one,
         ffn_far=ffn_far,
-        proj_pieces=proj_pieces,
+        weights_proj=weights_proj,
         mine=mine,
         theirs=theirs,
         got0=got[0],
     )
     sync()
 
+    out_blocks = jnp.concatenate([v["w_out"]] + v["out_z"], axis=0)
     one_far = [x_swap(chunks(v["ffn_one"])[0])]
     three = [z_down(chunks(v["w_ffn"])[0])]
+    own_cores = [core_swap(v["w_ffn"]), core_swap(v["ffn_far"])]
     first = attn_fwd(info, v["mine"][0][0], v["got0"], hd)
-    v.update(first=first, got1=got[1], one_far=one_far, three=three)
+    v.update(
+        first=first,
+        got1=got[1],
+        one_far=one_far,
+        three=three,
+        out_blocks=out_blocks,
+        own_cores=own_cores,
+    )
     sync()
 
     arrived = [y_swap(v["first"][1])]
     three = v["three"] + [z_down(chunks(v["w_ffn"])[1])]
-    out_far = [x_swap(block) for block in v["out_blocks"]]
-    own_cores = [core_swap(v["w_ffn"]), core_swap(v["ffn_far"])]
+    out_far = x_swap(v["out_blocks"])
+    one_cores = [core_swap(v["ffn_one"]), core_swap(v["one_far"][0])]
     second = attn_fwd(info, v["mine"][1][0], v["got1"], hd)
-    v.update(
-        second=second, arrived=arrived, three=three, out_far=out_far, own_cores=own_cores
-    )
+    v.update(second=second, arrived=arrived, three=three, out_far=out_far, one_cores=one_cores)
     sync()
 
     arrived = v["arrived"] + [y_swap(v["second"][1])]
     three = v["three"] + [z_down(chunks(v["w_ffn"])[2])]
     one_far = v["one_far"] + [x_swap(chunks(v["ffn_one"])[1])]
-    one_cores = [core_swap(v["ffn_one"]), core_swap(one_far[0])]
-    out_pieces = [
-        [block, far, core_swap(block), core_swap(far)]
-        for block, far in zip(v["out_blocks"], v["out_far"])
-    ]
-    v.update(
-        arrived=arrived, three=three, one_far=one_far, one_cores=one_cores, out_pieces=out_pieces
-    )
-    sync()
-
+    weights_out = [v["out_blocks"], v["out_far"]]
+    weights_out += [core_swap(v["out_blocks"]), core_swap(v["out_far"])]
+    v.update(arrived=arrived, three=three, one_far=one_far, weights_out=weights_out)
+    sync()
+
+    plan_out = [[(p, k * quarter) for p in range(4)] for k in range(4)]
     two = [z_up(chunks(v["ffn_one"])[0])]
     three_far = [x_swap(v["three"][0])]
     one_last = y_swap(v["one_far"][0])
     one_cores = v["one_cores"] + [core_swap(v["one_far"][1])]
-    three_cores = [core_swap(v["three"][0]), core_swap(v["three"][1])]
     resid, normed_two, normed_two_t, attended = out_proj(
         info,
         v["x_in"],
         [v["first"][0], v["second"][0]],
         v["arrived"],
-        v["out_pieces"],
+        (plan_out, v["weights_out"]),
         v["gain_two"],
         256,
     )
@@ -1690,7 +1677,6 @@
         three_far=three_far,
         one_last=one_last,
         one_cores=one_cores,
-        three_cores=three_cores,
         resid=resid,
         normed_two=normed_two,
         normed_two_t=normed_two_t,
@@ -1698,25 +1684,29 @@
     )
     sync()
 
-    in_block = lambda i: [(i, 0), (i, units), (i, 2 * units)]
-    in_row = lambda i: [(i, 0), (i + 1, 0), (i + 2, 0)]
+    in_block = lambda i: [(i, 0, j * units) for j in range(3)]
     plan0 = [in_block(i) for i in range(4)]
-    plan1 = [in_block(0), in_row(1), in_block(4), in_row(5)]
-    plan3 = [in_row(3 * i) for i in range(4)]
+    plan1 = [in_block(0), [(i, 0, 0) for i in (1, 2, 3)]]
+    plan1 += [in_block(4), [(i, 0, 0) for i in (5, 6, 7)]]
+    plan3 = [[(0, 0, 0), (1, 0, 0), (2, 0, 0)], [(3, 0, 0), (4, 0, 0), (5, 0, 0)]]
+    plan3 += [[(6, j * quarter, 0) for j in range(3)]]
+    plan3 += [[(6, 3 * quarter, 0), (7, 0, 0), (8, 0, 0)]]
+    plan2 = [[(0, 0, 0), (1, 0, 0), (1, 0, units)], [(2, quarter, 0), (3, 0, 0), (4, 0, 0)]]
+    plan2 += [[(5, 4 * quarter, 0), (6, 0, 0), (6, 0, units)]]
+    plan2 += [[(7, quarter, 0), (8, 0, 0), (9, 0, 0)]]
     scale = (slots / v["total_count"])[None]
     weights0 = [v["w_ffn"], v["ffn_far"]] + v["own_cores"]
     weights1 = [v["ffn_one"]] + v["one_far"] + [v["one_last"]]
     weights1 += v["one_cores"] + [core_swap(v["one_last"])]
-    two = v["two"] + [z_up(part) for part in chunks(v["ffn_one"])[1:]]
-    three_far = v["three_far"] + [x_swap(v["three"][1])]
-    two_far = [x_swap(v["two"][0])]
+    two = v["two"] + [z_up(v["ffn_one"][:, units:])]
+    mixed_far = x_swap(jnp.concatenate([v["three"][1], v["two"][0]], axis=0))
     three_last = y_swap(v["three_far"][0])
-    three_cores = v["three_cores"] + [core_swap(v["three"][2]), core_swap(v["three_far"][0])]
-    two_cores = [core_swap(v["two"][0])]
+    mixed = jnp.concatenate(v["three"] + [v["three_far"][0], v["two"][0]], axis=0)
+    mixed_core = core_swap(mixed)
     acts_a, hiddens_a, sum_a = ffn_fwd(
         info,
         scale,
-        v["normed_two"],
+        after(v["normed_two"], mixed),
         v["resid"],
         None,
         [(plan0, weights0), (plan1, weights1)],
@@ -1728,40 +1718,41 @@
         weights0=weights0,
         weights1=weights1,
         two=two,
-        three_far=three_far,
-        two_far=two_far,
+        mixed_far=mixed_far,
         three_last=three_last,
-        three_cores=three_cores,
-        two_cores=two_cores,
+        mixed_core=mixed_core,
         acts_a=acts_a,
         hiddens_a=hiddens_a,
         sum_a=sum_a,
     )
     sync()
 
-    weights3 = v["three"] + v["three_far"] + [v["three_last"]] + v["three_cores"]
-    weights3 += [core_swap(v["three_far"][1]), core_swap(v["three_last"])]
-    two_far = v["two_far"] + [x_swap(v["two"][1])]
-    two_last = y_swap(v["two_far"][0])
-    two_cores = v["two_cores"] + [core_swap(p) for p in v["two"][1:] + v["two_far"]]
+    far_core = core_swap(v["mixed_far"])
+    weights3 = v["three"] + [v["three_far"][0], v["mixed_far"], v["three_last"]]
+    weights3 += [v["mixed_core"], far_core, core_swap(v["three_last"])]
+    two_far = x_swap(v["two"][1][:, :units])
+    two_last = y_swap(v["mixed_far"][quarter:])
+    two_core = core_swap(v["two"][1])
     acts_b, hiddens_b, sum_b = ffn_fwd(
         info, v["scale"], v["normed_two"], v["sum_a"], None, [(plan3, weights3)], units, 256
     )
     v.update(
         weights3=weights3,
+        far_core=far_core,
         two_far=two_far,
         two_last=two_last,
-        two_cores=two_cores,
+        two_core=two_core,
         acts_b=acts_b,
         hiddens_b=hiddens_b,
         sum_b=sum_b,
     )
     sync()
 
-    weights2 = v["two"] + v["two_far"] + [v["two_last"]] + v["two_cores"]
-    weights2 += [core_swap(v["two_far"][1]), core_swap(v["two_last"])]
+    weights2 = v["two"] + [v["mixed_far"], v["two_far"], v["two_last"]]
+    weights2 += [v["mixed_core"], v["two_core"], v["far_core"]]
+    weights2 += [core_swap(v["two_far"]), core_swap(v["two_last"])]
     acts_c, hiddens_c, *results, grad_result, grad_low, grad_low_t, square = ffn_fwd(
-        info, v["scale"], v["normed_two"], v["sum_b"], teacher, [(plan3, weights2)], units, 256
+        info, v["scale"], v["normed_two"], v["sum_b"], teacher, [(plan2, weights2)], units, 256
     )
     v.update(
         weights2=weights2,
@@ -1786,9 +1777,12 @@
             256,
         )
 
+    def sum_of(k):
+        return [p[0] for p in core_sum(info, v[f"keep{k}"][None], v[f"came{k}"][None])]
+
     turned = [False, False, True]
     one = [z_up(v["results"][0])]
-    total, keep2, send2 = ffn_back(plan3, "weights2", "acts_c", "hiddens_c", 0, None)
+    total, keep2, send2 = ffn_back(plan2, "weights2", "acts_c", "hiddens_c", 0, None)
     v.update(one=one, total=total, keep2=keep2, send2=send2)
     sync()
 
@@ -1800,7 +1794,7 @@
 
     out_three = [z_down(v["results"][0])]
     came1 = core_swap(v["send1"])
-    sum2 = core_sum(info, v["keep2"], v["came2"])
+    sum2 = sum_of(2)
     far_t2 = x_swap(sum2[3])
     total, keep3, send3 = ffn_back(
         plan3, "weights3", "acts_b", "hiddens_b", 0, after(v["total"], sum2[0])
@@ -1820,7 +1814,7 @@
     came3 = core_swap(v["send3"])
     far_h2 = x_swap(v["sum2"][2])
     there2 = y_swap(summed([v["sum2"][1], v["far_t2"]]))
-    sum1 = core_sum(info, v["keep1"], v["came1"])
+    sum1 = sum_of(1)
     total, keep0, send0 = ffn_back(
         plan0, "weights0", "acts_a", "hiddens_a", 0, after(v["total"], sum1[0])
     )
@@ -1839,14 +1833,14 @@
     came0 = core_swap(v["send0"])
     far_t1 = x_swap(v["sum1"][3])
     down2 = z_down(summed([v["sum2"][0], v["far_h2"], v["there2"]], turned))
-    sum3 = core_sum(info, v["keep3"], v["came3"])
+    sum3 = sum_of(3)
     grad_resid, grad_attn_t, a0, a1, b0, b1, gain_two_sum = norm_two_back(
         info,
         after(v["total"], sum3[0]),
         v["resid"],
         v["grad_result"],
         v["gain_two"],
-        v["out_pieces"],
+        (plan_out, v["weights_out"]),
         256,
     )
     grad_got = [y_swap(b0), y_swap(b1)]
@@ -1873,8 +1867,8 @@
     far_h1 = x_swap(v["sum1"][2])
     there1 = y_swap(summed([v["sum1"][1], v["far_t1"]]))
     far_t3 = x_swap(v["sum3"][3])
-    sum0 = core_sum(info, v["keep0"], v["came0"])
-    back0 = attn_back(0, after(v["grad_mine"][0], sum0[0], there1))
+    sum0 = sum_of(0)
+    back0 = attn_back(0, after(v["grad_mine"][0], sum0[0]))
     v.update(
         out_two=two,
         far_h1=far_h1,
@@ -1919,7 +1913,7 @@
     *tokens_low, gain_one_sum = norm_one_back(
         info,
         [v["head0"][0], head1[0]],
-        v["proj_pieces"],
+        (plan_proj, v["weights_proj"]),
         v["x_in"],
         v["grad_resid"],
         v["gain_one"],
@@ -1929,50 +1923,40 @@
     sync()
 
     tok_one = [z_up(v["tokens_low"][0])]
+    keep, send = weight_grad(
+        v["normed_one_t"], [v["head0"][0], v["head1"][0]], v["grad_attn_t"], v["attended"]
+    )
+    v.update(tok_one=tok_one, keep=keep, send=send, there0=there0, far_h0=far_h0)
+    sync()
+
+    tok_one = v["tok_one"] + [z_up(v["tokens_low"][1])]
     tok_three = [z_down(v["tokens_low"][0])]
-    grads = []
-    for k in range(4):
-        grads.append(
-            weight_grad(
-                after(v["normed_one_t"], *(grads[-1] if grads else ())),
-                v[f"head{k % 2}"][0],
-                k // 2,
-                v["grad_attn_t"],
-                v["attended"],
-                k,
-            )
-        )
-    came = [core_swap(send) for _, send in grads]
-    v.update(tok_one=tok_one, keeps=[keep for keep, _ in grads], came=came, there0=there0)
-    v.update(far_h0=far_h0)
-    sync()
-
-    tok_one = v["tok_one"] + [z_up(v["tokens_low"][1])]
-    sums = []
-    for keep, other in zip(v["keeps"], v["came"]):
-        sums.append(core_sum(info, after(keep, *(sums[-1] if sums else ())), other))
-    far_t = [x_swap(s[3]) for s in sums]
-    far_h = [x_swap(s[2]) for s in sums]
+    rows = quarter // 2
+    flat = lambda a: a.reshape(4 * rows, a.shape[-1])
+    sums = [flat(p) for p in core_sum(info, v["keep"], core_swap(v["send"]))]
+    far_t = x_swap(sums[3])
+    far_h = x_swap(sums[2])
     part0 = summed([v["sum0"][0], v["far_h0"], v["there0"]], turned)
     ffn_sum = summed([part0, v["two_down"], v["up3"]], None, F32)
-    v.update(tok_three=tok_three, sums=sums, far_t=far_t, ffn_sum=ffn_sum)
-    sync()
-
-    tok_three = v["tok_three"] + [z_down(v["tokens_low"][1])]
-    there = [y_swap(summed([s[1], far])) for s, far in zip(v["sums"], v["far_t"])]
-    v.update(tok_one=tok_one, there=there, far_h=far_h)
-    sync()
-
-    parts = [summed([s[0], far, t]) for s, far, t in zip(v["sums"], v["far_h"], v["there"])]
+    v.update(sums=sums[:2], far_t=far_t, ffn_sum=ffn_sum, tok_one=tok_one)
+    sync()
+
+    tok_three.append(z_down(v["tokens_low"][1]))
+    there = y_swap(summed([v["sums"][1], v["far_t"]]))
+    ffn_other = y_swap(v["ffn_sum"])
+    v.update(tok_three=tok_three, there=there, far_h=far_h)
+    sync()
+
+    parts = summed([v["sums"][0], v["far_h"], v["there"]])
+    parts = [parts[k * rows : (k + 1) * rows] for k in range(4)]
     parts = [parts[0], z_down(parts[1]), z_far(parts[2]), z_up(parts[3])]
-    ffn_other = y_swap(v["ffn_sum"])
     tok_two = [z_up(v["tok_one"][0])]
-    v.update(parts=parts, tok_three=tok_three, ffn_other=ffn_other)
+    v.update(parts=parts, ffn_other=ffn_other, tok_two=tok_two)
     sync()
 
     attn_sum = summed(v["parts"], None, F32)
     attn_other = y_swap(attn_sum)
-    tok_two.append(z_up(v["tok_one"][1]))
+    tok_two = v["tok_two"] + [z_up(v["tok_one"][1])]
 
     def spread(own, one, two, three, dtype):
         out = jnp.zeros((rows_dev, tok, width), dtype)

time: 943 us -> 845 us (0.90)
  Pallas kernels: 464 us -> 345 us
  local copies, waits for them, and re-layouts: 58.6 us -> 121 us
  starting transfers between devices: 143 us -> 114 us
  waiting for transfers between devices: 232 us -> 216 us
    ppermute x12, waiting for transfers between devices: 6.81 us -> 81.7 us  [z_down(): return lax.ppermute(v, 'tp', Z_DOWN)]
    unnamed x197 -> x212, local copies, waits for them, and re-layouts: 14.5 us -> 71 us
    ppermute x21 -> x18, waiting for transfers between devices: 70.4 us -> 25.5 us  [y_swap(): return lax.ppermute(v, 'ctx', Y_SWAP)]
    pallas_call x12 -> x9, Pallas kernels: 92.3 us -> 53.2 us  [the longest x4 16 us: project(): pl.pallas_call(functools.partial(proj_kernel, heads, block, plan, len(pie...]
    ppermute x16 -> x15, waiting for transfers between devices: 70.9 us -> 35.5 us  [z_up(): return lax.ppermute(v, 'tp', Z_UP)]
    pallas_call x8 -> x5, Pallas kernels: 59.9 us -> 25.2 us  [core_sum(): pl.pallas_call(core_sum_kernel, grid_spec=pltpu.PrefetchScalarGridSpec(nu...]
    ppermute x3, waiting for transfers between devices: 43 us -> 13.7 us  [z_far(): return lax.ppermute(v, 'tp', Z_FAR)]
    ppermute x32 -> x20, waiting for transfers between devices: 29.5 us -> 49.3 us  [x_swap(): return lax.ppermute(v, 'fsdp', X_SWAP)]
  transfers between devices with their start and end apart: 132 -> 97, of which waited for: 43 -> 28; matrix products, arithmetic and copies ran while one was open for 8% -> 9% of each run, Pallas kernels for 44% -> 37%
where the time goes in v7:
time: 845 us; the launch traced here: 831 us
  Pallas kernels  345 us (41%)
  waiting for transfers between devices  216 us (26%)
  local copies, waits for them, and re-layouts  121 us (14%)
  starting transfers between devices  114 us (13%)
  other arithmetic  28.3 us (3%)
    pallas_call x4, Pallas kernels, ffn_bwd(): pl.pallas_call(functools.partial(ffn_bwd_kernel, steps, plan, first), gri...  103 us
    ppermute x12, waiting for transfers between devices, z_down(): return lax.ppermute(v, 'tp', Z_DOWN)  81.7 us
    unnamed x212, local copies, waits for them, and re-layouts  71 us
    pallas_call x3, Pallas kernels, ffn_fwd(): pl.pallas_call(functools.partial(ffn_fwd_kernel, tile, [plan for plan, _...  60.3 us
    ppermute x20, waiting for transfers between devices, x_swap(): return lax.ppermute(v, 'fsdp', X_SWAP)  49.3 us
    pallas_call x2, Pallas kernels, attn_bwd(): pl.pallas_call(functools.partial(attn_bwd_kernel, width, hd), grid_spec=p...  37.1 us
    ppermute x15, waiting for transfers between devices, z_up(): return lax.ppermute(v, 'tp', Z_UP)  35.5 us
    ppermute x15, starting transfers between devices, z_up(): return lax.ppermute(v, 'tp', Z_UP)  34.6 us
  transfers between devices with their start and end apart: 97, of which 28 were waited for; matrix products, arithmetic and copies ran while one was open for 9% of the time, Pallas kernels for 37%

profile of v7, /device:TPU:0, one launch (start us, length us, event | category | flops | bytes accessed | tf_op | source)
XLA Modules:
  0.0 830.5 jit_solution(15572355304462047946)
XLA Ops:
  77.8 10.7 %collective-permute-done.11.rest_1_ = bf16[256,3456]{1,0:T(8,128)(2,1)} collective-permute-done((bf16[256,3456]{1,0:T(8,128)(2,1)}, bf16[256,3456]{1,0:T(8,128)(2,1)}, u32[]{:S(2)}, u32[]{:S(2)}) %collective-permute-start.11) | collective-permute-done | bytes 1769504 | tf_op jit(solution)/shard_map/ppermute | solution.py:1529
  99.3 15.8 %attn_fwd.2 = (bf16[1024,256]{1,0:T(8,128)(2,1)}, bf16[1024,256]{1,0:T(8,128)(2,1)}, f32[2,2,2048]{2,1,0:T(2,128)}) custom-call(s32[4]{0:T(128)} %copy-done.45, bf16[512,1024]{1,0:T(8,128)(2,1)} %copy-done.57, bf16[512,1024]{1,0:T(8,128)(2,1)} %copy-done.96), custom_call_target="tpu_custom_call" | custom-call | flops 4398046511104 | bytes 1073741824 | tf_op jit(solution)/shard_map/attn_fwd/pallas_call | solution.py:747
  123.7 15.7 %attn_fwd.3 = (bf16[1024,256]{1,0:T(8,128)(2,1)}, bf16[1024,256]{1,0:T(8,128)(2,1)}, f32[2,2,2048]{2,1,0:T(2,128)}) custom-call(s32[4]{0:T(128)} %copy-done.45, bf16[512,1024]{1,0:T(8,128)(2,1)} %copy-done.56, bf16[512,1024]{1,0:T(8,128)(2,1)} %collective-permute-done.17.got_ref), custom_call_target="tpu_custom_call" | custom-call | flops 4398046511104 | bytes 1073741824 | tf_op jit(solution)/shard_map/attn_fwd/pallas_call | solution.py:747
  146.5 12.2 %collective-permute-done.27.refs_8_ = bf16[1024,256]{1,0:T(8,128)(2,1)S(1)} collective-permute-done((bf16[1024,256]{1,0:T(8,128)(2,1)}, bf16[1024,256]{1,0:T(8,128)(2,1)S(1)}, u32[]{:S(2)}, u32[]{:S(2)}) %collective-permute-start.27) | collective-permute-done | bytes 524320 | tf_op jit(solution)/shard_map/ppermute | solution.py:1535
  196.2 25.6 %ffn_fwd.3 = (bf16[2,1024,2304]{2,1,0:T(8,128)(2,1)}, bf16[2,1024,1152]{2,1,0:T(8,128)(2,1)}, f32[1024,1024]{1,0:T(8,128)}) custom-call(s32[4]{0:T(128)} %copy-done.45, f32[1]{0:T(128)} %bitcast.4.scale, bf16[1024,1024]{1,0:T(8,128)(2,1)} %copy-done.69, f32[1024,1024]{1,0:T(8,128)} %copy-done.64, bf16[256,3456]{1,0:T(8,128)(2,1)} %get-tuple-element.2007.rest_0_, ...), custom_call_target="tpu_custom_call" | custom-call | flops 4398046511104 | bytes 1073741824 | tf_op jit(solution)/shard_map/ffn_fwd/pallas_call | solution.py:1272
  230.4 15.2 %ffn_fwd.4 = (bf16[1,1024,2304]{2,1,0:T(8,128)(2,1)}, bf16[1,1024,1152]{2,1,0:T(8,128)(2,1)}, f32[1024,1024]{1,0:T(8,128)}) custom-call(s32[4]{0:T(128)} %copy-done.45, f32[1]{0:T(128)} %bitcast.4.scale, bf16[1024,1024]{1,0:T(8,128)(2,1)} %copy-done.69, f32[1024,1024]{1,0:T(8,128)} %get-tuple-element.1577.in_ref, ...), custom_call_target="tpu_custom_call" | custom-call | flops 4398046511104 | bytes 1073741824 | tf_op jit(solution)/shard_map/ffn_fwd/pallas_call | solution.py:1272
  248.9 19.4 %ffn_fwd.5 = (bf16[1,1024,2304]{2,1,0:T(8,128)(2,1)}, bf16[1,1024,1152]{2,1,0:T(8,128)(2,1)}, bf16[512,1024]{1,0:T(8,128)(2,1)}, bf16[512,1024]{1,0:T(8,128)(2,1...) custom-call(s32[4]{0:T(128)} %copy-done.45, ...), custom_call_target="tpu_custom_call" | custom-call | flops 4398046511104 | bytes 1073741824 | tf_op jit(solution)/shard_map/ffn_fwd/pallas_call | solution.py:1272
  268.6 25.4 %ffn_bwd.4 = (f32[1024,1024]{1,0:T(8,128)}, bf16[512,3456]{1,0:T(8,128)(2,1)}, bf16[512,3456]{1,0:T(8,128)(2,1)}) custom-call(bf16[1024,1024]{1,0:T(8,128)(2,1)} %get-tuple-element.2002.low_ref, bf16[1,1024,2304]{2,1,0:T(8,128)(2,1)} %get-tuple-element.1752.act_ref, bf16[1,1024,1152]{2,1,0:T(8,128)(2,1)} %get-tuple-element.1769.hid_ref, ...), custom_call_target="tpu_custom_call" | custom-call | flops 4398046511104 | bytes 1073741824 | tf_op jit(solution)/shard_map/ffn_bwd/pallas_call | solution.py:1359
  296.1 25.9 %ffn_bwd.5 = (f32[1024,1024]{1,0:T(8,128)}, bf16[512,3456]{1,0:T(8,128)(2,1)}, bf16[512,3456]{1,0:T(8,128)(2,1)}) custom-call(bf16[1024,1024]{1,0:T(8,128)(2,1)} %get-tuple-element.2002.low_ref, bf16[2,1024,2304]{2,1,0:T(8,128)(2,1)} %get-tuple-element.1986.act_ref, ...), custom_call_target="tpu_custom_call", output_to_operand_aliasing={{0}: (13, {})} | custom-call | flops 4398046511104 | bytes 1073741824 | tf_op jit(solution)/shard_map/ffn_bwd/pallas_call | solution.py:1359
  336.7 25.9 %ffn_bwd.6 = (f32[1024,1024]{1,0:T(8,128)}, bf16[512,3456]{1,0:T(8,128)(2,1)}, bf16[512,3456]{1,0:T(8,128)(2,1)}) custom-call(bf16[1024,1024]{1,0:T(8,128)(2,1)} %get-tuple-element.2002.low_ref, bf16[1,1024,2304]{2,1,0:T(8,128)(2,1)} %get-tuple-element.1911.act_ref, ...), custom_call_target="tpu_custom_call", output_to_operand_aliasing={{0}: (14, {})} | custom-call | flops 4398046511104 | bytes 1073741824 | tf_op jit(solution)/shard_map/ffn_bwd/pallas_call | solution.py:1359
  379.8 25.9 %ffn_bwd.7 = (f32[1024,1024]{1,0:T(8,128)}, bf16[512,3456]{1,0:T(8,128)(2,1)}, bf16[512,3456]{1,0:T(8,128)(2,1)}) custom-call(bf16[1024,1024]{1,0:T(8,128)(2,1)} %get-tuple-element.2002.low_ref, bf16[2,1024,2304]{2,1,0:T(8,128)(2,1)} %get-tuple-element.1986.act_ref, ...), custom_call_target="tpu_custom_call", output_to_operand_aliasing={{0}: (9, {})} | custom-call | flops 4398046511104 | bytes 1073741824 | tf_op jit(solution)/shard_map/ffn_bwd/pallas_call | solution.py:1359
  434.4 12.7 %collective-permute-done.61.gs_ref = bf16[1024,256]{1,0:T(8,128)(2,1)S(1)} collective-permute-done((bf16[1024,256]{1,0:T(8,128)(2,1)S(1)}, bf16[1024,256]{1,0:T(8,128)(2,1)S(1)}, u32[]{:S(2)}, u32[]{:S(2)}) %collective-permute-start.61) | collective-permute-done | bytes 524320 | tf_op jit(solution)/shard_map/ppermute | solution.py:1535
  464.2 18.5 %attn_bwd.2 = (bf16[512,1024]{1,0:T(8,128)(2,1)}, bf16[512,1024]{1,0:T(8,128)(2,1)}) custom-call(s32[4]{0:T(128)} %copy-done.45, bf16[512,1024]{1,0:T(8,128)(2,1)} %copy-done.57, bf16[512,1024]{1,0:T(8,128)(2,1)} %copy-done.96, bf16[1024,256]{1,0:T(8,128)(2,1)} %get-tuple-element.2127.refs_5_.ok_ref, bf16[1024,256]{1,0:T(8,128)(2,1)} %get-tuple-element.2128.os_ref, ...), custom_call_target="tpu_custom_call" | custom-call | flops 4398046511104 | bytes 1073741824 | tf_op jit(solution)/shard_map/attn_bwd/pallas_call | solution.py:901
  485.0 16.1 %collective-permute-done.63.refs_1_ = bf16[128,3456]{1,0:T(8,128)(2,1)} collective-permute-done((bf16[128,3456]{1,0:T(8,128)(2,1)}, bf16[128,3456]{1,0:T(8,128)(2,1)}, u32[]{:S(2)}, u32[]{:S(2)}) %collective-permute-start.63) | collective-permute-done | bytes 884768 | tf_op jit(solution)/shard_map/ppermute | solution.py:1529
  513.3 18.6 %attn_bwd.3 = (bf16[512,1024]{1,0:T(8,128)(2,1)}, bf16[512,1024]{1,0:T(8,128)(2,1)}) custom-call(s32[4]{0:T(128)} %copy-done.45, bf16[512,1024]{1,0:T(8,128)(2,1)} %copy-done.56, bf16[512,1024]{1,0:T(8,128)(2,1)} %collective-permute-done.17.got_ref, bf16[1024,256]{1,0:T(8,128)(2,1)} %get-tuple-element.2192.refs_6_.ok_ref, ...), custom_call_target="tpu_custom_call" | custom-call | flops 4398046511104 | bytes 1073741824 | tf_op jit(solution)/shard_map/attn_bwd/pallas_call | solution.py:901
  534.1 14.8 %collective-permute-done.68.refs_1_ = bf16[128,3456]{1,0:T(8,128)(2,1)} collective-permute-done((bf16[128,3456]{1,0:T(8,128)(2,1)}, bf16[128,3456]{1,0:T(8,128)(2,1)}, u32[]{:S(2)}, u32[]{:S(2)}) %collective-permute-start.68) | collective-permute-done | bytes 884768 | tf_op jit(solution)/shard_map/ppermute | solution.py:1529
  570.3 18.3 %collective-permute-done.73.refs_1_ = bf16[128,3456]{1,0:T(8,128)(2,1)} collective-permute-done((bf16[128,3456]{1,0:T(8,128)(2,1)}, bf16[128,3456]{1,0:T(8,128)(2,1)}, u32[]{:S(2)}, u32[]{:S(2)}) %collective-permute-start.73) | collective-permute-done | bytes 884768 | tf_op jit(solution)/shard_map/ppermute | solution.py:1544
  596.3 10.8 %norm_one_back.1 = (bf16[512,1024]{1,0:T(8,128)(2,1)}, bf16[512,1024]{1,0:T(8,128)(2,1)S(1)}, f32[1,1024]{1,0:T(1,128)S(1)}) custom-call(s32[4]{0:T(128)S(1)} %copy-done.48, bf16[256,512]{1,0:T(8,128)(2,1)S(1)} %join.1.refs_0_, bf16[256,512]{1,0:T(8,128)(2,1)} %collective-permute-done.2.refs_1_, bf16[768,512]{1,0:T(8,128)(2,1)S(1)} %pad_maximum_fusion.3.refs_2_, ...), custom_call_target="tpu_custom_call" | custom-call | flops 4398046511104 | bytes 1073741824 | tf_op jit(solution)/shard_map/norm_one_back/pallas_call | solution.py:1085
  635.7 16.3 %collective-permute-done.81 = bf16[512,1024]{1,0:T(8,128)(2,1)} collective-permute-done((bf16[512,1024]{1,0:T(8,128)(2,1)S(1)}, bf16[512,1024]{1,0:T(8,128)(2,1)}, u32[]{:S(2)}, u32[]{:S(2)}) %collective-permute-start.81) | collective-permute-done | bytes 1048608 | tf_op jit(solution)/shard_map/ppermute | solution.py:1538
  654.5 19.6 %collective-permute-done.83 = bf16[512,1024]{1,0:T(8,128)(2,1)S(1)} collective-permute-done((bf16[512,1024]{1,0:T(8,128)(2,1)}, bf16[512,1024]{1,0:T(8,128)(2,1)S(1)}, u32[]{:S(2)}, u32[]{:S(2)}) %collective-permute-start.83) | collective-permute-done | bytes 1048608 | tf_op jit(solution)/shard_map/ppermute | solution.py:1544
  674.1 22.4 %collective-permute-done.84 = bf16[512,1024]{1,0:T(8,128)(2,1)S(1)} collective-permute-done((bf16[512,1024]{1,0:T(8,128)(2,1)S(1)}, bf16[512,1024]{1,0:T(8,128)(2,1)S(1)}, u32[]{:S(2)}, u32[]{:S(2)}) %collective-permute-start.84) | collective-permute-done | bytes 1048608 | tf_op jit(solution)/shard_map/ppermute | solution.py:1544
  696.5 11.2 %collective-permute-start.89 = (bf16[512,1024]{1,0:T(8,128)(2,1)}, bf16[512,1024]{1,0:T(8,128)(2,1)}, u32[]{:S(2)}, u32[]{:S(2)}) collective-permute-start(bf16[512,1024]{1,0:T(8,128)(2,1)} %collective-permute-done.77), channel_id=1, source_target_pairs={{0,1},{1,2},{2,3},{3,0},{4,5},{5,6},{6,7},{7,4},{8,9},{9,10},{10,1... | collective-permute-start | bytes 3145736 | tf_op jit(solution)/shard_map/ppermute | solution.py:1538
  714.2 21.4 %collective-permute-done.86.refs_1_ = bf16[128,768]{1,0:T(8,128)(2,1)S(1)} collective-permute-done((bf16[128,768]{1,0:T(8,128)(2,1)S(1)}, bf16[128,768]{1,0:T(8,128)(2,1)S(1)}, u32[]{:S(2)}, u32[]{:S(2)}) %collective-permute-start.86) | collective-permute-done | bytes 196640 | tf_op jit(solution)/shard_map/ppermute | solution.py:1544
  735.6 12.3 %collective-permute-done.87.refs_2_ = bf16[128,768]{1,0:T(8,128)(2,1)S(1)} collective-permute-done((bf16[128,768]{1,0:T(8,128)(2,1)S(1)}, bf16[128,768]{1,0:T(8,128)(2,1)S(1)}, u32[]{:S(2)}, u32[]{:S(2)}) %collective-permute-start.87) | collective-permute-done | bytes 196640 | tf_op jit(solution)/shard_map/ppermute | solution.py:1541
  (509 shorter events, 393.3 us)
Async XLA Ops:
  47.6 40.8 %collective-permute-start.11 = (bf16[256,3456]{1,0:T(8,128)(2,1)}, bf16[256,3456]{1,0:T(8,128)(2,1)}, u32[]{:S(2)}, u32[]{:S(2)}) collective-permute-start(bf16[256,3456]{1,0:T(8,128)(2,1)} %get-tuple-element.2007.rest_0_), channel_id=1, source_target_pairs={{0,16},{16,0},{8,24},{24,8},{1,17},{17,1},{9,25},{25,9},{2,18},{18... | collective-permute-start | bytes 5308424 | tf_op jit(solution)/shard_map/ppermute | solution.py:1529
  48.5 44.1 %collective-permute-start.12 = (bf16[256,3456]{1,0:T(8,128)(2,1)}, bf16[256,3456]{1,0:T(8,128)(2,1)}, u32[]{:S(2)}, u32[]{:S(2)}) collective-permute-start(bf16[256,3456]{1,0:T(8,128)(2,1)} %get-tuple-element.2007.rest_0_), channel_id=1, source_target_pairs={{0,1},{1,2},{2,3},{3,0},{4,5},{5,6},{6,7},{7,4},{8,9},{9,10},{10,1... | collective-permute-start | bytes 5308424 | tf_op jit(solution)/shard_map/ppermute | solution.py:1538
  67.5 48.5 %collective-permute-start.17 = (bf16[512,1024]{1,0:T(8,128)(2,1)}, bf16[512,1024]{1,0:T(8,128)(2,1)}, u32[]{:S(2)}, u32[]{:S(2)}) collective-permute-start(bf16[512,1024]{1,0:T(8,128)(2,1)} %get-tuple-element.1268), channel_id=1, source_target_pairs={{0,4},{4,0},{1,5},{5,1},{2,6},{6,2},{3,7},{7,3},{8,12},{12,8},{9,1... | collective-permute-start | bytes 3145736 | tf_op jit(solution)/shard_map/ppermute | solution.py:1535
  180.3 41.5 %collective-permute-start.38 = (bf16[512,1152]{1,0:T(8,128)(2,1)}, bf16[512,1152]{1,0:T(8,128)(2,1)}, u32[]{:S(2)}, u32[]{:S(2)}) collective-permute-start(bf16[512,1152]{1,0:T(8,128)(2,1)} %pad_maximum_fusion), channel_id=1, source_target_pairs={{0,16},{16,0},{8,24},{24,8},{1,17},{17,1},{9,25},{25,9},{2,18},{18... | collective-permute-start | bytes 3538952 | tf_op jit(solution)/shard_map/ppermute | solution.py:1529
  185.8 36.0 %collective-permute-start.39 = (bf16[256,1152]{1,0:T(8,128)(2,1)}, bf16[256,1152]{1,0:T(8,128)(2,1)}, u32[]{:S(2)}, u32[]{:S(2)}) collective-permute-start(bf16[256,1152]{1,0:T(8,128)(2,1)} %collective-permute-done.34.rest_3_), channel_id=1, source_target_pairs={{0,4},{4,0},{1,5},{5,1},{2,6},{6,2},{3,7},{7,3},{8,12},{12,8},{9,1... | collective-permute-start | bytes 1769480 | tf_op jit(solution)/shard_map/ppermute | solution.py:1535
  366.1 39.7 %collective-permute-start.57 = (bf16[128,3456]{1,0:T(8,128)(2,1)}, bf16[128,3456]{1,0:T(8,128)(2,1)}, u32[]{:S(2)}, u32[]{:S(2)}) collective-permute-start(bf16[128,3456]{1,0:T(8,128)(2,1)} %summed.12), channel_id=1, source_target_pairs={{0,4},{4,0},{1,5},{5,1},{2,6},{6,2},{3,7},{7,3},{8,12},{12,8},{9,1... | collective-permute-start | bytes 2654216 | tf_op jit(solution)/shard_map/ppermute | solution.py:1535
  432.9 49.8 %collective-permute-start.64 = (bf16[1024,256]{1,0:T(8,128)(2,1)}, bf16[1024,256]{1,0:T(8,128)(2,1)}, u32[]{:S(2)}, u32[]{:S(2)}) collective-permute-start(bf16[1024,256]{1,0:T(8,128)(2,1)} %get-tuple-element.2149), channel_id=1, source_target_pairs={{0,4},{4,0},{1,5},{5,1},{2,6},{6,2},{3,7},{7,3},{8,12},{12,8},{9,1... | collective-permute-start | bytes 1572872 | tf_op jit(solution)/shard_map/ppermute | solution.py:1535
  460.3 40.8 %collective-permute-start.65 = (bf16[512,1024]{1,0:T(8,128)(2,1)}, bf16[512,1024]{1,0:T(8,128)(2,1)}, u32[]{:S(2)}, u32[]{:S(2)}) collective-permute-start(bf16[512,1024]{1,0:T(8,128)(2,1)} %collective-permute-done.48), channel_id=1, source_target_pairs={{0,1},{1,2},{2,3},{3,0},{4,5},{5,6},{6,7},{7,4},{8,9},{9,10},{10,1... | collective-permute-start | bytes 3145736 | tf_op jit(solution)/shard_map/ppermute | solution.py:1538
  462.8 38.3 %collective-permute-start.63 = (bf16[128,3456]{1,0:T(8,128)(2,1)}, bf16[128,3456]{1,0:T(8,128)(2,1)}, u32[]{:S(2)}, u32[]{:S(2)}) collective-permute-start(bf16[128,3456]{1,0:T(8,128)(2,1)} %bitcast.22), channel_id=1, source_target_pairs={{0,16},{16,0},{8,24},{24,8},{1,17},{17,1},{9,25},{25,9},{2,18},{18... | collective-permute-start | bytes 2654216 | tf_op jit(solution)/shard_map/ppermute | solution.py:1529
  509.3 39.7 %collective-permute-start.69 = (bf16[512,1024]{1,0:T(8,128)(2,1)}, bf16[512,1024]{1,0:T(8,128)(2,1)}, u32[]{:S(2)}, u32[]{:S(2)}) collective-permute-start(bf16[512,1024]{1,0:T(8,128)(2,1)} %get-tuple-element.2189), channel_id=1, source_target_pairs={{0,4},{4,0},{1,5},{5,1},{2,6},{6,2},{3,7},{7,3},{8,12},{12,8},{9,1... | collective-permute-start | bytes 3145736 | tf_op jit(solution)/shard_map/ppermute | solution.py:1535
  509.8 39.2 %collective-permute-start.70 = (bf16[512,1024]{1,0:T(8,128)(2,1)}, bf16[512,1024]{1,0:T(8,128)(2,1)}, u32[]{:S(2)}, u32[]{:S(2)}) collective-permute-start(bf16[512,1024]{1,0:T(8,128)(2,1)} %collective-permute-done.50), channel_id=1, source_target_pairs={{0,1},{1,2},{2,3},{3,0},{4,5},{5,6},{6,7},{7,4},{8,9},{9,10},{10,1... | collective-permute-start | bytes 3145736 | tf_op jit(solution)/shard_map/ppermute | solution.py:1538
  511.7 37.3 %collective-permute-start.68 = (bf16[128,3456]{1,0:T(8,128)(2,1)}, bf16[128,3456]{1,0:T(8,128)(2,1)}, u32[]{:S(2)}, u32[]{:S(2)}) collective-permute-start(bf16[128,3456]{1,0:T(8,128)(2,1)} %bitcast.28), channel_id=1, source_target_pairs={{0,16},{16,0},{8,24},{24,8},{1,17},{17,1},{9,25},{25,9},{2,18},{18... | collective-permute-start | bytes 2654216 | tf_op jit(solution)/shard_map/ppermute | solution.py:1529
  549.0 39.6 %collective-permute-start.72 = (bf16[512,1024]{1,0:T(8,128)(2,1)}, bf16[512,1024]{1,0:T(8,128)(2,1)}, u32[]{:S(2)}, u32[]{:S(2)}) collective-permute-start(bf16[512,1024]{1,0:T(8,128)(2,1)} %get-tuple-element.2246), channel_id=1, source_target_pairs={{0,4},{4,0},{1,5},{5,1},{2,6},{6,2},{3,7},{7,3},{8,12},{12,8},{9,1... | collective-permute-start | bytes 3145736 | tf_op jit(solution)/shard_map/ppermute | solution.py:1535
  550.5 38.1 %collective-permute-start.73 = (bf16[128,3456]{1,0:T(8,128)(2,1)}, bf16[128,3456]{1,0:T(8,128)(2,1)}, u32[]{:S(2)}, u32[]{:S(2)}) collective-permute-start(bf16[128,3456]{1,0:T(8,128)(2,1)} %copy-done.37), channel_id=1, source_target_pairs={{0,3},{1,0},{2,1},{3,2},{4,7},{5,4},{6,5},{7,6},{8,11},{9,8},{10,9... | collective-permute-start | bytes 2654216 | tf_op jit(solution)/shard_map/ppermute | solution.py:1544
  559.5 47.6 %collective-permute-start.74 = (bf16[128,3456]{1,0:T(8,128)(2,1)}, bf16[128,3456]{1,0:T(8,128)(2,1)}, u32[]{:S(2)}, u32[]{:S(2)}) collective-permute-start(bf16[128,3456]{1,0:T(8,128)(2,1)} %copy-done.26), channel_id=1, source_target_pairs={{0,1},{1,2},{2,3},{3,0},{4,5},{5,6},{6,7},{7,4},{8,9},{9,10},{10,1... | collective-permute-start | bytes 2654216 | tf_op jit(solution)/shard_map/ppermute | solution.py:1538
  559.8 57.2 %collective-permute-start.75 = (bf16[128,3456]{1,0:T(8,128)(2,1)}, bf16[128,3456]{1,0:T(8,128)(2,1)}, u32[]{:S(2)}, u32[]{:S(2)}) collective-permute-start(bf16[128,3456]{1,0:T(8,128)(2,1)} %bitcast.121), channel_id=1, source_target_pairs={{0,16},{16,0},{8,24},{24,8},{1,17},{17,1},{9,25},{25,9},{2,18},{18... | collective-permute-start | bytes 2654216 | tf_op jit(solution)/shard_map/ppermute | solution.py:1529
  632.1 42.0 %collective-permute-start.83 = (bf16[512,1024]{1,0:T(8,128)(2,1)}, bf16[512,1024]{1,0:T(8,128)(2,1)S(1)}, u32[]{:S(2)}, u32[]{:S(2)}) collective-permute-start(bf16[512,1024]{1,0:T(8,128)(2,1)} %get-tuple-element.2443), channel_id=1, source_target_pairs={{0,3},{1,0},{2,1},{3,2},{4,7},{5,4},{6,5},{7,6},{8,11},{9,8},{10,9... | collective-permute-start | bytes 3145736 | tf_op jit(solution)/shard_map/ppermute | solution.py:1544
  652.0 44.5 %collective-permute-start.84 = (bf16[512,1024]{1,0:T(8,128)(2,1)S(1)}, bf16[512,1024]{1,0:T(8,128)(2,1)S(1)}, u32[]{:S(2)}, u32[]{:S(2)}) collective-permute-start(bf16[512,1024]{1,0:T(8,128)(2,1)S(1)} %get-tuple-element.2444), channel_id=1, source_target_pairs={{0,3},{1,0},{2,1},{3,2},{4,7},{5,4},{6,5},{7,6},{8,11},{9,8},{10,9... | collective-permute-start | bytes 3145736 | tf_op jit(solution)/shard_map/ppermute | solution.py:1544
  654.0 93.9 %collective-permute-start.85 = (f32[128,3456]{1,0:T(8,128)S(1)}, f32[128,3456]{1,0:T(8,128)}, u32[]{:S(2)}, u32[]{:S(2)}) collective-permute-start(f32[128,3456]{1,0:T(8,128)S(1)} %summed.20), channel_id=1, source_target_pairs={{0,4},{4,0},{1,5},{5,1},{2,6},{6,2},{3,7},{7,3},{8,12},{12,8},{9,1... | collective-permute-start | bytes 5308424 | tf_op jit(solution)/shard_map/ppermute | solution.py:1535
  696.5 51.4 %collective-permute-start.89 = (bf16[512,1024]{1,0:T(8,128)(2,1)}, bf16[512,1024]{1,0:T(8,128)(2,1)}, u32[]{:S(2)}, u32[]{:S(2)}) collective-permute-start(bf16[512,1024]{1,0:T(8,128)(2,1)} %collective-permute-done.77), channel_id=1, source_target_pairs={{0,1},{1,2},{2,3},{3,0},{4,5},{5,6},{6,7},{7,4},{8,9},{9,10},{10,1... | collective-permute-start | bytes 3145736 | tf_op jit(solution)/shard_map/ppermute | solution.py:1538
  711.6 36.3 %collective-permute-start.87 = (bf16[128,768]{1,0:T(8,128)(2,1)S(1)}, bf16[128,768]{1,0:T(8,128)(2,1)S(1)}, u32[]{:S(2)}, u32[]{:S(2)}) collective-permute-start(bf16[128,768]{1,0:T(8,128)(2,1)S(1)} %get-tuple-element.2503), channel_id=1, source_target_pairs={{0,2},{2,0},{1,3},{3,1},{4,6},{6,4},{5,7},{7,5},{8,10},{10,8},{9,1... | collective-permute-start | bytes 589832 | tf_op jit(solution)/shard_map/ppermute | solution.py:1541
  712.2 35.7 %collective-permute-start.88 = (bf16[128,768]{1,0:T(8,128)(2,1)S(1)}, bf16[128,768]{1,0:T(8,128)(2,1)S(1)}, u32[]{:S(2)}, u32[]{:S(2)}) collective-permute-start(bf16[128,768]{1,0:T(8,128)(2,1)S(1)} %get-tuple-element.2502), channel_id=1, source_target_pairs={{0,1},{1,2},{2,3},{3,0},{4,5},{5,6},{6,7},{7,4},{8,9},{9,10},{10,1... | collective-permute-start | bytes 589832 | tf_op jit(solution)/shard_map/ppermute | solution.py:1538
  758.2 64.7 %collective-permute-start.96 = (f32[128,768]{1,0:T(8,128)S(1)}, f32[128,768]{1,0:T(8,128)}, u32[]{:S(2)}, u32[]{:S(2)}) collective-permute-start(f32[128,768]{1,0:T(8,128)S(1)} %summed.23), channel_id=1, source_target_pairs={{0,4},{4,0},{1,5},{5,1},{2,6},{6,2},{3,7},{7,3},{8,12},{12,8},{9,1... | collective-permute-start | bytes 1179656 | tf_op jit(solution)/shard_map/ppermute | solution.py:1535
  758.3 67.8 %collective-permute-start.95 = (bf16[512,1024]{1,0:T(8,128)(2,1)}, bf16[512,1024]{1,0:T(8,128)(2,1)}, u32[]{:S(2)}, u32[]{:S(2)}) collective-permute-start(bf16[512,1024]{1,0:T(8,128)(2,1)} %collective-permute-done.81), channel_id=1, source_target_pairs={{0,1},{1,2},{2,3},{3,0},{4,5},{5,6},{6,7},{7,4},{8,9},{9,10},{10,1... | collective-permute-start | bytes 3145736 | tf_op jit(solution)/shard_map/ppermute | solution.py:1538
  (171 other events, 2447.2 us)

commit v8 on v7

--- a/solution.py
+++ b/solution.py
@@ -412,7 +412,8 @@
     return pl.CostEstimate(flops=size, bytes_accessed=size >> 12, transcendentals=0)
 
 
-def pack_kernel(info, o_in, g_in, u_in, d_in, out_ref, ffn_ref, o_ref, g_ref, u_ref, d_ref, sems):
+def pack_kernel(info, o_in, g_in, u_in, d_in, *refs):
+    out_ref, ffn_ref, first_ref, second_ref, third_ref, o_ref, g_ref, u_ref, d_ref, sems = refs
     ctx = info[2]
     pairs = ((o_in, o_ref), (g_in, g_ref), (u_in, u_ref), (d_in, d_ref))
     copies = [pltpu.make_async_copy(a, b, sems.at[i]) for i, (a, b) in enumerate(pairs)]
@@ -420,24 +421,31 @@
         copy.start()
     for copy in copies:
         copy.wait()
-    out_ref[...] = o_ref[...].astype(F32).T.astype(BF16)
+    o_t = o_ref[...].astype(F32).T.astype(BF16)
+    out_ref[...] = o_t
     third = g_ref.shape[1] // 3
-    for j in range(3):
+    first_ref[:, 3 * third :] = o_t
+    for j, chunk in enumerate((first_ref, second_ref, third_ref)):
         at = pl.multiple_of(jnp.where(ctx == 0, j, 2 - j) * third, third)
-        base = 3 * third * j
-        ffn_ref[:, base : base + third] = g_ref[:, pl.ds(at, third)]
-        ffn_ref[:, base + third : base + 2 * third] = u_ref[:, pl.ds(at, third)]
-        down = d_ref[pl.ds(at, third), :].astype(F32).T.astype(BF16)
-        ffn_ref[:, base + 2 * third : base + 3 * third] = down
+        parts = [
+            g_ref[:, pl.ds(at, third)],
+            u_ref[:, pl.ds(at, third)],
+            d_ref[pl.ds(at, third), :].astype(F32).T.astype(BF16),
+        ]
+        for i, part in enumerate(parts):
+            chunk[:, i * third : (i + 1) * third] = part
+            ffn_ref[:, (3 * j + i) * third : (3 * j + i + 1) * third] = part
 
 
 def pack(info, o, g, u, d):
-    rows = g.shape[0]
+    rows, units = g.shape
+    feats = o.shape[0]
+    widths = (feats, 3 * units, units + feats, units, units)
     return pl.pallas_call(
         pack_kernel,
         in_specs=[SMEM] + [ANY] * 4,
-        out_specs=[pl.BlockSpec(memory_space=pltpu.VMEM)] * 2,
-        out_shape=[shape_of((rows, o.shape[0]), BF16), shape_of((rows, 3 * g.shape[1]), BF16)],
+        out_specs=[pl.BlockSpec(memory_space=pltpu.VMEM)] * 5,
+        out_shape=[shape_of((rows, n), BF16) for n in widths],
         scratch_shapes=[pltpu.VMEM(a.shape, BF16) for a in (o, g, u, d)]
         + [pltpu.SemaphoreType.DMA((4,))],
         compiler_params=pltpu.CompilerParams(vmem_limit_bytes=24 << 20),
@@ -1042,7 +1050,7 @@
 
 
 def norm_one_back_kernel(plan, count, info, *refs):
-    p0, p1, x_ref, gres_ref, gain_ref, outa_ref, outb_ref, gg_ref, w_ref, sem = refs[count:]
+    p0, p1, x_ref, gres_ref, gain_ref, *out_refs, gg_ref, w_ref, sem = refs[count:]
     load_blocks(plan, refs, w_ref, sem)
     quarter = x_ref.shape[1] // 4
     grad = dot(p0[0], w_ref[0], 1, 1)
@@ -1059,13 +1067,11 @@
         at = pl.multiple_of(jnp.bitwise_xor(info[1], mask) * quarter, quarter)
         part = total[:, p * quarter : (p + 1) * quarter]
 
-        @pl.when(pl.program_id(0) < pl.num_programs(0) // 2)
-        def _():
-            outa_ref[:, pl.ds(at, quarter)] = part
-
-        @pl.when(pl.program_id(0) >= pl.num_programs(0) // 2)
-        def _():
-            outb_ref[:, pl.ds(at, quarter)] = part
+        for i, out_ref in enumerate(out_refs):
+
+            @pl.when(pl.program_id(0) == i)
+            def _():
+                out_ref[:, pl.ds(at, quarter)] = part
 
     @pl.when(pl.program_id(0) == 0)
     def _():
@@ -1080,7 +1086,6 @@
     cols = pieces[0].shape[1]
     rows_of = lambda n: pl.BlockSpec((tile, n), lambda i, info: (i, 0))
     pair = pl.BlockSpec((2, tile, cols), lambda i, info: (0, i, 0))
-    half = tok // tile // 2
     row = pl.BlockSpec((1, width), lambda i, info: (0, 0))
     return pl.pallas_call(
         functools.partial(norm_one_back_kernel, plan, len(pieces)),
@@ -1088,14 +1093,10 @@
             num_scalar_prefetch=1,
             grid=(tok // tile,),
             in_specs=[ANY] * len(pieces) + [pair, pair, rows_of(width), rows_of(width), row],
-            out_specs=[
-                pl.BlockSpec((tile, width), lambda i, info: (jnp.minimum(i, half - 1), 0)),
-                pl.BlockSpec((tile, width), lambda i, info: (jnp.maximum(i - half, 0), 0)),
-                row,
-            ],
+            out_specs=[pl.BlockSpec((tile, width), lambda i, info: (0, 0))] * 4 + [row],
             scratch_shapes=[pltpu.VMEM((4, width, cols), BF16), pltpu.SemaphoreType.DMA],
         ),
-        out_shape=[shape_of((tok // 2, width), BF16)] * 2 + [shape_of((1, width), F32)],
+        out_shape=[shape_of((tile, width), BF16)] * 4 + [shape_of((1, width), F32)],
         compiler_params=settings(1, 32),
         cost_estimate=cost(True),
         name="norm_one_back",
@@ -1543,9 +1544,6 @@
     def z_down(v):
         return lax.ppermute(v, "tp", Z_DOWN)
 
-    def chunks(block):
-        return [block[:, j * units : (j + 1) * units] for j in range(3)]
-
     def natural(v):
         v = jnp.concatenate([v[0:1], v[2:3], v[1:2], v[3:4]], axis=0)
         v = jnp.where(fsdp % 2 == 0, v, jnp.concatenate([v[1:2], v[0:1], v[3:4], v[2:3]], axis=0))
@@ -1566,7 +1564,7 @@
     vector = jnp.concatenate([vector, count_here, jnp.zeros((640 - 545,), F32)])[None]
     vector = jnp.concatenate([vector, x_swap(vector)], axis=0)
     vector = jnp.concatenate([vector, core_swap(vector)], axis=0)
-    w_out, w_ffn = pack(info, o_weight, gate_weight, up_weight, down_weight)
+    w_out, w_ffn, *w_chunks = pack(info, o_weight, gate_weight, up_weight, down_weight)
     pos = (ctx * tok + jnp.arange(tok, dtype=jnp.int32)).astype(F32)
     frequency = THETA ** (-(2.0 * jnp.arange(hd // 2, dtype=F32)) / hd)
     angles = frequency[:, None] * pos[None, :]
@@ -1578,6 +1576,7 @@
         proj_z=jnp.concatenate(proj_z, axis=0),
         w_out=w_out,
         w_ffn=w_ffn,
+        w_chunks=w_chunks,
         gain_one=vector[:, :quarter].reshape(1, width),
         gain_two=vector[:, quarter : 2 * quarter].reshape(1, width),
         total_count=jnp.sum(vector[:, 544]),
@@ -1590,20 +1589,25 @@
     info = v["info"]
 
     proj_zfar = x_swap(v["proj_z"])
-    out_z = [z_up(v["w_out"]), z_far(v["w_out"]), z_down(v["w_out"])]
-    proj_core = core_swap(v["w_proj"])
+    one = [z_up(v["w_chunks"][0])]
+    out_two = z_far(v["w_out"])
+    proj_cores = [core_swap(v["w_proj"]), core_swap(v["proj_far"])]
     x_in, normed_one_t = norm_one(info, tokens, v["gain_one"], 256)
     v.update(
-        proj_zfar=proj_zfar, proj_core=proj_core, x_in=x_in, normed_one_t=normed_one_t, out_z=out_z
-    )
-    sync()
-
-    proj_cores = [v["proj_core"], core_swap(v["proj_far"])]
-    proj_cores += [core_swap(v["proj_z"]), core_swap(v["proj_zfar"])]
+        proj_zfar=proj_zfar,
+        proj_cores=proj_cores,
+        x_in=x_in,
+        normed_one_t=normed_one_t,
+        one=one,
+        out_two=out_two,
+    )
+    sync()
+
+    proj_cores = v["proj_cores"] + [core_swap(v["proj_z"]), core_swap(v["proj_zfar"])]
     plan_proj = [[(0, 0), (1, 0), (4, 0), (5, 0)]]
     plan_proj += [[(p, k * quarter) for p in (2, 3, 6, 7)] for k in range(3)]
     weights_proj = [v["w_proj"], v["proj_far"], v["proj_z"], v["proj_zfar"]] + proj_cores
-    ffn_one = z_up(v["w_ffn"])
+    one = v["one"] + [z_up(v["w_chunks"][1]), z_up(v["w_chunks"][2])]
     ffn_far = x_swap(v["w_ffn"])
     tables = [v[name] for name in ("cos_part", "sin_part", "gain_q", "gain_k")]
 
@@ -1618,7 +1622,7 @@
     mine = [make(lambda s: 2 * s[2], theirs[1][0])]
     mine.append(make(lambda s: 2 * s[2] + 1, mine[0][0]))
     v.update(
-        ffn_one=ffn_one,
+        one=one,
         ffn_far=ffn_far,
         weights_proj=weights_proj,
         mine=mine,
@@ -1627,42 +1631,54 @@
     )
     sync()
 
-    out_blocks = jnp.concatenate([v["w_out"]] + v["out_z"], axis=0)
-    one_far = [x_swap(chunks(v["ffn_one"])[0])]
-    three = [z_down(chunks(v["w_ffn"])[0])]
+    one_far = [x_swap(v["one"][0])]
+    three = [z_down(v["w_chunks"][0])]
     own_cores = [core_swap(v["w_ffn"]), core_swap(v["ffn_far"])]
     first = attn_fwd(info, v["mine"][0][0], v["got0"], hd)
+    v.update(first=first, got1=got[1], one_far=one_far, three=three, own_cores=own_cores)
+    sync()
+
+    arrived = [y_swap(v["first"][1])]
+    three = v["three"] + [z_down(v["w_chunks"][1])]
+    out_blocks = jnp.concatenate(
+        [v["w_out"], v["one"][0][:, units:], v["out_two"], v["three"][0][:, units:]], axis=0
+    )
+    out_far = x_swap(out_blocks)
+    one_cores = [core_swap(v["one"][0]), core_swap(v["one_far"][0])]
+    second = attn_fwd(info, v["mine"][1][0], v["got1"], hd)
     v.update(
-        first=first,
-        got1=got[1],
-        one_far=one_far,
+        second=second,
+        arrived=arrived,
         three=three,
         out_blocks=out_blocks,
-        own_cores=own_cores,
-    )
-    sync()
-
-    arrived = [y_swap(v["first"][1])]
-    three = v["three"] + [z_down(chunks(v["w_ffn"])[1])]
-    out_far = x_swap(v["out_blocks"])
-    one_cores = [core_swap(v["ffn_one"]), core_swap(v["one_far"][0])]
-    second = attn_fwd(info, v["mine"][1][0], v["got1"], hd)
-    v.update(second=second, arrived=arrived, three=three, out_far=out_far, one_cores=one_cores)
+        out_far=out_far,
+        one_cores=one_cores,
+    )
     sync()
 
     arrived = v["arrived"] + [y_swap(v["second"][1])]
-    three = v["three"] + [z_down(chunks(v["w_ffn"])[2])]
-    one_far = v["one_far"] + [x_swap(chunks(v["ffn_one"])[1])]
+    three = v["three"] + [z_down(v["w_chunks"][2])]
+    one_far = v["one_far"] + [x_swap(v["one"][1])]
     weights_out = [v["out_blocks"], v["out_far"]]
     weights_out += [core_swap(v["out_blocks"]), core_swap(v["out_far"])]
-    v.update(arrived=arrived, three=three, one_far=one_far, weights_out=weights_out)
+    one_cores = v["one_cores"] + [core_swap(v["one"][1])]
+    three_cores = [core_swap(part) for part in v["three"]]
+    v.update(
+        arrived=arrived,
+        three=three,
+        one_far=one_far,
+        weights_out=weights_out,
+        one_cores=one_cores,
+        three_cores=three_cores,
+    )
     sync()
 
     plan_out = [[(p, k * quarter) for p in range(4)] for k in range(4)]
-    two = [z_up(chunks(v["ffn_one"])[0])]
+    two = [z_up(v["one"][0])]
     three_far = [x_swap(v["three"][0])]
-    one_last = y_swap(v["one_far"][0])
+    one_far = v["one_far"] + [y_swap(v["one_far"][0])]
     one_cores = v["one_cores"] + [core_swap(v["one_far"][1])]
+    three_cores = v["three_cores"] + [core_swap(v["three"][2])]
     resid, normed_two, normed_two_t, attended = out_proj(
         info,
         v["x_in"],
@@ -1675,8 +1691,9 @@
     v.update(
         two=two,
         three_far=three_far,
-        one_last=one_last,
+        one_far=one_far,
         one_cores=one_cores,
+        three_cores=three_cores,
         resid=resid,
         normed_two=normed_two,
         normed_two_t=normed_two_t,
@@ -1684,32 +1701,24 @@
     )
     sync()
 
-    in_block = lambda i: [(i, 0, j * units) for j in range(3)]
-    plan0 = [in_block(i) for i in range(4)]
-    plan1 = [in_block(0), [(i, 0, 0) for i in (1, 2, 3)]]
-    plan1 += [in_block(4), [(i, 0, 0) for i in (5, 6, 7)]]
-    plan3 = [[(0, 0, 0), (1, 0, 0), (2, 0, 0)], [(3, 0, 0), (4, 0, 0), (5, 0, 0)]]
-    plan3 += [[(6, j * quarter, 0) for j in range(3)]]
-    plan3 += [[(6, 3 * quarter, 0), (7, 0, 0), (8, 0, 0)]]
-    plan2 = [[(0, 0, 0), (1, 0, 0), (1, 0, units)], [(2, quarter, 0), (3, 0, 0), (4, 0, 0)]]
-    plan2 += [[(5, 4 * quarter, 0), (6, 0, 0), (6, 0, units)]]
-    plan2 += [[(7, quarter, 0), (8, 0, 0), (9, 0, 0)]]
+    plan0 = [[(i, 0, j * units) for j in range(3)] for i in range(4)]
+    plan_chunks = [[(3 * p + j, 0, 0) for j in range(3)] for p in range(4)]
     scale = (slots / v["total_count"])[None]
     weights0 = [v["w_ffn"], v["ffn_far"]] + v["own_cores"]
-    weights1 = [v["ffn_one"]] + v["one_far"] + [v["one_last"]]
-    weights1 += v["one_cores"] + [core_swap(v["one_last"])]
-    two = v["two"] + [z_up(v["ffn_one"][:, units:])]
-    mixed_far = x_swap(jnp.concatenate([v["three"][1], v["two"][0]], axis=0))
-    three_last = y_swap(v["three_far"][0])
-    mixed = jnp.concatenate(v["three"] + [v["three_far"][0], v["two"][0]], axis=0)
-    mixed_core = core_swap(mixed)
+    c0, cf, c1, cb = v["one_cores"]
+    weights1 = v["one"] + v["one_far"] + [c0, c1, core_swap(v["one"][2])]
+    weights1 += [cf, cb, core_swap(v["one_far"][2])]
+    two = v["two"] + [z_up(v["one"][1])]
+    three_far = v["three_far"] + [x_swap(v["three"][1]), y_swap(v["three_far"][0])]
+    two_far = [x_swap(v["two"][0])]
+    three_fars = [core_swap(v["three_far"][0])]
     acts_a, hiddens_a, sum_a = ffn_fwd(
         info,
         scale,
-        after(v["normed_two"], mixed),
+        v["normed_two"],
         v["resid"],
         None,
-        [(plan0, weights0), (plan1, weights1)],
+        [(plan0, weights0), (plan_chunks, weights1)],
         units,
         256,
     )
@@ -1718,41 +1727,38 @@
         weights0=weights0,
         weights1=weights1,
         two=two,
-        mixed_far=mixed_far,
-        three_last=three_last,
-        mixed_core=mixed_core,
+        three_far=three_far,
+        two_far=two_far,
+        three_fars=three_fars,
         acts_a=acts_a,
         hiddens_a=hiddens_a,
         sum_a=sum_a,
     )
     sync()
 
-    far_core = core_swap(v["mixed_far"])
-    weights3 = v["three"] + [v["three_far"][0], v["mixed_far"], v["three_last"]]
-    weights3 += [v["mixed_core"], far_core, core_swap(v["three_last"])]
-    two_far = x_swap(v["two"][1][:, :units])
-    two_last = y_swap(v["mixed_far"][quarter:])
-    two_core = core_swap(v["two"][1])
+    weights3 = v["three"] + v["three_far"] + v["three_cores"] + v["three_fars"]
+    weights3 += [core_swap(part) for part in v["three_far"][1:]]
+    two = v["two"] + [z_up(v["one"][2])]
+    two_far = v["two_far"] + [x_swap(v["two"][1]), y_swap(v["two_far"][0])]
+    two_cores = [core_swap(part) for part in v["two"]]
     acts_b, hiddens_b, sum_b = ffn_fwd(
-        info, v["scale"], v["normed_two"], v["sum_a"], None, [(plan3, weights3)], units, 256
+        info, v["scale"], v["normed_two"], v["sum_a"], None, [(plan_chunks, weights3)], units, 256
     )
     v.update(
         weights3=weights3,
-        far_core=far_core,
+        two=two,
         two_far=two_far,
-        two_last=two_last,
-        two_core=two_core,
+        two_cores=two_cores,
         acts_b=acts_b,
         hiddens_b=hiddens_b,
         sum_b=sum_b,
     )
     sync()
 
-    weights2 = v["two"] + [v["mixed_far"], v["two_far"], v["two_last"]]
-    weights2 += [v["mixed_core"], v["two_core"], v["far_core"]]
-    weights2 += [core_swap(v["two_far"]), core_swap(v["two_last"])]
+    weights2 = v["two"] + v["two_far"] + v["two_cores"]
+    weights2 += [core_swap(part) for part in v["two"][2:] + v["two_far"]]
     acts_c, hiddens_c, *results, grad_result, grad_low, grad_low_t, square = ffn_fwd(
-        info, v["scale"], v["normed_two"], v["sum_b"], teacher, [(plan2, weights2)], units, 256
+        info, v["scale"], v["normed_two"], v["sum_b"], teacher, [(plan_chunks, weights2)], units, 256
     )
     v.update(
         weights2=weights2,
@@ -1782,13 +1788,13 @@
 
     turned = [False, False, True]
     one = [z_up(v["results"][0])]
-    total, keep2, send2 = ffn_back(plan2, "weights2", "acts_c", "hiddens_c", 0, None)
+    total, keep2, send2 = ffn_back(plan_chunks, "weights2", "acts_c", "hiddens_c", 0, None)
     v.update(one=one, total=total, keep2=keep2, send2=send2)
     sync()
 
     one = v["one"] + [z_up(v["results"][1])]
     came2 = core_swap(v["send2"])
-    total, keep1, send1 = ffn_back(plan1, "weights1", "acts_a", "hiddens_a", 1, v["total"])
+    total, keep1, send1 = ffn_back(plan_chunks, "weights1", "acts_a", "hiddens_a", 1, v["total"])
     v.update(one=one, came2=came2, total=total, keep1=keep1, send1=send1)
     sync()
 
@@ -1797,7 +1803,7 @@
     sum2 = sum_of(2)
     far_t2 = x_swap(sum2[3])
     total, keep3, send3 = ffn_back(
-        plan3, "weights3", "acts_b", "hiddens_b", 0, after(v["total"], sum2[0])
+        plan_chunks, "weights3", "acts_b", "hiddens_b", 0, after(v["total"], sum2[0])
     )
     v.update(
         out_three=out_three,
@@ -1917,59 +1923,91 @@
         v["x_in"],
         v["grad_resid"],
         v["gain_one"],
-        256,
+        tok // 4,
     )
     v.update(head1=head1, tokens_low=tokens_low, gain_one_sum=gain_one_sum, up3=up3)
-    sync()
-
-    tok_one = [z_up(v["tokens_low"][0])]
+    v.update(there0=there0, far_h0=far_h0)
+    sync()
+
+    def place(out, parts, k, first):
+        row = lax.rem(z - k + 4, 4)
+        for j, part in enumerate(parts):
+            at = (first + j) * part.shape[0]
+            out = lax.dynamic_update_slice(out, part.astype(out.dtype)[None], (row, at, 0))
+        return out
+
+    v.update(out_one=v["one"])
+    quarters = v["tokens_low"]
+    one = [z_up(quarters[0])]
     keep, send = weight_grad(
         v["normed_one_t"], [v["head0"][0], v["head1"][0]], v["grad_attn_t"], v["attended"]
     )
-    v.update(tok_one=tok_one, keep=keep, send=send, there0=there0, far_h0=far_h0)
-    sync()
-
-    tok_one = v["tok_one"] + [z_up(v["tokens_low"][1])]
-    tok_three = [z_down(v["tokens_low"][0])]
+    gain_heads = v["head0"][1] + v["head1"][1]
+    vector = jnp.concatenate(
+        [
+            natural(v["gain_one_sum"].reshape(4, quarter)).reshape(1, width),
+            natural(v["gain_two_sum"].reshape(4, quarter)).reshape(1, width),
+            gain_heads[:, 0].reshape(1, hd),
+            gain_heads[:, 1].reshape(1, hd),
+            jnp.sum(v["square"]).reshape(1, 1),
+            jnp.zeros((1, 127), F32),
+        ],
+        axis=1,
+    )
+    vector = vector + core_swap(vector)
+    v.update(one=one, keep=keep, came=core_swap(send))
+    v.update(vector=vector)
+    sync()
+
+    one = v["one"] + [z_up(part) for part in v["tokens_low"][1:3]]
     rows = quarter // 2
     flat = lambda a: a.reshape(4 * rows, a.shape[-1])
-    sums = [flat(p) for p in core_sum(info, v["keep"], core_swap(v["send"]))]
+    sums = [flat(p) for p in core_sum(info, v["keep"], v["came"])]
     far_t = x_swap(sums[3])
-    far_h = x_swap(sums[2])
     part0 = summed([v["sum0"][0], v["far_h0"], v["there0"]], turned)
     ffn_sum = summed([part0, v["two_down"], v["up3"]], None, F32)
-    v.update(sums=sums[:2], far_t=far_t, ffn_sum=ffn_sum, tok_one=tok_one)
-    sync()
-
-    tok_three.append(z_down(v["tokens_low"][1]))
+    vector = v["vector"] + x_swap(v["vector"])
+    v.update(one=one, sums=sums, far_t=far_t, ffn_sum=ffn_sum, vector=vector)
+    sync()
+
+    one = v["one"] + [z_up(v["tokens_low"][3])]
+    three = [z_down(v["tokens_low"][0])]
+    far_h = x_swap(v["sums"][2])
     there = y_swap(summed([v["sums"][1], v["far_t"]]))
-    ffn_other = y_swap(v["ffn_sum"])
-    v.update(tok_three=tok_three, there=there, far_h=far_h)
-    sync()
-
+    vector = v["vector"] + y_swap(v["vector"])
+    output = jnp.zeros((rows_dev, tok, width), BF16)
+    for k, parts in enumerate((v["results"], v["out_one"], v["out_two"], v["out_three"])):
+        output = place(output, parts, k, 0)
+    v.update(one=one, three=three, far_h=far_h, there=there, vector=vector, output=output)
+    sync()
+
+    three = v["three"] + [z_down(v["tokens_low"][1])]
     parts = summed([v["sums"][0], v["far_h"], v["there"]])
     parts = [parts[k * rows : (k + 1) * rows] for k in range(4)]
     parts = [parts[0], z_down(parts[1]), z_far(parts[2]), z_up(parts[3])]
-    tok_two = [z_up(v["tok_one"][0])]
-    v.update(parts=parts, ffn_other=ffn_other, tok_two=tok_two)
-    sync()
-
+    ffn_other = y_swap(v["ffn_sum"])
+    grad = place(jnp.zeros((rows_dev, tok, width), F32), v["tokens_low"], 0, 0)
+    v.update(three=three, parts=parts, grad=grad)
+    sync()
+
+    three = v["three"] + [z_down(part) for part in v["tokens_low"][2:]]
     attn_sum = summed(v["parts"], None, F32)
     attn_other = y_swap(attn_sum)
-    tok_two = v["tok_two"] + [z_up(v["tok_one"][1])]
-
-    def spread(own, one, two, three, dtype):
-        out = jnp.zeros((rows_dev, tok, width), dtype)
-        for k, parts in ((0, own), (1, one), (3, three), (2, two)):
-            row = lax.rem(z - k + 4, 4)
-            for j, part in enumerate(parts):
-                out = lax.dynamic_update_slice(
-                    out, part.astype(dtype)[None], (row, j * tok // 2, 0)
-                )
-        return out
-
-    tokens_grad = spread(v["tokens_low"], v["tok_one"], tok_two, v["tok_three"], F32)
-    output = spread(v["results"], v["one"], v["out_two"], v["out_three"], BF16)
+    vector = v["vector"] + lax.ppermute(v["vector"], "tp", Z_NEAR)
+    grad = place(v["grad"], v["one"], 1, 0)
+    v.update(three=three, attn_sum=attn_sum, attn_other=attn_other, vector=vector, grad=grad)
+    sync()
+
+    two = [z_up(part) for part in v["one"][:2]]
+    vector = v["vector"] + lax.ppermute(v["vector"], "tp", Z_FAR)
+    grad = place(v["grad"], v["three"], 3, 0)
+    v.update(two=two, vector=vector, grad=grad, ffn_other=ffn_other)
+    sync()
+
+    two = [z_up(part) for part in v["one"][2:]]
+    tokens_grad = place(place(v["grad"], v["two"], 2, 0), two, 2, 2)
+    output = v["output"]
+    sums = v["vector"][0]
 
     def finish(own, other):
         return jnp.concatenate(
@@ -1977,33 +2015,8 @@
         )
 
     ffn_grad = finish(v["ffn_sum"], turn_chunks(v["ffn_other"]))
-    attn_grad = finish(attn_sum, attn_other)
-
-    def total(v):
-        for axis, pairs in (("fsdp", CORE_SWAP), ("fsdp", X_SWAP), ("ctx", Y_SWAP)):
-            v = v + lax.ppermute(v, axis, pairs)
-        for pairs in (Z_NEAR, Z_FAR):
-            v = v + lax.ppermute(v, "tp", pairs)
-        return v
-
-    back = [v["head0"], v["head1"]]
-    gain_one_sum, gain_two_sum, square = v["gain_one_sum"], v["gain_two_sum"], v["square"]
-    total_count = v["total_count"]
-    gain_heads = back[0][1] + back[1][1]
-    sums = total(
-        jnp.concatenate(
-            [
-                natural(gain_one_sum.reshape(4, quarter)).reshape(1, width),
-                natural(gain_two_sum.reshape(4, quarter)).reshape(1, width),
-                gain_heads[:, 0].reshape(1, hd),
-                gain_heads[:, 1].reshape(1, hd),
-                jnp.sum(square).reshape(1, 1),
-                jnp.zeros((1, 127), F32),
-            ],
-            axis=1,
-        )
-    )[0]
-    teacher_loss = sums[2 * width + 2 * hd] / (total_count * width)
+    attn_grad = finish(v["attn_sum"], v["attn_other"])
+    teacher_loss = sums[2 * width + 2 * hd] / (v["total_count"] * width)
 
     def own_part(at, size):
         return lax.dynamic_slice_in_dim(sums, at + fsdp * (size // 4), size // 4, 0)

time: 845 us -> 833 us (0.986)
  local copies, waits for them, and re-layouts: 121 us -> 89.8 us
  Pallas kernels: 345 us -> 374 us
  starting transfers between devices: 114 us -> 98.2 us
    ppermute x12 -> x13, waiting for transfers between devices: 81.7 us -> 28.9 us  [z_down(): return lax.ppermute(v, 'tp', Z_DOWN)]
    ppermute x15 -> x21, waiting for transfers between devices: 35.5 us -> 66.1 us  [z_up(): return lax.ppermute(v, 'tp', Z_UP)]
    ppermute x18 -> x19, waiting for transfers between devices: 25.5 us -> 46.7 us  [y_swap(): return lax.ppermute(v, 'ctx', Y_SWAP)]
    ppermute x15 -> x21, starting transfers between devices: 34.6 us -> 16.8 us  [z_up(): return lax.ppermute(v, 'tp', Z_UP)]
    pallas_call x2, Pallas kernels: 37.1 us -> 53.7 us  [attn_bwd(): pl.pallas_call(functools.partial(attn_bwd_kernel, width, hd), grid_spec=p...]
    slice x10 -> x3, local copies, waits for them, and re-layouts: 17.6 us -> 2.34 us  [the longest x1 0.92 us: per_device_rows(): v['one'][0][:, units:]]
    unnamed x212 -> x242, local copies, waits for them, and re-layouts: 71 us -> 67.7 us
    ppermute x20 -> x22, starting transfers between devices: 20.3 us -> 22.4 us  [x_swap(): return lax.ppermute(v, 'fsdp', X_SWAP)]
  transfers between devices with their start and end apart: 97 -> 113, of which waited for: 28 -> 40; matrix products, arithmetic and copies ran while one was open for 9% -> 6% of each run, Pallas kernels for 37% -> 39%
where the time goes in v8:
time: 833 us; the launch traced here: 817 us
  Pallas kernels  374 us (45%)
  waiting for transfers between devices  219 us (26%)
  starting transfers between devices  98.2 us (12%)
  local copies, waits for them, and re-layouts  89.8 us (11%)
  other arithmetic  29.1 us (3%)
    pallas_call x4, Pallas kernels, ffn_bwd(): pl.pallas_call(functools.partial(ffn_bwd_kernel, steps, plan, first), gri...  104 us
    unnamed x242, local copies, waits for them, and re-layouts  67.7 us
    ppermute x21, waiting for transfers between devices, z_up(): return lax.ppermute(v, 'tp', Z_UP)  66.1 us
    pallas_call x3, Pallas kernels, ffn_fwd(): pl.pallas_call(functools.partial(ffn_fwd_kernel, tile, [plan for plan, _...  61.1 us
    pallas_call x2, Pallas kernels, attn_bwd(): pl.pallas_call(functools.partial(attn_bwd_kernel, width, hd), grid_spec=p...  53.7 us
    ppermute x22, waiting for transfers between devices, x_swap(): return lax.ppermute(v, 'fsdp', X_SWAP)  47.7 us
    ppermute x19, waiting for transfers between devices, y_swap(): return lax.ppermute(v, 'ctx', Y_SWAP)  46.7 us
    pallas_call x2, Pallas kernels, attn_fwd(): pl.pallas_call(functools.partial(attn_fwd_kernel, width, hd), grid_spec=p...  34.2 us
  transfers between devices with their start and end apart: 113, of which 40 were waited for; matrix products, arithmetic and copies ran while one was open for 6% of the time, Pallas kernels for 39%

profile of v8, /device:TPU:0, one launch (start us, length us, event | category | flops | bytes accessed | tf_op | source)
XLA Modules:
  0.0 817.1 jit_solution(10590294141280127467)
XLA Ops:
  44.1 16.2 %collective-permute-done.7 = bf16[256,256]{1,0:T(8,128)(2,1)S(1)} collective-permute-done((bf16[256,256]{1,0:T(8,128)(2,1)S(1)}, bf16[256,256]{1,0:T(8,128)(2,1)S(1)}, u32[]{:S(2)}, u32[]{:S(2)}) %collective-permute-start.7) | collective-permute-done | bytes 131104 | tf_op jit(solution)/shard_map/ppermute | solution.py:1542
  91.6 11.6 %collective-permute-done.16.rest_6_.rest_2_ = bf16[256,1152]{1,0:T(8,128)(2,1)} collective-permute-done((bf16[256,1152]{1,0:T(8,128)(2,1)S(1)}, bf16[256,1152]{1,0:T(8,128)(2,1)}, u32[]{:S(2)}, u32[]{:S(2)}) %collective-permute-start.16) | collective-permute-done | bytes 589856 | tf_op jit(solution)/shard_map/ppermute | solution.py:1539
  105.0 17.1 %attn_fwd.2 = (bf16[1024,256]{1,0:T(8,128)(2,1)}, bf16[1024,256]{1,0:T(8,128)(2,1)}, f32[2,2,2048]{2,1,0:T(2,128)}) custom-call(s32[4]{0:T(128)} %copy-done.53, bf16[512,1024]{1,0:T(8,128)(2,1)} %copy-done.65, bf16[512,1024]{1,0:T(8,128)(2,1)} %copy-done.107), custom_call_target="tpu_custom_call" | custom-call | flops 4398046511104 | bytes 1073741824 | tf_op jit(solution)/shard_map/attn_fwd/pallas_call | solution.py:755
  130.5 17.1 %attn_fwd.3 = (bf16[1024,256]{1,0:T(8,128)(2,1)}, bf16[1024,256]{1,0:T(8,128)(2,1)}, f32[2,2,2048]{2,1,0:T(2,128)}) custom-call(s32[4]{0:T(128)} %copy-done.53, bf16[512,1024]{1,0:T(8,128)(2,1)} %copy-done.64, bf16[512,1024]{1,0:T(8,128)(2,1)} %collective-permute-done.17.got_ref), custom_call_target="tpu_custom_call" | custom-call | flops 4398046511104 | bytes 1073741824 | tf_op jit(solution)/shard_map/attn_fwd/pallas_call | solution.py:755
  149.4 12.1 %collective-permute-done.27.refs_8_ = bf16[1024,256]{1,0:T(8,128)(2,1)S(1)} collective-permute-done((bf16[1024,256]{1,0:T(8,128)(2,1)}, bf16[1024,256]{1,0:T(8,128)(2,1)S(1)}, u32[]{:S(2)}, u32[]{:S(2)}) %collective-permute-start.27) | collective-permute-done | bytes 524320 | tf_op jit(solution)/shard_map/ppermute | solution.py:1536
  163.3 13.3 %collective-permute-done.29.rest_8_.rest_4_ = bf16[256,1152]{1,0:T(8,128)(2,1)} collective-permute-done((bf16[256,1152]{1,0:T(8,128)(2,1)}, bf16[256,1152]{1,0:T(8,128)(2,1)}, u32[]{:S(2)}, u32[]{:S(2)}) %collective-permute-start.29) | collective-permute-done | bytes 589856 | tf_op jit(solution)/shard_map/ppermute | solution.py:1530
  203.0 26.0 %ffn_fwd.3 = (bf16[2,1024,2304]{2,1,0:T(8,128)(2,1)}, bf16[2,1024,1152]{2,1,0:T(8,128)(2,1)}, f32[1024,1024]{1,0:T(8,128)}) custom-call(s32[4]{0:T(128)} %copy-done.53, f32[1]{0:T(128)} %bitcast.4.scale, bf16[1024,1024]{1,0:T(8,128)(2,1)} %copy-done.84, f32[1024,1024]{1,0:T(8,128)} %copy-done.79, bf16[256,3456]{1,0:T(8,128)(2,1)} %get-tuple-element.2314.rest_0_, ...), custom_call_target="tpu_custom_call" | custom-call | flops 4398046511104 | bytes 1073741824 | tf_op jit(solution)/shard_map/ffn_fwd/pallas_call | solution.py:1273
  237.3 15.5 %ffn_fwd.4 = (bf16[1,1024,2304]{2,1,0:T(8,128)(2,1)}, bf16[1,1024,1152]{2,1,0:T(8,128)(2,1)}, f32[1024,1024]{1,0:T(8,128)}) custom-call(s32[4]{0:T(128)} %copy-done.53, f32[1]{0:T(128)} %bitcast.4.scale, bf16[1024,1024]{1,0:T(8,128)(2,1)} %copy-done.84, f32[1024,1024]{1,0:T(8,128)} %get-tuple-element.1768.in_ref, ...), custom_call_target="tpu_custom_call" | custom-call | flops 4398046511104 | bytes 1073741824 | tf_op jit(solution)/shard_map/ffn_fwd/pallas_call | solution.py:1273
  259.1 19.5 %ffn_fwd.5 = (bf16[1,1024,2304]{2,1,0:T(8,128)(2,1)}, bf16[1,1024,1152]{2,1,0:T(8,128)(2,1)}, bf16[512,1024]{1,0:T(8,128)(2,1)}, bf16[512,1024]{1,0:T(8,128)(2,1...) custom-call(s32[4]{0:T(128)} %copy-done.53, ...), custom_call_target="tpu_custom_call" | custom-call | flops 4398046511104 | bytes 1073741824 | tf_op jit(solution)/shard_map/ffn_fwd/pallas_call | solution.py:1273
  279.8 25.6 %ffn_bwd.4 = (f32[1024,1024]{1,0:T(8,128)}, bf16[512,3456]{1,0:T(8,128)(2,1)}, bf16[512,3456]{1,0:T(8,128)(2,1)}) custom-call(bf16[1024,1024]{1,0:T(8,128)(2,1)} %get-tuple-element.2309.low_ref, bf16[1,1024,2304]{2,1,0:T(8,128)(2,1)} %get-tuple-element.1996.act_ref, bf16[1,1024,1152]{2,1,0:T(8,128)(2,1)} %get-tuple-element.2016.hid_ref, ...), custom_call_target="tpu_custom_call" | custom-call | flops 4398046511104 | bytes 1073741824 | tf_op jit(solution)/shard_map/ffn_bwd/pallas_call | solution.py:1360
  307.5 26.1 %ffn_bwd.5 = (f32[1024,1024]{1,0:T(8,128)}, bf16[512,3456]{1,0:T(8,128)(2,1)}, bf16[512,3456]{1,0:T(8,128)(2,1)}) custom-call(bf16[1024,1024]{1,0:T(8,128)(2,1)} %get-tuple-element.2309.low_ref, bf16[2,1024,2304]{2,1,0:T(8,128)(2,1)} %get-tuple-element.2293.act_ref, ...), custom_call_target="tpu_custom_call", output_to_operand_aliasing={{0}: (17, {})} | custom-call | flops 4398046511104 | bytes 1073741824 | tf_op jit(solution)/shard_map/ffn_bwd/pallas_call | solution.py:1360
  347.6 26.1 %ffn_bwd.6 = (f32[1024,1024]{1,0:T(8,128)}, bf16[512,3456]{1,0:T(8,128)(2,1)}, bf16[512,3456]{1,0:T(8,128)(2,1)}) custom-call(bf16[1024,1024]{1,0:T(8,128)(2,1)} %get-tuple-element.2309.low_ref, bf16[1,1024,2304]{2,1,0:T(8,128)(2,1)} %get-tuple-element.2215.act_ref, ...), custom_call_target="tpu_custom_call", output_to_operand_aliasing={{0}: (17, {})} | custom-call | flops 4398046511104 | bytes 1073741824 | tf_op jit(solution)/shard_map/ffn_bwd/pallas_call | solution.py:1360
  389.8 26.0 %ffn_bwd.7 = (f32[1024,1024]{1,0:T(8,128)}, bf16[512,3456]{1,0:T(8,128)(2,1)}, bf16[512,3456]{1,0:T(8,128)(2,1)}) custom-call(bf16[1024,1024]{1,0:T(8,128)(2,1)} %get-tuple-element.2309.low_ref, bf16[2,1024,2304]{2,1,0:T(8,128)(2,1)} %get-tuple-element.2293.act_ref, ...), custom_call_target="tpu_custom_call", output_to_operand_aliasing={{0}: (9, {})} | custom-call | flops 4398046511104 | bytes 1073741824 | tf_op jit(solution)/shard_map/ffn_bwd/pallas_call | solution.py:1360
  430.5 10.6 %norm_two_back.1 = (f32[1024,1024]{1,0:T(8,128)S(1)}, bf16[1024,1024]{1,0:T(8,128)(2,1)S(1)}, bf16[1024,256]{1,0:T(8,128)(2,1)S(1)}, bf16[1024,256]{1,0:T(8,128)...) custom-call(s32[4]{0:T(128)S(1)} %copy-done.55, ...), custom_call_target="tpu_custom_call" | custom-call | flops 4398046511104 | bytes 1073741824 | tf_op jit(solution)/shard_map/norm_two_back/pallas_call | solution.py:1032
  445.1 12.7 %collective-permute-done.71.gs_ref = bf16[1024,256]{1,0:T(8,128)(2,1)S(1)} collective-permute-done((bf16[1024,256]{1,0:T(8,128)(2,1)S(1)}, bf16[1024,256]{1,0:T(8,128)(2,1)S(1)}, u32[]{:S(2)}, u32[]{:S(2)}) %collective-permute-start.71) | collective-permute-done | bytes 524320 | tf_op jit(solution)/shard_map/ppermute | solution.py:1536
  475.6 26.8 %attn_bwd.2 = (bf16[512,1024]{1,0:T(8,128)(2,1)}, bf16[512,1024]{1,0:T(8,128)(2,1)}) custom-call(s32[4]{0:T(128)} %copy-done.53, bf16[512,1024]{1,0:T(8,128)(2,1)} %copy-done.65, bf16[512,1024]{1,0:T(8,128)(2,1)} %copy-done.107, bf16[1024,256]{1,0:T(8,128)(2,1)} %get-tuple-element.2434.refs_5_.ok_ref, bf16[1024,256]{1,0:T(8,128)(2,1)} %get-tuple-element.2435.os_ref, ...), custom_call_target="tpu_custom_call" | custom-call | flops 4398046511104 | bytes 1073741824 | tf_op jit(solution)/shard_map/attn_bwd/pallas_call | solution.py:909
  502.5 10.1 %collective-permute-done.73.refs_1_ = bf16[128,3456]{1,0:T(8,128)(2,1)} collective-permute-done((bf16[128,3456]{1,0:T(8,128)(2,1)}, bf16[128,3456]{1,0:T(8,128)(2,1)}, u32[]{:S(2)}, u32[]{:S(2)}) %collective-permute-start.73) | collective-permute-done | bytes 884768 | tf_op jit(solution)/shard_map/ppermute | solution.py:1530
  526.4 26.8 %attn_bwd.3 = (bf16[512,1024]{1,0:T(8,128)(2,1)}, bf16[512,1024]{1,0:T(8,128)(2,1)}) custom-call(s32[4]{0:T(128)} %copy-done.53, bf16[512,1024]{1,0:T(8,128)(2,1)} %copy-done.64, bf16[512,1024]{1,0:T(8,128)(2,1)} %collective-permute-done.17.got_ref, bf16[1024,256]{1,0:T(8,128)(2,1)} %get-tuple-element.2499.refs_6_.ok_ref, ...), custom_call_target="tpu_custom_call" | custom-call | flops 4398046511104 | bytes 1073741824 | tf_op jit(solution)/shard_map/attn_bwd/pallas_call | solution.py:909
  596.6 11.3 %norm_one_back.1 = (bf16[256,1024]{1,0:T(8,128)(2,1)}, bf16[256,1024]{1,0:T(8,128)(2,1)}, bf16[256,1024]{1,0:T(8,128)(2,1)}, bf16[256,1024]{1,0:T(8,128)(2,1)S(1)}, f32[1,1024]{1,0:T(1,128)S(1)}) custom-call(s32[4]{0:T(128)S(1)} %copy-done.56, bf16[256,512]{1,0:T(8,128)(2,1)S(1)} %join.1.refs_0_, bf16[256,512]{1,0:T(8,128)(2,1)} %collective-permute-done.2.refs_1_, ...), custom_call_target="tpu_custom_call" | custom-call | flops 4398046511104 | bytes 1073741824 | tf_op jit(solution)/shard_map/norm_one_back/pallas_call | solution.py:1090
  609.1 9.2 %weight_grad.1 = (bf16[4,512,768]{2,1,0:T(8,128)(2,1)S(1)}, bf16[4,512,768]{2,1,0:T(8,128)(2,1)}) custom-call(bf16[1024,1024]{1,0:T(8,128)(2,1)S(1)} %get-tuple-element.2639.refs_8_.nt_ref, bf16[2,1024,512]{2,1,0:T(8,128)(2,1)S(1)} %get-tuple-element.2640.refs_8_.back0_ref, bf16[2,1024,512]{2,1,0:T(8,128)(2,1)S(1)} %get-tuple-element.2641.refs_9_.back1_ref, ...), custom_call_target="tpu_custom_call" | custom-call | flops 4398046511104 | bytes 1073741824 | tf_op jit(solution)/shard_map/weight_grad/pallas_call | solution.py:1482
  625.7 10.9 %collective-permute-done.88 = bf16[256,1024]{1,0:T(8,128)(2,1)} collective-permute-done((bf16[256,1024]{1,0:T(8,128)(2,1)}, bf16[256,1024]{1,0:T(8,128)(2,1)}, u32[]{:S(2)}, u32[]{:S(2)}) %collective-permute-start.88) | collective-permute-done | bytes 524320 | tf_op jit(solution)/shard_map/ppermute | solution.py:1539
  653.4 12.0 %collective-permute-done.93 = f32[1,2304]{1,0:T(1,128)S(1)} collective-permute-done((f32[1,2304]{1,0:T(1,128)S(1)}, f32[1,2304]{1,0:T(1,128)S(1)}, u32[]{:S(2)}, u32[]{:S(2)}) %collective-permute-start.93) | collective-permute-done | bytes 9248 | tf_op jit(solution)/shard_map/ppermute | solution.py:1530
  737.9 20.0 %collective-permute-done.103 = f32[128,768]{1,0:T(8,128)S(1)} collective-permute-done((f32[128,768]{1,0:T(8,128)S(1)}, f32[128,768]{1,0:T(8,128)S(1)}, u32[]{:S(2)}, u32[]{:S(2)}) %collective-permute-start.103) | collective-permute-done | bytes 393248 | tf_op jit(solution)/shard_map/ppermute | solution.py:1536
  763.4 12.1 %collective-permute-done.108 = bf16[256,1024]{1,0:T(8,128)(2,1)S(1)} collective-permute-done((bf16[256,1024]{1,0:T(8,128)(2,1)}, bf16[256,1024]{1,0:T(8,128)(2,1)S(1)}, u32[]{:S(2)}, u32[]{:S(2)}) %collective-permute-start.108) | collective-permute-done | bytes 524320 | tf_op jit(solution)/shard_map/ppermute | solution.py:1539
  (571 shorter events, 395.7 us)
Async XLA Ops:
  3.3 29.2 %collective-permute-start.3 = (bf16[256,512]{1,0:T(8,128)(2,1)S(1)}, bf16[256,512]{1,0:T(8,128)(2,1)S(1)}, u32[]{:S(2)}, u32[]{:S(2)}) collective-permute-start(bf16[256,512]{1,0:T(8,128)(2,1)S(1)} %join.1.refs_0_), channel_id=1, source_target_pairs={{0,1},{1,2},{2,3},{3,0},{4,5},{5,6},{6,7},{7,4},{8,9},{9,10},{10,1... | collective-permute-start | bytes 786440 | tf_op jit(solution)/shard_map/ppermute | solution.py:1539
  62.3 41.0 %collective-permute-start.11 = (bf16[256,3456]{1,0:T(8,128)(2,1)}, bf16[256,3456]{1,0:T(8,128)(2,1)}, u32[]{:S(2)}, u32[]{:S(2)}) collective-permute-start(bf16[256,3456]{1,0:T(8,128)(2,1)} %get-tuple-element.2314.rest_0_), channel_id=1, source_target_pairs={{0,16},{16,0},{8,24},{24,8},{1,17},{17,1},{9,25},{25,9},{2,18},{18... | collective-permute-start | bytes 5308424 | tf_op jit(solution)/shard_map/ppermute | solution.py:1530
  72.3 31.0 %collective-permute-start.14 = (bf16[512,1024]{1,0:T(8,128)(2,1)S(1)}, bf16[512,1024]{1,0:T(8,128)(2,1)S(1)}, u32[]{:S(2)}, u32[]{:S(2)}) collective-permute-start(bf16[512,1024]{1,0:T(8,128)(2,1)S(1)} %get-tuple-element.1432), channel_id=1, source_target_pairs={{0,4},{4,0},{1,5},{5,1},{2,6},{6,2},{3,7},{7,3},{8,12},{12,8},{9,1... | collective-permute-start | bytes 3145736 | tf_op jit(solution)/shard_map/ppermute | solution.py:1536
  73.6 29.6 %collective-permute-start.16 = (bf16[256,1152]{1,0:T(8,128)(2,1)S(1)}, bf16[256,1152]{1,0:T(8,128)(2,1)}, u32[]{:S(2)}, u32[]{:S(2)}) collective-permute-start(bf16[256,1152]{1,0:T(8,128)(2,1)S(1)} %copy-done.70), channel_id=1, source_target_pairs={{0,1},{1,2},{2,3},{3,0},{4,5},{5,6},{6,7},{7,4},{8,9},{9,10},{10,1... | collective-permute-start | bytes 1769480 | tf_op jit(solution)/shard_map/ppermute | solution.py:1539
  78.3 43.8 %collective-permute-start.17 = (bf16[512,1024]{1,0:T(8,128)(2,1)}, bf16[512,1024]{1,0:T(8,128)(2,1)}, u32[]{:S(2)}, u32[]{:S(2)}) collective-permute-start(bf16[512,1024]{1,0:T(8,128)(2,1)} %get-tuple-element.1435), channel_id=1, source_target_pairs={{0,4},{4,0},{1,5},{5,1},{2,6},{6,2},{3,7},{7,3},{8,12},{12,8},{9,1... | collective-permute-start | bytes 3145736 | tf_op jit(solution)/shard_map/ppermute | solution.py:1536
  148.9 29.4 %collective-permute-start.31 = (bf16[256,1408]{1,0:T(8,128)(2,1)}, bf16[256,1408]{1,0:T(8,128)(2,1)S(1)}, u32[]{:S(2)}, u32[]{:S(2)}) collective-permute-start(bf16[256,1408]{1,0:T(8,128)(2,1)} %collective-permute-done.21.rest_0_), channel_id=1, source_target_pairs={{0,8},{8,0},{16,24},{24,16},{1,9},{9,1},{17,25},{25,17},{2,10},{10... | collective-permute-start | bytes 2162696 | tf_op jit(solution)/shard_map/ppermute | solution.py:1533
  198.4 32.9 %collective-permute-start.43 = (bf16[256,1408]{1,0:T(8,128)(2,1)}, bf16[256,1408]{1,0:T(8,128)(2,1)}, u32[]{:S(2)}, u32[]{:S(2)}) collective-permute-start(bf16[256,1408]{1,0:T(8,128)(2,1)} %collective-permute-done.38.rest_3_), channel_id=1, source_target_pairs={{0,4},{4,0},{1,5},{5,1},{2,6},{6,2},{3,7},{7,3},{8,12},{12,8},{9,1... | collective-permute-start | bytes 2162696 | tf_op jit(solution)/shard_map/ppermute | solution.py:1536
  199.8 31.5 %collective-permute-start.44 = (bf16[256,1408]{1,0:T(8,128)(2,1)}, bf16[256,1408]{1,0:T(8,128)(2,1)}, u32[]{:S(2)}, u32[]{:S(2)}) collective-permute-start(bf16[256,1408]{1,0:T(8,128)(2,1)} %collective-permute-done.38.rest_3_), channel_id=1, source_target_pairs={{0,8},{8,0},{16,24},{24,16},{1,9},{9,1},{17,25},{25,17},{2,10},{10... | collective-permute-start | bytes 2162696 | tf_op jit(solution)/shard_map/ppermute | solution.py:1533
  199.8 31.5 %collective-permute-start.46 = (bf16[256,1408]{1,0:T(8,128)(2,1)}, bf16[256,1408]{1,0:T(8,128)(2,1)}, u32[]{:S(2)}, u32[]{:S(2)}) collective-permute-start(bf16[256,1408]{1,0:T(8,128)(2,1)} %collective-permute-done.39.rest_1_.rest_0_), channel_id=1, source_target_pairs={{0,16},{16,0},{8,24},{24,8},{1,17},{17,1},{9,25},{25,9},{2,18},{18... | collective-permute-start | bytes 2162696 | tf_op jit(solution)/shard_map/ppermute | solution.py:1530
  202.3 29.0 %collective-permute-start.42 = (bf16[256,1152]{1,0:T(8,128)(2,1)}, bf16[256,1152]{1,0:T(8,128)(2,1)}, u32[]{:S(2)}, u32[]{:S(2)}) collective-permute-start(bf16[256,1152]{1,0:T(8,128)(2,1)} %collective-permute-done.26.rest_1_), channel_id=1, source_target_pairs={{0,16},{16,0},{8,24},{24,8},{1,17},{17,1},{9,25},{25,9},{2,18},{18... | collective-permute-start | bytes 1769480 | tf_op jit(solution)/shard_map/ppermute | solution.py:1530
  343.4 30.4 %collective-permute-start.62 = (bf16[128,3456]{1,0:T(8,128)(2,1)}, bf16[128,3456]{1,0:T(8,128)(2,1)}, u32[]{:S(2)}, u32[]{:S(2)}) collective-permute-start(bf16[128,3456]{1,0:T(8,128)(2,1)} %bitcast.7), channel_id=1, source_target_pairs={{0,16},{16,0},{8,24},{24,8},{1,17},{17,1},{9,25},{25,9},{2,18},{18... | collective-permute-start | bytes 2654216 | tf_op jit(solution)/shard_map/ppermute | solution.py:1530
  377.3 38.5 %collective-permute-start.67 = (bf16[128,3456]{1,0:T(8,128)(2,1)}, bf16[128,3456]{1,0:T(8,128)(2,1)}, u32[]{:S(2)}, u32[]{:S(2)}) collective-permute-start(bf16[128,3456]{1,0:T(8,128)(2,1)} %summed.12), channel_id=1, source_target_pairs={{0,4},{4,0},{1,5},{5,1},{2,6},{6,2},{3,7},{7,3},{8,12},{12,8},{9,1... | collective-permute-start | bytes 2654216 | tf_op jit(solution)/shard_map/ppermute | solution.py:1536
  428.3 29.5 %collective-permute-start.69 = (bf16[128,3456]{1,0:T(8,128)(2,1)}, bf16[128,3456]{1,0:T(8,128)(2,1)}, u32[]{:S(2)}, u32[]{:S(2)}) collective-permute-start(bf16[128,3456]{1,0:T(8,128)(2,1)} %summed.13), channel_id=1, source_target_pairs={{0,3},{1,0},{2,1},{3,2},{4,7},{5,4},{6,5},{7,6},{8,11},{9,8},{10,9... | collective-permute-start | bytes 2654216 | tf_op jit(solution)/shard_map/ppermute | solution.py:1545
  444.4 58.0 %collective-permute-start.74 = (bf16[1024,256]{1,0:T(8,128)(2,1)}, bf16[1024,256]{1,0:T(8,128)(2,1)}, u32[]{:S(2)}, u32[]{:S(2)}) collective-permute-start(bf16[1024,256]{1,0:T(8,128)(2,1)} %get-tuple-element.2456), channel_id=1, source_target_pairs={{0,4},{4,0},{1,5},{5,1},{2,6},{6,2},{3,7},{7,3},{8,12},{12,8},{9,1... | collective-permute-start | bytes 1572872 | tf_op jit(solution)/shard_map/ppermute | solution.py:1536
  460.4 42.1 %collective-permute-start.76 = (bf16[128,3456]{1,0:T(8,128)(2,1)}, bf16[128,3456]{1,0:T(8,128)(2,1)}, u32[]{:S(2)}, u32[]{:S(2)}) collective-permute-start(bf16[128,3456]{1,0:T(8,128)(2,1)} %summed.14), channel_id=1, source_target_pairs={{0,4},{4,0},{1,5},{5,1},{2,6},{6,2},{3,7},{7,3},{8,12},{12,8},{9,1... | collective-permute-start | bytes 2654216 | tf_op jit(solution)/shard_map/ppermute | solution.py:1536
  472.0 40.6 %collective-permute-start.75 = (bf16[512,1024]{1,0:T(8,128)(2,1)}, bf16[512,1024]{1,0:T(8,128)(2,1)}, u32[]{:S(2)}, u32[]{:S(2)}) collective-permute-start(bf16[512,1024]{1,0:T(8,128)(2,1)} %collective-permute-done.58), channel_id=1, source_target_pairs={{0,1},{1,2},{2,3},{3,0},{4,5},{5,6},{6,7},{7,4},{8,9},{9,10},{10,1... | collective-permute-start | bytes 3145736 | tf_op jit(solution)/shard_map/ppermute | solution.py:1539
  473.9 38.7 %collective-permute-start.73 = (bf16[128,3456]{1,0:T(8,128)(2,1)}, bf16[128,3456]{1,0:T(8,128)(2,1)}, u32[]{:S(2)}, u32[]{:S(2)}) collective-permute-start(bf16[128,3456]{1,0:T(8,128)(2,1)} %bitcast.22), channel_id=1, source_target_pairs={{0,16},{16,0},{8,24},{24,8},{1,17},{17,1},{9,25},{25,9},{2,18},{18... | collective-permute-start | bytes 2654216 | tf_op jit(solution)/shard_map/ppermute | solution.py:1530
  516.1 37.2 %collective-permute-start.81 = (bf16[128,3456]{1,0:T(8,128)(2,1)}, bf16[128,3456]{1,0:T(8,128)(2,1)}, u32[]{:S(2)}, u32[]{:S(2)}) collective-permute-start(bf16[128,3456]{1,0:T(8,128)(2,1)} %summed.15), channel_id=1, source_target_pairs={{0,4},{4,0},{1,5},{5,1},{2,6},{6,2},{3,7},{7,3},{8,12},{12,8},{9,1... | collective-permute-start | bytes 2654216 | tf_op jit(solution)/shard_map/ppermute | solution.py:1536
  521.2 40.8 %collective-permute-start.79 = (bf16[512,1024]{1,0:T(8,128)(2,1)}, bf16[512,1024]{1,0:T(8,128)(2,1)}, u32[]{:S(2)}, u32[]{:S(2)}) collective-permute-start(bf16[512,1024]{1,0:T(8,128)(2,1)} %get-tuple-element.2496), channel_id=1, source_target_pairs={{0,4},{4,0},{1,5},{5,1},{2,6},{6,2},{3,7},{7,3},{8,12},{12,8},{9,1... | collective-permute-start | bytes 3145736 | tf_op jit(solution)/shard_map/ppermute | solution.py:1536
  522.4 39.6 %collective-permute-start.80 = (bf16[512,1024]{1,0:T(8,128)(2,1)}, bf16[512,1024]{1,0:T(8,128)(2,1)}, u32[]{:S(2)}, u32[]{:S(2)}) collective-permute-start(bf16[512,1024]{1,0:T(8,128)(2,1)} %collective-permute-done.60), channel_id=1, source_target_pairs={{0,1},{1,2},{2,3},{3,0},{4,5},{5,6},{6,7},{7,4},{8,9},{9,10},{10,1... | collective-permute-start | bytes 3145736 | tf_op jit(solution)/shard_map/ppermute | solution.py:1539
  524.4 37.6 %collective-permute-start.78 = (bf16[128,3456]{1,0:T(8,128)(2,1)}, bf16[128,3456]{1,0:T(8,128)(2,1)}, u32[]{:S(2)}, u32[]{:S(2)}) collective-permute-start(bf16[128,3456]{1,0:T(8,128)(2,1)} %bitcast.28), channel_id=1, source_target_pairs={{0,16},{16,0},{8,24},{24,8},{1,17},{17,1},{9,25},{25,9},{2,18},{18... | collective-permute-start | bytes 2654216 | tf_op jit(solution)/shard_map/ppermute | solution.py:1530
  571.5 36.4 %collective-permute-start.86 = (bf16[128,3456]{1,0:T(8,128)(2,1)}, bf16[128,3456]{1,0:T(8,128)(2,1)}, u32[]{:S(2)}, u32[]{:S(2)}) collective-permute-start(bf16[128,3456]{1,0:T(8,128)(2,1)} %summed.18), channel_id=1, source_target_pairs={{0,1},{1,2},{2,3},{3,0},{4,5},{5,6},{6,7},{7,4},{8,9},{9,10},{10,1... | collective-permute-start | bytes 2654216 | tf_op jit(solution)/shard_map/ppermute | solution.py:1539
  572.0 36.0 %collective-permute-start.84 = (bf16[128,3456]{1,0:T(8,128)(2,1)}, bf16[128,3456]{1,0:T(8,128)(2,1)}, u32[]{:S(2)}, u32[]{:S(2)}) collective-permute-start(bf16[128,3456]{1,0:T(8,128)(2,1)} %bitcast.145), channel_id=1, source_target_pairs={{0,16},{16,0},{8,24},{24,8},{1,17},{17,1},{9,25},{25,9},{2,18},{18... | collective-permute-start | bytes 2654216 | tf_op jit(solution)/shard_map/ppermute | solution.py:1530
  712.7 71.0 %collective-permute-start.107 = (f32[128,3456]{1,0:T(8,128)S(1)}, f32[128,3456]{1,0:T(8,128)S(1)}, u32[]{:S(2)}, u32[]{:S(2)}) collective-permute-start(f32[128,3456]{1,0:T(8,128)S(1)} %summed.20), channel_id=1, source_target_pairs={{0,4},{4,0},{1,5},{5,1},{2,6},{6,2},{3,7},{7,3},{8,12},{12,8},{9,1... | collective-permute-start | bytes 5308424 | tf_op jit(solution)/shard_map/ppermute | solution.py:1536
  (204 other events, 2758.1 us)

commit v9 on v8

--- a/solution.py
+++ b/solution.py
@@ -413,7 +413,7 @@
 
 
 def pack_kernel(info, o_in, g_in, u_in, d_in, *refs):
-    out_ref, ffn_ref, first_ref, second_ref, third_ref, o_ref, g_ref, u_ref, d_ref, sems = refs
+    out_ref, ffn_ref, *chunk_refs, others_ref, o_ref, g_ref, u_ref, d_ref, sems = refs
     ctx = info[2]
     pairs = ((o_in, o_ref), (g_in, g_ref), (u_in, u_ref), (d_in, d_ref))
     copies = [pltpu.make_async_copy(a, b, sems.at[i]) for i, (a, b) in enumerate(pairs)]
@@ -421,11 +421,9 @@
         copy.start()
     for copy in copies:
         copy.wait()
-    o_t = o_ref[...].astype(F32).T.astype(BF16)
-    out_ref[...] = o_t
+    out_ref[...] = o_ref[...].astype(F32).T.astype(BF16)
     third = g_ref.shape[1] // 3
-    first_ref[:, 3 * third :] = o_t
-    for j, chunk in enumerate((first_ref, second_ref, third_ref)):
+    for j in range(3):
         at = pl.multiple_of(jnp.where(ctx == 0, j, 2 - j) * third, third)
         parts = [
             g_ref[:, pl.ds(at, third)],
@@ -433,18 +431,20 @@
             d_ref[pl.ds(at, third), :].astype(F32).T.astype(BF16),
         ]
         for i, part in enumerate(parts):
-            chunk[:, i * third : (i + 1) * third] = part
+            chunk_refs[j][:, i * third : (i + 1) * third] = part
+            if j:
+                others_ref[:, (3 * j - 3 + i) * third : (3 * j - 2 + i) * third] = part
             ffn_ref[:, (3 * j + i) * third : (3 * j + i + 1) * third] = part
 
 
 def pack(info, o, g, u, d):
     rows, units = g.shape
     feats = o.shape[0]
-    widths = (feats, 3 * units, units + feats, units, units)
+    widths = (feats, 3 * units, units, units, units, 2 * units)
     return pl.pallas_call(
         pack_kernel,
         in_specs=[SMEM] + [ANY] * 4,
-        out_specs=[pl.BlockSpec(memory_space=pltpu.VMEM)] * 5,
+        out_specs=[pl.BlockSpec(memory_space=pltpu.VMEM)] * 6,
         out_shape=[shape_of((rows, n), BF16) for n in widths],
         scratch_shapes=[pltpu.VMEM(a.shape, BF16) for a in (o, g, u, d)]
         + [pltpu.SemaphoreType.DMA((4,))],
@@ -1559,6 +1559,7 @@
     w_proj = join(q_weight, k_weight, v_weight)
     proj_z = [z_up(w_proj), z_far(w_proj), z_down(w_proj)]
     proj_far = x_swap(w_proj)
+    proj_core = core_swap(w_proj)
     count_here = jnp.sum(lengths).astype(F32)[None]
     vector = jnp.concatenate([attn_gain, ffn_gain, q_gain, k_gain]).astype(F32)
     vector = jnp.concatenate([vector, count_here, jnp.zeros((640 - 545,), F32)])[None]
@@ -1573,6 +1574,7 @@
         info=info,
         w_proj=w_proj,
         proj_far=proj_far,
+        proj_core=proj_core,
         proj_z=jnp.concatenate(proj_z, axis=0),
         w_out=w_out,
         w_ffn=w_ffn,
@@ -1589,17 +1591,15 @@
     info = v["info"]
 
     proj_zfar = x_swap(v["proj_z"])
-    one = [z_up(v["w_chunks"][0])]
-    out_two = z_far(v["w_out"])
-    proj_cores = [core_swap(v["w_proj"]), core_swap(v["proj_far"])]
+    out_z = [z_up(v["w_out"]), z_far(v["w_out"]), z_down(v["w_out"])]
+    proj_cores = [v["proj_core"], core_swap(v["proj_far"])]
     x_in, normed_one_t = norm_one(info, tokens, v["gain_one"], 256)
     v.update(
         proj_zfar=proj_zfar,
         proj_cores=proj_cores,
         x_in=x_in,
         normed_one_t=normed_one_t,
-        one=one,
-        out_two=out_two,
+        out_z=out_z,
     )
     sync()
 
@@ -1607,7 +1607,7 @@
     plan_proj = [[(0, 0), (1, 0), (4, 0), (5, 0)]]
     plan_proj += [[(p, k * quarter) for p in (2, 3, 6, 7)] for k in range(3)]
     weights_proj = [v["w_proj"], v["proj_far"], v["proj_z"], v["proj_zfar"]] + proj_cores
-    one = v["one"] + [z_up(v["w_chunks"][1]), z_up(v["w_chunks"][2])]
+    one = [z_up(v["w_chunks"][0]), z_up(v["w_chunks"][3])]
     ffn_far = x_swap(v["w_ffn"])
     tables = [v[name] for name in ("cos_part", "sin_part", "gain_q", "gain_k")]
 
@@ -1640,9 +1640,7 @@
 
     arrived = [y_swap(v["first"][1])]
     three = v["three"] + [z_down(v["w_chunks"][1])]
-    out_blocks = jnp.concatenate(
-        [v["w_out"], v["one"][0][:, units:], v["out_two"], v["three"][0][:, units:]], axis=0
-    )
+    out_blocks = jnp.concatenate([v["w_out"]] + v["out_z"], axis=0)
     out_far = x_swap(out_blocks)
     one_cores = [core_swap(v["one"][0]), core_swap(v["one_far"][0])]
     second = attn_fwd(info, v["mine"][1][0], v["got1"], hd)
@@ -1658,27 +1656,17 @@
 
     arrived = v["arrived"] + [y_swap(v["second"][1])]
     three = v["three"] + [z_down(v["w_chunks"][2])]
-    one_far = v["one_far"] + [x_swap(v["one"][1])]
+    one_far = v["one_far"] + [x_swap(v["one"][1][:, :units])]
     weights_out = [v["out_blocks"], v["out_far"]]
     weights_out += [core_swap(v["out_blocks"]), core_swap(v["out_far"])]
-    one_cores = v["one_cores"] + [core_swap(v["one"][1])]
-    three_cores = [core_swap(part) for part in v["three"]]
-    v.update(
-        arrived=arrived,
-        three=three,
-        one_far=one_far,
-        weights_out=weights_out,
-        one_cores=one_cores,
-        three_cores=three_cores,
-    )
+    v.update(arrived=arrived, three=three, one_far=one_far, weights_out=weights_out)
     sync()
 
     plan_out = [[(p, k * quarter) for p in range(4)] for k in range(4)]
     two = [z_up(v["one"][0])]
     three_far = [x_swap(v["three"][0])]
     one_far = v["one_far"] + [y_swap(v["one_far"][0])]
-    one_cores = v["one_cores"] + [core_swap(v["one_far"][1])]
-    three_cores = v["three_cores"] + [core_swap(v["three"][2])]
+    one_cores = v["one_cores"] + [core_swap(v["one"][1]), core_swap(v["one_far"][1])]
     resid, normed_two, normed_two_t, attended = out_proj(
         info,
         v["x_in"],
@@ -1693,7 +1681,6 @@
         three_far=three_far,
         one_far=one_far,
         one_cores=one_cores,
-        three_cores=three_cores,
         resid=resid,
         normed_two=normed_two,
         normed_two_t=normed_two_t,
@@ -1702,23 +1689,23 @@
     sync()
 
     plan0 = [[(i, 0, j * units) for j in range(3)] for i in range(4)]
-    plan_chunks = [[(3 * p + j, 0, 0) for j in range(3)] for p in range(4)]
+    plan_mixed = [[(0, 0, 0), (1, 0, 0), (1, 0, units)], [(i, 0, 0) for i in (2, 3, 4)]]
+    plan_mixed += [[(5, 0, 0), (6, 0, 0), (6, 0, units)], [(i, 0, 0) for i in (7, 8, 9)]]
     scale = (slots / v["total_count"])[None]
     weights0 = [v["w_ffn"], v["ffn_far"]] + v["own_cores"]
     c0, cf, c1, cb = v["one_cores"]
-    weights1 = v["one"] + v["one_far"] + [c0, c1, core_swap(v["one"][2])]
-    weights1 += [cf, cb, core_swap(v["one_far"][2])]
+    weights1 = v["one"] + v["one_far"] + [c0, c1, cf, cb, core_swap(v["one_far"][2])]
     two = v["two"] + [z_up(v["one"][1])]
     three_far = v["three_far"] + [x_swap(v["three"][1]), y_swap(v["three_far"][0])]
     two_far = [x_swap(v["two"][0])]
-    three_fars = [core_swap(v["three_far"][0])]
+    three_cores = [core_swap(v["three"][0])]
     acts_a, hiddens_a, sum_a = ffn_fwd(
         info,
         scale,
         v["normed_two"],
         v["resid"],
         None,
-        [(plan0, weights0), (plan_chunks, weights1)],
+        [(plan0, weights0), (plan_mixed, weights1)],
         units,
         256,
     )
@@ -1729,24 +1716,24 @@
         two=two,
         three_far=three_far,
         two_far=two_far,
-        three_fars=three_fars,
+        three_cores=three_cores,
         acts_a=acts_a,
         hiddens_a=hiddens_a,
         sum_a=sum_a,
     )
     sync()
 
-    weights3 = v["three"] + v["three_far"] + v["three_cores"] + v["three_fars"]
-    weights3 += [core_swap(part) for part in v["three_far"][1:]]
-    two = v["two"] + [z_up(v["one"][2])]
-    two_far = v["two_far"] + [x_swap(v["two"][1]), y_swap(v["two_far"][0])]
-    two_cores = [core_swap(part) for part in v["two"]]
+    plan_chunks = [[(3 * p + j, 0, 0) for j in range(3)] for p in range(4)]
+    weights3 = v["three"] + v["three_far"] + v["three_cores"]
+    weights3 += [core_swap(part) for part in v["three"][1:]]
+    weights3 += [core_swap(part) for part in v["three_far"]]
+    two_far = v["two_far"] + [x_swap(v["two"][1][:, :units]), y_swap(v["two_far"][0])]
+    two_cores = [core_swap(part) for part in v["two"] + v["two_far"]]
     acts_b, hiddens_b, sum_b = ffn_fwd(
         info, v["scale"], v["normed_two"], v["sum_a"], None, [(plan_chunks, weights3)], units, 256
     )
     v.update(
         weights3=weights3,
-        two=two,
         two_far=two_far,
         two_cores=two_cores,
         acts_b=acts_b,
@@ -1756,9 +1743,9 @@
     sync()
 
     weights2 = v["two"] + v["two_far"] + v["two_cores"]
-    weights2 += [core_swap(part) for part in v["two"][2:] + v["two_far"]]
+    weights2 += [core_swap(part) for part in v["two_far"][1:]]
     acts_c, hiddens_c, *results, grad_result, grad_low, grad_low_t, square = ffn_fwd(
-        info, v["scale"], v["normed_two"], v["sum_b"], teacher, [(plan_chunks, weights2)], units, 256
+        info, v["scale"], v["normed_two"], v["sum_b"], teacher, [(plan_mixed, weights2)], units, 256
     )
     v.update(
         weights2=weights2,
@@ -1788,13 +1775,13 @@
 
     turned = [False, False, True]
     one = [z_up(v["results"][0])]
-    total, keep2, send2 = ffn_back(plan_chunks, "weights2", "acts_c", "hiddens_c", 0, None)
+    total, keep2, send2 = ffn_back(plan_mixed, "weights2", "acts_c", "hiddens_c", 0, None)
     v.update(one=one, total=total, keep2=keep2, send2=send2)
     sync()
 
     one = v["one"] + [z_up(v["results"][1])]
     came2 = core_swap(v["send2"])
-    total, keep1, send1 = ffn_back(plan_chunks, "weights1", "acts_a", "hiddens_a", 1, v["total"])
+    total, keep1, send1 = ffn_back(plan_mixed, "weights1", "acts_a", "hiddens_a", 1, v["total"])
     v.update(one=one, came2=came2, total=total, keep1=keep1, send1=send1)
     sync()
 
@@ -1955,14 +1942,14 @@
         axis=1,
     )
     vector = vector + core_swap(vector)
-    v.update(one=one, keep=keep, came=core_swap(send))
+    v.update(one=one, keep=keep, send=send)
     v.update(vector=vector)
     sync()
 
     one = v["one"] + [z_up(part) for part in v["tokens_low"][1:3]]
     rows = quarter // 2
     flat = lambda a: a.reshape(4 * rows, a.shape[-1])
-    sums = [flat(p) for p in core_sum(info, v["keep"], v["came"])]
+    sums = [flat(p) for p in core_sum(info, v["keep"], core_swap(v["send"]))]
     far_t = x_swap(sums[3])
     part0 = summed([v["sum0"][0], v["far_h0"], v["there0"]], turned)
     ffn_sum = summed([part0, v["two_down"], v["up3"]], None, F32)
@@ -1992,16 +1979,16 @@
 
     three = v["three"] + [z_down(part) for part in v["tokens_low"][2:]]
     attn_sum = summed(v["parts"], None, F32)
-    attn_other = y_swap(attn_sum)
     vector = v["vector"] + lax.ppermute(v["vector"], "tp", Z_NEAR)
     grad = place(v["grad"], v["one"], 1, 0)
-    v.update(three=three, attn_sum=attn_sum, attn_other=attn_other, vector=vector, grad=grad)
+    v.update(three=three, attn_sum=attn_sum, vector=vector, grad=grad, ffn_other=ffn_other)
     sync()
 
     two = [z_up(part) for part in v["one"][:2]]
+    attn_other = y_swap(v["attn_sum"])
     vector = v["vector"] + lax.ppermute(v["vector"], "tp", Z_FAR)
     grad = place(v["grad"], v["three"], 3, 0)
-    v.update(two=two, vector=vector, grad=grad, ffn_other=ffn_other)
+    v.update(two=two, vector=vector, grad=grad, attn_other=attn_other)
     sync()
 
     two = [z_up(part) for part in v["one"][2:]]

time: 833 us -> 812 us (0.975); the launches traced: 817 us -> 808 us
  waiting for transfers between devices: 219 us -> 176 us
  Pallas kernels: 374 us -> 396 us
  local copies, waits for them, and re-layouts: 89.8 us -> 98.6 us
    ppermute x22, waiting for transfers between devices: 47.7 us -> 22.5 us  [x_swap(): return lax.ppermute(v, 'fsdp', X_SWAP)]
    pallas_call x2, Pallas kernels: 53.7 us -> 76.9 us  [attn_bwd(): pl.pallas_call(functools.partial(attn_bwd_kernel, width, hd), grid_spec=p...]
    ppermute x13 -> x14, waiting for transfers between devices: 28.9 us -> 50.6 us  [z_down(): return lax.ppermute(v, 'tp', Z_DOWN)]
    ppermute x19, waiting for transfers between devices: 46.7 us -> 30.9 us  [y_swap(): return lax.ppermute(v, 'ctx', Y_SWAP)]
    ppermute x21 -> x20, waiting for transfers between devices: 66.1 us -> 51.1 us  [z_up(): return lax.ppermute(v, 'tp', Z_UP)]
    unnamed x242 -> x263, local copies, waits for them, and re-layouts: 67.7 us -> 75.2 us
    ppermute x21 -> x20, starting transfers between devices: 16.8 us -> 19.2 us  [z_up(): return lax.ppermute(v, 'tp', Z_UP)]
    ppermute x13 -> x14, starting transfers between devices: 23.4 us -> 23 us  [z_down(): return lax.ppermute(v, 'tp', Z_DOWN)]
  transfers between devices with their start and end apart: 113 -> 111, of which waited for: 40 -> 30; matrix products, arithmetic and copies ran while one was open for 6% -> 5% of each run, Pallas kernels for 39% -> 44%
where the time goes in v9:
time: 812 us; the launch traced here: 808 us
  Pallas kernels  396 us (49%)
  waiting for transfers between devices  176 us (22%)
  starting transfers between devices  104 us (13%)
  local copies, waits for them, and re-layouts  98.6 us (12%)
  other arithmetic  26 us (3%)
    pallas_call x4, Pallas kernels, ffn_bwd(): pl.pallas_call(functools.partial(ffn_bwd_kernel, steps, plan, first), gri...  104 us
    pallas_call x2, Pallas kernels, attn_bwd(): pl.pallas_call(functools.partial(attn_bwd_kernel, width, hd), grid_spec=p...  76.9 us
    unnamed x263, local copies, waits for them, and re-layouts  75.2 us
    pallas_call x3, Pallas kernels, ffn_fwd(): pl.pallas_call(functools.partial(ffn_fwd_kernel, tile, [plan for plan, _...  61.5 us
    ppermute x20, waiting for transfers between devices, z_up(): return lax.ppermute(v, 'tp', Z_UP)  51.1 us
    ppermute x14, waiting for transfers between devices, z_down(): return lax.ppermute(v, 'tp', Z_DOWN)  50.6 us
    pallas_call x2, Pallas kernels, attn_fwd(): pl.pallas_call(functools.partial(attn_fwd_kernel, width, hd), grid_spec=p...  34.2 us
    ppermute x19, waiting for transfers between devices, y_swap(): return lax.ppermute(v, 'ctx', Y_SWAP)  30.9 us
  transfers between devices with their start and end apart: 111, of which 30 were waited for; matrix products, arithmetic and copies ran while one was open for 5% of the time, Pallas kernels for 44%

profile of v9, /device:TPU:0, one launch (start us, length us, event | category | flops | bytes accessed | tf_op | source)
XLA Modules:
  0.0 807.7 jit_solution(12090099848802080041)
XLA Ops:
  83.9 15.2 %collective-permute-done.16.rest_4_.rest_0_ = bf16[256,1152]{1,0:T(8,128)(2,1)} collective-permute-done((bf16[256,1152]{1,0:T(8,128)(2,1)}, bf16[256,1152]{1,0:T(8,128)(2,1)}, u32[]{:S(2)}, u32[]{:S(2)}) %collective-permute-start.16) | collective-permute-done | bytes 589856 | tf_op jit(solution)/shard_map/ppermute | solution.py:1539
  100.3 17.1 %attn_fwd.2 = (bf16[1024,256]{1,0:T(8,128)(2,1)}, bf16[1024,256]{1,0:T(8,128)(2,1)}, f32[2,2,2048]{2,1,0:T(2,128)}) custom-call(s32[4]{0:T(128)} %copy-done.53, bf16[512,1024]{1,0:T(8,128)(2,1)} %copy-done.69, bf16[512,1024]{1,0:T(8,128)(2,1)} %copy-done.116), custom_call_target="tpu_custom_call" | custom-call | flops 4398046511104 | bytes 1073741824 | tf_op jit(solution)/shard_map/attn_fwd/pallas_call | solution.py:755
  123.9 17.1 %attn_fwd.3 = (bf16[1024,256]{1,0:T(8,128)(2,1)}, bf16[1024,256]{1,0:T(8,128)(2,1)}, f32[2,2,2048]{2,1,0:T(2,128)}) custom-call(s32[4]{0:T(128)} %copy-done.53, bf16[512,1024]{1,0:T(8,128)(2,1)} %copy-done.68, bf16[512,1024]{1,0:T(8,128)(2,1)} %collective-permute-done.18.got_ref), custom_call_target="tpu_custom_call" | custom-call | flops 4398046511104 | bytes 1073741824 | tf_op jit(solution)/shard_map/attn_fwd/pallas_call | solution.py:755
  145.7 11.9 %collective-permute-done.28.refs_8_ = bf16[1024,256]{1,0:T(8,128)(2,1)S(1)} collective-permute-done((bf16[1024,256]{1,0:T(8,128)(2,1)}, bf16[1024,256]{1,0:T(8,128)(2,1)S(1)}, u32[]{:S(2)}, u32[]{:S(2)}) %collective-permute-start.28) | collective-permute-done | bytes 524320 | tf_op jit(solution)/shard_map/ppermute | solution.py:1536
  165.8 8.0 out_proj.1
  185.1 26.3 %ffn_fwd.3 = (bf16[2,1024,2304]{2,1,0:T(8,128)(2,1)}, bf16[2,1024,1152]{2,1,0:T(8,128)(2,1)}, f32[1024,1024]{1,0:T(8,128)}) custom-call(s32[4]{0:T(128)} %copy-done.53, f32[1]{0:T(128)} %bitcast.4.scale, bf16[1024,1024]{1,0:T(8,128)(2,1)} %copy-done.86, f32[1024,1024]{1,0:T(8,128)} %copy-done.81, bf16[256,3456]{1,0:T(8,128)(2,1)} %get-tuple-element.2342.rest_0_, ...), custom_call_target="tpu_custom_call" | custom-call | flops 4398046511104 | bytes 1073741824 | tf_op jit(solution)/shard_map/ffn_fwd/pallas_call | solution.py:1273
  219.2 15.6 %ffn_fwd.4 = (bf16[1,1024,2304]{2,1,0:T(8,128)(2,1)}, bf16[1,1024,1152]{2,1,0:T(8,128)(2,1)}, f32[1024,1024]{1,0:T(8,128)}) custom-call(s32[4]{0:T(128)} %copy-done.53, f32[1]{0:T(128)} %bitcast.4.scale, bf16[1024,1024]{1,0:T(8,128)(2,1)} %copy-done.86, f32[1024,1024]{1,0:T(8,128)} %get-tuple-element.1800.in_ref, ...), custom_call_target="tpu_custom_call" | custom-call | flops 4398046511104 | bytes 1073741824 | tf_op jit(solution)/shard_map/ffn_fwd/pallas_call | solution.py:1273
  238.3 19.6 %ffn_fwd.5 = (bf16[1,1024,2304]{2,1,0:T(8,128)(2,1)}, bf16[1,1024,1152]{2,1,0:T(8,128)(2,1)}, bf16[512,1024]{1,0:T(8,128)(2,1)}, bf16[512,1024]{1,0:T(8,128)(2,1...) custom-call(s32[4]{0:T(128)} %copy-done.53, ...), custom_call_target="tpu_custom_call" | custom-call | flops 4398046511104 | bytes 1073741824 | tf_op jit(solution)/shard_map/ffn_fwd/pallas_call | solution.py:1273
  259.3 25.5 %ffn_bwd.4 = (f32[1024,1024]{1,0:T(8,128)}, bf16[512,3456]{1,0:T(8,128)(2,1)}, bf16[512,3456]{1,0:T(8,128)(2,1)}) custom-call(bf16[1024,1024]{1,0:T(8,128)(2,1)} %get-tuple-element.2337.low_ref, bf16[1,1024,2304]{2,1,0:T(8,128)(2,1)} %get-tuple-element.2027.act_ref, bf16[1,1024,1152]{2,1,0:T(8,128)(2,1)} %get-tuple-element.2047.hid_ref, ...), custom_call_target="tpu_custom_call" | custom-call | flops 4398046511104 | bytes 1073741824 | tf_op jit(solution)/shard_map/ffn_bwd/pallas_call | solution.py:1360
  285.6 26.2 %ffn_bwd.5 = (f32[1024,1024]{1,0:T(8,128)}, bf16[512,3456]{1,0:T(8,128)(2,1)}, bf16[512,3456]{1,0:T(8,128)(2,1)}) custom-call(bf16[1024,1024]{1,0:T(8,128)(2,1)} %get-tuple-element.2337.low_ref, bf16[2,1024,2304]{2,1,0:T(8,128)(2,1)} %get-tuple-element.2321.act_ref, ...), custom_call_target="tpu_custom_call", output_to_operand_aliasing={{0}: (15, {})} | custom-call | flops 4398046511104 | bytes 1073741824 | tf_op jit(solution)/shard_map/ffn_bwd/pallas_call | solution.py:1360
  326.3 26.1 %ffn_bwd.6 = (f32[1024,1024]{1,0:T(8,128)}, bf16[512,3456]{1,0:T(8,128)(2,1)}, bf16[512,3456]{1,0:T(8,128)(2,1)}) custom-call(bf16[1024,1024]{1,0:T(8,128)(2,1)} %get-tuple-element.2337.low_ref, bf16[1,1024,2304]{2,1,0:T(8,128)(2,1)} %get-tuple-element.2243.act_ref, ...), custom_call_target="tpu_custom_call", output_to_operand_aliasing={{0}: (17, {})} | custom-call | flops 4398046511104 | bytes 1073741824 | tf_op jit(solution)/shard_map/ffn_bwd/pallas_call | solution.py:1360
  369.8 25.9 %ffn_bwd.7 = (f32[1024,1024]{1,0:T(8,128)}, bf16[512,3456]{1,0:T(8,128)(2,1)}, bf16[512,3456]{1,0:T(8,128)(2,1)}) custom-call(bf16[1024,1024]{1,0:T(8,128)(2,1)} %get-tuple-element.2337.low_ref, bf16[2,1024,2304]{2,1,0:T(8,128)(2,1)} %get-tuple-element.2321.act_ref, ...), custom_call_target="tpu_custom_call", output_to_operand_aliasing={{0}: (9, {})} | custom-call | flops 4398046511104 | bytes 1073741824 | tf_op jit(solution)/shard_map/ffn_bwd/pallas_call | solution.py:1360
  410.1 10.6 %norm_two_back.1 = (f32[1024,1024]{1,0:T(8,128)S(1)}, bf16[1024,1024]{1,0:T(8,128)(2,1)S(1)}, bf16[1024,256]{1,0:T(8,128)(2,1)S(1)}, bf16[1024,256]{1,0:T(8,128)...) custom-call(s32[4]{0:T(128)S(1)} %copy-done.55, ...), custom_call_target="tpu_custom_call" | custom-call | flops 4398046511104 | bytes 1073741824 | tf_op jit(solution)/shard_map/norm_two_back/pallas_call | solution.py:1032
  424.7 12.7 %collective-permute-done.69.gs_ref = bf16[1024,256]{1,0:T(8,128)(2,1)S(1)} collective-permute-done((bf16[1024,256]{1,0:T(8,128)(2,1)S(1)}, bf16[1024,256]{1,0:T(8,128)(2,1)S(1)}, u32[]{:S(2)}, u32[]{:S(2)}) %collective-permute-start.69) | collective-permute-done | bytes 524320 | tf_op jit(solution)/shard_map/ppermute | solution.py:1536
  454.0 38.5 %attn_bwd.2 = (bf16[512,1024]{1,0:T(8,128)(2,1)}, bf16[512,1024]{1,0:T(8,128)(2,1)}) custom-call(s32[4]{0:T(128)} %copy-done.53, bf16[512,1024]{1,0:T(8,128)(2,1)} %copy-done.69, bf16[512,1024]{1,0:T(8,128)(2,1)} %copy-done.116, bf16[1024,256]{1,0:T(8,128)(2,1)} %get-tuple-element.2462.refs_5_.ok_ref, bf16[1024,256]{1,0:T(8,128)(2,1)} %get-tuple-element.2463.os_ref, ...), custom_call_target="tpu_custom_call" | custom-call | flops 4398046511104 | bytes 1073741824 | tf_op jit(solution)/shard_map/attn_bwd/pallas_call | solution.py:909
  504.4 38.5 %attn_bwd.3 = (bf16[512,1024]{1,0:T(8,128)(2,1)}, bf16[512,1024]{1,0:T(8,128)(2,1)}) custom-call(s32[4]{0:T(128)} %copy-done.53, bf16[512,1024]{1,0:T(8,128)(2,1)} %copy-done.68, bf16[512,1024]{1,0:T(8,128)(2,1)} %collective-permute-done.18.got_ref, bf16[1024,256]{1,0:T(8,128)(2,1)} %get-tuple-element.2527.refs_6_.ok_ref, ...), custom_call_target="tpu_custom_call" | custom-call | flops 4398046511104 | bytes 1073741824 | tf_op jit(solution)/shard_map/attn_bwd/pallas_call | solution.py:909
  562.3 19.4 %collective-permute-done.81.refs_1_ = bf16[128,3456]{1,0:T(8,128)(2,1)} collective-permute-done((bf16[128,3456]{1,0:T(8,128)(2,1)}, bf16[128,3456]{1,0:T(8,128)(2,1)}, u32[]{:S(2)}, u32[]{:S(2)}) %collective-permute-start.81) | collective-permute-done | bytes 884768 | tf_op jit(solution)/shard_map/ppermute | solution.py:1545
  589.5 10.9 %norm_one_back.1 = (bf16[256,1024]{1,0:T(8,128)(2,1)S(1)}, bf16[256,1024]{1,0:T(8,128)(2,1)}, bf16[256,1024]{1,0:T(8,128)(2,1)}, bf16[256,1024]{1,0:T(8,128)(2,1)S(1)}, f32[1,1024]{1,0:T(1,128)S(1)}) custom-call(s32[4]{0:T(128)S(1)} %copy-done.56, bf16[256,512]{1,0:T(8,128)(2,1)S(1)} %join.1.refs_0_, bf16[256,512]{1,0:T(8,128)(2,1)} %collective-permute-done.3.refs_1_, ...), custom_call_target="tpu_custom_call" | custom-call | flops 4398046511104 | bytes 1073741824 | tf_op jit(solution)/shard_map/norm_one_back/pallas_call | solution.py:1090
  611.0 8.2 %weight_grad.1 = (bf16[4,512,768]{2,1,0:T(8,128)(2,1)S(1)}, bf16[4,512,768]{2,1,0:T(8,128)(2,1)S(1)}) custom-call(bf16[1024,1024]{1,0:T(8,128)(2,1)S(1)} %get-tuple-element.2675.refs_8_.nt_ref, bf16[2,1024,512]{2,1,0:T(8,128)(2,1)S(1)} %copy-done.65, bf16[2,1024,512]{2,1,0:T(8,128)(2,1)S(1)} %copy-done.67, bf16[1024,1024]{1,0:T(8,128)(2,1)S(1)} %copy-done.88, ...), custom_call_target="tpu_custom_call" | custom-call | flops 4398046511104 | bytes 1073741824 | tf_op jit(solution)/shard_map/weight_grad/pallas_call | solution.py:1482
  639.6 14.2 %collective-permute-done.91 = f32[1,2304]{1,0:T(1,128)S(1)} collective-permute-done((f32[1,2304]{1,0:T(1,128)S(1)}, f32[1,2304]{1,0:T(1,128)S(1)}, u32[]{:S(2)}, u32[]{:S(2)}) %collective-permute-start.91) | collective-permute-done | bytes 9248 | tf_op jit(solution)/shard_map/ppermute | solution.py:1530
  704.0 8.3 %collective-permute-done.98.refs_2_ = bf16[128,768]{1,0:T(8,128)(2,1)S(1)} collective-permute-done((bf16[128,768]{1,0:T(8,128)(2,1)S(1)}, bf16[128,768]{1,0:T(8,128)(2,1)S(1)}, u32[]{:S(2)}, u32[]{:S(2)}) %collective-permute-start.98) | collective-permute-done | bytes 196640 | tf_op jit(solution)/shard_map/ppermute | solution.py:1542
  726.9 9.9 %collective-permute-done.102 = bf16[256,1024]{1,0:T(8,128)(2,1)S(1)} collective-permute-done((bf16[256,1024]{1,0:T(8,128)(2,1)}, bf16[256,1024]{1,0:T(8,128)(2,1)S(1)}, u32[]{:S(2)}, u32[]{:S(2)}) %collective-permute-start.102) | collective-permute-done | bytes 524320 | tf_op jit(solution)/shard_map/ppermute | solution.py:1545
  736.8 9.9 %collective-permute-done.103 = bf16[256,1024]{1,0:T(8,128)(2,1)S(1)} collective-permute-done((bf16[256,1024]{1,0:T(8,128)(2,1)S(1)}, bf16[256,1024]{1,0:T(8,128)(2,1)S(1)}, u32[]{:S(2)}, u32[]{:S(2)}) %collective-permute-start.103) | collective-permute-done | bytes 524320 | tf_op jit(solution)/shard_map/ppermute | solution.py:1545
  765.8 8.6 %collective-permute-done.107 = bf16[256,1024]{1,0:T(8,128)(2,1)} collective-permute-done((bf16[256,1024]{1,0:T(8,128)(2,1)}, bf16[256,1024]{1,0:T(8,128)(2,1)}, u32[]{:S(2)}, u32[]{:S(2)}) %collective-permute-start.107) | collective-permute-done | bytes 524320 | tf_op jit(solution)/shard_map/ppermute | solution.py:1539
  (588 shorter events, 377.0 us)
Async XLA Ops:
  55.2 43.9 %collective-permute-start.12 = (bf16[256,3456]{1,0:T(8,128)(2,1)}, bf16[256,3456]{1,0:T(8,128)(2,1)}, u32[]{:S(2)}, u32[]{:S(2)}) collective-permute-start(bf16[256,3456]{1,0:T(8,128)(2,1)} %get-tuple-element.2342.rest_0_), channel_id=1, source_target_pairs={{0,16},{16,0},{8,24},{24,8},{1,17},{17,1},{9,25},{25,9},{2,18},{18... | collective-permute-start | bytes 5308424 | tf_op jit(solution)/shard_map/ppermute | solution.py:1530
  56.7 42.4 %collective-permute-start.17 = (bf16[256,2304]{1,0:T(8,128)(2,1)}, bf16[256,2304]{1,0:T(8,128)(2,1)}, u32[]{:S(2)}, u32[]{:S(2)}) collective-permute-start(bf16[256,2304]{1,0:T(8,128)(2,1)} %get-tuple-element.1460), channel_id=1, source_target_pairs={{0,1},{1,2},{2,3},{3,0},{4,5},{5,6},{6,7},{7,4},{8,9},{9,10},{10,1... | collective-permute-start | bytes 3538952 | tf_op jit(solution)/shard_map/ppermute | solution.py:1539
  65.2 33.9 %collective-permute-start.15 = (bf16[512,1024]{1,0:T(8,128)(2,1)S(1)}, bf16[512,1024]{1,0:T(8,128)(2,1)S(1)}, u32[]{:S(2)}, u32[]{:S(2)}) collective-permute-start(bf16[512,1024]{1,0:T(8,128)(2,1)S(1)} %get-tuple-element.1449), channel_id=1, source_target_pairs={{0,4},{4,0},{1,5},{5,1},{2,6},{6,2},{3,7},{7,3},{8,12},{12,8},{9,1... | collective-permute-start | bytes 3145736 | tf_op jit(solution)/shard_map/ppermute | solution.py:1536
  66.5 32.6 %collective-permute-start.16 = (bf16[256,1152]{1,0:T(8,128)(2,1)}, bf16[256,1152]{1,0:T(8,128)(2,1)}, u32[]{:S(2)}, u32[]{:S(2)}) collective-permute-start(bf16[256,1152]{1,0:T(8,128)(2,1)} %get-tuple-element.1505), channel_id=1, source_target_pairs={{0,1},{1,2},{2,3},{3,0},{4,5},{5,6},{6,7},{7,4},{8,9},{9,10},{10,1... | collective-permute-start | bytes 1769480 | tf_op jit(solution)/shard_map/ppermute | solution.py:1539
  71.7 45.7 %collective-permute-start.18 = (bf16[512,1024]{1,0:T(8,128)(2,1)}, bf16[512,1024]{1,0:T(8,128)(2,1)}, u32[]{:S(2)}, u32[]{:S(2)}) collective-permute-start(bf16[512,1024]{1,0:T(8,128)(2,1)} %get-tuple-element.1452), channel_id=1, source_target_pairs={{0,4},{4,0},{1,5},{5,1},{2,6},{6,2},{3,7},{7,3},{8,12},{12,8},{9,1... | collective-permute-start | bytes 3145736 | tf_op jit(solution)/shard_map/ppermute | solution.py:1536
  179.9 31.4 %collective-permute-start.42 = (bf16[256,2304]{1,0:T(8,128)(2,1)}, bf16[256,2304]{1,0:T(8,128)(2,1)}, u32[]{:S(2)}, u32[]{:S(2)}) collective-permute-start(bf16[256,2304]{1,0:T(8,128)(2,1)} %collective-permute-done.17.rest_5_.rest_1_), channel_id=1, source_target_pairs={{0,1},{1,2},{2,3},{3,0},{4,5},{5,6},{6,7},{7,4},{8,9},{9,10},{10,1... | collective-permute-start | bytes 3538952 | tf_op jit(solution)/shard_map/ppermute | solution.py:1539
  180.6 30.7 %collective-permute-start.39 = (bf16[256,1152]{1,0:T(8,128)(2,1)}, bf16[256,1152]{1,0:T(8,128)(2,1)}, u32[]{:S(2)}, u32[]{:S(2)}) collective-permute-start(bf16[256,1152]{1,0:T(8,128)(2,1)} %collective-permute-done.22.rest_0_), channel_id=1, source_target_pairs={{0,8},{8,0},{16,24},{24,16},{1,9},{9,1},{17,25},{25,17},{2,10},{10... | collective-permute-start | bytes 1769480 | tf_op jit(solution)/shard_map/ppermute | solution.py:1533
  180.8 30.5 %collective-permute-start.40 = (bf16[256,1152]{1,0:T(8,128)(2,1)}, bf16[256,1152]{1,0:T(8,128)(2,1)}, u32[]{:S(2)}, u32[]{:S(2)}) collective-permute-start(bf16[256,1152]{1,0:T(8,128)(2,1)} %collective-permute-done.27.rest_1_), channel_id=1, source_target_pairs={{0,16},{16,0},{8,24},{24,8},{1,17},{17,1},{9,25},{25,9},{2,18},{18... | collective-permute-start | bytes 1769480 | tf_op jit(solution)/shard_map/ppermute | solution.py:1530
  356.0 39.8 %collective-permute-start.65 = (bf16[128,3456]{1,0:T(8,128)(2,1)}, bf16[128,3456]{1,0:T(8,128)(2,1)}, u32[]{:S(2)}, u32[]{:S(2)}) collective-permute-start(bf16[128,3456]{1,0:T(8,128)(2,1)} %summed.12), channel_id=1, source_target_pairs={{0,4},{4,0},{1,5},{5,1},{2,6},{6,2},{3,7},{7,3},{8,12},{12,8},{9,1... | collective-permute-start | bytes 2654216 | tf_op jit(solution)/shard_map/ppermute | solution.py:1536
  423.2 69.3 %collective-permute-start.72 = (bf16[1024,256]{1,0:T(8,128)(2,1)}, bf16[1024,256]{1,0:T(8,128)(2,1)}, u32[]{:S(2)}, u32[]{:S(2)}) collective-permute-start(bf16[1024,256]{1,0:T(8,128)(2,1)} %get-tuple-element.2484), channel_id=1, source_target_pairs={{0,4},{4,0},{1,5},{5,1},{2,6},{6,2},{3,7},{7,3},{8,12},{12,8},{9,1... | collective-permute-start | bytes 1572872 | tf_op jit(solution)/shard_map/ppermute | solution.py:1536
  440.0 52.5 %collective-permute-start.74 = (bf16[128,3456]{1,0:T(8,128)(2,1)}, bf16[128,3456]{1,0:T(8,128)(2,1)}, u32[]{:S(2)}, u32[]{:S(2)}) collective-permute-start(bf16[128,3456]{1,0:T(8,128)(2,1)} %summed.14), channel_id=1, source_target_pairs={{0,4},{4,0},{1,5},{5,1},{2,6},{6,2},{3,7},{7,3},{8,12},{12,8},{9,1... | collective-permute-start | bytes 2654216 | tf_op jit(solution)/shard_map/ppermute | solution.py:1536
  450.6 41.9 %collective-permute-start.73 = (bf16[512,1024]{1,0:T(8,128)(2,1)}, bf16[512,1024]{1,0:T(8,128)(2,1)}, u32[]{:S(2)}, u32[]{:S(2)}) collective-permute-start(bf16[512,1024]{1,0:T(8,128)(2,1)} %collective-permute-done.56), channel_id=1, source_target_pairs={{0,1},{1,2},{2,3},{3,0},{4,5},{5,6},{6,7},{7,4},{8,9},{9,10},{10,1... | collective-permute-start | bytes 3145736 | tf_op jit(solution)/shard_map/ppermute | solution.py:1539
  452.0 40.5 %collective-permute-start.70 = (bf16[128,3456]{1,0:T(8,128)(2,1)}, bf16[128,3456]{1,0:T(8,128)(2,1)}, u32[]{:S(2)}, u32[]{:S(2)}) collective-permute-start(bf16[128,3456]{1,0:T(8,128)(2,1)} %bitcast.15), channel_id=1, source_target_pairs={{0,16},{16,0},{8,24},{24,8},{1,17},{17,1},{9,25},{25,9},{2,18},{18... | collective-permute-start | bytes 2654216 | tf_op jit(solution)/shard_map/ppermute | solution.py:1530
  453.1 39.4 %collective-permute-start.71 = (bf16[128,3456]{1,0:T(8,128)(2,1)}, bf16[128,3456]{1,0:T(8,128)(2,1)}, u32[]{:S(2)}, u32[]{:S(2)}) collective-permute-start(bf16[128,3456]{1,0:T(8,128)(2,1)} %bitcast.22), channel_id=1, source_target_pairs={{0,16},{16,0},{8,24},{24,8},{1,17},{17,1},{9,25},{25,9},{2,18},{18... | collective-permute-start | bytes 2654216 | tf_op jit(solution)/shard_map/ppermute | solution.py:1530
  496.1 46.9 %collective-permute-start.79 = (bf16[128,3456]{1,0:T(8,128)(2,1)}, bf16[128,3456]{1,0:T(8,128)(2,1)}, u32[]{:S(2)}, u32[]{:S(2)}) collective-permute-start(bf16[128,3456]{1,0:T(8,128)(2,1)} %summed.15), channel_id=1, source_target_pairs={{0,4},{4,0},{1,5},{5,1},{2,6},{6,2},{3,7},{7,3},{8,12},{12,8},{9,1... | collective-permute-start | bytes 2654216 | tf_op jit(solution)/shard_map/ppermute | solution.py:1536
  501.9 41.1 %collective-permute-start.77 = (bf16[512,1024]{1,0:T(8,128)(2,1)}, bf16[512,1024]{1,0:T(8,128)(2,1)}, u32[]{:S(2)}, u32[]{:S(2)}) collective-permute-start(bf16[512,1024]{1,0:T(8,128)(2,1)} %get-tuple-element.2524), channel_id=1, source_target_pairs={{0,4},{4,0},{1,5},{5,1},{2,6},{6,2},{3,7},{7,3},{8,12},{12,8},{9,1... | collective-permute-start | bytes 3145736 | tf_op jit(solution)/shard_map/ppermute | solution.py:1536
  502.4 40.6 %collective-permute-start.78 = (bf16[512,1024]{1,0:T(8,128)(2,1)}, bf16[512,1024]{1,0:T(8,128)(2,1)}, u32[]{:S(2)}, u32[]{:S(2)}) collective-permute-start(bf16[512,1024]{1,0:T(8,128)(2,1)} %collective-permute-done.58), channel_id=1, source_target_pairs={{0,1},{1,2},{2,3},{3,0},{4,5},{5,6},{6,7},{7,4},{8,9},{9,10},{10,1... | collective-permute-start | bytes 3145736 | tf_op jit(solution)/shard_map/ppermute | solution.py:1539
  502.4 40.5 %collective-permute-start.75 = (bf16[128,3456]{1,0:T(8,128)(2,1)}, bf16[128,3456]{1,0:T(8,128)(2,1)}, u32[]{:S(2)}, u32[]{:S(2)}) collective-permute-start(bf16[128,3456]{1,0:T(8,128)(2,1)} %bitcast.21), channel_id=1, source_target_pairs={{0,16},{16,0},{8,24},{24,8},{1,17},{17,1},{9,25},{25,9},{2,18},{18... | collective-permute-start | bytes 2654216 | tf_op jit(solution)/shard_map/ppermute | solution.py:1530
  504.0 39.0 %collective-permute-start.76 = (bf16[128,3456]{1,0:T(8,128)(2,1)}, bf16[128,3456]{1,0:T(8,128)(2,1)}, u32[]{:S(2)}, u32[]{:S(2)}) collective-permute-start(bf16[128,3456]{1,0:T(8,128)(2,1)} %bitcast.28), channel_id=1, source_target_pairs={{0,16},{16,0},{8,24},{24,8},{1,17},{17,1},{9,25},{25,9},{2,18},{18... | collective-permute-start | bytes 2654216 | tf_op jit(solution)/shard_map/ppermute | solution.py:1530
  543.0 38.8 %collective-permute-start.80 = (bf16[512,1024]{1,0:T(8,128)(2,1)}, bf16[512,1024]{1,0:T(8,128)(2,1)}, u32[]{:S(2)}, u32[]{:S(2)}) collective-permute-start(bf16[512,1024]{1,0:T(8,128)(2,1)} %get-tuple-element.2581), channel_id=1, source_target_pairs={{0,4},{4,0},{1,5},{5,1},{2,6},{6,2},{3,7},{7,3},{8,12},{12,8},{9,1... | collective-permute-start | bytes 3145736 | tf_op jit(solution)/shard_map/ppermute | solution.py:1536
  544.6 37.2 %collective-permute-start.81 = (bf16[128,3456]{1,0:T(8,128)(2,1)}, bf16[128,3456]{1,0:T(8,128)(2,1)}, u32[]{:S(2)}, u32[]{:S(2)}) collective-permute-start(bf16[128,3456]{1,0:T(8,128)(2,1)} %copy-done.37), channel_id=1, source_target_pairs={{0,3},{1,0},{2,1},{3,2},{4,7},{5,4},{6,5},{7,6},{8,11},{9,8},{10,9... | collective-permute-start | bytes 2654216 | tf_op jit(solution)/shard_map/ppermute | solution.py:1545
  549.2 52.8 %collective-permute-start.84 = (bf16[128,3456]{1,0:T(8,128)(2,1)}, bf16[128,3456]{1,0:T(8,128)(2,1)}, u32[]{:S(2)}, u32[]{:S(2)}) collective-permute-start(bf16[128,3456]{1,0:T(8,128)(2,1)} %summed.18), channel_id=1, source_target_pairs={{0,1},{1,2},{2,3},{3,0},{4,5},{5,6},{6,7},{7,4},{8,9},{9,10},{10,1... | collective-permute-start | bytes 2654216 | tf_op jit(solution)/shard_map/ppermute | solution.py:1539
  550.8 51.2 %collective-permute-start.82 = (bf16[128,3456]{1,0:T(8,128)(2,1)}, bf16[128,3456]{1,0:T(8,128)(2,1)}, u32[]{:S(2)}, u32[]{:S(2)}) collective-permute-start(bf16[128,3456]{1,0:T(8,128)(2,1)} %bitcast.145), channel_id=1, source_target_pairs={{0,16},{16,0},{8,24},{24,8},{1,17},{17,1},{9,25},{25,9},{2,18},{18... | collective-permute-start | bytes 2654216 | tf_op jit(solution)/shard_map/ppermute | solution.py:1530
  697.5 49.2 %collective-permute-start.101 = (f32[128,3456]{1,0:T(8,128)S(1)}, f32[128,3456]{1,0:T(8,128)S(1)}, u32[]{:S(2)}, u32[]{:S(2)}) collective-permute-start(f32[128,3456]{1,0:T(8,128)S(1)} %summed.20), channel_id=1, source_target_pairs={{0,4},{4,0},{1,5},{5,1},{2,6},{6,2},{3,7},{7,3},{8,12},{12,8},{9,1... | collective-permute-start | bytes 5308424 | tf_op jit(solution)/shard_map/ppermute | solution.py:1536
  (211 other events, 2824.8 us)

commit v10 on v9

--- a/solution.py
+++ b/solution.py
@@ -645,7 +645,7 @@
             ],
         ),
         out_shape=[shape_of((2, tok, cols), BF16), shape_of((gq.shape[0], 128), F32)],
-        compiler_params=settings(2, 24),
+        compiler_params=settings(2, 60),
         cost_estimate=cost(False),
         name="head_back",
     )(info, grad_mine, grad_theirs, raw_mine, raw_theirs, cos_part, sin_part, gq, gk)
@@ -994,7 +994,7 @@
             shape_of((width, tok), BF16),
             shape_of((4, tok, feats), BF16),
         ],
-        compiler_params=settings(1, 32),
+        compiler_params=settings(1, 60),
         cost_estimate=cost(True),
         name="out_proj",
     )(info, *pieces, x, *mine, *theirs, gain)
@@ -1043,7 +1043,7 @@
         out_shape=[shape_of((tok, width), F32), shape_of((width, tok), BF16)]
         + [shape_of((tok, feats), BF16)] * 4
         + [shape_of((1, width), F32)],
-        compiler_params=settings(1, 32),
+        compiler_params=settings(1, 60),
         cost_estimate=cost(True),
         name="norm_two_back",
     )(info, *pieces, grad, resid, grad_result, gain)
@@ -1097,7 +1097,7 @@
             scratch_shapes=[pltpu.VMEM((4, width, cols), BF16), pltpu.SemaphoreType.DMA],
         ),
         out_shape=[shape_of((tile, width), BF16)] * 4 + [shape_of((1, width), F32)],
-        compiler_params=settings(1, 32),
+        compiler_params=settings(1, 60),
         cost_estimate=cost(True),
         name="norm_one_back",
     )(info, *pieces, *pairs, x, grad_resid, gain)
@@ -1171,13 +1171,22 @@
         @pl.when((step == s) & (part == 0))
         def _():
             pltpu.make_async_copy(gate_up.at[s], gate_up.at[s], sems.at[s, 0]).wait()
-            pltpu.make_async_copy(down.at[s], down.at[s], sems.at[s, 1]).wait()
 
     rows = pl.ds(pl.multiple_of(part * tile, tile), tile)
     act = dot(x_ref[rows, :], gate_up[step], 1, 0)
     for j, (gate, upper) in enumerate(split_act(act)):
-        hid_ref[0, :, j * third : (j + 1) * third] = (gate * sigmoid(gate) * upper).astype(BF16)
-    act_ref[0] = act.astype(BF16)
+        sig = sigmoid(gate)
+        silu = gate * sig
+        hid_ref[0, :, j * third : (j + 1) * third] = (silu * upper).astype(BF16)
+        at = 2 * j * third
+        act_ref[0, :, at : at + third] = (upper * (sig + silu - silu * sig)).astype(BF16)
+        act_ref[0, :, at + third : at + 2 * third] = silu.astype(BF16)
+    for s in range(len(plans)):
+
+        @pl.when((step == s) & (part == 0))
+        def _():
+            pltpu.make_async_copy(down.at[s], down.at[s], sems.at[s, 1]).wait()
+
     grown = dot(hid_ref[0], down[step], 1, 1)
 
     @pl.when(step == 0)
@@ -1313,16 +1322,11 @@
     def _():
         rows = pl.ds(pl.multiple_of(step * tile, tile), tile)
         grad_hidden = dot(low_ref[...], down[...], 1, 0)
-        for j, (gate, upper) in enumerate(split_act(act_ref[0])):
+        for j, (to_gate, to_upper) in enumerate(split_act(act_ref[0])):
             grad = grad_hidden[:, j * third : (j + 1) * third]
-            gate, upper = gate.astype(F32), upper.astype(F32)
-            sig = sigmoid(gate)
-            silu = gate * sig
             at = 2 * j * third
-            dact_all[rows, at : at + third] = (
-                grad * upper * (sig + silu - silu * sig)
-            ).astype(BF16)
-            dact_all[rows, at + third : at + 2 * third] = (grad * silu).astype(BF16)
+            dact_all[rows, at : at + third] = (grad * to_gate.astype(F32)).astype(BF16)
+            dact_all[rows, at + third : at + 2 * third] = (grad * to_upper.astype(F32)).astype(BF16)
         hid_all[rows, :] = hid_ref[0]
 
         @pl.when(step == 0)
@@ -1419,10 +1423,71 @@
         in_specs=[spec] * len(terms),
         out_specs=spec,
         out_shape=shape_of((rows, cols), dtype),
-        compiler_params=settings(1, 24),
+        compiler_params=settings(1, 60),
         cost_estimate=cost(False),
         name="summed",
     )(*terms)
+
+
+def sums_kernel(jobs, count, info, *refs):
+    arrays, refs = refs[:count], refs[count:]
+    outs, (term_buf, out_buf, term_sems, out_sems) = refs[: len(jobs)], refs[len(jobs) :]
+    rows = term_buf.shape[1]
+    copies = []
+    for terms in jobs:
+        group = []
+        for array, base, pick, _ in terms:
+            at = base
+            if pick is not None:
+                at = pl.multiple_of(base + jnp.bitwise_xor(info[2], pick) * rows, rows)
+            i = len(copies) + len(group)
+            src = arrays[array].at[pl.ds(at, rows)]
+            group.append(pltpu.make_async_copy(src, term_buf.at[i], term_sems.at[i]))
+            group[-1].start()
+        copies += group
+    first = 0
+    stores = []
+    for j, terms in enumerate(jobs):
+        total = None
+        for i, (_, _, _, turn) in enumerate(terms):
+            copies[first + i].wait()
+            value = term_buf[first + i].astype(F32)
+            value = turn_chunks(value) if turn else value
+            total = value if total is None else total + value
+        first += len(terms)
+        out_buf[j] = total.astype(BF16)
+        stores.append(pltpu.make_async_copy(out_buf.at[j], outs[j], out_sems.at[j]))
+        stores[-1].start()
+    for store in stores:
+        store.wait()
+
+
+def sums(info, arrays, jobs):
+    cols = arrays[0].shape[1]
+    rows, terms = 128, sum(len(job) for job in jobs)
+    return pl.pallas_call(
+        functools.partial(sums_kernel, jobs, len(arrays)),
+        grid_spec=pltpu.PrefetchScalarGridSpec(
+            num_scalar_prefetch=1,
+            grid=(1,),
+            in_specs=[ANY] * len(arrays),
+            out_specs=[ANY] * len(jobs),
+            scratch_shapes=[
+                pltpu.VMEM((terms, rows, cols), BF16),
+                pltpu.VMEM((len(jobs), rows, cols), BF16),
+                pltpu.SemaphoreType.DMA((terms,)),
+                pltpu.SemaphoreType.DMA((len(jobs),)),
+            ],
+        ),
+        out_shape=[shape_of((rows, cols), BF16)] * len(jobs),
+        compiler_params=settings(1, 60),
+        cost_estimate=cost(False),
+        name="sums",
+    )(info, *arrays)
+
+
+def core_jobs(keep, came):
+    return [[(a, far * 256, pick, False) for a in (keep, came)] for far in (0, 1) for pick in (0, 1)]
 
 
 def core_sum_kernel(info, left_ref, right_ref, *outs):
@@ -1488,7 +1553,7 @@
             pl.BlockSpec(shape, lambda p, k: (jnp.where(p == 0, k, 3), 0, 0)),
         ],
         out_shape=[shape_of((4, width // 2, cols + feats), BF16)] * 2,
-        compiler_params=settings(2, 32),
+        compiler_params=settings(2, 60),
         cost_estimate=cost(True),
         name="weight_grad",
     )(normed_t, *backs, grad_t, attended)
@@ -1559,7 +1624,6 @@
     w_proj = join(q_weight, k_weight, v_weight)
     proj_z = [z_up(w_proj), z_far(w_proj), z_down(w_proj)]
     proj_far = x_swap(w_proj)
-    proj_core = core_swap(w_proj)
     count_here = jnp.sum(lengths).astype(F32)[None]
     vector = jnp.concatenate([attn_gain, ffn_gain, q_gain, k_gain]).astype(F32)
     vector = jnp.concatenate([vector, count_here, jnp.zeros((640 - 545,), F32)])[None]
@@ -1572,9 +1636,7 @@
     head_gains = natural(vector[:, 2 * quarter : 544])
     v.update(
         info=info,
-        w_proj=w_proj,
-        proj_far=proj_far,
-        proj_core=proj_core,
+        proj_own=jnp.concatenate([w_proj, proj_far], axis=0),
         proj_z=jnp.concatenate(proj_z, axis=0),
         w_out=w_out,
         w_ffn=w_ffn,
@@ -1592,21 +1654,21 @@
 
     proj_zfar = x_swap(v["proj_z"])
     out_z = [z_up(v["w_out"]), z_far(v["w_out"]), z_down(v["w_out"])]
-    proj_cores = [v["proj_core"], core_swap(v["proj_far"])]
+    own_core = core_swap(v["proj_own"])
     x_in, normed_one_t = norm_one(info, tokens, v["gain_one"], 256)
     v.update(
         proj_zfar=proj_zfar,
-        proj_cores=proj_cores,
+        own_core=own_core,
         x_in=x_in,
         normed_one_t=normed_one_t,
         out_z=out_z,
     )
     sync()
 
-    proj_cores = v["proj_cores"] + [core_swap(v["proj_z"]), core_swap(v["proj_zfar"])]
-    plan_proj = [[(0, 0), (1, 0), (4, 0), (5, 0)]]
-    plan_proj += [[(p, k * quarter) for p in (2, 3, 6, 7)] for k in range(3)]
-    weights_proj = [v["w_proj"], v["proj_far"], v["proj_z"], v["proj_zfar"]] + proj_cores
+    plan_proj = [[(0, 0), (0, quarter), (3, 0), (3, quarter)]]
+    plan_proj += [[(p, k * quarter) for p in (1, 2, 4, 5)] for k in range(3)]
+    weights_proj = [v["proj_own"], v["proj_z"], v["proj_zfar"], v["own_core"]]
+    weights_proj += [core_swap(v["proj_z"]), core_swap(v["proj_zfar"])]
     one = [z_up(v["w_chunks"][0]), z_up(v["w_chunks"][3])]
     ffn_far = x_swap(v["w_ffn"])
     tables = [v[name] for name in ("cos_part", "sin_part", "gain_q", "gain_k")]
@@ -1770,9 +1832,6 @@
             256,
         )
 
-    def sum_of(k):
-        return [p[0] for p in core_sum(info, v[f"keep{k}"][None], v[f"came{k}"][None])]
-
     turned = [False, False, True]
     one = [z_up(v["results"][0])]
     total, keep2, send2 = ffn_back(plan_mixed, "weights2", "acts_c", "hiddens_c", 0, None)
@@ -1787,7 +1846,7 @@
 
     out_three = [z_down(v["results"][0])]
     came1 = core_swap(v["send1"])
-    sum2 = sum_of(2)
+    sum2 = sums(info, [v["keep2"], v["came2"]], core_jobs(0, 1))
     far_t2 = x_swap(sum2[3])
     total, keep3, send3 = ffn_back(
         plan_chunks, "weights3", "acts_b", "hiddens_b", 0, after(v["total"], sum2[0])
@@ -1806,8 +1865,12 @@
     out_three = v["out_three"] + [z_down(v["results"][1])]
     came3 = core_swap(v["send3"])
     far_h2 = x_swap(v["sum2"][2])
-    there2 = y_swap(summed([v["sum2"][1], v["far_t2"]]))
-    sum1 = sum_of(1)
+    there2, *sum1 = sums(
+        info,
+        [v["sum2"][1], v["far_t2"], v["keep1"], v["came1"]],
+        [[(0, 0, None, False), (1, 0, None, False)]] + core_jobs(2, 3),
+    )
+    there2 = y_swap(there2)
     total, keep0, send0 = ffn_back(
         plan0, "weights0", "acts_a", "hiddens_a", 0, after(v["total"], sum1[0])
     )
@@ -1825,8 +1888,13 @@
 
     came0 = core_swap(v["send0"])
     far_t1 = x_swap(v["sum1"][3])
-    down2 = z_down(summed([v["sum2"][0], v["far_h2"], v["there2"]], turned))
-    sum3 = sum_of(3)
+    plane = [(0, 0, None, False), (1, 0, None, False), (2, 0, None, True)]
+    part2, *sum3 = sums(
+        info,
+        [v["sum2"][0], v["far_h2"], v["there2"], v["keep3"], v["came3"]],
+        [plane] + core_jobs(3, 4),
+    )
+    down2 = z_down(part2)
     grad_resid, grad_attn_t, a0, a1, b0, b1, gain_two_sum = norm_two_back(
         info,
         after(v["total"], sum3[0]),
@@ -1858,9 +1926,13 @@
 
     two = [z_up(v["one"][0])]
     far_h1 = x_swap(v["sum1"][2])
-    there1 = y_swap(summed([v["sum1"][1], v["far_t1"]]))
+    there1, *sum0 = sums(
+        info,
+        [v["sum1"][1], v["far_t1"], v["keep0"], v["came0"]],
+        [[(0, 0, None, False), (1, 0, None, False)]] + core_jobs(2, 3),
+    )
+    there1 = y_swap(there1)
     far_t3 = x_swap(v["sum3"][3])
-    sum0 = sum_of(0)
     back0 = attn_back(0, after(v["grad_mine"][0], sum0[0]))
     v.update(
         out_two=two,
@@ -1877,9 +1949,13 @@
     heads0 = y_swap(v["back0"][1])
     far_h3 = x_swap(v["sum3"][2])
     far_t0 = x_swap(v["sum0"][3])
-    there3 = summed([v["sum3"][1], v["far_t3"]])
-    two_down = summed(
-        [v["sum1"][0], v["far_h1"], v["there1"], v["down2"]], [False, False, True, False]
+    there3, two_down = sums(
+        info,
+        [v["sum3"][1], v["far_t3"], v["sum1"][0], v["far_h1"], v["there1"], v["down2"]],
+        [
+            [(0, 0, None, False), (1, 0, None, False)],
+            [(2, 0, None, False), (3, 0, None, False), (4, 0, None, True), (5, 0, None, False)],
+        ],
     )
     there3_got = y_swap(there3)
     two_down_got = z_down(two_down)
@@ -1891,15 +1967,20 @@
 
     heads1 = y_swap(v["back1"][1])
     far_h0 = x_swap(v["sum0"][2])
-    up3 = z_up(summed([v["sum3"][0], v["far_h3"], v["there3"]], turned))
+    part3, there0 = sums(
+        info,
+        [v["sum3"][0], v["far_h3"], v["there3"], v["sum0"][1], v["far_t0"]],
+        [plane, [(3, 0, None, False), (4, 0, None, False)]],
+    )
+    up3 = z_up(part3)
     tables = [v[name] for name in ("cos_part", "sin_part", "gain_q", "gain_k")]
     head0 = head_back(
         info, v["back0"][0], v["heads0"], v["mine"][0][1], v["theirs"][0][1], *tables, heads
     )
-    v.update(heads1=heads1, two_down=two_down_got, head0=head0)
-    sync()
-
-    there0 = y_swap(summed([v["sum0"][1], v["far_t0"]]))
+    v.update(heads1=heads1, two_down=two_down_got, head0=head0, there0=there0)
+    sync()
+
+    there0 = y_swap(v["there0"])
     head1 = head_back(
         info, v["back1"][0], v["heads1"], v["mine"][1][1], v["theirs"][1][1], *tables, heads
     )
@@ -1946,26 +2027,30 @@
     v.update(vector=vector)
     sync()
 
-    one = v["one"] + [z_up(part) for part in v["tokens_low"][1:3]]
+    one = v["one"] + [z_up(v["tokens_low"][1])]
     rows = quarter // 2
     flat = lambda a: a.reshape(4 * rows, a.shape[-1])
-    sums = [flat(p) for p in core_sum(info, v["keep"], core_swap(v["send"]))]
-    far_t = x_swap(sums[3])
+    attn_sums = [flat(p) for p in core_sum(info, v["keep"], core_swap(v["send"]))]
+    vector = v["vector"] + x_swap(v["vector"])
+    v.update(one=one, sums=attn_sums, vector=vector)
+    sync()
+
+    one = v["one"] + [z_up(v["tokens_low"][2])]
+    far_t = x_swap(v["sums"][3])
     part0 = summed([v["sum0"][0], v["far_h0"], v["there0"]], turned)
     ffn_sum = summed([part0, v["two_down"], v["up3"]], None, F32)
-    vector = v["vector"] + x_swap(v["vector"])
-    v.update(one=one, sums=sums, far_t=far_t, ffn_sum=ffn_sum, vector=vector)
+    vector = v["vector"] + y_swap(v["vector"])
+    v.update(one=one, far_t=far_t, ffn_sum=ffn_sum, vector=vector)
     sync()
 
     one = v["one"] + [z_up(v["tokens_low"][3])]
     three = [z_down(v["tokens_low"][0])]
     far_h = x_swap(v["sums"][2])
     there = y_swap(summed([v["sums"][1], v["far_t"]]))
-    vector = v["vector"] + y_swap(v["vector"])
     output = jnp.zeros((rows_dev, tok, width), BF16)
     for k, parts in enumerate((v["results"], v["out_one"], v["out_two"], v["out_three"])):
         output = place(output, parts, k, 0)
-    v.update(one=one, three=three, far_h=far_h, there=there, vector=vector, output=output)
+    v.update(one=one, three=three, far_h=far_h, there=there, output=output)
     sync()
 
     three = v["three"] + [z_down(v["tokens_low"][1])]
@@ -1984,39 +2069,45 @@
     v.update(three=three, attn_sum=attn_sum, vector=vector, grad=grad, ffn_other=ffn_other)
     sync()
 
+    def finish(own, other):
+        return jnp.concatenate(
+            [jnp.where(ctx == 0, own, other), jnp.where(ctx == 0, other, own)], axis=0
+        )
+
+    def columns(first):
+        parts = [ffn_grad[:, first(j) : first(j) + third] for j in range(3)]
+        return jnp.concatenate(
+            [
+                jnp.where(ctx == 0, parts[0], parts[2]),
+                parts[1],
+                jnp.where(ctx == 0, parts[2], parts[0]),
+            ],
+            axis=1,
+        )
+
     two = [z_up(part) for part in v["one"][:2]]
+    third = units // 3
+    ffn_grad = finish(v["ffn_sum"], turn_chunks(v["ffn_other"]))
+    grad_gate = columns(lambda j: 2 * j * third)
+    grad_up = columns(lambda j: (2 * j + 1) * third)
+    grad_down = columns(lambda j: 2 * units + j * third).T
     attn_other = y_swap(v["attn_sum"])
     vector = v["vector"] + lax.ppermute(v["vector"], "tp", Z_FAR)
     grad = place(v["grad"], v["three"], 3, 0)
     v.update(two=two, vector=vector, grad=grad, attn_other=attn_other)
+    v.update(grad_gate=grad_gate, grad_up=grad_up, grad_down=grad_down)
     sync()
 
     two = [z_up(part) for part in v["one"][2:]]
     tokens_grad = place(place(v["grad"], v["two"], 2, 0), two, 2, 2)
     output = v["output"]
-    sums = v["vector"][0]
-
-    def finish(own, other):
-        return jnp.concatenate(
-            [jnp.where(ctx == 0, own, other), jnp.where(ctx == 0, other, own)], axis=0
-        )
-
-    ffn_grad = finish(v["ffn_sum"], turn_chunks(v["ffn_other"]))
+    sums_all = v["vector"][0]
+
     attn_grad = finish(v["attn_sum"], v["attn_other"])
-    teacher_loss = sums[2 * width + 2 * hd] / (v["total_count"] * width)
+    teacher_loss = sums_all[2 * width + 2 * hd] / (v["total_count"] * width)
 
     def own_part(at, size):
-        return lax.dynamic_slice_in_dim(sums, at + fsdp * (size // 4), size // 4, 0)
-
-    third = units // 3
-
-    def columns(first):
-        starts = [first(j) for j in range(3)]
-        parts = [ffn_grad[:, s : s + third] for s in starts]
-        return jnp.concatenate(
-            [jnp.where(ctx == 0, parts[0], parts[2]), parts[1], jnp.where(ctx == 0, parts[2], parts[0])],
-            axis=1,
-        )
+        return lax.dynamic_slice_in_dim(sums_all, at + fsdp * (size // 4), size // 4, 0)
 
     return (
         output,
@@ -2030,9 +2121,9 @@
         own_part(2 * width + hd, hd),
         attn_grad[:, proj:].T,
         own_part(width, width),
-        columns(lambda j: 2 * j * third),
-        columns(lambda j: (2 * j + 1) * third),
-        columns(lambda j: 2 * units + j * third).T,
+        v["grad_gate"],
+        v["grad_up"],
+        v["grad_down"],
     )
 
 

time: 812 us -> 796 us (0.980)
  waiting for transfers between devices: 176 us -> 143 us
  Pallas kernels: 396 us -> 411 us
  local copies, waits for them, and re-layouts: 98.6 us -> 86.9 us
  other arithmetic: 26 us -> 35.5 us
    unnamed x263 -> x193, local copies, waits for them, and re-layouts: 75.2 us -> 41.1 us
    pallas_call x0 -> x6, Pallas kernels: none -> 33.5 us  [sums(): pl.pallas_call(functools.partial(sums_kernel, jobs, len(arrays)), grid_sp...]
    pallas_call x5 -> x1, Pallas kernels: 27.6 us -> 2.28 us  [core_sum(): pl.pallas_call(core_sum_kernel, grid_spec=pltpu.PrefetchScalarGridSpec(nu...]
    ppermute x22, waiting for transfers between devices: 22.5 us -> 9.83 us  [x_swap(): return lax.ppermute(v, 'fsdp', X_SWAP)]
    dynamic_update_slice x16, other arithmetic: 13.1 us -> 24.7 us  [place(): lax.dynamic_update_slice(out, part.astype(out.dtype)[None], (row, at, 0))]
    ppermute x14, waiting for transfers between devices: 50.6 us -> 40.3 us  [z_down(): return lax.ppermute(v, 'tp', Z_DOWN)]
    ppermute x3, waiting for transfers between devices: 10.8 us -> 1.69 us  [z_far(): return lax.ppermute(v, 'tp', Z_FAR)]
    pallas_call x12 -> x5, Pallas kernels: 23.8 us -> 15.5 us  [summed(): pl.pallas_call(functools.partial(sum_kernel, turns or [False] * len(terms...]
  transfers between devices with their start and end apart: 111 -> 110, of which waited for: 30 -> 30; matrix products, arithmetic and copies ran while one was open for 5% -> 10% of each run, Pallas kernels for 44% -> 46%
where the time goes in v10:
time: 796 us; the launch traced here: 785 us
  Pallas kernels  411 us (52%)
  waiting for transfers between devices  143 us (18%)
  starting transfers between devices  102 us (13%)
  local copies, waits for them, and re-layouts  86.9 us (11%)
  other arithmetic  35.5 us (4%)
    pallas_call x4, Pallas kernels, ffn_bwd(): pl.pallas_call(functools.partial(ffn_bwd_kernel, steps, plan, first), gri...  101 us
    pallas_call x2, Pallas kernels, attn_bwd(): pl.pallas_call(functools.partial(attn_bwd_kernel, width, hd), grid_spec=p...  76.5 us
    pallas_call x3, Pallas kernels, ffn_fwd(): pl.pallas_call(functools.partial(ffn_fwd_kernel, tile, [plan for plan, _...  63 us
    ppermute x20, waiting for transfers between devices, z_up(): return lax.ppermute(v, 'tp', Z_UP)  58.1 us
    unnamed x193, local copies, waits for them, and re-layouts  41.1 us
    ppermute x14, waiting for transfers between devices, z_down(): return lax.ppermute(v, 'tp', Z_DOWN)  40.3 us
    pallas_call x2, Pallas kernels, attn_fwd(): pl.pallas_call(functools.partial(attn_fwd_kernel, width, hd), grid_spec=p...  34.1 us
    pallas_call x6, Pallas kernels, sums(): pl.pallas_call(functools.partial(sums_kernel, jobs, len(arrays)), grid_sp...  33.5 us
  transfers between devices with their start and end apart: 110, of which 30 were waited for; matrix products, arithmetic and copies ran while one was open for 10% of the time, Pallas kernels for 46%

profile of v10, /device:TPU:0, one launch (start us, length us, event | category | flops | bytes accessed | tf_op | source)
XLA Modules:
  0.0 784.8 jit_solution(6136059983491092900)
XLA Ops:
  81.1 12.2 %collective-permute-done.15.rest_4_.rest_0_ = bf16[256,1152]{1,0:T(8,128)(2,1)} collective-permute-done((bf16[256,1152]{1,0:T(8,128)(2,1)}, bf16[256,1152]{1,0:T(8,128)(2,1)}, u32[]{:S(2)}, u32[]{:S(2)}) %collective-permute-start.15) | collective-permute-done | bytes 589856 | tf_op jit(solution)/shard_map/ppermute | solution.py:1604
  95.6 17.0 %attn_fwd.2 = (bf16[1024,256]{1,0:T(8,128)(2,1)}, bf16[1024,256]{1,0:T(8,128)(2,1)}, f32[2,2,2048]{2,1,0:T(2,128)}) custom-call(s32[4]{0:T(128)} %copy-done.22, bf16[512,1024]{1,0:T(8,128)(2,1)} %copy-done.29, bf16[512,1024]{1,0:T(8,128)(2,1)} %copy-done.73), custom_call_target="tpu_custom_call" | custom-call | flops 4398046511104 | bytes 1073741824 | tf_op jit(solution)/shard_map/attn_fwd/pallas_call | solution.py:755
  121.0 17.0 %attn_fwd.3 = (bf16[1024,256]{1,0:T(8,128)(2,1)}, bf16[1024,256]{1,0:T(8,128)(2,1)}, f32[2,2,2048]{2,1,0:T(2,128)}) custom-call(s32[4]{0:T(128)} %copy-done.22, bf16[512,1024]{1,0:T(8,128)(2,1)} %copy-done.28, bf16[512,1024]{1,0:T(8,128)(2,1)} %collective-permute-done.17.got_ref), custom_call_target="tpu_custom_call" | custom-call | flops 4398046511104 | bytes 1073741824 | tf_op jit(solution)/shard_map/attn_fwd/pallas_call | solution.py:755
  143.0 11.8 %collective-permute-done.27.refs_8_ = bf16[1024,256]{1,0:T(8,128)(2,1)S(1)} collective-permute-done((bf16[1024,256]{1,0:T(8,128)(2,1)}, bf16[1024,256]{1,0:T(8,128)(2,1)S(1)}, u32[]{:S(2)}, u32[]{:S(2)}) %collective-permute-start.27) | collective-permute-done | bytes 524320 | tf_op jit(solution)/shard_map/ppermute | solution.py:1601
  159.0 10.4 %out_proj.1 = (f32[1024,1024]{1,0:T(8,128)}, bf16[1024,1024]{1,0:T(8,128)(2,1)}, bf16[1024,1024]{1,0:T(8,128)(2,1)}, bf16[4,1024,256]{2,1,0:T(8,128)(2,1)}) custom-call(s32[4]{0:T(128)} %copy-done.22, bf16[1024,256]{1,0:T(8,128)(2,1)} %constant_dynamic-update-slice_fusion.refs_0_, bf16[1024,256]{1,0:T(8,128)(2,1)} %collective-permute-done.25.refs_1_, ...), custom_call_target="tpu_custom_call" | custom-call | flops 4398046511104 | bytes 1073741824 | tf_op jit(solution)/shard_map/out_proj/pallas_call | solution.py:974
  180.0 27.3 %ffn_fwd.3 = (bf16[2,1024,2304]{2,1,0:T(8,128)(2,1)}, bf16[2,1024,1152]{2,1,0:T(8,128)(2,1)}, f32[1024,1024]{1,0:T(8,128)}) custom-call(s32[4]{0:T(128)} %copy-done.22, f32[1]{0:T(128)} %bitcast.4.scale, bf16[1024,1024]{1,0:T(8,128)(2,1)} %get-tuple-element.1897.x_ref, f32[1024,1024]{1,0:T(8,128)} %get-tuple-element.2452.in_ref.refs_5_, ...), custom_call_target="tpu_custom_call" | custom-call | flops 4398046511104 | bytes 1073741824 | tf_op jit(solution)/shard_map/ffn_fwd/pallas_call | solution.py:1282
  214.6 15.9 %ffn_fwd.4 = (bf16[1,1024,2304]{2,1,0:T(8,128)(2,1)}, bf16[1,1024,1152]{2,1,0:T(8,128)(2,1)}, f32[1024,1024]{1,0:T(8,128)}) custom-call(s32[4]{0:T(128)} %copy-done.22, f32[1]{0:T(128)} %bitcast.4.scale, bf16[1024,1024]{1,0:T(8,128)(2,1)} %get-tuple-element.1897.x_ref, f32[1024,1024]{1,0:T(8,128)} %get-tuple-element.1799.in_ref, ...), custom_call_target="tpu_custom_call" | custom-call | flops 4398046511104 | bytes 1073741824 | tf_op jit(solution)/shard_map/ffn_fwd/pallas_call | solution.py:1282
  234.5 19.8 %ffn_fwd.5 = (bf16[1,1024,2304]{2,1,0:T(8,128)(2,1)}, bf16[1,1024,1152]{2,1,0:T(8,128)(2,1)}, bf16[512,1024]{1,0:T(8,128)(2,1)}, bf16[512,1024]{1,0:T(8,128)(2,1...) custom-call(s32[4]{0:T(128)} %copy-done.22, ...), custom_call_target="tpu_custom_call" | custom-call | flops 4398046511104 | bytes 1073741824 | tf_op jit(solution)/shard_map/ffn_fwd/pallas_call | solution.py:1282
  254.6 24.9 %ffn_bwd.4 = (f32[1024,1024]{1,0:T(8,128)}, bf16[512,3456]{1,0:T(8,128)(2,1)}, bf16[512,3456]{1,0:T(8,128)(2,1)}) custom-call(bf16[1024,1024]{1,0:T(8,128)(2,1)} %get-tuple-element.2375.low_ref, bf16[1,1024,2304]{2,1,0:T(8,128)(2,1)} %get-tuple-element.2016.act_ref, bf16[1,1024,1152]{2,1,0:T(8,128)(2,1)} %get-tuple-element.2036.hid_ref, ...), custom_call_target="tpu_custom_call" | custom-call | flops 4398046511104 | bytes 1073741824 | tf_op jit(solution)/shard_map/ffn_bwd/pallas_call | solution.py:1364
  281.9 25.4 %ffn_bwd.5 = (f32[1024,1024]{1,0:T(8,128)}, bf16[512,3456]{1,0:T(8,128)(2,1)}, bf16[512,3456]{1,0:T(8,128)(2,1)}) custom-call(bf16[1024,1024]{1,0:T(8,128)(2,1)} %get-tuple-element.2375.low_ref, bf16[2,1024,2304]{2,1,0:T(8,128)(2,1)} %get-tuple-element.2359.act_ref, ...), custom_call_target="tpu_custom_call", output_to_operand_aliasing={{0}: (15, {})} | custom-call | flops 4398046511104 | bytes 1073741824 | tf_op jit(solution)/shard_map/ffn_bwd/pallas_call | solution.py:1364
  317.9 25.4 %ffn_bwd.6 = (f32[1024,1024]{1,0:T(8,128)}, bf16[512,3456]{1,0:T(8,128)(2,1)}, bf16[512,3456]{1,0:T(8,128)(2,1)}) custom-call(bf16[1024,1024]{1,0:T(8,128)(2,1)} %get-tuple-element.2375.low_ref, bf16[1,1024,2304]{2,1,0:T(8,128)(2,1)} %get-tuple-element.2283.act_ref, ...), custom_call_target="tpu_custom_call", output_to_operand_aliasing={{0}: (17, {})} | custom-call | flops 4398046511104 | bytes 1073741824 | tf_op jit(solution)/shard_map/ffn_bwd/pallas_call | solution.py:1364
  354.2 25.3 %ffn_bwd.7 = (f32[1024,1024]{1,0:T(8,128)}, bf16[512,3456]{1,0:T(8,128)(2,1)}, bf16[512,3456]{1,0:T(8,128)(2,1)}) custom-call(bf16[1024,1024]{1,0:T(8,128)(2,1)} %get-tuple-element.2375.low_ref, bf16[2,1024,2304]{2,1,0:T(8,128)(2,1)} %get-tuple-element.2359.act_ref, ...), custom_call_target="tpu_custom_call", output_to_operand_aliasing={{0}: (9, {})} | custom-call | flops 4398046511104 | bytes 1073741824 | tf_op jit(solution)/shard_map/ffn_bwd/pallas_call | solution.py:1364
  388.5 12.4 %norm_two_back.1 = (f32[1024,1024]{1,0:T(8,128)}, bf16[1024,1024]{1,0:T(8,128)(2,1)}, bf16[1024,256]{1,0:T(8,128)(2,1)}, bf16[1024,256]{1,0:T(8,128)(2,1)}, bf16...) custom-call(s32[4]{0:T(128)} %copy-done.22, ...), custom_call_target="tpu_custom_call" | custom-call | flops 4398046511104 | bytes 1073741824 | tf_op jit(solution)/shard_map/norm_two_back/pallas_call | solution.py:1032
  403.0 12.9 %collective-permute-done.68.gs_ref = bf16[1024,256]{1,0:T(8,128)(2,1)S(1)} collective-permute-done((bf16[1024,256]{1,0:T(8,128)(2,1)}, bf16[1024,256]{1,0:T(8,128)(2,1)S(1)}, u32[]{:S(2)}, u32[]{:S(2)}) %collective-permute-start.68) | collective-permute-done | bytes 524320 | tf_op jit(solution)/shard_map/ppermute | solution.py:1601
  426.7 38.2 %attn_bwd.2 = (bf16[512,1024]{1,0:T(8,128)(2,1)}, bf16[512,1024]{1,0:T(8,128)(2,1)}) custom-call(s32[4]{0:T(128)} %copy-done.22, bf16[512,1024]{1,0:T(8,128)(2,1)} %copy-done.29, bf16[512,1024]{1,0:T(8,128)(2,1)} %copy-done.73, bf16[1024,256]{1,0:T(8,128)(2,1)} %get-tuple-element.2498.refs_5_.ok_ref, bf16[1024,256]{1,0:T(8,128)(2,1)} %get-tuple-element.2499.os_ref, ...), custom_call_target="tpu_custom_call" | custom-call | flops 4398046511104 | bytes 1073741824 | tf_op jit(solution)/shard_map/attn_bwd/pallas_call | solution.py:909
  473.4 38.3 %attn_bwd.3 = (bf16[512,1024]{1,0:T(8,128)(2,1)}, bf16[512,1024]{1,0:T(8,128)(2,1)}) custom-call(s32[4]{0:T(128)} %copy-done.22, bf16[512,1024]{1,0:T(8,128)(2,1)} %copy-done.28, bf16[512,1024]{1,0:T(8,128)(2,1)} %collective-permute-done.17.got_ref, bf16[1024,256]{1,0:T(8,128)(2,1)} %get-tuple-element.2562.refs_6_.ok_ref, ...), custom_call_target="tpu_custom_call" | custom-call | flops 4398046511104 | bytes 1073741824 | tf_op jit(solution)/shard_map/attn_bwd/pallas_call | solution.py:909
  527.8 21.0 %collective-permute-done.80.refs_1_ = bf16[128,3456]{1,0:T(8,128)(2,1)S(1)} collective-permute-done((bf16[128,3456]{1,0:T(8,128)(2,1)S(1)}, bf16[128,3456]{1,0:T(8,128)(2,1)S(1)}, u32[]{:S(2)}, u32[]{:S(2)}) %collective-permute-start.80) | collective-permute-done | bytes 884768 | tf_op jit(solution)/shard_map/ppermute | solution.py:1610
  556.7 13.2 %norm_one_back.1 = (bf16[256,1024]{1,0:T(8,128)(2,1)}, bf16[256,1024]{1,0:T(8,128)(2,1)}, bf16[256,1024]{1,0:T(8,128)(2,1)}, bf16[256,1024]{1,0:T(8,128)(2,1)}, f32[1,1024]{1,0:T(1,128)}) custom-call(s32[4]{0:T(128)} %copy-done.22, bf16[512,512]{1,0:T(8,128)(2,1)} %copy-done.2, bf16[768,512]{1,0:T(8,128)(2,1)} %copy-done.1, ...), custom_call_target="tpu_custom_call" | custom-call | flops 4398046511104 | bytes 1073741824 | tf_op jit(solution)/shard_map/norm_one_back/pallas_call | solution.py:1090
  574.8 15.2 %weight_grad.1 = (bf16[4,512,768]{2,1,0:T(8,128)(2,1)}, bf16[4,512,768]{2,1,0:T(8,128)(2,1)}) custom-call(bf16[1024,1024]{1,0:T(8,128)(2,1)} %copy-done, bf16[2,1024,512]{2,1,0:T(8,128)(2,1)} %get-tuple-element.2703.refs_6_.back0_ref, bf16[2,1024,512]{2,1,0:T(8,128)(2,1)} %get-tuple-element.2705.refs_7_.back1_ref, ...), custom_call_target="tpu_custom_call" | custom-call | flops 4398046511104 | bytes 1073741824 | tf_op jit(solution)/shard_map/weight_grad/pallas_call | solution.py:1547
  615.4 7.7 collective-permute-done.90
  672.4 8.3 %broadcast_in_dim.157 = f32[4,1024,1024]{2,1,0:T(8,128)} broadcast(f32[]{:T(128)} %constant.92.clone.1), dimensions={} | broadcast | bytes 16777220 | tf_op jit(solution)/shard_map/broadcast_in_dim | solution.py:2061
  709.8 10.1 %collective-permute-done.102 = bf16[256,1024]{1,0:T(8,128)(2,1)} collective-permute-done((bf16[256,1024]{1,0:T(8,128)(2,1)S(1)}, bf16[256,1024]{1,0:T(8,128)(2,1)}, u32[]{:S(2)}, u32[]{:S(2)}) %collective-permute-start.102) | collective-permute-done | bytes 524320 | tf_op jit(solution)/shard_map/ppermute | solution.py:1610
  744.3 9.2 %collective-permute-done.106 = bf16[256,1024]{1,0:T(8,128)(2,1)S(1)} collective-permute-done((bf16[256,1024]{1,0:T(8,128)(2,1)}, bf16[256,1024]{1,0:T(8,128)(2,1)S(1)}, u32[]{:S(2)}, u32[]{:S(2)}) %collective-permute-start.106) | collective-permute-done | bytes 524320 | tf_op jit(solution)/shard_map/ppermute | solution.py:1604
  765.2 7.6 collective-permute-done.108
  (512 shorter events, 352.0 us)
Async XLA Ops:
  50.0 43.3 %collective-permute-start.11 = (bf16[256,3456]{1,0:T(8,128)(2,1)}, bf16[256,3456]{1,0:T(8,128)(2,1)}, u32[]{:S(2)}, u32[]{:S(2)}) collective-permute-start(bf16[256,3456]{1,0:T(8,128)(2,1)} %get-tuple-element.2380.rest_0_), channel_id=1, source_target_pairs={{0,16},{16,0},{8,24},{24,8},{1,17},{17,1},{9,25},{25,9},{2,18},{18... | collective-permute-start | bytes 5308424 | tf_op jit(solution)/shard_map/ppermute | solution.py:1595
  50.8 42.4 %collective-permute-start.16 = (bf16[256,2304]{1,0:T(8,128)(2,1)}, bf16[256,2304]{1,0:T(8,128)(2,1)}, u32[]{:S(2)}, u32[]{:S(2)}) collective-permute-start(bf16[256,2304]{1,0:T(8,128)(2,1)} %get-tuple-element.1485), channel_id=1, source_target_pairs={{0,1},{1,2},{2,3},{3,0},{4,5},{5,6},{6,7},{7,4},{8,9},{9,10},{10,1... | collective-permute-start | bytes 3538952 | tf_op jit(solution)/shard_map/ppermute | solution.py:1604
  68.9 43.7 %collective-permute-start.17 = (bf16[512,1024]{1,0:T(8,128)(2,1)}, bf16[512,1024]{1,0:T(8,128)(2,1)}, u32[]{:S(2)}, u32[]{:S(2)}) collective-permute-start(bf16[512,1024]{1,0:T(8,128)(2,1)} %get-tuple-element.1477), channel_id=1, source_target_pairs={{0,4},{4,0},{1,5},{5,1},{2,6},{6,2},{3,7},{7,3},{8,12},{12,8},{9,1... | collective-permute-start | bytes 3145736 | tf_op jit(solution)/shard_map/ppermute | solution.py:1601
  175.1 32.2 %collective-permute-start.41 = (bf16[256,2304]{1,0:T(8,128)(2,1)}, bf16[256,2304]{1,0:T(8,128)(2,1)}, u32[]{:S(2)}, u32[]{:S(2)}) collective-permute-start(bf16[256,2304]{1,0:T(8,128)(2,1)} %collective-permute-done.16.rest_5_.rest_1_), channel_id=1, source_target_pairs={{0,1},{1,2},{2,3},{3,0},{4,5},{5,6},{6,7},{7,4},{8,9},{9,10},{10,1... | collective-permute-start | bytes 3538952 | tf_op jit(solution)/shard_map/ppermute | solution.py:1604
  175.1 32.1 %collective-permute-start.38 = (bf16[256,1152]{1,0:T(8,128)(2,1)}, bf16[256,1152]{1,0:T(8,128)(2,1)}, u32[]{:S(2)}, u32[]{:S(2)}) collective-permute-start(bf16[256,1152]{1,0:T(8,128)(2,1)} %collective-permute-done.21.rest_0_), channel_id=1, source_target_pairs={{0,8},{8,0},{16,24},{24,16},{1,9},{9,1},{17,25},{25,17},{2,10},{10... | collective-permute-start | bytes 1769480 | tf_op jit(solution)/shard_map/ppermute | solution.py:1598
  175.6 31.7 %collective-permute-start.39 = (bf16[256,1152]{1,0:T(8,128)(2,1)}, bf16[256,1152]{1,0:T(8,128)(2,1)}, u32[]{:S(2)}, u32[]{:S(2)}) collective-permute-start(bf16[256,1152]{1,0:T(8,128)(2,1)} %collective-permute-done.26.rest_1_), channel_id=1, source_target_pairs={{0,16},{16,0},{8,24},{24,8},{1,17},{17,1},{9,25},{25,9},{2,18},{18... | collective-permute-start | bytes 1769480 | tf_op jit(solution)/shard_map/ppermute | solution.py:1595
  176.0 31.3 %collective-permute-start.40 = (bf16[256,1152]{1,0:T(8,128)(2,1)}, bf16[256,1152]{1,0:T(8,128)(2,1)}, u32[]{:S(2)}, u32[]{:S(2)}) collective-permute-start(bf16[256,1152]{1,0:T(8,128)(2,1)} %collective-permute-done.35.rest_3_), channel_id=1, source_target_pairs={{0,4},{4,0},{1,5},{5,1},{2,6},{6,2},{3,7},{7,3},{8,12},{12,8},{9,1... | collective-permute-start | bytes 1769480 | tf_op jit(solution)/shard_map/ppermute | solution.py:1601
  349.7 29.8 %collective-permute-start.64 = (bf16[128,3456]{1,0:T(8,128)(2,1)}, bf16[128,3456]{1,0:T(8,128)(2,1)}, u32[]{:S(2)}, u32[]{:S(2)}) collective-permute-start(bf16[128,3456]{1,0:T(8,128)(2,1)} %get-tuple-element.2414), channel_id=1, source_target_pairs={{0,4},{4,0},{1,5},{5,1},{2,6},{6,2},{3,7},{7,3},{8,12},{12,8},{9,1... | collective-permute-start | bytes 2654216 | tf_op jit(solution)/shard_map/ppermute | solution.py:1601
  386.2 29.8 %collective-permute-start.66 = (bf16[128,3456]{1,0:T(8,128)(2,1)}, bf16[128,3456]{1,0:T(8,128)(2,1)}, u32[]{:S(2)}, u32[]{:S(2)}) collective-permute-start(bf16[128,3456]{1,0:T(8,128)(2,1)} %get-tuple-element.2436), channel_id=1, source_target_pairs={{0,3},{1,0},{2,1},{3,2},{4,7},{5,4},{6,5},{7,6},{8,11},{9,8},{10,9... | collective-permute-start | bytes 2654216 | tf_op jit(solution)/shard_map/ppermute | solution.py:1610
  402.5 62.3 %collective-permute-start.71 = (bf16[1024,256]{1,0:T(8,128)(2,1)}, bf16[1024,256]{1,0:T(8,128)(2,1)}, u32[]{:S(2)}, u32[]{:S(2)}) collective-permute-start(bf16[1024,256]{1,0:T(8,128)(2,1)} %get-tuple-element.2521), channel_id=1, source_target_pairs={{0,4},{4,0},{1,5},{5,1},{2,6},{6,2},{3,7},{7,3},{8,12},{12,8},{9,1... | collective-permute-start | bytes 1572872 | tf_op jit(solution)/shard_map/ppermute | solution.py:1601
  422.4 42.5 %collective-permute-start.73 = (bf16[128,3456]{1,0:T(8,128)(2,1)}, bf16[128,3456]{1,0:T(8,128)(2,1)}, u32[]{:S(2)}, u32[]{:S(2)}) collective-permute-start(bf16[128,3456]{1,0:T(8,128)(2,1)} %get-tuple-element.2548), channel_id=1, source_target_pairs={{0,4},{4,0},{1,5},{5,1},{2,6},{6,2},{3,7},{7,3},{8,12},{12,8},{9,1... | collective-permute-start | bytes 2654216 | tf_op jit(solution)/shard_map/ppermute | solution.py:1601
  424.0 40.9 %collective-permute-start.72 = (bf16[512,1024]{1,0:T(8,128)(2,1)}, bf16[512,1024]{1,0:T(8,128)(2,1)}, u32[]{:S(2)}, u32[]{:S(2)}) collective-permute-start(bf16[512,1024]{1,0:T(8,128)(2,1)} %collective-permute-done.55), channel_id=1, source_target_pairs={{0,1},{1,2},{2,3},{3,0},{4,5},{5,6},{6,7},{7,4},{8,9},{9,10},{10,1... | collective-permute-start | bytes 3145736 | tf_op jit(solution)/shard_map/ppermute | solution.py:1604
  424.6 40.2 %collective-permute-start.69 = (bf16[128,3456]{1,0:T(8,128)(2,1)}, bf16[128,3456]{1,0:T(8,128)(2,1)}, u32[]{:S(2)}, u32[]{:S(2)}) collective-permute-start(bf16[128,3456]{1,0:T(8,128)(2,1)} %get-tuple-element.2513), channel_id=1, source_target_pairs={{0,16},{16,0},{8,24},{24,8},{1,17},{17,1},{9,25},{25,9},{2,18},{18... | collective-permute-start | bytes 2654216 | tf_op jit(solution)/shard_map/ppermute | solution.py:1595
  425.9 39.0 %collective-permute-start.70 = (bf16[128,3456]{1,0:T(8,128)(2,1)}, bf16[128,3456]{1,0:T(8,128)(2,1)}, u32[]{:S(2)}, u32[]{:S(2)}) collective-permute-start(bf16[128,3456]{1,0:T(8,128)(2,1)} %get-tuple-element.2514), channel_id=1, source_target_pairs={{0,16},{16,0},{8,24},{24,8},{1,17},{17,1},{9,25},{25,9},{2,18},{18... | collective-permute-start | bytes 2654216 | tf_op jit(solution)/shard_map/ppermute | solution.py:1595
  469.2 42.4 %collective-permute-start.78 = (bf16[128,3456]{1,0:T(8,128)(2,1)}, bf16[128,3456]{1,0:T(8,128)(2,1)}, u32[]{:S(2)}, u32[]{:S(2)}) collective-permute-start(bf16[128,3456]{1,0:T(8,128)(2,1)} %get-tuple-element.2571), channel_id=1, source_target_pairs={{0,4},{4,0},{1,5},{5,1},{2,6},{6,2},{3,7},{7,3},{8,12},{12,8},{9,1... | collective-permute-start | bytes 2654216 | tf_op jit(solution)/shard_map/ppermute | solution.py:1601
  470.1 41.6 %collective-permute-start.76 = (bf16[512,1024]{1,0:T(8,128)(2,1)}, bf16[512,1024]{1,0:T(8,128)(2,1)}, u32[]{:S(2)}, u32[]{:S(2)}) collective-permute-start(bf16[512,1024]{1,0:T(8,128)(2,1)} %get-tuple-element.2559), channel_id=1, source_target_pairs={{0,4},{4,0},{1,5},{5,1},{2,6},{6,2},{3,7},{7,3},{8,12},{12,8},{9,1... | collective-permute-start | bytes 3145736 | tf_op jit(solution)/shard_map/ppermute | solution.py:1601
  471.3 40.4 %collective-permute-start.77 = (bf16[512,1024]{1,0:T(8,128)(2,1)}, bf16[512,1024]{1,0:T(8,128)(2,1)}, u32[]{:S(2)}, u32[]{:S(2)}) collective-permute-start(bf16[512,1024]{1,0:T(8,128)(2,1)} %collective-permute-done.57), channel_id=1, source_target_pairs={{0,1},{1,2},{2,3},{3,0},{4,5},{5,6},{6,7},{7,4},{8,9},{9,10},{10,1... | collective-permute-start | bytes 3145736 | tf_op jit(solution)/shard_map/ppermute | solution.py:1604
  471.3 40.3 %collective-permute-start.74 = (bf16[128,3456]{1,0:T(8,128)(2,1)}, bf16[128,3456]{1,0:T(8,128)(2,1)}, u32[]{:S(2)}, u32[]{:S(2)}) collective-permute-start(bf16[128,3456]{1,0:T(8,128)(2,1)} %get-tuple-element.2579), channel_id=1, source_target_pairs={{0,16},{16,0},{8,24},{24,8},{1,17},{17,1},{9,25},{25,9},{2,18},{18... | collective-permute-start | bytes 2654216 | tf_op jit(solution)/shard_map/ppermute | solution.py:1595
  472.6 39.1 %collective-permute-start.75 = (bf16[128,3456]{1,0:T(8,128)(2,1)}, bf16[128,3456]{1,0:T(8,128)(2,1)}, u32[]{:S(2)}, u32[]{:S(2)}) collective-permute-start(bf16[128,3456]{1,0:T(8,128)(2,1)} %get-tuple-element.2580), channel_id=1, source_target_pairs={{0,16},{16,0},{8,24},{24,8},{1,17},{17,1},{9,25},{25,9},{2,18},{18... | collective-permute-start | bytes 2654216 | tf_op jit(solution)/shard_map/ppermute | solution.py:1595
  511.7 37.1 %collective-permute-start.79 = (bf16[512,1024]{1,0:T(8,128)(2,1)}, bf16[512,1024]{1,0:T(8,128)(2,1)S(1)}, u32[]{:S(2)}, u32[]{:S(2)}) collective-permute-start(bf16[512,1024]{1,0:T(8,128)(2,1)} %get-tuple-element.2616), channel_id=1, source_target_pairs={{0,4},{4,0},{1,5},{5,1},{2,6},{6,2},{3,7},{7,3},{8,12},{12,8},{9,1... | collective-permute-start | bytes 3145736 | tf_op jit(solution)/shard_map/ppermute | solution.py:1601
  512.6 36.3 %collective-permute-start.80 = (bf16[128,3456]{1,0:T(8,128)(2,1)S(1)}, bf16[128,3456]{1,0:T(8,128)(2,1)S(1)}, u32[]{:S(2)}, u32[]{:S(2)}) collective-permute-start(bf16[128,3456]{1,0:T(8,128)(2,1)S(1)} %copy-done.74), channel_id=1, source_target_pairs={{0,3},{1,0},{2,1},{3,2},{4,7},{5,4},{6,5},{7,6},{8,11},{9,8},{10,9... | collective-permute-start | bytes 2654216 | tf_op jit(solution)/shard_map/ppermute | solution.py:1610
  519.6 50.4 %collective-permute-start.83 = (bf16[128,3456]{1,0:T(8,128)(2,1)}, bf16[128,3456]{1,0:T(8,128)(2,1)}, u32[]{:S(2)}, u32[]{:S(2)}) collective-permute-start(bf16[128,3456]{1,0:T(8,128)(2,1)} %get-tuple-element.2697), channel_id=1, source_target_pairs={{0,1},{1,2},{2,3},{3,0},{4,5},{5,6},{6,7},{7,4},{8,9},{9,10},{10,1... | collective-permute-start | bytes 2654216 | tf_op jit(solution)/shard_map/ppermute | solution.py:1604
  520.2 49.7 %collective-permute-start.81 = (bf16[128,3456]{1,0:T(8,128)(2,1)}, bf16[128,3456]{1,0:T(8,128)(2,1)}, u32[]{:S(2)}, u32[]{:S(2)}) collective-permute-start(bf16[128,3456]{1,0:T(8,128)(2,1)} %get-tuple-element.2645), channel_id=1, source_target_pairs={{0,16},{16,0},{8,24},{24,8},{1,17},{17,1},{9,25},{25,9},{2,18},{18... | collective-permute-start | bytes 2654216 | tf_op jit(solution)/shard_map/ppermute | solution.py:1595
  671.3 48.5 %collective-permute-start.100 = (f32[128,3456]{1,0:T(8,128)S(1)}, f32[128,3456]{1,0:T(8,128)}, u32[]{:S(2)}, u32[]{:S(2)}) collective-permute-start(f32[128,3456]{1,0:T(8,128)S(1)} %copy-done.32), channel_id=1, source_target_pairs={{0,4},{4,0},{1,5},{5,1},{2,6},{6,2},{3,7},{7,3},{8,12},{12,8},{9,1... | collective-permute-start | bytes 5308424 | tf_op jit(solution)/shard_map/ppermute | solution.py:1601
  (175 other events, 2444.2 us)

commit v11 on v10

--- a/solution.py
+++ b/solution.py
@@ -677,9 +677,26 @@
     return jnp.concatenate([pair, one_row.astype(BF16)], axis=0)
 
 
-def causal(scores, width):
-    key_pos = lax.broadcasted_iota(jnp.int32, (width, width), 0)
-    query_pos = lax.broadcasted_iota(jnp.int32, (width, width), 1)
+def by_halves(left, right):
+    half = left.shape[1] // 2
+    return jnp.concatenate(
+        [left[:, :half], right[:, :half], left[:, half:], right[:, half:]], axis=1
+    )
+
+
+def by_heads(both):
+    quarter = both.shape[1] // 4
+    part = lambda i: both[:, i * quarter : (i + 1) * quarter]
+    return (
+        jnp.concatenate([part(0), part(2)], axis=1),
+        jnp.concatenate([part(1), part(3)], axis=1),
+    )
+
+
+def causal(scores):
+    half = scores.shape[0]
+    key_pos = lax.broadcasted_iota(jnp.int32, (half, half), 0)
+    query_pos = lax.broadcasted_iota(jnp.int32, (half, half), 1)
     allowed = key_pos <= query_pos
     return jnp.where(jnp.concatenate([allowed, allowed], axis=1), scores, NEGATIVE)
 
@@ -705,26 +722,36 @@
 
     start = pl.multiple_of(block * width, width)
     both = rows[pl.ds(query_at, 2 * hd), pl.ds(start, width)]
-    query = query_with_one(jnp.concatenate([both[:hd], both[hd:]], axis=1))
-
-    def tile(at, carried, diagonal):
-        out, total = carried
-        scores = dot(key_rows[pl.ds(at, width), :], query, 1, 0)
-        if diagonal:
-            scores = causal(scores, width)
+    query = query_with_one(by_halves(both[:hd], both[hd:]))
+    half = width // 2
+
+    def terms(at, keys, query, mask):
+        scores = dot(key_rows[pl.ds(at, keys), :], query, 1, 0)
+        if mask:
+            part = causal(scores[:, :width])
+            wide = scores.shape[1] > width
+            scores = jnp.concatenate([part, scores[:, width:]], axis=1) if wide else part
         probs = jnp.exp2(scores * scale)
-        total = total + jnp.sum(probs, axis=0, keepdims=True)
-        out = out + dot(rows[pl.ds(value_at, hd), pl.ds(at, width)], probs.astype(BF16), 1, 0)
-        return out, total
+        total = jnp.sum(probs, axis=0, keepdims=True)
+        return dot(rows[pl.ds(value_at, hd), pl.ds(at, keys)], probs.astype(BF16), 1, 0), total
+
+    def tile(at, carried):
+        more, sums = terms(at, width, query, False)
+        return carried[0] + more, carried[1] + sums
 
     carried = (jnp.zeros((hd, 2 * width), F32), jnp.zeros((1, 2 * width), F32))
     full = jnp.minimum(block, lax.div(length + width - 1, width))
     carried = lax.fori_loop(
-        0, full, lambda j, c: tile(pl.multiple_of(j * width, width), c, False), carried
-    )
-    out, total = tile(start, carried, True)
+        0, full, lambda j, c: tile(pl.multiple_of(j * width, width), c), carried
+    )
+    more, sums = terms(start, half, query, True)
+    out, total = carried[0] + more, carried[1] + sums
+    later = pl.multiple_of(start + half, half)
+    more, sums = terms(later, half, query[:, width:], True)
+    out = jnp.concatenate([out[:, :width], out[:, width:] + more], axis=1)
+    total = jnp.concatenate([total[:, :width], total[:, width:] + sums], axis=1)
     out = out * (1.0 / total)
-    out = jnp.concatenate([out[:, :width], out[:, width:]], axis=0).T.astype(BF16)
+    out = jnp.concatenate(by_heads(out), axis=0).T.astype(BF16)
     here = block // 2 == info[2]
 
     @pl.when(here)
@@ -735,9 +762,9 @@
     def _():
         send_ref[...] = out
 
-    log_total = jnp.log2(total)
-    lse_ref[0, 0:1, :] = log_total[:, :width]
-    lse_ref[0, 1:2, :] = log_total[:, width:]
+    log_first, log_second = by_heads(jnp.log2(total))
+    lse_ref[0, 0:1, :] = log_first
+    lse_ref[0, 1:2, :] = log_second
 
 
 def keep_block(i, info):
@@ -838,45 +865,52 @@
     @pl.when(block * width < length)
     def _():
         both = rows[pl.ds(query_at, 2 * hd), pl.ds(start, width)]
-        pair = jnp.concatenate([both[:hd], both[hd:]], axis=1)
+        pair = by_halves(both[:hd], both[hd:])
         query = query_with_one(pair)
         query_rows = pair.astype(F32).T.astype(BF16)
         grad_wide = jnp.where(here, gk_ref[...].astype(F32), gs_ref[...].astype(F32))
         out_wide = jnp.where(here, ok_ref[...].astype(F32), os_ref[...].astype(F32))
-        grad_rows = jnp.concatenate([grad_wide[:, :hd], grad_wide[:, hd:]], axis=0).astype(BF16)
         grad_t = grad_wide.T
         prod = (grad_wide * out_wide).T
-        grad = jnp.concatenate([grad_t[:hd], grad_t[hd:]], axis=1).astype(BF16)
-        delta = jnp.concatenate(
+        grad = by_halves(grad_t[:hd], grad_t[hd:]).astype(BF16)
+        half = width // 2
+        grad_rows = jnp.concatenate(
             [
-                jnp.sum(prod[:hd], axis=0, keepdims=True),
-                jnp.sum(prod[hd:], axis=0, keepdims=True),
+                grad_wide[:half, :hd],
+                grad_wide[:half, hd:],
+                grad_wide[half:, :hd],
+                grad_wide[half:, hd:],
             ],
-            axis=1,
+            axis=0,
+        ).astype(BF16)
+        delta = by_halves(
+            jnp.sum(prod[:hd], axis=0, keepdims=True), jnp.sum(prod[hd:], axis=0, keepdims=True)
         )
-        lse = jnp.concatenate([lse_ref[0, 0:1, :], lse_ref[0, 1:2, :]], axis=1)
-
-        def tile(at, query_sum, diagonal):
-            scores = dot(key_rows[pl.ds(at, width), :], query, 1, 0)
-            if diagonal:
-                scores = causal(scores, width)
-            probs = jnp.exp2(scores * (scale * LOG2E) - lse)
-            grad_probs = dot(value_rows[pl.ds(at, width), :], grad, 1, 0)
-            grad_scores = (probs * (grad_probs - delta)).astype(BF16)
-            value_sum[pl.ds(at, width), :] += dot(probs.astype(BF16), grad_rows, 1, 0)
-            key_sum[pl.ds(at, width), :] += dot(grad_scores, query_rows, 1, 0)
-            return query_sum + dot(rows[pl.ds(key_at, hd), pl.ds(at, width)], grad_scores, 1, 0)
+        lse = by_halves(lse_ref[0, 0:1, :], lse_ref[0, 1:2, :])
+
+        def terms(at, keys, first, mask):
+            scores = dot(key_rows[pl.ds(at, keys), :], query[:, first:], 1, 0)
+            if mask:
+                part = causal(scores[:, :width])
+                wide = scores.shape[1] > width
+                scores = jnp.concatenate([part, scores[:, width:]], axis=1) if wide else part
+            probs = jnp.exp2(scores * (scale * LOG2E) - lse[:, first:])
+            grad_probs = dot(value_rows[pl.ds(at, keys), :], grad[:, first:], 1, 0)
+            grad_scores = (probs * (grad_probs - delta[:, first:])).astype(BF16)
+            value_sum[pl.ds(at, keys), :] += dot(probs.astype(BF16), grad_rows[first:], 1, 0)
+            key_sum[pl.ds(at, keys), :] += dot(grad_scores, query_rows[first:], 1, 0)
+            return dot(rows[pl.ds(key_at, hd), pl.ds(at, keys)], grad_scores, 1, 0)
 
         query_sum = lax.fori_loop(
             0,
             block,
-            lambda j, s: tile(pl.multiple_of(j * width, width), s, False),
+            lambda j, s: s + terms(pl.multiple_of(j * width, width), width, 0, False),
             jnp.zeros((hd, 2 * width), F32),
         )
-        query_sum = tile(start, query_sum, True) * scale
-        store_query(
-            jnp.concatenate([query_sum[:, :width], query_sum[:, width:]], axis=0).astype(BF16)
-        )
+        query_sum = query_sum + terms(start, half, 0, True)
+        later = terms(pl.multiple_of(start + half, half), half, width, True)
+        query_sum = jnp.concatenate([query_sum[:, :width], query_sum[:, width:] + later], axis=1)
+        store_query(jnp.concatenate(by_heads(query_sum * scale), axis=0).astype(BF16))
 
     @pl.when(block * width >= length)
     def _():
@@ -1623,7 +1657,10 @@
     info = jnp.concatenate([jnp.stack([z, fsdp, ctx]).astype(jnp.int32), length])
     w_proj = join(q_weight, k_weight, v_weight)
     proj_z = [z_up(w_proj), z_far(w_proj), z_down(w_proj)]
-    proj_far = x_swap(w_proj)
+    proj_z[2] = after(proj_z[2], proj_z[0])
+    proj_z[1] = after(proj_z[1], proj_z[2])
+    proj_zfar = [x_swap(block) for block in proj_z]
+    proj_own = jnp.concatenate([w_proj, x_swap(w_proj)], axis=0)
     count_here = jnp.sum(lengths).astype(F32)[None]
     vector = jnp.concatenate([attn_gain, ffn_gain, q_gain, k_gain]).astype(F32)
     vector = jnp.concatenate([vector, count_here, jnp.zeros((640 - 545,), F32)])[None]
@@ -1634,14 +1671,23 @@
     frequency = THETA ** (-(2.0 * jnp.arange(hd // 2, dtype=F32)) / hd)
     angles = frequency[:, None] * pos[None, :]
     head_gains = natural(vector[:, 2 * quarter : 544])
+    gain_one = vector[:, :quarter].reshape(1, width)
+    x_in, normed_one_t = norm_one(info, tokens, gain_one, 256)
+    out_start = after(w_out, proj_z[1])
+    out_z = [z_up(out_start), z_far(out_start), z_down(out_start)]
     v.update(
         info=info,
-        proj_own=jnp.concatenate([w_proj, proj_far], axis=0),
+        proj_own=proj_own,
         proj_z=jnp.concatenate(proj_z, axis=0),
+        proj_zfar=proj_zfar,
+        own_core=core_swap(proj_own),
         w_out=w_out,
+        out_z=out_z,
         w_ffn=w_ffn,
         w_chunks=w_chunks,
-        gain_one=vector[:, :quarter].reshape(1, width),
+        x_in=x_in,
+        normed_one_t=normed_one_t,
+        gain_one=gain_one,
         gain_two=vector[:, quarter : 2 * quarter].reshape(1, width),
         total_count=jnp.sum(vector[:, 544]),
         gain_q=head_gains[:, : hd // 4].reshape(hd, 1),
@@ -1652,23 +1698,10 @@
     sync()
     info = v["info"]
 
-    proj_zfar = x_swap(v["proj_z"])
-    out_z = [z_up(v["w_out"]), z_far(v["w_out"]), z_down(v["w_out"])]
-    own_core = core_swap(v["proj_own"])
-    x_in, normed_one_t = norm_one(info, tokens, v["gain_one"], 256)
-    v.update(
-        proj_zfar=proj_zfar,
-        own_core=own_core,
-        x_in=x_in,
-        normed_one_t=normed_one_t,
-        out_z=out_z,
-    )
-    sync()
-
-    plan_proj = [[(0, 0), (0, quarter), (3, 0), (3, quarter)]]
-    plan_proj += [[(p, k * quarter) for p in (1, 2, 4, 5)] for k in range(3)]
-    weights_proj = [v["proj_own"], v["proj_z"], v["proj_zfar"], v["own_core"]]
-    weights_proj += [core_swap(v["proj_z"]), core_swap(v["proj_zfar"])]
+    plan_proj = [[(0, 0), (0, quarter), (5, 0), (5, quarter)]]
+    plan_proj += [[(1, k * quarter), (2 + k, 0), (6, k * quarter), (7 + k, 0)] for k in range(3)]
+    weights_proj = [v["proj_own"], v["proj_z"]] + v["proj_zfar"] + [v["own_core"]]
+    weights_proj += [core_swap(part) for part in [v["proj_z"]] + v["proj_zfar"]]
     one = [z_up(v["w_chunks"][0]), z_up(v["w_chunks"][3])]
     ffn_far = x_swap(v["w_ffn"])
     tables = [v[name] for name in ("cos_part", "sin_part", "gain_q", "gain_k")]
@@ -2063,10 +2096,12 @@
     sync()
 
     three = v["three"] + [z_down(part) for part in v["tokens_low"][2:]]
+    two = [z_up(v["one"][0])]
     attn_sum = summed(v["parts"], None, F32)
     vector = v["vector"] + lax.ppermute(v["vector"], "tp", Z_NEAR)
     grad = place(v["grad"], v["one"], 1, 0)
-    v.update(three=three, attn_sum=attn_sum, vector=vector, grad=grad, ffn_other=ffn_other)
+    v.update(three=three, two=two, attn_sum=attn_sum, vector=vector, grad=grad)
+    v.update(ffn_other=ffn_other)
     sync()
 
     def finish(own, other):
@@ -2085,21 +2120,21 @@
             axis=1,
         )
 
-    two = [z_up(part) for part in v["one"][:2]]
+    two = v["two"] + [z_up(part) for part in v["one"][1:]]
+    attn_other = y_swap(v["attn_sum"])
+    vector = v["vector"] + lax.ppermute(v["vector"], "tp", Z_FAR)
     third = units // 3
     ffn_grad = finish(v["ffn_sum"], turn_chunks(v["ffn_other"]))
     grad_gate = columns(lambda j: 2 * j * third)
     grad_up = columns(lambda j: (2 * j + 1) * third)
     grad_down = columns(lambda j: 2 * units + j * third).T
-    attn_other = y_swap(v["attn_sum"])
-    vector = v["vector"] + lax.ppermute(v["vector"], "tp", Z_FAR)
     grad = place(v["grad"], v["three"], 3, 0)
-    v.update(two=two, vector=vector, grad=grad, attn_other=attn_other)
-    v.update(grad_gate=grad_gate, grad_up=grad_up, grad_down=grad_down)
-    sync()
-
-    two = [z_up(part) for part in v["one"][2:]]
-    tokens_grad = place(place(v["grad"], v["two"], 2, 0), two, 2, 2)
+    grad = place(grad, v["two"], 2, 0)
+    v.update(vector=vector, grad=grad, attn_other=attn_other)
+    v.update(grad_gate=grad_gate, grad_up=grad_up, grad_down=grad_down, two=two)
+    sync()
+
+    tokens_grad = place(v["grad"], v["two"][1:], 2, 1)
     output = v["output"]
     sums_all = v["vector"][0]
 

time: 796 us -> 803 us (level)
  waiting for transfers between devices: 143 us -> 190 us
  Pallas kernels: 411 us -> 368 us
    pallas_call x2, Pallas kernels: 76.5 us -> 34.5 us  [attn_bwd(): pl.pallas_call(functools.partial(attn_bwd_kernel, width, hd), grid_spec=p...]
    ppermute x22 -> x24, waiting for transfers between devices: 9.83 us -> 46.7 us  [x_swap(): return lax.ppermute(v, 'fsdp', X_SWAP)]
    ppermute x14, waiting for transfers between devices: 40.3 us -> 28.5 us  [z_down(): return lax.ppermute(v, 'tp', Z_DOWN)]
    ppermute x20, waiting for transfers between devices: 58.1 us -> 67.1 us  [z_up(): return lax.ppermute(v, 'tp', Z_UP)]
    ppermute x22 -> x24, starting transfers between devices: 23.1 us -> 28 us  [x_swap(): return lax.ppermute(v, 'fsdp', X_SWAP)]
    unnamed x193 -> x201, local copies, waits for them, and re-layouts: 41.1 us -> 40.8 us
  transfers between devices with their start and end apart: 110 -> 114, of which waited for: 30 -> 42; matrix products, arithmetic and copies ran while one was open for 10% -> 9% of each run, Pallas kernels for 46% -> 40%
where the time goes in v11:
time: 803 us; the launch traced here: 792 us
  Pallas kernels  368 us (46%)
  waiting for transfers between devices  190 us (24%)
  starting transfers between devices  106 us (13%)
  local copies, waits for them, and re-layouts  86.7 us (11%)
  other arithmetic  34.5 us (4%)
    pallas_call x4, Pallas kernels, ffn_bwd(): pl.pallas_call(functools.partial(ffn_bwd_kernel, steps, plan, first), gri...  101 us
    ppermute x20, waiting for transfers between devices, z_up(): return lax.ppermute(v, 'tp', Z_UP)  67.1 us
    pallas_call x3, Pallas kernels, ffn_fwd(): pl.pallas_call(functools.partial(ffn_fwd_kernel, tile, [plan for plan, _...  62.9 us
    ppermute x24, waiting for transfers between devices, x_swap(): return lax.ppermute(v, 'fsdp', X_SWAP)  46.7 us
    unnamed x201, local copies, waits for them, and re-layouts  40.8 us
    pallas_call x2, Pallas kernels, attn_bwd(): pl.pallas_call(functools.partial(attn_bwd_kernel, width, hd), grid_spec=p...  34.5 us
    ppermute x19, waiting for transfers between devices, y_swap(): return lax.ppermute(v, 'ctx', Y_SWAP)  33.4 us
    pallas_call x6, Pallas kernels, sums(): pl.pallas_call(functools.partial(sums_kernel, jobs, len(arrays)), grid_sp...  33.3 us
  transfers between devices with their start and end apart: 114, of which 42 were waited for; matrix products, arithmetic and copies ran while one was open for 9% of the time, Pallas kernels for 40%

profile of v11, /device:TPU:0, one launch (start us, length us, event | category | flops | bytes accessed | tf_op | source)
XLA Modules:
  0.0 792.0 jit_solution(16138107018742768502)
XLA Ops:
  95.0 13.0 %collective-permute-done.19.rest_4_.rest_0_ = bf16[256,1152]{1,0:T(8,128)(2,1)} collective-permute-done((bf16[256,1152]{1,0:T(8,128)(2,1)}, bf16[256,1152]{1,0:T(8,128)(2,1)}, u32[]{:S(2)}, u32[]{:S(2)}) %collective-permute-start.19) | collective-permute-done | bytes 589856 | tf_op jit(solution)/shard_map/ppermute | solution.py:1638
  110.1 16.6 %attn_fwd.2 = (bf16[1024,256]{1,0:T(8,128)(2,1)}, bf16[1024,256]{1,0:T(8,128)(2,1)}, f32[2,2,2048]{2,1,0:T(2,128)}) custom-call(s32[4]{0:T(128)} %copy-done.22, bf16[512,1024]{1,0:T(8,128)(2,1)} %copy-done.30, bf16[512,1024]{1,0:T(8,128)(2,1)} %copy-done.77), custom_call_target="tpu_custom_call" | custom-call | flops 4398046511104 | bytes 1073741824 | tf_op jit(solution)/shard_map/attn_fwd/pallas_call | solution.py:782
  135.5 16.6 %attn_fwd.3 = (bf16[1024,256]{1,0:T(8,128)(2,1)}, bf16[1024,256]{1,0:T(8,128)(2,1)}, f32[2,2,2048]{2,1,0:T(2,128)}) custom-call(s32[4]{0:T(128)} %copy-done.22, bf16[512,1024]{1,0:T(8,128)(2,1)} %copy-done.29, bf16[512,1024]{1,0:T(8,128)(2,1)} %collective-permute-done.21.got_ref), custom_call_target="tpu_custom_call" | custom-call | flops 4398046511104 | bytes 1073741824 | tf_op jit(solution)/shard_map/attn_fwd/pallas_call | solution.py:782
  159.2 11.9 %collective-permute-done.31.refs_8_ = bf16[1024,256]{1,0:T(8,128)(2,1)S(1)} collective-permute-done((bf16[1024,256]{1,0:T(8,128)(2,1)}, bf16[1024,256]{1,0:T(8,128)(2,1)S(1)}, u32[]{:S(2)}, u32[]{:S(2)}) %collective-permute-start.31) | collective-permute-done | bytes 524320 | tf_op jit(solution)/shard_map/ppermute | solution.py:1635
  174.2 10.3 %out_proj.1 = (f32[1024,1024]{1,0:T(8,128)}, bf16[1024,1024]{1,0:T(8,128)(2,1)}, bf16[1024,1024]{1,0:T(8,128)(2,1)}, bf16[4,1024,256]{2,1,0:T(8,128)(2,1)}) custom-call(s32[4]{0:T(128)} %copy-done.22, bf16[1024,256]{1,0:T(8,128)(2,1)} %constant_dynamic-update-slice_fusion.refs_0_, bf16[1024,256]{1,0:T(8,128)(2,1)} %collective-permute-done.29.refs_1_, ...), custom_call_target="tpu_custom_call" | custom-call | flops 4398046511104 | bytes 1073741824 | tf_op jit(solution)/shard_map/out_proj/pallas_call | solution.py:1008
  195.5 27.3 %ffn_fwd.3 = (bf16[2,1024,2304]{2,1,0:T(8,128)(2,1)}, bf16[2,1024,1152]{2,1,0:T(8,128)(2,1)}, f32[1024,1024]{1,0:T(8,128)}) custom-call(s32[4]{0:T(128)} %copy-done.22, f32[1]{0:T(128)} %bitcast.4.scale, bf16[1024,1024]{1,0:T(8,128)(2,1)} %get-tuple-element.1990.x_ref, f32[1024,1024]{1,0:T(8,128)} %get-tuple-element.2569.in_ref.refs_5_, ...), custom_call_target="tpu_custom_call" | custom-call | flops 4398046511104 | bytes 1073741824 | tf_op jit(solution)/shard_map/ffn_fwd/pallas_call | solution.py:1316
  230.1 15.8 %ffn_fwd.4 = (bf16[1,1024,2304]{2,1,0:T(8,128)(2,1)}, bf16[1,1024,1152]{2,1,0:T(8,128)(2,1)}, f32[1024,1024]{1,0:T(8,128)}) custom-call(s32[4]{0:T(128)} %copy-done.22, f32[1]{0:T(128)} %bitcast.4.scale, bf16[1024,1024]{1,0:T(8,128)(2,1)} %get-tuple-element.1990.x_ref, f32[1024,1024]{1,0:T(8,128)} %get-tuple-element.1886.in_ref, ...), custom_call_target="tpu_custom_call" | custom-call | flops 4398046511104 | bytes 1073741824 | tf_op jit(solution)/shard_map/ffn_fwd/pallas_call | solution.py:1316
  250.0 19.8 %ffn_fwd.5 = (bf16[1,1024,2304]{2,1,0:T(8,128)(2,1)}, bf16[1,1024,1152]{2,1,0:T(8,128)(2,1)}, bf16[512,1024]{1,0:T(8,128)(2,1)}, bf16[512,1024]{1,0:T(8,128)(2,1...) custom-call(s32[4]{0:T(128)} %copy-done.22, ...), custom_call_target="tpu_custom_call" | custom-call | flops 4398046511104 | bytes 1073741824 | tf_op jit(solution)/shard_map/ffn_fwd/pallas_call | solution.py:1316
  270.0 24.9 %ffn_bwd.4 = (f32[1024,1024]{1,0:T(8,128)}, bf16[512,3456]{1,0:T(8,128)(2,1)}, bf16[512,3456]{1,0:T(8,128)(2,1)}) custom-call(bf16[1024,1024]{1,0:T(8,128)(2,1)} %get-tuple-element.2488.low_ref, bf16[1,1024,2304]{2,1,0:T(8,128)(2,1)} %get-tuple-element.2115.act_ref, bf16[1,1024,1152]{2,1,0:T(8,128)(2,1)} %get-tuple-element.2135.hid_ref, ...), custom_call_target="tpu_custom_call" | custom-call | flops 4398046511104 | bytes 1073741824 | tf_op jit(solution)/shard_map/ffn_bwd/pallas_call | solution.py:1398
  297.3 25.4 %ffn_bwd.5 = (f32[1024,1024]{1,0:T(8,128)}, bf16[512,3456]{1,0:T(8,128)(2,1)}, bf16[512,3456]{1,0:T(8,128)(2,1)}) custom-call(bf16[1024,1024]{1,0:T(8,128)(2,1)} %get-tuple-element.2488.low_ref, bf16[2,1024,2304]{2,1,0:T(8,128)(2,1)} %get-tuple-element.2472.act_ref, ...), custom_call_target="tpu_custom_call", output_to_operand_aliasing={{0}: (15, {})} | custom-call | flops 4398046511104 | bytes 1073741824 | tf_op jit(solution)/shard_map/ffn_bwd/pallas_call | solution.py:1398
  333.8 25.4 %ffn_bwd.6 = (f32[1024,1024]{1,0:T(8,128)}, bf16[512,3456]{1,0:T(8,128)(2,1)}, bf16[512,3456]{1,0:T(8,128)(2,1)}) custom-call(bf16[1024,1024]{1,0:T(8,128)(2,1)} %get-tuple-element.2488.low_ref, bf16[1,1024,2304]{2,1,0:T(8,128)(2,1)} %get-tuple-element.2392.act_ref, ...), custom_call_target="tpu_custom_call", output_to_operand_aliasing={{0}: (17, {})} | custom-call | flops 4398046511104 | bytes 1073741824 | tf_op jit(solution)/shard_map/ffn_bwd/pallas_call | solution.py:1398
  369.8 25.3 %ffn_bwd.7 = (f32[1024,1024]{1,0:T(8,128)}, bf16[512,3456]{1,0:T(8,128)(2,1)}, bf16[512,3456]{1,0:T(8,128)(2,1)}) custom-call(bf16[1024,1024]{1,0:T(8,128)(2,1)} %get-tuple-element.2488.low_ref, bf16[2,1024,2304]{2,1,0:T(8,128)(2,1)} %get-tuple-element.2472.act_ref, ...), custom_call_target="tpu_custom_call", output_to_operand_aliasing={{0}: (9, {})} | custom-call | flops 4398046511104 | bytes 1073741824 | tf_op jit(solution)/shard_map/ffn_bwd/pallas_call | solution.py:1398
  404.1 12.4 %norm_two_back.1 = (f32[1024,1024]{1,0:T(8,128)}, bf16[1024,1024]{1,0:T(8,128)(2,1)}, bf16[1024,256]{1,0:T(8,128)(2,1)}, bf16[1024,256]{1,0:T(8,128)(2,1)}, bf16...) custom-call(s32[4]{0:T(128)} %copy-done.22, ...), custom_call_target="tpu_custom_call" | custom-call | flops 4398046511104 | bytes 1073741824 | tf_op jit(solution)/shard_map/norm_two_back/pallas_call | solution.py:1066
  418.6 12.9 %collective-permute-done.72.gs_ref = bf16[1024,256]{1,0:T(8,128)(2,1)S(1)} collective-permute-done((bf16[1024,256]{1,0:T(8,128)(2,1)}, bf16[1024,256]{1,0:T(8,128)(2,1)S(1)}, u32[]{:S(2)}, u32[]{:S(2)}) %collective-permute-start.72) | collective-permute-done | bytes 524320 | tf_op jit(solution)/shard_map/ppermute | solution.py:1635
  442.5 17.2 %attn_bwd.2 = (bf16[512,1024]{1,0:T(8,128)(2,1)}, bf16[512,1024]{1,0:T(8,128)(2,1)}) custom-call(s32[4]{0:T(128)} %copy-done.22, bf16[512,1024]{1,0:T(8,128)(2,1)} %copy-done.30, bf16[512,1024]{1,0:T(8,128)(2,1)} %copy-done.77, bf16[1024,256]{1,0:T(8,128)(2,1)} %get-tuple-element.2619.refs_5_.ok_ref, bf16[1024,256]{1,0:T(8,128)(2,1)} %get-tuple-element.2620.os_ref, ...), custom_call_target="tpu_custom_call" | custom-call | flops 4398046511104 | bytes 1073741824 | tf_op jit(solution)/shard_map/attn_bwd/pallas_call | solution.py:943
  463.3 16.1 %collective-permute-done.74.refs_1_ = bf16[128,3456]{1,0:T(8,128)(2,1)} collective-permute-done((bf16[128,3456]{1,0:T(8,128)(2,1)}, bf16[128,3456]{1,0:T(8,128)(2,1)}, u32[]{:S(2)}, u32[]{:S(2)}) %collective-permute-start.74) | collective-permute-done | bytes 884768 | tf_op jit(solution)/shard_map/ppermute | solution.py:1629
  488.2 17.3 %attn_bwd.3 = (bf16[512,1024]{1,0:T(8,128)(2,1)}, bf16[512,1024]{1,0:T(8,128)(2,1)}) custom-call(s32[4]{0:T(128)} %copy-done.22, bf16[512,1024]{1,0:T(8,128)(2,1)} %copy-done.29, bf16[512,1024]{1,0:T(8,128)(2,1)} %collective-permute-done.21.got_ref, bf16[1024,256]{1,0:T(8,128)(2,1)} %get-tuple-element.2687.refs_6_.ok_ref, ...), custom_call_target="tpu_custom_call" | custom-call | flops 4398046511104 | bytes 1073741824 | tf_op jit(solution)/shard_map/attn_bwd/pallas_call | solution.py:943
  509.1 14.6 %collective-permute-done.79.refs_4_ = bf16[128,3456]{1,0:T(8,128)(2,1)} collective-permute-done((bf16[128,3456]{1,0:T(8,128)(2,1)}, bf16[128,3456]{1,0:T(8,128)(2,1)}, u32[]{:S(2)}, u32[]{:S(2)}) %collective-permute-start.79) | collective-permute-done | bytes 884768 | tf_op jit(solution)/shard_map/ppermute | solution.py:1629
  557.6 13.2 %norm_one_back.1 = (bf16[256,1024]{1,0:T(8,128)(2,1)}, bf16[256,1024]{1,0:T(8,128)(2,1)}, bf16[256,1024]{1,0:T(8,128)(2,1)}, bf16[256,1024]{1,0:T(8,128)(2,1)}, f32[1,1024]{1,0:T(1,128)}) custom-call(s32[4]{0:T(128)} %copy-done.22, bf16[512,512]{1,0:T(8,128)(2,1)} %copy-done.2, bf16[768,512]{1,0:T(8,128)(2,1)} %copy-done.1, ...), custom_call_target="tpu_custom_call" | custom-call | flops 4398046511104 | bytes 1073741824 | tf_op jit(solution)/shard_map/norm_one_back/pallas_call | solution.py:1124
  574.0 15.2 %weight_grad.1 = (bf16[4,512,768]{2,1,0:T(8,128)(2,1)}, bf16[4,512,768]{2,1,0:T(8,128)(2,1)}) custom-call(bf16[1024,1024]{1,0:T(8,128)(2,1)} %copy-done, bf16[2,1024,512]{2,1,0:T(8,128)(2,1)} %get-tuple-element.2840.refs_10_.back0_ref, bf16[2,1024,512]{2,1,0:T(8,128)(2,1)} %get-tuple-element.2842.refs_11_.back1_ref, ...), custom_call_target="tpu_custom_call" | custom-call | flops 4398046511104 | bytes 1073741824 | tf_op jit(solution)/shard_map/weight_grad/pallas_call | solution.py:1581
  710.7 11.2 %collective-permute-done.106 = bf16[256,1024]{1,0:T(8,128)(2,1)} collective-permute-done((bf16[256,1024]{1,0:T(8,128)(2,1)S(1)}, bf16[256,1024]{1,0:T(8,128)(2,1)}, u32[]{:S(2)}, u32[]{:S(2)}) %collective-permute-start.106) | collective-permute-done | bytes 524320 | tf_op jit(solution)/shard_map/ppermute | solution.py:1644
  721.9 11.1 %collective-permute-done.107 = bf16[256,1024]{1,0:T(8,128)(2,1)} collective-permute-done((bf16[256,1024]{1,0:T(8,128)(2,1)}, bf16[256,1024]{1,0:T(8,128)(2,1)}, u32[]{:S(2)}, u32[]{:S(2)}) %collective-permute-start.107) | collective-permute-done | bytes 524320 | tf_op jit(solution)/shard_map/ppermute | solution.py:1638
  758.1 11.2 %collective-permute-done.111 = bf16[256,1024]{1,0:T(8,128)(2,1)S(1)} collective-permute-done((bf16[256,1024]{1,0:T(8,128)(2,1)}, bf16[256,1024]{1,0:T(8,128)(2,1)S(1)}, u32[]{:S(2)}, u32[]{:S(2)}) %collective-permute-start.111) | collective-permute-done | bytes 524320 | tf_op jit(solution)/shard_map/ppermute | solution.py:1638
  769.3 10.0 %collective-permute-done.112 = bf16[256,1024]{1,0:T(8,128)(2,1)S(1)} collective-permute-done((bf16[256,1024]{1,0:T(8,128)(2,1)}, bf16[256,1024]{1,0:T(8,128)(2,1)S(1)}, u32[]{:S(2)}, u32[]{:S(2)}) %collective-permute-start.112) | collective-permute-done | bytes 524320 | tf_op jit(solution)/shard_map/ppermute | solution.py:1638
  (528 shorter events, 391.1 us)
Async XLA Ops:
  31.7 29.4 %collective-permute-start.9 = (bf16[512,512]{1,0:T(8,128)(2,1)S(1)}, bf16[512,512]{1,0:T(8,128)(2,1)}, u32[]{:S(2)}, u32[]{:S(2)}) collective-permute-start(bf16[512,512]{1,0:T(8,128)(2,1)S(1)} %pad_maximum_fusion.2.refs_0_), channel_id=1, source_target_pairs={{0,8},{8,0},{16,24},{24,16},{1,9},{9,1},{17,25},{25,17},{2,10},{10... | collective-permute-start | bytes 1572872 | tf_op jit(solution)/shard_map/ppermute | solution.py:1632
  61.1 46.8 %collective-permute-start.13 = (bf16[256,3456]{1,0:T(8,128)(2,1)}, bf16[256,3456]{1,0:T(8,128)(2,1)}, u32[]{:S(2)}, u32[]{:S(2)}) collective-permute-start(bf16[256,3456]{1,0:T(8,128)(2,1)} %get-tuple-element.2493.rest_0_), channel_id=1, source_target_pairs={{0,16},{16,0},{8,24},{24,8},{1,17},{17,1},{9,25},{25,9},{2,18},{18... | collective-permute-start | bytes 5308424 | tf_op jit(solution)/shard_map/ppermute | solution.py:1629
  65.1 42.9 %collective-permute-start.20 = (bf16[256,2304]{1,0:T(8,128)(2,1)}, bf16[256,2304]{1,0:T(8,128)(2,1)}, u32[]{:S(2)}, u32[]{:S(2)}) collective-permute-start(bf16[256,2304]{1,0:T(8,128)(2,1)} %copy-done.28), channel_id=1, source_target_pairs={{0,1},{1,2},{2,3},{3,0},{4,5},{5,6},{6,7},{7,4},{8,9},{9,10},{10,1... | collective-permute-start | bytes 3538952 | tf_op jit(solution)/shard_map/ppermute | solution.py:1638
  76.9 31.0 %collective-permute-start.18 = (bf16[512,1024]{1,0:T(8,128)(2,1)S(1)}, bf16[512,1024]{1,0:T(8,128)(2,1)S(1)}, u32[]{:S(2)}, u32[]{:S(2)}) collective-permute-start(bf16[512,1024]{1,0:T(8,128)(2,1)S(1)} %get-tuple-element.1532), channel_id=1, source_target_pairs={{0,4},{4,0},{1,5},{5,1},{2,6},{6,2},{3,7},{7,3},{8,12},{12,8},{9,1... | collective-permute-start | bytes 3145736 | tf_op jit(solution)/shard_map/ppermute | solution.py:1635
  78.3 29.6 %collective-permute-start.19 = (bf16[256,1152]{1,0:T(8,128)(2,1)}, bf16[256,1152]{1,0:T(8,128)(2,1)}, u32[]{:S(2)}, u32[]{:S(2)}) collective-permute-start(bf16[256,1152]{1,0:T(8,128)(2,1)} %get-tuple-element.1586), channel_id=1, source_target_pairs={{0,1},{1,2},{2,3},{3,0},{4,5},{5,6},{6,7},{7,4},{8,9},{9,10},{10,1... | collective-permute-start | bytes 1769480 | tf_op jit(solution)/shard_map/ppermute | solution.py:1638
  82.9 43.8 %collective-permute-start.21 = (bf16[512,1024]{1,0:T(8,128)(2,1)}, bf16[512,1024]{1,0:T(8,128)(2,1)}, u32[]{:S(2)}, u32[]{:S(2)}) collective-permute-start(bf16[512,1024]{1,0:T(8,128)(2,1)} %get-tuple-element.1534), channel_id=1, source_target_pairs={{0,4},{4,0},{1,5},{5,1},{2,6},{6,2},{3,7},{7,3},{8,12},{12,8},{9,1... | collective-permute-start | bytes 3145736 | tf_op jit(solution)/shard_map/ppermute | solution.py:1635
  190.5 32.3 %collective-permute-start.45 = (bf16[256,2304]{1,0:T(8,128)(2,1)}, bf16[256,2304]{1,0:T(8,128)(2,1)}, u32[]{:S(2)}, u32[]{:S(2)}) collective-permute-start(bf16[256,2304]{1,0:T(8,128)(2,1)} %collective-permute-done.20.rest_5_.rest_1_), channel_id=1, source_target_pairs={{0,1},{1,2},{2,3},{3,0},{4,5},{5,6},{6,7},{7,4},{8,9},{9,10},{10,1... | collective-permute-start | bytes 3538952 | tf_op jit(solution)/shard_map/ppermute | solution.py:1638
  190.5 32.2 %collective-permute-start.42 = (bf16[256,1152]{1,0:T(8,128)(2,1)}, bf16[256,1152]{1,0:T(8,128)(2,1)}, u32[]{:S(2)}, u32[]{:S(2)}) collective-permute-start(bf16[256,1152]{1,0:T(8,128)(2,1)} %collective-permute-done.25.rest_0_), channel_id=1, source_target_pairs={{0,8},{8,0},{16,24},{24,16},{1,9},{9,1},{17,25},{25,17},{2,10},{10... | collective-permute-start | bytes 1769480 | tf_op jit(solution)/shard_map/ppermute | solution.py:1632
  191.0 31.7 %collective-permute-start.43 = (bf16[256,1152]{1,0:T(8,128)(2,1)}, bf16[256,1152]{1,0:T(8,128)(2,1)}, u32[]{:S(2)}, u32[]{:S(2)}) collective-permute-start(bf16[256,1152]{1,0:T(8,128)(2,1)} %collective-permute-done.30.rest_1_), channel_id=1, source_target_pairs={{0,16},{16,0},{8,24},{24,8},{1,17},{17,1},{9,25},{25,9},{2,18},{18... | collective-permute-start | bytes 1769480 | tf_op jit(solution)/shard_map/ppermute | solution.py:1629
  192.4 30.3 %collective-permute-start.44 = (bf16[256,1152]{1,0:T(8,128)(2,1)}, bf16[256,1152]{1,0:T(8,128)(2,1)}, u32[]{:S(2)}, u32[]{:S(2)}) collective-permute-start(bf16[256,1152]{1,0:T(8,128)(2,1)} %collective-permute-done.39.rest_3_), channel_id=1, source_target_pairs={{0,4},{4,0},{1,5},{5,1},{2,6},{6,2},{3,7},{7,3},{8,12},{12,8},{9,1... | collective-permute-start | bytes 1769480 | tf_op jit(solution)/shard_map/ppermute | solution.py:1635
  365.5 29.5 %collective-permute-start.68 = (bf16[128,3456]{1,0:T(8,128)(2,1)}, bf16[128,3456]{1,0:T(8,128)(2,1)}, u32[]{:S(2)}, u32[]{:S(2)}) collective-permute-start(bf16[128,3456]{1,0:T(8,128)(2,1)} %get-tuple-element.2527), channel_id=1, source_target_pairs={{0,4},{4,0},{1,5},{5,1},{2,6},{6,2},{3,7},{7,3},{8,12},{12,8},{9,1... | collective-permute-start | bytes 2654216 | tf_op jit(solution)/shard_map/ppermute | solution.py:1635
  366.1 29.0 %collective-permute-start.65 = (bf16[512,3456]{1,0:T(8,128)(2,1)}, bf16[512,3456]{1,0:T(8,128)(2,1)}, u32[]{:S(2)}, u32[]{:S(2)}) collective-permute-start(bf16[512,3456]{1,0:T(8,128)(2,1)} %get-tuple-element.2475), channel_id=1, source_target_pairs={{0,8},{8,0},{16,24},{24,16},{1,9},{9,1},{17,25},{25,17},{2,10},{10... | collective-permute-start | bytes 10616840 | tf_op jit(solution)/shard_map/ppermute | solution.py:1632
  401.7 29.8 %collective-permute-start.70 = (bf16[128,3456]{1,0:T(8,128)(2,1)}, bf16[128,3456]{1,0:T(8,128)(2,1)}, u32[]{:S(2)}, u32[]{:S(2)}) collective-permute-start(bf16[128,3456]{1,0:T(8,128)(2,1)} %get-tuple-element.2553), channel_id=1, source_target_pairs={{0,3},{1,0},{2,1},{3,2},{4,7},{5,4},{6,5},{7,6},{8,11},{9,8},{10,9... | collective-permute-start | bytes 2654216 | tf_op jit(solution)/shard_map/ppermute | solution.py:1644
  417.8 41.8 %collective-permute-start.75 = (bf16[1024,256]{1,0:T(8,128)(2,1)}, bf16[1024,256]{1,0:T(8,128)(2,1)}, u32[]{:S(2)}, u32[]{:S(2)}) collective-permute-start(bf16[1024,256]{1,0:T(8,128)(2,1)} %get-tuple-element.2642), channel_id=1, source_target_pairs={{0,4},{4,0},{1,5},{5,1},{2,6},{6,2},{3,7},{7,3},{8,12},{12,8},{9,1... | collective-permute-start | bytes 1572872 | tf_op jit(solution)/shard_map/ppermute | solution.py:1635
  439.3 40.1 %collective-permute-start.76 = (bf16[512,1024]{1,0:T(8,128)(2,1)}, bf16[512,1024]{1,0:T(8,128)(2,1)}, u32[]{:S(2)}, u32[]{:S(2)}) collective-permute-start(bf16[512,1024]{1,0:T(8,128)(2,1)} %collective-permute-done.59), channel_id=1, source_target_pairs={{0,1},{1,2},{2,3},{3,0},{4,5},{5,6},{6,7},{7,4},{8,9},{9,10},{10,1... | collective-permute-start | bytes 3145736 | tf_op jit(solution)/shard_map/ppermute | solution.py:1638
  441.2 38.2 %collective-permute-start.74 = (bf16[128,3456]{1,0:T(8,128)(2,1)}, bf16[128,3456]{1,0:T(8,128)(2,1)}, u32[]{:S(2)}, u32[]{:S(2)}) collective-permute-start(bf16[128,3456]{1,0:T(8,128)(2,1)} %get-tuple-element.2635), channel_id=1, source_target_pairs={{0,16},{16,0},{8,24},{24,8},{1,17},{17,1},{9,25},{25,9},{2,18},{18... | collective-permute-start | bytes 2654216 | tf_op jit(solution)/shard_map/ppermute | solution.py:1629
  484.3 41.7 %collective-permute-start.80 = (bf16[512,1024]{1,0:T(8,128)(2,1)}, bf16[512,1024]{1,0:T(8,128)(2,1)}, u32[]{:S(2)}, u32[]{:S(2)}) collective-permute-start(bf16[512,1024]{1,0:T(8,128)(2,1)} %get-tuple-element.2684), channel_id=1, source_target_pairs={{0,4},{4,0},{1,5},{5,1},{2,6},{6,2},{3,7},{7,3},{8,12},{12,8},{9,1... | collective-permute-start | bytes 3145736 | tf_op jit(solution)/shard_map/ppermute | solution.py:1635
  485.8 40.3 %collective-permute-start.81 = (bf16[512,1024]{1,0:T(8,128)(2,1)}, bf16[512,1024]{1,0:T(8,128)(2,1)}, u32[]{:S(2)}, u32[]{:S(2)}) collective-permute-start(bf16[512,1024]{1,0:T(8,128)(2,1)} %collective-permute-done.61), channel_id=1, source_target_pairs={{0,1},{1,2},{2,3},{3,0},{4,5},{5,6},{6,7},{7,4},{8,9},{9,10},{10,1... | collective-permute-start | bytes 3145736 | tf_op jit(solution)/shard_map/ppermute | solution.py:1638
  486.9 36.8 %collective-permute-start.79 = (bf16[128,3456]{1,0:T(8,128)(2,1)}, bf16[128,3456]{1,0:T(8,128)(2,1)}, u32[]{:S(2)}, u32[]{:S(2)}) collective-permute-start(bf16[128,3456]{1,0:T(8,128)(2,1)} %get-tuple-element.2705), channel_id=1, source_target_pairs={{0,16},{16,0},{8,24},{24,8},{1,17},{17,1},{9,25},{25,9},{2,18},{18... | collective-permute-start | bytes 2654216 | tf_op jit(solution)/shard_map/ppermute | solution.py:1629
  535.1 35.8 %collective-permute-start.87 = (bf16[128,3456]{1,0:T(8,128)(2,1)}, bf16[128,3456]{1,0:T(8,128)(2,1)}, u32[]{:S(2)}, u32[]{:S(2)}) collective-permute-start(bf16[128,3456]{1,0:T(8,128)(2,1)} %get-tuple-element.2834), channel_id=1, source_target_pairs={{0,1},{1,2},{2,3},{3,0},{4,5},{5,6},{6,7},{7,4},{8,9},{9,10},{10,1... | collective-permute-start | bytes 2654216 | tf_op jit(solution)/shard_map/ppermute | solution.py:1638
  535.3 35.6 %collective-permute-start.85 = (bf16[128,3456]{1,0:T(8,128)(2,1)}, bf16[128,3456]{1,0:T(8,128)(2,1)}, u32[]{:S(2)}, u32[]{:S(2)}) collective-permute-start(bf16[128,3456]{1,0:T(8,128)(2,1)} %get-tuple-element.2774), channel_id=1, source_target_pairs={{0,16},{16,0},{8,24},{24,8},{1,17},{17,1},{9,25},{25,9},{2,18},{18... | collective-permute-start | bytes 2654216 | tf_op jit(solution)/shard_map/ppermute | solution.py:1629
  671.9 61.1 %collective-permute-start.104 = (f32[128,3456]{1,0:T(8,128)S(1)}, f32[128,3456]{1,0:T(8,128)}, u32[]{:S(2)}, u32[]{:S(2)}) collective-permute-start(f32[128,3456]{1,0:T(8,128)S(1)} %copy-done.33), channel_id=1, source_target_pairs={{0,4},{4,0},{1,5},{5,1},{2,6},{6,2},{3,7},{7,3},{8,12},{12,8},{9,1... | collective-permute-start | bytes 5308424 | tf_op jit(solution)/shard_map/ppermute | solution.py:1635
  698.4 34.6 %collective-permute-start.107 = (bf16[256,1024]{1,0:T(8,128)(2,1)}, bf16[256,1024]{1,0:T(8,128)(2,1)}, u32[]{:S(2)}, u32[]{:S(2)}) collective-permute-start(bf16[256,1024]{1,0:T(8,128)(2,1)} %collective-permute-done.88), channel_id=1, source_target_pairs={{0,1},{1,2},{2,3},{3,0},{4,5},{5,6},{6,7},{7,4},{8,9},{9,10},{10,1... | collective-permute-start | bytes 1572872 | tf_op jit(solution)/shard_map/ppermute | solution.py:1638
  742.5 36.8 %collective-permute-start.112 = (bf16[256,1024]{1,0:T(8,128)(2,1)}, bf16[256,1024]{1,0:T(8,128)(2,1)S(1)}, u32[]{:S(2)}, u32[]{:S(2)}) collective-permute-start(bf16[256,1024]{1,0:T(8,128)(2,1)} %copy-done.49), channel_id=1, source_target_pairs={{0,1},{1,2},{2,3},{3,0},{4,5},{5,6},{6,7},{7,4},{8,9},{9,10},{10,1... | collective-permute-start | bytes 1572872 | tf_op jit(solution)/shard_map/ppermute | solution.py:1638
  (183 other events, 2649.9 us)

commit v12 on v11

--- a/solution.py
+++ b/solution.py
@@ -1084,7 +1084,7 @@
 
 
 def norm_one_back_kernel(plan, count, info, *refs):
-    p0, p1, x_ref, gres_ref, gain_ref, *out_refs, gg_ref, w_ref, sem = refs[count:]
+    p0, p1, x_ref, gres_ref, gain_ref, out_ref, gg_ref, w_ref, sem = refs[count:]
     load_blocks(plan, refs, w_ref, sem)
     quarter = x_ref.shape[1] // 4
     grad = dot(p0[0], w_ref[0], 1, 1)
@@ -1101,11 +1101,7 @@
         at = pl.multiple_of(jnp.bitwise_xor(info[1], mask) * quarter, quarter)
         part = total[:, p * quarter : (p + 1) * quarter]
 
-        for i, out_ref in enumerate(out_refs):
-
-            @pl.when(pl.program_id(0) == i)
-            def _():
-                out_ref[:, pl.ds(at, quarter)] = part
+        out_ref[:, pl.ds(at, quarter)] = part
 
     @pl.when(pl.program_id(0) == 0)
     def _():
@@ -1127,10 +1123,10 @@
             num_scalar_prefetch=1,
             grid=(tok // tile,),
             in_specs=[ANY] * len(pieces) + [pair, pair, rows_of(width), rows_of(width), row],
-            out_specs=[pl.BlockSpec((tile, width), lambda i, info: (0, 0))] * 4 + [row],
+            out_specs=[rows_of(width), row],
             scratch_shapes=[pltpu.VMEM((4, width, cols), BF16), pltpu.SemaphoreType.DMA],
         ),
-        out_shape=[shape_of((tile, width), BF16)] * 4 + [shape_of((1, width), F32)],
+        out_shape=[shape_of((tok, width), BF16), shape_of((1, width), F32)],
         compiler_params=settings(1, 60),
         cost_estimate=cost(True),
         name="norm_one_back",
@@ -1657,9 +1653,6 @@
     info = jnp.concatenate([jnp.stack([z, fsdp, ctx]).astype(jnp.int32), length])
     w_proj = join(q_weight, k_weight, v_weight)
     proj_z = [z_up(w_proj), z_far(w_proj), z_down(w_proj)]
-    proj_z[2] = after(proj_z[2], proj_z[0])
-    proj_z[1] = after(proj_z[1], proj_z[2])
-    proj_zfar = [x_swap(block) for block in proj_z]
     proj_own = jnp.concatenate([w_proj, x_swap(w_proj)], axis=0)
     count_here = jnp.sum(lengths).astype(F32)[None]
     vector = jnp.concatenate([attn_gain, ffn_gain, q_gain, k_gain]).astype(F32)
@@ -1671,23 +1664,14 @@
     frequency = THETA ** (-(2.0 * jnp.arange(hd // 2, dtype=F32)) / hd)
     angles = frequency[:, None] * pos[None, :]
     head_gains = natural(vector[:, 2 * quarter : 544])
-    gain_one = vector[:, :quarter].reshape(1, width)
-    x_in, normed_one_t = norm_one(info, tokens, gain_one, 256)
-    out_start = after(w_out, proj_z[1])
-    out_z = [z_up(out_start), z_far(out_start), z_down(out_start)]
     v.update(
         info=info,
         proj_own=proj_own,
         proj_z=jnp.concatenate(proj_z, axis=0),
-        proj_zfar=proj_zfar,
-        own_core=core_swap(proj_own),
         w_out=w_out,
-        out_z=out_z,
         w_ffn=w_ffn,
         w_chunks=w_chunks,
-        x_in=x_in,
-        normed_one_t=normed_one_t,
-        gain_one=gain_one,
+        gain_one=vector[:, :quarter].reshape(1, width),
         gain_two=vector[:, quarter : 2 * quarter].reshape(1, width),
         total_count=jnp.sum(vector[:, 544]),
         gain_q=head_gains[:, : hd // 4].reshape(hd, 1),
@@ -1698,10 +1682,19 @@
     sync()
     info = v["info"]
 
-    plan_proj = [[(0, 0), (0, quarter), (5, 0), (5, quarter)]]
-    plan_proj += [[(1, k * quarter), (2 + k, 0), (6, k * quarter), (7 + k, 0)] for k in range(3)]
-    weights_proj = [v["proj_own"], v["proj_z"]] + v["proj_zfar"] + [v["own_core"]]
-    weights_proj += [core_swap(part) for part in [v["proj_z"]] + v["proj_zfar"]]
+    proj_zfar = x_swap(v["proj_z"])
+    out_z = [z_up(v["w_out"]), z_far(v["w_out"]), z_down(v["w_out"])]
+    own_core = core_swap(v["proj_own"])
+    x_in, normed_one_t = norm_one(info, tokens, v["gain_one"], 256)
+    v.update(
+        proj_zfar=proj_zfar, own_core=own_core, x_in=x_in, normed_one_t=normed_one_t, out_z=out_z
+    )
+    sync()
+
+    plan_proj = [[(0, 0), (0, quarter), (3, 0), (3, quarter)]]
+    plan_proj += [[(p, k * quarter) for p in (1, 2, 4, 5)] for k in range(3)]
+    weights_proj = [v["proj_own"], v["proj_z"], v["proj_zfar"], v["own_core"]]
+    weights_proj += [core_swap(v["proj_z"]), core_swap(v["proj_zfar"])]
     one = [z_up(v["w_chunks"][0]), z_up(v["w_chunks"][3])]
     ffn_far = x_swap(v["w_ffn"])
     tables = [v[name] for name in ("cos_part", "sin_part", "gain_q", "gain_k")]
@@ -2017,7 +2010,7 @@
     head1 = head_back(
         info, v["back1"][0], v["heads1"], v["mine"][1][1], v["theirs"][1][1], *tables, heads
     )
-    *tokens_low, gain_one_sum = norm_one_back(
+    tokens_low, gain_one_sum = norm_one_back(
         info,
         [v["head0"][0], head1[0]],
         (plan_proj, v["weights_proj"]),
@@ -2038,8 +2031,7 @@
         return out
 
     v.update(out_one=v["one"])
-    quarters = v["tokens_low"]
-    one = [z_up(quarters[0])]
+    gathered = lax.all_gather(v["tokens_low"], "tp", axis=0, tiled=False)
     keep, send = weight_grad(
         v["normed_one_t"], [v["head0"][0], v["head1"][0]], v["grad_attn_t"], v["attended"]
     )
@@ -2056,51 +2048,42 @@
         axis=1,
     )
     vector = vector + core_swap(vector)
-    v.update(one=one, keep=keep, send=send)
+    v.update(keep=keep, send=send)
     v.update(vector=vector)
     sync()
 
-    one = v["one"] + [z_up(v["tokens_low"][1])]
     rows = quarter // 2
     flat = lambda a: a.reshape(4 * rows, a.shape[-1])
     attn_sums = [flat(p) for p in core_sum(info, v["keep"], core_swap(v["send"]))]
     vector = v["vector"] + x_swap(v["vector"])
-    v.update(one=one, sums=attn_sums, vector=vector)
-    sync()
-
-    one = v["one"] + [z_up(v["tokens_low"][2])]
+    v.update(sums=attn_sums, vector=vector)
+    sync()
+
     far_t = x_swap(v["sums"][3])
     part0 = summed([v["sum0"][0], v["far_h0"], v["there0"]], turned)
     ffn_sum = summed([part0, v["two_down"], v["up3"]], None, F32)
     vector = v["vector"] + y_swap(v["vector"])
-    v.update(one=one, far_t=far_t, ffn_sum=ffn_sum, vector=vector)
-    sync()
-
-    one = v["one"] + [z_up(v["tokens_low"][3])]
-    three = [z_down(v["tokens_low"][0])]
+    v.update(far_t=far_t, ffn_sum=ffn_sum, vector=vector)
+    sync()
+
     far_h = x_swap(v["sums"][2])
     there = y_swap(summed([v["sums"][1], v["far_t"]]))
     output = jnp.zeros((rows_dev, tok, width), BF16)
     for k, parts in enumerate((v["results"], v["out_one"], v["out_two"], v["out_three"])):
         output = place(output, parts, k, 0)
-    v.update(one=one, three=three, far_h=far_h, there=there, output=output)
-    sync()
-
-    three = v["three"] + [z_down(v["tokens_low"][1])]
+    v.update(far_h=far_h, there=there, output=output)
+    sync()
+
     parts = summed([v["sums"][0], v["far_h"], v["there"]])
     parts = [parts[k * rows : (k + 1) * rows] for k in range(4)]
     parts = [parts[0], z_down(parts[1]), z_far(parts[2]), z_up(parts[3])]
     ffn_other = y_swap(v["ffn_sum"])
-    grad = place(jnp.zeros((rows_dev, tok, width), F32), v["tokens_low"], 0, 0)
-    v.update(three=three, parts=parts, grad=grad)
-    sync()
-
-    three = v["three"] + [z_down(part) for part in v["tokens_low"][2:]]
-    two = [z_up(v["one"][0])]
+    v.update(parts=parts)
+    sync()
+
     attn_sum = summed(v["parts"], None, F32)
     vector = v["vector"] + lax.ppermute(v["vector"], "tp", Z_NEAR)
-    grad = place(v["grad"], v["one"], 1, 0)
-    v.update(three=three, two=two, attn_sum=attn_sum, vector=vector, grad=grad)
+    v.update(attn_sum=attn_sum, vector=vector)
     v.update(ffn_other=ffn_other)
     sync()
 
@@ -2120,7 +2103,6 @@
             axis=1,
         )
 
-    two = v["two"] + [z_up(part) for part in v["one"][1:]]
     attn_other = y_swap(v["attn_sum"])
     vector = v["vector"] + lax.ppermute(v["vector"], "tp", Z_FAR)
     third = units // 3
@@ -2128,13 +2110,11 @@
     grad_gate = columns(lambda j: 2 * j * third)
     grad_up = columns(lambda j: (2 * j + 1) * third)
     grad_down = columns(lambda j: 2 * units + j * third).T
-    grad = place(v["grad"], v["three"], 3, 0)
-    grad = place(grad, v["two"], 2, 0)
-    v.update(vector=vector, grad=grad, attn_other=attn_other)
-    v.update(grad_gate=grad_gate, grad_up=grad_up, grad_down=grad_down, two=two)
-    sync()
-
-    tokens_grad = place(v["grad"], v["two"][1:], 2, 1)
+    v.update(vector=vector, attn_other=attn_other)
+    v.update(grad_gate=grad_gate, grad_up=grad_up, grad_down=grad_down)
+    sync()
+
+    tokens_grad = gathered.astype(F32)
     output = v["output"]
     sums_all = v["vector"][0]
 

time: 803 us -> 764 us (0.951)
  starting transfers between devices: 106 us -> 83.6 us
  local copies, waits for them, and re-layouts: 86.7 us -> 66.4 us
  Pallas kernels: 368 us -> 385 us
  between operations: 6.37 us -> 19.4 us
  waiting for transfers between devices: 190 us -> 177 us
  other arithmetic: 34.5 us -> 22.3 us
    ppermute x20 -> x12, waiting for transfers between devices: 67.1 us -> 21 us  [z_up(): return lax.ppermute(v, 'tp', Z_UP)]
    ppermute x3, waiting for transfers between devices: 8.51 us -> 31.3 us  [z_far(): return lax.ppermute(v, 'tp', Z_FAR)]
    dynamic_update_slice x16 -> x0, other arithmetic: 22.6 us -> none  [place(): lax.dynamic_update_slice(out, part.astype(out.dtype)[None], (row, at, 0))]
    all_gather x0 -> x1, waiting for transfers between devices: none -> 20.4 us  [per_device_rows(): gathered = lax.all_gather(v['tokens_low'], 'tp', axis=0, tiled=False)]
    pallas_call x2, Pallas kernels: 34.5 us -> 49.4 us  [attn_bwd(): pl.pallas_call(functools.partial(attn_bwd_kernel, width, hd), grid_spec=p...]
    ppermute x14 -> x10, waiting for transfers between devices: 28.5 us -> 15.7 us  [z_down(): return lax.ppermute(v, 'tp', Z_DOWN)]
    convert_element_type x0 -> x1, other arithmetic: none -> 11.7 us  [per_device_rows(): tokens_grad = gathered.astype(F32)]
    ppermute x14 -> x10, starting transfers between devices: 28 us -> 17.3 us  [z_down(): return lax.ppermute(v, 'tp', Z_DOWN)]
  transfers between devices with their start and end apart: 114 -> 99, of which waited for: 42 -> 31; matrix products, arithmetic and copies ran while one was open for 9% -> 5% of each run, Pallas kernels for 40% -> 45%
where the time goes in v12:
time: 764 us; the launch traced here: 753 us
  Pallas kernels  385 us (50%)
  waiting for transfers between devices  177 us (23%)
  starting transfers between devices  83.6 us (11%)
  local copies, waits for them, and re-layouts  66.4 us (9%)
  other arithmetic  22.3 us (3%)
  between operations  19.4 us (3%)
    pallas_call x4, Pallas kernels, ffn_bwd(): pl.pallas_call(functools.partial(ffn_bwd_kernel, steps, plan, first), gri...  101 us
    pallas_call x3, Pallas kernels, ffn_fwd(): pl.pallas_call(functools.partial(ffn_fwd_kernel, tile, [plan for plan, _...  62.8 us
    pallas_call x2, Pallas kernels, attn_bwd(): pl.pallas_call(functools.partial(attn_bwd_kernel, width, hd), grid_spec=p...  49.4 us
    ppermute x22, waiting for transfers between devices, x_swap(): return lax.ppermute(v, 'fsdp', X_SWAP)  42.7 us
    unnamed x161, local copies, waits for them, and re-layouts  39.7 us
    ppermute x19, waiting for transfers between devices, y_swap(): return lax.ppermute(v, 'ctx', Y_SWAP)  36.8 us
    pallas_call x2, Pallas kernels, attn_fwd(): pl.pallas_call(functools.partial(attn_fwd_kernel, width, hd), grid_spec=p...  35.5 us
    pallas_call x6, Pallas kernels, sums(): pl.pallas_call(functools.partial(sums_kernel, jobs, len(arrays)), grid_sp...  33.4 us
  transfers between devices with their start and end apart: 99, of which 31 were waited for; matrix products, arithmetic and copies ran while one was open for 5% of the time, Pallas kernels for 45%

profile of v12, /device:TPU:0, one launch (start us, length us, event | category | flops | bytes accessed | tf_op | source)
XLA Modules:
  0.0 753.4 jit_solution(15496963240654353423)
XLA Ops:
  86.7 13.0 %collective-permute-done.15.rest_4_.rest_0_ = bf16[256,1152]{1,0:T(8,128)(2,1)} collective-permute-done((bf16[256,1152]{1,0:T(8,128)(2,1)}, bf16[256,1152]{1,0:T(8,128)(2,1)}, u32[]{:S(2)}, u32[]{:S(2)}) %collective-permute-start.15) | collective-permute-done | bytes 589856 | tf_op jit(solution)/shard_map/ppermute | solution.py:1634
  102.2 17.8 %attn_fwd.2 = (bf16[1024,256]{1,0:T(8,128)(2,1)}, bf16[1024,256]{1,0:T(8,128)(2,1)}, f32[2,2,2048]{2,1,0:T(2,128)}) custom-call(s32[4]{0:T(128)} %copy-done.22, bf16[512,1024]{1,0:T(8,128)(2,1)} %copy-done.29, bf16[512,1024]{1,0:T(8,128)(2,1)} %copy-done.57), custom_call_target="tpu_custom_call" | custom-call | flops 4398046511104 | bytes 1073741824 | tf_op jit(solution)/shard_map/attn_fwd/pallas_call | solution.py:782
  127.1 17.8 %attn_fwd.3 = (bf16[1024,256]{1,0:T(8,128)(2,1)}, bf16[1024,256]{1,0:T(8,128)(2,1)}, f32[2,2,2048]{2,1,0:T(2,128)}) custom-call(s32[4]{0:T(128)} %copy-done.22, bf16[512,1024]{1,0:T(8,128)(2,1)} %copy-done.28, bf16[512,1024]{1,0:T(8,128)(2,1)} %collective-permute-done.17.got_ref), custom_call_target="tpu_custom_call" | custom-call | flops 4398046511104 | bytes 1073741824 | tf_op jit(solution)/shard_map/attn_fwd/pallas_call | solution.py:782
  150.3 12.2 %collective-permute-done.27.refs_8_ = bf16[1024,256]{1,0:T(8,128)(2,1)S(1)} collective-permute-done((bf16[1024,256]{1,0:T(8,128)(2,1)}, bf16[1024,256]{1,0:T(8,128)(2,1)S(1)}, u32[]{:S(2)}, u32[]{:S(2)}) %collective-permute-start.27) | collective-permute-done | bytes 524320 | tf_op jit(solution)/shard_map/ppermute | solution.py:1631
  166.2 10.3 %out_proj.1 = (f32[1024,1024]{1,0:T(8,128)}, bf16[1024,1024]{1,0:T(8,128)(2,1)}, bf16[1024,1024]{1,0:T(8,128)(2,1)}, bf16[4,1024,256]{2,1,0:T(8,128)(2,1)}) custom-call(s32[4]{0:T(128)} %copy-done.22, bf16[1024,256]{1,0:T(8,128)(2,1)} %constant_dynamic-update-slice_fusion.refs_0_, bf16[1024,256]{1,0:T(8,128)(2,1)} %collective-permute-done.25.refs_1_, ...), custom_call_target="tpu_custom_call" | custom-call | flops 4398046511104 | bytes 1073741824 | tf_op jit(solution)/shard_map/out_proj/pallas_call | solution.py:1008
  187.8 27.2 %ffn_fwd.3 = (bf16[2,1024,2304]{2,1,0:T(8,128)(2,1)}, bf16[2,1024,1152]{2,1,0:T(8,128)(2,1)}, f32[1024,1024]{1,0:T(8,128)}) custom-call(s32[4]{0:T(128)} %copy-done.22, f32[1]{0:T(128)} %bitcast.4.scale, bf16[1024,1024]{1,0:T(8,128)(2,1)} %get-tuple-element.1852.x_ref, f32[1024,1024]{1,0:T(8,128)} %get-tuple-element.2418.in_ref.refs_5_, ...), custom_call_target="tpu_custom_call" | custom-call | flops 4398046511104 | bytes 1073741824 | tf_op jit(solution)/shard_map/ffn_fwd/pallas_call | solution.py:1312
  222.4 15.8 %ffn_fwd.4 = (bf16[1,1024,2304]{2,1,0:T(8,128)(2,1)}, bf16[1,1024,1152]{2,1,0:T(8,128)(2,1)}, f32[1024,1024]{1,0:T(8,128)}) custom-call(s32[4]{0:T(128)} %copy-done.22, f32[1]{0:T(128)} %bitcast.4.scale, bf16[1024,1024]{1,0:T(8,128)(2,1)} %get-tuple-element.1852.x_ref, f32[1024,1024]{1,0:T(8,128)} %get-tuple-element.1754.in_ref, ...), custom_call_target="tpu_custom_call" | custom-call | flops 4398046511104 | bytes 1073741824 | tf_op jit(solution)/shard_map/ffn_fwd/pallas_call | solution.py:1312
  242.1 19.8 %ffn_fwd.5 = (bf16[1,1024,2304]{2,1,0:T(8,128)(2,1)}, bf16[1,1024,1152]{2,1,0:T(8,128)(2,1)}, bf16[512,1024]{1,0:T(8,128)(2,1)}, bf16[512,1024]{1,0:T(8,128)(2,1...) custom-call(s32[4]{0:T(128)} %copy-done.22, ...), custom_call_target="tpu_custom_call" | custom-call | flops 4398046511104 | bytes 1073741824 | tf_op jit(solution)/shard_map/ffn_fwd/pallas_call | solution.py:1312
  262.4 24.9 %ffn_bwd.4 = (f32[1024,1024]{1,0:T(8,128)}, bf16[512,3456]{1,0:T(8,128)(2,1)}, bf16[512,3456]{1,0:T(8,128)(2,1)}) custom-call(bf16[1024,1024]{1,0:T(8,128)(2,1)} %get-tuple-element.2341.low_ref, bf16[1,1024,2304]{2,1,0:T(8,128)(2,1)} %get-tuple-element.1974.act_ref, bf16[1,1024,1152]{2,1,0:T(8,128)(2,1)} %get-tuple-element.1994.hid_ref, ...), custom_call_target="tpu_custom_call" | custom-call | flops 4398046511104 | bytes 1073741824 | tf_op jit(solution)/shard_map/ffn_bwd/pallas_call | solution.py:1394
  289.7 25.3 %ffn_bwd.5 = (f32[1024,1024]{1,0:T(8,128)}, bf16[512,3456]{1,0:T(8,128)(2,1)}, bf16[512,3456]{1,0:T(8,128)(2,1)}) custom-call(bf16[1024,1024]{1,0:T(8,128)(2,1)} %get-tuple-element.2341.low_ref, bf16[2,1024,2304]{2,1,0:T(8,128)(2,1)} %get-tuple-element.2325.act_ref, ...), custom_call_target="tpu_custom_call", output_to_operand_aliasing={{0}: (15, {})} | custom-call | flops 4398046511104 | bytes 1073741824 | tf_op jit(solution)/shard_map/ffn_bwd/pallas_call | solution.py:1394
  325.6 25.3 %ffn_bwd.6 = (f32[1024,1024]{1,0:T(8,128)}, bf16[512,3456]{1,0:T(8,128)(2,1)}, bf16[512,3456]{1,0:T(8,128)(2,1)}) custom-call(bf16[1024,1024]{1,0:T(8,128)(2,1)} %get-tuple-element.2341.low_ref, bf16[1,1024,2304]{2,1,0:T(8,128)(2,1)} %get-tuple-element.2249.act_ref, ...), custom_call_target="tpu_custom_call", output_to_operand_aliasing={{0}: (17, {})} | custom-call | flops 4398046511104 | bytes 1073741824 | tf_op jit(solution)/shard_map/ffn_bwd/pallas_call | solution.py:1394
  361.6 25.3 %ffn_bwd.7 = (f32[1024,1024]{1,0:T(8,128)}, bf16[512,3456]{1,0:T(8,128)(2,1)}, bf16[512,3456]{1,0:T(8,128)(2,1)}) custom-call(bf16[1024,1024]{1,0:T(8,128)(2,1)} %get-tuple-element.2341.low_ref, bf16[2,1024,2304]{2,1,0:T(8,128)(2,1)} %get-tuple-element.2325.act_ref, ...), custom_call_target="tpu_custom_call", output_to_operand_aliasing={{0}: (9, {})} | custom-call | flops 4398046511104 | bytes 1073741824 | tf_op jit(solution)/shard_map/ffn_bwd/pallas_call | solution.py:1394
  396.0 12.4 %norm_two_back.1 = (f32[1024,1024]{1,0:T(8,128)}, bf16[1024,1024]{1,0:T(8,128)(2,1)}, bf16[1024,256]{1,0:T(8,128)(2,1)}, bf16[1024,256]{1,0:T(8,128)(2,1)}, bf16...) custom-call(s32[4]{0:T(128)} %copy-done.22, ...), custom_call_target="tpu_custom_call" | custom-call | flops 4398046511104 | bytes 1073741824 | tf_op jit(solution)/shard_map/norm_two_back/pallas_call | solution.py:1066
  410.5 12.9 %collective-permute-done.68.gs_ref = bf16[1024,256]{1,0:T(8,128)(2,1)S(1)} collective-permute-done((bf16[1024,256]{1,0:T(8,128)(2,1)}, bf16[1024,256]{1,0:T(8,128)(2,1)S(1)}, u32[]{:S(2)}, u32[]{:S(2)}) %collective-permute-start.68) | collective-permute-done | bytes 524320 | tf_op jit(solution)/shard_map/ppermute | solution.py:1631
  434.4 24.6 %attn_bwd.2 = (bf16[512,1024]{1,0:T(8,128)(2,1)}, bf16[512,1024]{1,0:T(8,128)(2,1)}) custom-call(s32[4]{0:T(128)} %copy-done.22, bf16[512,1024]{1,0:T(8,128)(2,1)} %copy-done.29, bf16[512,1024]{1,0:T(8,128)(2,1)} %copy-done.57, bf16[1024,256]{1,0:T(8,128)(2,1)} %get-tuple-element.2464.refs_5_.ok_ref, bf16[1024,256]{1,0:T(8,128)(2,1)} %get-tuple-element.2465.os_ref, ...), custom_call_target="tpu_custom_call" | custom-call | flops 4398046511104 | bytes 1073741824 | tf_op jit(solution)/shard_map/attn_bwd/pallas_call | solution.py:943
  459.1 12.3 %collective-permute-done.70.refs_1_ = bf16[128,3456]{1,0:T(8,128)(2,1)} collective-permute-done((bf16[128,3456]{1,0:T(8,128)(2,1)}, bf16[128,3456]{1,0:T(8,128)(2,1)}, u32[]{:S(2)}, u32[]{:S(2)}) %collective-permute-start.70) | collective-permute-done | bytes 884768 | tf_op jit(solution)/shard_map/ppermute | solution.py:1625
  480.2 24.8 %attn_bwd.3 = (bf16[512,1024]{1,0:T(8,128)(2,1)}, bf16[512,1024]{1,0:T(8,128)(2,1)}) custom-call(s32[4]{0:T(128)} %copy-done.22, bf16[512,1024]{1,0:T(8,128)(2,1)} %copy-done.28, bf16[512,1024]{1,0:T(8,128)(2,1)} %collective-permute-done.17.got_ref, bf16[1024,256]{1,0:T(8,128)(2,1)} %get-tuple-element.2528.refs_6_.ok_ref, ...), custom_call_target="tpu_custom_call" | custom-call | flops 4398046511104 | bytes 1073741824 | tf_op jit(solution)/shard_map/attn_bwd/pallas_call | solution.py:943
  505.0 10.6 %collective-permute-done.75.refs_4_ = bf16[128,3456]{1,0:T(8,128)(2,1)} collective-permute-done((bf16[128,3456]{1,0:T(8,128)(2,1)}, bf16[128,3456]{1,0:T(8,128)(2,1)}, u32[]{:S(2)}, u32[]{:S(2)}) %collective-permute-start.75) | collective-permute-done | bytes 884768 | tf_op jit(solution)/shard_map/ppermute | solution.py:1625
  550.1 12.3 %norm_one_back.1 = (bf16[1024,1024]{1,0:T(8,128)(2,1)}, f32[1,1024]{1,0:T(1,128)}) custom-call(s32[4]{0:T(128)} %copy-done.22, bf16[512,512]{1,0:T(8,128)(2,1)} %copy-done.2, bf16[768,512]{1,0:T(8,128)(2,1)} %copy-done.1, bf16[768,512]{1,0:T(8,128)(2,1)} %collective-permute-done.10.refs_2_, bf16[512,512]{1,0:T(8,128)(2,1)} %copy-done.4, ...), custom_call_target="tpu_custom_call" | custom-call | flops 4398046511104 | bytes 1073741824 | tf_op jit(solution)/shard_map/norm_one_back/pallas_call | solution.py:1120
  565.5 16.1 %weight_grad.1 = (bf16[4,512,768]{2,1,0:T(8,128)(2,1)}, bf16[4,512,768]{2,1,0:T(8,128)(2,1)}) custom-call(bf16[1024,1024]{1,0:T(8,128)(2,1)} %copy-done, bf16[2,1024,512]{2,1,0:T(8,128)(2,1)} %get-tuple-element.2666.refs_6_.back0_ref, bf16[2,1024,512]{2,1,0:T(8,128)(2,1)} %get-tuple-element.2668.refs_7_.back1_ref, ...), custom_call_target="tpu_custom_call" | custom-call | flops 4398046511104 | bytes 1073741824 | tf_op jit(solution)/shard_map/weight_grad/pallas_call | solution.py:1577
  602.3 11.8 %collective-permute-done.87.refs_1_ = bf16[512,768]{1,0:T(8,128)(2,1)S(1)} collective-permute-done((bf16[512,768]{1,0:T(8,128)(2,1)S(1)}, bf16[512,768]{1,0:T(8,128)(2,1)S(1)}, u32[]{:S(2)}, u32[]{:S(2)}) %collective-permute-start.87) | collective-permute-done | bytes 786464 | tf_op jit(solution)/shard_map/ppermute | solution.py:1625
  660.1 29.6 %collective-permute-done.92.refs_2_ = bf16[128,768]{1,0:T(8,128)(2,1)S(1)} collective-permute-done((bf16[128,768]{1,0:T(8,128)(2,1)S(1)}, bf16[128,768]{1,0:T(8,128)(2,1)S(1)}, u32[]{:S(2)}, u32[]{:S(2)}) %collective-permute-start.92) | collective-permute-done | bytes 196640 | tf_op jit(solution)/shard_map/ppermute | solution.py:1637
  713.1 20.4 %all-gather.3.cloned.1.call-done = bf16[4096,1024]{1,0:T(8,128)(2,1)} async-done(((bf16[1024,1024]{1,0:T(8,128)(2,1)}), bf16[4096,1024]{1,0:T(8,128)(2,1)}) %all-gather.3.cloned.1.call-update) | async-done | bytes 8388624 | tf_op jit(solution)/shard_map/all_gather | solution.py:2034
  733.5 11.7 %convert = f32[4,1024,1024]{2,1,0:T(8,128)} convert(bf16[4,1024,1024]{2,1,0:T(8,128)(2,1)} %bitcast.63) | non-fusion elementwise | flops 4194304 | bytes 25165824 | tf_op jit(solution)/shard_map/convert_element_type | solution.py:2117
  (443 shorter events, 299.7 us)
Async XLA Ops:
  7.2 726.3 %all-gather.3.cloned.1.call-start = ((), (), s32[]{:S(2)}) async-start(), calls=%async_computation | async-start | bytes 10485760 | tf_op jit(solution)/shard_map/all_gather | solution.py:2034
  56.4 43.3 %collective-permute-start.11 = (bf16[256,3456]{1,0:T(8,128)(2,1)}, bf16[256,3456]{1,0:T(8,128)(2,1)}, u32[]{:S(2)}, u32[]{:S(2)}) collective-permute-start(bf16[256,3456]{1,0:T(8,128)(2,1)} %get-tuple-element.2346.rest_0_), channel_id=1, source_target_pairs={{0,16},{16,0},{8,24},{24,8},{1,17},{17,1},{9,25},{25,9},{2,18},{18... | collective-permute-start | bytes 5308424 | tf_op jit(solution)/shard_map/ppermute | solution.py:1625
  57.3 42.4 %collective-permute-start.16 = (bf16[256,2304]{1,0:T(8,128)(2,1)}, bf16[256,2304]{1,0:T(8,128)(2,1)}, u32[]{:S(2)}, u32[]{:S(2)}) collective-permute-start(bf16[256,2304]{1,0:T(8,128)(2,1)} %get-tuple-element.1440), channel_id=1, source_target_pairs={{0,1},{1,2},{2,3},{3,0},{4,5},{5,6},{6,7},{7,4},{8,9},{9,10},{10,1... | collective-permute-start | bytes 3538952 | tf_op jit(solution)/shard_map/ppermute | solution.py:1634
  70.1 29.6 %collective-permute-start.14 = (bf16[512,1024]{1,0:T(8,128)(2,1)S(1)}, bf16[512,1024]{1,0:T(8,128)(2,1)S(1)}, u32[]{:S(2)}, u32[]{:S(2)}) collective-permute-start(bf16[512,1024]{1,0:T(8,128)(2,1)S(1)} %get-tuple-element.1429), channel_id=1, source_target_pairs={{0,4},{4,0},{1,5},{5,1},{2,6},{6,2},{3,7},{7,3},{8,12},{12,8},{9,1... | collective-permute-start | bytes 3145736 | tf_op jit(solution)/shard_map/ppermute | solution.py:1631
  75.5 44.5 %collective-permute-start.17 = (bf16[512,1024]{1,0:T(8,128)(2,1)}, bf16[512,1024]{1,0:T(8,128)(2,1)}, u32[]{:S(2)}, u32[]{:S(2)}) collective-permute-start(bf16[512,1024]{1,0:T(8,128)(2,1)} %get-tuple-element.1432), channel_id=1, source_target_pairs={{0,4},{4,0},{1,5},{5,1},{2,6},{6,2},{3,7},{7,3},{8,12},{12,8},{9,1... | collective-permute-start | bytes 3145736 | tf_op jit(solution)/shard_map/ppermute | solution.py:1631
  182.9 32.1 %collective-permute-start.41 = (bf16[256,2304]{1,0:T(8,128)(2,1)}, bf16[256,2304]{1,0:T(8,128)(2,1)}, u32[]{:S(2)}, u32[]{:S(2)}) collective-permute-start(bf16[256,2304]{1,0:T(8,128)(2,1)} %collective-permute-done.16.rest_5_.rest_1_), channel_id=1, source_target_pairs={{0,1},{1,2},{2,3},{3,0},{4,5},{5,6},{6,7},{7,4},{8,9},{9,10},{10,1... | collective-permute-start | bytes 3538952 | tf_op jit(solution)/shard_map/ppermute | solution.py:1634
  182.9 32.1 %collective-permute-start.38 = (bf16[256,1152]{1,0:T(8,128)(2,1)}, bf16[256,1152]{1,0:T(8,128)(2,1)}, u32[]{:S(2)}, u32[]{:S(2)}) collective-permute-start(bf16[256,1152]{1,0:T(8,128)(2,1)} %collective-permute-done.21.rest_0_), channel_id=1, source_target_pairs={{0,8},{8,0},{16,24},{24,16},{1,9},{9,1},{17,25},{25,17},{2,10},{10... | collective-permute-start | bytes 1769480 | tf_op jit(solution)/shard_map/ppermute | solution.py:1628
  183.4 31.6 %collective-permute-start.39 = (bf16[256,1152]{1,0:T(8,128)(2,1)}, bf16[256,1152]{1,0:T(8,128)(2,1)}, u32[]{:S(2)}, u32[]{:S(2)}) collective-permute-start(bf16[256,1152]{1,0:T(8,128)(2,1)} %collective-permute-done.26.rest_1_), channel_id=1, source_target_pairs={{0,16},{16,0},{8,24},{24,8},{1,17},{17,1},{9,25},{25,9},{2,18},{18... | collective-permute-start | bytes 1769480 | tf_op jit(solution)/shard_map/ppermute | solution.py:1625
  183.8 31.2 %collective-permute-start.40 = (bf16[256,1152]{1,0:T(8,128)(2,1)}, bf16[256,1152]{1,0:T(8,128)(2,1)}, u32[]{:S(2)}, u32[]{:S(2)}) collective-permute-start(bf16[256,1152]{1,0:T(8,128)(2,1)} %collective-permute-done.35.rest_3_), channel_id=1, source_target_pairs={{0,4},{4,0},{1,5},{5,1},{2,6},{6,2},{3,7},{7,3},{8,12},{12,8},{9,1... | collective-permute-start | bytes 1769480 | tf_op jit(solution)/shard_map/ppermute | solution.py:1631
  357.2 29.7 %collective-permute-start.64 = (bf16[128,3456]{1,0:T(8,128)(2,1)}, bf16[128,3456]{1,0:T(8,128)(2,1)}, u32[]{:S(2)}, u32[]{:S(2)}) collective-permute-start(bf16[128,3456]{1,0:T(8,128)(2,1)} %get-tuple-element.2380), channel_id=1, source_target_pairs={{0,4},{4,0},{1,5},{5,1},{2,6},{6,2},{3,7},{7,3},{8,12},{12,8},{9,1... | collective-permute-start | bytes 2654216 | tf_op jit(solution)/shard_map/ppermute | solution.py:1631
  393.7 29.8 %collective-permute-start.66 = (bf16[128,3456]{1,0:T(8,128)(2,1)}, bf16[128,3456]{1,0:T(8,128)(2,1)}, u32[]{:S(2)}, u32[]{:S(2)}) collective-permute-start(bf16[128,3456]{1,0:T(8,128)(2,1)} %get-tuple-element.2402), channel_id=1, source_target_pairs={{0,3},{1,0},{2,1},{3,2},{4,7},{5,4},{6,5},{7,6},{8,11},{9,8},{10,9... | collective-permute-start | bytes 2654216 | tf_op jit(solution)/shard_map/ppermute | solution.py:1640
  410.0 49.0 %collective-permute-start.71 = (bf16[1024,256]{1,0:T(8,128)(2,1)}, bf16[1024,256]{1,0:T(8,128)(2,1)}, u32[]{:S(2)}, u32[]{:S(2)}) collective-permute-start(bf16[1024,256]{1,0:T(8,128)(2,1)} %get-tuple-element.2487), channel_id=1, source_target_pairs={{0,4},{4,0},{1,5},{5,1},{2,6},{6,2},{3,7},{7,3},{8,12},{12,8},{9,1... | collective-permute-start | bytes 1572872 | tf_op jit(solution)/shard_map/ppermute | solution.py:1631
  429.9 29.2 %collective-permute-start.73 = (bf16[128,3456]{1,0:T(8,128)(2,1)}, bf16[128,3456]{1,0:T(8,128)(2,1)}, u32[]{:S(2)}, u32[]{:S(2)}) collective-permute-start(bf16[128,3456]{1,0:T(8,128)(2,1)} %get-tuple-element.2514), channel_id=1, source_target_pairs={{0,4},{4,0},{1,5},{5,1},{2,6},{6,2},{3,7},{7,3},{8,12},{12,8},{9,1... | collective-permute-start | bytes 2654216 | tf_op jit(solution)/shard_map/ppermute | solution.py:1631
  431.5 39.9 %collective-permute-start.72 = (bf16[512,1024]{1,0:T(8,128)(2,1)}, bf16[512,1024]{1,0:T(8,128)(2,1)}, u32[]{:S(2)}, u32[]{:S(2)}) collective-permute-start(bf16[512,1024]{1,0:T(8,128)(2,1)} %collective-permute-done.55), channel_id=1, source_target_pairs={{0,1},{1,2},{2,3},{3,0},{4,5},{5,6},{6,7},{7,4},{8,9},{9,10},{10,1... | collective-permute-start | bytes 3145736 | tf_op jit(solution)/shard_map/ppermute | solution.py:1634
  433.6 37.7 %collective-permute-start.70 = (bf16[128,3456]{1,0:T(8,128)(2,1)}, bf16[128,3456]{1,0:T(8,128)(2,1)}, u32[]{:S(2)}, u32[]{:S(2)}) collective-permute-start(bf16[128,3456]{1,0:T(8,128)(2,1)} %get-tuple-element.2480), channel_id=1, source_target_pairs={{0,16},{16,0},{8,24},{24,8},{1,17},{17,1},{9,25},{25,9},{2,18},{18... | collective-permute-start | bytes 2654216 | tf_op jit(solution)/shard_map/ppermute | solution.py:1625
  475.7 29.3 %collective-permute-start.78 = (bf16[128,3456]{1,0:T(8,128)(2,1)}, bf16[128,3456]{1,0:T(8,128)(2,1)}, u32[]{:S(2)}, u32[]{:S(2)}) collective-permute-start(bf16[128,3456]{1,0:T(8,128)(2,1)} %get-tuple-element.2537), channel_id=1, source_target_pairs={{0,4},{4,0},{1,5},{5,1},{2,6},{6,2},{3,7},{7,3},{8,12},{12,8},{9,1... | collective-permute-start | bytes 2654216 | tf_op jit(solution)/shard_map/ppermute | solution.py:1631
  476.5 41.5 %collective-permute-start.76 = (bf16[512,1024]{1,0:T(8,128)(2,1)}, bf16[512,1024]{1,0:T(8,128)(2,1)}, u32[]{:S(2)}, u32[]{:S(2)}) collective-permute-start(bf16[512,1024]{1,0:T(8,128)(2,1)} %get-tuple-element.2525), channel_id=1, source_target_pairs={{0,4},{4,0},{1,5},{5,1},{2,6},{6,2},{3,7},{7,3},{8,12},{12,8},{9,1... | collective-permute-start | bytes 3145736 | tf_op jit(solution)/shard_map/ppermute | solution.py:1631
  477.8 40.3 %collective-permute-start.77 = (bf16[512,1024]{1,0:T(8,128)(2,1)}, bf16[512,1024]{1,0:T(8,128)(2,1)}, u32[]{:S(2)}, u32[]{:S(2)}) collective-permute-start(bf16[512,1024]{1,0:T(8,128)(2,1)} %collective-permute-done.57), channel_id=1, source_target_pairs={{0,1},{1,2},{2,3},{3,0},{4,5},{5,6},{6,7},{7,4},{8,9},{9,10},{10,1... | collective-permute-start | bytes 3145736 | tf_op jit(solution)/shard_map/ppermute | solution.py:1634
  479.4 36.2 %collective-permute-start.75 = (bf16[128,3456]{1,0:T(8,128)(2,1)}, bf16[128,3456]{1,0:T(8,128)(2,1)}, u32[]{:S(2)}, u32[]{:S(2)}) collective-permute-start(bf16[128,3456]{1,0:T(8,128)(2,1)} %get-tuple-element.2546), channel_id=1, source_target_pairs={{0,16},{16,0},{8,24},{24,8},{1,17},{17,1},{9,25},{25,9},{2,18},{18... | collective-permute-start | bytes 2654216 | tf_op jit(solution)/shard_map/ppermute | solution.py:1625
  527.3 35.1 %collective-permute-start.83 = (bf16[128,3456]{1,0:T(8,128)(2,1)}, bf16[128,3456]{1,0:T(8,128)(2,1)}, u32[]{:S(2)}, u32[]{:S(2)}) collective-permute-start(bf16[128,3456]{1,0:T(8,128)(2,1)} %get-tuple-element.2660), channel_id=1, source_target_pairs={{0,1},{1,2},{2,3},{3,0},{4,5},{5,6},{6,7},{7,4},{8,9},{9,10},{10,1... | collective-permute-start | bytes 2654216 | tf_op jit(solution)/shard_map/ppermute | solution.py:1634
  527.5 34.9 %collective-permute-start.81 = (bf16[128,3456]{1,0:T(8,128)(2,1)}, bf16[128,3456]{1,0:T(8,128)(2,1)}, u32[]{:S(2)}, u32[]{:S(2)}) collective-permute-start(bf16[128,3456]{1,0:T(8,128)(2,1)} %get-tuple-element.2611), channel_id=1, source_target_pairs={{0,16},{16,0},{8,24},{24,8},{1,17},{17,1},{9,25},{25,9},{2,18},{18... | collective-permute-start | bytes 2654216 | tf_op jit(solution)/shard_map/ppermute | solution.py:1625
  639.4 56.0 %collective-permute-start.94 = (f32[128,3456]{1,0:T(8,128)S(1)}, f32[128,3456]{1,0:T(8,128)}, u32[]{:S(2)}, u32[]{:S(2)}) collective-permute-start(f32[128,3456]{1,0:T(8,128)S(1)} %copy-done.33), channel_id=1, source_target_pairs={{0,4},{4,0},{1,5},{5,1},{2,6},{6,2},{3,7},{7,3},{8,12},{12,8},{9,1... | collective-permute-start | bytes 5308424 | tf_op jit(solution)/shard_map/ppermute | solution.py:1631
  650.4 39.2 %collective-permute-start.92 = (bf16[128,768]{1,0:T(8,128)(2,1)S(1)}, bf16[128,768]{1,0:T(8,128)(2,1)S(1)}, u32[]{:S(2)}, u32[]{:S(2)}) collective-permute-start(bf16[128,768]{1,0:T(8,128)(2,1)S(1)} %get-tuple-element.2819), channel_id=1, source_target_pairs={{0,2},{2,0},{1,3},{3,1},{4,6},{6,4},{5,7},{7,5},{8,10},{10,8},{9,1... | collective-permute-start | bytes 589832 | tf_op jit(solution)/shard_map/ppermute | solution.py:1637
  650.4 39.2 %collective-permute-start.93 = (bf16[128,768]{1,0:T(8,128)(2,1)S(1)}, bf16[128,768]{1,0:T(8,128)(2,1)S(1)}, u32[]{:S(2)}, u32[]{:S(2)}) collective-permute-start(bf16[128,768]{1,0:T(8,128)(2,1)S(1)} %get-tuple-element.2818), channel_id=1, source_target_pairs={{0,1},{1,2},{2,3},{3,0},{4,5},{5,6},{6,7},{7,4},{8,9},{9,10},{10,1... | collective-permute-start | bytes 589832 | tf_op jit(solution)/shard_map/ppermute | solution.py:1634
  (148 other events, 1980.7 us)
Sparse Core Ops, SparseCore 0:
  565.6 167.8 all-gather.2

commit v13 on v12

--- a/solution.py
+++ b/solution.py
@@ -407,8 +407,10 @@
     return jax.ShapeDtypeStruct(shape, dtype)
 
 
-def cost(large):
+def cost(large, microseconds=None):
     size = 1 << 42 if large else 1 << 10
+    if microseconds is not None:
+        size = int(microseconds * 1.15e9)
     return pl.CostEstimate(flops=size, bytes_accessed=size >> 12, transcendentals=0)
 
 
@@ -723,33 +725,27 @@
     start = pl.multiple_of(block * width, width)
     both = rows[pl.ds(query_at, 2 * hd), pl.ds(start, width)]
     query = query_with_one(by_halves(both[:hd], both[hd:]))
-    half = width // 2
-
-    def terms(at, keys, query, mask):
-        scores = dot(key_rows[pl.ds(at, keys), :], query, 1, 0)
-        if mask:
-            part = causal(scores[:, :width])
-            wide = scores.shape[1] > width
-            scores = jnp.concatenate([part, scores[:, width:]], axis=1) if wide else part
+
+    def tile(at, carried, diagonal):
+        out, total = carried
+        scores = dot(key_rows[pl.ds(at, width), :], query, 1, 0)
+        if diagonal:
+            key_pos = lax.broadcasted_iota(jnp.int32, (width, width), 0)
+            query_pos = lax.broadcasted_iota(jnp.int32, (width, width), 1)
+            allowed = key_pos <= query_pos
+            allowed = by_halves(allowed, allowed)
+            scores = jnp.where(allowed, scores, NEGATIVE)
         probs = jnp.exp2(scores * scale)
-        total = jnp.sum(probs, axis=0, keepdims=True)
-        return dot(rows[pl.ds(value_at, hd), pl.ds(at, keys)], probs.astype(BF16), 1, 0), total
-
-    def tile(at, carried):
-        more, sums = terms(at, width, query, False)
-        return carried[0] + more, carried[1] + sums
+        total = total + jnp.sum(probs, axis=0, keepdims=True)
+        out = out + dot(rows[pl.ds(value_at, hd), pl.ds(at, width)], probs.astype(BF16), 1, 0)
+        return out, total
 
     carried = (jnp.zeros((hd, 2 * width), F32), jnp.zeros((1, 2 * width), F32))
     full = jnp.minimum(block, lax.div(length + width - 1, width))
     carried = lax.fori_loop(
-        0, full, lambda j, c: tile(pl.multiple_of(j * width, width), c), carried
-    )
-    more, sums = terms(start, half, query, True)
-    out, total = carried[0] + more, carried[1] + sums
-    later = pl.multiple_of(start + half, half)
-    more, sums = terms(later, half, query[:, width:], True)
-    out = jnp.concatenate([out[:, :width], out[:, width:] + more], axis=1)
-    total = jnp.concatenate([total[:, :width], total[:, width:] + sums], axis=1)
+        0, full, lambda j, c: tile(pl.multiple_of(j * width, width), c, False), carried
+    )
+    out, total = tile(start, carried, True)
     out = out * (1.0 / total)
     out = jnp.concatenate(by_heads(out), axis=0).T.astype(BF16)
     here = block // 2 == info[2]
@@ -966,7 +962,7 @@
         ),
         out_shape=[shape_of((cols, tok), BF16), shape_of((cols, tok), BF16)],
         compiler_params=settings(2, 60),
-        cost_estimate=cost(True),
+        cost_estimate=cost(True, 26),
         name="attn_bwd",
     )(info, mine, got, out_keep, out_send, grad_keep, grad_send, lse)
 
@@ -1078,7 +1074,7 @@
         + [shape_of((tok, feats), BF16)] * 4
         + [shape_of((1, width), F32)],
         compiler_params=settings(1, 60),
-        cost_estimate=cost(True),
+        cost_estimate=cost(True, 9),
         name="norm_two_back",
     )(info, *pieces, grad, resid, grad_result, gain)
 
@@ -1174,8 +1170,8 @@
         rest = rest[count:]
     act_ref, hid_ref = rest[:2]
     if last:
-        outa_ref, outb_ref, gres_ref, low_ref, lowt_ref, sq_ref = rest[2:8]
-        gate_up, down, total, sems = rest[8:]
+        out_ref, gres_ref, low_ref, lowt_ref, sq_ref = rest[2:7]
+        gate_up, down, total, sems = rest[7:]
     else:
         sum_ref, gate_up, down, total, sems = rest[2:]
     step, part = pl.program_id(0), pl.program_id(1)
@@ -1241,16 +1237,7 @@
             at = pl.multiple_of(jnp.bitwise_xor(info[1], mask) * quarter, quarter)
             cols = slice(p * quarter, (p + 1) * quarter)
             value = result[:, cols]
-            low = value.astype(BF16)
-
-            @pl.when(part < pl.num_programs(1) // 2)
-            def _():
-                outa_ref[:, pl.ds(at, quarter)] = low
-
-            @pl.when(part >= pl.num_programs(1) // 2)
-            def _():
-                outb_ref[:, pl.ds(at, quarter)] = low
-
+            out_ref[:, pl.ds(at, quarter)] = value.astype(BF16)
             error = valid * (value - teach_ref[0, :, pl.ds(at, quarter)].astype(F32))
             square = square + error * error
             grad = error * scale[0]
@@ -1285,22 +1272,15 @@
         in_specs.append(
             pl.BlockSpec((1, tile, width), lambda s, i, info: (info[0], leave(s, i), 0))
         )
-        half = tok // tile // 2
         out_specs += [
-            pl.BlockSpec(
-                (tile, width), lambda s, i, info: (jnp.minimum(leave(s, i), half - 1), 0)
-            ),
-            pl.BlockSpec(
-                (tile, width), lambda s, i, info: (jnp.maximum(leave(s, i) - half, 0), 0)
-            ),
+            tiles(width),
             tiles(width),
             tiles(width),
             pl.BlockSpec((width, tile), lambda s, i, info: (0, leave(s, i))),
             pl.BlockSpec((1, width // 4), lambda s, i, info: (0, 0)),
         ]
         out_shape += [
-            shape_of((tok // 2, width), BF16),
-            shape_of((tok // 2, width), BF16),
+            shape_of((tok, width), BF16),
             shape_of((tok, width), F32),
             shape_of((tok, width), BF16),
             shape_of((width, tok), BF16),
@@ -1422,7 +1402,7 @@
         ],
         input_output_aliases={} if first else {5 + len(pieces): 0},
         compiler_params=settings(1, 60),
-        cost_estimate=cost(True),
+        cost_estimate=cost(True, 18),
         name="ffn_bwd",
     )(low, acts, hiddens, xt, lowt, *pieces, *([] if first else [total]))
 
@@ -1832,14 +1812,14 @@
 
     weights2 = v["two"] + v["two_far"] + v["two_cores"]
     weights2 += [core_swap(part) for part in v["two_far"][1:]]
-    acts_c, hiddens_c, *results, grad_result, grad_low, grad_low_t, square = ffn_fwd(
+    acts_c, hiddens_c, result_low, grad_result, grad_low, grad_low_t, square = ffn_fwd(
         info, v["scale"], v["normed_two"], v["sum_b"], teacher, [(plan_mixed, weights2)], units, 256
     )
     v.update(
         weights2=weights2,
         acts_c=acts_c,
         hiddens_c=hiddens_c,
-        results=results,
+        result_low=result_low,
         grad_result=grad_result,
         grad_low=grad_low,
         grad_low_t=grad_low_t,
@@ -1859,18 +1839,16 @@
         )
 
     turned = [False, False, True]
-    one = [z_up(v["results"][0])]
+    output = lax.all_gather(v["result_low"], "tp", axis=0, tiled=False)
     total, keep2, send2 = ffn_back(plan_mixed, "weights2", "acts_c", "hiddens_c", 0, None)
-    v.update(one=one, total=total, keep2=keep2, send2=send2)
-    sync()
-
-    one = v["one"] + [z_up(v["results"][1])]
+    v.update(total=total, keep2=keep2, send2=send2)
+    sync()
+
     came2 = core_swap(v["send2"])
     total, keep1, send1 = ffn_back(plan_mixed, "weights1", "acts_a", "hiddens_a", 1, v["total"])
-    v.update(one=one, came2=came2, total=total, keep1=keep1, send1=send1)
-    sync()
-
-    out_three = [z_down(v["results"][0])]
+    v.update(came2=came2, total=total, keep1=keep1, send1=send1)
+    sync()
+
     came1 = core_swap(v["send1"])
     sum2 = sums(info, [v["keep2"], v["came2"]], core_jobs(0, 1))
     far_t2 = x_swap(sum2[3])
@@ -1878,7 +1856,6 @@
         plan_chunks, "weights3", "acts_b", "hiddens_b", 0, after(v["total"], sum2[0])
     )
     v.update(
-        out_three=out_three,
         came1=came1,
         sum2=sum2,
         far_t2=far_t2,
@@ -1888,7 +1865,6 @@
     )
     sync()
 
-    out_three = v["out_three"] + [z_down(v["results"][1])]
     came3 = core_swap(v["send3"])
     far_h2 = x_swap(v["sum2"][2])
     there2, *sum1 = sums(
@@ -1901,7 +1877,6 @@
         plan0, "weights0", "acts_a", "hiddens_a", 0, after(v["total"], sum1[0])
     )
     v.update(
-        out_three=out_three,
         came3=came3,
         far_h2=far_h2,
         there2=there2,
@@ -1950,31 +1925,25 @@
             info, v["mine"][j][0], got_ref, out[0], out[1], grad, v[f"grad_got{j}"], out[2], hd
         )
 
-    two = [z_up(v["one"][0])]
     far_h1 = x_swap(v["sum1"][2])
-    there1, *sum0 = sums(
-        info,
-        [v["sum1"][1], v["far_t1"], v["keep0"], v["came0"]],
-        [[(0, 0, None, False), (1, 0, None, False)]] + core_jobs(2, 3),
-    )
-    there1 = y_swap(there1)
+    [there1] = sums(
+        info, [v["sum1"][1], v["far_t1"]], [[(0, 0, None, False), (1, 0, None, False)]]
+    )
+    there1_got = y_swap(there1)
     far_t3 = x_swap(v["sum3"][3])
-    back0 = attn_back(0, after(v["grad_mine"][0], sum0[0]))
+    back0 = attn_back(0, after(v["grad_mine"][0], there1))
     v.update(
-        out_two=two,
         far_h1=far_h1,
-        there1=there1,
+        there1=there1_got,
         far_t3=far_t3,
-        sum0=sum0,
+        output=output,
         back0=back0,
         grad_got1=grad_got[1],
     )
     sync()
 
-    two = v["out_two"] + [z_up(v["one"][1])]
     heads0 = y_swap(v["back0"][1])
     far_h3 = x_swap(v["sum3"][2])
-    far_t0 = x_swap(v["sum0"][3])
     there3, two_down = sums(
         info,
         [v["sum3"][1], v["far_t3"], v["sum1"][0], v["far_h1"], v["there1"], v["down2"]],
@@ -1987,26 +1956,20 @@
     two_down_got = z_down(two_down)
     back1 = attn_back(1, after(v["grad_mine"][1], there3, two_down))
     v.update(
-        out_two=two, heads0=heads0, far_h3=far_h3, far_t0=far_t0, there3=there3_got, back1=back1
+        heads0=heads0, far_h3=far_h3, there3=there3_got, back1=back1
     )
     sync()
 
     heads1 = y_swap(v["back1"][1])
-    far_h0 = x_swap(v["sum0"][2])
-    part3, there0 = sums(
-        info,
-        [v["sum3"][0], v["far_h3"], v["there3"], v["sum0"][1], v["far_t0"]],
-        [plane, [(3, 0, None, False), (4, 0, None, False)]],
-    )
+    [part3] = sums(info, [v["sum3"][0], v["far_h3"], v["there3"]], [plane])
     up3 = z_up(part3)
     tables = [v[name] for name in ("cos_part", "sin_part", "gain_q", "gain_k")]
     head0 = head_back(
         info, v["back0"][0], v["heads0"], v["mine"][0][1], v["theirs"][0][1], *tables, heads
     )
-    v.update(heads1=heads1, two_down=two_down_got, head0=head0, there0=there0)
-    sync()
-
-    there0 = y_swap(v["there0"])
+    v.update(heads1=heads1, two_down=two_down_got, head0=head0)
+    sync()
+
     head1 = head_back(
         info, v["back1"][0], v["heads1"], v["mine"][1][1], v["theirs"][1][1], *tables, heads
     )
@@ -2020,17 +1983,8 @@
         tok // 4,
     )
     v.update(head1=head1, tokens_low=tokens_low, gain_one_sum=gain_one_sum, up3=up3)
-    v.update(there0=there0, far_h0=far_h0)
-    sync()
-
-    def place(out, parts, k, first):
-        row = lax.rem(z - k + 4, 4)
-        for j, part in enumerate(parts):
-            at = (first + j) * part.shape[0]
-            out = lax.dynamic_update_slice(out, part.astype(out.dtype)[None], (row, at, 0))
-        return out
-
-    v.update(out_one=v["one"])
+    sync()
+
     gathered = lax.all_gather(v["tokens_low"], "tp", axis=0, tiled=False)
     keep, send = weight_grad(
         v["normed_one_t"], [v["head0"][0], v["head1"][0]], v["grad_attn_t"], v["attended"]
@@ -2056,29 +2010,30 @@
     flat = lambda a: a.reshape(4 * rows, a.shape[-1])
     attn_sums = [flat(p) for p in core_sum(info, v["keep"], core_swap(v["send"]))]
     vector = v["vector"] + x_swap(v["vector"])
-    v.update(sums=attn_sums, vector=vector)
+    sum0 = sums(info, [v["keep0"], v["came0"]], core_jobs(0, 1))
+    v.update(sums=attn_sums, vector=vector, sum0=sum0)
     sync()
 
     far_t = x_swap(v["sums"][3])
-    part0 = summed([v["sum0"][0], v["far_h0"], v["there0"]], turned)
-    ffn_sum = summed([part0, v["two_down"], v["up3"]], None, F32)
+    far_t0 = x_swap(v["sum0"][3])
     vector = v["vector"] + y_swap(v["vector"])
-    v.update(far_t=far_t, ffn_sum=ffn_sum, vector=vector)
+    v.update(far_t=far_t, far_t0=far_t0, vector=vector)
     sync()
 
     far_h = x_swap(v["sums"][2])
     there = y_swap(summed([v["sums"][1], v["far_t"]]))
-    output = jnp.zeros((rows_dev, tok, width), BF16)
-    for k, parts in enumerate((v["results"], v["out_one"], v["out_two"], v["out_three"])):
-        output = place(output, parts, k, 0)
-    v.update(far_h=far_h, there=there, output=output)
+    far_h0 = x_swap(v["sum0"][2])
+    there0 = y_swap(summed([v["sum0"][1], v["far_t0"]]))
+    v.update(far_h=far_h, there=there, far_h0=far_h0, there0=there0)
     sync()
 
     parts = summed([v["sums"][0], v["far_h"], v["there"]])
     parts = [parts[k * rows : (k + 1) * rows] for k in range(4)]
     parts = [parts[0], z_down(parts[1]), z_far(parts[2]), z_up(parts[3])]
-    ffn_other = y_swap(v["ffn_sum"])
-    v.update(parts=parts)
+    part0 = summed([v["sum0"][0], v["far_h0"], v["there0"]], turned)
+    ffn_sum = summed([part0, v["two_down"], v["up3"]], None, F32)
+    ffn_other = y_swap(ffn_sum)
+    v.update(parts=parts, ffn_sum=ffn_sum)
     sync()
 
     attn_sum = summed(v["parts"], None, F32)
@@ -2115,7 +2070,6 @@
     sync()
 
     tokens_grad = gathered.astype(F32)
-    output = v["output"]
     sums_all = v["vector"][0]
 
     attn_grad = finish(v["attn_sum"], v["attn_other"])
@@ -2125,7 +2079,7 @@
         return lax.dynamic_slice_in_dim(sums_all, at + fsdp * (size // 4), size // 4, 0)
 
     return (
-        output,
+        v["output"],
         teacher_loss,
         tokens_grad,
         own_part(0, width),

time: 764 us -> 828 us (1.084)
  waiting for transfers between devices: 177 us -> 220 us
  starting transfers between devices: 83.6 us -> 99.1 us
  Pallas kernels: 385 us -> 395 us
    ppermute x19, waiting for transfers between devices: 36.8 us -> 78.1 us  [y_swap(): return lax.ppermute(v, 'ctx', Y_SWAP)]
    ppermute x10 -> x8, waiting for transfers between devices: 15.7 us -> 47.6 us  [z_down(): return lax.ppermute(v, 'tp', Z_DOWN)]
    all_gather x1, waiting for transfers between devices: 20.4 us -> 0.01 us  [per_device_rows(): gathered = lax.all_gather(v['tokens_low'], 'tp', axis=0, tiled=False)]
    ppermute x22, starting transfers between devices: 22.9 us -> 39.1 us  [x_swap(): return lax.ppermute(v, 'fsdp', X_SWAP)]
    dynamic_update_slice x8 -> x0, local copies, waits for them, and re-layouts: 10.8 us -> none  [place(): lax.dynamic_update_slice(out, part.astype(out.dtype)[None], (row, at, 0))]
    ppermute x3, waiting for transfers between devices: 31.3 us -> 21.5 us  [z_far(): return lax.ppermute(v, 'tp', Z_FAR)]
    ppermute x22, waiting for transfers between devices: 42.7 us -> 51.6 us  [x_swap(): return lax.ppermute(v, 'fsdp', X_SWAP)]
    unnamed x161 -> x180, local copies, waits for them, and re-layouts: 39.7 us -> 47.5 us
  transfers between devices with their start and end apart: 99 -> 94, of which waited for: 31 -> 28; matrix products, arithmetic and copies ran while one was open for 5% -> 3% of each run, Pallas kernels for 45% -> 43%
where the time goes in v13:
time: 828 us; the launch traced here: 817 us
  Pallas kernels  395 us (48%)
  waiting for transfers between devices  220 us (27%)
  starting transfers between devices  99.1 us (12%)
  local copies, waits for them, and re-layouts  61.4 us (7%)
  other arithmetic  22.3 us (3%)
  between operations  19.5 us (2%)
    pallas_call x4, Pallas kernels, ffn_bwd(): pl.pallas_call(functools.partial(ffn_bwd_kernel, steps, plan, first), gri...  103 us
    ppermute x19, waiting for transfers between devices, y_swap(): return lax.ppermute(v, 'ctx', Y_SWAP)  78.1 us
    pallas_call x3, Pallas kernels, ffn_fwd(): pl.pallas_call(functools.partial(ffn_fwd_kernel, tile, [plan for plan, _...  60.9 us
    ppermute x22, waiting for transfers between devices, x_swap(): return lax.ppermute(v, 'fsdp', X_SWAP)  51.6 us
    pallas_call x2, Pallas kernels, attn_bwd(): pl.pallas_call(functools.partial(attn_bwd_kernel, width, hd), grid_spec=p...  49.4 us
    ppermute x8, waiting for transfers between devices, z_down(): return lax.ppermute(v, 'tp', Z_DOWN)  47.6 us
    unnamed x180, local copies, waits for them, and re-layouts  47.5 us
    ppermute x22, starting transfers between devices, x_swap(): return lax.ppermute(v, 'fsdp', X_SWAP)  39.1 us
  transfers between devices with their start and end apart: 94, of which 28 were waited for; matrix products, arithmetic and copies ran while one was open for 3% of the time, Pallas kernels for 43%

profile of v13, /device:TPU:0, one launch (start us, length us, event | category | flops | bytes accessed | tf_op | source)
XLA Modules:
  0.0 816.8 jit_solution(14339510703162193027)
XLA Ops:
  86.7 13.0 %collective-permute-done.15.rest_4_.rest_0_ = bf16[256,1152]{1,0:T(8,128)(2,1)} collective-permute-done((bf16[256,1152]{1,0:T(8,128)(2,1)}, bf16[256,1152]{1,0:T(8,128)(2,1)}, u32[]{:S(2)}, u32[]{:S(2)}) %collective-permute-start.15) | collective-permute-done | bytes 589856 | tf_op jit(solution)/shard_map/ppermute | solution.py:1614
  102.2 17.0 %attn_fwd.2 = (bf16[1024,256]{1,0:T(8,128)(2,1)}, bf16[1024,256]{1,0:T(8,128)(2,1)}, f32[2,2,2048]{2,1,0:T(2,128)}) custom-call(s32[4]{0:T(128)} %copy-done.20, bf16[512,1024]{1,0:T(8,128)(2,1)} %copy-done.29, bf16[512,1024]{1,0:T(8,128)(2,1)} %copy-done.65), custom_call_target="tpu_custom_call" | custom-call | flops 4398046511104 | bytes 1073741824 | tf_op jit(solution)/shard_map/attn_fwd/pallas_call | solution.py:778
  127.6 17.0 %attn_fwd.3 = (bf16[1024,256]{1,0:T(8,128)(2,1)}, bf16[1024,256]{1,0:T(8,128)(2,1)}, f32[2,2,2048]{2,1,0:T(2,128)}) custom-call(s32[4]{0:T(128)} %copy-done.20, bf16[512,1024]{1,0:T(8,128)(2,1)} %copy-done.28, bf16[512,1024]{1,0:T(8,128)(2,1)} %collective-permute-done.17.got_ref), custom_call_target="tpu_custom_call" | custom-call | flops 4398046511104 | bytes 1073741824 | tf_op jit(solution)/shard_map/attn_fwd/pallas_call | solution.py:778
  149.4 11.9 %collective-permute-done.27.refs_8_ = bf16[1024,256]{1,0:T(8,128)(2,1)S(1)} collective-permute-done((bf16[1024,256]{1,0:T(8,128)(2,1)}, bf16[1024,256]{1,0:T(8,128)(2,1)S(1)}, u32[]{:S(2)}, u32[]{:S(2)}) %collective-permute-start.27) | collective-permute-done | bytes 524320 | tf_op jit(solution)/shard_map/ppermute | solution.py:1611
  186.0 27.2 %ffn_fwd.3 = (bf16[2,1024,2304]{2,1,0:T(8,128)(2,1)}, bf16[2,1024,1152]{2,1,0:T(8,128)(2,1)}, f32[1024,1024]{1,0:T(8,128)}) custom-call(s32[4]{0:T(128)} %copy-done.20, f32[1]{0:T(128)} %bitcast.4.scale, bf16[1024,1024]{1,0:T(8,128)(2,1)} %get-tuple-element.1790.x_ref, f32[1024,1024]{1,0:T(8,128)} %get-tuple-element.2349.in_ref.refs_5_, ...), custom_call_target="tpu_custom_call" | custom-call | flops 4398046511104 | bytes 1073741824 | tf_op jit(solution)/shard_map/ffn_fwd/pallas_call | solution.py:1292
  220.6 15.6 %ffn_fwd.4 = (bf16[1,1024,2304]{2,1,0:T(8,128)(2,1)}, bf16[1,1024,1152]{2,1,0:T(8,128)(2,1)}, f32[1024,1024]{1,0:T(8,128)}) custom-call(s32[4]{0:T(128)} %copy-done.20, f32[1]{0:T(128)} %bitcast.4.scale, bf16[1024,1024]{1,0:T(8,128)(2,1)} %get-tuple-element.1790.x_ref, f32[1024,1024]{1,0:T(8,128)} %get-tuple-element.1690.in_ref, ...), custom_call_target="tpu_custom_call" | custom-call | flops 4398046511104 | bytes 1073741824 | tf_op jit(solution)/shard_map/ffn_fwd/pallas_call | solution.py:1292
  240.3 18.1 %ffn_fwd.5 = (bf16[1,1024,2304]{2,1,0:T(8,128)(2,1)}, bf16[1,1024,1152]{2,1,0:T(8,128)(2,1)}, bf16[1024,1024]{1,0:T(8,128)(2,1)}, f32[1024,1024]{1,0:T(8,128)}, ...) custom-call(s32[4]{0:T(128)} %copy-done.20, f32[1]{0:T(128)} %bitcast.4.scale, ...), custom_call_target="tpu_custom_call" | custom-call | flops 4398046511104 | bytes 1073741824 | tf_op jit(solution)/shard_map/ffn_fwd/pallas_call | solution.py:1292
  258.4 25.2 %ffn_bwd.4 = (f32[1024,1024]{1,0:T(8,128)}, bf16[512,3456]{1,0:T(8,128)(2,1)}, bf16[512,3456]{1,0:T(8,128)(2,1)}) custom-call(bf16[1024,1024]{1,0:T(8,128)(2,1)} %get-tuple-element.2277.low_ref, bf16[1,1024,2304]{2,1,0:T(8,128)(2,1)} %get-tuple-element.1913.act_ref, bf16[1,1024,1152]{2,1,0:T(8,128)(2,1)} %get-tuple-element.1933.hid_ref, ...), custom_call_target="tpu_custom_call" | custom-call | flops 20700000256 | bytes 5053710 | tf_op jit(solution)/shard_map/ffn_bwd/pallas_call | solution.py:1374
  283.8 25.2 %ffn_bwd.5 = (f32[1024,1024]{1,0:T(8,128)}, bf16[512,3456]{1,0:T(8,128)(2,1)}, bf16[512,3456]{1,0:T(8,128)(2,1)}) custom-call(bf16[1024,1024]{1,0:T(8,128)(2,1)} %get-tuple-element.2277.low_ref, bf16[2,1024,2304]{2,1,0:T(8,128)(2,1)} %get-tuple-element.2261.act_ref, ...), custom_call_target="tpu_custom_call", output_to_operand_aliasing={{0}: (15, {})} | custom-call | flops 20700000256 | bytes 5053710 | tf_op jit(solution)/shard_map/ffn_bwd/pallas_call | solution.py:1374
  317.4 26.6 %ffn_bwd.6 = (f32[1024,1024]{1,0:T(8,128)}, bf16[512,3456]{1,0:T(8,128)(2,1)}, bf16[512,3456]{1,0:T(8,128)(2,1)}) custom-call(bf16[1024,1024]{1,0:T(8,128)(2,1)} %get-tuple-element.2277.low_ref, bf16[1,1024,2304]{2,1,0:T(8,128)(2,1)} %get-tuple-element.2189.act_ref, ...), custom_call_target="tpu_custom_call", output_to_operand_aliasing={{0}: (17, {})} | custom-call | flops 20700000256 | bytes 5053710 | tf_op jit(solution)/shard_map/ffn_bwd/pallas_call | solution.py:1374
  353.6 25.7 %ffn_bwd.7 = (f32[1024,1024]{1,0:T(8,128)}, bf16[512,3456]{1,0:T(8,128)(2,1)}, bf16[512,3456]{1,0:T(8,128)(2,1)}) custom-call(bf16[1024,1024]{1,0:T(8,128)(2,1)} %get-tuple-element.2277.low_ref, bf16[2,1024,2304]{2,1,0:T(8,128)(2,1)} %get-tuple-element.2261.act_ref, ...), custom_call_target="tpu_custom_call", output_to_operand_aliasing={{0}: (9, {})} | custom-call | flops 20700000256 | bytes 5053710 | tf_op jit(solution)/shard_map/ffn_bwd/pallas_call | solution.py:1374
  392.4 12.5 %norm_two_back.1 = (f32[1024,1024]{1,0:T(8,128)}, bf16[1024,1024]{1,0:T(8,128)(2,1)}, bf16[1024,256]{1,0:T(8,128)(2,1)}, bf16[1024,256]{1,0:T(8,128)(2,1)}, bf16...) custom-call(s32[4]{0:T(128)} %copy-done.20, ...), custom_call_target="tpu_custom_call" | custom-call | flops 10350000128 | bytes 2526855 | tf_op jit(solution)/shard_map/norm_two_back/pallas_call | solution.py:1062
  407.0 13.0 %collective-permute-done.64.gs_ref = bf16[1024,256]{1,0:T(8,128)(2,1)S(1)} collective-permute-done((bf16[1024,256]{1,0:T(8,128)(2,1)}, bf16[1024,256]{1,0:T(8,128)(2,1)S(1)}, u32[]{:S(2)}, u32[]{:S(2)}) %collective-permute-start.64) | collective-permute-done | bytes 524320 | tf_op jit(solution)/shard_map/ppermute | solution.py:1611
  420.0 27.4 %collective-permute-done.62.refs_5_ = bf16[128,3456]{1,0:T(8,128)(2,1)} collective-permute-done((bf16[128,3456]{1,0:T(8,128)(2,1)}, bf16[128,3456]{1,0:T(8,128)(2,1)}, u32[]{:S(2)}, u32[]{:S(2)}) %collective-permute-start.62) | collective-permute-done | bytes 884768 | tf_op jit(solution)/shard_map/ppermute | solution.py:1620
  454.7 24.7 %attn_bwd.2 = (bf16[512,1024]{1,0:T(8,128)(2,1)}, bf16[512,1024]{1,0:T(8,128)(2,1)}) custom-call(s32[4]{0:T(128)} %copy-done.20, bf16[512,1024]{1,0:T(8,128)(2,1)} %copy-done.29, bf16[512,1024]{1,0:T(8,128)(2,1)} %copy-done.65, bf16[1024,256]{1,0:T(8,128)(2,1)} %get-tuple-element.2389.refs_5_.ok_ref, bf16[1024,256]{1,0:T(8,128)(2,1)} %get-tuple-element.2390.os_ref, ...), custom_call_target="tpu_custom_call" | custom-call | flops 29899999232 | bytes 7299804 | tf_op jit(solution)/shard_map/attn_bwd/pallas_call | solution.py:939
  479.5 13.4 %collective-permute-done.66.refs_1_ = bf16[128,3456]{1,0:T(8,128)(2,1)} collective-permute-done((bf16[128,3456]{1,0:T(8,128)(2,1)}, bf16[128,3456]{1,0:T(8,128)(2,1)}, u32[]{:S(2)}, u32[]{:S(2)}) %collective-permute-start.66) | collective-permute-done | bytes 884768 | tf_op jit(solution)/shard_map/ppermute | solution.py:1605
  500.6 24.7 %attn_bwd.3 = (bf16[512,1024]{1,0:T(8,128)(2,1)}, bf16[512,1024]{1,0:T(8,128)(2,1)}) custom-call(s32[4]{0:T(128)} %copy-done.20, bf16[512,1024]{1,0:T(8,128)(2,1)} %copy-done.28, bf16[512,1024]{1,0:T(8,128)(2,1)} %collective-permute-done.17.got_ref, bf16[1024,256]{1,0:T(8,128)(2,1)} %get-tuple-element.2442.refs_6_.ok_ref, ...), custom_call_target="tpu_custom_call" | custom-call | flops 29899999232 | bytes 7299804 | tf_op jit(solution)/shard_map/attn_bwd/pallas_call | solution.py:939
  525.3 14.8 %collective-permute-done.70.dt_ref = bf16[512,1024]{1,0:T(8,128)(2,1)S(1)} collective-permute-done((bf16[512,1024]{1,0:T(8,128)(2,1)}, bf16[512,1024]{1,0:T(8,128)(2,1)S(1)}, u32[]{:S(2)}, u32[]{:S(2)}) %collective-permute-start.70) | collective-permute-done | bytes 1048608 | tf_op jit(solution)/shard_map/ppermute | solution.py:1611
  574.5 12.3 %norm_one_back.1 = (bf16[1024,1024]{1,0:T(8,128)(2,1)}, f32[1,1024]{1,0:T(1,128)}) custom-call(s32[4]{0:T(128)} %copy-done.20, bf16[512,512]{1,0:T(8,128)(2,1)} %copy-done.2, bf16[768,512]{1,0:T(8,128)(2,1)} %copy-done.1, bf16[768,512]{1,0:T(8,128)(2,1)} %collective-permute-done.10.refs_2_, bf16[512,512]{1,0:T(8,128)(2,1)} %copy-done.4, ...), custom_call_target="tpu_custom_call" | custom-call | flops 4398046511104 | bytes 1073741824 | tf_op jit(solution)/shard_map/norm_one_back/pallas_call | solution.py:1116
  589.9 15.1 %weight_grad.1 = (bf16[4,512,768]{2,1,0:T(8,128)(2,1)}, bf16[4,512,768]{2,1,0:T(8,128)(2,1)}) custom-call(bf16[1024,1024]{1,0:T(8,128)(2,1)} %copy-done, bf16[2,1024,512]{2,1,0:T(8,128)(2,1)} %get-tuple-element.2554.refs_6_.back0_ref, bf16[2,1024,512]{2,1,0:T(8,128)(2,1)} %get-tuple-element.2556.refs_7_.back1_ref, ...), custom_call_target="tpu_custom_call" | custom-call | flops 4398046511104 | bytes 1073741824 | tf_op jit(solution)/shard_map/weight_grad/pallas_call | solution.py:1557
  606.4 17.6 %collective-permute-start.77 = (f32[1,2304]{1,0:T(1,128)S(1)}, f32[1,2304]{1,0:T(1,128)S(1)}, u32[]{:S(2)}, u32[]{:S(2)}) collective-permute-start(f32[1,2304]{1,0:T(1,128)S(1)} %add.64), channel_id=1, source_target_pairs={{0,16},{16,0},{8,24},{24,8},{1,17},{17,1},{9,25},{25,9},{2,18},{18... | collective-permute-start | bytes 27656 | tf_op jit(solution)/shard_map/ppermute | solution.py:1605
  646.7 32.5 %collective-permute-done.78.refs_1_ = bf16[512,768]{1,0:T(8,128)(2,1)S(1)} collective-permute-done((bf16[512,768]{1,0:T(8,128)(2,1)S(1)}, bf16[512,768]{1,0:T(8,128)(2,1)S(1)}, u32[]{:S(2)}, u32[]{:S(2)}) %collective-permute-start.78) | collective-permute-done | bytes 786464 | tf_op jit(solution)/shard_map/ppermute | solution.py:1605
  690.3 30.1 %collective-permute-done.83.refs_2_ = bf16[512,768]{1,0:T(8,128)(2,1)S(1)} collective-permute-done((bf16[512,768]{1,0:T(8,128)(2,1)}, bf16[512,768]{1,0:T(8,128)(2,1)S(1)}, u32[]{:S(2)}, u32[]{:S(2)}) %collective-permute-start.83) | collective-permute-done | bytes 786464 | tf_op jit(solution)/shard_map/ppermute | solution.py:1611
  750.8 19.8 %collective-permute-done.86.refs_2_ = bf16[128,768]{1,0:T(8,128)(2,1)S(1)} collective-permute-done((bf16[128,768]{1,0:T(8,128)(2,1)S(1)}, bf16[128,768]{1,0:T(8,128)(2,1)S(1)}, u32[]{:S(2)}, u32[]{:S(2)}) %collective-permute-start.86) | collective-permute-done | bytes 196640 | tf_op jit(solution)/shard_map/ppermute | solution.py:1617
  (446 shorter events, 316.7 us)
Async XLA Ops:
  7.2 472.3 %all-gather.5.cloned.1.call-start = ((), (), s32[]{:S(2)}) async-start(), calls=%async_computation | async-start | bytes 10485760 | tf_op jit(solution)/shard_map/all_gather | solution.py:1842
  56.5 43.3 %collective-permute-start.11 = (bf16[256,3456]{1,0:T(8,128)(2,1)}, bf16[256,3456]{1,0:T(8,128)(2,1)}, u32[]{:S(2)}, u32[]{:S(2)}) collective-permute-start(bf16[256,3456]{1,0:T(8,128)(2,1)} %get-tuple-element.2282.rest_0_), channel_id=1, source_target_pairs={{0,16},{16,0},{8,24},{24,8},{1,17},{17,1},{9,25},{25,9},{2,18},{18... | collective-permute-start | bytes 5308424 | tf_op jit(solution)/shard_map/ppermute | solution.py:1605
  57.4 42.4 %collective-permute-start.16 = (bf16[256,2304]{1,0:T(8,128)(2,1)}, bf16[256,2304]{1,0:T(8,128)(2,1)}, u32[]{:S(2)}, u32[]{:S(2)}) collective-permute-start(bf16[256,2304]{1,0:T(8,128)(2,1)} %get-tuple-element.1376), channel_id=1, source_target_pairs={{0,1},{1,2},{2,3},{3,0},{4,5},{5,6},{6,7},{7,4},{8,9},{9,10},{10,1... | collective-permute-start | bytes 3538952 | tf_op jit(solution)/shard_map/ppermute | solution.py:1614
  75.5 43.7 %collective-permute-start.17 = (bf16[512,1024]{1,0:T(8,128)(2,1)}, bf16[512,1024]{1,0:T(8,128)(2,1)}, u32[]{:S(2)}, u32[]{:S(2)}) collective-permute-start(bf16[512,1024]{1,0:T(8,128)(2,1)} %get-tuple-element.1368), channel_id=1, source_target_pairs={{0,4},{4,0},{1,5},{5,1},{2,6},{6,2},{3,7},{7,3},{8,12},{12,8},{9,1... | collective-permute-start | bytes 3145736 | tf_op jit(solution)/shard_map/ppermute | solution.py:1611
  181.2 32.1 %collective-permute-start.41 = (bf16[256,2304]{1,0:T(8,128)(2,1)}, bf16[256,2304]{1,0:T(8,128)(2,1)}, u32[]{:S(2)}, u32[]{:S(2)}) collective-permute-start(bf16[256,2304]{1,0:T(8,128)(2,1)} %collective-permute-done.16.rest_5_.rest_1_), channel_id=1, source_target_pairs={{0,1},{1,2},{2,3},{3,0},{4,5},{5,6},{6,7},{7,4},{8,9},{9,10},{10,1... | collective-permute-start | bytes 3538952 | tf_op jit(solution)/shard_map/ppermute | solution.py:1614
  181.2 32.1 %collective-permute-start.38 = (bf16[256,1152]{1,0:T(8,128)(2,1)}, bf16[256,1152]{1,0:T(8,128)(2,1)}, u32[]{:S(2)}, u32[]{:S(2)}) collective-permute-start(bf16[256,1152]{1,0:T(8,128)(2,1)} %collective-permute-done.21.rest_0_), channel_id=1, source_target_pairs={{0,8},{8,0},{16,24},{24,16},{1,9},{9,1},{17,25},{25,17},{2,10},{10... | collective-permute-start | bytes 1769480 | tf_op jit(solution)/shard_map/ppermute | solution.py:1608
  309.0 35.1 %collective-permute-start.56 = (bf16[512,3456]{1,0:T(8,128)(2,1)}, bf16[512,3456]{1,0:T(8,128)(2,1)}, u32[]{:S(2)}, u32[]{:S(2)}) collective-permute-start(bf16[512,3456]{1,0:T(8,128)(2,1)} %get-tuple-element.2191), channel_id=1, source_target_pairs={{0,8},{8,0},{16,24},{24,16},{1,9},{9,1},{17,25},{25,17},{2,10},{10... | collective-permute-start | bytes 10616840 | tf_op jit(solution)/shard_map/ppermute | solution.py:1608
  309.5 479.7 %all-gather.7.cloned.1.call-start = ((), (), s32[]{:S(2)}) async-start(), calls=%async_computation.1 | async-start | bytes 10485760 | tf_op jit(solution)/shard_map/all_gather | solution.py:1988
  345.0 34.3 %collective-permute-start.58 = (bf16[512,3456]{1,0:T(8,128)(2,1)}, bf16[512,3456]{1,0:T(8,128)(2,1)S(1)}, u32[]{:S(2)}, u32[]{:S(2)}) collective-permute-start(bf16[512,3456]{1,0:T(8,128)(2,1)} %get-tuple-element.2264), channel_id=1, source_target_pairs={{0,8},{8,0},{16,24},{24,16},{1,9},{9,1},{17,25},{25,17},{2,10},{10... | collective-permute-start | bytes 10616840 | tf_op jit(solution)/shard_map/ppermute | solution.py:1608
  381.1 66.3 %collective-permute-start.61 = (bf16[512,3456]{1,0:T(8,128)(2,1)}, bf16[512,3456]{1,0:T(8,128)(2,1)S(1)}, u32[]{:S(2)}, u32[]{:S(2)}) collective-permute-start(bf16[512,3456]{1,0:T(8,128)(2,1)} %get-tuple-element.2326), channel_id=1, source_target_pairs={{0,8},{8,0},{16,24},{24,16},{1,9},{9,1},{17,25},{25,17},{2,10},{10... | collective-permute-start | bytes 10616840 | tf_op jit(solution)/shard_map/ppermute | solution.py:1608
  387.8 59.6 %collective-permute-start.62 = (bf16[128,3456]{1,0:T(8,128)(2,1)}, bf16[128,3456]{1,0:T(8,128)(2,1)}, u32[]{:S(2)}, u32[]{:S(2)}) collective-permute-start(bf16[128,3456]{1,0:T(8,128)(2,1)} %get-tuple-element.2333), channel_id=1, source_target_pairs={{0,3},{1,0},{2,1},{3,2},{4,7},{5,4},{6,5},{7,6},{8,11},{9,8},{10,9... | collective-permute-start | bytes 2654216 | tf_op jit(solution)/shard_map/ppermute | solution.py:1620
  391.5 55.9 %collective-permute-start.63 = (bf16[128,3456]{1,0:T(8,128)(2,1)}, bf16[128,3456]{1,0:T(8,128)(2,1)}, u32[]{:S(2)}, u32[]{:S(2)}) collective-permute-start(bf16[128,3456]{1,0:T(8,128)(2,1)} %get-tuple-element.2334), channel_id=1, source_target_pairs={{0,16},{16,0},{8,24},{24,8},{1,17},{17,1},{9,25},{25,9},{2,18},{18... | collective-permute-start | bytes 2654216 | tf_op jit(solution)/shard_map/ppermute | solution.py:1605
  406.1 73.3 %collective-permute-start.67 = (bf16[1024,256]{1,0:T(8,128)(2,1)}, bf16[1024,256]{1,0:T(8,128)(2,1)S(1)}, u32[]{:S(2)}, u32[]{:S(2)}) collective-permute-start(bf16[1024,256]{1,0:T(8,128)(2,1)} %get-tuple-element.2410), channel_id=1, source_target_pairs={{0,4},{4,0},{1,5},{5,1},{2,6},{6,2},{3,7},{7,3},{8,12},{12,8},{9,1... | collective-permute-start | bytes 1572872 | tf_op jit(solution)/shard_map/ppermute | solution.py:1611
  453.6 39.4 %collective-permute-start.66 = (bf16[128,3456]{1,0:T(8,128)(2,1)}, bf16[128,3456]{1,0:T(8,128)(2,1)}, u32[]{:S(2)}, u32[]{:S(2)}) collective-permute-start(bf16[128,3456]{1,0:T(8,128)(2,1)} %get-tuple-element.2403), channel_id=1, source_target_pairs={{0,16},{16,0},{8,24},{24,8},{1,17},{17,1},{9,25},{25,9},{2,18},{18... | collective-permute-start | bytes 2654216 | tf_op jit(solution)/shard_map/ppermute | solution.py:1605
  498.0 42.2 %collective-permute-start.70 = (bf16[512,1024]{1,0:T(8,128)(2,1)}, bf16[512,1024]{1,0:T(8,128)(2,1)S(1)}, u32[]{:S(2)}, u32[]{:S(2)}) collective-permute-start(bf16[512,1024]{1,0:T(8,128)(2,1)} %get-tuple-element.2439), channel_id=1, source_target_pairs={{0,4},{4,0},{1,5},{5,1},{2,6},{6,2},{3,7},{7,3},{8,12},{12,8},{9,1... | collective-permute-start | bytes 3145736 | tf_op jit(solution)/shard_map/ppermute | solution.py:1611
  544.2 42.6 %collective-permute-start.74 = (bf16[128,3456]{1,0:T(8,128)(2,1)}, bf16[128,3456]{1,0:T(8,128)(2,1)}, u32[]{:S(2)}, u32[]{:S(2)}) collective-permute-start(bf16[128,3456]{1,0:T(8,128)(2,1)} %sums.12), channel_id=1, source_target_pairs={{0,1},{1,2},{2,3},{3,0},{4,5},{5,6},{6,7},{7,4},{8,9},{9,10},{10,1... | collective-permute-start | bytes 2654216 | tf_op jit(solution)/shard_map/ppermute | solution.py:1614
  641.0 38.2 %collective-permute-start.79 = (bf16[128,3456]{1,0:T(8,128)(2,1)S(1)}, bf16[128,3456]{1,0:T(8,128)(2,1)S(1)}, u32[]{:S(2)}, u32[]{:S(2)}) collective-permute-start(bf16[128,3456]{1,0:T(8,128)(2,1)S(1)} %copy-done.66), channel_id=1, source_target_pairs={{0,16},{16,0},{8,24},{24,8},{1,17},{17,1},{9,25},{25,9},{2,18},{18... | collective-permute-start | bytes 2654216 | tf_op jit(solution)/shard_map/ppermute | solution.py:1605
  641.0 38.2 %collective-permute-start.78 = (bf16[512,768]{1,0:T(8,128)(2,1)S(1)}, bf16[512,768]{1,0:T(8,128)(2,1)S(1)}, u32[]{:S(2)}, u32[]{:S(2)}) collective-permute-start(bf16[512,768]{1,0:T(8,128)(2,1)S(1)} %bitcast.47), channel_id=1, source_target_pairs={{0,16},{16,0},{8,24},{24,8},{1,17},{17,1},{9,25},{25,9},{2,18},{18... | collective-permute-start | bytes 2359304 | tf_op jit(solution)/shard_map/ppermute | solution.py:1605
  682.7 38.8 %collective-permute-start.84 = (bf16[128,3456]{1,0:T(8,128)(2,1)}, bf16[128,3456]{1,0:T(8,128)(2,1)S(1)}, u32[]{:S(2)}, u32[]{:S(2)}) collective-permute-start(bf16[128,3456]{1,0:T(8,128)(2,1)} %summed.7), channel_id=1, source_target_pairs={{0,4},{4,0},{1,5},{5,1},{2,6},{6,2},{3,7},{7,3},{8,12},{12,8},{9,1... | collective-permute-start | bytes 2654216 | tf_op jit(solution)/shard_map/ppermute | solution.py:1611
  684.1 38.3 %collective-permute-start.82 = (bf16[128,3456]{1,0:T(8,128)(2,1)}, bf16[128,3456]{1,0:T(8,128)(2,1)S(1)}, u32[]{:S(2)}, u32[]{:S(2)}) collective-permute-start(bf16[128,3456]{1,0:T(8,128)(2,1)} %get-tuple-element.2599), channel_id=1, source_target_pairs={{0,16},{16,0},{8,24},{24,8},{1,17},{17,1},{9,25},{25,9},{2,18},{18... | collective-permute-start | bytes 2654216 | tf_op jit(solution)/shard_map/ppermute | solution.py:1605
  687.9 32.4 %collective-permute-start.83 = (bf16[512,768]{1,0:T(8,128)(2,1)}, bf16[512,768]{1,0:T(8,128)(2,1)S(1)}, u32[]{:S(2)}, u32[]{:S(2)}) collective-permute-start(bf16[512,768]{1,0:T(8,128)(2,1)} %summed.6), channel_id=1, source_target_pairs={{0,4},{4,0},{1,5},{5,1},{2,6},{6,2},{3,7},{7,3},{8,12},{12,8},{9,1... | collective-permute-start | bytes 2359304 | tf_op jit(solution)/shard_map/ppermute | solution.py:1611
  688.5 32.9 %collective-permute-start.81 = (bf16[512,768]{1,0:T(8,128)(2,1)S(1)}, bf16[512,768]{1,0:T(8,128)(2,1)S(1)}, u32[]{:S(2)}, u32[]{:S(2)}) collective-permute-start(bf16[512,768]{1,0:T(8,128)(2,1)S(1)} %bitcast.46), channel_id=1, source_target_pairs={{0,16},{16,0},{8,24},{24,8},{1,17},{17,1},{9,25},{25,9},{2,18},{18... | collective-permute-start | bytes 2359304 | tf_op jit(solution)/shard_map/ppermute | solution.py:1605
  730.3 44.0 %collective-permute-start.88 = (f32[128,3456]{1,0:T(8,128)}, f32[128,3456]{1,0:T(8,128)S(1)}, u32[]{:S(2)}, u32[]{:S(2)}) collective-permute-start(f32[128,3456]{1,0:T(8,128)} %summed.9), channel_id=1, source_target_pairs={{0,4},{4,0},{1,5},{5,1},{2,6},{6,2},{3,7},{7,3},{8,12},{12,8},{9,1... | collective-permute-start | bytes 5308424 | tf_op jit(solution)/shard_map/ppermute | solution.py:1611
  736.6 34.0 %collective-permute-start.86 = (bf16[128,768]{1,0:T(8,128)(2,1)S(1)}, bf16[128,768]{1,0:T(8,128)(2,1)S(1)}, u32[]{:S(2)}, u32[]{:S(2)}) collective-permute-start(bf16[128,768]{1,0:T(8,128)(2,1)S(1)} %get-tuple-element.2691), channel_id=1, source_target_pairs={{0,2},{2,0},{1,3},{3,1},{4,6},{6,4},{5,7},{7,5},{8,10},{10,8},{9,1... | collective-permute-start | bytes 589832 | tf_op jit(solution)/shard_map/ppermute | solution.py:1617
  (152 other events, 1970.6 us)
Sparse Core Ops, SparseCore 0:
  309.6 168.0 all-gather.4
  590.0 180.6 all-gather.6

commit v14 on v12

--- a/solution.py
+++ b/solution.py
@@ -723,33 +723,27 @@
     start = pl.multiple_of(block * width, width)
     both = rows[pl.ds(query_at, 2 * hd), pl.ds(start, width)]
     query = query_with_one(by_halves(both[:hd], both[hd:]))
-    half = width // 2
-
-    def terms(at, keys, query, mask):
-        scores = dot(key_rows[pl.ds(at, keys), :], query, 1, 0)
-        if mask:
-            part = causal(scores[:, :width])
-            wide = scores.shape[1] > width
-            scores = jnp.concatenate([part, scores[:, width:]], axis=1) if wide else part
+
+    def tile(at, carried, diagonal):
+        out, total = carried
+        scores = dot(key_rows[pl.ds(at, width), :], query, 1, 0)
+        if diagonal:
+            key_pos = lax.broadcasted_iota(jnp.int32, (width, width), 0)
+            query_pos = lax.broadcasted_iota(jnp.int32, (width, width), 1)
+            allowed = key_pos <= query_pos
+            allowed = by_halves(allowed, allowed)
+            scores = jnp.where(allowed, scores, NEGATIVE)
         probs = jnp.exp2(scores * scale)
-        total = jnp.sum(probs, axis=0, keepdims=True)
-        return dot(rows[pl.ds(value_at, hd), pl.ds(at, keys)], probs.astype(BF16), 1, 0), total
-
-    def tile(at, carried):
-        more, sums = terms(at, width, query, False)
-        return carried[0] + more, carried[1] + sums
+        total = total + jnp.sum(probs, axis=0, keepdims=True)
+        out = out + dot(rows[pl.ds(value_at, hd), pl.ds(at, width)], probs.astype(BF16), 1, 0)
+        return out, total
 
     carried = (jnp.zeros((hd, 2 * width), F32), jnp.zeros((1, 2 * width), F32))
     full = jnp.minimum(block, lax.div(length + width - 1, width))
     carried = lax.fori_loop(
-        0, full, lambda j, c: tile(pl.multiple_of(j * width, width), c), carried
-    )
-    more, sums = terms(start, half, query, True)
-    out, total = carried[0] + more, carried[1] + sums
-    later = pl.multiple_of(start + half, half)
-    more, sums = terms(later, half, query[:, width:], True)
-    out = jnp.concatenate([out[:, :width], out[:, width:] + more], axis=1)
-    total = jnp.concatenate([total[:, :width], total[:, width:] + sums], axis=1)
+        0, full, lambda j, c: tile(pl.multiple_of(j * width, width), c, False), carried
+    )
+    out, total = tile(start, carried, True)
     out = out * (1.0 / total)
     out = jnp.concatenate(by_heads(out), axis=0).T.astype(BF16)
     here = block // 2 == info[2]
@@ -1110,23 +1104,26 @@
     gg_ref[...] += jnp.sum(grad * unit, axis=0, keepdims=True)
 
 
-def norm_one_back(info, pairs, weights, x, grad_resid, gain, tile):
+def norm_one_back(info, pairs, weights, x, grad_resid, gain, tile, part):
     plan, pieces = weights
     tok, width = x.shape
     cols = pieces[0].shape[1]
-    rows_of = lambda n: pl.BlockSpec((tile, n), lambda i, info: (i, 0))
-    pair = pl.BlockSpec((2, tile, cols), lambda i, info: (0, i, 0))
+    steps = tok // tile // 2
+    first = part * steps
+    rows_of = lambda n: pl.BlockSpec((tile, n), lambda i, info: (first + i, 0))
+    out_rows = pl.BlockSpec((tile, width), lambda i, info: (i, 0))
+    pair = pl.BlockSpec((2, tile, cols), lambda i, info: (0, first + i, 0))
     row = pl.BlockSpec((1, width), lambda i, info: (0, 0))
     return pl.pallas_call(
         functools.partial(norm_one_back_kernel, plan, len(pieces)),
         grid_spec=pltpu.PrefetchScalarGridSpec(
             num_scalar_prefetch=1,
-            grid=(tok // tile,),
+            grid=(steps,),
             in_specs=[ANY] * len(pieces) + [pair, pair, rows_of(width), rows_of(width), row],
-            out_specs=[rows_of(width), row],
+            out_specs=[out_rows, row],
             scratch_shapes=[pltpu.VMEM((4, width, cols), BF16), pltpu.SemaphoreType.DMA],
         ),
-        out_shape=[shape_of((tok, width), BF16), shape_of((1, width), F32)],
+        out_shape=[shape_of((tok // 2, width), BF16), shape_of((1, width), F32)],
         compiler_params=settings(1, 60),
         cost_estimate=cost(True),
         name="norm_one_back",
@@ -2003,24 +2000,31 @@
     head0 = head_back(
         info, v["back0"][0], v["heads0"], v["mine"][0][1], v["theirs"][0][1], *tables, heads
     )
-    v.update(heads1=heads1, two_down=two_down_got, head0=head0, there0=there0)
+    v.update(heads1=heads1, head0=head0, there0=there0)
     sync()
 
     there0 = y_swap(v["there0"])
     head1 = head_back(
         info, v["back1"][0], v["heads1"], v["mine"][1][1], v["theirs"][1][1], *tables, heads
     )
-    tokens_low, gain_one_sum = norm_one_back(
-        info,
-        [v["head0"][0], head1[0]],
-        (plan_proj, v["weights_proj"]),
-        v["x_in"],
-        v["grad_resid"],
-        v["gain_one"],
-        tok // 4,
-    )
+    def last_norm(part, *then):
+        return norm_one_back(
+            info,
+            [v["head0"][0], after(head1[0], *then)],
+            (plan_proj, v["weights_proj"]),
+            v["x_in"],
+            v["grad_resid"],
+            v["gain_one"],
+            tok // 4,
+            part,
+        )
+
+    low_first, gain_first = last_norm(0)
+    low_second, gain_second = last_norm(1, low_first)
+    gathered = [lax.all_gather(low_first, "tp", axis=0, tiled=False)]
+    tokens_low, gain_one_sum = low_second, gain_first + gain_second
     v.update(head1=head1, tokens_low=tokens_low, gain_one_sum=gain_one_sum, up3=up3)
-    v.update(there0=there0, far_h0=far_h0)
+    v.update(there0=there0, far_h0=far_h0, two_down=two_down_got)
     sync()
 
     def place(out, parts, k, first):
@@ -2031,7 +2035,7 @@
         return out
 
     v.update(out_one=v["one"])
-    gathered = lax.all_gather(v["tokens_low"], "tp", axis=0, tiled=False)
+    gathered.append(lax.all_gather(v["tokens_low"], "tp", axis=0, tiled=False))
     keep, send = weight_grad(
         v["normed_one_t"], [v["head0"][0], v["head1"][0]], v["grad_attn_t"], v["attended"]
     )
@@ -2110,11 +2114,13 @@
     grad_gate = columns(lambda j: 2 * j * third)
     grad_up = columns(lambda j: (2 * j + 1) * third)
     grad_down = columns(lambda j: 2 * units + j * third).T
-    v.update(vector=vector, attn_other=attn_other)
+    grad = jnp.zeros((rows_dev, tok, width), F32)
+    grad = lax.dynamic_update_slice(grad, gathered[0].astype(F32), (0, 0, 0))
+    v.update(vector=vector, attn_other=attn_other, grad=grad)
     v.update(grad_gate=grad_gate, grad_up=grad_up, grad_down=grad_down)
     sync()
 
-    tokens_grad = gathered.astype(F32)
+    tokens_grad = lax.dynamic_update_slice(v["grad"], gathered[1].astype(F32), (0, tok // 2, 0))
     output = v["output"]
     sums_all = v["vector"][0]
 

time: 764 us -> 760 us (level)
  Pallas kernels: 385 us -> 370 us
    dynamic_update_slice x0 -> x2, other arithmetic: none -> 17.2 us  [the longest x1 10.6 us: per_device_rows(): grad = lax.dynamic_update_slice(grad, gathered[0].astype(F32), (0, 0, 0))]
    pallas_call x2, Pallas kernels: 49.4 us -> 34.4 us  [attn_bwd(): pl.pallas_call(functools.partial(attn_bwd_kernel, width, hd), grid_spec=p...]
    ppermute x19, waiting for transfers between devices: 36.8 us -> 50.9 us  [y_swap(): return lax.ppermute(v, 'ctx', Y_SWAP)]
    all_gather x1 -> x2, waiting for transfers between devices: 20.4 us -> 6.37 us  [the longest x1 6.35 us: per_device_rows(): gathered.append(lax.all_gather(v['tokens_low'], 'tp', axis=0, tiled=False))]
    ppermute x22, waiting for transfers between devices: 42.7 us -> 54.6 us  [x_swap(): return lax.ppermute(v, 'fsdp', X_SWAP)]
    convert_element_type x1 -> x0, other arithmetic: 11.7 us -> none  [per_device_rows(): tokens_grad = gathered.astype(F32)]
    pallas_call x1 -> x2, Pallas kernels: 12.3 us -> 17.7 us  [norm_one_back(): pl.pallas_call(functools.partial(norm_one_back_kernel, plan, len(pieces))...]
    unnamed x161 -> x159, local copies, waits for them, and re-layouts: 39.7 us -> 40.1 us
  transfers between devices with their start and end apart: 99 -> 100, of which waited for: 31 -> 34; matrix products, arithmetic and copies ran while one was open for 5% -> 7% of each run, Pallas kernels for 45% -> 44%
where the time goes in v14:
time: 760 us; the launch traced here: 750 us
  Pallas kernels  370 us (49%)
  waiting for transfers between devices  178 us (23%)
  starting transfers between devices  86.5 us (11%)
  local copies, waits for them, and re-layouts  66.1 us (9%)
  other arithmetic  28.5 us (4%)
  between operations  19.6 us (3%)
    pallas_call x4, Pallas kernels, ffn_bwd(): pl.pallas_call(functools.partial(ffn_bwd_kernel, steps, plan, first), gri...  101 us
    pallas_call x3, Pallas kernels, ffn_fwd(): pl.pallas_call(functools.partial(ffn_fwd_kernel, tile, [plan for plan, _...  62.9 us
    ppermute x22, waiting for transfers between devices, x_swap(): return lax.ppermute(v, 'fsdp', X_SWAP)  54.6 us
    ppermute x19, waiting for transfers between devices, y_swap(): return lax.ppermute(v, 'ctx', Y_SWAP)  50.9 us
    unnamed x159, local copies, waits for them, and re-layouts  40.1 us
    pallas_call x2, Pallas kernels, attn_bwd(): pl.pallas_call(functools.partial(attn_bwd_kernel, width, hd), grid_spec=p...  34.4 us
    pallas_call x6, Pallas kernels, sums(): pl.pallas_call(functools.partial(sums_kernel, jobs, len(arrays)), grid_sp...  33.3 us
    pallas_call x2, Pallas kernels, attn_fwd(): pl.pallas_call(functools.partial(attn_fwd_kernel, width, hd), grid_spec=p...  31.7 us
  transfers between devices with their start and end apart: 100, of which 34 were waited for; matrix products, arithmetic and copies ran while one was open for 7% of the time, Pallas kernels for 44%

profile of v14, /device:TPU:0, one launch (start us, length us, event | category | flops | bytes accessed | tf_op | source)
XLA Modules:
  0.0 749.5 jit_solution(6873432158895902358)
XLA Ops:
  86.8 13.0 %collective-permute-done.15.rest_4_.rest_0_ = bf16[256,1152]{1,0:T(8,128)(2,1)} collective-permute-done((bf16[256,1152]{1,0:T(8,128)(2,1)}, bf16[256,1152]{1,0:T(8,128)(2,1)}, u32[]{:S(2)}, u32[]{:S(2)}) %collective-permute-start.15) | collective-permute-done | bytes 589856 | tf_op jit(solution)/shard_map/ppermute | solution.py:1631
  102.2 15.9 %attn_fwd.2 = (bf16[1024,256]{1,0:T(8,128)(2,1)}, bf16[1024,256]{1,0:T(8,128)(2,1)}, f32[2,2,2048]{2,1,0:T(2,128)}) custom-call(s32[4]{0:T(128)} %copy-done.22, bf16[512,1024]{1,0:T(8,128)(2,1)} %copy-done.29, bf16[512,1024]{1,0:T(8,128)(2,1)} %copy-done.57), custom_call_target="tpu_custom_call" | custom-call | flops 4398046511104 | bytes 1073741824 | tf_op jit(solution)/shard_map/attn_fwd/pallas_call | solution.py:776
  127.6 15.9 %attn_fwd.3 = (bf16[1024,256]{1,0:T(8,128)(2,1)}, bf16[1024,256]{1,0:T(8,128)(2,1)}, f32[2,2,2048]{2,1,0:T(2,128)}) custom-call(s32[4]{0:T(128)} %copy-done.22, bf16[512,1024]{1,0:T(8,128)(2,1)} %copy-done.28, bf16[512,1024]{1,0:T(8,128)(2,1)} %collective-permute-done.17.got_ref), custom_call_target="tpu_custom_call" | custom-call | flops 4398046511104 | bytes 1073741824 | tf_op jit(solution)/shard_map/attn_fwd/pallas_call | solution.py:776
  149.2 11.8 %collective-permute-done.27.refs_8_ = bf16[1024,256]{1,0:T(8,128)(2,1)S(1)} collective-permute-done((bf16[1024,256]{1,0:T(8,128)(2,1)}, bf16[1024,256]{1,0:T(8,128)(2,1)S(1)}, u32[]{:S(2)}, u32[]{:S(2)}) %collective-permute-start.27) | collective-permute-done | bytes 524320 | tf_op jit(solution)/shard_map/ppermute | solution.py:1628
  164.5 10.3 %out_proj.1 = (f32[1024,1024]{1,0:T(8,128)}, bf16[1024,1024]{1,0:T(8,128)(2,1)}, bf16[1024,1024]{1,0:T(8,128)(2,1)}, bf16[4,1024,256]{2,1,0:T(8,128)(2,1)}) custom-call(s32[4]{0:T(128)} %copy-done.22, bf16[1024,256]{1,0:T(8,128)(2,1)} %constant_dynamic-update-slice_fusion.refs_0_, bf16[1024,256]{1,0:T(8,128)(2,1)} %collective-permute-done.25.refs_1_, ...), custom_call_target="tpu_custom_call" | custom-call | flops 4398046511104 | bytes 1073741824 | tf_op jit(solution)/shard_map/out_proj/pallas_call | solution.py:1002
  185.4 27.2 %ffn_fwd.3 = (bf16[2,1024,2304]{2,1,0:T(8,128)(2,1)}, bf16[2,1024,1152]{2,1,0:T(8,128)(2,1)}, f32[1024,1024]{1,0:T(8,128)}) custom-call(s32[4]{0:T(128)} %copy-done.22, f32[1]{0:T(128)} %bitcast.4.scale, bf16[1024,1024]{1,0:T(8,128)(2,1)} %get-tuple-element.1855.x_ref, f32[1024,1024]{1,0:T(8,128)} %get-tuple-element.2421.in_ref.refs_5_, ...), custom_call_target="tpu_custom_call" | custom-call | flops 4398046511104 | bytes 1073741824 | tf_op jit(solution)/shard_map/ffn_fwd/pallas_call | solution.py:1309
  220.0 15.9 %ffn_fwd.4 = (bf16[1,1024,2304]{2,1,0:T(8,128)(2,1)}, bf16[1,1024,1152]{2,1,0:T(8,128)(2,1)}, f32[1024,1024]{1,0:T(8,128)}) custom-call(s32[4]{0:T(128)} %copy-done.22, f32[1]{0:T(128)} %bitcast.4.scale, bf16[1024,1024]{1,0:T(8,128)(2,1)} %get-tuple-element.1855.x_ref, f32[1024,1024]{1,0:T(8,128)} %get-tuple-element.1757.in_ref, ...), custom_call_target="tpu_custom_call" | custom-call | flops 4398046511104 | bytes 1073741824 | tf_op jit(solution)/shard_map/ffn_fwd/pallas_call | solution.py:1309
  239.9 19.8 %ffn_fwd.5 = (bf16[1,1024,2304]{2,1,0:T(8,128)(2,1)}, bf16[1,1024,1152]{2,1,0:T(8,128)(2,1)}, bf16[512,1024]{1,0:T(8,128)(2,1)}, bf16[512,1024]{1,0:T(8,128)(2,1...) custom-call(s32[4]{0:T(128)} %copy-done.22, ...), custom_call_target="tpu_custom_call" | custom-call | flops 4398046511104 | bytes 1073741824 | tf_op jit(solution)/shard_map/ffn_fwd/pallas_call | solution.py:1309
  260.2 24.8 %ffn_bwd.4 = (f32[1024,1024]{1,0:T(8,128)}, bf16[512,3456]{1,0:T(8,128)(2,1)}, bf16[512,3456]{1,0:T(8,128)(2,1)}) custom-call(bf16[1024,1024]{1,0:T(8,128)(2,1)} %get-tuple-element.2344.low_ref, bf16[1,1024,2304]{2,1,0:T(8,128)(2,1)} %get-tuple-element.1977.act_ref, bf16[1,1024,1152]{2,1,0:T(8,128)(2,1)} %get-tuple-element.1997.hid_ref, ...), custom_call_target="tpu_custom_call" | custom-call | flops 4398046511104 | bytes 1073741824 | tf_op jit(solution)/shard_map/ffn_bwd/pallas_call | solution.py:1391
  287.2 25.3 %ffn_bwd.5 = (f32[1024,1024]{1,0:T(8,128)}, bf16[512,3456]{1,0:T(8,128)(2,1)}, bf16[512,3456]{1,0:T(8,128)(2,1)}) custom-call(bf16[1024,1024]{1,0:T(8,128)(2,1)} %get-tuple-element.2344.low_ref, bf16[2,1024,2304]{2,1,0:T(8,128)(2,1)} %get-tuple-element.2328.act_ref, ...), custom_call_target="tpu_custom_call", output_to_operand_aliasing={{0}: (15, {})} | custom-call | flops 4398046511104 | bytes 1073741824 | tf_op jit(solution)/shard_map/ffn_bwd/pallas_call | solution.py:1391
  323.6 25.3 %ffn_bwd.6 = (f32[1024,1024]{1,0:T(8,128)}, bf16[512,3456]{1,0:T(8,128)(2,1)}, bf16[512,3456]{1,0:T(8,128)(2,1)}) custom-call(bf16[1024,1024]{1,0:T(8,128)(2,1)} %get-tuple-element.2344.low_ref, bf16[1,1024,2304]{2,1,0:T(8,128)(2,1)} %get-tuple-element.2252.act_ref, ...), custom_call_target="tpu_custom_call", output_to_operand_aliasing={{0}: (17, {})} | custom-call | flops 4398046511104 | bytes 1073741824 | tf_op jit(solution)/shard_map/ffn_bwd/pallas_call | solution.py:1391
  359.6 25.3 %ffn_bwd.7 = (f32[1024,1024]{1,0:T(8,128)}, bf16[512,3456]{1,0:T(8,128)(2,1)}, bf16[512,3456]{1,0:T(8,128)(2,1)}) custom-call(bf16[1024,1024]{1,0:T(8,128)(2,1)} %get-tuple-element.2344.low_ref, bf16[2,1024,2304]{2,1,0:T(8,128)(2,1)} %get-tuple-element.2328.act_ref, ...), custom_call_target="tpu_custom_call", output_to_operand_aliasing={{0}: (9, {})} | custom-call | flops 4398046511104 | bytes 1073741824 | tf_op jit(solution)/shard_map/ffn_bwd/pallas_call | solution.py:1391
  393.9 12.4 %norm_two_back.1 = (f32[1024,1024]{1,0:T(8,128)}, bf16[1024,1024]{1,0:T(8,128)(2,1)}, bf16[1024,256]{1,0:T(8,128)(2,1)}, bf16[1024,256]{1,0:T(8,128)(2,1)}, bf16...) custom-call(s32[4]{0:T(128)} %copy-done.22, ...), custom_call_target="tpu_custom_call" | custom-call | flops 4398046511104 | bytes 1073741824 | tf_op jit(solution)/shard_map/norm_two_back/pallas_call | solution.py:1060
  408.5 12.9 %collective-permute-done.68.gs_ref = bf16[1024,256]{1,0:T(8,128)(2,1)S(1)} collective-permute-done((bf16[1024,256]{1,0:T(8,128)(2,1)}, bf16[1024,256]{1,0:T(8,128)(2,1)S(1)}, u32[]{:S(2)}, u32[]{:S(2)}) %collective-permute-start.68) | collective-permute-done | bytes 524320 | tf_op jit(solution)/shard_map/ppermute | solution.py:1628
  432.3 17.2 %attn_bwd.2 = (bf16[512,1024]{1,0:T(8,128)(2,1)}, bf16[512,1024]{1,0:T(8,128)(2,1)}) custom-call(s32[4]{0:T(128)} %copy-done.22, bf16[512,1024]{1,0:T(8,128)(2,1)} %copy-done.29, bf16[512,1024]{1,0:T(8,128)(2,1)} %copy-done.57, bf16[1024,256]{1,0:T(8,128)(2,1)} %get-tuple-element.2467.refs_5_.ok_ref, bf16[1024,256]{1,0:T(8,128)(2,1)} %get-tuple-element.2468.os_ref, ...), custom_call_target="tpu_custom_call" | custom-call | flops 4398046511104 | bytes 1073741824 | tf_op jit(solution)/shard_map/attn_bwd/pallas_call | solution.py:937
  453.1 16.1 %collective-permute-done.70.refs_1_ = bf16[128,3456]{1,0:T(8,128)(2,1)} collective-permute-done((bf16[128,3456]{1,0:T(8,128)(2,1)}, bf16[128,3456]{1,0:T(8,128)(2,1)}, u32[]{:S(2)}, u32[]{:S(2)}) %collective-permute-start.70) | collective-permute-done | bytes 884768 | tf_op jit(solution)/shard_map/ppermute | solution.py:1622
  478.0 17.2 %attn_bwd.3 = (bf16[512,1024]{1,0:T(8,128)(2,1)}, bf16[512,1024]{1,0:T(8,128)(2,1)}) custom-call(s32[4]{0:T(128)} %copy-done.22, bf16[512,1024]{1,0:T(8,128)(2,1)} %copy-done.28, bf16[512,1024]{1,0:T(8,128)(2,1)} %collective-permute-done.17.got_ref, bf16[1024,256]{1,0:T(8,128)(2,1)} %get-tuple-element.2531.refs_6_.ok_ref, ...), custom_call_target="tpu_custom_call" | custom-call | flops 4398046511104 | bytes 1073741824 | tf_op jit(solution)/shard_map/attn_bwd/pallas_call | solution.py:937
  498.9 14.6 %collective-permute-done.75.refs_4_ = bf16[128,3456]{1,0:T(8,128)(2,1)} collective-permute-done((bf16[128,3456]{1,0:T(8,128)(2,1)}, bf16[128,3456]{1,0:T(8,128)(2,1)}, u32[]{:S(2)}, u32[]{:S(2)}) %collective-permute-start.75) | collective-permute-done | bytes 884768 | tf_op jit(solution)/shard_map/ppermute | solution.py:1622
  554.5 9.0 %norm_one_back.3 = (bf16[512,1024]{1,0:T(8,128)(2,1)}, f32[1,1024]{1,0:T(1,128)}) custom-call(s32[4]{0:T(128)} %copy-done.22, bf16[512,512]{1,0:T(8,128)(2,1)} %copy-done.2, bf16[768,512]{1,0:T(8,128)(2,1)} %copy-done.1, bf16[768,512]{1,0:T(8,128)(2,1)} %collective-permute-done.10.refs_2_, bf16[512,512]{1,0:T(8,128)(2,1)} %copy-done.4, ...), custom_call_target="tpu_custom_call" | custom-call | flops 4398046511104 | bytes 1073741824 | tf_op jit(solution)/shard_map/norm_one_back/pallas_call | solution.py:1117
  573.7 15.2 %weight_grad.1 = (bf16[4,512,768]{2,1,0:T(8,128)(2,1)}, bf16[4,512,768]{2,1,0:T(8,128)(2,1)}) custom-call(bf16[1024,1024]{1,0:T(8,128)(2,1)} %copy-done, bf16[2,1024,512]{2,1,0:T(8,128)(2,1)} %get-tuple-element.2671.refs_6_.back0_ref, bf16[2,1024,512]{2,1,0:T(8,128)(2,1)} %get-tuple-element.2673.refs_7_.back1_ref, ...), custom_call_target="tpu_custom_call" | custom-call | flops 4398046511104 | bytes 1073741824 | tf_op jit(solution)/shard_map/weight_grad/pallas_call | solution.py:1574
  609.4 12.0 %collective-permute-done.87.refs_1_ = bf16[512,768]{1,0:T(8,128)(2,1)S(1)} collective-permute-done((bf16[512,768]{1,0:T(8,128)(2,1)S(1)}, bf16[512,768]{1,0:T(8,128)(2,1)S(1)}, u32[]{:S(2)}, u32[]{:S(2)}) %collective-permute-start.87) | collective-permute-done | bytes 786464 | tf_op jit(solution)/shard_map/ppermute | solution.py:1622
  656.9 10.9 %collective-permute-done.91.refs_1_ = bf16[128,768]{1,0:T(8,128)(2,1)S(1)} collective-permute-done((bf16[128,768]{1,0:T(8,128)(2,1)S(1)}, bf16[128,768]{1,0:T(8,128)(2,1)S(1)}, u32[]{:S(2)}, u32[]{:S(2)}) %collective-permute-start.91) | collective-permute-done | bytes 196640 | tf_op jit(solution)/shard_map/ppermute | solution.py:1637
  667.8 25.4 %collective-permute-done.92.refs_2_ = bf16[128,768]{1,0:T(8,128)(2,1)S(1)} collective-permute-done((bf16[128,768]{1,0:T(8,128)(2,1)S(1)}, bf16[128,768]{1,0:T(8,128)(2,1)S(1)}, u32[]{:S(2)}, u32[]{:S(2)}) %collective-permute-start.92) | collective-permute-done | bytes 196640 | tf_op jit(solution)/shard_map/ppermute | solution.py:1634
  699.8 10.6 %pad_convert_fusion = f32[4,1024,1024]{2,1,0:T(8,128)} fusion(bf16[4,512,1024]{2,1,0:T(8,128)(2,1)} %bitcast.65), kind=kLoop, calls=%fused_computation.1 | loop fusion | flops 4194304 | bytes 20971520 | tf_op jit(solution)/shard_map/dynamic_update_slice | solution.py:2118
  (447 shorter events, 326.0 us)
Async XLA Ops:
  7.2 692.6 %all-gather.5.cloned.1.call-start = ((), (), s32[]{:S(2)}) async-start(), calls=%async_computation | async-start | bytes 5242880 | tf_op jit(solution)/shard_map/all_gather | solution.py:2024
  56.5 43.3 %collective-permute-start.11 = (bf16[256,3456]{1,0:T(8,128)(2,1)}, bf16[256,3456]{1,0:T(8,128)(2,1)}, u32[]{:S(2)}, u32[]{:S(2)}) collective-permute-start(bf16[256,3456]{1,0:T(8,128)(2,1)} %get-tuple-element.2349.rest_0_), channel_id=1, source_target_pairs={{0,16},{16,0},{8,24},{24,8},{1,17},{17,1},{9,25},{25,9},{2,18},{18... | collective-permute-start | bytes 5308424 | tf_op jit(solution)/shard_map/ppermute | solution.py:1622
  57.4 42.4 %collective-permute-start.16 = (bf16[256,2304]{1,0:T(8,128)(2,1)}, bf16[256,2304]{1,0:T(8,128)(2,1)}, u32[]{:S(2)}, u32[]{:S(2)}) collective-permute-start(bf16[256,2304]{1,0:T(8,128)(2,1)} %get-tuple-element.1443), channel_id=1, source_target_pairs={{0,1},{1,2},{2,3},{3,0},{4,5},{5,6},{6,7},{7,4},{8,9},{9,10},{10,1... | collective-permute-start | bytes 3538952 | tf_op jit(solution)/shard_map/ppermute | solution.py:1631
  70.2 29.7 %collective-permute-start.14 = (bf16[512,1024]{1,0:T(8,128)(2,1)S(1)}, bf16[512,1024]{1,0:T(8,128)(2,1)S(1)}, u32[]{:S(2)}, u32[]{:S(2)}) collective-permute-start(bf16[512,1024]{1,0:T(8,128)(2,1)S(1)} %get-tuple-element.1432), channel_id=1, source_target_pairs={{0,4},{4,0},{1,5},{5,1},{2,6},{6,2},{3,7},{7,3},{8,12},{12,8},{9,1... | collective-permute-start | bytes 3145736 | tf_op jit(solution)/shard_map/ppermute | solution.py:1628
  75.5 42.6 %collective-permute-start.17 = (bf16[512,1024]{1,0:T(8,128)(2,1)}, bf16[512,1024]{1,0:T(8,128)(2,1)}, u32[]{:S(2)}, u32[]{:S(2)}) collective-permute-start(bf16[512,1024]{1,0:T(8,128)(2,1)} %get-tuple-element.1435), channel_id=1, source_target_pairs={{0,4},{4,0},{1,5},{5,1},{2,6},{6,2},{3,7},{7,3},{8,12},{12,8},{9,1... | collective-permute-start | bytes 3145736 | tf_op jit(solution)/shard_map/ppermute | solution.py:1628
  180.5 32.1 %collective-permute-start.41 = (bf16[256,2304]{1,0:T(8,128)(2,1)}, bf16[256,2304]{1,0:T(8,128)(2,1)}, u32[]{:S(2)}, u32[]{:S(2)}) collective-permute-start(bf16[256,2304]{1,0:T(8,128)(2,1)} %collective-permute-done.16.rest_5_.rest_1_), channel_id=1, source_target_pairs={{0,1},{1,2},{2,3},{3,0},{4,5},{5,6},{6,7},{7,4},{8,9},{9,10},{10,1... | collective-permute-start | bytes 3538952 | tf_op jit(solution)/shard_map/ppermute | solution.py:1631
  180.5 32.1 %collective-permute-start.38 = (bf16[256,1152]{1,0:T(8,128)(2,1)}, bf16[256,1152]{1,0:T(8,128)(2,1)}, u32[]{:S(2)}, u32[]{:S(2)}) collective-permute-start(bf16[256,1152]{1,0:T(8,128)(2,1)} %collective-permute-done.21.rest_0_), channel_id=1, source_target_pairs={{0,8},{8,0},{16,24},{24,16},{1,9},{9,1},{17,25},{25,17},{2,10},{10... | collective-permute-start | bytes 1769480 | tf_op jit(solution)/shard_map/ppermute | solution.py:1625
  181.1 31.6 %collective-permute-start.39 = (bf16[256,1152]{1,0:T(8,128)(2,1)}, bf16[256,1152]{1,0:T(8,128)(2,1)}, u32[]{:S(2)}, u32[]{:S(2)}) collective-permute-start(bf16[256,1152]{1,0:T(8,128)(2,1)} %collective-permute-done.26.rest_1_), channel_id=1, source_target_pairs={{0,16},{16,0},{8,24},{24,8},{1,17},{17,1},{9,25},{25,9},{2,18},{18... | collective-permute-start | bytes 1769480 | tf_op jit(solution)/shard_map/ppermute | solution.py:1622
  182.3 30.4 %collective-permute-start.40 = (bf16[256,1152]{1,0:T(8,128)(2,1)}, bf16[256,1152]{1,0:T(8,128)(2,1)}, u32[]{:S(2)}, u32[]{:S(2)}) collective-permute-start(bf16[256,1152]{1,0:T(8,128)(2,1)} %collective-permute-done.35.rest_3_), channel_id=1, source_target_pairs={{0,4},{4,0},{1,5},{5,1},{2,6},{6,2},{3,7},{7,3},{8,12},{12,8},{9,1... | collective-permute-start | bytes 1769480 | tf_op jit(solution)/shard_map/ppermute | solution.py:1628
  355.2 29.6 %collective-permute-start.64 = (bf16[128,3456]{1,0:T(8,128)(2,1)}, bf16[128,3456]{1,0:T(8,128)(2,1)}, u32[]{:S(2)}, u32[]{:S(2)}) collective-permute-start(bf16[128,3456]{1,0:T(8,128)(2,1)} %get-tuple-element.2383), channel_id=1, source_target_pairs={{0,4},{4,0},{1,5},{5,1},{2,6},{6,2},{3,7},{7,3},{8,12},{12,8},{9,1... | collective-permute-start | bytes 2654216 | tf_op jit(solution)/shard_map/ppermute | solution.py:1628
  391.6 29.9 %collective-permute-start.66 = (bf16[128,3456]{1,0:T(8,128)(2,1)}, bf16[128,3456]{1,0:T(8,128)(2,1)}, u32[]{:S(2)}, u32[]{:S(2)}) collective-permute-start(bf16[128,3456]{1,0:T(8,128)(2,1)} %get-tuple-element.2405), channel_id=1, source_target_pairs={{0,3},{1,0},{2,1},{3,2},{4,7},{5,4},{6,5},{7,6},{8,11},{9,8},{10,9... | collective-permute-start | bytes 2654216 | tf_op jit(solution)/shard_map/ppermute | solution.py:1637
  407.7 41.8 %collective-permute-start.71 = (bf16[1024,256]{1,0:T(8,128)(2,1)}, bf16[1024,256]{1,0:T(8,128)(2,1)}, u32[]{:S(2)}, u32[]{:S(2)}) collective-permute-start(bf16[1024,256]{1,0:T(8,128)(2,1)} %get-tuple-element.2490), channel_id=1, source_target_pairs={{0,4},{4,0},{1,5},{5,1},{2,6},{6,2},{3,7},{7,3},{8,12},{12,8},{9,1... | collective-permute-start | bytes 1572872 | tf_op jit(solution)/shard_map/ppermute | solution.py:1628
  429.1 40.1 %collective-permute-start.72 = (bf16[512,1024]{1,0:T(8,128)(2,1)}, bf16[512,1024]{1,0:T(8,128)(2,1)}, u32[]{:S(2)}, u32[]{:S(2)}) collective-permute-start(bf16[512,1024]{1,0:T(8,128)(2,1)} %collective-permute-done.55), channel_id=1, source_target_pairs={{0,1},{1,2},{2,3},{3,0},{4,5},{5,6},{6,7},{7,4},{8,9},{9,10},{10,1... | collective-permute-start | bytes 3145736 | tf_op jit(solution)/shard_map/ppermute | solution.py:1631
  431.0 38.2 %collective-permute-start.70 = (bf16[128,3456]{1,0:T(8,128)(2,1)}, bf16[128,3456]{1,0:T(8,128)(2,1)}, u32[]{:S(2)}, u32[]{:S(2)}) collective-permute-start(bf16[128,3456]{1,0:T(8,128)(2,1)} %get-tuple-element.2483), channel_id=1, source_target_pairs={{0,16},{16,0},{8,24},{24,8},{1,17},{17,1},{9,25},{25,9},{2,18},{18... | collective-permute-start | bytes 2654216 | tf_op jit(solution)/shard_map/ppermute | solution.py:1622
  474.1 41.8 %collective-permute-start.76 = (bf16[512,1024]{1,0:T(8,128)(2,1)}, bf16[512,1024]{1,0:T(8,128)(2,1)}, u32[]{:S(2)}, u32[]{:S(2)}) collective-permute-start(bf16[512,1024]{1,0:T(8,128)(2,1)} %get-tuple-element.2528), channel_id=1, source_target_pairs={{0,4},{4,0},{1,5},{5,1},{2,6},{6,2},{3,7},{7,3},{8,12},{12,8},{9,1... | collective-permute-start | bytes 3145736 | tf_op jit(solution)/shard_map/ppermute | solution.py:1628
  475.6 40.3 %collective-permute-start.77 = (bf16[512,1024]{1,0:T(8,128)(2,1)}, bf16[512,1024]{1,0:T(8,128)(2,1)}, u32[]{:S(2)}, u32[]{:S(2)}) collective-permute-start(bf16[512,1024]{1,0:T(8,128)(2,1)} %collective-permute-done.57), channel_id=1, source_target_pairs={{0,1},{1,2},{2,3},{3,0},{4,5},{5,6},{6,7},{7,4},{8,9},{9,10},{10,1... | collective-permute-start | bytes 3145736 | tf_op jit(solution)/shard_map/ppermute | solution.py:1631
  476.7 36.8 %collective-permute-start.75 = (bf16[128,3456]{1,0:T(8,128)(2,1)}, bf16[128,3456]{1,0:T(8,128)(2,1)}, u32[]{:S(2)}, u32[]{:S(2)}) collective-permute-start(bf16[128,3456]{1,0:T(8,128)(2,1)} %get-tuple-element.2549), channel_id=1, source_target_pairs={{0,16},{16,0},{8,24},{24,8},{1,17},{17,1},{9,25},{25,9},{2,18},{18... | collective-permute-start | bytes 2654216 | tf_op jit(solution)/shard_map/ppermute | solution.py:1622
  516.3 47.8 %collective-permute-start.82 = (bf16[128,3456]{1,0:T(8,128)(2,1)}, bf16[128,3456]{1,0:T(8,128)(2,1)}, u32[]{:S(2)}, u32[]{:S(2)}) collective-permute-start(bf16[128,3456]{1,0:T(8,128)(2,1)} %get-tuple-element.2541), channel_id=1, source_target_pairs={{0,3},{1,0},{2,1},{3,2},{4,7},{5,4},{6,5},{7,6},{8,11},{9,8},{10,9... | collective-permute-start | bytes 2654216 | tf_op jit(solution)/shard_map/ppermute | solution.py:1637
  525.0 39.2 %collective-permute-start.83 = (bf16[128,3456]{1,0:T(8,128)(2,1)}, bf16[128,3456]{1,0:T(8,128)(2,1)}, u32[]{:S(2)}, u32[]{:S(2)}) collective-permute-start(bf16[128,3456]{1,0:T(8,128)(2,1)} %get-tuple-element.2665), channel_id=1, source_target_pairs={{0,1},{1,2},{2,3},{3,0},{4,5},{5,6},{6,7},{7,4},{8,9},{9,10},{10,1... | collective-permute-start | bytes 2654216 | tf_op jit(solution)/shard_map/ppermute | solution.py:1631
  525.2 39.0 %collective-permute-start.80 = (bf16[128,3456]{1,0:T(8,128)(2,1)}, bf16[128,3456]{1,0:T(8,128)(2,1)}, u32[]{:S(2)}, u32[]{:S(2)}) collective-permute-start(bf16[128,3456]{1,0:T(8,128)(2,1)} %get-tuple-element.2614), channel_id=1, source_target_pairs={{0,16},{16,0},{8,24},{24,8},{1,17},{17,1},{9,25},{25,9},{2,18},{18... | collective-permute-start | bytes 2654216 | tf_op jit(solution)/shard_map/ppermute | solution.py:1622
  553.8 178.2 %all-gather.7.cloned.1.call-start = ((), (), s32[]{:S(2)}) async-start(), calls=%async_computation.1 | async-start | bytes 5242880 | tf_op jit(solution)/shard_map/all_gather | solution.py:2038
  646.1 64.2 %collective-permute-start.94 = (f32[128,3456]{1,0:T(8,128)S(1)}, f32[128,3456]{1,0:T(8,128)}, u32[]{:S(2)}, u32[]{:S(2)}) collective-permute-start(f32[128,3456]{1,0:T(8,128)S(1)} %copy-done.33), channel_id=1, source_target_pairs={{0,4},{4,0},{1,5},{5,1},{2,6},{6,2},{3,7},{7,3},{8,12},{12,8},{9,1... | collective-permute-start | bytes 5308424 | tf_op jit(solution)/shard_map/ppermute | solution.py:1628
  656.1 37.1 %collective-permute-start.92 = (bf16[128,768]{1,0:T(8,128)(2,1)S(1)}, bf16[128,768]{1,0:T(8,128)(2,1)S(1)}, u32[]{:S(2)}, u32[]{:S(2)}) collective-permute-start(bf16[128,768]{1,0:T(8,128)(2,1)S(1)} %get-tuple-element.2825), channel_id=1, source_target_pairs={{0,2},{2,0},{1,3},{3,1},{4,6},{6,4},{5,7},{7,5},{8,10},{10,8},{9,1... | collective-permute-start | bytes 589832 | tf_op jit(solution)/shard_map/ppermute | solution.py:1634
  656.1 37.1 %collective-permute-start.93 = (bf16[128,768]{1,0:T(8,128)(2,1)S(1)}, bf16[128,768]{1,0:T(8,128)(2,1)S(1)}, u32[]{:S(2)}, u32[]{:S(2)}) collective-permute-start(bf16[128,768]{1,0:T(8,128)(2,1)S(1)} %get-tuple-element.2824), channel_id=1, source_target_pairs={{0,1},{1,2},{2,3},{3,0},{4,5},{5,6},{6,7},{7,4},{8,9},{9,10},{10,1... | collective-permute-start | bytes 589832 | tf_op jit(solution)/shard_map/ppermute | solution.py:1631
  (148 other events, 1961.6 us)
Sparse Core Ops, SparseCore 0:
  554.0 80.0 all-gather.4
  635.7 96.3 all-gather.6

commit v15 on v14

--- a/solution.py
+++ b/solution.py
@@ -407,8 +407,10 @@
     return jax.ShapeDtypeStruct(shape, dtype)
 
 
-def cost(large):
+def cost(large, microseconds=None):
     size = 1 << 42 if large else 1 << 10
+    if microseconds is not None:
+        size = int(microseconds * 1.15e9)
     return pl.CostEstimate(flops=size, bytes_accessed=size >> 12, transcendentals=0)
 
 
@@ -960,7 +962,7 @@
         ),
         out_shape=[shape_of((cols, tok), BF16), shape_of((cols, tok), BF16)],
         compiler_params=settings(2, 60),
-        cost_estimate=cost(True),
+        cost_estimate=cost(True, 16.2),
         name="attn_bwd",
     )(info, mine, got, out_keep, out_send, grad_keep, grad_send, lse)
 
@@ -1072,7 +1074,7 @@
         + [shape_of((tok, feats), BF16)] * 4
         + [shape_of((1, width), F32)],
         compiler_params=settings(1, 60),
-        cost_estimate=cost(True),
+        cost_estimate=cost(True, 5.4),
         name="norm_two_back",
     )(info, *pieces, grad, resid, grad_result, gain)
 
@@ -1171,8 +1173,8 @@
         rest = rest[count:]
     act_ref, hid_ref = rest[:2]
     if last:
-        outa_ref, outb_ref, gres_ref, low_ref, lowt_ref, sq_ref = rest[2:8]
-        gate_up, down, total, sems = rest[8:]
+        out_ref, gres_ref, low_ref, lowt_ref, sq_ref = rest[2:7]
+        gate_up, down, total, sems = rest[7:]
     else:
         sum_ref, gate_up, down, total, sems = rest[2:]
     step, part = pl.program_id(0), pl.program_id(1)
@@ -1238,16 +1240,7 @@
             at = pl.multiple_of(jnp.bitwise_xor(info[1], mask) * quarter, quarter)
             cols = slice(p * quarter, (p + 1) * quarter)
             value = result[:, cols]
-            low = value.astype(BF16)
-
-            @pl.when(part < pl.num_programs(1) // 2)
-            def _():
-                outa_ref[:, pl.ds(at, quarter)] = low
-
-            @pl.when(part >= pl.num_programs(1) // 2)
-            def _():
-                outb_ref[:, pl.ds(at, quarter)] = low
-
+            out_ref[:, pl.ds(at, quarter)] = value.astype(BF16)
             error = valid * (value - teach_ref[0, :, pl.ds(at, quarter)].astype(F32))
             square = square + error * error
             grad = error * scale[0]
@@ -1282,22 +1275,15 @@
         in_specs.append(
             pl.BlockSpec((1, tile, width), lambda s, i, info: (info[0], leave(s, i), 0))
         )
-        half = tok // tile // 2
         out_specs += [
-            pl.BlockSpec(
-                (tile, width), lambda s, i, info: (jnp.minimum(leave(s, i), half - 1), 0)
-            ),
-            pl.BlockSpec(
-                (tile, width), lambda s, i, info: (jnp.maximum(leave(s, i) - half, 0), 0)
-            ),
+            tiles(width),
             tiles(width),
             tiles(width),
             pl.BlockSpec((width, tile), lambda s, i, info: (0, leave(s, i))),
             pl.BlockSpec((1, width // 4), lambda s, i, info: (0, 0)),
         ]
         out_shape += [
-            shape_of((tok // 2, width), BF16),
-            shape_of((tok // 2, width), BF16),
+            shape_of((tok, width), BF16),
             shape_of((tok, width), F32),
             shape_of((tok, width), BF16),
             shape_of((width, tok), BF16),
@@ -1419,7 +1405,7 @@
         ],
         input_output_aliases={} if first else {5 + len(pieces): 0},
         compiler_params=settings(1, 60),
-        cost_estimate=cost(True),
+        cost_estimate=cost(True, 11.2),
         name="ffn_bwd",
     )(low, acts, hiddens, xt, lowt, *pieces, *([] if first else [total]))
 
@@ -1829,14 +1815,14 @@
 
     weights2 = v["two"] + v["two_far"] + v["two_cores"]
     weights2 += [core_swap(part) for part in v["two_far"][1:]]
-    acts_c, hiddens_c, *results, grad_result, grad_low, grad_low_t, square = ffn_fwd(
+    acts_c, hiddens_c, result_low, grad_result, grad_low, grad_low_t, square = ffn_fwd(
         info, v["scale"], v["normed_two"], v["sum_b"], teacher, [(plan_mixed, weights2)], units, 256
     )
     v.update(
         weights2=weights2,
         acts_c=acts_c,
         hiddens_c=hiddens_c,
-        results=results,
+        result_low=result_low,
         grad_result=grad_result,
         grad_low=grad_low,
         grad_low_t=grad_low_t,
@@ -1856,18 +1842,16 @@
         )
 
     turned = [False, False, True]
-    one = [z_up(v["results"][0])]
+    output = lax.all_gather(v["result_low"], "tp", axis=0, tiled=False)
     total, keep2, send2 = ffn_back(plan_mixed, "weights2", "acts_c", "hiddens_c", 0, None)
-    v.update(one=one, total=total, keep2=keep2, send2=send2)
-    sync()
-
-    one = v["one"] + [z_up(v["results"][1])]
+    v.update(total=total, keep2=keep2, send2=send2)
+    sync()
+
     came2 = core_swap(v["send2"])
     total, keep1, send1 = ffn_back(plan_mixed, "weights1", "acts_a", "hiddens_a", 1, v["total"])
-    v.update(one=one, came2=came2, total=total, keep1=keep1, send1=send1)
-    sync()
-
-    out_three = [z_down(v["results"][0])]
+    v.update(came2=came2, total=total, keep1=keep1, send1=send1)
+    sync()
+
     came1 = core_swap(v["send1"])
     sum2 = sums(info, [v["keep2"], v["came2"]], core_jobs(0, 1))
     far_t2 = x_swap(sum2[3])
@@ -1875,7 +1859,6 @@
         plan_chunks, "weights3", "acts_b", "hiddens_b", 0, after(v["total"], sum2[0])
     )
     v.update(
-        out_three=out_three,
         came1=came1,
         sum2=sum2,
         far_t2=far_t2,
@@ -1885,7 +1868,6 @@
     )
     sync()
 
-    out_three = v["out_three"] + [z_down(v["results"][1])]
     came3 = core_swap(v["send3"])
     far_h2 = x_swap(v["sum2"][2])
     there2, *sum1 = sums(
@@ -1898,7 +1880,6 @@
         plan0, "weights0", "acts_a", "hiddens_a", 0, after(v["total"], sum1[0])
     )
     v.update(
-        out_three=out_three,
         came3=came3,
         far_h2=far_h2,
         there2=there2,
@@ -1931,7 +1912,6 @@
     v.update(
         came0=came0,
         far_t1=far_t1,
-        down2=down2,
         sum3=sum3,
         grad_resid=grad_resid,
         grad_attn_t=grad_attn_t,
@@ -1947,7 +1927,6 @@
             info, v["mine"][j][0], got_ref, out[0], out[1], grad, v[f"grad_got{j}"], out[2], hd
         )
 
-    two = [z_up(v["one"][0])]
     far_h1 = x_swap(v["sum1"][2])
     there1, *sum0 = sums(
         info,
@@ -1958,17 +1937,16 @@
     far_t3 = x_swap(v["sum3"][3])
     back0 = attn_back(0, after(v["grad_mine"][0], sum0[0]))
     v.update(
-        out_two=two,
         far_h1=far_h1,
         there1=there1,
         far_t3=far_t3,
+        down2=down2,
         sum0=sum0,
         back0=back0,
         grad_got1=grad_got[1],
     )
     sync()
 
-    two = v["out_two"] + [z_up(v["one"][1])]
     heads0 = y_swap(v["back0"][1])
     far_h3 = x_swap(v["sum3"][2])
     far_t0 = x_swap(v["sum0"][3])
@@ -1982,9 +1960,9 @@
     )
     there3_got = y_swap(there3)
     two_down_got = z_down(two_down)
-    back1 = attn_back(1, after(v["grad_mine"][1], there3, two_down))
+    back1 = attn_back(1, after(v["grad_mine"][1], there3, two_down, output))
     v.update(
-        out_two=two, heads0=heads0, far_h3=far_h3, far_t0=far_t0, there3=there3_got, back1=back1
+        heads0=heads0, far_h3=far_h3, far_t0=far_t0, there3=there3_got, back1=back1
     )
     sync()
 
@@ -2027,14 +2005,6 @@
     v.update(there0=there0, far_h0=far_h0, two_down=two_down_got)
     sync()
 
-    def place(out, parts, k, first):
-        row = lax.rem(z - k + 4, 4)
-        for j, part in enumerate(parts):
-            at = (first + j) * part.shape[0]
-            out = lax.dynamic_update_slice(out, part.astype(out.dtype)[None], (row, at, 0))
-        return out
-
-    v.update(out_one=v["one"])
     gathered.append(lax.all_gather(v["tokens_low"], "tp", axis=0, tiled=False))
     keep, send = weight_grad(
         v["normed_one_t"], [v["head0"][0], v["head1"][0]], v["grad_attn_t"], v["attended"]
@@ -2072,10 +2042,7 @@
 
     far_h = x_swap(v["sums"][2])
     there = y_swap(summed([v["sums"][1], v["far_t"]]))
-    output = jnp.zeros((rows_dev, tok, width), BF16)
-    for k, parts in enumerate((v["results"], v["out_one"], v["out_two"], v["out_three"])):
-        output = place(output, parts, k, 0)
-    v.update(far_h=far_h, there=there, output=output)
+    v.update(far_h=far_h, there=there)
     sync()
 
     parts = summed([v["sums"][0], v["far_h"], v["there"]])
@@ -2121,7 +2088,6 @@
     sync()
 
     tokens_grad = lax.dynamic_update_slice(v["grad"], gathered[1].astype(F32), (0, tok // 2, 0))
-    output = v["output"]
     sums_all = v["vector"][0]
 
     attn_grad = finish(v["attn_sum"], v["attn_other"])

time: 760 us -> 765 us (level)
  Pallas kernels: 370 us -> 387 us
  waiting for transfers between devices: 178 us -> 168 us
    pallas_call x2, Pallas kernels: 34.4 us -> 49.7 us  [attn_bwd(): pl.pallas_call(functools.partial(attn_bwd_kernel, width, hd), grid_spec=p...]
    unnamed x159 -> x178, local copies, waits for them, and re-layouts: 40.1 us -> 55.2 us
    ppermute x22, waiting for transfers between devices: 54.6 us -> 42.3 us  [x_swap(): return lax.ppermute(v, 'fsdp', X_SWAP)]
    dynamic_update_slice x8 -> x0, local copies, waits for them, and re-layouts: 10.8 us -> none  [place(): lax.dynamic_update_slice(out, part.astype(out.dtype)[None], (row, at, 0))]
    ppermute x10 -> x8, starting transfers between devices: 19.9 us -> 15.7 us  [z_down(): return lax.ppermute(v, 'tp', Z_DOWN)]
    ppermute x12 -> x8, waiting for transfers between devices: 19.9 us -> 16.1 us  [z_up(): return lax.ppermute(v, 'tp', Z_UP)]
  transfers between devices with their start and end apart: 100 -> 95, of which waited for: 34 -> 29; matrix products, arithmetic and copies ran while one was open for 7% -> 5% of each run, Pallas kernels for 44% -> 46%
where the time goes in v15:
time: 765 us; the launch traced here: 754 us
  Pallas kernels  387 us (51%)
  waiting for transfers between devices  168 us (22%)
  starting transfers between devices  82.1 us (11%)
  local copies, waits for them, and re-layouts  69.3 us (9%)
  other arithmetic  28.5 us (4%)
  between operations  18.9 us (2%)
    pallas_call x4, Pallas kernels, ffn_bwd(): pl.pallas_call(functools.partial(ffn_bwd_kernel, steps, plan, first), gri...  101 us
    pallas_call x3, Pallas kernels, ffn_fwd(): pl.pallas_call(functools.partial(ffn_fwd_kernel, tile, [plan for plan, _...  60.9 us
    ppermute x19, waiting for transfers between devices, y_swap(): return lax.ppermute(v, 'ctx', Y_SWAP)  56.8 us
    unnamed x178, local copies, waits for them, and re-layouts  55.2 us
    pallas_call x2, Pallas kernels, attn_bwd(): pl.pallas_call(functools.partial(attn_bwd_kernel, width, hd), grid_spec=p...  49.7 us
    ppermute x22, waiting for transfers between devices, x_swap(): return lax.ppermute(v, 'fsdp', X_SWAP)  42.3 us
    pallas_call x2, Pallas kernels, attn_fwd(): pl.pallas_call(functools.partial(attn_fwd_kernel, width, hd), grid_spec=p...  34.1 us
    pallas_call x6, Pallas kernels, sums(): pl.pallas_call(functools.partial(sums_kernel, jobs, len(arrays)), grid_sp...  33.6 us
  transfers between devices with their start and end apart: 95, of which 29 were waited for; matrix products, arithmetic and copies ran while one was open for 5% of the time, Pallas kernels for 46%

profile of v15, /device:TPU:0, one launch (start us, length us, event | category | flops | bytes accessed | tf_op | source)
XLA Modules:
  0.0 754.3 jit_solution(17944936069978397611)
XLA Ops:
  86.7 13.1 %collective-permute-done.15.rest_4_.rest_0_ = bf16[256,1152]{1,0:T(8,128)(2,1)} collective-permute-done((bf16[256,1152]{1,0:T(8,128)(2,1)}, bf16[256,1152]{1,0:T(8,128)(2,1)}, u32[]{:S(2)}, u32[]{:S(2)}) %collective-permute-start.15) | collective-permute-done | bytes 589856 | tf_op jit(solution)/shard_map/ppermute | solution.py:1617
  102.2 17.1 %attn_fwd.2 = (bf16[1024,256]{1,0:T(8,128)(2,1)}, bf16[1024,256]{1,0:T(8,128)(2,1)}, f32[2,2,2048]{2,1,0:T(2,128)}) custom-call(s32[4]{0:T(128)} %copy-done.22, bf16[512,1024]{1,0:T(8,128)(2,1)} %copy-done.29, bf16[512,1024]{1,0:T(8,128)(2,1)} %copy-done.65), custom_call_target="tpu_custom_call" | custom-call | flops 4398046511104 | bytes 1073741824 | tf_op jit(solution)/shard_map/attn_fwd/pallas_call | solution.py:778
  126.3 17.1 %attn_fwd.3 = (bf16[1024,256]{1,0:T(8,128)(2,1)}, bf16[1024,256]{1,0:T(8,128)(2,1)}, f32[2,2,2048]{2,1,0:T(2,128)}) custom-call(s32[4]{0:T(128)} %copy-done.22, bf16[512,1024]{1,0:T(8,128)(2,1)} %copy-done.28, bf16[512,1024]{1,0:T(8,128)(2,1)} %collective-permute-done.17.got_ref), custom_call_target="tpu_custom_call" | custom-call | flops 4398046511104 | bytes 1073741824 | tf_op jit(solution)/shard_map/attn_fwd/pallas_call | solution.py:778
  148.4 13.1 %collective-permute-done.27.refs_8_ = bf16[1024,256]{1,0:T(8,128)(2,1)S(1)} collective-permute-done((bf16[1024,256]{1,0:T(8,128)(2,1)}, bf16[1024,256]{1,0:T(8,128)(2,1)S(1)}, u32[]{:S(2)}, u32[]{:S(2)}) %collective-permute-start.27) | collective-permute-done | bytes 524320 | tf_op jit(solution)/shard_map/ppermute | solution.py:1614
  165.4 10.3 %out_proj.1 = (f32[1024,1024]{1,0:T(8,128)}, bf16[1024,1024]{1,0:T(8,128)(2,1)}, bf16[1024,1024]{1,0:T(8,128)(2,1)}, bf16[4,1024,256]{2,1,0:T(8,128)(2,1)}) custom-call(s32[4]{0:T(128)} %copy-done.22, bf16[1024,256]{1,0:T(8,128)(2,1)} %constant_dynamic-update-slice_fusion.refs_0_, bf16[1024,256]{1,0:T(8,128)(2,1)} %collective-permute-done.25.refs_1_, ...), custom_call_target="tpu_custom_call" | custom-call | flops 4398046511104 | bytes 1073741824 | tf_op jit(solution)/shard_map/out_proj/pallas_call | solution.py:1004
  186.5 27.2 %ffn_fwd.3 = (bf16[2,1024,2304]{2,1,0:T(8,128)(2,1)}, bf16[2,1024,1152]{2,1,0:T(8,128)(2,1)}, f32[1024,1024]{1,0:T(8,128)}) custom-call(s32[4]{0:T(128)} %copy-done.22, f32[1]{0:T(128)} %bitcast.4.scale, bf16[1024,1024]{1,0:T(8,128)(2,1)} %get-tuple-element.1780.x_ref, f32[1024,1024]{1,0:T(8,128)} %get-tuple-element.2338.in_ref.refs_5_, ...), custom_call_target="tpu_custom_call" | custom-call | flops 4398046511104 | bytes 1073741824 | tf_op jit(solution)/shard_map/ffn_fwd/pallas_call | solution.py:1295
  221.1 15.6 %ffn_fwd.4 = (bf16[1,1024,2304]{2,1,0:T(8,128)(2,1)}, bf16[1,1024,1152]{2,1,0:T(8,128)(2,1)}, f32[1024,1024]{1,0:T(8,128)}) custom-call(s32[4]{0:T(128)} %copy-done.22, f32[1]{0:T(128)} %bitcast.4.scale, bf16[1024,1024]{1,0:T(8,128)(2,1)} %get-tuple-element.1780.x_ref, f32[1024,1024]{1,0:T(8,128)} %get-tuple-element.1680.in_ref, ...), custom_call_target="tpu_custom_call" | custom-call | flops 4398046511104 | bytes 1073741824 | tf_op jit(solution)/shard_map/ffn_fwd/pallas_call | solution.py:1295
  240.9 18.1 %ffn_fwd.5 = (bf16[1,1024,2304]{2,1,0:T(8,128)(2,1)}, bf16[1,1024,1152]{2,1,0:T(8,128)(2,1)}, bf16[1024,1024]{1,0:T(8,128)(2,1)}, f32[1024,1024]{1,0:T(8,128)}, ...) custom-call(s32[4]{0:T(128)} %copy-done.22, f32[1]{0:T(128)} %bitcast.4.scale, ...), custom_call_target="tpu_custom_call" | custom-call | flops 4398046511104 | bytes 1073741824 | tf_op jit(solution)/shard_map/ffn_fwd/pallas_call | solution.py:1295
  259.0 24.8 %ffn_bwd.4 = (f32[1024,1024]{1,0:T(8,128)}, bf16[512,3456]{1,0:T(8,128)(2,1)}, bf16[512,3456]{1,0:T(8,128)(2,1)}) custom-call(bf16[1024,1024]{1,0:T(8,128)(2,1)} %get-tuple-element.2267.low_ref, bf16[1,1024,2304]{2,1,0:T(8,128)(2,1)} %get-tuple-element.1904.act_ref, bf16[1,1024,1152]{2,1,0:T(8,128)(2,1)} %get-tuple-element.1924.hid_ref, ...), custom_call_target="tpu_custom_call" | custom-call | flops 12880000000 | bytes 3144531 | tf_op jit(solution)/shard_map/ffn_bwd/pallas_call | solution.py:1377
  284.1 25.7 %ffn_bwd.5 = (f32[1024,1024]{1,0:T(8,128)}, bf16[512,3456]{1,0:T(8,128)(2,1)}, bf16[512,3456]{1,0:T(8,128)(2,1)}) custom-call(bf16[1024,1024]{1,0:T(8,128)(2,1)} %get-tuple-element.2267.low_ref, bf16[2,1024,2304]{2,1,0:T(8,128)(2,1)} %get-tuple-element.2251.act_ref, ...), custom_call_target="tpu_custom_call", output_to_operand_aliasing={{0}: (15, {})} | custom-call | flops 12880000000 | bytes 3144531 | tf_op jit(solution)/shard_map/ffn_bwd/pallas_call | solution.py:1377
  318.0 25.5 %ffn_bwd.6 = (f32[1024,1024]{1,0:T(8,128)}, bf16[512,3456]{1,0:T(8,128)(2,1)}, bf16[512,3456]{1,0:T(8,128)(2,1)}) custom-call(bf16[1024,1024]{1,0:T(8,128)(2,1)} %get-tuple-element.2267.low_ref, bf16[1,1024,2304]{2,1,0:T(8,128)(2,1)} %get-tuple-element.2179.act_ref, ...), custom_call_target="tpu_custom_call", output_to_operand_aliasing={{0}: (17, {})} | custom-call | flops 12880000000 | bytes 3144531 | tf_op jit(solution)/shard_map/ffn_bwd/pallas_call | solution.py:1377
  352.8 25.3 %ffn_bwd.7 = (f32[1024,1024]{1,0:T(8,128)}, bf16[512,3456]{1,0:T(8,128)(2,1)}, bf16[512,3456]{1,0:T(8,128)(2,1)}) custom-call(bf16[1024,1024]{1,0:T(8,128)(2,1)} %get-tuple-element.2267.low_ref, bf16[2,1024,2304]{2,1,0:T(8,128)(2,1)} %get-tuple-element.2251.act_ref, ...), custom_call_target="tpu_custom_call", output_to_operand_aliasing={{0}: (9, {})} | custom-call | flops 12880000000 | bytes 3144531 | tf_op jit(solution)/shard_map/ffn_bwd/pallas_call | solution.py:1377
  387.7 12.5 %norm_two_back.1 = (f32[1024,1024]{1,0:T(8,128)}, bf16[1024,1024]{1,0:T(8,128)(2,1)}, bf16[1024,256]{1,0:T(8,128)(2,1)}, bf16[1024,256]{1,0:T(8,128)(2,1)}, bf16...) custom-call(s32[4]{0:T(128)} %copy-done.22, ...), custom_call_target="tpu_custom_call" | custom-call | flops 6209999872 | bytes 1516113 | tf_op jit(solution)/shard_map/norm_two_back/pallas_call | solution.py:1062
  405.9 9.2 %collective-permute-done.63.gs_ref = bf16[1024,256]{1,0:T(8,128)(2,1)S(1)} collective-permute-done((bf16[1024,256]{1,0:T(8,128)(2,1)}, bf16[1024,256]{1,0:T(8,128)(2,1)S(1)}, u32[]{:S(2)}, u32[]{:S(2)}) %collective-permute-start.63) | collective-permute-done | bytes 524320 | tf_op jit(solution)/shard_map/ppermute | solution.py:1614
  427.6 25.1 %attn_bwd.2 = (bf16[512,1024]{1,0:T(8,128)(2,1)}, bf16[512,1024]{1,0:T(8,128)(2,1)}) custom-call(s32[4]{0:T(128)} %copy-done.22, bf16[512,1024]{1,0:T(8,128)(2,1)} %copy-done.29, bf16[512,1024]{1,0:T(8,128)(2,1)} %copy-done.65, bf16[1024,256]{1,0:T(8,128)(2,1)} %get-tuple-element.2378.refs_5_.ok_ref, bf16[1024,256]{1,0:T(8,128)(2,1)} %get-tuple-element.2379.os_ref, ...), custom_call_target="tpu_custom_call" | custom-call | flops 18630000640 | bytes 4548339 | tf_op jit(solution)/shard_map/attn_bwd/pallas_call | solution.py:939
  452.7 12.1 %collective-permute-done.66.refs_1_ = bf16[128,3456]{1,0:T(8,128)(2,1)S(1)} collective-permute-done((bf16[128,3456]{1,0:T(8,128)(2,1)}, bf16[128,3456]{1,0:T(8,128)(2,1)S(1)}, u32[]{:S(2)}, u32[]{:S(2)}) %collective-permute-start.66) | collective-permute-done | bytes 884768 | tf_op jit(solution)/shard_map/ppermute | solution.py:1608
  474.1 24.6 %attn_bwd.3 = (bf16[512,1024]{1,0:T(8,128)(2,1)}, bf16[512,1024]{1,0:T(8,128)(2,1)}) custom-call(s32[4]{0:T(128)} %copy-done.22, bf16[512,1024]{1,0:T(8,128)(2,1)} %copy-done.28, bf16[512,1024]{1,0:T(8,128)(2,1)} %collective-permute-done.17.got_ref, bf16[1024,256]{1,0:T(8,128)(2,1)} %get-tuple-element.2436.refs_6_.ok_ref, ...), custom_call_target="tpu_custom_call" | custom-call | flops 18630000640 | bytes 4548339 | tf_op jit(solution)/shard_map/attn_bwd/pallas_call | solution.py:939
  498.8 11.2 %collective-permute-done.70.refs_4_ = bf16[128,3456]{1,0:T(8,128)(2,1)} collective-permute-done((bf16[128,3456]{1,0:T(8,128)(2,1)}, bf16[128,3456]{1,0:T(8,128)(2,1)}, u32[]{:S(2)}, u32[]{:S(2)}) %collective-permute-start.70) | collective-permute-done | bytes 884768 | tf_op jit(solution)/shard_map/ppermute | solution.py:1608
  571.1 15.2 %weight_grad.1 = (bf16[4,512,768]{2,1,0:T(8,128)(2,1)}, bf16[4,512,768]{2,1,0:T(8,128)(2,1)}) custom-call(bf16[1024,1024]{1,0:T(8,128)(2,1)} %copy-done, bf16[2,1024,512]{2,1,0:T(8,128)(2,1)} %get-tuple-element.2553.refs_6_.back0_ref, bf16[2,1024,512]{2,1,0:T(8,128)(2,1)} %get-tuple-element.2555.refs_7_.back1_ref, ...), custom_call_target="tpu_custom_call" | custom-call | flops 4398046511104 | bytes 1073741824 | tf_op jit(solution)/shard_map/weight_grad/pallas_call | solution.py:1560
  607.0 11.9 %collective-permute-done.81.refs_1_ = bf16[512,768]{1,0:T(8,128)(2,1)} collective-permute-done((bf16[512,768]{1,0:T(8,128)(2,1)S(1)}, bf16[512,768]{1,0:T(8,128)(2,1)}, u32[]{:S(2)}, u32[]{:S(2)}) %collective-permute-start.81) | collective-permute-done | bytes 786464 | tf_op jit(solution)/shard_map/ppermute | solution.py:1608
  624.3 17.4 %collective-permute-done.84.refs_2_ = bf16[512,768]{1,0:T(8,128)(2,1)S(1)} collective-permute-done((bf16[512,768]{1,0:T(8,128)(2,1)}, bf16[512,768]{1,0:T(8,128)(2,1)S(1)}, u32[]{:S(2)}, u32[]{:S(2)}) %collective-permute-start.84) | collective-permute-done | bytes 786464 | tf_op jit(solution)/shard_map/ppermute | solution.py:1614
  653.1 10.4 %collective-permute-done.85.refs_1_ = bf16[128,768]{1,0:T(8,128)(2,1)S(1)} collective-permute-done((bf16[128,768]{1,0:T(8,128)(2,1)S(1)}, bf16[128,768]{1,0:T(8,128)(2,1)S(1)}, u32[]{:S(2)}, u32[]{:S(2)}) %collective-permute-start.85) | collective-permute-done | bytes 196640 | tf_op jit(solution)/shard_map/ppermute | solution.py:1623
  663.5 26.2 %collective-permute-done.86.refs_2_ = bf16[128,768]{1,0:T(8,128)(2,1)S(1)} collective-permute-done((bf16[128,768]{1,0:T(8,128)(2,1)S(1)}, bf16[128,768]{1,0:T(8,128)(2,1)S(1)}, u32[]{:S(2)}, u32[]{:S(2)}) %collective-permute-start.86) | collective-permute-done | bytes 196640 | tf_op jit(solution)/shard_map/ppermute | solution.py:1620
  693.7 10.6 %pad_convert_fusion = f32[4,1024,1024]{2,1,0:T(8,128)} fusion(bf16[4,512,1024]{2,1,0:T(8,128)(2,1)} %bitcast.51), kind=kLoop, calls=%fused_computation.1 | loop fusion | flops 4194304 | bytes 20971520 | tf_op jit(solution)/shard_map/dynamic_update_slice | solution.py:2085
  (448 shorter events, 316.1 us)
Async XLA Ops:
  7.2 463.6 %all-gather.7.cloned.1.call-start = ((), (), s32[]{:S(2)}) async-start(), calls=%async_computation | async-start | bytes 10485760 | tf_op jit(solution)/shard_map/all_gather | solution.py:1845
  56.5 43.3 %collective-permute-start.11 = (bf16[256,3456]{1,0:T(8,128)(2,1)}, bf16[256,3456]{1,0:T(8,128)(2,1)}, u32[]{:S(2)}, u32[]{:S(2)}) collective-permute-start(bf16[256,3456]{1,0:T(8,128)(2,1)} %get-tuple-element.2272.rest_0_), channel_id=1, source_target_pairs={{0,16},{16,0},{8,24},{24,8},{1,17},{17,1},{9,25},{25,9},{2,18},{18... | collective-permute-start | bytes 5308424 | tf_op jit(solution)/shard_map/ppermute | solution.py:1608
  57.4 42.4 %collective-permute-start.16 = (bf16[256,2304]{1,0:T(8,128)(2,1)}, bf16[256,2304]{1,0:T(8,128)(2,1)}, u32[]{:S(2)}, u32[]{:S(2)}) collective-permute-start(bf16[256,2304]{1,0:T(8,128)(2,1)} %get-tuple-element.1366), channel_id=1, source_target_pairs={{0,1},{1,2},{2,3},{3,0},{4,5},{5,6},{6,7},{7,4},{8,9},{9,10},{10,1... | collective-permute-start | bytes 3538952 | tf_op jit(solution)/shard_map/ppermute | solution.py:1617
  75.5 43.7 %collective-permute-start.17 = (bf16[512,1024]{1,0:T(8,128)(2,1)}, bf16[512,1024]{1,0:T(8,128)(2,1)}, u32[]{:S(2)}, u32[]{:S(2)}) collective-permute-start(bf16[512,1024]{1,0:T(8,128)(2,1)} %get-tuple-element.1358), channel_id=1, source_target_pairs={{0,4},{4,0},{1,5},{5,1},{2,6},{6,2},{3,7},{7,3},{8,12},{12,8},{9,1... | collective-permute-start | bytes 3145736 | tf_op jit(solution)/shard_map/ppermute | solution.py:1614
  181.7 32.1 %collective-permute-start.41 = (bf16[256,2304]{1,0:T(8,128)(2,1)}, bf16[256,2304]{1,0:T(8,128)(2,1)}, u32[]{:S(2)}, u32[]{:S(2)}) collective-permute-start(bf16[256,2304]{1,0:T(8,128)(2,1)} %collective-permute-done.16.rest_5_.rest_1_), channel_id=1, source_target_pairs={{0,1},{1,2},{2,3},{3,0},{4,5},{5,6},{6,7},{7,4},{8,9},{9,10},{10,1... | collective-permute-start | bytes 3538952 | tf_op jit(solution)/shard_map/ppermute | solution.py:1617
  181.7 32.0 %collective-permute-start.38 = (bf16[256,1152]{1,0:T(8,128)(2,1)}, bf16[256,1152]{1,0:T(8,128)(2,1)}, u32[]{:S(2)}, u32[]{:S(2)}) collective-permute-start(bf16[256,1152]{1,0:T(8,128)(2,1)} %collective-permute-done.21.rest_0_), channel_id=1, source_target_pairs={{0,8},{8,0},{16,24},{24,16},{1,9},{9,1},{17,25},{25,17},{2,10},{10... | collective-permute-start | bytes 1769480 | tf_op jit(solution)/shard_map/ppermute | solution.py:1611
  182.2 31.5 %collective-permute-start.39 = (bf16[256,1152]{1,0:T(8,128)(2,1)}, bf16[256,1152]{1,0:T(8,128)(2,1)}, u32[]{:S(2)}, u32[]{:S(2)}) collective-permute-start(bf16[256,1152]{1,0:T(8,128)(2,1)} %collective-permute-done.26.rest_1_), channel_id=1, source_target_pairs={{0,16},{16,0},{8,24},{24,8},{1,17},{17,1},{9,25},{25,9},{2,18},{18... | collective-permute-start | bytes 1769480 | tf_op jit(solution)/shard_map/ppermute | solution.py:1608
  182.8 31.0 %collective-permute-start.40 = (bf16[256,1152]{1,0:T(8,128)(2,1)}, bf16[256,1152]{1,0:T(8,128)(2,1)}, u32[]{:S(2)}, u32[]{:S(2)}) collective-permute-start(bf16[256,1152]{1,0:T(8,128)(2,1)} %collective-permute-done.35.rest_3_), channel_id=1, source_target_pairs={{0,4},{4,0},{1,5},{5,1},{2,6},{6,2},{3,7},{7,3},{8,12},{12,8},{9,1... | collective-permute-start | bytes 1769480 | tf_op jit(solution)/shard_map/ppermute | solution.py:1614
  284.0 409.6 %all-gather.9.cloned.1.call-start = ((), (), s32[]{:S(2)}) async-start(), calls=%async_computation.1 | async-start | bytes 5242880 | tf_op jit(solution)/shard_map/all_gather | solution.py:2002
  309.8 33.7 %collective-permute-start.56 = (bf16[512,3456]{1,0:T(8,128)(2,1)}, bf16[512,3456]{1,0:T(8,128)(2,1)}, u32[]{:S(2)}, u32[]{:S(2)}) collective-permute-start(bf16[512,3456]{1,0:T(8,128)(2,1)} %get-tuple-element.2181), channel_id=1, source_target_pairs={{0,8},{8,0},{16,24},{24,16},{1,9},{9,1},{17,25},{25,17},{2,10},{10... | collective-permute-start | bytes 10616840 | tf_op jit(solution)/shard_map/ppermute | solution.py:1611
  344.4 33.7 %collective-permute-start.58 = (bf16[512,3456]{1,0:T(8,128)(2,1)}, bf16[512,3456]{1,0:T(8,128)(2,1)S(1)}, u32[]{:S(2)}, u32[]{:S(2)}) collective-permute-start(bf16[512,3456]{1,0:T(8,128)(2,1)} %get-tuple-element.2254), channel_id=1, source_target_pairs={{0,8},{8,0},{16,24},{24,16},{1,9},{9,1},{17,25},{25,17},{2,10},{10... | collective-permute-start | bytes 10616840 | tf_op jit(solution)/shard_map/ppermute | solution.py:1611
  379.9 35.3 %collective-permute-start.61 = (bf16[512,3456]{1,0:T(8,128)(2,1)}, bf16[512,3456]{1,0:T(8,128)(2,1)S(1)}, u32[]{:S(2)}, u32[]{:S(2)}) collective-permute-start(bf16[512,3456]{1,0:T(8,128)(2,1)} %get-tuple-element.2316), channel_id=1, source_target_pairs={{0,8},{8,0},{16,24},{24,16},{1,9},{9,1},{17,25},{25,17},{2,10},{10... | collective-permute-start | bytes 10616840 | tf_op jit(solution)/shard_map/ppermute | solution.py:1611
  401.6 51.1 %collective-permute-start.67 = (bf16[1024,256]{1,0:T(8,128)(2,1)}, bf16[1024,256]{1,0:T(8,128)(2,1)S(1)}, u32[]{:S(2)}, u32[]{:S(2)}) collective-permute-start(bf16[1024,256]{1,0:T(8,128)(2,1)} %get-tuple-element.2401), channel_id=1, source_target_pairs={{0,4},{4,0},{1,5},{5,1},{2,6},{6,2},{3,7},{7,3},{8,12},{12,8},{9,1... | collective-permute-start | bytes 1572872 | tf_op jit(solution)/shard_map/ppermute | solution.py:1614
  402.2 50.4 %collective-permute-start.64 = (bf16[128,3456]{1,0:T(8,128)(2,1)}, bf16[128,3456]{1,0:T(8,128)(2,1)}, u32[]{:S(2)}, u32[]{:S(2)}) collective-permute-start(bf16[128,3456]{1,0:T(8,128)(2,1)} %get-tuple-element.2392), channel_id=1, source_target_pairs={{0,3},{1,0},{2,1},{3,2},{4,7},{5,4},{6,5},{7,6},{8,11},{9,8},{10,9... | collective-permute-start | bytes 2654216 | tf_op jit(solution)/shard_map/ppermute | solution.py:1623
  426.9 37.9 %collective-permute-start.66 = (bf16[128,3456]{1,0:T(8,128)(2,1)}, bf16[128,3456]{1,0:T(8,128)(2,1)S(1)}, u32[]{:S(2)}, u32[]{:S(2)}) collective-permute-start(bf16[128,3456]{1,0:T(8,128)(2,1)} %get-tuple-element.2394), channel_id=1, source_target_pairs={{0,16},{16,0},{8,24},{24,8},{1,17},{17,1},{9,25},{25,9},{2,18},{18... | collective-permute-start | bytes 2654216 | tf_op jit(solution)/shard_map/ppermute | solution.py:1608
  470.8 41.5 %collective-permute-start.71 = (bf16[512,1024]{1,0:T(8,128)(2,1)}, bf16[512,1024]{1,0:T(8,128)(2,1)S(1)}, u32[]{:S(2)}, u32[]{:S(2)}) collective-permute-start(bf16[512,1024]{1,0:T(8,128)(2,1)} %get-tuple-element.2433), channel_id=1, source_target_pairs={{0,4},{4,0},{1,5},{5,1},{2,6},{6,2},{3,7},{7,3},{8,12},{12,8},{9,1... | collective-permute-start | bytes 3145736 | tf_op jit(solution)/shard_map/ppermute | solution.py:1614
  473.5 36.5 %collective-permute-start.70 = (bf16[128,3456]{1,0:T(8,128)(2,1)}, bf16[128,3456]{1,0:T(8,128)(2,1)}, u32[]{:S(2)}, u32[]{:S(2)}) collective-permute-start(bf16[128,3456]{1,0:T(8,128)(2,1)} %get-tuple-element.2454), channel_id=1, source_target_pairs={{0,16},{16,0},{8,24},{24,8},{1,17},{17,1},{9,25},{25,9},{2,18},{18... | collective-permute-start | bytes 2654216 | tf_op jit(solution)/shard_map/ppermute | solution.py:1608
  512.9 48.3 %collective-permute-start.76 = (bf16[128,3456]{1,0:T(8,128)(2,1)}, bf16[128,3456]{1,0:T(8,128)(2,1)}, u32[]{:S(2)}, u32[]{:S(2)}) collective-permute-start(bf16[128,3456]{1,0:T(8,128)(2,1)} %get-tuple-element.2446), channel_id=1, source_target_pairs={{0,3},{1,0},{2,1},{3,2},{4,7},{5,4},{6,5},{7,6},{8,11},{9,8},{10,9... | collective-permute-start | bytes 2654216 | tf_op jit(solution)/shard_map/ppermute | solution.py:1623
  522.1 39.1 %collective-permute-start.77 = (bf16[128,3456]{1,0:T(8,128)(2,1)}, bf16[128,3456]{1,0:T(8,128)(2,1)}, u32[]{:S(2)}, u32[]{:S(2)}) collective-permute-start(bf16[128,3456]{1,0:T(8,128)(2,1)} %get-tuple-element.2547), channel_id=1, source_target_pairs={{0,1},{1,2},{2,3},{3,0},{4,5},{5,6},{6,7},{7,4},{8,9},{9,10},{10,1... | collective-permute-start | bytes 2654216 | tf_op jit(solution)/shard_map/ppermute | solution.py:1617
  522.1 39.1 %collective-permute-start.74 = (bf16[128,3456]{1,0:T(8,128)(2,1)}, bf16[128,3456]{1,0:T(8,128)(2,1)}, u32[]{:S(2)}, u32[]{:S(2)}) collective-permute-start(bf16[128,3456]{1,0:T(8,128)(2,1)} %get-tuple-element.2504), channel_id=1, source_target_pairs={{0,16},{16,0},{8,24},{24,8},{1,17},{17,1},{9,25},{25,9},{2,18},{18... | collective-permute-start | bytes 2654216 | tf_op jit(solution)/shard_map/ppermute | solution.py:1608
  550.7 178.9 %all-gather.11.cloned.1.call-start = ((), (), s32[]{:S(2)}) async-start(), calls=%async_computation.2 | async-start | bytes 5242880 | tf_op jit(solution)/shard_map/all_gather | solution.py:2008
  642.0 62.2 %collective-permute-start.88 = (f32[128,3456]{1,0:T(8,128)S(1)}, f32[128,3456]{1,0:T(8,128)}, u32[]{:S(2)}, u32[]{:S(2)}) collective-permute-start(f32[128,3456]{1,0:T(8,128)S(1)} %copy-done.32), channel_id=1, source_target_pairs={{0,4},{4,0},{1,5},{5,1},{2,6},{6,2},{3,7},{7,3},{8,12},{12,8},{9,1... | collective-permute-start | bytes 5308424 | tf_op jit(solution)/shard_map/ppermute | solution.py:1614
  652.3 37.4 %collective-permute-start.86 = (bf16[128,768]{1,0:T(8,128)(2,1)S(1)}, bf16[128,768]{1,0:T(8,128)(2,1)S(1)}, u32[]{:S(2)}, u32[]{:S(2)}) collective-permute-start(bf16[128,768]{1,0:T(8,128)(2,1)S(1)} %get-tuple-element.2671), channel_id=1, source_target_pairs={{0,2},{2,0},{1,3},{3,1},{4,6},{6,4},{5,7},{7,5},{8,10},{10,8},{9,1... | collective-permute-start | bytes 589832 | tf_op jit(solution)/shard_map/ppermute | solution.py:1620
  652.4 37.4 %collective-permute-start.87 = (bf16[128,768]{1,0:T(8,128)(2,1)S(1)}, bf16[128,768]{1,0:T(8,128)(2,1)S(1)}, u32[]{:S(2)}, u32[]{:S(2)}) collective-permute-start(bf16[128,768]{1,0:T(8,128)(2,1)S(1)} %get-tuple-element.2670), channel_id=1, source_target_pairs={{0,1},{1,2},{2,3},{3,0},{4,5},{5,6},{6,7},{7,4},{8,9},{9,10},{10,1... | collective-permute-start | bytes 589832 | tf_op jit(solution)/shard_map/ppermute | solution.py:1617
  (152 other events, 1943.9 us)
Sparse Core Ops, SparseCore 0:
  284.2 165.8 all-gather.6
  550.9 80.7 all-gather.8
  633.3 96.2 all-gather.10

commit v16 on v15

--- a/solution.py
+++ b/solution.py
@@ -2042,7 +2042,11 @@
 
     far_h = x_swap(v["sums"][2])
     there = y_swap(summed([v["sums"][1], v["far_t"]]))
-    v.update(far_h=far_h, there=there)
+    spread = jnp.zeros((rows_dev, tok, width), BF16)
+    for j in range(2):
+        part = output[:, j * tok // 2 : (j + 1) * tok // 2]
+        spread = lax.dynamic_update_slice(spread, part, (0, j * tok // 2, 0))
+    v.update(far_h=far_h, there=there, spread=spread)
     sync()
 
     parts = summed([v["sums"][0], v["far_h"], v["there"]])
@@ -2097,7 +2101,7 @@
         return lax.dynamic_slice_in_dim(sums_all, at + fsdp * (size // 4), size // 4, 0)
 
     return (
-        output,
+        v["spread"],
         teacher_loss,
         tokens_grad,
         own_part(0, width),

time: 765 us -> 764 us (level)
  no operation moved by 1% of the time
where the time goes in v16:
time: 764 us; the launch traced here: 753 us
  Pallas kernels  387 us (51%)
  waiting for transfers between devices  165 us (22%)
  starting transfers between devices  83.8 us (11%)
  local copies, waits for them, and re-layouts  69.3 us (9%)
  other arithmetic  28.5 us (4%)
  between operations  19.1 us (3%)
    pallas_call x4, Pallas kernels, ffn_bwd(): pl.pallas_call(functools.partial(ffn_bwd_kernel, steps, plan, first), gri...  101 us
    pallas_call x3, Pallas kernels, ffn_fwd(): pl.pallas_call(functools.partial(ffn_fwd_kernel, tile, [plan for plan, _...  61 us
    unnamed x178, local copies, waits for them, and re-layouts  55.2 us
    ppermute x19, waiting for transfers between devices, y_swap(): return lax.ppermute(v, 'ctx', Y_SWAP)  53.7 us
    pallas_call x2, Pallas kernels, attn_bwd(): pl.pallas_call(functools.partial(attn_bwd_kernel, width, hd), grid_spec=p...  49.7 us
    ppermute x22, waiting for transfers between devices, x_swap(): return lax.ppermute(v, 'fsdp', X_SWAP)  42.5 us
    pallas_call x2, Pallas kernels, attn_fwd(): pl.pallas_call(functools.partial(attn_fwd_kernel, width, hd), grid_spec=p...  34.1 us
    pallas_call x6, Pallas kernels, sums(): pl.pallas_call(functools.partial(sums_kernel, jobs, len(arrays)), grid_sp...  33.6 us
  transfers between devices with their start and end apart: 95, of which 29 were waited for; matrix products, arithmetic and copies ran while one was open for 5% of the time, Pallas kernels for 46%

profile of v16, /device:TPU:0, one launch (start us, length us, event | category | flops | bytes accessed | tf_op | source)
XLA Modules:
  0.0 753.2 jit_solution(8632573909268551663)
XLA Ops:
  86.8 13.0 %collective-permute-done.15.rest_4_.rest_0_ = bf16[256,1152]{1,0:T(8,128)(2,1)} collective-permute-done((bf16[256,1152]{1,0:T(8,128)(2,1)}, bf16[256,1152]{1,0:T(8,128)(2,1)}, u32[]{:S(2)}, u32[]{:S(2)}) %collective-permute-start.15) | collective-permute-done | bytes 589856 | tf_op jit(solution)/shard_map/ppermute | solution.py:1617
  102.2 17.1 %attn_fwd.2 = (bf16[1024,256]{1,0:T(8,128)(2,1)}, bf16[1024,256]{1,0:T(8,128)(2,1)}, f32[2,2,2048]{2,1,0:T(2,128)}) custom-call(s32[4]{0:T(128)} %copy-done.22, bf16[512,1024]{1,0:T(8,128)(2,1)} %copy-done.29, bf16[512,1024]{1,0:T(8,128)(2,1)} %copy-done.65), custom_call_target="tpu_custom_call" | custom-call | flops 4398046511104 | bytes 1073741824 | tf_op jit(solution)/shard_map/attn_fwd/pallas_call | solution.py:778
  126.3 17.1 %attn_fwd.3 = (bf16[1024,256]{1,0:T(8,128)(2,1)}, bf16[1024,256]{1,0:T(8,128)(2,1)}, f32[2,2,2048]{2,1,0:T(2,128)}) custom-call(s32[4]{0:T(128)} %copy-done.22, bf16[512,1024]{1,0:T(8,128)(2,1)} %copy-done.28, bf16[512,1024]{1,0:T(8,128)(2,1)} %collective-permute-done.17.got_ref), custom_call_target="tpu_custom_call" | custom-call | flops 4398046511104 | bytes 1073741824 | tf_op jit(solution)/shard_map/attn_fwd/pallas_call | solution.py:778
  149.1 11.1 %collective-permute-done.27.refs_8_ = bf16[1024,256]{1,0:T(8,128)(2,1)S(1)} collective-permute-done((bf16[1024,256]{1,0:T(8,128)(2,1)}, bf16[1024,256]{1,0:T(8,128)(2,1)S(1)}, u32[]{:S(2)}, u32[]{:S(2)}) %collective-permute-start.27) | collective-permute-done | bytes 524320 | tf_op jit(solution)/shard_map/ppermute | solution.py:1614
  165.4 10.3 %out_proj.1 = (f32[1024,1024]{1,0:T(8,128)}, bf16[1024,1024]{1,0:T(8,128)(2,1)}, bf16[1024,1024]{1,0:T(8,128)(2,1)}, bf16[4,1024,256]{2,1,0:T(8,128)(2,1)}) custom-call(s32[4]{0:T(128)} %copy-done.22, bf16[1024,256]{1,0:T(8,128)(2,1)} %constant_dynamic-update-slice_fusion.refs_0_, bf16[1024,256]{1,0:T(8,128)(2,1)} %collective-permute-done.25.refs_1_, ...), custom_call_target="tpu_custom_call" | custom-call | flops 4398046511104 | bytes 1073741824 | tf_op jit(solution)/shard_map/out_proj/pallas_call | solution.py:1004
  185.4 27.2 %ffn_fwd.3 = (bf16[2,1024,2304]{2,1,0:T(8,128)(2,1)}, bf16[2,1024,1152]{2,1,0:T(8,128)(2,1)}, f32[1024,1024]{1,0:T(8,128)}) custom-call(s32[4]{0:T(128)} %copy-done.22, f32[1]{0:T(128)} %bitcast.4.scale, bf16[1024,1024]{1,0:T(8,128)(2,1)} %get-tuple-element.1784.x_ref, f32[1024,1024]{1,0:T(8,128)} %get-tuple-element.2342.in_ref.refs_5_, ...), custom_call_target="tpu_custom_call" | custom-call | flops 4398046511104 | bytes 1073741824 | tf_op jit(solution)/shard_map/ffn_fwd/pallas_call | solution.py:1295
  220.0 15.6 %ffn_fwd.4 = (bf16[1,1024,2304]{2,1,0:T(8,128)(2,1)}, bf16[1,1024,1152]{2,1,0:T(8,128)(2,1)}, f32[1024,1024]{1,0:T(8,128)}) custom-call(s32[4]{0:T(128)} %copy-done.22, f32[1]{0:T(128)} %bitcast.4.scale, bf16[1024,1024]{1,0:T(8,128)(2,1)} %get-tuple-element.1784.x_ref, f32[1024,1024]{1,0:T(8,128)} %get-tuple-element.1684.in_ref, ...), custom_call_target="tpu_custom_call" | custom-call | flops 4398046511104 | bytes 1073741824 | tf_op jit(solution)/shard_map/ffn_fwd/pallas_call | solution.py:1295
  239.7 18.1 %ffn_fwd.5 = (bf16[1,1024,2304]{2,1,0:T(8,128)(2,1)}, bf16[1,1024,1152]{2,1,0:T(8,128)(2,1)}, bf16[1024,1024]{1,0:T(8,128)(2,1)}, f32[1024,1024]{1,0:T(8,128)}, ...) custom-call(s32[4]{0:T(128)} %copy-done.22, f32[1]{0:T(128)} %bitcast.4.scale, ...), custom_call_target="tpu_custom_call" | custom-call | flops 4398046511104 | bytes 1073741824 | tf_op jit(solution)/shard_map/ffn_fwd/pallas_call | solution.py:1295
  257.8 24.8 %ffn_bwd.4 = (f32[1024,1024]{1,0:T(8,128)}, bf16[512,3456]{1,0:T(8,128)(2,1)}, bf16[512,3456]{1,0:T(8,128)(2,1)}) custom-call(bf16[1024,1024]{1,0:T(8,128)(2,1)} %get-tuple-element.2271.low_ref, bf16[1,1024,2304]{2,1,0:T(8,128)(2,1)} %get-tuple-element.1907.act_ref, bf16[1,1024,1152]{2,1,0:T(8,128)(2,1)} %get-tuple-element.1927.hid_ref, ...), custom_call_target="tpu_custom_call" | custom-call | flops 12880000000 | bytes 3144531 | tf_op jit(solution)/shard_map/ffn_bwd/pallas_call | solution.py:1377
  282.9 25.7 %ffn_bwd.5 = (f32[1024,1024]{1,0:T(8,128)}, bf16[512,3456]{1,0:T(8,128)(2,1)}, bf16[512,3456]{1,0:T(8,128)(2,1)}) custom-call(bf16[1024,1024]{1,0:T(8,128)(2,1)} %get-tuple-element.2271.low_ref, bf16[2,1024,2304]{2,1,0:T(8,128)(2,1)} %get-tuple-element.2255.act_ref, ...), custom_call_target="tpu_custom_call", output_to_operand_aliasing={{0}: (15, {})} | custom-call | flops 12880000000 | bytes 3144531 | tf_op jit(solution)/shard_map/ffn_bwd/pallas_call | solution.py:1377
  316.8 25.5 %ffn_bwd.6 = (f32[1024,1024]{1,0:T(8,128)}, bf16[512,3456]{1,0:T(8,128)(2,1)}, bf16[512,3456]{1,0:T(8,128)(2,1)}) custom-call(bf16[1024,1024]{1,0:T(8,128)(2,1)} %get-tuple-element.2271.low_ref, bf16[1,1024,2304]{2,1,0:T(8,128)(2,1)} %get-tuple-element.2183.act_ref, ...), custom_call_target="tpu_custom_call", output_to_operand_aliasing={{0}: (17, {})} | custom-call | flops 12880000000 | bytes 3144531 | tf_op jit(solution)/shard_map/ffn_bwd/pallas_call | solution.py:1377
  351.6 25.3 %ffn_bwd.7 = (f32[1024,1024]{1,0:T(8,128)}, bf16[512,3456]{1,0:T(8,128)(2,1)}, bf16[512,3456]{1,0:T(8,128)(2,1)}) custom-call(bf16[1024,1024]{1,0:T(8,128)(2,1)} %get-tuple-element.2271.low_ref, bf16[2,1024,2304]{2,1,0:T(8,128)(2,1)} %get-tuple-element.2255.act_ref, ...), custom_call_target="tpu_custom_call", output_to_operand_aliasing={{0}: (9, {})} | custom-call | flops 12880000000 | bytes 3144531 | tf_op jit(solution)/shard_map/ffn_bwd/pallas_call | solution.py:1377
  386.5 12.5 %norm_two_back.1 = (f32[1024,1024]{1,0:T(8,128)}, bf16[1024,1024]{1,0:T(8,128)(2,1)}, bf16[1024,256]{1,0:T(8,128)(2,1)}, bf16[1024,256]{1,0:T(8,128)(2,1)}, bf16...) custom-call(s32[4]{0:T(128)} %copy-done.22, ...), custom_call_target="tpu_custom_call" | custom-call | flops 6209999872 | bytes 1516113 | tf_op jit(solution)/shard_map/norm_two_back/pallas_call | solution.py:1062
  404.8 9.2 %collective-permute-done.63.gs_ref = bf16[1024,256]{1,0:T(8,128)(2,1)S(1)} collective-permute-done((bf16[1024,256]{1,0:T(8,128)(2,1)}, bf16[1024,256]{1,0:T(8,128)(2,1)S(1)}, u32[]{:S(2)}, u32[]{:S(2)}) %collective-permute-start.63) | collective-permute-done | bytes 524320 | tf_op jit(solution)/shard_map/ppermute | solution.py:1614
  426.4 25.1 %attn_bwd.2 = (bf16[512,1024]{1,0:T(8,128)(2,1)}, bf16[512,1024]{1,0:T(8,128)(2,1)}) custom-call(s32[4]{0:T(128)} %copy-done.22, bf16[512,1024]{1,0:T(8,128)(2,1)} %copy-done.29, bf16[512,1024]{1,0:T(8,128)(2,1)} %copy-done.65, bf16[1024,256]{1,0:T(8,128)(2,1)} %get-tuple-element.2382.refs_5_.ok_ref, bf16[1024,256]{1,0:T(8,128)(2,1)} %get-tuple-element.2383.os_ref, ...), custom_call_target="tpu_custom_call" | custom-call | flops 18630000640 | bytes 4548339 | tf_op jit(solution)/shard_map/attn_bwd/pallas_call | solution.py:939
  451.5 12.1 %collective-permute-done.66.refs_1_ = bf16[128,3456]{1,0:T(8,128)(2,1)S(1)} collective-permute-done((bf16[128,3456]{1,0:T(8,128)(2,1)}, bf16[128,3456]{1,0:T(8,128)(2,1)S(1)}, u32[]{:S(2)}, u32[]{:S(2)}) %collective-permute-start.66) | collective-permute-done | bytes 884768 | tf_op jit(solution)/shard_map/ppermute | solution.py:1608
  473.0 24.6 %attn_bwd.3 = (bf16[512,1024]{1,0:T(8,128)(2,1)}, bf16[512,1024]{1,0:T(8,128)(2,1)}) custom-call(s32[4]{0:T(128)} %copy-done.22, bf16[512,1024]{1,0:T(8,128)(2,1)} %copy-done.28, bf16[512,1024]{1,0:T(8,128)(2,1)} %collective-permute-done.17.got_ref, bf16[1024,256]{1,0:T(8,128)(2,1)} %get-tuple-element.2440.refs_6_.ok_ref, ...), custom_call_target="tpu_custom_call" | custom-call | flops 18630000640 | bytes 4548339 | tf_op jit(solution)/shard_map/attn_bwd/pallas_call | solution.py:939
  497.7 11.2 %collective-permute-done.70.refs_4_ = bf16[128,3456]{1,0:T(8,128)(2,1)} collective-permute-done((bf16[128,3456]{1,0:T(8,128)(2,1)}, bf16[128,3456]{1,0:T(8,128)(2,1)}, u32[]{:S(2)}, u32[]{:S(2)}) %collective-permute-start.70) | collective-permute-done | bytes 884768 | tf_op jit(solution)/shard_map/ppermute | solution.py:1608
  569.9 15.2 %weight_grad.1 = (bf16[4,512,768]{2,1,0:T(8,128)(2,1)}, bf16[4,512,768]{2,1,0:T(8,128)(2,1)}) custom-call(bf16[1024,1024]{1,0:T(8,128)(2,1)} %copy-done, bf16[2,1024,512]{2,1,0:T(8,128)(2,1)} %get-tuple-element.2557.refs_6_.back0_ref, bf16[2,1024,512]{2,1,0:T(8,128)(2,1)} %get-tuple-element.2559.refs_7_.back1_ref, ...), custom_call_target="tpu_custom_call" | custom-call | flops 4398046511104 | bytes 1073741824 | tf_op jit(solution)/shard_map/weight_grad/pallas_call | solution.py:1560
  605.7 12.1 %collective-permute-done.81.refs_1_ = bf16[512,768]{1,0:T(8,128)(2,1)} collective-permute-done((bf16[512,768]{1,0:T(8,128)(2,1)S(1)}, bf16[512,768]{1,0:T(8,128)(2,1)}, u32[]{:S(2)}, u32[]{:S(2)}) %collective-permute-start.81) | collective-permute-done | bytes 786464 | tf_op jit(solution)/shard_map/ppermute | solution.py:1608
  623.1 17.4 %collective-permute-done.84.refs_2_ = bf16[512,768]{1,0:T(8,128)(2,1)S(1)} collective-permute-done((bf16[512,768]{1,0:T(8,128)(2,1)}, bf16[512,768]{1,0:T(8,128)(2,1)S(1)}, u32[]{:S(2)}, u32[]{:S(2)}) %collective-permute-start.84) | collective-permute-done | bytes 786464 | tf_op jit(solution)/shard_map/ppermute | solution.py:1614
  651.9 10.5 %collective-permute-done.85.refs_1_ = bf16[128,768]{1,0:T(8,128)(2,1)S(1)} collective-permute-done((bf16[128,768]{1,0:T(8,128)(2,1)S(1)}, bf16[128,768]{1,0:T(8,128)(2,1)S(1)}, u32[]{:S(2)}, u32[]{:S(2)}) %collective-permute-start.85) | collective-permute-done | bytes 196640 | tf_op jit(solution)/shard_map/ppermute | solution.py:1623
  662.4 26.3 %collective-permute-done.86.refs_2_ = bf16[128,768]{1,0:T(8,128)(2,1)S(1)} collective-permute-done((bf16[128,768]{1,0:T(8,128)(2,1)S(1)}, bf16[128,768]{1,0:T(8,128)(2,1)S(1)}, u32[]{:S(2)}, u32[]{:S(2)}) %collective-permute-start.86) | collective-permute-done | bytes 196640 | tf_op jit(solution)/shard_map/ppermute | solution.py:1620
  692.7 10.6 %pad_convert_fusion = f32[4,1024,1024]{2,1,0:T(8,128)} fusion(bf16[4,512,1024]{2,1,0:T(8,128)(2,1)} %bitcast.51), kind=kLoop, calls=%fused_computation.1 | loop fusion | flops 4194304 | bytes 20971520 | tf_op jit(solution)/shard_map/dynamic_update_slice | solution.py:2089
  (448 shorter events, 316.5 us)
Async XLA Ops:
  7.2 462.4 %all-gather.7.cloned.1.call-start = ((), (), s32[]{:S(2)}) async-start(), calls=%async_computation | async-start | bytes 10485760 | tf_op jit(solution)/shard_map/all_gather | solution.py:1845
  56.5 43.3 %collective-permute-start.11 = (bf16[256,3456]{1,0:T(8,128)(2,1)}, bf16[256,3456]{1,0:T(8,128)(2,1)}, u32[]{:S(2)}, u32[]{:S(2)}) collective-permute-start(bf16[256,3456]{1,0:T(8,128)(2,1)} %get-tuple-element.2276.rest_0_), channel_id=1, source_target_pairs={{0,16},{16,0},{8,24},{24,8},{1,17},{17,1},{9,25},{25,9},{2,18},{18... | collective-permute-start | bytes 5308424 | tf_op jit(solution)/shard_map/ppermute | solution.py:1608
  57.4 42.4 %collective-permute-start.16 = (bf16[256,2304]{1,0:T(8,128)(2,1)}, bf16[256,2304]{1,0:T(8,128)(2,1)}, u32[]{:S(2)}, u32[]{:S(2)}) collective-permute-start(bf16[256,2304]{1,0:T(8,128)(2,1)} %get-tuple-element.1370), channel_id=1, source_target_pairs={{0,1},{1,2},{2,3},{3,0},{4,5},{5,6},{6,7},{7,4},{8,9},{9,10},{10,1... | collective-permute-start | bytes 3538952 | tf_op jit(solution)/shard_map/ppermute | solution.py:1617
  75.5 43.7 %collective-permute-start.17 = (bf16[512,1024]{1,0:T(8,128)(2,1)}, bf16[512,1024]{1,0:T(8,128)(2,1)}, u32[]{:S(2)}, u32[]{:S(2)}) collective-permute-start(bf16[512,1024]{1,0:T(8,128)(2,1)} %get-tuple-element.1362), channel_id=1, source_target_pairs={{0,4},{4,0},{1,5},{5,1},{2,6},{6,2},{3,7},{7,3},{8,12},{12,8},{9,1... | collective-permute-start | bytes 3145736 | tf_op jit(solution)/shard_map/ppermute | solution.py:1614
  180.5 32.1 %collective-permute-start.41 = (bf16[256,2304]{1,0:T(8,128)(2,1)}, bf16[256,2304]{1,0:T(8,128)(2,1)}, u32[]{:S(2)}, u32[]{:S(2)}) collective-permute-start(bf16[256,2304]{1,0:T(8,128)(2,1)} %collective-permute-done.16.rest_5_.rest_1_), channel_id=1, source_target_pairs={{0,1},{1,2},{2,3},{3,0},{4,5},{5,6},{6,7},{7,4},{8,9},{9,10},{10,1... | collective-permute-start | bytes 3538952 | tf_op jit(solution)/shard_map/ppermute | solution.py:1617
  180.5 32.1 %collective-permute-start.38 = (bf16[256,1152]{1,0:T(8,128)(2,1)}, bf16[256,1152]{1,0:T(8,128)(2,1)}, u32[]{:S(2)}, u32[]{:S(2)}) collective-permute-start(bf16[256,1152]{1,0:T(8,128)(2,1)} %collective-permute-done.21.rest_0_), channel_id=1, source_target_pairs={{0,8},{8,0},{16,24},{24,16},{1,9},{9,1},{17,25},{25,17},{2,10},{10... | collective-permute-start | bytes 1769480 | tf_op jit(solution)/shard_map/ppermute | solution.py:1611
  181.0 31.6 %collective-permute-start.39 = (bf16[256,1152]{1,0:T(8,128)(2,1)}, bf16[256,1152]{1,0:T(8,128)(2,1)}, u32[]{:S(2)}, u32[]{:S(2)}) collective-permute-start(bf16[256,1152]{1,0:T(8,128)(2,1)} %collective-permute-done.26.rest_1_), channel_id=1, source_target_pairs={{0,16},{16,0},{8,24},{24,8},{1,17},{17,1},{9,25},{25,9},{2,18},{18... | collective-permute-start | bytes 1769480 | tf_op jit(solution)/shard_map/ppermute | solution.py:1608
  181.6 31.1 %collective-permute-start.40 = (bf16[256,1152]{1,0:T(8,128)(2,1)}, bf16[256,1152]{1,0:T(8,128)(2,1)}, u32[]{:S(2)}, u32[]{:S(2)}) collective-permute-start(bf16[256,1152]{1,0:T(8,128)(2,1)} %collective-permute-done.35.rest_3_), channel_id=1, source_target_pairs={{0,4},{4,0},{1,5},{5,1},{2,6},{6,2},{3,7},{7,3},{8,12},{12,8},{9,1... | collective-permute-start | bytes 1769480 | tf_op jit(solution)/shard_map/ppermute | solution.py:1614
  282.9 409.8 %all-gather.9.cloned.1.call-start = ((), (), s32[]{:S(2)}) async-start(), calls=%async_computation.1 | async-start | bytes 5242880 | tf_op jit(solution)/shard_map/all_gather | solution.py:2002
  308.7 33.7 %collective-permute-start.56 = (bf16[512,3456]{1,0:T(8,128)(2,1)}, bf16[512,3456]{1,0:T(8,128)(2,1)}, u32[]{:S(2)}, u32[]{:S(2)}) collective-permute-start(bf16[512,3456]{1,0:T(8,128)(2,1)} %get-tuple-element.2185), channel_id=1, source_target_pairs={{0,8},{8,0},{16,24},{24,16},{1,9},{9,1},{17,25},{25,17},{2,10},{10... | collective-permute-start | bytes 10616840 | tf_op jit(solution)/shard_map/ppermute | solution.py:1611
  343.3 33.7 %collective-permute-start.58 = (bf16[512,3456]{1,0:T(8,128)(2,1)}, bf16[512,3456]{1,0:T(8,128)(2,1)S(1)}, u32[]{:S(2)}, u32[]{:S(2)}) collective-permute-start(bf16[512,3456]{1,0:T(8,128)(2,1)} %get-tuple-element.2258), channel_id=1, source_target_pairs={{0,8},{8,0},{16,24},{24,16},{1,9},{9,1},{17,25},{25,17},{2,10},{10... | collective-permute-start | bytes 10616840 | tf_op jit(solution)/shard_map/ppermute | solution.py:1611
  378.8 35.2 %collective-permute-start.61 = (bf16[512,3456]{1,0:T(8,128)(2,1)}, bf16[512,3456]{1,0:T(8,128)(2,1)S(1)}, u32[]{:S(2)}, u32[]{:S(2)}) collective-permute-start(bf16[512,3456]{1,0:T(8,128)(2,1)} %get-tuple-element.2320), channel_id=1, source_target_pairs={{0,8},{8,0},{16,24},{24,16},{1,9},{9,1},{17,25},{25,17},{2,10},{10... | collective-permute-start | bytes 10616840 | tf_op jit(solution)/shard_map/ppermute | solution.py:1611
  400.4 51.1 %collective-permute-start.67 = (bf16[1024,256]{1,0:T(8,128)(2,1)}, bf16[1024,256]{1,0:T(8,128)(2,1)S(1)}, u32[]{:S(2)}, u32[]{:S(2)}) collective-permute-start(bf16[1024,256]{1,0:T(8,128)(2,1)} %get-tuple-element.2405), channel_id=1, source_target_pairs={{0,4},{4,0},{1,5},{5,1},{2,6},{6,2},{3,7},{7,3},{8,12},{12,8},{9,1... | collective-permute-start | bytes 1572872 | tf_op jit(solution)/shard_map/ppermute | solution.py:1614
  401.1 50.4 %collective-permute-start.64 = (bf16[128,3456]{1,0:T(8,128)(2,1)}, bf16[128,3456]{1,0:T(8,128)(2,1)}, u32[]{:S(2)}, u32[]{:S(2)}) collective-permute-start(bf16[128,3456]{1,0:T(8,128)(2,1)} %get-tuple-element.2396), channel_id=1, source_target_pairs={{0,3},{1,0},{2,1},{3,2},{4,7},{5,4},{6,5},{7,6},{8,11},{9,8},{10,9... | collective-permute-start | bytes 2654216 | tf_op jit(solution)/shard_map/ppermute | solution.py:1623
  425.8 37.9 %collective-permute-start.66 = (bf16[128,3456]{1,0:T(8,128)(2,1)}, bf16[128,3456]{1,0:T(8,128)(2,1)S(1)}, u32[]{:S(2)}, u32[]{:S(2)}) collective-permute-start(bf16[128,3456]{1,0:T(8,128)(2,1)} %get-tuple-element.2398), channel_id=1, source_target_pairs={{0,16},{16,0},{8,24},{24,8},{1,17},{17,1},{9,25},{25,9},{2,18},{18... | collective-permute-start | bytes 2654216 | tf_op jit(solution)/shard_map/ppermute | solution.py:1608
  469.6 41.5 %collective-permute-start.71 = (bf16[512,1024]{1,0:T(8,128)(2,1)}, bf16[512,1024]{1,0:T(8,128)(2,1)S(1)}, u32[]{:S(2)}, u32[]{:S(2)}) collective-permute-start(bf16[512,1024]{1,0:T(8,128)(2,1)} %get-tuple-element.2437), channel_id=1, source_target_pairs={{0,4},{4,0},{1,5},{5,1},{2,6},{6,2},{3,7},{7,3},{8,12},{12,8},{9,1... | collective-permute-start | bytes 3145736 | tf_op jit(solution)/shard_map/ppermute | solution.py:1614
  472.3 36.5 %collective-permute-start.70 = (bf16[128,3456]{1,0:T(8,128)(2,1)}, bf16[128,3456]{1,0:T(8,128)(2,1)}, u32[]{:S(2)}, u32[]{:S(2)}) collective-permute-start(bf16[128,3456]{1,0:T(8,128)(2,1)} %get-tuple-element.2458), channel_id=1, source_target_pairs={{0,16},{16,0},{8,24},{24,8},{1,17},{17,1},{9,25},{25,9},{2,18},{18... | collective-permute-start | bytes 2654216 | tf_op jit(solution)/shard_map/ppermute | solution.py:1608
  511.8 48.3 %collective-permute-start.76 = (bf16[128,3456]{1,0:T(8,128)(2,1)}, bf16[128,3456]{1,0:T(8,128)(2,1)}, u32[]{:S(2)}, u32[]{:S(2)}) collective-permute-start(bf16[128,3456]{1,0:T(8,128)(2,1)} %get-tuple-element.2450), channel_id=1, source_target_pairs={{0,3},{1,0},{2,1},{3,2},{4,7},{5,4},{6,5},{7,6},{8,11},{9,8},{10,9... | collective-permute-start | bytes 2654216 | tf_op jit(solution)/shard_map/ppermute | solution.py:1623
  520.9 39.1 %collective-permute-start.77 = (bf16[128,3456]{1,0:T(8,128)(2,1)}, bf16[128,3456]{1,0:T(8,128)(2,1)}, u32[]{:S(2)}, u32[]{:S(2)}) collective-permute-start(bf16[128,3456]{1,0:T(8,128)(2,1)} %get-tuple-element.2551), channel_id=1, source_target_pairs={{0,1},{1,2},{2,3},{3,0},{4,5},{5,6},{6,7},{7,4},{8,9},{9,10},{10,1... | collective-permute-start | bytes 2654216 | tf_op jit(solution)/shard_map/ppermute | solution.py:1617
  520.9 39.1 %collective-permute-start.74 = (bf16[128,3456]{1,0:T(8,128)(2,1)}, bf16[128,3456]{1,0:T(8,128)(2,1)}, u32[]{:S(2)}, u32[]{:S(2)}) collective-permute-start(bf16[128,3456]{1,0:T(8,128)(2,1)} %get-tuple-element.2508), channel_id=1, source_target_pairs={{0,16},{16,0},{8,24},{24,8},{1,17},{17,1},{9,25},{25,9},{2,18},{18... | collective-permute-start | bytes 2654216 | tf_op jit(solution)/shard_map/ppermute | solution.py:1608
  549.6 178.9 %all-gather.11.cloned.1.call-start = ((), (), s32[]{:S(2)}) async-start(), calls=%async_computation.2 | async-start | bytes 5242880 | tf_op jit(solution)/shard_map/all_gather | solution.py:2008
  640.9 62.4 %collective-permute-start.88 = (f32[128,3456]{1,0:T(8,128)S(1)}, f32[128,3456]{1,0:T(8,128)}, u32[]{:S(2)}, u32[]{:S(2)}) collective-permute-start(f32[128,3456]{1,0:T(8,128)S(1)} %copy-done.32), channel_id=1, source_target_pairs={{0,4},{4,0},{1,5},{5,1},{2,6},{6,2},{3,7},{7,3},{8,12},{12,8},{9,1... | collective-permute-start | bytes 5308424 | tf_op jit(solution)/shard_map/ppermute | solution.py:1614
  651.2 37.5 %collective-permute-start.86 = (bf16[128,768]{1,0:T(8,128)(2,1)S(1)}, bf16[128,768]{1,0:T(8,128)(2,1)S(1)}, u32[]{:S(2)}, u32[]{:S(2)}) collective-permute-start(bf16[128,768]{1,0:T(8,128)(2,1)S(1)} %get-tuple-element.2679), channel_id=1, source_target_pairs={{0,2},{2,0},{1,3},{3,1},{4,6},{6,4},{5,7},{7,5},{8,10},{10,8},{9,1... | collective-permute-start | bytes 589832 | tf_op jit(solution)/shard_map/ppermute | solution.py:1620
  651.2 37.5 %collective-permute-start.87 = (bf16[128,768]{1,0:T(8,128)(2,1)S(1)}, bf16[128,768]{1,0:T(8,128)(2,1)S(1)}, u32[]{:S(2)}, u32[]{:S(2)}) collective-permute-start(bf16[128,768]{1,0:T(8,128)(2,1)S(1)} %get-tuple-element.2678), channel_id=1, source_target_pairs={{0,1},{1,2},{2,3},{3,0},{4,5},{5,6},{6,7},{7,4},{8,9},{9,10},{10,1... | collective-permute-start | bytes 589832 | tf_op jit(solution)/shard_map/ppermute | solution.py:1617
  (152 other events, 1940.3 us)
Sparse Core Ops, SparseCore 0:
  283.0 165.7 all-gather.6
  549.7 80.8 all-gather.8
  632.1 96.2 all-gather.10

commit v17 on v16

--- a/solution.py
+++ b/solution.py
@@ -1572,6 +1572,24 @@
     )(normed_t, *backs, grad_t, attended)
 
 
+def copy_kernel(in_ref, out_ref):
+    out_ref[...] = in_ref[...]
+
+
+def copied(array):
+    spec = pl.BlockSpec((1,) + array.shape[1:], lambda i: (i, 0, 0))
+    return pl.pallas_call(
+        copy_kernel,
+        grid=(array.shape[0],),
+        in_specs=[spec],
+        out_specs=spec,
+        out_shape=shape_of(array.shape, array.dtype),
+        compiler_params=settings(1, 24),
+        cost_estimate=cost(False),
+        name="copied",
+    )(array)
+
+
 def after(value, *others):
     return lax.optimization_barrier((value,) + others)[0]
 
@@ -2042,10 +2060,7 @@
 
     far_h = x_swap(v["sums"][2])
     there = y_swap(summed([v["sums"][1], v["far_t"]]))
-    spread = jnp.zeros((rows_dev, tok, width), BF16)
-    for j in range(2):
-        part = output[:, j * tok // 2 : (j + 1) * tok // 2]
-        spread = lax.dynamic_update_slice(spread, part, (0, j * tok // 2, 0))
+    spread = copied(output)
     v.update(far_h=far_h, there=there, spread=spread)
     sync()
 

time: 764 us -> 757 us (level)
    unnamed x178 -> x179, local copies, waits for them, and re-layouts: 55.2 us -> 50.9 us
  transfers between devices with their start and end apart: 95 -> 95, of which waited for: 29 -> 28; matrix products, arithmetic and copies ran while one was open for 5% -> 5% of each run, Pallas kernels for 46% -> 47%
where the time goes in v17:
time: 757 us; the launch traced here: 746 us
  Pallas kernels  391 us (52%)
  waiting for transfers between devices  158 us (21%)
  starting transfers between devices  85.2 us (11%)
  local copies, waits for them, and re-layouts  64.9 us (9%)
  other arithmetic  28.5 us (4%)
  between operations  18.9 us (2%)
    pallas_call x4, Pallas kernels, ffn_bwd(): pl.pallas_call(functools.partial(ffn_bwd_kernel, steps, plan, first), gri...  101 us
    pallas_call x3, Pallas kernels, ffn_fwd(): pl.pallas_call(functools.partial(ffn_fwd_kernel, tile, [plan for plan, _...  60.9 us
    unnamed x179, local copies, waits for them, and re-layouts  50.9 us
    ppermute x19, waiting for transfers between devices, y_swap(): return lax.ppermute(v, 'ctx', Y_SWAP)  50.4 us
    pallas_call x2, Pallas kernels, attn_bwd(): pl.pallas_call(functools.partial(attn_bwd_kernel, width, hd), grid_spec=p...  49.7 us
    ppermute x22, waiting for transfers between devices, x_swap(): return lax.ppermute(v, 'fsdp', X_SWAP)  42.7 us
    pallas_call x2, Pallas kernels, attn_fwd(): pl.pallas_call(functools.partial(attn_fwd_kernel, width, hd), grid_spec=p...  34.1 us
    pallas_call x6, Pallas kernels, sums(): pl.pallas_call(functools.partial(sums_kernel, jobs, len(arrays)), grid_sp...  33.7 us
  transfers between devices with their start and end apart: 95, of which 28 were waited for; matrix products, arithmetic and copies ran while one was open for 5% of the time, Pallas kernels for 47%

profile of v17, /device:TPU:0, one launch (start us, length us, event | category | flops | bytes accessed | tf_op | source)
XLA Modules:
  0.0 746.3 jit_solution(7257543281636434012)
XLA Ops:
  86.7 13.1 %collective-permute-done.15.rest_4_.rest_0_ = bf16[256,1152]{1,0:T(8,128)(2,1)} collective-permute-done((bf16[256,1152]{1,0:T(8,128)(2,1)}, bf16[256,1152]{1,0:T(8,128)(2,1)}, u32[]{:S(2)}, u32[]{:S(2)}) %collective-permute-start.15) | collective-permute-done | bytes 589856 | tf_op jit(solution)/shard_map/ppermute | solution.py:1635
  102.2 17.1 %attn_fwd.2 = (bf16[1024,256]{1,0:T(8,128)(2,1)}, bf16[1024,256]{1,0:T(8,128)(2,1)}, f32[2,2,2048]{2,1,0:T(2,128)}) custom-call(s32[4]{0:T(128)} %copy-done.23, bf16[512,1024]{1,0:T(8,128)(2,1)} %copy-done.30, bf16[512,1024]{1,0:T(8,128)(2,1)} %copy-done.66), custom_call_target="tpu_custom_call" | custom-call | flops 4398046511104 | bytes 1073741824 | tf_op jit(solution)/shard_map/attn_fwd/pallas_call | solution.py:778
  126.4 17.1 %attn_fwd.3 = (bf16[1024,256]{1,0:T(8,128)(2,1)}, bf16[1024,256]{1,0:T(8,128)(2,1)}, f32[2,2,2048]{2,1,0:T(2,128)}) custom-call(s32[4]{0:T(128)} %copy-done.23, bf16[512,1024]{1,0:T(8,128)(2,1)} %copy-done.29, bf16[512,1024]{1,0:T(8,128)(2,1)} %collective-permute-done.17.got_ref), custom_call_target="tpu_custom_call" | custom-call | flops 4398046511104 | bytes 1073741824 | tf_op jit(solution)/shard_map/attn_fwd/pallas_call | solution.py:778
  149.2 11.8 %collective-permute-done.27.refs_8_ = bf16[1024,256]{1,0:T(8,128)(2,1)S(1)} collective-permute-done((bf16[1024,256]{1,0:T(8,128)(2,1)}, bf16[1024,256]{1,0:T(8,128)(2,1)S(1)}, u32[]{:S(2)}, u32[]{:S(2)}) %collective-permute-start.27) | collective-permute-done | bytes 524320 | tf_op jit(solution)/shard_map/ppermute | solution.py:1632
  164.4 10.3 %out_proj.1 = (f32[1024,1024]{1,0:T(8,128)}, bf16[1024,1024]{1,0:T(8,128)(2,1)}, bf16[1024,1024]{1,0:T(8,128)(2,1)}, bf16[4,1024,256]{2,1,0:T(8,128)(2,1)}) custom-call(s32[4]{0:T(128)} %copy-done.23, bf16[1024,256]{1,0:T(8,128)(2,1)} %constant_dynamic-update-slice_fusion.refs_0_, bf16[1024,256]{1,0:T(8,128)(2,1)} %collective-permute-done.25.refs_1_, ...), custom_call_target="tpu_custom_call" | custom-call | flops 4398046511104 | bytes 1073741824 | tf_op jit(solution)/shard_map/out_proj/pallas_call | solution.py:1004
  185.7 27.2 %ffn_fwd.3 = (bf16[2,1024,2304]{2,1,0:T(8,128)(2,1)}, bf16[2,1024,1152]{2,1,0:T(8,128)(2,1)}, f32[1024,1024]{1,0:T(8,128)}) custom-call(s32[4]{0:T(128)} %copy-done.23, f32[1]{0:T(128)} %bitcast.4.scale, bf16[1024,1024]{1,0:T(8,128)(2,1)} %get-tuple-element.1784.x_ref, f32[1024,1024]{1,0:T(8,128)} %get-tuple-element.2342.in_ref.refs_5_, ...), custom_call_target="tpu_custom_call" | custom-call | flops 4398046511104 | bytes 1073741824 | tf_op jit(solution)/shard_map/ffn_fwd/pallas_call | solution.py:1295
  220.3 15.6 %ffn_fwd.4 = (bf16[1,1024,2304]{2,1,0:T(8,128)(2,1)}, bf16[1,1024,1152]{2,1,0:T(8,128)(2,1)}, f32[1024,1024]{1,0:T(8,128)}) custom-call(s32[4]{0:T(128)} %copy-done.23, f32[1]{0:T(128)} %bitcast.4.scale, bf16[1024,1024]{1,0:T(8,128)(2,1)} %get-tuple-element.1784.x_ref, f32[1024,1024]{1,0:T(8,128)} %get-tuple-element.1684.in_ref, ...), custom_call_target="tpu_custom_call" | custom-call | flops 4398046511104 | bytes 1073741824 | tf_op jit(solution)/shard_map/ffn_fwd/pallas_call | solution.py:1295
  240.1 18.1 %ffn_fwd.5 = (bf16[1,1024,2304]{2,1,0:T(8,128)(2,1)}, bf16[1,1024,1152]{2,1,0:T(8,128)(2,1)}, bf16[1024,1024]{1,0:T(8,128)(2,1)}, f32[1024,1024]{1,0:T(8,128)}, ...) custom-call(s32[4]{0:T(128)} %copy-done.23, f32[1]{0:T(128)} %bitcast.4.scale, ...), custom_call_target="tpu_custom_call" | custom-call | flops 4398046511104 | bytes 1073741824 | tf_op jit(solution)/shard_map/ffn_fwd/pallas_call | solution.py:1295
  258.2 24.8 %ffn_bwd.4 = (f32[1024,1024]{1,0:T(8,128)}, bf16[512,3456]{1,0:T(8,128)(2,1)}, bf16[512,3456]{1,0:T(8,128)(2,1)}) custom-call(bf16[1024,1024]{1,0:T(8,128)(2,1)} %get-tuple-element.2271.low_ref, bf16[1,1024,2304]{2,1,0:T(8,128)(2,1)} %get-tuple-element.1907.act_ref, bf16[1,1024,1152]{2,1,0:T(8,128)(2,1)} %get-tuple-element.1927.hid_ref, ...), custom_call_target="tpu_custom_call" | custom-call | flops 12880000000 | bytes 3144531 | tf_op jit(solution)/shard_map/ffn_bwd/pallas_call | solution.py:1377
  283.3 25.7 %ffn_bwd.5 = (f32[1024,1024]{1,0:T(8,128)}, bf16[512,3456]{1,0:T(8,128)(2,1)}, bf16[512,3456]{1,0:T(8,128)(2,1)}) custom-call(bf16[1024,1024]{1,0:T(8,128)(2,1)} %get-tuple-element.2271.low_ref, bf16[2,1024,2304]{2,1,0:T(8,128)(2,1)} %get-tuple-element.2255.act_ref, ...), custom_call_target="tpu_custom_call", output_to_operand_aliasing={{0}: (15, {})} | custom-call | flops 12880000000 | bytes 3144531 | tf_op jit(solution)/shard_map/ffn_bwd/pallas_call | solution.py:1377
  317.8 25.5 %ffn_bwd.6 = (f32[1024,1024]{1,0:T(8,128)}, bf16[512,3456]{1,0:T(8,128)(2,1)}, bf16[512,3456]{1,0:T(8,128)(2,1)}) custom-call(bf16[1024,1024]{1,0:T(8,128)(2,1)} %get-tuple-element.2271.low_ref, bf16[1,1024,2304]{2,1,0:T(8,128)(2,1)} %get-tuple-element.2183.act_ref, ...), custom_call_target="tpu_custom_call", output_to_operand_aliasing={{0}: (17, {})} | custom-call | flops 12880000000 | bytes 3144531 | tf_op jit(solution)/shard_map/ffn_bwd/pallas_call | solution.py:1377
  352.3 25.3 %ffn_bwd.7 = (f32[1024,1024]{1,0:T(8,128)}, bf16[512,3456]{1,0:T(8,128)(2,1)}, bf16[512,3456]{1,0:T(8,128)(2,1)}) custom-call(bf16[1024,1024]{1,0:T(8,128)(2,1)} %get-tuple-element.2271.low_ref, bf16[2,1024,2304]{2,1,0:T(8,128)(2,1)} %get-tuple-element.2255.act_ref, ...), custom_call_target="tpu_custom_call", output_to_operand_aliasing={{0}: (9, {})} | custom-call | flops 12880000000 | bytes 3144531 | tf_op jit(solution)/shard_map/ffn_bwd/pallas_call | solution.py:1377
  387.0 12.5 %norm_two_back.1 = (f32[1024,1024]{1,0:T(8,128)}, bf16[1024,1024]{1,0:T(8,128)(2,1)}, bf16[1024,256]{1,0:T(8,128)(2,1)}, bf16[1024,256]{1,0:T(8,128)(2,1)}, bf16...) custom-call(s32[4]{0:T(128)} %copy-done.23, ...), custom_call_target="tpu_custom_call" | custom-call | flops 6209999872 | bytes 1516113 | tf_op jit(solution)/shard_map/norm_two_back/pallas_call | solution.py:1062
  405.4 9.2 %collective-permute-done.63.gs_ref = bf16[1024,256]{1,0:T(8,128)(2,1)S(1)} collective-permute-done((bf16[1024,256]{1,0:T(8,128)(2,1)}, bf16[1024,256]{1,0:T(8,128)(2,1)S(1)}, u32[]{:S(2)}, u32[]{:S(2)}) %collective-permute-start.63) | collective-permute-done | bytes 524320 | tf_op jit(solution)/shard_map/ppermute | solution.py:1632
  427.4 25.1 %attn_bwd.2 = (bf16[512,1024]{1,0:T(8,128)(2,1)}, bf16[512,1024]{1,0:T(8,128)(2,1)}) custom-call(s32[4]{0:T(128)} %copy-done.23, bf16[512,1024]{1,0:T(8,128)(2,1)} %copy-done.30, bf16[512,1024]{1,0:T(8,128)(2,1)} %copy-done.66, bf16[1024,256]{1,0:T(8,128)(2,1)} %get-tuple-element.2382.refs_5_.ok_ref, bf16[1024,256]{1,0:T(8,128)(2,1)} %get-tuple-element.2383.os_ref, ...), custom_call_target="tpu_custom_call" | custom-call | flops 18630000640 | bytes 4548339 | tf_op jit(solution)/shard_map/attn_bwd/pallas_call | solution.py:939
  452.6 12.1 %collective-permute-done.66.refs_1_ = bf16[128,3456]{1,0:T(8,128)(2,1)S(1)} collective-permute-done((bf16[128,3456]{1,0:T(8,128)(2,1)}, bf16[128,3456]{1,0:T(8,128)(2,1)S(1)}, u32[]{:S(2)}, u32[]{:S(2)}) %collective-permute-start.66) | collective-permute-done | bytes 884768 | tf_op jit(solution)/shard_map/ppermute | solution.py:1626
  474.0 24.7 %attn_bwd.3 = (bf16[512,1024]{1,0:T(8,128)(2,1)}, bf16[512,1024]{1,0:T(8,128)(2,1)}) custom-call(s32[4]{0:T(128)} %copy-done.23, bf16[512,1024]{1,0:T(8,128)(2,1)} %copy-done.29, bf16[512,1024]{1,0:T(8,128)(2,1)} %collective-permute-done.17.got_ref, bf16[1024,256]{1,0:T(8,128)(2,1)} %get-tuple-element.2440.refs_6_.ok_ref, ...), custom_call_target="tpu_custom_call" | custom-call | flops 18630000640 | bytes 4548339 | tf_op jit(solution)/shard_map/attn_bwd/pallas_call | solution.py:939
  498.7 11.1 %collective-permute-done.70.refs_4_ = bf16[128,3456]{1,0:T(8,128)(2,1)} collective-permute-done((bf16[128,3456]{1,0:T(8,128)(2,1)}, bf16[128,3456]{1,0:T(8,128)(2,1)}, u32[]{:S(2)}, u32[]{:S(2)}) %collective-permute-start.70) | collective-permute-done | bytes 884768 | tf_op jit(solution)/shard_map/ppermute | solution.py:1626
  571.0 15.2 %weight_grad.1 = (bf16[4,512,768]{2,1,0:T(8,128)(2,1)}, bf16[4,512,768]{2,1,0:T(8,128)(2,1)}) custom-call(bf16[1024,1024]{1,0:T(8,128)(2,1)} %copy-done, bf16[2,1024,512]{2,1,0:T(8,128)(2,1)} %get-tuple-element.2557.refs_6_.back0_ref, bf16[2,1024,512]{2,1,0:T(8,128)(2,1)} %get-tuple-element.2559.refs_7_.back1_ref, ...), custom_call_target="tpu_custom_call" | custom-call | flops 4398046511104 | bytes 1073741824 | tf_op jit(solution)/shard_map/weight_grad/pallas_call | solution.py:1560
  606.5 12.2 %collective-permute-done.81.refs_1_ = bf16[512,768]{1,0:T(8,128)(2,1)S(1)} collective-permute-done((bf16[512,768]{1,0:T(8,128)(2,1)S(1)}, bf16[512,768]{1,0:T(8,128)(2,1)S(1)}, u32[]{:S(2)}, u32[]{:S(2)}) %collective-permute-start.81) | collective-permute-done | bytes 786464 | tf_op jit(solution)/shard_map/ppermute | solution.py:1626
  631.7 10.8 %collective-permute-done.84.refs_2_ = bf16[512,768]{1,0:T(8,128)(2,1)S(1)} collective-permute-done((bf16[512,768]{1,0:T(8,128)(2,1)}, bf16[512,768]{1,0:T(8,128)(2,1)S(1)}, u32[]{:S(2)}, u32[]{:S(2)}) %collective-permute-start.84) | collective-permute-done | bytes 786464 | tf_op jit(solution)/shard_map/ppermute | solution.py:1632
  654.0 10.2 %collective-permute-done.85.refs_1_ = bf16[128,768]{1,0:T(8,128)(2,1)S(1)} collective-permute-done((bf16[128,768]{1,0:T(8,128)(2,1)S(1)}, bf16[128,768]{1,0:T(8,128)(2,1)S(1)}, u32[]{:S(2)}, u32[]{:S(2)}) %collective-permute-start.85) | collective-permute-done | bytes 196640 | tf_op jit(solution)/shard_map/ppermute | solution.py:1641
  664.2 25.4 %collective-permute-done.86.refs_2_ = bf16[128,768]{1,0:T(8,128)(2,1)S(1)} collective-permute-done((bf16[128,768]{1,0:T(8,128)(2,1)S(1)}, bf16[128,768]{1,0:T(8,128)(2,1)S(1)}, u32[]{:S(2)}, u32[]{:S(2)}) %collective-permute-start.86) | collective-permute-done | bytes 196640 | tf_op jit(solution)/shard_map/ppermute | solution.py:1638
  693.9 10.6 %pad_convert_fusion = f32[4,1024,1024]{2,1,0:T(8,128)} fusion(bf16[4,512,1024]{2,1,0:T(8,128)(2,1)} %bitcast.51), kind=kLoop, calls=%fused_computation.1 | loop fusion | flops 4194304 | bytes 20971520 | tf_op jit(solution)/shard_map/dynamic_update_slice | solution.py:2104
  (450 shorter events, 316.7 us)
Async XLA Ops:
  7.2 463.1 %all-gather.7.cloned.1.call-start = ((), (), s32[]{:S(2)}) async-start(), calls=%async_computation | async-start | bytes 10485760 | tf_op jit(solution)/shard_map/all_gather | solution.py:1863
  56.5 43.3 %collective-permute-start.11 = (bf16[256,3456]{1,0:T(8,128)(2,1)}, bf16[256,3456]{1,0:T(8,128)(2,1)}, u32[]{:S(2)}, u32[]{:S(2)}) collective-permute-start(bf16[256,3456]{1,0:T(8,128)(2,1)} %get-tuple-element.2276.rest_0_), channel_id=1, source_target_pairs={{0,16},{16,0},{8,24},{24,8},{1,17},{17,1},{9,25},{25,9},{2,18},{18... | collective-permute-start | bytes 5308424 | tf_op jit(solution)/shard_map/ppermute | solution.py:1626
  57.4 42.4 %collective-permute-start.16 = (bf16[256,2304]{1,0:T(8,128)(2,1)}, bf16[256,2304]{1,0:T(8,128)(2,1)}, u32[]{:S(2)}, u32[]{:S(2)}) collective-permute-start(bf16[256,2304]{1,0:T(8,128)(2,1)} %get-tuple-element.1370), channel_id=1, source_target_pairs={{0,1},{1,2},{2,3},{3,0},{4,5},{5,6},{6,7},{7,4},{8,9},{9,10},{10,1... | collective-permute-start | bytes 3538952 | tf_op jit(solution)/shard_map/ppermute | solution.py:1635
  75.5 43.8 %collective-permute-start.17 = (bf16[512,1024]{1,0:T(8,128)(2,1)}, bf16[512,1024]{1,0:T(8,128)(2,1)}, u32[]{:S(2)}, u32[]{:S(2)}) collective-permute-start(bf16[512,1024]{1,0:T(8,128)(2,1)} %get-tuple-element.1362), channel_id=1, source_target_pairs={{0,4},{4,0},{1,5},{5,1},{2,6},{6,2},{3,7},{7,3},{8,12},{12,8},{9,1... | collective-permute-start | bytes 3145736 | tf_op jit(solution)/shard_map/ppermute | solution.py:1632
  180.5 32.4 %collective-permute-start.41 = (bf16[256,2304]{1,0:T(8,128)(2,1)}, bf16[256,2304]{1,0:T(8,128)(2,1)}, u32[]{:S(2)}, u32[]{:S(2)}) collective-permute-start(bf16[256,2304]{1,0:T(8,128)(2,1)} %collective-permute-done.16.rest_5_.rest_1_), channel_id=1, source_target_pairs={{0,1},{1,2},{2,3},{3,0},{4,5},{5,6},{6,7},{7,4},{8,9},{9,10},{10,1... | collective-permute-start | bytes 3538952 | tf_op jit(solution)/shard_map/ppermute | solution.py:1635
  180.5 32.4 %collective-permute-start.38 = (bf16[256,1152]{1,0:T(8,128)(2,1)}, bf16[256,1152]{1,0:T(8,128)(2,1)}, u32[]{:S(2)}, u32[]{:S(2)}) collective-permute-start(bf16[256,1152]{1,0:T(8,128)(2,1)} %collective-permute-done.21.rest_0_), channel_id=1, source_target_pairs={{0,8},{8,0},{16,24},{24,16},{1,9},{9,1},{17,25},{25,17},{2,10},{10... | collective-permute-start | bytes 1769480 | tf_op jit(solution)/shard_map/ppermute | solution.py:1629
  181.0 31.9 %collective-permute-start.39 = (bf16[256,1152]{1,0:T(8,128)(2,1)}, bf16[256,1152]{1,0:T(8,128)(2,1)}, u32[]{:S(2)}, u32[]{:S(2)}) collective-permute-start(bf16[256,1152]{1,0:T(8,128)(2,1)} %collective-permute-done.26.rest_1_), channel_id=1, source_target_pairs={{0,16},{16,0},{8,24},{24,8},{1,17},{17,1},{9,25},{25,9},{2,18},{18... | collective-permute-start | bytes 1769480 | tf_op jit(solution)/shard_map/ppermute | solution.py:1626
  182.7 30.3 %collective-permute-start.40 = (bf16[256,1152]{1,0:T(8,128)(2,1)}, bf16[256,1152]{1,0:T(8,128)(2,1)}, u32[]{:S(2)}, u32[]{:S(2)}) collective-permute-start(bf16[256,1152]{1,0:T(8,128)(2,1)} %collective-permute-done.35.rest_3_), channel_id=1, source_target_pairs={{0,4},{4,0},{1,5},{5,1},{2,6},{6,2},{3,7},{7,3},{8,12},{12,8},{9,1... | collective-permute-start | bytes 1769480 | tf_op jit(solution)/shard_map/ppermute | solution.py:1632
  283.2 410.7 %all-gather.9.cloned.1.call-start = ((), (), s32[]{:S(2)}) async-start(), calls=%async_computation.1 | async-start | bytes 5242880 | tf_op jit(solution)/shard_map/all_gather | solution.py:2020
  309.0 34.3 %collective-permute-start.56 = (bf16[512,3456]{1,0:T(8,128)(2,1)}, bf16[512,3456]{1,0:T(8,128)(2,1)}, u32[]{:S(2)}, u32[]{:S(2)}) collective-permute-start(bf16[512,3456]{1,0:T(8,128)(2,1)} %get-tuple-element.2185), channel_id=1, source_target_pairs={{0,8},{8,0},{16,24},{24,16},{1,9},{9,1},{17,25},{25,17},{2,10},{10... | collective-permute-start | bytes 10616840 | tf_op jit(solution)/shard_map/ppermute | solution.py:1629
  344.2 33.4 %collective-permute-start.58 = (bf16[512,3456]{1,0:T(8,128)(2,1)}, bf16[512,3456]{1,0:T(8,128)(2,1)S(1)}, u32[]{:S(2)}, u32[]{:S(2)}) collective-permute-start(bf16[512,3456]{1,0:T(8,128)(2,1)} %get-tuple-element.2258), channel_id=1, source_target_pairs={{0,8},{8,0},{16,24},{24,16},{1,9},{9,1},{17,25},{25,17},{2,10},{10... | collective-permute-start | bytes 10616840 | tf_op jit(solution)/shard_map/ppermute | solution.py:1629
  379.4 35.2 %collective-permute-start.61 = (bf16[512,3456]{1,0:T(8,128)(2,1)}, bf16[512,3456]{1,0:T(8,128)(2,1)S(1)}, u32[]{:S(2)}, u32[]{:S(2)}) collective-permute-start(bf16[512,3456]{1,0:T(8,128)(2,1)} %get-tuple-element.2320), channel_id=1, source_target_pairs={{0,8},{8,0},{16,24},{24,16},{1,9},{9,1},{17,25},{25,17},{2,10},{10... | collective-permute-start | bytes 10616840 | tf_op jit(solution)/shard_map/ppermute | solution.py:1629
  401.3 51.1 %collective-permute-start.67 = (bf16[1024,256]{1,0:T(8,128)(2,1)}, bf16[1024,256]{1,0:T(8,128)(2,1)S(1)}, u32[]{:S(2)}, u32[]{:S(2)}) collective-permute-start(bf16[1024,256]{1,0:T(8,128)(2,1)} %get-tuple-element.2405), channel_id=1, source_target_pairs={{0,4},{4,0},{1,5},{5,1},{2,6},{6,2},{3,7},{7,3},{8,12},{12,8},{9,1... | collective-permute-start | bytes 1572872 | tf_op jit(solution)/shard_map/ppermute | solution.py:1632
  401.7 50.8 %collective-permute-start.64 = (bf16[128,3456]{1,0:T(8,128)(2,1)}, bf16[128,3456]{1,0:T(8,128)(2,1)}, u32[]{:S(2)}, u32[]{:S(2)}) collective-permute-start(bf16[128,3456]{1,0:T(8,128)(2,1)} %get-tuple-element.2396), channel_id=1, source_target_pairs={{0,3},{1,0},{2,1},{3,2},{4,7},{5,4},{6,5},{7,6},{8,11},{9,8},{10,9... | collective-permute-start | bytes 2654216 | tf_op jit(solution)/shard_map/ppermute | solution.py:1641
  426.2 38.4 %collective-permute-start.66 = (bf16[128,3456]{1,0:T(8,128)(2,1)}, bf16[128,3456]{1,0:T(8,128)(2,1)S(1)}, u32[]{:S(2)}, u32[]{:S(2)}) collective-permute-start(bf16[128,3456]{1,0:T(8,128)(2,1)} %get-tuple-element.2398), channel_id=1, source_target_pairs={{0,16},{16,0},{8,24},{24,8},{1,17},{17,1},{9,25},{25,9},{2,18},{18... | collective-permute-start | bytes 2654216 | tf_op jit(solution)/shard_map/ppermute | solution.py:1626
  470.3 41.8 %collective-permute-start.71 = (bf16[512,1024]{1,0:T(8,128)(2,1)}, bf16[512,1024]{1,0:T(8,128)(2,1)S(1)}, u32[]{:S(2)}, u32[]{:S(2)}) collective-permute-start(bf16[512,1024]{1,0:T(8,128)(2,1)} %get-tuple-element.2437), channel_id=1, source_target_pairs={{0,4},{4,0},{1,5},{5,1},{2,6},{6,2},{3,7},{7,3},{8,12},{12,8},{9,1... | collective-permute-start | bytes 3145736 | tf_op jit(solution)/shard_map/ppermute | solution.py:1632
  472.8 37.1 %collective-permute-start.70 = (bf16[128,3456]{1,0:T(8,128)(2,1)}, bf16[128,3456]{1,0:T(8,128)(2,1)}, u32[]{:S(2)}, u32[]{:S(2)}) collective-permute-start(bf16[128,3456]{1,0:T(8,128)(2,1)} %get-tuple-element.2458), channel_id=1, source_target_pairs={{0,16},{16,0},{8,24},{24,8},{1,17},{17,1},{9,25},{25,9},{2,18},{18... | collective-permute-start | bytes 2654216 | tf_op jit(solution)/shard_map/ppermute | solution.py:1626
  512.5 48.3 %collective-permute-start.76 = (bf16[128,3456]{1,0:T(8,128)(2,1)}, bf16[128,3456]{1,0:T(8,128)(2,1)}, u32[]{:S(2)}, u32[]{:S(2)}) collective-permute-start(bf16[128,3456]{1,0:T(8,128)(2,1)} %get-tuple-element.2450), channel_id=1, source_target_pairs={{0,3},{1,0},{2,1},{3,2},{4,7},{5,4},{6,5},{7,6},{8,11},{9,8},{10,9... | collective-permute-start | bytes 2654216 | tf_op jit(solution)/shard_map/ppermute | solution.py:1641
  521.7 39.1 %collective-permute-start.77 = (bf16[128,3456]{1,0:T(8,128)(2,1)}, bf16[128,3456]{1,0:T(8,128)(2,1)}, u32[]{:S(2)}, u32[]{:S(2)}) collective-permute-start(bf16[128,3456]{1,0:T(8,128)(2,1)} %get-tuple-element.2551), channel_id=1, source_target_pairs={{0,1},{1,2},{2,3},{3,0},{4,5},{5,6},{6,7},{7,4},{8,9},{9,10},{10,1... | collective-permute-start | bytes 2654216 | tf_op jit(solution)/shard_map/ppermute | solution.py:1635
  521.7 39.1 %collective-permute-start.74 = (bf16[128,3456]{1,0:T(8,128)(2,1)}, bf16[128,3456]{1,0:T(8,128)(2,1)}, u32[]{:S(2)}, u32[]{:S(2)}) collective-permute-start(bf16[128,3456]{1,0:T(8,128)(2,1)} %get-tuple-element.2508), channel_id=1, source_target_pairs={{0,16},{16,0},{8,24},{24,8},{1,17},{17,1},{9,25},{25,9},{2,18},{18... | collective-permute-start | bytes 2654216 | tf_op jit(solution)/shard_map/ppermute | solution.py:1626
  550.6 178.7 %all-gather.11.cloned.1.call-start = ((), (), s32[]{:S(2)}) async-start(), calls=%async_computation.2 | async-start | bytes 5242880 | tf_op jit(solution)/shard_map/all_gather | solution.py:2026
  642.5 61.9 %collective-permute-start.88 = (f32[128,3456]{1,0:T(8,128)S(1)}, f32[128,3456]{1,0:T(8,128)}, u32[]{:S(2)}, u32[]{:S(2)}) collective-permute-start(f32[128,3456]{1,0:T(8,128)S(1)} %copy-done.33), channel_id=1, source_target_pairs={{0,4},{4,0},{1,5},{5,1},{2,6},{6,2},{3,7},{7,3},{8,12},{12,8},{9,1... | collective-permute-start | bytes 5308424 | tf_op jit(solution)/shard_map/ppermute | solution.py:1632
  653.2 36.4 %collective-permute-start.86 = (bf16[128,768]{1,0:T(8,128)(2,1)S(1)}, bf16[128,768]{1,0:T(8,128)(2,1)S(1)}, u32[]{:S(2)}, u32[]{:S(2)}) collective-permute-start(bf16[128,768]{1,0:T(8,128)(2,1)S(1)} %get-tuple-element.2679), channel_id=1, source_target_pairs={{0,2},{2,0},{1,3},{3,1},{4,6},{6,4},{5,7},{7,5},{8,10},{10,8},{9,1... | collective-permute-start | bytes 589832 | tf_op jit(solution)/shard_map/ppermute | solution.py:1638
  653.2 36.4 %collective-permute-start.87 = (bf16[128,768]{1,0:T(8,128)(2,1)S(1)}, bf16[128,768]{1,0:T(8,128)(2,1)S(1)}, u32[]{:S(2)}, u32[]{:S(2)}) collective-permute-start(bf16[128,768]{1,0:T(8,128)(2,1)S(1)} %get-tuple-element.2678), channel_id=1, source_target_pairs={{0,1},{1,2},{2,3},{3,0},{4,5},{5,6},{6,7},{7,4},{8,9},{9,10},{10,1... | collective-permute-start | bytes 589832 | tf_op jit(solution)/shard_map/ppermute | solution.py:1635
  (153 other events, 1926.1 us)
Sparse Core Ops, SparseCore 0:
  283.3 166.3 all-gather.6
  550.7 80.6 all-gather.8
  633.0 96.3 all-gather.10

commit v18 on v17

--- a/solution.py
+++ b/solution.py
@@ -1594,6 +1594,12 @@
     return lax.optimization_barrier((value,) + others)[0]
 
 
+class Live:
+
+    def update(self, **values):
+        vars(self).update(values)
+
+
 def per_device_rows(
     tokens,
     teacher,
@@ -1645,10 +1651,10 @@
         v = jnp.where(fsdp % 2 == 0, v, jnp.concatenate([v[1:2], v[0:1], v[3:4], v[2:3]], axis=0))
         return jnp.where(fsdp // 2 == 0, v, jnp.concatenate([v[2:4], v[0:2]], axis=0))
 
-    v = {}
+    v = Live()
 
     def sync():
-        v.update(lax.optimization_barrier(dict(v)))
+        v.update(**lax.optimization_barrier(dict(vars(v))))
 
     length = lax.dynamic_slice_in_dim(lengths, z, 1, 0)
     info = jnp.concatenate([jnp.stack([z, fsdp, ctx]).astype(jnp.int32), length])
@@ -1681,12 +1687,12 @@
         sin_part=jnp.sin(angles),
     )
     sync()
-    info = v["info"]
-
-    proj_zfar = x_swap(v["proj_z"])
-    out_z = [z_up(v["w_out"]), z_far(v["w_out"]), z_down(v["w_out"])]
-    own_core = core_swap(v["proj_own"])
-    x_in, normed_one_t = norm_one(info, tokens, v["gain_one"], 256)
+    info = v.info
+
+    proj_zfar = x_swap(v.proj_z)
+    out_z = [z_up(v.w_out), z_far(v.w_out), z_down(v.w_out)]
+    own_core = core_swap(v.proj_own)
+    x_in, normed_one_t = norm_one(info, tokens, v.gain_one, 256)
     v.update(
         proj_zfar=proj_zfar, own_core=own_core, x_in=x_in, normed_one_t=normed_one_t, out_z=out_z
     )
@@ -1694,14 +1700,14 @@
 
     plan_proj = [[(0, 0), (0, quarter), (3, 0), (3, quarter)]]
     plan_proj += [[(p, k * quarter) for p in (1, 2, 4, 5)] for k in range(3)]
-    weights_proj = [v["proj_own"], v["proj_z"], v["proj_zfar"], v["own_core"]]
-    weights_proj += [core_swap(v["proj_z"]), core_swap(v["proj_zfar"])]
-    one = [z_up(v["w_chunks"][0]), z_up(v["w_chunks"][3])]
-    ffn_far = x_swap(v["w_ffn"])
-    tables = [v[name] for name in ("cos_part", "sin_part", "gain_q", "gain_k")]
+    weights_proj = [v.proj_own, v.proj_z, v.proj_zfar, v.own_core]
+    weights_proj += [core_swap(v.proj_z), core_swap(v.proj_zfar)]
+    one = [z_up(v.w_chunks[0]), z_up(v.w_chunks[3])]
+    ffn_far = x_swap(v.w_ffn)
+    tables = [v.cos_part, v.sin_part, v.gain_q, v.gain_k]
 
     def make(block, *then):
-        normed_t = after(v["normed_one_t"], *then)
+        normed_t = after(v.normed_one_t, *then)
         return project(info, (plan_proj, weights_proj), normed_t, *tables, heads, block)
 
     theirs = [make(lambda s: 2 * (1 - s[2]))]
@@ -1720,19 +1726,19 @@
     )
     sync()
 
-    one_far = [x_swap(v["one"][0])]
-    three = [z_down(v["w_chunks"][0])]
-    own_cores = [core_swap(v["w_ffn"]), core_swap(v["ffn_far"])]
-    first = attn_fwd(info, v["mine"][0][0], v["got0"], hd)
+    one_far = [x_swap(v.one[0])]
+    three = [z_down(v.w_chunks[0])]
+    own_cores = [core_swap(v.w_ffn), core_swap(v.ffn_far)]
+    first = attn_fwd(info, v.mine[0][0], v.got0, hd)
     v.update(first=first, got1=got[1], one_far=one_far, three=three, own_cores=own_cores)
     sync()
 
-    arrived = [y_swap(v["first"][1])]
-    three = v["three"] + [z_down(v["w_chunks"][1])]
-    out_blocks = jnp.concatenate([v["w_out"]] + v["out_z"], axis=0)
+    arrived = [y_swap(v.first[1])]
+    three = v.three + [z_down(v.w_chunks[1])]
+    out_blocks = jnp.concatenate([v.w_out] + v.out_z, axis=0)
     out_far = x_swap(out_blocks)
-    one_cores = [core_swap(v["one"][0]), core_swap(v["one_far"][0])]
-    second = attn_fwd(info, v["mine"][1][0], v["got1"], hd)
+    one_cores = [core_swap(v.one[0]), core_swap(v.one_far[0])]
+    second = attn_fwd(info, v.mine[1][0], v.got1, hd)
     v.update(
         second=second,
         arrived=arrived,
@@ -1743,26 +1749,26 @@
     )
     sync()
 
-    arrived = v["arrived"] + [y_swap(v["second"][1])]
-    three = v["three"] + [z_down(v["w_chunks"][2])]
-    one_far = v["one_far"] + [x_swap(v["one"][1][:, :units])]
-    weights_out = [v["out_blocks"], v["out_far"]]
-    weights_out += [core_swap(v["out_blocks"]), core_swap(v["out_far"])]
+    arrived = v.arrived + [y_swap(v.second[1])]
+    three = v.three + [z_down(v.w_chunks[2])]
+    one_far = v.one_far + [x_swap(v.one[1][:, :units])]
+    weights_out = [v.out_blocks, v.out_far]
+    weights_out += [core_swap(v.out_blocks), core_swap(v.out_far)]
     v.update(arrived=arrived, three=three, one_far=one_far, weights_out=weights_out)
     sync()
 
     plan_out = [[(p, k * quarter) for p in range(4)] for k in range(4)]
-    two = [z_up(v["one"][0])]
-    three_far = [x_swap(v["three"][0])]
-    one_far = v["one_far"] + [y_swap(v["one_far"][0])]
-    one_cores = v["one_cores"] + [core_swap(v["one"][1]), core_swap(v["one_far"][1])]
+    two = [z_up(v.one[0])]
+    three_far = [x_swap(v.three[0])]
+    one_far = v.one_far + [y_swap(v.one_far[0])]
+    one_cores = v.one_cores + [core_swap(v.one[1]), core_swap(v.one_far[1])]
     resid, normed_two, normed_two_t, attended = out_proj(
         info,
-        v["x_in"],
-        [v["first"][0], v["second"][0]],
-        v["arrived"],
-        (plan_out, v["weights_out"]),
-        v["gain_two"],
+        v.x_in,
+        [v.first[0], v.second[0]],
+        v.arrived,
+        (plan_out, v.weights_out),
+        v.gain_two,
         256,
     )
     v.update(
@@ -1780,19 +1786,19 @@
     plan0 = [[(i, 0, j * units) for j in range(3)] for i in range(4)]
     plan_mixed = [[(0, 0, 0), (1, 0, 0), (1, 0, units)], [(i, 0, 0) for i in (2, 3, 4)]]
     plan_mixed += [[(5, 0, 0), (6, 0, 0), (6, 0, units)], [(i, 0, 0) for i in (7, 8, 9)]]
-    scale = (slots / v["total_count"])[None]
-    weights0 = [v["w_ffn"], v["ffn_far"]] + v["own_cores"]
-    c0, cf, c1, cb = v["one_cores"]
-    weights1 = v["one"] + v["one_far"] + [c0, c1, cf, cb, core_swap(v["one_far"][2])]
-    two = v["two"] + [z_up(v["one"][1])]
-    three_far = v["three_far"] + [x_swap(v["three"][1]), y_swap(v["three_far"][0])]
-    two_far = [x_swap(v["two"][0])]
-    three_cores = [core_swap(v["three"][0])]
+    scale = (slots / v.total_count)[None]
+    weights0 = [v.w_ffn, v.ffn_far] + v.own_cores
+    c0, cf, c1, cb = v.one_cores
+    weights1 = v.one + v.one_far + [c0, c1, cf, cb, core_swap(v.one_far[2])]
+    two = v.two + [z_up(v.one[1])]
+    three_far = v.three_far + [x_swap(v.three[1]), y_swap(v.three_far[0])]
+    two_far = [x_swap(v.two[0])]
+    three_cores = [core_swap(v.three[0])]
     acts_a, hiddens_a, sum_a = ffn_fwd(
         info,
         scale,
-        v["normed_two"],
-        v["resid"],
+        v.normed_two,
+        v.resid,
         None,
         [(plan0, weights0), (plan_mixed, weights1)],
         units,
@@ -1813,13 +1819,13 @@
     sync()
 
     plan_chunks = [[(3 * p + j, 0, 0) for j in range(3)] for p in range(4)]
-    weights3 = v["three"] + v["three_far"] + v["three_cores"]
-    weights3 += [core_swap(part) for part in v["three"][1:]]
-    weights3 += [core_swap(part) for part in v["three_far"]]
-    two_far = v["two_far"] + [x_swap(v["two"][1][:, :units]), y_swap(v["two_far"][0])]
-    two_cores = [core_swap(part) for part in v["two"] + v["two_far"]]
+    weights3 = v.three + v.three_far + v.three_cores
+    weights3 += [core_swap(part) for part in v.three[1:]]
+    weights3 += [core_swap(part) for part in v.three_far]
+    two_far = v.two_far + [x_swap(v.two[1][:, :units]), y_swap(v.two_far[0])]
+    two_cores = [core_swap(part) for part in v.two + v.two_far]
     acts_b, hiddens_b, sum_b = ffn_fwd(
-        info, v["scale"], v["normed_two"], v["sum_a"], None, [(plan_chunks, weights3)], units, 256
+        info, v.scale, v.normed_two, v.sum_a, None, [(plan_chunks, weights3)], units, 256
     )
     v.update(
         weights3=weights3,
@@ -1831,10 +1837,10 @@
     )
     sync()
 
-    weights2 = v["two"] + v["two_far"] + v["two_cores"]
-    weights2 += [core_swap(part) for part in v["two_far"][1:]]
+    weights2 = v.two + v.two_far + v.two_cores
+    weights2 += [core_swap(part) for part in v.two_far[1:]]
     acts_c, hiddens_c, result_low, grad_result, grad_low, grad_low_t, square = ffn_fwd(
-        info, v["scale"], v["normed_two"], v["sum_b"], teacher, [(plan_mixed, weights2)], units, 256
+        info, v.scale, v.normed_two, v.sum_b, teacher, [(plan_mixed, weights2)], units, 256
     )
     v.update(
         weights2=weights2,
@@ -1850,31 +1856,31 @@
 
     def ffn_back(plan, weights, acts, hiddens, block, total):
         return ffn_bwd(
-            v["grad_low"],
-            (v[acts], v[hiddens], block),
-            (plan, v[weights]),
+            v.grad_low,
+            (acts, hiddens, block),
+            (plan, weights),
             total,
-            v["normed_two_t"],
-            v["grad_low_t"],
+            v.normed_two_t,
+            v.grad_low_t,
             256,
         )
 
     turned = [False, False, True]
-    output = lax.all_gather(v["result_low"], "tp", axis=0, tiled=False)
-    total, keep2, send2 = ffn_back(plan_mixed, "weights2", "acts_c", "hiddens_c", 0, None)
+    output = lax.all_gather(v.result_low, "tp", axis=0, tiled=False)
+    total, keep2, send2 = ffn_back(plan_mixed, v.weights2, v.acts_c, v.hiddens_c, 0, None)
     v.update(total=total, keep2=keep2, send2=send2)
     sync()
 
-    came2 = core_swap(v["send2"])
-    total, keep1, send1 = ffn_back(plan_mixed, "weights1", "acts_a", "hiddens_a", 1, v["total"])
+    came2 = core_swap(v.send2)
+    total, keep1, send1 = ffn_back(plan_mixed, v.weights1, v.acts_a, v.hiddens_a, 1, v.total)
     v.update(came2=came2, total=total, keep1=keep1, send1=send1)
     sync()
 
-    came1 = core_swap(v["send1"])
-    sum2 = sums(info, [v["keep2"], v["came2"]], core_jobs(0, 1))
+    came1 = core_swap(v.send1)
+    sum2 = sums(info, [v.keep2, v.came2], core_jobs(0, 1))
     far_t2 = x_swap(sum2[3])
     total, keep3, send3 = ffn_back(
-        plan_chunks, "weights3", "acts_b", "hiddens_b", 0, after(v["total"], sum2[0])
+        plan_chunks, v.weights3, v.acts_b, v.hiddens_b, 0, after(v.total, sum2[0])
     )
     v.update(
         came1=came1,
@@ -1886,16 +1892,16 @@
     )
     sync()
 
-    came3 = core_swap(v["send3"])
-    far_h2 = x_swap(v["sum2"][2])
+    came3 = core_swap(v.send3)
+    far_h2 = x_swap(v.sum2[2])
     there2, *sum1 = sums(
         info,
-        [v["sum2"][1], v["far_t2"], v["keep1"], v["came1"]],
+        [v.sum2[1], v.far_t2, v.keep1, v.came1],
         [[(0, 0, None, False), (1, 0, None, False)]] + core_jobs(2, 3),
     )
     there2 = y_swap(there2)
     total, keep0, send0 = ffn_back(
-        plan0, "weights0", "acts_a", "hiddens_a", 0, after(v["total"], sum1[0])
+        plan0, v.weights0, v.acts_a, v.hiddens_a, 0, after(v.total, sum1[0])
     )
     v.update(
         came3=came3,
@@ -1908,22 +1914,22 @@
     )
     sync()
 
-    came0 = core_swap(v["send0"])
-    far_t1 = x_swap(v["sum1"][3])
+    came0 = core_swap(v.send0)
+    far_t1 = x_swap(v.sum1[3])
     plane = [(0, 0, None, False), (1, 0, None, False), (2, 0, None, True)]
     part2, *sum3 = sums(
         info,
-        [v["sum2"][0], v["far_h2"], v["there2"], v["keep3"], v["came3"]],
+        [v.sum2[0], v.far_h2, v.there2, v.keep3, v.came3],
         [plane] + core_jobs(3, 4),
     )
     down2 = z_down(part2)
     grad_resid, grad_attn_t, a0, a1, b0, b1, gain_two_sum = norm_two_back(
         info,
-        after(v["total"], sum3[0]),
-        v["resid"],
-        v["grad_result"],
-        v["gain_two"],
-        (plan_out, v["weights_out"]),
+        after(v.total, sum3[0]),
+        v.resid,
+        v.grad_result,
+        v.gain_two,
+        (plan_out, v.weights_out),
         256,
     )
     grad_got = [y_swap(b0), y_swap(b1)]
@@ -1935,25 +1941,27 @@
         grad_attn_t=grad_attn_t,
         grad_mine=[a0, a1],
         gain_two_sum=gain_two_sum,
-        grad_got0=grad_got[0],
     )
     sync()
 
     def attn_back(j, grad):
-        out, got_ref = v["first" if j == 0 else "second"], v[f"got{j}"]
+        out = (v.first, v.second)[j]
+        got_ref = (v.got0, v.got1)[j]
+        arrived = (v.grad_got0, grad_got[1] if j == 0 else v.grad_got1)[j]
         return attn_bwd(
-            info, v["mine"][j][0], got_ref, out[0], out[1], grad, v[f"grad_got{j}"], out[2], hd
+            info, v.mine[j][0], got_ref, out[0], out[1], grad, arrived, out[2], hd
         )
 
-    far_h1 = x_swap(v["sum1"][2])
+    far_h1 = x_swap(v.sum1[2])
     there1, *sum0 = sums(
         info,
-        [v["sum1"][1], v["far_t1"], v["keep0"], v["came0"]],
+        [v.sum1[1], v.far_t1, v.keep0, v.came0],
         [[(0, 0, None, False), (1, 0, None, False)]] + core_jobs(2, 3),
     )
     there1 = y_swap(there1)
-    far_t3 = x_swap(v["sum3"][3])
-    back0 = attn_back(0, after(v["grad_mine"][0], sum0[0]))
+    far_t3 = x_swap(v.sum3[3])
+    v.update(grad_got0=grad_got[0])
+    back0 = attn_back(0, after(v.grad_mine[0], sum0[0]))
     v.update(
         far_h1=far_h1,
         there1=there1,
@@ -1965,12 +1973,12 @@
     )
     sync()
 
-    heads0 = y_swap(v["back0"][1])
-    far_h3 = x_swap(v["sum3"][2])
-    far_t0 = x_swap(v["sum0"][3])
+    heads0 = y_swap(v.back0[1])
+    far_h3 = x_swap(v.sum3[2])
+    far_t0 = x_swap(v.sum0[3])
     there3, two_down = sums(
         info,
-        [v["sum3"][1], v["far_t3"], v["sum1"][0], v["far_h1"], v["there1"], v["down2"]],
+        [v.sum3[1], v.far_t3, v.sum1[0], v.far_h1, v.there1, v.down2],
         [
             [(0, 0, None, False), (1, 0, None, False)],
             [(2, 0, None, False), (3, 0, None, False), (4, 0, None, True), (5, 0, None, False)],
@@ -1978,39 +1986,39 @@
     )
     there3_got = y_swap(there3)
     two_down_got = z_down(two_down)
-    back1 = attn_back(1, after(v["grad_mine"][1], there3, two_down, output))
+    back1 = attn_back(1, after(v.grad_mine[1], there3, two_down, output))
     v.update(
         heads0=heads0, far_h3=far_h3, far_t0=far_t0, there3=there3_got, back1=back1
     )
     sync()
 
-    heads1 = y_swap(v["back1"][1])
-    far_h0 = x_swap(v["sum0"][2])
+    heads1 = y_swap(v.back1[1])
+    far_h0 = x_swap(v.sum0[2])
     part3, there0 = sums(
         info,
-        [v["sum3"][0], v["far_h3"], v["there3"], v["sum0"][1], v["far_t0"]],
+        [v.sum3[0], v.far_h3, v.there3, v.sum0[1], v.far_t0],
         [plane, [(3, 0, None, False), (4, 0, None, False)]],
     )
     up3 = z_up(part3)
-    tables = [v[name] for name in ("cos_part", "sin_part", "gain_q", "gain_k")]
+    tables = [v.cos_part, v.sin_part, v.gain_q, v.gain_k]
     head0 = head_back(
-        info, v["back0"][0], v["heads0"], v["mine"][0][1], v["theirs"][0][1], *tables, heads
+        info, v.back0[0], v.heads0, v.mine[0][1], v.theirs[0][1], *tables, heads
     )
     v.update(heads1=heads1, head0=head0, there0=there0)
     sync()
 
-    there0 = y_swap(v["there0"])
+    there0 = y_swap(v.there0)
     head1 = head_back(
-        info, v["back1"][0], v["heads1"], v["mine"][1][1], v["theirs"][1][1], *tables, heads
+        info, v.back1[0], v.heads1, v.mine[1][1], v.theirs[1][1], *tables, heads
     )
     def last_norm(part, *then):
         return norm_one_back(
             info,
-            [v["head0"][0], after(head1[0], *then)],
-            (plan_proj, v["weights_proj"]),
-            v["x_in"],
-            v["grad_resid"],
-            v["gain_one"],
+            [v.head0[0], after(head1[0], *then)],
+            (plan_proj, v.weights_proj),
+            v.x_in,
+            v.grad_resid,
+            v.gain_one,
             tok // 4,
             part,
         )
@@ -2023,18 +2031,18 @@
     v.update(there0=there0, far_h0=far_h0, two_down=two_down_got)
     sync()
 
-    gathered.append(lax.all_gather(v["tokens_low"], "tp", axis=0, tiled=False))
+    gathered.append(lax.all_gather(v.tokens_low, "tp", axis=0, tiled=False))
     keep, send = weight_grad(
-        v["normed_one_t"], [v["head0"][0], v["head1"][0]], v["grad_attn_t"], v["attended"]
-    )
-    gain_heads = v["head0"][1] + v["head1"][1]
+        v.normed_one_t, [v.head0[0], v.head1[0]], v.grad_attn_t, v.attended
+    )
+    gain_heads = v.head0[1] + v.head1[1]
     vector = jnp.concatenate(
         [
-            natural(v["gain_one_sum"].reshape(4, quarter)).reshape(1, width),
-            natural(v["gain_two_sum"].reshape(4, quarter)).reshape(1, width),
+            natural(v.gain_one_sum.reshape(4, quarter)).reshape(1, width),
+            natural(v.gain_two_sum.reshape(4, quarter)).reshape(1, width),
             gain_heads[:, 0].reshape(1, hd),
             gain_heads[:, 1].reshape(1, hd),
-            jnp.sum(v["square"]).reshape(1, 1),
+            jnp.sum(v.square).reshape(1, 1),
             jnp.zeros((1, 127), F32),
         ],
         axis=1,
@@ -2046,33 +2054,33 @@
 
     rows = quarter // 2
     flat = lambda a: a.reshape(4 * rows, a.shape[-1])
-    attn_sums = [flat(p) for p in core_sum(info, v["keep"], core_swap(v["send"]))]
-    vector = v["vector"] + x_swap(v["vector"])
+    attn_sums = [flat(p) for p in core_sum(info, v.keep, core_swap(v.send))]
+    vector = v.vector + x_swap(v.vector)
     v.update(sums=attn_sums, vector=vector)
     sync()
 
-    far_t = x_swap(v["sums"][3])
-    part0 = summed([v["sum0"][0], v["far_h0"], v["there0"]], turned)
-    ffn_sum = summed([part0, v["two_down"], v["up3"]], None, F32)
-    vector = v["vector"] + y_swap(v["vector"])
+    far_t = x_swap(v.sums[3])
+    part0 = summed([v.sum0[0], v.far_h0, v.there0], turned)
+    ffn_sum = summed([part0, v.two_down, v.up3], None, F32)
+    vector = v.vector + y_swap(v.vector)
     v.update(far_t=far_t, ffn_sum=ffn_sum, vector=vector)
     sync()
 
-    far_h = x_swap(v["sums"][2])
-    there = y_swap(summed([v["sums"][1], v["far_t"]]))
+    far_h = x_swap(v.sums[2])
+    there = y_swap(summed([v.sums[1], v.far_t]))
     spread = copied(output)
     v.update(far_h=far_h, there=there, spread=spread)
     sync()
 
-    parts = summed([v["sums"][0], v["far_h"], v["there"]])
+    parts = summed([v.sums[0], v.far_h, v.there])
     parts = [parts[k * rows : (k + 1) * rows] for k in range(4)]
     parts = [parts[0], z_down(parts[1]), z_far(parts[2]), z_up(parts[3])]
-    ffn_other = y_swap(v["ffn_sum"])
+    ffn_other = y_swap(v.ffn_sum)
     v.update(parts=parts)
     sync()
 
-    attn_sum = summed(v["parts"], None, F32)
-    vector = v["vector"] + lax.ppermute(v["vector"], "tp", Z_NEAR)
+    attn_sum = summed(v.parts, None, F32)
+    vector = v.vector + lax.ppermute(v.vector, "tp", Z_NEAR)
     v.update(attn_sum=attn_sum, vector=vector)
     v.update(ffn_other=ffn_other)
     sync()
@@ -2093,10 +2101,10 @@
             axis=1,
         )
 
-    attn_other = y_swap(v["attn_sum"])
-    vector = v["vector"] + lax.ppermute(v["vector"], "tp", Z_FAR)
+    attn_other = y_swap(v.attn_sum)
+    vector = v.vector + lax.ppermute(v.vector, "tp", Z_FAR)
     third = units // 3
-    ffn_grad = finish(v["ffn_sum"], turn_chunks(v["ffn_other"]))
+    ffn_grad = finish(v.ffn_sum, turn_chunks(v.ffn_other))
     grad_gate = columns(lambda j: 2 * j * third)
     grad_up = columns(lambda j: (2 * j + 1) * third)
     grad_down = columns(lambda j: 2 * units + j * third).T
@@ -2106,17 +2114,17 @@
     v.update(grad_gate=grad_gate, grad_up=grad_up, grad_down=grad_down)
     sync()
 
-    tokens_grad = lax.dynamic_update_slice(v["grad"], gathered[1].astype(F32), (0, tok // 2, 0))
-    sums_all = v["vector"][0]
-
-    attn_grad = finish(v["attn_sum"], v["attn_other"])
-    teacher_loss = sums_all[2 * width + 2 * hd] / (v["total_count"] * width)
+    tokens_grad = lax.dynamic_update_slice(v.grad, gathered[1].astype(F32), (0, tok // 2, 0))
+    sums_all = v.vector[0]
+
+    attn_grad = finish(v.attn_sum, v.attn_other)
+    teacher_loss = sums_all[2 * width + 2 * hd] / (v.total_count * width)
 
     def own_part(at, size):
         return lax.dynamic_slice_in_dim(sums_all, at + fsdp * (size // 4), size // 4, 0)
 
     return (
-        v["spread"],
+        v.spread,
         teacher_loss,
         tokens_grad,
         own_part(0, width),
@@ -2127,9 +2135,9 @@
         own_part(2 * width + hd, hd),
         attn_grad[:, proj:].T,
         own_part(width, width),
-        v["grad_gate"],
-        v["grad_up"],
-        v["grad_down"],
+        v.grad_gate,
+        v.grad_up,
+        v.grad_down,
     )
 
 

time: 757 us -> 752 us (level)
  Pallas kernels: 391 us -> 413 us
  waiting for transfers between devices: 158 us -> 136 us
    pallas_call x2, Pallas kernels: 49.7 us -> 71.3 us  [attn_bwd(): pl.pallas_call(functools.partial(attn_bwd_kernel, width, hd), grid_spec=p...]
    ppermute x22, waiting for transfers between devices: 42.7 us -> 26.3 us  [x_swap(): return lax.ppermute(v, 'fsdp', X_SWAP)]
    ppermute x19, waiting for transfers between devices: 50.4 us -> 42.1 us  [y_swap(): return lax.ppermute(v, 'ctx', Y_SWAP)]
    unnamed x179 -> x177, local copies, waits for them, and re-layouts: 50.9 us -> 49.3 us
  transfers between devices with their start and end apart: 95 -> 95, of which waited for: 28 -> 30; matrix products, arithmetic and copies ran while one was open for 5% -> 5% of each run, Pallas kernels for 47% -> 50%
where the time goes in v18:
time: 752 us; the launch traced here: 742 us
  Pallas kernels  413 us (55%)
  waiting for transfers between devices  136 us (18%)
  starting transfers between devices  82 us (11%)
  local copies, waits for them, and re-layouts  63.4 us (8%)
  other arithmetic  28.5 us (4%)
  between operations  18.9 us (3%)
    pallas_call x4, Pallas kernels, ffn_bwd(): pl.pallas_call(functools.partial(ffn_bwd_kernel, steps, plan, first), gri...  101 us
    pallas_call x2, Pallas kernels, attn_bwd(): pl.pallas_call(functools.partial(attn_bwd_kernel, width, hd), grid_spec=p...  71.3 us
    pallas_call x3, Pallas kernels, ffn_fwd(): pl.pallas_call(functools.partial(ffn_fwd_kernel, tile, [plan for plan, _...  61 us
    unnamed x177, local copies, waits for them, and re-layouts  49.3 us
    ppermute x19, waiting for transfers between devices, y_swap(): return lax.ppermute(v, 'ctx', Y_SWAP)  42.1 us
    pallas_call x2, Pallas kernels, attn_fwd(): pl.pallas_call(functools.partial(attn_fwd_kernel, width, hd), grid_spec=p...  34.1 us
    pallas_call x6, Pallas kernels, sums(): pl.pallas_call(functools.partial(sums_kernel, jobs, len(arrays)), grid_sp...  33.6 us
    ppermute x22, waiting for transfers between devices, x_swap(): return lax.ppermute(v, 'fsdp', X_SWAP)  26.3 us
  transfers between devices with their start and end apart: 95, of which 30 were waited for; matrix products, arithmetic and copies ran while one was open for 5% of the time, Pallas kernels for 50%

profile of v18, /device:TPU:0, one launch (start us, length us, event | category | flops | bytes accessed | tf_op | source)
XLA Modules:
  0.0 741.5 jit_solution(1725956422169225791)
XLA Ops:
  86.7 13.1 %collective-permute-done.15.rest_4_.rest_0_ = bf16[256,1152]{1,0:T(8,128)(2,1)} collective-permute-done((bf16[256,1152]{1,0:T(8,128)(2,1)}, bf16[256,1152]{1,0:T(8,128)(2,1)}, u32[]{:S(2)}, u32[]{:S(2)}) %collective-permute-start.15) | collective-permute-done | bytes 589856 | tf_op jit(solution)/shard_map/ppermute | solution.py:1641
  102.2 17.1 %attn_fwd.2 = (bf16[1024,256]{1,0:T(8,128)(2,1)}, bf16[1024,256]{1,0:T(8,128)(2,1)}, f32[2,2,2048]{2,1,0:T(2,128)}) custom-call(s32[4]{0:T(128)} %copy-done.23, bf16[512,1024]{1,0:T(8,128)(2,1)} %copy-done.30, bf16[512,1024]{1,0:T(8,128)(2,1)} %copy-done.66), custom_call_target="tpu_custom_call" | custom-call | flops 4398046511104 | bytes 1073741824 | tf_op jit(solution)/shard_map/attn_fwd/pallas_call | solution.py:778
  127.6 17.1 %attn_fwd.3 = (bf16[1024,256]{1,0:T(8,128)(2,1)}, bf16[1024,256]{1,0:T(8,128)(2,1)}, f32[2,2,2048]{2,1,0:T(2,128)}) custom-call(s32[4]{0:T(128)} %copy-done.23, bf16[512,1024]{1,0:T(8,128)(2,1)} %copy-done.29, bf16[512,1024]{1,0:T(8,128)(2,1)} %collective-permute-done.17.got_ref), custom_call_target="tpu_custom_call" | custom-call | flops 4398046511104 | bytes 1073741824 | tf_op jit(solution)/shard_map/attn_fwd/pallas_call | solution.py:778
  148.4 12.4 %collective-permute-done.27.refs_8_ = bf16[1024,256]{1,0:T(8,128)(2,1)S(1)} collective-permute-done((bf16[1024,256]{1,0:T(8,128)(2,1)}, bf16[1024,256]{1,0:T(8,128)(2,1)S(1)}, u32[]{:S(2)}, u32[]{:S(2)}) %collective-permute-start.27) | collective-permute-done | bytes 524320 | tf_op jit(solution)/shard_map/ppermute | solution.py:1638
  165.2 10.3 %out_proj.1 = (f32[1024,1024]{1,0:T(8,128)}, bf16[1024,1024]{1,0:T(8,128)(2,1)}, bf16[1024,1024]{1,0:T(8,128)(2,1)}, bf16[4,1024,256]{2,1,0:T(8,128)(2,1)}) custom-call(s32[4]{0:T(128)} %copy-done.23, bf16[1024,256]{1,0:T(8,128)(2,1)} %constant_dynamic-update-slice_fusion.refs_0_, bf16[1024,256]{1,0:T(8,128)(2,1)} %collective-permute-done.25.refs_1_, ...), custom_call_target="tpu_custom_call" | custom-call | flops 4398046511104 | bytes 1073741824 | tf_op jit(solution)/shard_map/out_proj/pallas_call | solution.py:1004
  186.1 27.2 %ffn_fwd.3 = (bf16[2,1024,2304]{2,1,0:T(8,128)(2,1)}, bf16[2,1024,1152]{2,1,0:T(8,128)(2,1)}, f32[1024,1024]{1,0:T(8,128)}) custom-call(s32[4]{0:T(128)} %copy-done.23, f32[1]{0:T(128)} %bitcast.4.scale, bf16[1024,1024]{1,0:T(8,128)(2,1)} %get-tuple-element.1783.x_ref, f32[1024,1024]{1,0:T(8,128)} %get-tuple-element.2341.in_ref.refs_5_, ...), custom_call_target="tpu_custom_call" | custom-call | flops 4398046511104 | bytes 1073741824 | tf_op jit(solution)/shard_map/ffn_fwd/pallas_call | solution.py:1295
  220.7 15.6 %ffn_fwd.4 = (bf16[1,1024,2304]{2,1,0:T(8,128)(2,1)}, bf16[1,1024,1152]{2,1,0:T(8,128)(2,1)}, f32[1024,1024]{1,0:T(8,128)}) custom-call(s32[4]{0:T(128)} %copy-done.23, f32[1]{0:T(128)} %bitcast.4.scale, bf16[1024,1024]{1,0:T(8,128)(2,1)} %get-tuple-element.1783.x_ref, f32[1024,1024]{1,0:T(8,128)} %get-tuple-element.1683.in_ref, ...), custom_call_target="tpu_custom_call" | custom-call | flops 4398046511104 | bytes 1073741824 | tf_op jit(solution)/shard_map/ffn_fwd/pallas_call | solution.py:1295
  240.5 18.1 %ffn_fwd.5 = (bf16[1,1024,2304]{2,1,0:T(8,128)(2,1)}, bf16[1,1024,1152]{2,1,0:T(8,128)(2,1)}, bf16[1024,1024]{1,0:T(8,128)(2,1)}, f32[1024,1024]{1,0:T(8,128)}, ...) custom-call(s32[4]{0:T(128)} %copy-done.23, f32[1]{0:T(128)} %bitcast.4.scale, ...), custom_call_target="tpu_custom_call" | custom-call | flops 4398046511104 | bytes 1073741824 | tf_op jit(solution)/shard_map/ffn_fwd/pallas_call | solution.py:1295
  258.6 24.8 %ffn_bwd.4 = (f32[1024,1024]{1,0:T(8,128)}, bf16[512,3456]{1,0:T(8,128)(2,1)}, bf16[512,3456]{1,0:T(8,128)(2,1)}) custom-call(bf16[1024,1024]{1,0:T(8,128)(2,1)} %get-tuple-element.2270.low_ref, bf16[1,1024,2304]{2,1,0:T(8,128)(2,1)} %get-tuple-element.1906.act_ref, bf16[1,1024,1152]{2,1,0:T(8,128)(2,1)} %get-tuple-element.1926.hid_ref, ...), custom_call_target="tpu_custom_call" | custom-call | flops 12880000000 | bytes 3144531 | tf_op jit(solution)/shard_map/ffn_bwd/pallas_call | solution.py:1377
  283.7 25.7 %ffn_bwd.5 = (f32[1024,1024]{1,0:T(8,128)}, bf16[512,3456]{1,0:T(8,128)(2,1)}, bf16[512,3456]{1,0:T(8,128)(2,1)}) custom-call(bf16[1024,1024]{1,0:T(8,128)(2,1)} %get-tuple-element.2270.low_ref, bf16[2,1024,2304]{2,1,0:T(8,128)(2,1)} %get-tuple-element.2254.act_ref, ...), custom_call_target="tpu_custom_call", output_to_operand_aliasing={{0}: (15, {})} | custom-call | flops 12880000000 | bytes 3144531 | tf_op jit(solution)/shard_map/ffn_bwd/pallas_call | solution.py:1377
  317.5 25.5 %ffn_bwd.6 = (f32[1024,1024]{1,0:T(8,128)}, bf16[512,3456]{1,0:T(8,128)(2,1)}, bf16[512,3456]{1,0:T(8,128)(2,1)}) custom-call(bf16[1024,1024]{1,0:T(8,128)(2,1)} %get-tuple-element.2270.low_ref, bf16[1,1024,2304]{2,1,0:T(8,128)(2,1)} %get-tuple-element.2182.act_ref, ...), custom_call_target="tpu_custom_call", output_to_operand_aliasing={{0}: (17, {})} | custom-call | flops 12880000000 | bytes 3144531 | tf_op jit(solution)/shard_map/ffn_bwd/pallas_call | solution.py:1377
  352.4 25.3 %ffn_bwd.7 = (f32[1024,1024]{1,0:T(8,128)}, bf16[512,3456]{1,0:T(8,128)(2,1)}, bf16[512,3456]{1,0:T(8,128)(2,1)}) custom-call(bf16[1024,1024]{1,0:T(8,128)(2,1)} %get-tuple-element.2270.low_ref, bf16[2,1024,2304]{2,1,0:T(8,128)(2,1)} %get-tuple-element.2254.act_ref, ...), custom_call_target="tpu_custom_call", output_to_operand_aliasing={{0}: (9, {})} | custom-call | flops 12880000000 | bytes 3144531 | tf_op jit(solution)/shard_map/ffn_bwd/pallas_call | solution.py:1377
  387.2 12.5 %norm_two_back.1 = (f32[1024,1024]{1,0:T(8,128)}, bf16[1024,1024]{1,0:T(8,128)(2,1)}, bf16[1024,256]{1,0:T(8,128)(2,1)}, bf16[1024,256]{1,0:T(8,128)(2,1)}, bf16...) custom-call(s32[4]{0:T(128)} %copy-done.23, ...), custom_call_target="tpu_custom_call" | custom-call | flops 6209999872 | bytes 1516113 | tf_op jit(solution)/shard_map/norm_two_back/pallas_call | solution.py:1062
  420.6 35.9 %attn_bwd.2 = (bf16[512,1024]{1,0:T(8,128)(2,1)}, bf16[512,1024]{1,0:T(8,128)(2,1)}) custom-call(s32[4]{0:T(128)} %copy-done.23, bf16[512,1024]{1,0:T(8,128)(2,1)} %copy-done.30, bf16[512,1024]{1,0:T(8,128)(2,1)} %copy-done.66, bf16[1024,256]{1,0:T(8,128)(2,1)} %get-tuple-element.2380.refs_5_.ok_ref, bf16[1024,256]{1,0:T(8,128)(2,1)} %get-tuple-element.2381.os_ref, ...), custom_call_target="tpu_custom_call" | custom-call | flops 18630000640 | bytes 4548339 | tf_op jit(solution)/shard_map/attn_bwd/pallas_call | solution.py:939
  468.1 35.4 %attn_bwd.3 = (bf16[512,1024]{1,0:T(8,128)(2,1)}, bf16[512,1024]{1,0:T(8,128)(2,1)}) custom-call(s32[4]{0:T(128)} %copy-done.23, bf16[512,1024]{1,0:T(8,128)(2,1)} %copy-done.29, bf16[512,1024]{1,0:T(8,128)(2,1)} %collective-permute-done.17.got_ref, bf16[1024,256]{1,0:T(8,128)(2,1)} %get-tuple-element.2438.refs_6_.ok_ref, ...), custom_call_target="tpu_custom_call" | custom-call | flops 18630000640 | bytes 4548339 | tf_op jit(solution)/shard_map/attn_bwd/pallas_call | solution.py:939
  537.2 8.8 %norm_one_back.2 = (bf16[512,1024]{1,0:T(8,128)(2,1)}, f32[1,1024]{1,0:T(1,128)}) custom-call(s32[4]{0:T(128)} %copy-done.23, bf16[512,512]{1,0:T(8,128)(2,1)} %copy-done.2, bf16[768,512]{1,0:T(8,128)(2,1)} %copy-done.1, bf16[768,512]{1,0:T(8,128)(2,1)} %collective-permute-done.10.refs_2_, bf16[512,512]{1,0:T(8,128)(2,1)} %copy-done.5, ...), custom_call_target="tpu_custom_call" | custom-call | flops 4398046511104 | bytes 1073741824 | tf_op jit(solution)/shard_map/norm_one_back/pallas_call | solution.py:1119
  546.6 8.9 %norm_one_back.3 = (bf16[512,1024]{1,0:T(8,128)(2,1)}, f32[1,1024]{1,0:T(1,128)}) custom-call(s32[4]{0:T(128)} %copy-done.23, bf16[512,512]{1,0:T(8,128)(2,1)} %copy-done.2, bf16[768,512]{1,0:T(8,128)(2,1)} %copy-done.1, bf16[768,512]{1,0:T(8,128)(2,1)} %collective-permute-done.10.refs_2_, bf16[512,512]{1,0:T(8,128)(2,1)} %copy-done.5, ...), custom_call_target="tpu_custom_call" | custom-call | flops 4398046511104 | bytes 1073741824 | tf_op jit(solution)/shard_map/norm_one_back/pallas_call | solution.py:1119
  556.3 8.7 %collective-permute-done.75.refs_2_ = bf16[128,3456]{1,0:T(8,128)(2,1)} collective-permute-done((bf16[128,3456]{1,0:T(8,128)(2,1)}, bf16[128,3456]{1,0:T(8,128)(2,1)}, u32[]{:S(2)}, u32[]{:S(2)}) %collective-permute-start.75) | collective-permute-done | bytes 884768 | tf_op jit(solution)/shard_map/ppermute | solution.py:1638
  567.2 15.2 %weight_grad.1 = (bf16[4,512,768]{2,1,0:T(8,128)(2,1)}, bf16[4,512,768]{2,1,0:T(8,128)(2,1)}) custom-call(bf16[1024,1024]{1,0:T(8,128)(2,1)} %copy-done, bf16[2,1024,512]{2,1,0:T(8,128)(2,1)} %get-tuple-element.2555.refs_6_.back0_ref, bf16[2,1024,512]{2,1,0:T(8,128)(2,1)} %get-tuple-element.2557.refs_7_.back1_ref, ...), custom_call_target="tpu_custom_call" | custom-call | flops 4398046511104 | bytes 1073741824 | tf_op jit(solution)/shard_map/weight_grad/pallas_call | solution.py:1560
  602.7 12.2 %collective-permute-done.81.refs_1_ = bf16[512,768]{1,0:T(8,128)(2,1)S(1)} collective-permute-done((bf16[512,768]{1,0:T(8,128)(2,1)S(1)}, bf16[512,768]{1,0:T(8,128)(2,1)S(1)}, u32[]{:S(2)}, u32[]{:S(2)}) %collective-permute-start.81) | collective-permute-done | bytes 786464 | tf_op jit(solution)/shard_map/ppermute | solution.py:1632
  627.8 10.9 %collective-permute-done.84.refs_2_ = bf16[512,768]{1,0:T(8,128)(2,1)S(1)} collective-permute-done((bf16[512,768]{1,0:T(8,128)(2,1)}, bf16[512,768]{1,0:T(8,128)(2,1)S(1)}, u32[]{:S(2)}, u32[]{:S(2)}) %collective-permute-start.84) | collective-permute-done | bytes 786464 | tf_op jit(solution)/shard_map/ppermute | solution.py:1638
  650.3 10.4 %collective-permute-done.85.refs_1_ = bf16[128,768]{1,0:T(8,128)(2,1)S(1)} collective-permute-done((bf16[128,768]{1,0:T(8,128)(2,1)S(1)}, bf16[128,768]{1,0:T(8,128)(2,1)S(1)}, u32[]{:S(2)}, u32[]{:S(2)}) %collective-permute-start.85) | collective-permute-done | bytes 196640 | tf_op jit(solution)/shard_map/ppermute | solution.py:1647
  660.7 24.5 %collective-permute-done.86.refs_2_ = bf16[128,768]{1,0:T(8,128)(2,1)S(1)} collective-permute-done((bf16[128,768]{1,0:T(8,128)(2,1)S(1)}, bf16[128,768]{1,0:T(8,128)(2,1)S(1)}, u32[]{:S(2)}, u32[]{:S(2)}) %collective-permute-start.86) | collective-permute-done | bytes 196640 | tf_op jit(solution)/shard_map/ppermute | solution.py:1644
  692.3 10.6 %pad_convert_fusion = f32[4,1024,1024]{2,1,0:T(8,128)} fusion(bf16[4,512,1024]{2,1,0:T(8,128)(2,1)} %bitcast.51), kind=kLoop, calls=%fused_computation.1 | loop fusion | flops 4194304 | bytes 20971520 | tf_op jit(solution)/shard_map/dynamic_update_slice | solution.py:2112
  (448 shorter events, 296.5 us)
Async XLA Ops:
  7.2 457.2 %all-gather.7.cloned.1.call-start = ((), (), s32[]{:S(2)}) async-start(), calls=%async_computation | async-start | bytes 10485760 | tf_op jit(solution)/shard_map/all_gather | solution.py:1869
  56.5 43.3 %collective-permute-start.11 = (bf16[256,3456]{1,0:T(8,128)(2,1)}, bf16[256,3456]{1,0:T(8,128)(2,1)}, u32[]{:S(2)}, u32[]{:S(2)}) collective-permute-start(bf16[256,3456]{1,0:T(8,128)(2,1)} %get-tuple-element.2275.rest_0_), channel_id=1, source_target_pairs={{0,16},{16,0},{8,24},{24,8},{1,17},{17,1},{9,25},{25,9},{2,18},{18... | collective-permute-start | bytes 5308424 | tf_op jit(solution)/shard_map/ppermute | solution.py:1632
  57.4 42.4 %collective-permute-start.16 = (bf16[256,2304]{1,0:T(8,128)(2,1)}, bf16[256,2304]{1,0:T(8,128)(2,1)}, u32[]{:S(2)}, u32[]{:S(2)}) collective-permute-start(bf16[256,2304]{1,0:T(8,128)(2,1)} %get-tuple-element.1369), channel_id=1, source_target_pairs={{0,1},{1,2},{2,3},{3,0},{4,5},{5,6},{6,7},{7,4},{8,9},{9,10},{10,1... | collective-permute-start | bytes 3538952 | tf_op jit(solution)/shard_map/ppermute | solution.py:1641
  75.5 43.7 %collective-permute-start.17 = (bf16[512,1024]{1,0:T(8,128)(2,1)}, bf16[512,1024]{1,0:T(8,128)(2,1)}, u32[]{:S(2)}, u32[]{:S(2)}) collective-permute-start(bf16[512,1024]{1,0:T(8,128)(2,1)} %get-tuple-element.1361), channel_id=1, source_target_pairs={{0,4},{4,0},{1,5},{5,1},{2,6},{6,2},{3,7},{7,3},{8,12},{12,8},{9,1... | collective-permute-start | bytes 3145736 | tf_op jit(solution)/shard_map/ppermute | solution.py:1638
  181.3 32.0 %collective-permute-start.41 = (bf16[256,2304]{1,0:T(8,128)(2,1)}, bf16[256,2304]{1,0:T(8,128)(2,1)}, u32[]{:S(2)}, u32[]{:S(2)}) collective-permute-start(bf16[256,2304]{1,0:T(8,128)(2,1)} %collective-permute-done.16.rest_5_.rest_1_), channel_id=1, source_target_pairs={{0,1},{1,2},{2,3},{3,0},{4,5},{5,6},{6,7},{7,4},{8,9},{9,10},{10,1... | collective-permute-start | bytes 3538952 | tf_op jit(solution)/shard_map/ppermute | solution.py:1641
  283.6 408.7 %all-gather.9.cloned.1.call-start = ((), (), s32[]{:S(2)}) async-start(), calls=%async_computation.1 | async-start | bytes 5242880 | tf_op jit(solution)/shard_map/all_gather | solution.py:2028
  309.4 33.7 %collective-permute-start.56 = (bf16[512,3456]{1,0:T(8,128)(2,1)}, bf16[512,3456]{1,0:T(8,128)(2,1)}, u32[]{:S(2)}, u32[]{:S(2)}) collective-permute-start(bf16[512,3456]{1,0:T(8,128)(2,1)} %get-tuple-element.2184), channel_id=1, source_target_pairs={{0,8},{8,0},{16,24},{24,16},{1,9},{9,1},{17,25},{25,17},{2,10},{10... | collective-permute-start | bytes 10616840 | tf_op jit(solution)/shard_map/ppermute | solution.py:1635
  344.0 33.8 %collective-permute-start.58 = (bf16[512,3456]{1,0:T(8,128)(2,1)}, bf16[512,3456]{1,0:T(8,128)(2,1)S(1)}, u32[]{:S(2)}, u32[]{:S(2)}) collective-permute-start(bf16[512,3456]{1,0:T(8,128)(2,1)} %get-tuple-element.2257), channel_id=1, source_target_pairs={{0,8},{8,0},{16,24},{24,16},{1,9},{9,1},{17,25},{25,17},{2,10},{10... | collective-permute-start | bytes 10616840 | tf_op jit(solution)/shard_map/ppermute | solution.py:1635
  401.1 55.4 %collective-permute-start.67 = (bf16[1024,256]{1,0:T(8,128)(2,1)}, bf16[1024,256]{1,0:T(8,128)(2,1)S(1)}, u32[]{:S(2)}, u32[]{:S(2)}) collective-permute-start(bf16[1024,256]{1,0:T(8,128)(2,1)} %get-tuple-element.2403), channel_id=1, source_target_pairs={{0,4},{4,0},{1,5},{5,1},{2,6},{6,2},{3,7},{7,3},{8,12},{12,8},{9,1... | collective-permute-start | bytes 1572872 | tf_op jit(solution)/shard_map/ppermute | solution.py:1638
  401.8 54.7 %collective-permute-start.64 = (bf16[128,3456]{1,0:T(8,128)(2,1)}, bf16[128,3456]{1,0:T(8,128)(2,1)}, u32[]{:S(2)}, u32[]{:S(2)}) collective-permute-start(bf16[128,3456]{1,0:T(8,128)(2,1)} %get-tuple-element.2394), channel_id=1, source_target_pairs={{0,3},{1,0},{2,1},{3,2},{4,7},{5,4},{6,5},{7,6},{8,11},{9,8},{10,9... | collective-permute-start | bytes 2654216 | tf_op jit(solution)/shard_map/ppermute | solution.py:1647
  416.9 39.7 %collective-permute-start.68 = (bf16[128,3456]{1,0:T(8,128)(2,1)}, bf16[128,3456]{1,0:T(8,128)(2,1)S(1)}, u32[]{:S(2)}, u32[]{:S(2)}) collective-permute-start(bf16[128,3456]{1,0:T(8,128)(2,1)} %get-tuple-element.2424), channel_id=1, source_target_pairs={{0,4},{4,0},{1,5},{5,1},{2,6},{6,2},{3,7},{7,3},{8,12},{12,8},{9,1... | collective-permute-start | bytes 2654216 | tf_op jit(solution)/shard_map/ppermute | solution.py:1638
  418.6 38.0 %collective-permute-start.65 = (bf16[128,3456]{1,0:T(8,128)(2,1)}, bf16[128,3456]{1,0:T(8,128)(2,1)S(1)}, u32[]{:S(2)}, u32[]{:S(2)}) collective-permute-start(bf16[128,3456]{1,0:T(8,128)(2,1)} %get-tuple-element.2395), channel_id=1, source_target_pairs={{0,16},{16,0},{8,24},{24,8},{1,17},{17,1},{9,25},{25,9},{2,18},{18... | collective-permute-start | bytes 2654216 | tf_op jit(solution)/shard_map/ppermute | solution.py:1632
  419.2 39.5 %collective-permute-start.66 = (bf16[128,3456]{1,0:T(8,128)(2,1)}, bf16[128,3456]{1,0:T(8,128)(2,1)S(1)}, u32[]{:S(2)}, u32[]{:S(2)}) collective-permute-start(bf16[128,3456]{1,0:T(8,128)(2,1)} %get-tuple-element.2396), channel_id=1, source_target_pairs={{0,16},{16,0},{8,24},{24,8},{1,17},{17,1},{9,25},{25,9},{2,18},{18... | collective-permute-start | bytes 2654216 | tf_op jit(solution)/shard_map/ppermute | solution.py:1632
  464.0 39.6 %collective-permute-start.72 = (bf16[128,3456]{1,0:T(8,128)(2,1)}, bf16[128,3456]{1,0:T(8,128)(2,1)S(1)}, u32[]{:S(2)}, u32[]{:S(2)}) collective-permute-start(bf16[128,3456]{1,0:T(8,128)(2,1)} %get-tuple-element.2447), channel_id=1, source_target_pairs={{0,4},{4,0},{1,5},{5,1},{2,6},{6,2},{3,7},{7,3},{8,12},{12,8},{9,1... | collective-permute-start | bytes 2654216 | tf_op jit(solution)/shard_map/ppermute | solution.py:1638
  464.4 42.4 %collective-permute-start.71 = (bf16[512,1024]{1,0:T(8,128)(2,1)}, bf16[512,1024]{1,0:T(8,128)(2,1)S(1)}, u32[]{:S(2)}, u32[]{:S(2)}) collective-permute-start(bf16[512,1024]{1,0:T(8,128)(2,1)} %get-tuple-element.2435), channel_id=1, source_target_pairs={{0,4},{4,0},{1,5},{5,1},{2,6},{6,2},{3,7},{7,3},{8,12},{12,8},{9,1... | collective-permute-start | bytes 3145736 | tf_op jit(solution)/shard_map/ppermute | solution.py:1638
  466.0 37.5 %collective-permute-start.69 = (bf16[128,3456]{1,0:T(8,128)(2,1)}, bf16[128,3456]{1,0:T(8,128)(2,1)S(1)}, u32[]{:S(2)}, u32[]{:S(2)}) collective-permute-start(bf16[128,3456]{1,0:T(8,128)(2,1)} %get-tuple-element.2455), channel_id=1, source_target_pairs={{0,16},{16,0},{8,24},{24,8},{1,17},{17,1},{9,25},{25,9},{2,18},{18... | collective-permute-start | bytes 2654216 | tf_op jit(solution)/shard_map/ppermute | solution.py:1632
  466.7 38.1 %collective-permute-start.70 = (bf16[128,3456]{1,0:T(8,128)(2,1)}, bf16[128,3456]{1,0:T(8,128)(2,1)}, u32[]{:S(2)}, u32[]{:S(2)}) collective-permute-start(bf16[128,3456]{1,0:T(8,128)(2,1)} %get-tuple-element.2456), channel_id=1, source_target_pairs={{0,16},{16,0},{8,24},{24,8},{1,17},{17,1},{9,25},{25,9},{2,18},{18... | collective-permute-start | bytes 2654216 | tf_op jit(solution)/shard_map/ppermute | solution.py:1632
  507.2 49.1 %collective-permute-start.76 = (bf16[128,3456]{1,0:T(8,128)(2,1)}, bf16[128,3456]{1,0:T(8,128)(2,1)}, u32[]{:S(2)}, u32[]{:S(2)}) collective-permute-start(bf16[128,3456]{1,0:T(8,128)(2,1)} %get-tuple-element.2448), channel_id=1, source_target_pairs={{0,3},{1,0},{2,1},{3,2},{4,7},{5,4},{6,5},{7,6},{8,11},{9,8},{10,9... | collective-permute-start | bytes 2654216 | tf_op jit(solution)/shard_map/ppermute | solution.py:1647
  516.4 39.8 %collective-permute-start.77 = (bf16[128,3456]{1,0:T(8,128)(2,1)}, bf16[128,3456]{1,0:T(8,128)(2,1)}, u32[]{:S(2)}, u32[]{:S(2)}) collective-permute-start(bf16[128,3456]{1,0:T(8,128)(2,1)} %get-tuple-element.2549), channel_id=1, source_target_pairs={{0,1},{1,2},{2,3},{3,0},{4,5},{5,6},{6,7},{7,4},{8,9},{9,10},{10,1... | collective-permute-start | bytes 2654216 | tf_op jit(solution)/shard_map/ppermute | solution.py:1641
  516.4 39.8 %collective-permute-start.74 = (bf16[128,3456]{1,0:T(8,128)(2,1)}, bf16[128,3456]{1,0:T(8,128)(2,1)}, u32[]{:S(2)}, u32[]{:S(2)}) collective-permute-start(bf16[128,3456]{1,0:T(8,128)(2,1)} %get-tuple-element.2506), channel_id=1, source_target_pairs={{0,16},{16,0},{8,24},{24,8},{1,17},{17,1},{9,25},{25,9},{2,18},{18... | collective-permute-start | bytes 2654216 | tf_op jit(solution)/shard_map/ppermute | solution.py:1632
  546.1 178.5 %all-gather.11.cloned.1.call-start = ((), (), s32[]{:S(2)}) async-start(), calls=%async_computation.2 | async-start | bytes 5242880 | tf_op jit(solution)/shard_map/all_gather | solution.py:2034
  638.7 64.2 %collective-permute-start.88 = (f32[128,3456]{1,0:T(8,128)S(1)}, f32[128,3456]{1,0:T(8,128)}, u32[]{:S(2)}, u32[]{:S(2)}) collective-permute-start(f32[128,3456]{1,0:T(8,128)S(1)} %copy-done.33), channel_id=1, source_target_pairs={{0,4},{4,0},{1,5},{5,1},{2,6},{6,2},{3,7},{7,3},{8,12},{12,8},{9,1... | collective-permute-start | bytes 5308424 | tf_op jit(solution)/shard_map/ppermute | solution.py:1638
  649.5 35.6 %collective-permute-start.86 = (bf16[128,768]{1,0:T(8,128)(2,1)S(1)}, bf16[128,768]{1,0:T(8,128)(2,1)S(1)}, u32[]{:S(2)}, u32[]{:S(2)}) collective-permute-start(bf16[128,768]{1,0:T(8,128)(2,1)S(1)} %get-tuple-element.2677), channel_id=1, source_target_pairs={{0,2},{2,0},{1,3},{3,1},{4,6},{6,4},{5,7},{7,5},{8,10},{10,8},{9,1... | collective-permute-start | bytes 589832 | tf_op jit(solution)/shard_map/ppermute | solution.py:1644
  649.5 35.6 %collective-permute-start.87 = (bf16[128,768]{1,0:T(8,128)(2,1)S(1)}, bf16[128,768]{1,0:T(8,128)(2,1)S(1)}, u32[]{:S(2)}, u32[]{:S(2)}) collective-permute-start(bf16[128,768]{1,0:T(8,128)(2,1)S(1)} %get-tuple-element.2676), channel_id=1, source_target_pairs={{0,1},{1,2},{2,3},{3,0},{4,5},{5,6},{6,7},{7,4},{8,9},{9,10},{10,1... | collective-permute-start | bytes 589832 | tf_op jit(solution)/shard_map/ppermute | solution.py:1641
  (152 other events, 1877.3 us)
Sparse Core Ops, SparseCore 0:
  283.7 166.0 all-gather.6
  546.2 80.4 all-gather.8
  628.2 96.3 all-gather.10

commit v19 on v18

--- a/solution.py
+++ b/solution.py
@@ -1039,9 +1039,9 @@
     unit = resid * rho
     scaled = grad * gain_ref[...]
     back = rho * (scaled - unit * jnp.mean(scaled * unit, axis=-1, keepdims=True))
-    total = gr_ref[...] + back
-    gres_ref[...] = total
+    total = gr_ref[...].astype(F32) + back
     low = total.astype(BF16)
+    gres_ref[...] = low
     gat_ref[...] = total.T.astype(BF16)
 
     @pl.when(pl.program_id(0) == 0)
@@ -1070,7 +1070,7 @@
             + [row],
             scratch_shapes=[pltpu.VMEM((4, width, feats), BF16), pltpu.SemaphoreType.DMA],
         ),
-        out_shape=[shape_of((tok, width), F32), shape_of((width, tok), BF16)]
+        out_shape=[shape_of((tok, width), BF16), shape_of((width, tok), BF16)]
         + [shape_of((tok, feats), BF16)] * 4
         + [shape_of((1, width), F32)],
         compiler_params=settings(1, 60),
@@ -1092,7 +1092,7 @@
     unit = x * rho
     scaled = grad * gain_ref[...]
     back = rho * (scaled - unit * jnp.mean(scaled * unit, axis=-1, keepdims=True))
-    total = (gres_ref[...] + back).astype(BF16)
+    total = (gres_ref[...].astype(F32) + back).astype(BF16)
     for p, mask in enumerate(MASKS):
         at = pl.multiple_of(jnp.bitwise_xor(info[1], mask) * quarter, quarter)
         part = total[:, p * quarter : (p + 1) * quarter]
@@ -1173,8 +1173,8 @@
         rest = rest[count:]
     act_ref, hid_ref = rest[:2]
     if last:
-        out_ref, gres_ref, low_ref, lowt_ref, sq_ref = rest[2:7]
-        gate_up, down, total, sems = rest[7:]
+        out_ref, low_ref, lowt_ref, sq_ref = rest[2:6]
+        gate_up, down, total, sems = rest[6:]
     else:
         sum_ref, gate_up, down, total, sems = rest[2:]
     step, part = pl.program_id(0), pl.program_id(1)
@@ -1244,7 +1244,6 @@
             error = valid * (value - teach_ref[0, :, pl.ds(at, quarter)].astype(F32))
             square = square + error * error
             grad = error * scale[0]
-            gres_ref[:, cols] = grad
             low_ref[:, cols] = grad.astype(BF16)
             lowt_ref[cols, :] = grad.T.astype(BF16)
 
@@ -1278,13 +1277,11 @@
         out_specs += [
             tiles(width),
             tiles(width),
-            tiles(width),
             pl.BlockSpec((width, tile), lambda s, i, info: (0, leave(s, i))),
             pl.BlockSpec((1, width // 4), lambda s, i, info: (0, 0)),
         ]
         out_shape += [
             shape_of((tok, width), BF16),
-            shape_of((tok, width), F32),
             shape_of((tok, width), BF16),
             shape_of((width, tok), BF16),
             shape_of((1, width // 4), F32),
@@ -1839,7 +1836,7 @@
 
     weights2 = v.two + v.two_far + v.two_cores
     weights2 += [core_swap(part) for part in v.two_far[1:]]
-    acts_c, hiddens_c, result_low, grad_result, grad_low, grad_low_t, square = ffn_fwd(
+    acts_c, hiddens_c, result_low, grad_low, grad_low_t, square = ffn_fwd(
         info, v.scale, v.normed_two, v.sum_b, teacher, [(plan_mixed, weights2)], units, 256
     )
     v.update(
@@ -1847,7 +1844,6 @@
         acts_c=acts_c,
         hiddens_c=hiddens_c,
         result_low=result_low,
-        grad_result=grad_result,
         grad_low=grad_low,
         grad_low_t=grad_low_t,
         square=square,
@@ -1927,7 +1923,7 @@
         info,
         after(v.total, sum3[0]),
         v.resid,
-        v.grad_result,
+        v.grad_low,
         v.gain_two,
         (plan_out, v.weights_out),
         256,

time: 752 us -> 752 us (level)
  transfers between devices with their start and end apart: 95 -> 95, of which waited for: 30 -> 28; matrix products, arithmetic and copies ran while one was open for 5% -> 6% of each run, Pallas kernels for 50% -> 50%
where the time goes in v19:
time: 752 us; the launch traced here: 742 us
  Pallas kernels  411 us (55%)
  waiting for transfers between devices  137 us (18%)
  starting transfers between devices  82.5 us (11%)
  local copies, waits for them, and re-layouts  63.5 us (8%)
  other arithmetic  28.5 us (4%)
  between operations  19 us (3%)
    pallas_call x4, Pallas kernels, ffn_bwd(): pl.pallas_call(functools.partial(ffn_bwd_kernel, steps, plan, first), gri...  101 us
    pallas_call x2, Pallas kernels, attn_bwd(): pl.pallas_call(functools.partial(attn_bwd_kernel, width, hd), grid_spec=p...  71.3 us
    pallas_call x3, Pallas kernels, ffn_fwd(): pl.pallas_call(functools.partial(ffn_fwd_kernel, tile, [plan for plan, _...  60.7 us
    unnamed x177, local copies, waits for them, and re-layouts  49.4 us
    ppermute x19, waiting for transfers between devices, y_swap(): return lax.ppermute(v, 'ctx', Y_SWAP)  42 us
    pallas_call x2, Pallas kernels, attn_fwd(): pl.pallas_call(functools.partial(attn_fwd_kernel, width, hd), grid_spec=p...  34.1 us
    pallas_call x6, Pallas kernels, sums(): pl.pallas_call(functools.partial(sums_kernel, jobs, len(arrays)), grid_sp...  33.6 us
    ppermute x22, waiting for transfers between devices, x_swap(): return lax.ppermute(v, 'fsdp', X_SWAP)  27.5 us
  transfers between devices with their start and end apart: 95, of which 28 were waited for; matrix products, arithmetic and copies ran while one was open for 6% of the time, Pallas kernels for 50%

profile of v19, /device:TPU:0, one launch (start us, length us, event | category | flops | bytes accessed | tf_op | source)
XLA Modules:
  0.0 741.5 jit_solution(3612045700126943802)
XLA Ops:
  86.7 13.1 %collective-permute-done.15.rest_4_.rest_0_ = bf16[256,1152]{1,0:T(8,128)(2,1)} collective-permute-done((bf16[256,1152]{1,0:T(8,128)(2,1)}, bf16[256,1152]{1,0:T(8,128)(2,1)}, u32[]{:S(2)}, u32[]{:S(2)}) %collective-permute-start.15) | collective-permute-done | bytes 589856 | tf_op jit(solution)/shard_map/ppermute | solution.py:1638
  102.2 17.1 %attn_fwd.2 = (bf16[1024,256]{1,0:T(8,128)(2,1)}, bf16[1024,256]{1,0:T(8,128)(2,1)}, f32[2,2,2048]{2,1,0:T(2,128)}) custom-call(s32[4]{0:T(128)} %copy-done.23, bf16[512,1024]{1,0:T(8,128)(2,1)} %copy-done.30, bf16[512,1024]{1,0:T(8,128)(2,1)} %copy-done.66), custom_call_target="tpu_custom_call" | custom-call | flops 4398046511104 | bytes 1073741824 | tf_op jit(solution)/shard_map/attn_fwd/pallas_call | solution.py:778
  127.6 17.1 %attn_fwd.3 = (bf16[1024,256]{1,0:T(8,128)(2,1)}, bf16[1024,256]{1,0:T(8,128)(2,1)}, f32[2,2,2048]{2,1,0:T(2,128)}) custom-call(s32[4]{0:T(128)} %copy-done.23, bf16[512,1024]{1,0:T(8,128)(2,1)} %copy-done.29, bf16[512,1024]{1,0:T(8,128)(2,1)} %collective-permute-done.17.got_ref), custom_call_target="tpu_custom_call" | custom-call | flops 4398046511104 | bytes 1073741824 | tf_op jit(solution)/shard_map/attn_fwd/pallas_call | solution.py:778
  149.6 11.7 %collective-permute-done.27.refs_8_ = bf16[1024,256]{1,0:T(8,128)(2,1)S(1)} collective-permute-done((bf16[1024,256]{1,0:T(8,128)(2,1)}, bf16[1024,256]{1,0:T(8,128)(2,1)S(1)}, u32[]{:S(2)}, u32[]{:S(2)}) %collective-permute-start.27) | collective-permute-done | bytes 524320 | tf_op jit(solution)/shard_map/ppermute | solution.py:1635
  165.3 10.3 %out_proj.1 = (f32[1024,1024]{1,0:T(8,128)}, bf16[1024,1024]{1,0:T(8,128)(2,1)}, bf16[1024,1024]{1,0:T(8,128)(2,1)}, bf16[4,1024,256]{2,1,0:T(8,128)(2,1)}) custom-call(s32[4]{0:T(128)} %copy-done.23, bf16[1024,256]{1,0:T(8,128)(2,1)} %constant_dynamic-update-slice_fusion.refs_0_, bf16[1024,256]{1,0:T(8,128)(2,1)} %collective-permute-done.25.refs_1_, ...), custom_call_target="tpu_custom_call" | custom-call | flops 4398046511104 | bytes 1073741824 | tf_op jit(solution)/shard_map/out_proj/pallas_call | solution.py:1004
  186.6 27.2 %ffn_fwd.3 = (bf16[2,1024,2304]{2,1,0:T(8,128)(2,1)}, bf16[2,1024,1152]{2,1,0:T(8,128)(2,1)}, f32[1024,1024]{1,0:T(8,128)}) custom-call(s32[4]{0:T(128)} %copy-done.23, f32[1]{0:T(128)} %bitcast.4.scale, bf16[1024,1024]{1,0:T(8,128)(2,1)} %get-tuple-element.1778.x_ref, f32[1024,1024]{1,0:T(8,128)} %get-tuple-element.2331.in_ref.refs_5_, ...), custom_call_target="tpu_custom_call" | custom-call | flops 4398046511104 | bytes 1073741824 | tf_op jit(solution)/shard_map/ffn_fwd/pallas_call | solution.py:1292
  221.2 15.7 %ffn_fwd.4 = (bf16[1,1024,2304]{2,1,0:T(8,128)(2,1)}, bf16[1,1024,1152]{2,1,0:T(8,128)(2,1)}, f32[1024,1024]{1,0:T(8,128)}) custom-call(s32[4]{0:T(128)} %copy-done.23, f32[1]{0:T(128)} %bitcast.4.scale, bf16[1024,1024]{1,0:T(8,128)(2,1)} %get-tuple-element.1778.x_ref, f32[1024,1024]{1,0:T(8,128)} %get-tuple-element.1678.in_ref, ...), custom_call_target="tpu_custom_call" | custom-call | flops 4398046511104 | bytes 1073741824 | tf_op jit(solution)/shard_map/ffn_fwd/pallas_call | solution.py:1292
  241.0 17.7 %ffn_fwd.5 = (bf16[1,1024,2304]{2,1,0:T(8,128)(2,1)}, bf16[1,1024,1152]{2,1,0:T(8,128)(2,1)}, bf16[1024,1024]{1,0:T(8,128)(2,1)}, bf16[1024,1024]{1,0:T(8,128)(2...) custom-call(s32[4]{0:T(128)} %copy-done.23, f32[1]{0:T(128)} %bitcast.4.scale, ...), custom_call_target="tpu_custom_call" | custom-call | flops 4398046511104 | bytes 1073741824 | tf_op jit(solution)/shard_map/ffn_fwd/pallas_call | solution.py:1292
  258.8 24.8 %ffn_bwd.4 = (f32[1024,1024]{1,0:T(8,128)}, bf16[512,3456]{1,0:T(8,128)(2,1)}, bf16[512,3456]{1,0:T(8,128)(2,1)}) custom-call(bf16[1024,1024]{1,0:T(8,128)(2,1)} %get-tuple-element.2332.low_ref.refs_6_, bf16[1,1024,2304]{2,1,0:T(8,128)(2,1)} %get-tuple-element.1900.act_ref, bf16[1,1024,1152]{2,1,0:T(8,128)(2,1)} %get-tuple-element.1919.hid_ref, ...), custom_call_target="tpu_custom_call" | custom-call | flops 12880000000 | bytes 3144531 | tf_op jit(solution)/shard_map/ffn_bwd/pallas_call | solution.py:1374
  283.8 25.7 %ffn_bwd.5 = (f32[1024,1024]{1,0:T(8,128)}, bf16[512,3456]{1,0:T(8,128)(2,1)}, bf16[512,3456]{1,0:T(8,128)(2,1)}) custom-call(bf16[1024,1024]{1,0:T(8,128)(2,1)} %get-tuple-element.2332.low_ref.refs_6_, bf16[2,1024,2304]{2,1,0:T(8,128)(2,1)} %get-tuple-element.2245.act_ref, ...), custom_call_target="tpu_custom_call", output_to_operand_aliasing={{0}: (15, {})} | custom-call | flops 12880000000 | bytes 3144531 | tf_op jit(solution)/shard_map/ffn_bwd/pallas_call | solution.py:1374
  317.7 25.5 %ffn_bwd.6 = (f32[1024,1024]{1,0:T(8,128)}, bf16[512,3456]{1,0:T(8,128)(2,1)}, bf16[512,3456]{1,0:T(8,128)(2,1)}) custom-call(bf16[1024,1024]{1,0:T(8,128)(2,1)} %get-tuple-element.2332.low_ref.refs_6_, bf16[1,1024,2304]{2,1,0:T(8,128)(2,1)} %get-tuple-element.2174.act_ref, ...), custom_call_target="tpu_custom_call", output_to_operand_aliasing={{0}: (17, {})} | custom-call | flops 12880000000 | bytes 3144531 | tf_op jit(solution)/shard_map/ffn_bwd/pallas_call | solution.py:1374
  352.5 25.4 %ffn_bwd.7 = (f32[1024,1024]{1,0:T(8,128)}, bf16[512,3456]{1,0:T(8,128)(2,1)}, bf16[512,3456]{1,0:T(8,128)(2,1)}) custom-call(bf16[1024,1024]{1,0:T(8,128)(2,1)} %get-tuple-element.2332.low_ref.refs_6_, bf16[2,1024,2304]{2,1,0:T(8,128)(2,1)} %get-tuple-element.2245.act_ref, ...), custom_call_target="tpu_custom_call", output_to_operand_aliasing={{0}: (9, {})} | custom-call | flops 12880000000 | bytes 3144531 | tf_op jit(solution)/shard_map/ffn_bwd/pallas_call | solution.py:1374
  387.4 11.2 %norm_two_back.1 = (bf16[1024,1024]{1,0:T(8,128)(2,1)}, bf16[1024,1024]{1,0:T(8,128)(2,1)}, bf16[1024,256]{1,0:T(8,128)(2,1)}, bf16[1024,256]{1,0:T(8,128)(2,1)}...) custom-call(s32[4]{0:T(128)} %copy-done.23, ...), custom_call_target="tpu_custom_call" | custom-call | flops 6209999872 | bytes 1516113 | tf_op jit(solution)/shard_map/norm_two_back/pallas_call | solution.py:1062
  420.8 35.8 %attn_bwd.2 = (bf16[512,1024]{1,0:T(8,128)(2,1)}, bf16[512,1024]{1,0:T(8,128)(2,1)}) custom-call(s32[4]{0:T(128)} %copy-done.23, bf16[512,1024]{1,0:T(8,128)(2,1)} %copy-done.30, bf16[512,1024]{1,0:T(8,128)(2,1)} %copy-done.66, bf16[1024,256]{1,0:T(8,128)(2,1)} %get-tuple-element.2370.refs_5_.ok_ref, bf16[1024,256]{1,0:T(8,128)(2,1)} %get-tuple-element.2371.os_ref, ...), custom_call_target="tpu_custom_call" | custom-call | flops 18630000640 | bytes 4548339 | tf_op jit(solution)/shard_map/attn_bwd/pallas_call | solution.py:939
  468.3 35.5 %attn_bwd.3 = (bf16[512,1024]{1,0:T(8,128)(2,1)}, bf16[512,1024]{1,0:T(8,128)(2,1)}) custom-call(s32[4]{0:T(128)} %copy-done.23, bf16[512,1024]{1,0:T(8,128)(2,1)} %copy-done.29, bf16[512,1024]{1,0:T(8,128)(2,1)} %collective-permute-done.17.got_ref, bf16[1024,256]{1,0:T(8,128)(2,1)} %get-tuple-element.2428.refs_6_.ok_ref, ...), custom_call_target="tpu_custom_call" | custom-call | flops 18630000640 | bytes 4548339 | tf_op jit(solution)/shard_map/attn_bwd/pallas_call | solution.py:939
  537.5 8.6 %norm_one_back.2 = (bf16[512,1024]{1,0:T(8,128)(2,1)}, f32[1,1024]{1,0:T(1,128)}) custom-call(s32[4]{0:T(128)} %copy-done.23, bf16[512,512]{1,0:T(8,128)(2,1)} %copy-done.2, bf16[768,512]{1,0:T(8,128)(2,1)} %copy-done.1, bf16[768,512]{1,0:T(8,128)(2,1)} %collective-permute-done.10.refs_2_, bf16[512,512]{1,0:T(8,128)(2,1)} %copy-done.5, ...), custom_call_target="tpu_custom_call" | custom-call | flops 4398046511104 | bytes 1073741824 | tf_op jit(solution)/shard_map/norm_one_back/pallas_call | solution.py:1119
  546.6 8.8 %norm_one_back.3 = (bf16[512,1024]{1,0:T(8,128)(2,1)}, f32[1,1024]{1,0:T(1,128)}) custom-call(s32[4]{0:T(128)} %copy-done.23, bf16[512,512]{1,0:T(8,128)(2,1)} %copy-done.2, bf16[768,512]{1,0:T(8,128)(2,1)} %copy-done.1, bf16[768,512]{1,0:T(8,128)(2,1)} %collective-permute-done.10.refs_2_, bf16[512,512]{1,0:T(8,128)(2,1)} %copy-done.5, ...), custom_call_target="tpu_custom_call" | custom-call | flops 4398046511104 | bytes 1073741824 | tf_op jit(solution)/shard_map/norm_one_back/pallas_call | solution.py:1119
  556.1 8.9 %collective-permute-done.75.refs_2_ = bf16[128,3456]{1,0:T(8,128)(2,1)} collective-permute-done((bf16[128,3456]{1,0:T(8,128)(2,1)}, bf16[128,3456]{1,0:T(8,128)(2,1)}, u32[]{:S(2)}, u32[]{:S(2)}) %collective-permute-start.75) | collective-permute-done | bytes 884768 | tf_op jit(solution)/shard_map/ppermute | solution.py:1635
  567.3 15.2 %weight_grad.1 = (bf16[4,512,768]{2,1,0:T(8,128)(2,1)}, bf16[4,512,768]{2,1,0:T(8,128)(2,1)}) custom-call(bf16[1024,1024]{1,0:T(8,128)(2,1)} %copy-done, bf16[2,1024,512]{2,1,0:T(8,128)(2,1)} %get-tuple-element.2545.refs_6_.back0_ref, bf16[2,1024,512]{2,1,0:T(8,128)(2,1)} %get-tuple-element.2547.refs_7_.back1_ref, ...), custom_call_target="tpu_custom_call" | custom-call | flops 4398046511104 | bytes 1073741824 | tf_op jit(solution)/shard_map/weight_grad/pallas_call | solution.py:1557
  602.8 12.2 %collective-permute-done.81.refs_1_ = bf16[512,768]{1,0:T(8,128)(2,1)S(1)} collective-permute-done((bf16[512,768]{1,0:T(8,128)(2,1)S(1)}, bf16[512,768]{1,0:T(8,128)(2,1)S(1)}, u32[]{:S(2)}, u32[]{:S(2)}) %collective-permute-start.81) | collective-permute-done | bytes 786464 | tf_op jit(solution)/shard_map/ppermute | solution.py:1629
  627.9 10.8 %collective-permute-done.84.refs_2_ = bf16[512,768]{1,0:T(8,128)(2,1)S(1)} collective-permute-done((bf16[512,768]{1,0:T(8,128)(2,1)}, bf16[512,768]{1,0:T(8,128)(2,1)S(1)}, u32[]{:S(2)}, u32[]{:S(2)}) %collective-permute-start.84) | collective-permute-done | bytes 786464 | tf_op jit(solution)/shard_map/ppermute | solution.py:1635
  650.3 10.6 %collective-permute-done.85.refs_1_ = bf16[128,768]{1,0:T(8,128)(2,1)S(1)} collective-permute-done((bf16[128,768]{1,0:T(8,128)(2,1)S(1)}, bf16[128,768]{1,0:T(8,128)(2,1)S(1)}, u32[]{:S(2)}, u32[]{:S(2)}) %collective-permute-start.85) | collective-permute-done | bytes 196640 | tf_op jit(solution)/shard_map/ppermute | solution.py:1644
  660.9 24.5 %collective-permute-done.86.refs_2_ = bf16[128,768]{1,0:T(8,128)(2,1)S(1)} collective-permute-done((bf16[128,768]{1,0:T(8,128)(2,1)S(1)}, bf16[128,768]{1,0:T(8,128)(2,1)S(1)}, u32[]{:S(2)}, u32[]{:S(2)}) %collective-permute-start.86) | collective-permute-done | bytes 196640 | tf_op jit(solution)/shard_map/ppermute | solution.py:1641
  692.3 10.6 %pad_convert_fusion = f32[4,1024,1024]{2,1,0:T(8,128)} fusion(bf16[4,512,1024]{2,1,0:T(8,128)(2,1)} %bitcast.51), kind=kLoop, calls=%fused_computation.1 | loop fusion | flops 4194304 | bytes 20971520 | tf_op jit(solution)/shard_map/dynamic_update_slice | solution.py:2108
  (448 shorter events, 298.5 us)
Async XLA Ops:
  7.2 457.4 %all-gather.7.cloned.1.call-start = ((), (), s32[]{:S(2)}) async-start(), calls=%async_computation | async-start | bytes 10485760 | tf_op jit(solution)/shard_map/all_gather | solution.py:1865
  56.6 43.3 %collective-permute-start.11 = (bf16[256,3456]{1,0:T(8,128)(2,1)}, bf16[256,3456]{1,0:T(8,128)(2,1)}, u32[]{:S(2)}, u32[]{:S(2)}) collective-permute-start(bf16[256,3456]{1,0:T(8,128)(2,1)} %get-tuple-element.2265.rest_0_), channel_id=1, source_target_pairs={{0,16},{16,0},{8,24},{24,8},{1,17},{17,1},{9,25},{25,9},{2,18},{18... | collective-permute-start | bytes 5308424 | tf_op jit(solution)/shard_map/ppermute | solution.py:1629
  57.4 42.4 %collective-permute-start.16 = (bf16[256,2304]{1,0:T(8,128)(2,1)}, bf16[256,2304]{1,0:T(8,128)(2,1)}, u32[]{:S(2)}, u32[]{:S(2)}) collective-permute-start(bf16[256,2304]{1,0:T(8,128)(2,1)} %get-tuple-element.1364), channel_id=1, source_target_pairs={{0,1},{1,2},{2,3},{3,0},{4,5},{5,6},{6,7},{7,4},{8,9},{9,10},{10,1... | collective-permute-start | bytes 3538952 | tf_op jit(solution)/shard_map/ppermute | solution.py:1638
  75.5 43.8 %collective-permute-start.17 = (bf16[512,1024]{1,0:T(8,128)(2,1)}, bf16[512,1024]{1,0:T(8,128)(2,1)}, u32[]{:S(2)}, u32[]{:S(2)}) collective-permute-start(bf16[512,1024]{1,0:T(8,128)(2,1)} %get-tuple-element.1356), channel_id=1, source_target_pairs={{0,4},{4,0},{1,5},{5,1},{2,6},{6,2},{3,7},{7,3},{8,12},{12,8},{9,1... | collective-permute-start | bytes 3145736 | tf_op jit(solution)/shard_map/ppermute | solution.py:1635
  181.8 32.1 %collective-permute-start.41 = (bf16[256,2304]{1,0:T(8,128)(2,1)}, bf16[256,2304]{1,0:T(8,128)(2,1)}, u32[]{:S(2)}, u32[]{:S(2)}) collective-permute-start(bf16[256,2304]{1,0:T(8,128)(2,1)} %collective-permute-done.16.rest_5_.rest_1_), channel_id=1, source_target_pairs={{0,1},{1,2},{2,3},{3,0},{4,5},{5,6},{6,7},{7,4},{8,9},{9,10},{10,1... | collective-permute-start | bytes 3538952 | tf_op jit(solution)/shard_map/ppermute | solution.py:1638
  283.8 408.5 %all-gather.9.cloned.1.call-start = ((), (), s32[]{:S(2)}) async-start(), calls=%async_computation.1 | async-start | bytes 5242880 | tf_op jit(solution)/shard_map/all_gather | solution.py:2024
  309.5 33.7 %collective-permute-start.56 = (bf16[512,3456]{1,0:T(8,128)(2,1)}, bf16[512,3456]{1,0:T(8,128)(2,1)}, u32[]{:S(2)}, u32[]{:S(2)}) collective-permute-start(bf16[512,3456]{1,0:T(8,128)(2,1)} %get-tuple-element.2176), channel_id=1, source_target_pairs={{0,8},{8,0},{16,24},{24,16},{1,9},{9,1},{17,25},{25,17},{2,10},{10... | collective-permute-start | bytes 10616840 | tf_op jit(solution)/shard_map/ppermute | solution.py:1632
  344.1 33.8 %collective-permute-start.58 = (bf16[512,3456]{1,0:T(8,128)(2,1)}, bf16[512,3456]{1,0:T(8,128)(2,1)S(1)}, u32[]{:S(2)}, u32[]{:S(2)}) collective-permute-start(bf16[512,3456]{1,0:T(8,128)(2,1)} %get-tuple-element.2248), channel_id=1, source_target_pairs={{0,8},{8,0},{16,24},{24,16},{1,9},{9,1},{17,25},{25,17},{2,10},{10... | collective-permute-start | bytes 10616840 | tf_op jit(solution)/shard_map/ppermute | solution.py:1632
  400.1 56.5 %collective-permute-start.67 = (bf16[1024,256]{1,0:T(8,128)(2,1)}, bf16[1024,256]{1,0:T(8,128)(2,1)S(1)}, u32[]{:S(2)}, u32[]{:S(2)}) collective-permute-start(bf16[1024,256]{1,0:T(8,128)(2,1)} %get-tuple-element.2393), channel_id=1, source_target_pairs={{0,4},{4,0},{1,5},{5,1},{2,6},{6,2},{3,7},{7,3},{8,12},{12,8},{9,1... | collective-permute-start | bytes 1572872 | tf_op jit(solution)/shard_map/ppermute | solution.py:1635
  400.8 55.9 %collective-permute-start.64 = (bf16[128,3456]{1,0:T(8,128)(2,1)}, bf16[128,3456]{1,0:T(8,128)(2,1)}, u32[]{:S(2)}, u32[]{:S(2)}) collective-permute-start(bf16[128,3456]{1,0:T(8,128)(2,1)} %get-tuple-element.2384), channel_id=1, source_target_pairs={{0,3},{1,0},{2,1},{3,2},{4,7},{5,4},{6,5},{7,6},{8,11},{9,8},{10,9... | collective-permute-start | bytes 2654216 | tf_op jit(solution)/shard_map/ppermute | solution.py:1644
  417.0 39.6 %collective-permute-start.68 = (bf16[128,3456]{1,0:T(8,128)(2,1)}, bf16[128,3456]{1,0:T(8,128)(2,1)S(1)}, u32[]{:S(2)}, u32[]{:S(2)}) collective-permute-start(bf16[128,3456]{1,0:T(8,128)(2,1)} %get-tuple-element.2414), channel_id=1, source_target_pairs={{0,4},{4,0},{1,5},{5,1},{2,6},{6,2},{3,7},{7,3},{8,12},{12,8},{9,1... | collective-permute-start | bytes 2654216 | tf_op jit(solution)/shard_map/ppermute | solution.py:1635
  418.7 37.9 %collective-permute-start.65 = (bf16[128,3456]{1,0:T(8,128)(2,1)}, bf16[128,3456]{1,0:T(8,128)(2,1)S(1)}, u32[]{:S(2)}, u32[]{:S(2)}) collective-permute-start(bf16[128,3456]{1,0:T(8,128)(2,1)} %get-tuple-element.2385), channel_id=1, source_target_pairs={{0,16},{16,0},{8,24},{24,8},{1,17},{17,1},{9,25},{25,9},{2,18},{18... | collective-permute-start | bytes 2654216 | tf_op jit(solution)/shard_map/ppermute | solution.py:1629
  419.4 39.5 %collective-permute-start.66 = (bf16[128,3456]{1,0:T(8,128)(2,1)}, bf16[128,3456]{1,0:T(8,128)(2,1)S(1)}, u32[]{:S(2)}, u32[]{:S(2)}) collective-permute-start(bf16[128,3456]{1,0:T(8,128)(2,1)} %get-tuple-element.2386), channel_id=1, source_target_pairs={{0,16},{16,0},{8,24},{24,8},{1,17},{17,1},{9,25},{25,9},{2,18},{18... | collective-permute-start | bytes 2654216 | tf_op jit(solution)/shard_map/ppermute | solution.py:1629
  464.1 39.7 %collective-permute-start.72 = (bf16[128,3456]{1,0:T(8,128)(2,1)}, bf16[128,3456]{1,0:T(8,128)(2,1)S(1)}, u32[]{:S(2)}, u32[]{:S(2)}) collective-permute-start(bf16[128,3456]{1,0:T(8,128)(2,1)} %get-tuple-element.2437), channel_id=1, source_target_pairs={{0,4},{4,0},{1,5},{5,1},{2,6},{6,2},{3,7},{7,3},{8,12},{12,8},{9,1... | collective-permute-start | bytes 2654216 | tf_op jit(solution)/shard_map/ppermute | solution.py:1635
  464.6 42.4 %collective-permute-start.71 = (bf16[512,1024]{1,0:T(8,128)(2,1)}, bf16[512,1024]{1,0:T(8,128)(2,1)S(1)}, u32[]{:S(2)}, u32[]{:S(2)}) collective-permute-start(bf16[512,1024]{1,0:T(8,128)(2,1)} %get-tuple-element.2425), channel_id=1, source_target_pairs={{0,4},{4,0},{1,5},{5,1},{2,6},{6,2},{3,7},{7,3},{8,12},{12,8},{9,1... | collective-permute-start | bytes 3145736 | tf_op jit(solution)/shard_map/ppermute | solution.py:1635
  466.2 37.6 %collective-permute-start.69 = (bf16[128,3456]{1,0:T(8,128)(2,1)}, bf16[128,3456]{1,0:T(8,128)(2,1)S(1)}, u32[]{:S(2)}, u32[]{:S(2)}) collective-permute-start(bf16[128,3456]{1,0:T(8,128)(2,1)} %get-tuple-element.2445), channel_id=1, source_target_pairs={{0,16},{16,0},{8,24},{24,8},{1,17},{17,1},{9,25},{25,9},{2,18},{18... | collective-permute-start | bytes 2654216 | tf_op jit(solution)/shard_map/ppermute | solution.py:1629
  466.9 38.1 %collective-permute-start.70 = (bf16[128,3456]{1,0:T(8,128)(2,1)}, bf16[128,3456]{1,0:T(8,128)(2,1)}, u32[]{:S(2)}, u32[]{:S(2)}) collective-permute-start(bf16[128,3456]{1,0:T(8,128)(2,1)} %get-tuple-element.2446), channel_id=1, source_target_pairs={{0,16},{16,0},{8,24},{24,8},{1,17},{17,1},{9,25},{25,9},{2,18},{18... | collective-permute-start | bytes 2654216 | tf_op jit(solution)/shard_map/ppermute | solution.py:1629
  507.3 48.8 %collective-permute-start.76 = (bf16[128,3456]{1,0:T(8,128)(2,1)}, bf16[128,3456]{1,0:T(8,128)(2,1)}, u32[]{:S(2)}, u32[]{:S(2)}) collective-permute-start(bf16[128,3456]{1,0:T(8,128)(2,1)} %get-tuple-element.2438), channel_id=1, source_target_pairs={{0,3},{1,0},{2,1},{3,2},{4,7},{5,4},{6,5},{7,6},{8,11},{9,8},{10,9... | collective-permute-start | bytes 2654216 | tf_op jit(solution)/shard_map/ppermute | solution.py:1644
  516.5 39.6 %collective-permute-start.77 = (bf16[128,3456]{1,0:T(8,128)(2,1)}, bf16[128,3456]{1,0:T(8,128)(2,1)}, u32[]{:S(2)}, u32[]{:S(2)}) collective-permute-start(bf16[128,3456]{1,0:T(8,128)(2,1)} %get-tuple-element.2539), channel_id=1, source_target_pairs={{0,1},{1,2},{2,3},{3,0},{4,5},{5,6},{6,7},{7,4},{8,9},{9,10},{10,1... | collective-permute-start | bytes 2654216 | tf_op jit(solution)/shard_map/ppermute | solution.py:1638
  516.5 39.6 %collective-permute-start.74 = (bf16[128,3456]{1,0:T(8,128)(2,1)}, bf16[128,3456]{1,0:T(8,128)(2,1)}, u32[]{:S(2)}, u32[]{:S(2)}) collective-permute-start(bf16[128,3456]{1,0:T(8,128)(2,1)} %get-tuple-element.2496), channel_id=1, source_target_pairs={{0,16},{16,0},{8,24},{24,8},{1,17},{17,1},{9,25},{25,9},{2,18},{18... | collective-permute-start | bytes 2654216 | tf_op jit(solution)/shard_map/ppermute | solution.py:1629
  546.1 178.4 %all-gather.11.cloned.1.call-start = ((), (), s32[]{:S(2)}) async-start(), calls=%async_computation.2 | async-start | bytes 5242880 | tf_op jit(solution)/shard_map/all_gather | solution.py:2030
  638.8 64.1 %collective-permute-start.88 = (f32[128,3456]{1,0:T(8,128)S(1)}, f32[128,3456]{1,0:T(8,128)}, u32[]{:S(2)}, u32[]{:S(2)}) collective-permute-start(f32[128,3456]{1,0:T(8,128)S(1)} %copy-done.33), channel_id=1, source_target_pairs={{0,4},{4,0},{1,5},{5,1},{2,6},{6,2},{3,7},{7,3},{8,12},{12,8},{9,1... | collective-permute-start | bytes 5308424 | tf_op jit(solution)/shard_map/ppermute | solution.py:1635
  649.6 35.9 %collective-permute-start.86 = (bf16[128,768]{1,0:T(8,128)(2,1)S(1)}, bf16[128,768]{1,0:T(8,128)(2,1)S(1)}, u32[]{:S(2)}, u32[]{:S(2)}) collective-permute-start(bf16[128,768]{1,0:T(8,128)(2,1)S(1)} %get-tuple-element.2667), channel_id=1, source_target_pairs={{0,2},{2,0},{1,3},{3,1},{4,6},{6,4},{5,7},{7,5},{8,10},{10,8},{9,1... | collective-permute-start | bytes 589832 | tf_op jit(solution)/shard_map/ppermute | solution.py:1641
  649.6 35.9 %collective-permute-start.87 = (bf16[128,768]{1,0:T(8,128)(2,1)S(1)}, bf16[128,768]{1,0:T(8,128)(2,1)S(1)}, u32[]{:S(2)}, u32[]{:S(2)}) collective-permute-start(bf16[128,768]{1,0:T(8,128)(2,1)S(1)} %get-tuple-element.2666), channel_id=1, source_target_pairs={{0,1},{1,2},{2,3},{3,0},{4,5},{5,6},{6,7},{7,4},{8,9},{9,10},{10,1... | collective-permute-start | bytes 589832 | tf_op jit(solution)/shard_map/ppermute | solution.py:1638
  (152 other events, 1878.3 us)
Sparse Core Ops, SparseCore 0:
  283.9 166.0 all-gather.6
  546.3 80.3 all-gather.8
  628.2 96.3 all-gather.10

commit v20 on v19

--- a/solution.py
+++ b/solution.py
@@ -1972,17 +1972,9 @@
     heads0 = y_swap(v.back0[1])
     far_h3 = x_swap(v.sum3[2])
     far_t0 = x_swap(v.sum0[3])
-    there3, two_down = sums(
-        info,
-        [v.sum3[1], v.far_t3, v.sum1[0], v.far_h1, v.there1, v.down2],
-        [
-            [(0, 0, None, False), (1, 0, None, False)],
-            [(2, 0, None, False), (3, 0, None, False), (4, 0, None, True), (5, 0, None, False)],
-        ],
-    )
+    [there3] = sums(info, [v.sum3[1], v.far_t3], [[(0, 0, None, False), (1, 0, None, False)]])
     there3_got = y_swap(there3)
-    two_down_got = z_down(two_down)
-    back1 = attn_back(1, after(v.grad_mine[1], there3, two_down, output))
+    back1 = attn_back(1, after(v.grad_mine[1], there3, output))
     v.update(
         heads0=heads0, far_h3=far_h3, far_t0=far_t0, there3=there3_got, back1=back1
     )
@@ -1990,11 +1982,26 @@
 
     heads1 = y_swap(v.back1[1])
     far_h0 = x_swap(v.sum0[2])
-    part3, there0 = sums(
+    part3, two_down, there0 = sums(
         info,
-        [v.sum3[0], v.far_h3, v.there3, v.sum0[1], v.far_t0],
-        [plane, [(3, 0, None, False), (4, 0, None, False)]],
-    )
+        [
+            v.sum3[0],
+            v.far_h3,
+            v.there3,
+            v.sum1[0],
+            v.far_h1,
+            v.there1,
+            v.down2,
+            v.sum0[1],
+            v.far_t0,
+        ],
+        [
+            plane,
+            [(3, 0, None, False), (4, 0, None, False), (5, 0, None, True), (6, 0, None, False)],
+            [(7, 0, None, False), (8, 0, None, False)],
+        ],
+    )
+    two_down_got = z_down(two_down)
     up3 = z_up(part3)
     tables = [v.cos_part, v.sin_part, v.gain_q, v.gain_k]
     head0 = head_back(

time: 752 us -> 751 us (level)
    unnamed x177 -> x175, local copies, waits for them, and re-layouts: 49.4 us -> 49.4 us
  transfers between devices with their start and end apart: 95 -> 95, of which waited for: 28 -> 29; matrix products, arithmetic and copies ran while one was open for 6% -> 6% of each run, Pallas kernels for 50% -> 50%
where the time goes in v20:
time: 751 us; the launch traced here: 740 us
  Pallas kernels  411 us (55%)
  waiting for transfers between devices  135 us (18%)
  starting transfers between devices  82.9 us (11%)
  local copies, waits for them, and re-layouts  63.5 us (8%)
  other arithmetic  28.5 us (4%)
  between operations  19 us (3%)
    pallas_call x4, Pallas kernels, ffn_bwd(): pl.pallas_call(functools.partial(ffn_bwd_kernel, steps, plan, first), gri...  101 us
    pallas_call x2, Pallas kernels, attn_bwd(): pl.pallas_call(functools.partial(attn_bwd_kernel, width, hd), grid_spec=p...  71.3 us
    pallas_call x3, Pallas kernels, ffn_fwd(): pl.pallas_call(functools.partial(ffn_fwd_kernel, tile, [plan for plan, _...  60.5 us
    unnamed x175, local copies, waits for them, and re-layouts  49.4 us
    ppermute x19, waiting for transfers between devices, y_swap(): return lax.ppermute(v, 'ctx', Y_SWAP)  41.6 us
    pallas_call x2, Pallas kernels, attn_fwd(): pl.pallas_call(functools.partial(attn_fwd_kernel, width, hd), grid_spec=p...  34.1 us
    pallas_call x6, Pallas kernels, sums(): pl.pallas_call(functools.partial(sums_kernel, jobs, len(arrays)), grid_sp...  34 us
    ppermute x22, waiting for transfers between devices, x_swap(): return lax.ppermute(v, 'fsdp', X_SWAP)  27 us
  transfers between devices with their start and end apart: 95, of which 29 were waited for; matrix products, arithmetic and copies ran while one was open for 6% of the time, Pallas kernels for 50%

profile of v20, /device:TPU:0, one launch (start us, length us, event | category | flops | bytes accessed | tf_op | source)
XLA Modules:
  0.0 739.9 jit_solution(10513728681349229235)
XLA Ops:
  86.7 13.1 %collective-permute-done.15.rest_4_.rest_0_ = bf16[256,1152]{1,0:T(8,128)(2,1)} collective-permute-done((bf16[256,1152]{1,0:T(8,128)(2,1)}, bf16[256,1152]{1,0:T(8,128)(2,1)}, u32[]{:S(2)}, u32[]{:S(2)}) %collective-permute-start.15) | collective-permute-done | bytes 589856 | tf_op jit(solution)/shard_map/ppermute | solution.py:1638
  102.2 17.1 %attn_fwd.2 = (bf16[1024,256]{1,0:T(8,128)(2,1)}, bf16[1024,256]{1,0:T(8,128)(2,1)}, f32[2,2,2048]{2,1,0:T(2,128)}) custom-call(s32[4]{0:T(128)} %copy-done.23, bf16[512,1024]{1,0:T(8,128)(2,1)} %copy-done.30, bf16[512,1024]{1,0:T(8,128)(2,1)} %copy-done.65), custom_call_target="tpu_custom_call" | custom-call | flops 4398046511104 | bytes 1073741824 | tf_op jit(solution)/shard_map/attn_fwd/pallas_call | solution.py:778
  126.4 17.0 %attn_fwd.3 = (bf16[1024,256]{1,0:T(8,128)(2,1)}, bf16[1024,256]{1,0:T(8,128)(2,1)}, f32[2,2,2048]{2,1,0:T(2,128)}) custom-call(s32[4]{0:T(128)} %copy-done.23, bf16[512,1024]{1,0:T(8,128)(2,1)} %copy-done.29, bf16[512,1024]{1,0:T(8,128)(2,1)} %collective-permute-done.17.got_ref), custom_call_target="tpu_custom_call" | custom-call | flops 4398046511104 | bytes 1073741824 | tf_op jit(solution)/shard_map/attn_fwd/pallas_call | solution.py:778
  148.4 13.1 %collective-permute-done.27.refs_8_ = bf16[1024,256]{1,0:T(8,128)(2,1)S(1)} collective-permute-done((bf16[1024,256]{1,0:T(8,128)(2,1)}, bf16[1024,256]{1,0:T(8,128)(2,1)S(1)}, u32[]{:S(2)}, u32[]{:S(2)}) %collective-permute-start.27) | collective-permute-done | bytes 524320 | tf_op jit(solution)/shard_map/ppermute | solution.py:1635
  164.6 10.3 %out_proj.1 = (f32[1024,1024]{1,0:T(8,128)}, bf16[1024,1024]{1,0:T(8,128)(2,1)}, bf16[1024,1024]{1,0:T(8,128)(2,1)}, bf16[4,1024,256]{2,1,0:T(8,128)(2,1)}) custom-call(s32[4]{0:T(128)} %copy-done.23, bf16[1024,256]{1,0:T(8,128)(2,1)} %constant_dynamic-update-slice_fusion.refs_0_, bf16[1024,256]{1,0:T(8,128)(2,1)} %collective-permute-done.25.refs_1_, ...), custom_call_target="tpu_custom_call" | custom-call | flops 4398046511104 | bytes 1073741824 | tf_op jit(solution)/shard_map/out_proj/pallas_call | solution.py:1004
  185.8 27.2 %ffn_fwd.3 = (bf16[2,1024,2304]{2,1,0:T(8,128)(2,1)}, bf16[2,1024,1152]{2,1,0:T(8,128)(2,1)}, f32[1024,1024]{1,0:T(8,128)}) custom-call(s32[4]{0:T(128)} %copy-done.23, f32[1]{0:T(128)} %bitcast.4.scale, bf16[1024,1024]{1,0:T(8,128)(2,1)} %get-tuple-element.1781.x_ref, f32[1024,1024]{1,0:T(8,128)} %get-tuple-element.2334.in_ref.refs_5_, ...), custom_call_target="tpu_custom_call" | custom-call | flops 4398046511104 | bytes 1073741824 | tf_op jit(solution)/shard_map/ffn_fwd/pallas_call | solution.py:1292
  220.4 15.7 %ffn_fwd.4 = (bf16[1,1024,2304]{2,1,0:T(8,128)(2,1)}, bf16[1,1024,1152]{2,1,0:T(8,128)(2,1)}, f32[1024,1024]{1,0:T(8,128)}) custom-call(s32[4]{0:T(128)} %copy-done.23, f32[1]{0:T(128)} %bitcast.4.scale, bf16[1024,1024]{1,0:T(8,128)(2,1)} %get-tuple-element.1781.x_ref, f32[1024,1024]{1,0:T(8,128)} %get-tuple-element.1681.in_ref, ...), custom_call_target="tpu_custom_call" | custom-call | flops 4398046511104 | bytes 1073741824 | tf_op jit(solution)/shard_map/ffn_fwd/pallas_call | solution.py:1292
  240.2 17.7 %ffn_fwd.5 = (bf16[1,1024,2304]{2,1,0:T(8,128)(2,1)}, bf16[1,1024,1152]{2,1,0:T(8,128)(2,1)}, bf16[1024,1024]{1,0:T(8,128)(2,1)}, bf16[1024,1024]{1,0:T(8,128)(2...) custom-call(s32[4]{0:T(128)} %copy-done.23, f32[1]{0:T(128)} %bitcast.4.scale, ...), custom_call_target="tpu_custom_call" | custom-call | flops 4398046511104 | bytes 1073741824 | tf_op jit(solution)/shard_map/ffn_fwd/pallas_call | solution.py:1292
  257.9 24.8 %ffn_bwd.4 = (f32[1024,1024]{1,0:T(8,128)}, bf16[512,3456]{1,0:T(8,128)(2,1)}, bf16[512,3456]{1,0:T(8,128)(2,1)}) custom-call(bf16[1024,1024]{1,0:T(8,128)(2,1)} %get-tuple-element.2335.low_ref.refs_6_, bf16[1,1024,2304]{2,1,0:T(8,128)(2,1)} %get-tuple-element.1903.act_ref, bf16[1,1024,1152]{2,1,0:T(8,128)(2,1)} %get-tuple-element.1922.hid_ref, ...), custom_call_target="tpu_custom_call" | custom-call | flops 12880000000 | bytes 3144531 | tf_op jit(solution)/shard_map/ffn_bwd/pallas_call | solution.py:1374
  282.9 25.7 %ffn_bwd.5 = (f32[1024,1024]{1,0:T(8,128)}, bf16[512,3456]{1,0:T(8,128)(2,1)}, bf16[512,3456]{1,0:T(8,128)(2,1)}) custom-call(bf16[1024,1024]{1,0:T(8,128)(2,1)} %get-tuple-element.2335.low_ref.refs_6_, bf16[2,1024,2304]{2,1,0:T(8,128)(2,1)} %get-tuple-element.2248.act_ref, ...), custom_call_target="tpu_custom_call", output_to_operand_aliasing={{0}: (15, {})} | custom-call | flops 12880000000 | bytes 3144531 | tf_op jit(solution)/shard_map/ffn_bwd/pallas_call | solution.py:1374
  317.5 25.5 %ffn_bwd.6 = (f32[1024,1024]{1,0:T(8,128)}, bf16[512,3456]{1,0:T(8,128)(2,1)}, bf16[512,3456]{1,0:T(8,128)(2,1)}) custom-call(bf16[1024,1024]{1,0:T(8,128)(2,1)} %get-tuple-element.2335.low_ref.refs_6_, bf16[1,1024,2304]{2,1,0:T(8,128)(2,1)} %get-tuple-element.2177.act_ref, ...), custom_call_target="tpu_custom_call", output_to_operand_aliasing={{0}: (17, {})} | custom-call | flops 12880000000 | bytes 3144531 | tf_op jit(solution)/shard_map/ffn_bwd/pallas_call | solution.py:1374
  352.0 25.4 %ffn_bwd.7 = (f32[1024,1024]{1,0:T(8,128)}, bf16[512,3456]{1,0:T(8,128)(2,1)}, bf16[512,3456]{1,0:T(8,128)(2,1)}) custom-call(bf16[1024,1024]{1,0:T(8,128)(2,1)} %get-tuple-element.2335.low_ref.refs_6_, bf16[2,1024,2304]{2,1,0:T(8,128)(2,1)} %get-tuple-element.2248.act_ref, ...), custom_call_target="tpu_custom_call", output_to_operand_aliasing={{0}: (9, {})} | custom-call | flops 12880000000 | bytes 3144531 | tf_op jit(solution)/shard_map/ffn_bwd/pallas_call | solution.py:1374
  386.9 11.2 %norm_two_back.1 = (bf16[1024,1024]{1,0:T(8,128)(2,1)}, bf16[1024,1024]{1,0:T(8,128)(2,1)}, bf16[1024,256]{1,0:T(8,128)(2,1)}, bf16[1024,256]{1,0:T(8,128)(2,1)}...) custom-call(s32[4]{0:T(128)} %copy-done.23, ...), custom_call_target="tpu_custom_call" | custom-call | flops 6209999872 | bytes 1516113 | tf_op jit(solution)/shard_map/norm_two_back/pallas_call | solution.py:1062
  420.0 35.9 %attn_bwd.2 = (bf16[512,1024]{1,0:T(8,128)(2,1)}, bf16[512,1024]{1,0:T(8,128)(2,1)}) custom-call(s32[4]{0:T(128)} %copy-done.23, bf16[512,1024]{1,0:T(8,128)(2,1)} %copy-done.30, bf16[512,1024]{1,0:T(8,128)(2,1)} %copy-done.65, bf16[1024,256]{1,0:T(8,128)(2,1)} %get-tuple-element.2373.refs_5_.ok_ref, bf16[1024,256]{1,0:T(8,128)(2,1)} %get-tuple-element.2374.os_ref, ...), custom_call_target="tpu_custom_call" | custom-call | flops 18630000640 | bytes 4548339 | tf_op jit(solution)/shard_map/attn_bwd/pallas_call | solution.py:939
  466.3 35.4 %attn_bwd.3 = (bf16[512,1024]{1,0:T(8,128)(2,1)}, bf16[512,1024]{1,0:T(8,128)(2,1)}) custom-call(s32[4]{0:T(128)} %copy-done.23, bf16[512,1024]{1,0:T(8,128)(2,1)} %copy-done.29, bf16[512,1024]{1,0:T(8,128)(2,1)} %collective-permute-done.17.got_ref, bf16[1024,256]{1,0:T(8,128)(2,1)} %get-tuple-element.2431.refs_6_.ok_ref, ...), custom_call_target="tpu_custom_call" | custom-call | flops 18630000640 | bytes 4548339 | tf_op jit(solution)/shard_map/attn_bwd/pallas_call | solution.py:939
  535.5 8.6 %norm_one_back.2 = (bf16[512,1024]{1,0:T(8,128)(2,1)}, f32[1,1024]{1,0:T(1,128)}) custom-call(s32[4]{0:T(128)} %copy-done.23, bf16[512,512]{1,0:T(8,128)(2,1)} %copy-done.2, bf16[768,512]{1,0:T(8,128)(2,1)} %copy-done.1, bf16[768,512]{1,0:T(8,128)(2,1)} %collective-permute-done.10.refs_2_, bf16[512,512]{1,0:T(8,128)(2,1)} %copy-done.5, ...), custom_call_target="tpu_custom_call" | custom-call | flops 4398046511104 | bytes 1073741824 | tf_op jit(solution)/shard_map/norm_one_back/pallas_call | solution.py:1119
  545.0 8.8 %norm_one_back.3 = (bf16[512,1024]{1,0:T(8,128)(2,1)}, f32[1,1024]{1,0:T(1,128)}) custom-call(s32[4]{0:T(128)} %copy-done.23, bf16[512,512]{1,0:T(8,128)(2,1)} %copy-done.2, bf16[768,512]{1,0:T(8,128)(2,1)} %copy-done.1, bf16[768,512]{1,0:T(8,128)(2,1)} %collective-permute-done.10.refs_2_, bf16[512,512]{1,0:T(8,128)(2,1)} %copy-done.5, ...), custom_call_target="tpu_custom_call" | custom-call | flops 4398046511104 | bytes 1073741824 | tf_op jit(solution)/shard_map/norm_one_back/pallas_call | solution.py:1119
  554.5 8.5 %collective-permute-done.75.refs_2_ = bf16[128,3456]{1,0:T(8,128)(2,1)} collective-permute-done((bf16[128,3456]{1,0:T(8,128)(2,1)}, bf16[128,3456]{1,0:T(8,128)(2,1)}, u32[]{:S(2)}, u32[]{:S(2)}) %collective-permute-start.75) | collective-permute-done | bytes 884768 | tf_op jit(solution)/shard_map/ppermute | solution.py:1635
  565.3 15.2 %weight_grad.1 = (bf16[4,512,768]{2,1,0:T(8,128)(2,1)}, bf16[4,512,768]{2,1,0:T(8,128)(2,1)}) custom-call(bf16[1024,1024]{1,0:T(8,128)(2,1)} %copy-done, bf16[2,1024,512]{2,1,0:T(8,128)(2,1)} %get-tuple-element.2551.refs_6_.back0_ref, bf16[2,1024,512]{2,1,0:T(8,128)(2,1)} %get-tuple-element.2553.refs_7_.back1_ref, ...), custom_call_target="tpu_custom_call" | custom-call | flops 4398046511104 | bytes 1073741824 | tf_op jit(solution)/shard_map/weight_grad/pallas_call | solution.py:1557
  601.2 11.8 %collective-permute-done.81.refs_1_ = bf16[512,768]{1,0:T(8,128)(2,1)S(1)} collective-permute-done((bf16[512,768]{1,0:T(8,128)(2,1)S(1)}, bf16[512,768]{1,0:T(8,128)(2,1)S(1)}, u32[]{:S(2)}, u32[]{:S(2)}) %collective-permute-start.81) | collective-permute-done | bytes 786464 | tf_op jit(solution)/shard_map/ppermute | solution.py:1629
  626.3 10.5 %collective-permute-done.84.refs_2_ = bf16[512,768]{1,0:T(8,128)(2,1)S(1)} collective-permute-done((bf16[512,768]{1,0:T(8,128)(2,1)}, bf16[512,768]{1,0:T(8,128)(2,1)S(1)}, u32[]{:S(2)}, u32[]{:S(2)}) %collective-permute-start.84) | collective-permute-done | bytes 786464 | tf_op jit(solution)/shard_map/ppermute | solution.py:1635
  648.4 10.3 %collective-permute-done.85.refs_1_ = bf16[128,768]{1,0:T(8,128)(2,1)S(1)} collective-permute-done((bf16[128,768]{1,0:T(8,128)(2,1)S(1)}, bf16[128,768]{1,0:T(8,128)(2,1)S(1)}, u32[]{:S(2)}, u32[]{:S(2)}) %collective-permute-start.85) | collective-permute-done | bytes 196640 | tf_op jit(solution)/shard_map/ppermute | solution.py:1644
  658.7 24.9 %collective-permute-done.86.refs_2_ = bf16[128,768]{1,0:T(8,128)(2,1)S(1)} collective-permute-done((bf16[128,768]{1,0:T(8,128)(2,1)S(1)}, bf16[128,768]{1,0:T(8,128)(2,1)S(1)}, u32[]{:S(2)}, u32[]{:S(2)}) %collective-permute-start.86) | collective-permute-done | bytes 196640 | tf_op jit(solution)/shard_map/ppermute | solution.py:1641
  690.5 10.6 %pad_convert_fusion = f32[4,1024,1024]{2,1,0:T(8,128)} fusion(bf16[4,512,1024]{2,1,0:T(8,128)(2,1)} %bitcast.51), kind=kLoop, calls=%fused_computation.1 | loop fusion | flops 4194304 | bytes 20971520 | tf_op jit(solution)/shard_map/dynamic_update_slice | solution.py:2115
  (446 shorter events, 296.6 us)
Async XLA Ops:
  7.2 455.8 %all-gather.7.cloned.1.call-start = ((), (), s32[]{:S(2)}) async-start(), calls=%async_computation | async-start | bytes 10485760 | tf_op jit(solution)/shard_map/all_gather | solution.py:1865
  56.5 43.3 %collective-permute-start.11 = (bf16[256,3456]{1,0:T(8,128)(2,1)}, bf16[256,3456]{1,0:T(8,128)(2,1)}, u32[]{:S(2)}, u32[]{:S(2)}) collective-permute-start(bf16[256,3456]{1,0:T(8,128)(2,1)} %get-tuple-element.2268.rest_0_), channel_id=1, source_target_pairs={{0,16},{16,0},{8,24},{24,8},{1,17},{17,1},{9,25},{25,9},{2,18},{18... | collective-permute-start | bytes 5308424 | tf_op jit(solution)/shard_map/ppermute | solution.py:1629
  57.4 42.4 %collective-permute-start.16 = (bf16[256,2304]{1,0:T(8,128)(2,1)}, bf16[256,2304]{1,0:T(8,128)(2,1)}, u32[]{:S(2)}, u32[]{:S(2)}) collective-permute-start(bf16[256,2304]{1,0:T(8,128)(2,1)} %get-tuple-element.1367), channel_id=1, source_target_pairs={{0,1},{1,2},{2,3},{3,0},{4,5},{5,6},{6,7},{7,4},{8,9},{9,10},{10,1... | collective-permute-start | bytes 3538952 | tf_op jit(solution)/shard_map/ppermute | solution.py:1638
  75.5 43.7 %collective-permute-start.17 = (bf16[512,1024]{1,0:T(8,128)(2,1)}, bf16[512,1024]{1,0:T(8,128)(2,1)}, u32[]{:S(2)}, u32[]{:S(2)}) collective-permute-start(bf16[512,1024]{1,0:T(8,128)(2,1)} %get-tuple-element.1359), channel_id=1, source_target_pairs={{0,4},{4,0},{1,5},{5,1},{2,6},{6,2},{3,7},{7,3},{8,12},{12,8},{9,1... | collective-permute-start | bytes 3145736 | tf_op jit(solution)/shard_map/ppermute | solution.py:1635
  181.0 32.1 %collective-permute-start.41 = (bf16[256,2304]{1,0:T(8,128)(2,1)}, bf16[256,2304]{1,0:T(8,128)(2,1)}, u32[]{:S(2)}, u32[]{:S(2)}) collective-permute-start(bf16[256,2304]{1,0:T(8,128)(2,1)} %collective-permute-done.16.rest_5_.rest_1_), channel_id=1, source_target_pairs={{0,1},{1,2},{2,3},{3,0},{4,5},{5,6},{6,7},{7,4},{8,9},{9,10},{10,1... | collective-permute-start | bytes 3538952 | tf_op jit(solution)/shard_map/ppermute | solution.py:1638
  282.9 407.6 %all-gather.9.cloned.1.call-start = ((), (), s32[]{:S(2)}) async-start(), calls=%async_computation.1 | async-start | bytes 5242880 | tf_op jit(solution)/shard_map/all_gather | solution.py:2031
  308.7 34.3 %collective-permute-start.56 = (bf16[512,3456]{1,0:T(8,128)(2,1)}, bf16[512,3456]{1,0:T(8,128)(2,1)}, u32[]{:S(2)}, u32[]{:S(2)}) collective-permute-start(bf16[512,3456]{1,0:T(8,128)(2,1)} %get-tuple-element.2179), channel_id=1, source_target_pairs={{0,8},{8,0},{16,24},{24,16},{1,9},{9,1},{17,25},{25,17},{2,10},{10... | collective-permute-start | bytes 10616840 | tf_op jit(solution)/shard_map/ppermute | solution.py:1632
  343.9 33.5 %collective-permute-start.58 = (bf16[512,3456]{1,0:T(8,128)(2,1)}, bf16[512,3456]{1,0:T(8,128)(2,1)S(1)}, u32[]{:S(2)}, u32[]{:S(2)}) collective-permute-start(bf16[512,3456]{1,0:T(8,128)(2,1)} %get-tuple-element.2251), channel_id=1, source_target_pairs={{0,8},{8,0},{16,24},{24,16},{1,9},{9,1},{17,25},{25,17},{2,10},{10... | collective-permute-start | bytes 10616840 | tf_op jit(solution)/shard_map/ppermute | solution.py:1632
  399.8 56.1 %collective-permute-start.67 = (bf16[1024,256]{1,0:T(8,128)(2,1)}, bf16[1024,256]{1,0:T(8,128)(2,1)S(1)}, u32[]{:S(2)}, u32[]{:S(2)}) collective-permute-start(bf16[1024,256]{1,0:T(8,128)(2,1)} %get-tuple-element.2396), channel_id=1, source_target_pairs={{0,4},{4,0},{1,5},{5,1},{2,6},{6,2},{3,7},{7,3},{8,12},{12,8},{9,1... | collective-permute-start | bytes 1572872 | tf_op jit(solution)/shard_map/ppermute | solution.py:1635
  400.2 55.7 %collective-permute-start.64 = (bf16[128,3456]{1,0:T(8,128)(2,1)}, bf16[128,3456]{1,0:T(8,128)(2,1)}, u32[]{:S(2)}, u32[]{:S(2)}) collective-permute-start(bf16[128,3456]{1,0:T(8,128)(2,1)} %get-tuple-element.2387), channel_id=1, source_target_pairs={{0,3},{1,0},{2,1},{3,2},{4,7},{5,4},{6,5},{7,6},{8,11},{9,8},{10,9... | collective-permute-start | bytes 2654216 | tf_op jit(solution)/shard_map/ppermute | solution.py:1644
  416.5 39.4 %collective-permute-start.68 = (bf16[128,3456]{1,0:T(8,128)(2,1)}, bf16[128,3456]{1,0:T(8,128)(2,1)S(1)}, u32[]{:S(2)}, u32[]{:S(2)}) collective-permute-start(bf16[128,3456]{1,0:T(8,128)(2,1)} %get-tuple-element.2417), channel_id=1, source_target_pairs={{0,4},{4,0},{1,5},{5,1},{2,6},{6,2},{3,7},{7,3},{8,12},{12,8},{9,1... | collective-permute-start | bytes 2654216 | tf_op jit(solution)/shard_map/ppermute | solution.py:1635
  417.9 38.0 %collective-permute-start.65 = (bf16[128,3456]{1,0:T(8,128)(2,1)}, bf16[128,3456]{1,0:T(8,128)(2,1)S(1)}, u32[]{:S(2)}, u32[]{:S(2)}) collective-permute-start(bf16[128,3456]{1,0:T(8,128)(2,1)} %get-tuple-element.2388), channel_id=1, source_target_pairs={{0,16},{16,0},{8,24},{24,8},{1,17},{17,1},{9,25},{25,9},{2,18},{18... | collective-permute-start | bytes 2654216 | tf_op jit(solution)/shard_map/ppermute | solution.py:1629
  419.1 39.0 %collective-permute-start.66 = (bf16[128,3456]{1,0:T(8,128)(2,1)}, bf16[128,3456]{1,0:T(8,128)(2,1)S(1)}, u32[]{:S(2)}, u32[]{:S(2)}) collective-permute-start(bf16[128,3456]{1,0:T(8,128)(2,1)} %get-tuple-element.2389), channel_id=1, source_target_pairs={{0,16},{16,0},{8,24},{24,8},{1,17},{17,1},{9,25},{25,9},{2,18},{18... | collective-permute-start | bytes 2654216 | tf_op jit(solution)/shard_map/ppermute | solution.py:1629
  462.2 39.6 %collective-permute-start.72 = (bf16[128,3456]{1,0:T(8,128)(2,1)}, bf16[128,3456]{1,0:T(8,128)(2,1)S(1)}, u32[]{:S(2)}, u32[]{:S(2)}) collective-permute-start(bf16[128,3456]{1,0:T(8,128)(2,1)} %sums.10), channel_id=1, source_target_pairs={{0,4},{4,0},{1,5},{5,1},{2,6},{6,2},{3,7},{7,3},{8,12},{12,8},{9,1... | collective-permute-start | bytes 2654216 | tf_op jit(solution)/shard_map/ppermute | solution.py:1635
  463.0 42.0 %collective-permute-start.71 = (bf16[512,1024]{1,0:T(8,128)(2,1)}, bf16[512,1024]{1,0:T(8,128)(2,1)S(1)}, u32[]{:S(2)}, u32[]{:S(2)}) collective-permute-start(bf16[512,1024]{1,0:T(8,128)(2,1)} %get-tuple-element.2428), channel_id=1, source_target_pairs={{0,4},{4,0},{1,5},{5,1},{2,6},{6,2},{3,7},{7,3},{8,12},{12,8},{9,1... | collective-permute-start | bytes 3145736 | tf_op jit(solution)/shard_map/ppermute | solution.py:1635
  464.3 37.5 %collective-permute-start.69 = (bf16[128,3456]{1,0:T(8,128)(2,1)}, bf16[128,3456]{1,0:T(8,128)(2,1)}, u32[]{:S(2)}, u32[]{:S(2)}) collective-permute-start(bf16[128,3456]{1,0:T(8,128)(2,1)} %get-tuple-element.2444), channel_id=1, source_target_pairs={{0,16},{16,0},{8,24},{24,8},{1,17},{17,1},{9,25},{25,9},{2,18},{18... | collective-permute-start | bytes 2654216 | tf_op jit(solution)/shard_map/ppermute | solution.py:1629
  465.5 37.5 %collective-permute-start.70 = (bf16[128,3456]{1,0:T(8,128)(2,1)}, bf16[128,3456]{1,0:T(8,128)(2,1)}, u32[]{:S(2)}, u32[]{:S(2)}) collective-permute-start(bf16[128,3456]{1,0:T(8,128)(2,1)} %get-tuple-element.2445), channel_id=1, source_target_pairs={{0,16},{16,0},{8,24},{24,8},{1,17},{17,1},{9,25},{25,9},{2,18},{18... | collective-permute-start | bytes 2654216 | tf_op jit(solution)/shard_map/ppermute | solution.py:1629
  512.6 41.9 %collective-permute-start.76 = (bf16[128,3456]{1,0:T(8,128)(2,1)}, bf16[128,3456]{1,0:T(8,128)(2,1)}, u32[]{:S(2)}, u32[]{:S(2)}) collective-permute-start(bf16[128,3456]{1,0:T(8,128)(2,1)} %get-tuple-element.2544), channel_id=1, source_target_pairs={{0,3},{1,0},{2,1},{3,2},{4,7},{5,4},{6,5},{7,6},{8,11},{9,8},{10,9... | collective-permute-start | bytes 2654216 | tf_op jit(solution)/shard_map/ppermute | solution.py:1644
  516.3 38.3 %collective-permute-start.77 = (bf16[128,3456]{1,0:T(8,128)(2,1)}, bf16[128,3456]{1,0:T(8,128)(2,1)}, u32[]{:S(2)}, u32[]{:S(2)}) collective-permute-start(bf16[128,3456]{1,0:T(8,128)(2,1)} %get-tuple-element.2545), channel_id=1, source_target_pairs={{0,1},{1,2},{2,3},{3,0},{4,5},{5,6},{6,7},{7,4},{8,9},{9,10},{10,1... | collective-permute-start | bytes 2654216 | tf_op jit(solution)/shard_map/ppermute | solution.py:1638
  516.3 38.3 %collective-permute-start.74 = (bf16[128,3456]{1,0:T(8,128)(2,1)}, bf16[128,3456]{1,0:T(8,128)(2,1)}, u32[]{:S(2)}, u32[]{:S(2)}) collective-permute-start(bf16[128,3456]{1,0:T(8,128)(2,1)} %get-tuple-element.2499), channel_id=1, source_target_pairs={{0,16},{16,0},{8,24},{24,8},{1,17},{17,1},{9,25},{25,9},{2,18},{18... | collective-permute-start | bytes 2654216 | tf_op jit(solution)/shard_map/ppermute | solution.py:1629
  544.2 178.8 %all-gather.11.cloned.1.call-start = ((), (), s32[]{:S(2)}) async-start(), calls=%async_computation.2 | async-start | bytes 5242880 | tf_op jit(solution)/shard_map/all_gather | solution.py:2037
  637.2 63.9 %collective-permute-start.88 = (f32[128,3456]{1,0:T(8,128)S(1)}, f32[128,3456]{1,0:T(8,128)}, u32[]{:S(2)}, u32[]{:S(2)}) collective-permute-start(f32[128,3456]{1,0:T(8,128)S(1)} %copy-done.33), channel_id=1, source_target_pairs={{0,4},{4,0},{1,5},{5,1},{2,6},{6,2},{3,7},{7,3},{8,12},{12,8},{9,1... | collective-permute-start | bytes 5308424 | tf_op jit(solution)/shard_map/ppermute | solution.py:1635
  647.6 36.0 %collective-permute-start.86 = (bf16[128,768]{1,0:T(8,128)(2,1)S(1)}, bf16[128,768]{1,0:T(8,128)(2,1)S(1)}, u32[]{:S(2)}, u32[]{:S(2)}) collective-permute-start(bf16[128,768]{1,0:T(8,128)(2,1)S(1)} %get-tuple-element.2673), channel_id=1, source_target_pairs={{0,2},{2,0},{1,3},{3,1},{4,6},{6,4},{5,7},{7,5},{8,10},{10,8},{9,1... | collective-permute-start | bytes 589832 | tf_op jit(solution)/shard_map/ppermute | solution.py:1641
  647.6 36.0 %collective-permute-start.87 = (bf16[128,768]{1,0:T(8,128)(2,1)S(1)}, bf16[128,768]{1,0:T(8,128)(2,1)S(1)}, u32[]{:S(2)}, u32[]{:S(2)}) collective-permute-start(bf16[128,768]{1,0:T(8,128)(2,1)S(1)} %get-tuple-element.2672), channel_id=1, source_target_pairs={{0,1},{1,2},{2,3},{3,0},{4,5},{5,6},{6,7},{7,4},{8,9},{9,10},{10,1... | collective-permute-start | bytes 589832 | tf_op jit(solution)/shard_map/ppermute | solution.py:1638
  (151 other events, 1908.0 us)
Sparse Core Ops, SparseCore 0:
  283.0 166.3 all-gather.6
  544.3 80.6 all-gather.8
  626.6 96.3 all-gather.10
